TPU v7x, 32 devices: a whole 2x2x4 slice. The times are simulated.
32 devices in a mesh: groups: 2 (over x), blk: 8 (over z, y), head: 2 (over core).
Axes of the slice: x: 2, y: 2, z: 4, core: 2. Of those that a mesh axis runs over, the one named last changes fastest.
Arguments:
- queries: bfloat16 [1024, 36864], P(('groups', 'blk'), 'head'), parts along dimension 0, may hold values from -750 to 750
- latent_cache: bfloat16 [128, 576, 256], P(('groups', 'blk')), parts along dimension 0, may hold values from -6 to 6
- new_latent: bfloat16 [576, 1024], P(None, ('groups', 'blk')), parts along dimension 1, may hold values from -6 to 6
- span_len: int32 [16], P('groups'), parts along dimension 0, may hold values from 2 to 57, as said below
- dec_count: int32 [16], P('groups'), parts along dimension 0, may hold values from 1 to 7, as said below
- span_start: int32 [16], P(('groups', 'blk')), parts along dimension 0, may hold values from 0 to 256, as said below
- cache_len: int32 [16, 7], P(('groups', 'blk')), parts along dimension 0, may hold values from 2 to 256, as said below
- value_weight: bfloat16 [64, 512, 128], P('head'), may hold values from -0.25 to 0.25
- out_weight: bfloat16 [8192, 7168], P('head', 'blk'), may hold values from -0.0625 to 0.0625
- residual: bfloat16 [1024, 7168], P(('groups', 'blk')), parts along dimension 0, may hold values from -34 to 34
- norm_gain: float32 [7168], replicated, may hold values from 0.1 to 1.9
- gate_weight: bfloat16 [7168, 9216], P(None, ('blk', 'head')), may hold values from -0.0625 to 0.0625
- up_weight: bfloat16 [7168, 9216], P(None, ('blk', 'head')), may hold values from -0.0625 to 0.0625
- down_weight: bfloat16 [9216, 7168], P(('blk', 'head')), may hold values from -0.0625 to 0.0625
Outputs:
- mixed: bfloat16 [1024, 7168], P(('groups', 'blk', 'head')), parts along dimension 0
There are 2 independent parts, one for each index of `groups`. A program takes and returns all parts, laid end to end along the dimension named above; an argument that names none is the same for every part. Nothing has to cross between parts.
Inputs may be any that keep to these rules, and one draw needn't show every extreme that they name: span_len + dec_count is at most 64 on every rank, exactly 64 on one rank, at most 32 on every other rank and exactly 32 on some other rank; its sum over all ranks is exactly 256. `dec_count`: decode row j of a rank uses the rank's sequence slot j + 1. `span_start`: the cached positions of a rank's sequence slot 0. `cache_len`: entry j belongs to sequence slot j + 1; entries at or past a rank's dec_count are unused.
All inputs are finite; a program needn't handle non-finite values.
Results may differ from a plain program's by a relative error of at most 0.02.
Values may be sent and summed in bfloat16 or wider, within the bound.
No kernel may reach another device: no remote copies, remote signals or barrier semaphores. Data moves between devices by JAX's collectives and lax.ppermute only.
A program may use at most 128 MiB of HBM per device.

v0:
```python
import jax
import jax.numpy as jnp
from jax import lax
from jax.sharding import PartitionSpec as P

score_scale = 192.0 ** (-0.5)
norm_eps = 1e-06
masked_score = -1e30


def rounded(values):
    return lax.optimization_barrier(values.astype(jnp.bfloat16)).astype(jnp.float32)


def pick_rank(values, rank_index):
    matches = jnp.arange(values.shape[0], dtype=jnp.int32) == rank_index
    return jnp.sum(jnp.where(matches, values, 0))


def local_attention(
    query_rows, cache_slots, fresh_keys, span_rows, decode_rows, start_pos, lengths, key_width
):
    row_count = query_rows.shape[0]
    slot_count = cache_slots.shape[0]
    positions = jnp.arange(cache_slots.shape[2], dtype=jnp.int32)
    local_rows = jnp.arange(row_count, dtype=jnp.int32)
    cached_scores = (
        jnp.einsum("rhl,lt->rht", query_rows, cache_slots[0], preferred_element_type=jnp.float32)
        * score_scale
    )
    fresh_scores = (
        jnp.einsum("rhl,lj->rhj", query_rows, fresh_keys, preferred_element_type=jnp.float32)
        * score_scale
    )
    cached_seen = (positions < start_pos)[None, None, :]
    fresh_seen = (local_rows[None, :] <= local_rows[:, None])[:, None, :]
    cached_scores = jnp.where(cached_seen, cached_scores, masked_score)
    fresh_scores = jnp.where(fresh_seen, fresh_scores, masked_score)
    peak_score = jnp.maximum(jnp.max(cached_scores, axis=2), jnp.max(fresh_scores, axis=2))[
        :, :, None
    ]
    cached_exp = jnp.where(cached_seen, jnp.exp(cached_scores - peak_score), 0.0)
    fresh_exp = jnp.where(fresh_seen, jnp.exp(fresh_scores - peak_score), 0.0)
    totals = jnp.sum(cached_exp, axis=2, keepdims=True) + jnp.sum(fresh_exp, axis=2, keepdims=True)
    span_out = jnp.einsum(
        "rht,lt->rhl",
        (cached_exp / totals).astype(jnp.bfloat16),
        cache_slots[0, :key_width],
        preferred_element_type=jnp.float32,
    )
    span_out = span_out + jnp.einsum(
        "rhj,lj->rhl",
        (fresh_exp / totals).astype(jnp.bfloat16),
        fresh_keys[:key_width],
        preferred_element_type=jnp.float32,
    )
    decode_slots = jnp.arange(slot_count - 1, dtype=jnp.int32)
    decode_index = jnp.clip(span_rows + decode_slots, 0, row_count - 1)
    decode_query = jnp.take(query_rows, decode_index, axis=0)
    decode_keys = cache_slots[1:]
    own_keys = jnp.take(fresh_keys, decode_index, axis=1)
    slot_scores = (
        jnp.einsum("shl,slt->sht", decode_query, decode_keys, preferred_element_type=jnp.float32)
        * score_scale
    )
    slot_seen = (positions[None, :] < lengths[:, None])[:, None, :]
    slot_scores = jnp.where(slot_seen, slot_scores, masked_score)
    own_scores = (
        jnp.einsum("shl,ls->sh", decode_query, own_keys, preferred_element_type=jnp.float32)
        * score_scale
    )
    slot_peak = jnp.maximum(jnp.max(slot_scores, axis=2), own_scores)
    slot_exp = jnp.where(slot_seen, jnp.exp(slot_scores - slot_peak[:, :, None]), 0.0)
    own_exp = jnp.exp(own_scores - slot_peak)
    slot_totals = jnp.sum(slot_exp, axis=2) + own_exp
    decode_out = jnp.einsum(
        "sht,slt->shl",
        (slot_exp / slot_totals[:, :, None]).astype(jnp.bfloat16),
        decode_keys[:, :key_width],
        preferred_element_type=jnp.float32,
    )
    decode_out = (
        decode_out
        + rounded(own_exp / slot_totals)[:, :, None]
        * own_keys[:key_width].T.astype(jnp.float32)[:, None, :]
    )
    placing = (
        (local_rows[:, None] == span_rows + decode_slots[None, :])
        & (decode_slots[None, :] < decode_rows)
    ).astype(jnp.float32)
    latent_out = jnp.where((local_rows < span_rows)[:, None, None], span_out, 0.0)
    latent_out = latent_out + jnp.einsum("is,shl->ihl", placing, decode_out)
    return latent_out.astype(jnp.bfloat16)


def padded_term(hidden, down_weight):
    return jnp.dot(hidden, down_weight, preferred_element_type=jnp.float32)


def on_device(
    queries,
    latent_cache,
    new_latent,
    span_len,
    dec_count,
    span_start,
    cache_len,
    value_weight,
    out_weight,
    residual,
    norm_gain,
    gate_weight,
    up_weight,
    down_weight,
):
    rank_index = lax.axis_index("blk")
    rows_dev = residual.shape[0]
    heads_here = value_weight.shape[0]
    lives = span_len + dec_count
    query_rows = queries.reshape(rows_dev, heads_here, queries.shape[1] // heads_here)
    latent_out = local_attention(
        query_rows,
        latent_cache,
        new_latent,
        pick_rank(span_len, rank_index),
        pick_rank(dec_count, rank_index),
        span_start[0],
        cache_len[0],
        value_weight.shape[1],
    )
    head_values = jnp.einsum(
        "rhl,hlv->rhv", latent_out, value_weight, preferred_element_type=jnp.float32
    )
    head_values = head_values.astype(jnp.bfloat16).reshape(
        rows_dev, heads_here * value_weight.shape[2]
    )
    partial_out = jnp.dot(
        lax.all_gather(head_values, "blk", axis=0, tiled=True),
        out_weight,
        preferred_element_type=jnp.float32,
    )
    summed_out = lax.psum(partial_out.astype(jnp.bfloat16), "head").astype(jnp.float32)
    attended = lax.all_to_all(
        summed_out.astype(jnp.bfloat16), "blk", split_axis=0, concat_axis=1, tiled=True
    ).astype(summed_out.dtype)
    stream = residual.astype(jnp.float32) + attended
    scale_rows = lax.rsqrt(jnp.mean(stream * stream, axis=1, keepdims=True) + norm_eps)
    normed = (stream * scale_rows * norm_gain[None, :]).astype(jnp.bfloat16)
    head_index = lax.axis_index("head")
    half_rows = rows_dev // lax.axis_size("head")
    row_piece = lax.all_gather(normed, "blk", axis=0, tiled=True)
    gate_values = jnp.dot(row_piece, gate_weight, preferred_element_type=jnp.float32)
    up_values = jnp.dot(row_piece, up_weight, preferred_element_type=jnp.float32)
    hidden = (jax.nn.silu(gate_values) * up_values).astype(jnp.bfloat16)
    projected = lax.psum_scatter(
        padded_term(hidden, down_weight).astype(jnp.bfloat16),
        ("blk", "head"),
        scatter_dimension=0,
        tiled=True,
    ).astype(jnp.float32)
    own_rows = head_index * half_rows + jnp.arange(half_rows, dtype=jnp.int32)
    alive = own_rows < pick_rank(lives, rank_index)
    stream_half = lax.dynamic_slice_in_dim(stream, head_index * half_rows, half_rows, 0)
    return jnp.where(alive[:, None], stream_half + projected, 0.0).astype(jnp.bfloat16)


def solution(mesh):
    placed = (
        P(("groups", "blk"), "head"),
        P(("groups", "blk"), None, None),
        P(None, ("groups", "blk")),
        P("groups"),
        P("groups"),
        P(("groups", "blk")),
        P(("groups", "blk"), None),
        P("head", None, None),
        P("head", "blk"),
        P(("groups", "blk"), None),
        P(),
        P(None, ("blk", "head")),
        P(None, ("blk", "head")),
        P(("blk", "head"), None),
    )
    return jax.shard_map(
        on_device,
        mesh=mesh,
        in_specs=placed,
        out_specs=P(("groups", "blk", "head"), None),
        check_vma=False,
    )
```

profile of v0, /device:TPU:0, one launch (start us, length us, event | category | flops | bytes accessed | tf_op | source)
XLA Modules:
  0.0 421.8 jit_solution(16827265597548043617)
XLA Ops:
  6.5 0.0 all-gather.3.cloned.1.call-start
  6.5 1.4 select_reduce_fusion.2
  7.9 0.6 fusion.55
  8.5 0.6 iota_add_fusion
  9.1 0.6 iota_compare_fusion.5
  10.3 0.0 copy-start
  10.3 4.5 %reshape.113 = bf16[64,32,576]{2,1,0:T(8,128)(2,1)S(1)} reshape(bf16[64,18432]{1,0:T(8,128)(2,1)} %param.14) | data formatting | bytes 4718592 | tf_op jit(solution)/shard_map/reshape | solution.py:120
  14.9 0.0 copy-done
  14.9 0.6 gather_fusion.1
  15.5 0.6 gather_fusion
  16.1 0.0 copy-start.4
  16.1 0.9 fusion.61
  17.0 0.7 copy-done.4
  17.7 1.1 fusion.2
  18.8 0.7 fusion.22
  19.5 1.0 fusion.6
  20.5 0.0 copy-start.6
  20.5 0.8 divide_convert_fusion
  21.3 0.7 divide_convert_fusion.1
  22.0 1.3 compare_and_fusion
  23.3 0.0 copy-done.6
  23.3 0.1 iota_compare_fusion.2
  23.4 0.1 fusion.51
  23.5 0.3 fusion.34
  23.7 0.6 fusion.62
  24.3 0.2 fusion.33
  24.5 2.9 fusion.20
  27.4 2.7 fusion.26
  30.1 0.6 fusion.11
  30.7 6.3 %fusion.10 = bf16[32,8,8,128]{3,2,1,0:T(8,128)(2,1)S(1)} fusion(bf16[32,512,128]{2,1,0:T(8,128)(2,1)} %param.21, f32[64,32,512]{2,0,1:T(8,128)} %fusion.20, f32[64,32,512]{2,0,1:T(8,128)} %fusion.26, pred[64]{0:T(512)(128)(4,1)S(1)} %iota_compare_fusion.5, bf16[7,32,512]{2,1,0:T(8,128)(2,1)S(1)} %fusion.11, s32[7]{0:T(128)S(1)} %iota_add_fusion, ...), kind=kOutput, calls=%fused_computation.24 | convolution fusion | flops 287572864 | bytes 13336675 | tf_op jit(solution)/shard_map/rhl,hlv->rhv/dot_general | solution.py:131
  37.1 0.9 copy.50
  37.9 0.0 all-gather.3.cloned.1.call-update
  38.0 0.0 all-reduce.2.cloned.1.call-start
  38.0 76.2 %all-gather.3.cloned.1.call-done = bf16[512,4096]{1,0:T(8,128)(2,1)} async-done(((bf16[64,4096]{1,0:T(8,128)(2,1)}), bf16[512,4096]{1,0:T(8,128)(2,1)}) %all-gather.3.cloned.1.call-update) | async-done | bytes 4194320 | tf_op jit(solution)/shard_map/all_gather | solution.py:138
  114.2 9.8 %convolution_convert_fusion.1 = bf16[512,896]{1,0:T(8,128)(2,1)} fusion(bf16[512,4096]{1,0:T(8,128)(2,1)} %all-gather.3.cloned.1.call-done, bf16[4096,896]{1,0:T(8,128)(2,1)} %param.22), kind=kOutput, calls=%fused_computation.18 | convolution fusion | flops 3758555136 | bytes 12451840 | tf_op jit(solution)/shard_map/dot_general | solution.py:137
  124.0 0.0 all-reduce.2.cloned.1.call-update
  124.0 0.2 all-gather.5.cloned.1.call-start
  124.3 17.6 %all-reduce.2.cloned.1.call-done = bf16[8,64,896]{2,1,0:T(8,128)(2,1)} async-done(((bf16[8,64,896]{2,1,0:T(8,128)(2,1)}), bf16[8,64,896]{2,1,0:T(8,128)(2,1)}) %all-reduce.2.cloned.1.call-update) | async-done | bytes 917520 | tf_op jit(solution)/shard_map/psum | solution.py:142
  141.9 29.5 %all_to_all.13 = bf16[8,64,896]{2,1,0:T(8,128)(2,1)S(1)} all-to-all(bf16[8,64,896]{2,1,0:T(8,128)(2,1)} %all-reduce.2.cloned.1.call-done), channel_id=1, replica_groups=mesh['groups'=2,'blk'=8,'head'=2] {'blk'}, dimensions={0} | all-to-all | bytes 1835008 | tf_op jit(solution)/shard_map/all_to_all | solution.py:143
  171.4 0.1 convert_bitcast_fusion
  171.5 0.0 copy-start.3
  171.6 0.1 copy.24
  171.7 0.0 copy-start.5
  171.7 1.0 copy-done.3
  172.7 0.3 multiply_reduce_fusion
  173.1 0.0 copy-start.1
  173.1 1.2 copy-done.1
  174.3 0.0 copy-done.5
  174.3 1.2 multiply_convert_fusion
  175.5 0.0 all-gather.5.cloned.1.call-update
  175.5 0.0 reduce-scatter.2.cloned.1.call-start
  175.6 110.8 %all-gather.5.cloned.1.call-done = bf16[512,7168]{1,0:T(8,128)(2,1)} async-done(((bf16[64,7168]{1,0:T(8,128)(2,1)}), bf16[512,7168]{1,0:T(8,128)(2,1)}) %all-gather.5.cloned.1.call-update) | async-done | bytes 7340048 | tf_op jit(solution)/shard_map/all_gather | solution.py:151
  286.3 9.0 %fusion.63 = f32[512,576]{0,1:T(8,128)S(1)} fusion(bf16[512,7168]{1,0:T(8,128)(2,1)} %all-gather.5.cloned.1.call-done, bf16[7168,576]{0,1:T(8,128)(2,1)} %param.25), kind=kOutput, calls=%fused_computation.95 | convolution fusion | flops 4227858432 | bytes 16777216 | tf_op jit(solution)/shard_map/dot_general | solution.py:152
  295.4 27.8 %convolution_convert_fusion = bf16[512,7168]{1,0:T(8,128)(2,1)} fusion(bf16[576,7168]{1,0:T(8,128)(2,1)} %param.27, bf16[512,7168]{1,0:T(8,128)(2,1)} %all-gather.5.cloned.1.call-done, bf16[7168,576]{0,1:T(8,128)(2,1)} %param.26, f32[512,576]{0,1:T(8,128)S(1)} %fusion.63), kind=kOutput, calls=%fused_computation.2 | convolution fusion | flops 8461156352 | bytes 32374784 | tf_op jit(solution)/shard_map/dot_general | solution.py:97
  323.2 0.0 copy-start.2
  323.2 0.0 reduce-scatter.2.cloned.1.call-update
  323.2 0.7 add_compare_fusion
  323.9 89.4 %reduce-scatter.2.cloned.1.call-done = bf16[32,7168]{1,0:T(8,128)(2,1)} async-done(((bf16[512,7168]{1,0:T(8,128)(2,1)}), bf16[32,7168]{1,0:T(8,128)(2,1)}) %reduce-scatter.2.cloned.1.call-update) | async-done | bytes 458768 | tf_op jit(solution)/shard_map/reduce_scatter | solution.py:155
  413.3 0.0 copy-done.2
  413.3 1.9 select_convert_fusion
  (10 shorter events, 0.1 us)
Async XLA Ops:
  6.5 107.7 %all-gather.3.cloned.1.call-start = ((), (), s32[]{:S(2)}) async-start(), calls=%async_computation.2 | async-start | bytes 4718592 | tf_op jit(solution)/shard_map/all_gather | solution.py:138
  10.3 4.5 %copy-start = (bf16[576,64]{0,1:T(8,128)(2,1)S(1)}, bf16[576,64]{0,1:T(8,128)(2,1)}, u32[]{:S(2)}) copy-start(bf16[576,64]{0,1:T(8,128)(2,1)} %param.16) | copy-start | bytes 221188
  16.1 1.7 copy-start.4
  20.5 2.8 copy-start.6
  38.0 103.9 %all-reduce.2.cloned.1.call-start = ((), (), s32[]{:S(2)}) async-start(), calls=%async_computation.3 | async-start | bytes 1835008 | tf_op jit(solution)/shard_map/psum | solution.py:142
  124.0 162.3 %all-gather.5.cloned.1.call-start = ((), (), s32[]{:S(2)}) async-start(), calls=%async_computation.4 | async-start | bytes 8257536 | tf_op jit(solution)/shard_map/all_gather | solution.py:151
  171.5 1.2 copy-start.3
  171.7 2.6 copy-start.5
  173.1 1.3 copy-start.1
  175.5 237.8 %reduce-scatter.2.cloned.1.call-start = ((), (), s32[]{:S(2)}) async-start(), calls=%async_computation.5 | async-start | bytes 7798784 | tf_op jit(solution)/shard_map/reduce_scatter | solution.py:155
  323.2 90.1 %copy-start.2 = (f32[64,7168]{1,0:T(8,128)S(1)}, f32[64,7168]{1,0:T(8,128)}, u32[]{:S(2)}) copy-start(f32[64,7168]{1,0:T(8,128)} %copy-done.1) | copy-start | bytes 5505028
Sparse Core Ops, SparseCore 0:
  38.1 76.0 all-gather.2
  124.2 17.6 all-reduce.1
  175.6 110.6 all-gather.4
  323.3 89.9 reduce-scatter.1
where the time goes:
time: 422 us
  waiting for transfers between devices  294 us (70%)
  matrix products  62 us (15%)
  blocking collectives  29.5 us (7%)
  between operations  14 us (3%)
  other arithmetic  12.1 us (3%)
  local copies, waits for them, and re-layouts  9.72 us (2%)
    all_gather x1, waiting for transfers between devices, on_device(): row_piece = lax.all_gather(normed, 'blk', axis=0, tiled=True)  111 us
    reduce_scatter x1, waiting for transfers between devices, on_device(): lax.psum_scatter(padded_term(hidden, down_weight).astype(jnp.bfloat16), (...  89.4 us
    all_gather x1, waiting for transfers between devices, on_device(): lax.all_gather(head_values, 'blk', axis=0, tiled=True)  76.2 us
    all_to_all x1, blocking collectives, on_device(): lax.all_to_all(summed_out.astype(jnp.bfloat16), 'blk', split_axis=0, conc...  29.5 us
    dot_general x1, matrix products, padded_term(): return jnp.dot(hidden, down_weight, preferred_element_type=jnp.float32)  27.8 us
    psum x1, waiting for transfers between devices, on_device(): lax.psum(partial_out.astype(jnp.bfloat16), 'head').astype(jnp.float32)  17.6 us
    dot_general x1, matrix products, on_device(): jnp.dot(lax.all_gather(head_values, 'blk', axis=0, tiled=True), out_weigh...  9.78 us
    dot_general x1, matrix products, on_device(): jnp.dot(row_piece, gate_weight, preferred_element_type=jnp.float32)  9.03 us
  transfers between devices with their start and end apart: 4, of which 4 were waited for; matrix products, arithmetic and copies ran while one was open for 0% of the time, Pallas kernels for 0%

commit v1 on v0

--- a/solution.py
+++ b/solution.py
@@ -15,6 +15,23 @@
 def pick_rank(values, rank_index):
     matches = jnp.arange(values.shape[0], dtype=jnp.int32) == rank_index
     return jnp.sum(jnp.where(matches, values, 0))
+
+
+def ring_order(mesh):
+    count = mesh.shape["blk"]
+    natural = list(range(count))
+    snake = natural[0::2] + natural[1::2][::-1]
+    names = list(mesh.axis_names)
+    lane = mesh.devices.transpose([names.index("blk")] + [a for a, x in enumerate(names) if x != "blk"])
+    firsts = [lane[i].reshape(-1)[0] for i in natural]
+    if not all(hasattr(d, "coords") for d in firsts):
+        return snake
+
+    def length(order):
+        hops = zip(order, order[1:] + order[:1])
+        return sum(sum(abs(u - v) for u, v in zip(firsts[a].coords, firsts[b].coords)) for a, b in hops)
+
+    return natural if length(natural) <= length(snake) else snake
 
 
 def local_attention(
@@ -93,11 +110,8 @@
     return latent_out.astype(jnp.bfloat16)
 
 
-def padded_term(hidden, down_weight):
-    return jnp.dot(hidden, down_weight, preferred_element_type=jnp.float32)
-
-
 def on_device(
+    order,
     queries,
     latent_cache,
     new_latent,
@@ -113,55 +127,197 @@
     up_weight,
     down_weight,
 ):
-    rank_index = lax.axis_index("blk")
-    rows_dev = residual.shape[0]
+    f32, bf16 = jnp.float32, jnp.bfloat16
+    ranks = len(order)
+    reach = ranks // 2
+    rank = lax.axis_index("blk")
+    core = lax.axis_index("head")
+    cores = lax.axis_size("head")
+    rows_dev, width = residual.shape
+    block = rows_dev // 2
+    half = block // cores
+    nodes = ranks + 1
+    features = out_weight.shape[1]
+    lives = span_len + dec_count
+    at = jnp.asarray([order.index(i) for i in range(ranks)], jnp.int32)
+    who = jnp.asarray(order, jnp.int32)
+    busy_rank = jnp.argmax(lives).astype(jnp.int32)
+    place = at[rank]
+    busy_place = at[busy_rank]
+    busy = rank == busy_rank
+
+    forward = [(order[i], order[(i + 1) % ranks]) for i in range(ranks)]
+    backward = [(b, a) for a, b in forward]
+    exchange = [(c, cores - 1 - c) for c in range(cores)]
+
+    def send_next(x):
+        return lax.ppermute(x, "blk", forward)
+
+    def send_prev(x):
+        return lax.ppermute(x, "blk", backward)
+
+    def swap(x):
+        return lax.ppermute(x, "head", exchange)
+
+    def node_ahead(k):
+        e = (busy_place - place) % ranks
+        far = (e > 0) & (k > e + 1)
+        slot = who[(place + k - far.astype(jnp.int32)) % ranks]
+        return jnp.where((e > 0) & (k == e + 1), ranks, slot)
+
+    def node_behind(k):
+        e = (place - busy_place) % ranks
+        far = (e > 0) & (k > e)
+        slot = who[(place - k + far.astype(jnp.int32)) % ranks]
+        return jnp.where((e > 0) & (k == e), ranks, slot)
+
+    res_halves = lax.dynamic_slice_in_dim(
+        residual.reshape(2, cores, half, width), core, 1, 1
+    ).reshape(2, half, width)
+
+    def res_for(target):
+        return lax.dynamic_slice_in_dim(res_halves, target * features, features, 2)
+
+    res_parts = [res_for(rank)]
+    for shift in range(1, ranks):
+        res_parts.append(
+            lax.ppermute(
+                res_for((rank + shift) % ranks),
+                "blk",
+                [(i, (i + shift) % ranks) for i in range(ranks)],
+            )
+        )
+
     heads_here = value_weight.shape[0]
-    lives = span_len + dec_count
     query_rows = queries.reshape(rows_dev, heads_here, queries.shape[1] // heads_here)
     latent_out = local_attention(
         query_rows,
         latent_cache,
         new_latent,
-        pick_rank(span_len, rank_index),
-        pick_rank(dec_count, rank_index),
+        pick_rank(span_len, rank),
+        pick_rank(dec_count, rank),
         span_start[0],
         cache_len[0],
         value_weight.shape[1],
     )
-    head_values = jnp.einsum(
-        "rhl,hlv->rhv", latent_out, value_weight, preferred_element_type=jnp.float32
-    )
-    head_values = head_values.astype(jnp.bfloat16).reshape(
-        rows_dev, heads_here * value_weight.shape[2]
-    )
-    partial_out = jnp.dot(
-        lax.all_gather(head_values, "blk", axis=0, tiled=True),
-        out_weight,
-        preferred_element_type=jnp.float32,
-    )
-    summed_out = lax.psum(partial_out.astype(jnp.bfloat16), "head").astype(jnp.float32)
-    attended = lax.all_to_all(
-        summed_out.astype(jnp.bfloat16), "blk", split_axis=0, concat_axis=1, tiled=True
-    ).astype(summed_out.dtype)
-    stream = residual.astype(jnp.float32) + attended
-    scale_rows = lax.rsqrt(jnp.mean(stream * stream, axis=1, keepdims=True) + norm_eps)
-    normed = (stream * scale_rows * norm_gain[None, :]).astype(jnp.bfloat16)
-    head_index = lax.axis_index("head")
-    half_rows = rows_dev // lax.axis_size("head")
-    row_piece = lax.all_gather(normed, "blk", axis=0, tiled=True)
-    gate_values = jnp.dot(row_piece, gate_weight, preferred_element_type=jnp.float32)
-    up_values = jnp.dot(row_piece, up_weight, preferred_element_type=jnp.float32)
-    hidden = (jax.nn.silu(gate_values) * up_values).astype(jnp.bfloat16)
-    projected = lax.psum_scatter(
-        padded_term(hidden, down_weight).astype(jnp.bfloat16),
-        ("blk", "head"),
-        scatter_dimension=0,
-        tiled=True,
-    ).astype(jnp.float32)
-    own_rows = head_index * half_rows + jnp.arange(half_rows, dtype=jnp.int32)
-    alive = own_rows < pick_rank(lives, rank_index)
-    stream_half = lax.dynamic_slice_in_dim(stream, head_index * half_rows, half_rows, 0)
-    return jnp.where(alive[:, None], stream_half + projected, 0.0).astype(jnp.bfloat16)
+    head_values = jnp.einsum("rhl,hlv->rhv", latent_out, value_weight, preferred_element_type=f32)
+    head_values = head_values.astype(bf16).reshape(rows_dev, heads_here * value_weight.shape[2])
+
+    main, extra = head_values[:block], head_values[block:]
+    from_behind, from_ahead = [], []
+    for step in range(reach):
+        if step == 0:
+            out_f, out_b = jnp.where(busy, extra, main), main
+        elif step == 1:
+            out_f = jnp.where(busy, main, from_behind[0])
+            out_b = jnp.where(busy, extra, from_ahead[0])
+        else:
+            out_f = jnp.where(busy, from_behind[step - 2], from_behind[step - 1])
+            out_b = jnp.where(busy, from_ahead[step - 2], from_ahead[step - 1])
+        from_behind.append(send_next(out_f))
+        from_ahead.append(send_prev(out_b))
+    blocks = [main] + from_behind + from_ahead[:-1] + [jnp.where(busy, extra, from_ahead[-1])]
+    slots = [rank] + [node_behind(k + 1) for k in range(reach)]
+    slots += [node_ahead(k + 1) for k in range(reach - 1)]
+    slots += [jnp.where(busy, ranks, node_ahead(reach))]
+    slots = jnp.stack(slots)
+    sources = jnp.argmax(slots[None, :] == jnp.arange(nodes)[:, None], axis=1)
+
+    partial_out = jnp.dot(jnp.concatenate(blocks, 0), out_weight, preferred_element_type=f32)
+    partial_out = jnp.take(partial_out.reshape(nodes, cores, half, features), sources, axis=0)
+    first, second = partial_out[:, 0], partial_out[:, 1]
+    kept = jnp.where(core == 0, first, second)
+    given = jnp.where(core == 0, second, first).astype(bf16)
+    res_all = jnp.stack(res_parts)
+    res_main = jnp.take(res_all[:, 0], (rank - jnp.arange(ranks)) % ranks, axis=0)
+    res_extra = lax.dynamic_index_in_dim(res_all[:, 1], (rank - busy_rank) % ranks, 0)
+    res_here = jnp.concatenate([res_main, res_extra], 0).astype(f32)
+    stream = (kept + swap(given).astype(f32) + res_here).astype(bf16).reshape(nodes * half, features)
+
+    gain_blocks = norm_gain.reshape(ranks, features)
+
+    def chunk(mine, owner):
+        both = jnp.concatenate([mine, swap(mine)], 0).astype(f32)
+        squares = jnp.sum(both * both, axis=1, keepdims=True)
+        scaled = (both * gain_blocks[owner][None, :]).astype(bf16)
+        gate_part = lax.dynamic_slice_in_dim(gate_weight, owner * features, features, 0)
+        up_part = lax.dynamic_slice_in_dim(up_weight, owner * features, features, 0)
+        return (
+            squares,
+            jnp.dot(scaled, gate_part, preferred_element_type=f32),
+            jnp.dot(scaled, up_part, preferred_element_type=f32),
+        )
+
+    held = [(stream, rank)]
+    ahead, behind = stream, stream
+    for step in range(1, reach + 1):
+        ahead = send_next(ahead)
+        held.append((ahead, who[(place - step) % ranks]))
+        if step < reach:
+            behind = send_prev(behind)
+            held.append((behind, who[(place + step) % ranks]))
+    sums = chunk(*held[0])
+    for piece in held[1:]:
+        sums = tuple(a + b for a, b in zip(sums, chunk(*piece)))
+    squares, gate_values, up_values = sums
+    scale_rows = lax.rsqrt(squares / width + norm_eps)
+    hidden = (jax.nn.silu(gate_values * scale_rows) * (up_values * scale_rows)).astype(bf16)
+
+    own_parts = jnp.stack(
+        [
+            jnp.stack(
+                [
+                    lax.dynamic_slice_in_dim(piece, rank * half, half, 0),
+                    piece[ranks * half :],
+                ]
+            )
+            for piece, _ in held
+        ]
+    )
+    owners = jnp.stack([owner for _, owner in held])
+    arrival = jnp.argmax(owners[None, :] == jnp.arange(ranks)[:, None], axis=1)
+    own_stream = jnp.take(own_parts, arrival, axis=0)
+    own_stream = own_stream.transpose(1, 2, 0, 3).reshape(2, half, width).astype(f32)
+
+    rows_here = nodes * half
+    other = jnp.dot(hidden[rows_here:], down_weight, preferred_element_type=f32).astype(bf16)
+    theirs = swap(other).reshape(nodes, half, width)
+    mine = jnp.dot(hidden[:rows_here], down_weight, preferred_element_type=f32).astype(bf16)
+    mine = mine.reshape(nodes, half, width)
+
+    def share(slot):
+        a = lax.dynamic_index_in_dim(mine, slot, 0, keepdims=False).astype(f32)
+        b = lax.dynamic_index_in_dim(theirs, slot, 0, keepdims=False).astype(f32)
+        return a + b
+
+    got_f, got_b = [], []
+    for step in range(1, reach + 1):
+        add_f = share(node_ahead(reach + 1 - step))
+        add_b = share(node_behind(reach + 1 - step))
+        if step == 1:
+            add_f = jnp.where(busy, 0.0, add_f)
+        elif step == 2:
+            add_f = add_f + jnp.where(busy, 0.0, got_f[0].astype(f32))
+            add_b = add_b + jnp.where(busy, 0.0, got_b[0].astype(f32))
+        else:
+            add_f = add_f + jnp.where(busy, got_f[step - 3], got_f[step - 2]).astype(f32)
+            add_b = add_b + jnp.where(busy, got_b[step - 3], got_b[step - 2]).astype(f32)
+        got_f.append(send_next(add_f.astype(bf16)))
+        got_b.append(send_prev(add_b.astype(bf16)))
+    main_sum = share(rank) + got_f[-1].astype(f32)
+    main_sum = main_sum + jnp.where(busy, got_b[-2], got_b[-1]).astype(f32)
+    extra_sum = share(jnp.int32(ranks)) + got_f[-2].astype(f32) + got_b[-1].astype(f32)
+
+    main_out = (own_stream[0] + main_sum).astype(bf16)
+    extra_out = (own_stream[1] + extra_sum).astype(bf16)
+    kept_out = jnp.where(core == 0, main_out, extra_out)
+    swapped = swap(jnp.where(core == 0, extra_out, main_out))
+    low = jnp.where(core == 0, kept_out, swapped)
+    high = jnp.where(core == 0, swapped, kept_out)
+    result = jnp.concatenate([low, high], 0)
+    own_rows = core * block + jnp.arange(block, dtype=jnp.int32)
+    alive = own_rows < pick_rank(lives, rank)
+    return jnp.where(alive[:, None], result, jnp.zeros_like(result))
 
 
 def solution(mesh):
@@ -181,8 +337,9 @@
         P(None, ("blk", "head")),
         P(("blk", "head"), None),
     )
+    order = ring_order(mesh)
     return jax.shard_map(
-        on_device,
+        lambda *args: on_device(order, *args),
         mesh=mesh,
         in_specs=placed,
         out_specs=P(("groups", "blk", "head"), None),

time: 422 us -> 244 us (0.58)
  waiting for transfers between devices: 294 us -> 68.4 us
  starting transfers between devices: 0.31 us -> 37.1 us
  blocking collectives: 29.5 us -> 0 us
  between operations: 14 us -> 35.1 us
  other arithmetic: 12.1 us -> 32.7 us
  matrix products: 62 us -> 49 us
  local copies, waits for them, and re-layouts: 9.72 us -> 20.4 us
    all_gather x2 -> x0, waiting for transfers between devices: 187 us -> none  [the longest x1 111 us: on_device(): row_piece = lax.all_gather(normed, 'blk', axis=0, tiled=True)]
    reduce_scatter x1 -> x0, waiting for transfers between devices: 89.4 us -> none  [on_device(): lax.psum_scatter(padded_term(hidden, down_weight).astype(jnp.bfloat16), (...]
    ppermute x0 -> x41, waiting for transfers between devices: none -> 68.4 us  [the longest x12 30.2 us: send_next(): return lax.ppermute(x, 'blk', forward)]
    ppermute x0 -> x41, starting transfers between devices: none -> 37.1 us  [the longest x12 16.1 us: send_next(): return lax.ppermute(x, 'blk', forward)]
    all_to_all x1 -> x0, blocking collectives: 29.5 us -> none  [on_device(): lax.all_to_all(summed_out.astype(jnp.bfloat16), 'blk', split_axis=0, conc...]
    psum x1 -> x0, waiting for transfers between devices: 17.6 us -> none  [on_device(): lax.psum(partial_out.astype(jnp.bfloat16), 'head').astype(jnp.float32)]
    dot_general x3 -> x19, matrix products: 46.6 us -> 33.1 us  [the longest x8 10.6 us: chunk(): jnp.dot(scaled, up_part, preferred_element_type=f32)]
    select_n x0 -> x14, other arithmetic: none -> 7.21 us  [the longest x2 1.53 us: on_device(): out_b = jnp.where(busy, from_ahead[step - 2], from_ahead[step - 1])]
  transfers between devices with their start and end apart: 4 -> 41, of which waited for: 4 -> 21; matrix products, arithmetic and copies ran while one was open for 0% -> 19% of each run, Pallas kernels for 0% -> 0%
where the time goes in v1:
time: 244 us; the launch traced here: 243 us
  waiting for transfers between devices  68.4 us (28%)
  matrix products  49 us (20%)
  starting transfers between devices  37.1 us (15%)
  between operations  35.1 us (14%)
  other arithmetic  32.7 us (13%)
  local copies, waits for them, and re-layouts  20.4 us (8%)
    ppermute x12, waiting for transfers between devices, send_next(): return lax.ppermute(x, 'blk', forward)  30.2 us
    ppermute x11, waiting for transfers between devices, send_prev(): return lax.ppermute(x, 'blk', backward)  24.4 us
    ppermute x12, starting transfers between devices, send_next(): return lax.ppermute(x, 'blk', forward)  16.1 us
    ppermute x7, waiting for transfers between devices, on_device(): lax.ppermute(res_for((rank + shift) % ranks), 'blk', [(i, (i + shift) % r...  12.1 us
    dot_general x8, matrix products, chunk(): jnp.dot(scaled, up_part, preferred_element_type=f32)  10.6 us
    ppermute x7, starting transfers between devices, on_device(): lax.ppermute(res_for((rank + shift) % ranks), 'blk', [(i, (i + shift) % r...  10.1 us
    ppermute x11, starting transfers between devices, send_prev(): return lax.ppermute(x, 'blk', backward)  9.32 us
    dot_general x8, matrix products, chunk(): jnp.dot(scaled, gate_part, preferred_element_type=f32)  7.97 us
  transfers between devices with their start and end apart: 41, of which 21 were waited for; matrix products, arithmetic and copies ran while one was open for 19% of the time, Pallas kernels for 0%

profile of v1, /device:TPU:0, one launch (start us, length us, event | category | flops | bytes accessed | tf_op | source)
XLA Modules:
  0.0 242.7 jit_solution(16852601404834086214)
XLA Ops:
  0.0 1.3 iota_reduce_fusion.2
  3.6 1.3 fusion.185
  12.9 1.4 select_reduce_fusion.2
  16.8 2.0 fusion.184
  24.5 4.5 %reshape.297 = bf16[64,32,576]{2,1,0:T(8,128)(2,1)S(1)} reshape(bf16[64,18432]{1,0:T(8,128)(2,1)} %param.16) | data formatting | bytes 4718592 | tf_op jit(solution)/shard_map/reshape | solution.py:192
  30.3 0.9 fusion.186
  31.9 1.1 fusion.2
  33.7 1.0 fusion.6
  36.2 1.3 compare_and_fusion.1
  38.7 2.9 %fusion.23 = f32[64,32,512]{2,0,1:T(8,128)} fusion(bf16[64,32,256]{2,1,0:T(8,128)(2,1)S(1)} %divide_convert_fusion, bf16[8,576,256]{2,1,0:T(8,128)(2,1)S(1)} %copy-done.2), kind=kOutput, calls=%fused_computation.59 | convolution fusion | flops 536870912 | bytes 5505024 | tf_op jit(solution)/shard_map/rht,lt->rhl/dot_general | solution.py:62
  41.6 2.7 %fusion.62 = f32[64,32,512]{2,0,1:T(8,128)} fusion(bf16[64,32,64]{2,1,0:T(8,128)(2,1)S(1)} %divide_convert_fusion.1, bf16[576,64]{0,1:T(8,128)(2,1)S(1)} %copy-done), kind=kOutput, calls=%fused_computation.100 | convolution fusion | flops 134217728 | bytes 4784128 | tf_op jit(solution)/shard_map/rhj,lj->rhl/dot_general | solution.py:68
  44.9 6.9 %fusion.13 = bf16[64,32,128]{2,0,1:T(8,128)(2,1)S(1)} fusion(bf16[32,512,128]{2,1,0:T(8,128)(2,1)} %param.23, f32[64,32,512]{2,0,1:T(8,128)} %fusion.23, f32[64,32,512]{2,0,1:T(8,128)} %fusion.62, pred[64]{0:T(512)(128)(4,1)S(1)} %iota_compare_fusion.7, bf16[7,32,512]{2,1,0:T(8,128)(2,1)S(1)} %fusion.14, s32[7]{0:T(128)S(1)} %iota_add_fusion, ...), kind=kOutput, calls=%fused_computation.55 | convolution fusion | flops 287572864 | bytes 13336675 | tf_op jit(solution)/shard_map/rhl,hlv->rhv/dot_general | solution.py:203
  51.8 3.0 %collective-permute-start.4 = (bf16[32,4096]{1,0:T(8,128)(2,1)S(1)}, bf16[32,4096]{1,0:T(8,128)(2,1)S(1)}, u32[]{:S(2)}, u32[]{:S(2)}) collective-permute-start(bf16[32,4096]{1,0:T(8,128)(2,1)S(1)} %bitcast.314), channel_id=1, source_target_pairs={{4,0},{8,4},{12,8},{14,12},{10,14},{6,10},{2,6},{0,2},{5,1},{9,5},... | collective-permute-start | bytes 786440 | tf_op jit(solution)/shard_map/ppermute | solution.py:157
  55.1 3.6 %collective-permute-start.15 = (bf16[2,16,896]{2,1,0:T(8,128)(2,1)S(1)}, bf16[2,16,896]{2,1,0:T(8,128)(2,1)S(1)}, u32[]{:S(2)}, u32[]{:S(2)}) collective-permute-start(bf16[2,16,896]{2,1,0:T(8,128)(2,1)S(1)} %get-tuple-element.33), channel_id=1, source_target_pairs={{0,14},{2,0},{4,2},{6,4},{8,6},{10,8},{12,10},{14,12},{1,15},{3,1}... | collective-permute-start | bytes 172040 | tf_op jit(solution)/shard_map/ppermute | solution.py:184
  58.6 1.5 collective-permute-start.14
  60.9 1.1 collective-permute-done.4
  62.9 2.1 collective-permute-start
  64.9 5.2 %collective-permute-done = bf16[32,4096]{1,0:T(8,128)(2,1)S(1)} collective-permute-done((bf16[32,4096]{1,0:T(8,128)(2,1)S(1)}, bf16[32,4096]{1,0:T(8,128)(2,1)S(1)}, u32[]{:S(2)}, u32[]{:S(2)}) %collective-permute-start) | collective-permute-done | bytes 262176 | tf_op jit(solution)/shard_map/ppermute | solution.py:154
  70.9 1.8 collective-permute-start.1
  73.3 4.5 %stack.159 = s32[8]{0:T(128)S(1)} concatenate(s32[1]{0:T(128)} %bitcast, s32[1]{0:T(128)} %get-tuple-element.89, s32[1]{0:T(128)} %get-tuple-element.88, s32[1]{0:T(128)} %get-tuple-element.87, s32[1]{0:T(128)} %get-tuple-element.86, s32[1]{0:T(128)} %get-tuple-element.85, s32[1]{0:T(128)} %get-tuple-element.84, s32[1]{0:T(128)} %get-tuple-element.77), dimensions={0} | concatenate | bytes 64 | tf_op jit(solution)/shard_map/stack | solution.py:277
  78.5 1.7 collective-permute-start.9
  80.9 6.8 %collective-permute-done.9 = bf16[2,16,896]{2,1,0:T(8,128)(2,1)S(1)} collective-permute-done((bf16[2,16,896]{2,1,0:T(8,128)(2,1)S(1)}, bf16[2,16,896]{2,1,0:T(8,128)(2,1)S(1)}, u32[]{:S(2)}, u32[]{:S(2)}) %collective-permute-start.9) | collective-permute-done | bytes 57376 | tf_op jit(solution)/shard_map/ppermute | solution.py:184
  87.7 2.7 %collective-permute-start.12 = (bf16[2,16,896]{2,1,0:T(8,128)(2,1)S(1)}, bf16[2,16,896]{2,1,0:T(8,128)(2,1)S(1)}, u32[]{:S(2)}, u32[]{:S(2)}) collective-permute-start(bf16[2,16,896]{2,1,0:T(8,128)(2,1)S(1)} %get-tuple-element.36), channel_id=1, source_target_pairs={{0,8},{2,10},{4,12},{6,14},{8,0},{10,2},{12,4},{14,6},{1,9},{3,11}... | collective-permute-start | bytes 172040 | tf_op jit(solution)/shard_map/ppermute | solution.py:184
  90.4 4.3 %collective-permute-done.2 = bf16[32,4096]{1,0:T(8,128)(2,1)S(1)} collective-permute-done((bf16[32,4096]{1,0:T(8,128)(2,1)S(1)}, bf16[32,4096]{1,0:T(8,128)(2,1)S(1)}, u32[]{:S(2)}, u32[]{:S(2)}) %collective-permute-start.2) | collective-permute-done | bytes 262176 | tf_op jit(solution)/shard_map/ppermute | solution.py:154
  95.5 5.3 %collective-permute-done.11 = bf16[2,16,896]{2,1,0:T(8,128)(2,1)S(1)} collective-permute-done((bf16[2,16,896]{2,1,0:T(8,128)(2,1)S(1)}, bf16[2,16,896]{2,1,0:T(8,128)(2,1)S(1)}, u32[]{:S(2)}, u32[]{:S(2)}) %collective-permute-start.11) | collective-permute-done | bytes 57376 | tf_op jit(solution)/shard_map/ppermute | solution.py:184
  100.8 2.1 collective-permute-start.5
  102.9 4.3 %collective-permute-done.3 = bf16[32,4096]{1,0:T(8,128)(2,1)S(1)} collective-permute-done((bf16[32,4096]{1,0:T(8,128)(2,1)S(1)}, bf16[32,4096]{1,0:T(8,128)(2,1)S(1)}, u32[]{:S(2)}, u32[]{:S(2)}) %collective-permute-start.3) | collective-permute-done | bytes 262176 | tf_op jit(solution)/shard_map/ppermute | solution.py:154
  110.2 1.0 collective-permute-start.6
  111.2 6.5 %collective-permute-done.6 = bf16[32,4096]{1,0:T(8,128)(2,1)S(1)} collective-permute-done((bf16[32,4096]{1,0:T(8,128)(2,1)S(1)}, bf16[32,4096]{1,0:T(8,128)(2,1)S(1)}, u32[]{:S(2)}, u32[]{:S(2)}) %collective-permute-start.6) | collective-permute-done | bytes 262176 | tf_op jit(solution)/shard_map/ppermute | solution.py:157
  118.8 6.0 %collective-permute-done.7 = bf16[32,4096]{1,0:T(8,128)(2,1)S(1)} collective-permute-done((bf16[32,4096]{1,0:T(8,128)(2,1)S(1)}, bf16[32,4096]{1,0:T(8,128)(2,1)S(1)}, u32[]{:S(2)}, u32[]{:S(2)}) %collective-permute-start.7) | collective-permute-done | bytes 262176 | tf_op jit(solution)/shard_map/ppermute | solution.py:157
  125.6 6.4 %fusion.188 = f32[288,896]{1,0:T(8,128)S(1)} fusion(bf16[288,4096]{1,0:T(8,128)(2,1)} %fusion.96, bf16[4096,896]{1,0:T(8,128)(2,1)} %param.24), kind=kOutput, calls=%fused_computation.345 | convolution fusion | flops 2113929216 | bytes 10731520 | tf_op jit(solution)/shard_map/dot_general | solution.py:226
  135.1 1.7 collective-permute-start.16
  155.3 1.7 collective-permute-start.18
  157.3 2.0 fusion.48
  159.3 1.9 fusion.57
  161.2 2.2 collective-permute-done.19
  163.9 1.7 collective-permute-start.20
  166.1 2.0 convolution_add_fusion.6
  168.2 2.0 convolution_add_fusion.13
  170.2 1.9 convolution_add_fusion.5
  172.9 1.2 collective-permute-start.22
  174.8 1.9 convolution_add_fusion.4
  179.1 2.4 collective-permute-done.22
  186.8 3.1 %convolution_convert_fusion = bf16[144,7168]{1,0:T(8,128)(2,1)} fusion(bf16[576,7168]{1,0:T(8,128)(2,1)S(1)} %bitcast.291, bf16[288,576]{1,0:T(8,128)(2,1)S(1)} %fusion.12), kind=kOutput, calls=%fused_computation.5 | convolution fusion | flops 1190117376 | bytes 10506240 | tf_op jit(solution)/shard_map/dot_general | solution.py:283
  192.9 5.1 %convolution_convert_fusion.1 = bf16[144,7168]{1,0:T(8,128)(2,1)S(1)} fusion(bf16[576,7168]{1,0:T(8,128)(2,1)} %param.29, bf16[288,576]{1,0:T(8,128)(2,1)S(1)} %fusion.12), kind=kOutput, calls=%fused_computation.6 | convolution fusion | flops 1190117376 | bytes 10506240 | tf_op jit(solution)/shard_map/dot_general | solution.py:285
  198.1 1.2 fusion.100
  199.3 1.3 collective-permute-start.32
  202.0 4.9 %collective-permute-done.32 = bf16[16,7168]{1,0:T(8,128)(2,1)S(1)} collective-permute-done((bf16[16,7168]{1,0:T(8,128)(2,1)S(1)}, bf16[16,7168]{1,0:T(8,128)(2,1)S(1)}, u32[]{:S(2)}, u32[]{:S(2)}) %collective-permute-start.32) | collective-permute-done | bytes 229408 | tf_op jit(solution)/shard_map/ppermute | solution.py:154
  206.9 1.0 fusion.72
  207.9 1.3 collective-permute-start.33
  210.5 4.2 %collective-permute-done.33 = bf16[16,7168]{1,0:T(8,128)(2,1)S(1)} collective-permute-done((bf16[16,7168]{1,0:T(8,128)(2,1)S(1)}, bf16[16,7168]{1,0:T(8,128)(2,1)S(1)}, u32[]{:S(2)}, u32[]{:S(2)}) %collective-permute-start.33) | collective-permute-done | bytes 229408 | tf_op jit(solution)/shard_map/ppermute | solution.py:154
  214.7 2.1 fusion.71
  217.7 1.6 gather_fusion.4
  219.3 1.8 collective-permute-start.34
  221.2 1.9 collective-permute-done.37
  223.0 1.1 fusion.70
  224.5 1.1 collective-permute-done.34
  225.6 4.6 %collective-permute-done.38 = bf16[16,7168]{1,0:T(8,128)(2,1)S(1)} collective-permute-done((bf16[16,7168]{1,0:T(8,128)(2,1)S(1)}, bf16[16,7168]{1,0:T(8,128)(2,1)S(1)}, u32[]{:S(2)}, u32[]{:S(2)}) %collective-permute-start.38) | collective-permute-done | bytes 229408 | tf_op jit(solution)/shard_map/ppermute | solution.py:157
  230.2 1.3 fusion.73
  231.4 1.3 collective-permute-start.35
  233.7 3.8 %collective-permute-done.35 = bf16[16,7168]{1,0:T(8,128)(2,1)S(1)} collective-permute-done((bf16[16,7168]{1,0:T(8,128)(2,1)S(1)}, bf16[16,7168]{1,0:T(8,128)(2,1)S(1)}, u32[]{:S(2)}, u32[]{:S(2)}) %collective-permute-start.35) | collective-permute-done | bytes 229408 | tf_op jit(solution)/shard_map/ppermute | solution.py:154
  237.5 1.3 collective-permute-done.39
  238.8 1.4 broadcast_select_fusion.10
  241.7 0.9 maximum_select_fusion
  (179 shorter events, 41.6 us)
Async XLA Ops:
  24.5 4.6 %copy-start = (bf16[576,64]{0,1:T(8,128)(2,1)S(1)}, bf16[576,64]{0,1:T(8,128)(2,1)}, u32[]{:S(2)}) copy-start(bf16[576,64]{0,1:T(8,128)(2,1)} %param.18) | copy-start | bytes 221188
  30.2 1.7 copy-start.2
  34.6 2.8 %copy-start.4 = (s32[1,7]{1,0:T(1,128)S(1)}, s32[1,7]{1,0:T(1,128)}, u32[]{:S(2)}) copy-start(s32[1,7]{1,0:T(1,128)} %param.22) | copy-start | bytes 88
  44.9 10.0 %copy-start.1 = (bf16[64,7168]{1,0:T(8,128)(2,1)S(1)}, bf16[64,7168]{1,0:T(8,128)(2,1)}, u32[]{:S(2)}) copy-start(bf16[64,7168]{1,0:T(8,128)(2,1)} %param.25) | copy-start | bytes 2752516
  51.8 10.2 %collective-permute-start.4 = (bf16[32,4096]{1,0:T(8,128)(2,1)S(1)}, bf16[32,4096]{1,0:T(8,128)(2,1)S(1)}, u32[]{:S(2)}, u32[]{:S(2)}) collective-permute-start(bf16[32,4096]{1,0:T(8,128)(2,1)S(1)} %bitcast.314), channel_id=1, source_target_pairs={{4,0},{8,4},{12,8},{14,12},{10,14},{6,10},{2,6},{0,2},{5,1},{9,5},... | collective-permute-start | bytes 786440 | tf_op jit(solution)/shard_map/ppermute | solution.py:157
  55.1 63.7 %collective-permute-start.15 = (bf16[2,16,896]{2,1,0:T(8,128)(2,1)S(1)}, bf16[2,16,896]{2,1,0:T(8,128)(2,1)S(1)}, u32[]{:S(2)}, u32[]{:S(2)}) collective-permute-start(bf16[2,16,896]{2,1,0:T(8,128)(2,1)S(1)} %get-tuple-element.33), channel_id=1, source_target_pairs={{0,14},{2,0},{4,2},{6,4},{8,6},{10,8},{12,10},{14,12},{1,15},{3,1}... | collective-permute-start | bytes 172040 | tf_op jit(solution)/shard_map/ppermute | solution.py:184
  58.6 52.5 %collective-permute-start.14 = (bf16[2,16,896]{2,1,0:T(8,128)(2,1)S(1)}, bf16[2,16,896]{2,1,0:T(8,128)(2,1)S(1)}, u32[]{:S(2)}, u32[]{:S(2)}) collective-permute-start(bf16[2,16,896]{2,1,0:T(8,128)(2,1)S(1)} %get-tuple-element.34), channel_id=1, source_target_pairs={{0,12},{2,14},{4,0},{6,2},{8,4},{10,6},{12,8},{14,10},{1,13},{3,15... | collective-permute-start | bytes 172040 | tf_op jit(solution)/shard_map/ppermute | solution.py:184
  60.2 51.0 %collective-permute-start.13 = (bf16[2,16,896]{2,1,0:T(8,128)(2,1)S(1)}, bf16[2,16,896]{2,1,0:T(8,128)(2,1)S(1)}, u32[]{:S(2)}, u32[]{:S(2)}) collective-permute-start(bf16[2,16,896]{2,1,0:T(8,128)(2,1)S(1)} %get-tuple-element.35), channel_id=1, source_target_pairs={{0,10},{2,12},{4,14},{6,0},{8,2},{10,4},{12,6},{14,8},{1,11},{3,13... | collective-permute-start | bytes 172040 | tf_op jit(solution)/shard_map/ppermute | solution.py:184
  60.2 27.6 %collective-permute-start.10 = (bf16[2,16,896]{2,1,0:T(8,128)(2,1)S(1)}, bf16[2,16,896]{2,1,0:T(8,128)(2,1)S(1)}, u32[]{:S(2)}, u32[]{:S(2)}) collective-permute-start(bf16[2,16,896]{2,1,0:T(8,128)(2,1)S(1)} %get-tuple-element.38), channel_id=1, source_target_pairs={{0,4},{2,6},{4,8},{6,10},{8,12},{10,14},{12,0},{14,2},{1,5},{3,7},... | collective-permute-start | bytes 172040 | tf_op jit(solution)/shard_map/ppermute | solution.py:184
  62.9 7.3 %collective-permute-start = (bf16[32,4096]{1,0:T(8,128)(2,1)S(1)}, bf16[32,4096]{1,0:T(8,128)(2,1)S(1)}, u32[]{:S(2)}, u32[]{:S(2)}) collective-permute-start(bf16[32,4096]{1,0:T(8,128)(2,1)S(1)} %get-tuple-element.51), channel_id=1, source_target_pairs={{0,4},{4,8},{8,12},{12,14},{14,10},{10,6},{6,2},{2,0},{1,5},{5,9},... | collective-permute-start | bytes 786440 | tf_op jit(solution)/shard_map/ppermute | solution.py:154
  70.9 7.6 %collective-permute-start.1 = (bf16[32,4096]{1,0:T(8,128)(2,1)S(1)}, bf16[32,4096]{1,0:T(8,128)(2,1)S(1)}, u32[]{:S(2)}, u32[]{:S(2)}) collective-permute-start(bf16[32,4096]{1,0:T(8,128)(2,1)S(1)} %get-tuple-element.57), channel_id=1, source_target_pairs={{0,4},{4,8},{8,12},{12,14},{14,10},{10,6},{6,2},{2,0},{1,5},{5,9},... | collective-permute-start | bytes 786440 | tf_op jit(solution)/shard_map/ppermute | solution.py:154
  78.5 9.3 %collective-permute-start.9 = (bf16[2,16,896]{2,1,0:T(8,128)(2,1)S(1)}, bf16[2,16,896]{2,1,0:T(8,128)(2,1)S(1)}, u32[]{:S(2)}, u32[]{:S(2)}) collective-permute-start(bf16[2,16,896]{2,1,0:T(8,128)(2,1)S(1)} %get-tuple-element.39), channel_id=1, source_target_pairs={{0,2},{2,4},{4,6},{6,8},{8,10},{10,12},{12,14},{14,0},{1,3},{3,5},... | collective-permute-start | bytes 172040 | tf_op jit(solution)/shard_map/ppermute | solution.py:184
  87.7 7.0 %collective-permute-start.2 = (bf16[32,4096]{1,0:T(8,128)(2,1)S(1)}, bf16[32,4096]{1,0:T(8,128)(2,1)S(1)}, u32[]{:S(2)}, u32[]{:S(2)}) collective-permute-start(bf16[32,4096]{1,0:T(8,128)(2,1)S(1)} %get-tuple-element.55), channel_id=1, source_target_pairs={{0,4},{4,8},{8,12},{12,14},{14,10},{10,6},{6,2},{2,0},{1,5},{5,9},... | collective-permute-start | bytes 786440 | tf_op jit(solution)/shard_map/ppermute | solution.py:154
  87.7 13.0 %collective-permute-start.12 = (bf16[2,16,896]{2,1,0:T(8,128)(2,1)S(1)}, bf16[2,16,896]{2,1,0:T(8,128)(2,1)S(1)}, u32[]{:S(2)}, u32[]{:S(2)}) collective-permute-start(bf16[2,16,896]{2,1,0:T(8,128)(2,1)S(1)} %get-tuple-element.36), channel_id=1, source_target_pairs={{0,8},{2,10},{4,12},{6,14},{8,0},{10,2},{12,4},{14,6},{1,9},{3,11}... | collective-permute-start | bytes 172040 | tf_op jit(solution)/shard_map/ppermute | solution.py:184
  94.7 6.0 %collective-permute-start.11 = (bf16[2,16,896]{2,1,0:T(8,128)(2,1)S(1)}, bf16[2,16,896]{2,1,0:T(8,128)(2,1)S(1)}, u32[]{:S(2)}, u32[]{:S(2)}) collective-permute-start(bf16[2,16,896]{2,1,0:T(8,128)(2,1)S(1)} %get-tuple-element.37), channel_id=1, source_target_pairs={{0,6},{2,8},{4,10},{6,12},{8,14},{10,0},{12,2},{14,4},{1,7},{3,9},... | collective-permute-start | bytes 172040 | tf_op jit(solution)/shard_map/ppermute | solution.py:184
  100.7 6.4 %collective-permute-start.3 = (bf16[32,4096]{1,0:T(8,128)(2,1)S(1)}, bf16[32,4096]{1,0:T(8,128)(2,1)S(1)}, u32[]{:S(2)}, u32[]{:S(2)}) collective-permute-start(bf16[32,4096]{1,0:T(8,128)(2,1)S(1)} %get-tuple-element.53), channel_id=1, source_target_pairs={{0,4},{4,8},{8,12},{12,14},{14,10},{10,6},{6,2},{2,0},{1,5},{5,9},... | collective-permute-start | bytes 786440 | tf_op jit(solution)/shard_map/ppermute | solution.py:154
  100.8 8.6 %collective-permute-start.5 = (bf16[32,4096]{1,0:T(8,128)(2,1)S(1)}, bf16[32,4096]{1,0:T(8,128)(2,1)S(1)}, u32[]{:S(2)}, u32[]{:S(2)}) collective-permute-start(bf16[32,4096]{1,0:T(8,128)(2,1)S(1)} %get-tuple-element.50), channel_id=1, source_target_pairs={{4,0},{8,4},{12,8},{14,12},{10,14},{6,10},{2,6},{0,2},{5,1},{9,5},... | collective-permute-start | bytes 786440 | tf_op jit(solution)/shard_map/ppermute | solution.py:157
  110.2 7.5 %collective-permute-start.6 = (bf16[32,4096]{1,0:T(8,128)(2,1)S(1)}, bf16[32,4096]{1,0:T(8,128)(2,1)S(1)}, u32[]{:S(2)}, u32[]{:S(2)}) collective-permute-start(bf16[32,4096]{1,0:T(8,128)(2,1)S(1)} %get-tuple-element.48), channel_id=1, source_target_pairs={{4,0},{8,4},{12,8},{14,12},{10,14},{6,10},{2,6},{0,2},{5,1},{9,5},... | collective-permute-start | bytes 786440 | tf_op jit(solution)/shard_map/ppermute | solution.py:157
  118.4 6.4 %collective-permute-start.7 = (bf16[32,4096]{1,0:T(8,128)(2,1)S(1)}, bf16[32,4096]{1,0:T(8,128)(2,1)S(1)}, u32[]{:S(2)}, u32[]{:S(2)}) collective-permute-start(bf16[32,4096]{1,0:T(8,128)(2,1)S(1)} %get-tuple-element.46), channel_id=1, source_target_pairs={{4,0},{8,4},{12,8},{14,12},{10,14},{6,10},{2,6},{0,2},{5,1},{9,5},... | collective-permute-start | bytes 786440 | tf_op jit(solution)/shard_map/ppermute | solution.py:157
  132.6 17.5 %copy-start.3 = (f32[7168]{0:T(1024)S(1)}, f32[7168]{0:T(1024)}, u32[]{:S(2)}) copy-start(f32[7168]{0:T(1024)} %param.26) | copy-start | bytes 86020
  132.9 1.6 collective-permute-start.8
  134.6 22.5 %collective-permute-start.23 = (bf16[144,896]{1,0:T(8,128)(2,1)S(1)}, bf16[144,896]{1,0:T(8,128)(2,1)S(1)}, u32[]{:S(2)}, u32[]{:S(2)}) collective-permute-start(bf16[144,896]{1,0:T(8,128)(2,1)S(1)} %bitcast.306), channel_id=1, source_target_pairs={{0,1},{1,0},{2,3},{3,2},{4,5},{5,4},{6,7},{7,6},{8,9},{9,8},{10,11... | collective-permute-start | bytes 774152 | tf_op jit(solution)/shard_map/ppermute | solution.py:160
  134.8 19.9 %collective-permute-start.17 = (bf16[144,896]{1,0:T(8,128)(2,1)S(1)}, bf16[144,896]{1,0:T(8,128)(2,1)S(1)}, u32[]{:S(2)}, u32[]{:S(2)}) collective-permute-start(bf16[144,896]{1,0:T(8,128)(2,1)S(1)} %bitcast.307), channel_id=1, source_target_pairs={{4,0},{8,4},{12,8},{14,12},{10,14},{6,10},{2,6},{0,2},{5,1},{9,5},... | collective-permute-start | bytes 774152 | tf_op jit(solution)/shard_map/ppermute | solution.py:157
  135.1 20.1 %collective-permute-start.16 = (bf16[144,896]{1,0:T(8,128)(2,1)S(1)}, bf16[144,896]{1,0:T(8,128)(2,1)S(1)}, u32[]{:S(2)}, u32[]{:S(2)}) collective-permute-start(bf16[144,896]{1,0:T(8,128)(2,1)S(1)} %bitcast.308), channel_id=1, source_target_pairs={{0,4},{4,8},{8,12},{12,14},{14,10},{10,6},{6,2},{2,0},{1,5},{5,9},... | collective-permute-start | bytes 774152 | tf_op jit(solution)/shard_map/ppermute | solution.py:154
  154.7 9.2 %collective-permute-start.25 = (bf16[144,896]{1,0:T(8,128)(2,1)S(1)}, bf16[144,896]{1,0:T(8,128)(2,1)S(1)}, u32[]{:S(2)}, u32[]{:S(2)}) collective-permute-start(bf16[144,896]{1,0:T(8,128)(2,1)S(1)} %collective-permute-done.17), channel_id=1, source_target_pairs={{0,1},{1,0},{2,3},{3,2},{4,5},{5,4},{6,7},{7,6},{8,9},{9,8},{10,11... | collective-permute-start | bytes 774152 | tf_op jit(solution)/shard_map/ppermute | solution.py:160
  154.8 8.6 %collective-permute-start.19 = (bf16[144,896]{1,0:T(8,128)(2,1)S(1)}, bf16[144,896]{1,0:T(8,128)(2,1)S(1)}, u32[]{:S(2)}, u32[]{:S(2)}) collective-permute-start(bf16[144,896]{1,0:T(8,128)(2,1)S(1)} %collective-permute-done.17), channel_id=1, source_target_pairs={{4,0},{8,4},{12,8},{14,12},{10,14},{6,10},{2,6},{0,2},{5,1},{9,5},... | collective-permute-start | bytes 774152 | tf_op jit(solution)/shard_map/ppermute | solution.py:157
  155.1 10.7 %collective-permute-start.24 = (bf16[144,896]{1,0:T(8,128)(2,1)S(1)}, bf16[144,896]{1,0:T(8,128)(2,1)S(1)}, u32[]{:S(2)}, u32[]{:S(2)}) collective-permute-start(bf16[144,896]{1,0:T(8,128)(2,1)S(1)} %collective-permute-done.16), channel_id=1, source_target_pairs={{0,1},{1,0},{2,3},{3,2},{4,5},{5,4},{6,7},{7,6},{8,9},{9,8},{10,11... | collective-permute-start | bytes 774152 | tf_op jit(solution)/shard_map/ppermute | solution.py:160
  155.3 8.5 %collective-permute-start.18 = (bf16[144,896]{1,0:T(8,128)(2,1)S(1)}, bf16[144,896]{1,0:T(8,128)(2,1)S(1)}, u32[]{:S(2)}, u32[]{:S(2)}) collective-permute-start(bf16[144,896]{1,0:T(8,128)(2,1)S(1)} %collective-permute-done.16), channel_id=1, source_target_pairs={{0,4},{4,8},{8,12},{12,14},{14,10},{10,6},{6,2},{2,0},{1,5},{5,9},... | collective-permute-start | bytes 774152 | tf_op jit(solution)/shard_map/ppermute | solution.py:154
  157.3 14.8 %slice-start.2 = ((s8[8257536]{0:T(1024)(128)(4,1)}), s8[4194304]{0:T(1024)(128)(4,1)S(1)}, s32[]{:S(2)}) async-start(s8[8257536]{0:T(1024)(128)(4,1)} %bitcast.298), calls=%async_computation.2 | async-start | bytes 8388608
  163.4 11.0 %collective-permute-start.27 = (bf16[144,896]{1,0:T(8,128)(2,1)S(1)}, bf16[144,896]{1,0:T(8,128)(2,1)S(1)}, u32[]{:S(2)}, u32[]{:S(2)}) collective-permute-start(bf16[144,896]{1,0:T(8,128)(2,1)S(1)} %collective-permute-done.19), channel_id=1, source_target_pairs={{0,1},{1,0},{2,3},{3,2},{4,5},{5,4},{6,7},{7,6},{8,9},{9,8},{10,11... | collective-permute-start | bytes 774152 | tf_op jit(solution)/shard_map/ppermute | solution.py:160
  163.4 10.7 %collective-permute-start.21 = (bf16[144,896]{1,0:T(8,128)(2,1)S(1)}, bf16[144,896]{1,0:T(8,128)(2,1)S(1)}, u32[]{:S(2)}, u32[]{:S(2)}) collective-permute-start(bf16[144,896]{1,0:T(8,128)(2,1)S(1)} %collective-permute-done.19), channel_id=1, source_target_pairs={{4,0},{8,4},{12,8},{14,12},{10,14},{6,10},{2,6},{0,2},{5,1},{9,5},... | collective-permute-start | bytes 774152 | tf_op jit(solution)/shard_map/ppermute | solution.py:157
  163.8 10.8 %collective-permute-start.26 = (bf16[144,896]{1,0:T(8,128)(2,1)S(1)}, bf16[144,896]{1,0:T(8,128)(2,1)S(1)}, u32[]{:S(2)}, u32[]{:S(2)}) collective-permute-start(bf16[144,896]{1,0:T(8,128)(2,1)S(1)} %collective-permute-done.18), channel_id=1, source_target_pairs={{0,1},{1,0},{2,3},{3,2},{4,5},{5,4},{6,7},{7,6},{8,9},{9,8},{10,11... | collective-permute-start | bytes 774152 | tf_op jit(solution)/shard_map/ppermute | solution.py:160
  163.9 8.9 %collective-permute-start.20 = (bf16[144,896]{1,0:T(8,128)(2,1)S(1)}, bf16[144,896]{1,0:T(8,128)(2,1)S(1)}, u32[]{:S(2)}, u32[]{:S(2)}) collective-permute-start(bf16[144,896]{1,0:T(8,128)(2,1)S(1)} %collective-permute-done.18), channel_id=1, source_target_pairs={{0,4},{4,8},{8,12},{12,14},{14,10},{10,6},{6,2},{2,0},{1,5},{5,9},... | collective-permute-start | bytes 774152 | tf_op jit(solution)/shard_map/ppermute | solution.py:154
  166.1 6.0 %slice-start.3 = ((s8[8257536]{0:T(1024)(128)(4,1)}), s8[4063232]{0:T(1024)(128)(4,1)S(1)}, s32[]{:S(2)}) async-start(s8[8257536]{0:T(1024)(128)(4,1)} %bitcast.298), calls=%async_computation.3 | async-start | bytes 8126464
  168.1 9.2 %slice-start.4 = ((s8[8257536]{0:T(1024)(128)(4,1)}), s8[4194304]{0:T(1024)(128)(4,1)S(1)}, s32[]{:S(2)}) async-start(s8[8257536]{0:T(1024)(128)(4,1)} %bitcast.300), calls=%async_computation.4 | async-start | bytes 8388608
  172.1 5.3 %slice-start.5 = ((s8[8257536]{0:T(1024)(128)(4,1)}), s8[4063232]{0:T(1024)(128)(4,1)S(1)}, s32[]{:S(2)}) async-start(s8[8257536]{0:T(1024)(128)(4,1)} %bitcast.300), calls=%async_computation.5 | async-start | bytes 8126464
  172.8 6.1 %collective-permute-start.28 = (bf16[144,896]{1,0:T(8,128)(2,1)S(1)}, bf16[144,896]{1,0:T(8,128)(2,1)S(1)}, u32[]{:S(2)}, u32[]{:S(2)}) collective-permute-start(bf16[144,896]{1,0:T(8,128)(2,1)S(1)} %collective-permute-done.20), channel_id=1, source_target_pairs={{0,1},{1,0},{2,3},{3,2},{4,5},{5,4},{6,7},{7,6},{8,9},{9,8},{10,11... | collective-permute-start | bytes 774152 | tf_op jit(solution)/shard_map/ppermute | solution.py:160
  172.9 8.6 %collective-permute-start.22 = (bf16[144,896]{1,0:T(8,128)(2,1)S(1)}, bf16[144,896]{1,0:T(8,128)(2,1)S(1)}, u32[]{:S(2)}, u32[]{:S(2)}) collective-permute-start(bf16[144,896]{1,0:T(8,128)(2,1)S(1)} %collective-permute-done.20), channel_id=1, source_target_pairs={{0,4},{4,8},{8,12},{12,14},{14,10},{10,6},{6,2},{2,0},{1,5},{5,9},... | collective-permute-start | bytes 774152 | tf_op jit(solution)/shard_map/ppermute | solution.py:154
  174.2 4.6 %collective-permute-start.29 = (bf16[144,896]{1,0:T(8,128)(2,1)S(1)}, bf16[144,896]{1,0:T(8,128)(2,1)S(1)}, u32[]{:S(2)}, u32[]{:S(2)}) collective-permute-start(bf16[144,896]{1,0:T(8,128)(2,1)S(1)} %collective-permute-done.21), channel_id=1, source_target_pairs={{0,1},{1,0},{2,3},{3,2},{4,5},{5,4},{6,7},{7,6},{8,9},{9,8},{10,11... | collective-permute-start | bytes 774152 | tf_op jit(solution)/shard_map/ppermute | solution.py:160
  181.5 2.7 %collective-permute-start.30 = (bf16[144,896]{1,0:T(8,128)(2,1)S(1)}, bf16[144,896]{1,0:T(8,128)(2,1)S(1)}, u32[]{:S(2)}, u32[]{:S(2)}) collective-permute-start(bf16[144,896]{1,0:T(8,128)(2,1)S(1)} %collective-permute-done.22), channel_id=1, source_target_pairs={{0,1},{1,0},{2,3},{3,2},{4,5},{5,4},{6,7},{7,6},{8,9},{9,8},{10,11... | collective-permute-start | bytes 774152 | tf_op jit(solution)/shard_map/ppermute | solution.py:160
  182.9 3.0 %slice-start = ((s8[8257536]{0:T(1024)(128)(4,1)}), s8[4194304]{0:T(1024)(128)(4,1)S(1)}, s32[]{:S(2)}) async-start(s8[8257536]{0:T(1024)(128)(4,1)} %bitcast.290), calls=%async_computation | async-start | bytes 8388608
  184.5 2.3 slice-start.1
  189.8 8.2 %collective-permute-start.31 = (bf16[144,7168]{1,0:T(8,128)(2,1)}, bf16[144,7168]{1,0:T(8,128)(2,1)}, u32[]{:S(2)}, u32[]{:S(2)}) collective-permute-start(bf16[144,7168]{1,0:T(8,128)(2,1)} %convolution_convert_fusion), channel_id=1, source_target_pairs={{0,1},{1,0},{2,3},{3,2},{4,5},{5,4},{6,7},{7,6},{8,9},{9,8},{10,11... | collective-permute-start | bytes 6193160 | tf_op jit(solution)/shard_map/ppermute | solution.py:160
  199.3 7.6 %collective-permute-start.32 = (bf16[16,7168]{1,0:T(8,128)(2,1)S(1)}, bf16[16,7168]{1,0:T(8,128)(2,1)S(1)}, u32[]{:S(2)}, u32[]{:S(2)}) collective-permute-start(bf16[16,7168]{1,0:T(8,128)(2,1)S(1)} %get-tuple-element.29), channel_id=1, source_target_pairs={{0,4},{4,8},{8,12},{12,14},{14,10},{10,6},{6,2},{2,0},{1,5},{5,9},... | collective-permute-start | bytes 688136 | tf_op jit(solution)/shard_map/ppermute | solution.py:154
  201.2 9.3 %collective-permute-start.36 = (bf16[16,7168]{1,0:T(8,128)(2,1)S(1)}, bf16[16,7168]{1,0:T(8,128)(2,1)S(1)}, u32[]{:S(2)}, u32[]{:S(2)}) collective-permute-start(bf16[16,7168]{1,0:T(8,128)(2,1)S(1)} %get-tuple-element.30), channel_id=1, source_target_pairs={{4,0},{8,4},{12,8},{14,12},{10,14},{6,10},{2,6},{0,2},{5,1},{9,5},... | collective-permute-start | bytes 688136 | tf_op jit(solution)/shard_map/ppermute | solution.py:157
  207.9 6.8 %collective-permute-start.33 = (bf16[16,7168]{1,0:T(8,128)(2,1)S(1)}, bf16[16,7168]{1,0:T(8,128)(2,1)S(1)}, u32[]{:S(2)}, u32[]{:S(2)}) collective-permute-start(bf16[16,7168]{1,0:T(8,128)(2,1)S(1)} %fusion.72), channel_id=1, source_target_pairs={{0,4},{4,8},{8,12},{12,14},{14,10},{10,6},{6,2},{2,0},{1,5},{5,9},... | collective-permute-start | bytes 688136 | tf_op jit(solution)/shard_map/ppermute | solution.py:154
  216.8 6.2 %collective-permute-start.37 = (bf16[16,7168]{1,0:T(8,128)(2,1)}, bf16[16,7168]{1,0:T(8,128)(2,1)S(1)}, u32[]{:S(2)}, u32[]{:S(2)}) collective-permute-start(bf16[16,7168]{1,0:T(8,128)(2,1)} %get-tuple-element.28), channel_id=1, source_target_pairs={{4,0},{8,4},{12,8},{14,12},{10,14},{6,10},{2,6},{0,2},{5,1},{9,5},... | collective-permute-start | bytes 688136 | tf_op jit(solution)/shard_map/ppermute | solution.py:157
  219.3 6.3 %collective-permute-start.34 = (bf16[16,7168]{1,0:T(8,128)(2,1)}, bf16[16,7168]{1,0:T(8,128)(2,1)S(1)}, u32[]{:S(2)}, u32[]{:S(2)}) collective-permute-start(bf16[16,7168]{1,0:T(8,128)(2,1)} %get-tuple-element.27), channel_id=1, source_target_pairs={{0,4},{4,8},{8,12},{12,14},{14,10},{10,6},{6,2},{2,0},{1,5},{5,9},... | collective-permute-start | bytes 688136 | tf_op jit(solution)/shard_map/ppermute | solution.py:154
  224.1 6.1 %collective-permute-start.38 = (bf16[16,7168]{1,0:T(8,128)(2,1)S(1)}, bf16[16,7168]{1,0:T(8,128)(2,1)S(1)}, u32[]{:S(2)}, u32[]{:S(2)}) collective-permute-start(bf16[16,7168]{1,0:T(8,128)(2,1)S(1)} %fusion.70), channel_id=1, source_target_pairs={{4,0},{8,4},{12,8},{14,12},{10,14},{6,10},{2,6},{0,2},{5,1},{9,5},... | collective-permute-start | bytes 688136 | tf_op jit(solution)/shard_map/ppermute | solution.py:157
  231.4 6.1 %collective-permute-start.35 = (bf16[16,7168]{1,0:T(8,128)(2,1)S(1)}, bf16[16,7168]{1,0:T(8,128)(2,1)S(1)}, u32[]{:S(2)}, u32[]{:S(2)}) collective-permute-start(bf16[16,7168]{1,0:T(8,128)(2,1)S(1)} %get-tuple-element.25), channel_id=1, source_target_pairs={{0,4},{4,8},{8,12},{12,14},{14,10},{10,6},{6,2},{2,0},{1,5},{5,9},... | collective-permute-start | bytes 688136 | tf_op jit(solution)/shard_map/ppermute | solution.py:154
  232.8 6.0 %collective-permute-start.39 = (bf16[16,7168]{1,0:T(8,128)(2,1)S(1)}, bf16[16,7168]{1,0:T(8,128)(2,1)S(1)}, u32[]{:S(2)}, u32[]{:S(2)}) collective-permute-start(bf16[16,7168]{1,0:T(8,128)(2,1)S(1)} %get-tuple-element.26), channel_id=1, source_target_pairs={{4,0},{8,4},{12,8},{14,12},{10,14},{6,10},{2,6},{0,2},{5,1},{9,5},... | collective-permute-start | bytes 688136 | tf_op jit(solution)/shard_map/ppermute | solution.py:157
  240.1 1.6 collective-permute-start.40

commit v2 on v0

v2 whole, which is shorter than its diff:
```python
import functools

import jax
import jax.numpy as jnp
from jax import lax
from jax.experimental import pallas as pl
from jax.experimental.pallas import tpu as pltpu
from jax.sharding import PartitionSpec as P

score_scale = 192.0 ** (-0.5)
norm_eps = 1e-06
masked_score = -1e30
f32, bf16, i32 = jnp.float32, jnp.bfloat16, jnp.int32
SMEM = pltpu.SMEM
MIB = 1 << 20

RANK, CORE, BUSY, BUSY_RANK, SPAN, DEC, LIVE, START, LENGTHS = range(9)


def mm(a, b):
    return lax.dot_general(a, b, (((1,), (0,)), ((), ())), preferred_element_type=f32)


def mm_nt(a, b):
    return lax.dot_general(a, b, (((1,), (1,)), ((), ())), preferred_element_type=f32)


def smem():
    return pl.BlockSpec(memory_space=SMEM)


def whole():
    return pl.BlockSpec(memory_space=pltpu.VMEM)


def params(mib=32):
    return pltpu.CompilerParams(vmem_limit_bytes=mib * MIB)


def cost(flops, moved, exps=0):
    return pl.CostEstimate(flops=int(flops), bytes_accessed=int(moved), transcendentals=int(exps))


def ring_order(mesh):
    count = mesh.shape["blk"]
    natural = list(range(count))
    snake = natural[0::2] + natural[1::2][::-1]
    names = list(mesh.axis_names)
    axes = [names.index("blk")] + [a for a, x in enumerate(names) if x != "blk"]
    lane = mesh.devices.transpose(axes)
    firsts = [lane[i].reshape(-1)[0] for i in natural]
    if not all(hasattr(d, "coords") for d in firsts):
        return snake

    def length(order):
        hops = zip(order, order[1:] + order[:1])
        return sum(
            sum(abs(u - v) for u, v in zip(firsts[a].coords, firsts[b].coords)) for a, b in hops
        )

    return natural if length(natural) <= length(snake) else snake


class Table:
    def __init__(self, ranks, slots):
        self.reach = ranks // 2
        self.source = LENGTHS + slots
        self.ahead = self.source + ranks + 1
        self.behind = self.ahead + self.reach + 1
        self.owner_back = self.behind + self.reach + 1
        self.owner_fore = self.owner_back + self.reach + 1
        self.size = self.owner_fore + self.reach + 1


def table_kernel(table, ranks, ids, span, dec, start, lengths, at, who, out):
    reach = table.reach
    rank, core = ids[0], ids[1]
    most, busy_rank = span[0] + dec[0], jnp.int32(0)
    for i in range(1, ranks):
        here = span[i] + dec[i]
        busy_rank = jnp.where(here > most, i, busy_rank)
        most = jnp.maximum(here, most)
    busy = rank == busy_rank

    def wrap(x):
        x = jnp.where(x < 0, x + ranks, x)
        return jnp.where(x >= ranks, x - ranks, x)

    place, busy_place = at[rank], at[busy_rank]
    to_busy = wrap(busy_place - place)
    from_busy = wrap(place - busy_place)

    def node_ahead(k):
        far = (to_busy > 0) & (k > to_busy + 1)
        slot = who[wrap(place + k - jnp.where(far, 1, 0))]
        return jnp.where((to_busy > 0) & (k == to_busy + 1), ranks, slot)

    def node_behind(k):
        far = (from_busy > 0) & (k > from_busy)
        slot = who[wrap(place - k + jnp.where(far, 1, 0))]
        return jnp.where((from_busy > 0) & (k == from_busy), ranks, slot)

    out[RANK] = rank
    out[CORE] = core
    out[BUSY] = jnp.where(busy, 1, 0)
    out[BUSY_RANK] = busy_rank
    out[SPAN] = span[rank]
    out[DEC] = dec[rank]
    out[LIVE] = span[rank] + dec[rank]
    out[START] = start[0]
    for j in range(lengths.shape[1]):
        out[LENGTHS + j] = lengths[0, j]
    out[table.source + rank] = 0
    for k in range(1, reach + 1):
        out[table.ahead + k] = node_ahead(k)
        out[table.behind + k] = node_behind(k)
        out[table.owner_back + k] = who[wrap(place - k)]
        out[table.owner_fore + k] = who[wrap(place + k)]
        out[table.source + node_behind(k)] = k
        last = jnp.where(busy, ranks, node_ahead(k)) if k == reach else node_ahead(k)
        out[table.source + last] = reach + k


def attend_kernel(
    heads, group, rows, lat, cached, value, start_step,
    tab, q, cache, fresh, vw, main, extra, k0, k1, kpad, dq, dec,
):
    pair = 2 * lat
    wide = -(-lat // 128) * 128
    shift = wide - lat
    keys = cached + rows
    cols = -(-keys // 128) * 128
    slots = cache.shape[0] - 1
    dr = 8
    span, decs = tab[SPAN], tab[DEC]

    def onehot(shape, row_dim, slot_dim):
        r = lax.broadcasted_iota(i32, shape, row_dim)
        j = lax.broadcasted_iota(i32, shape, slot_dim)
        return jnp.where((r == span + j) & (j < decs), 1.0, 0.0).astype(bf16)

    @pl.when(pl.program_id(0) == 0)
    def _():
        k0[...] = jnp.zeros_like(k0)
        k1[...] = jnp.zeros_like(k1)
        for ref, off in ((k0, 0), (k1, shift)):
            ref[off : off + lat, :cached] = cache[0]
            ref[off : off + lat, cached:keys] = fresh[...]
        kpad[...] = jnp.zeros_like(kpad)
        for s in range(slots):
            kpad[s, :lat] = cache[s + 1]
        pick = onehot((16, rows), 1, 0)
        for p in range(heads // 2):
            got = mm(pick, q[:, pair * p : pair * (p + 1)])[:dr]
            dq[2 * p * dr : (2 * p + 1) * dr] = got[:, :wide]
            dq[(2 * p + 1) * dr : (2 * p + 2) * dr] = pltpu.roll(got[:, pair - wide :], wide - shift, 1)
        n = heads * dr
        queries = dq[...].astype(bf16)
        slot = lax.broadcasted_iota(i32, (n, 1), 0) % dr
        length = jnp.zeros((n, 1), i32)
        scores = jnp.zeros((n, cached), f32)
        for s in range(slots):
            scores = jnp.where(slot == s, mm(queries, kpad[s]), scores)
            length = jnp.where(slot == s, tab[LENGTHS + s], length)
        seen = lax.broadcasted_iota(i32, (n, cached), 1) < length
        scores = jnp.where(seen, scores * score_scale, masked_score)
        own = mm(queries, k0[:, cached:])
        column = lax.broadcasted_iota(i32, own.shape, 1)
        own = jnp.sum(jnp.where(column == span + slot, own, 0.0), axis=1, keepdims=True)
        own = own * score_scale
        peak = jnp.maximum(jnp.max(scores, axis=1, keepdims=True), own)
        e = jnp.where(seen, jnp.exp(scores - peak), 0.0)
        e_own = jnp.exp(own - peak)
        total = jnp.sum(e, axis=1, keepdims=True) + e_own
        w = e / total
        acc = jnp.zeros((n, value), f32)
        for s in range(slots):
            acc = acc + mm_nt(jnp.where(slot == s, w, 0.0).astype(bf16), cache[s + 1, :value])
        own_value = mm_nt(pick, fresh[:value])[:dr]
        own_value = jnp.broadcast_to(own_value[None], (heads, dr, value)).reshape(n, value)
        dec[...] = acc + (e_own / total).astype(bf16).astype(f32) * own_value

    step = pl.program_id(0)
    start = step * (group * lat)
    pairs = group // 2

    def stacked(off):
        return jnp.concatenate(
            [q[:, pl.ds(pl.multiple_of(start + pair * p + off, 128), wide)] for p in range(pairs)], 0
        )

    m = pairs * rows
    row = lax.broadcasted_iota(i32, (m, 1), 0) % rows
    col = lax.broadcasted_iota(i32, (m, cols), 1)
    seen = (col < jnp.where(col < cached, tab[START], cached + 1 + row)) & (col < keys)
    values = k0[:value]

    def latent(lhs, ref):
        s = jnp.where(seen, mm(lhs, ref[...]) * score_scale, masked_score)
        e = jnp.where(seen, jnp.exp(s - jnp.max(s, axis=1, keepdims=True)), 0.0)
        w = (e * (1.0 / jnp.sum(e, axis=1, keepdims=True))).astype(bf16)
        o = mm_nt(w, values)
        return jnp.where(row < span, o, 0.0).astype(bf16)

    even, odd = latent(stacked(0), k0), latent(stacked(pair - wide), k1)
    outs, decoded = [], []
    for p in range(pairs):
        at = pl.multiple_of((step * group + 2 * p) * dr, 16)
        lhs = jnp.concatenate(
            [even[p * rows : (p + 1) * rows], odd[p * rows : (p + 1) * rows], dec[pl.ds(at, 16)].astype(bf16)], 0
        )
        vh = vw.shape[2]
        r = mm(lhs, jnp.concatenate([vw[2 * p], vw[2 * p + 1]], 1))
        outs += [r[:rows, :vh], r[rows : 2 * rows, vh:]]
        decoded += [r[2 * rows : 2 * rows + dr, :vh], r[2 * rows + dr :, vh:]]
    decoded = jnp.concatenate(decoded, 1)
    decoded = jnp.concatenate([decoded, jnp.zeros_like(decoded)], 0).astype(bf16)
    out = jnp.concatenate(outs, 1) + mm(onehot((rows, 16), 0, 1), decoded)
    out = out.astype(bf16)
    main[...] = out[: rows // 2]
    extra[...] = out[rows // 2 :]


def attend(tab, queries, cache, fresh, vw, part, parts):
    rows, heads = queries.shape[0], vw.shape[0] // parts
    lat = queries.shape[1] // vw.shape[0]
    slots, _, cached = cache.shape
    value, vh = vw.shape[1:]
    group = min(8, heads)
    wide, cols = -(-lat // 128) * 128, -(-(cached + rows) // 128) * 128
    steps = heads // group
    half = jax.ShapeDtypeStruct((rows // 2, heads * vh), bf16)
    return pl.pallas_call(
        functools.partial(attend_kernel, heads, group, rows, lat, cached, value, part),
        grid=(steps,),
        in_specs=[
            smem(),
            pl.BlockSpec((rows, heads * lat), lambda i: (0, part)),
            pl.BlockSpec(cache.shape, lambda i: (0, 0, 0)),
            pl.BlockSpec(fresh.shape, lambda i: (0, 0)),
            pl.BlockSpec((group, value, vh), lambda i: (part * steps + i, 0, 0)),
        ],
        out_specs=[pl.BlockSpec((rows // 2, group * vh), lambda i: (0, i))] * 2,
        out_shape=[half, half],
        scratch_shapes=[
            pltpu.VMEM((wide, cols), bf16),
            pltpu.VMEM((wide, cols), bf16),
            pltpu.VMEM((slots - 1, wide, cached), bf16),
            pltpu.VMEM((heads * 8, wide), f32),
            pltpu.VMEM((heads * 8, value), f32),
        ],
        compiler_params=params(40),
        cost_estimate=cost(
            2 * rows * heads * (cached + rows) * (lat + value),
            2 * (queries.size // parts + cache.size + vw.size // parts),
            rows * heads * (cached + rows),
        ),
        name="attend",
    )(tab, queries, cache, fresh, vw)


def pack_kernel(ranks, features, half, tab, res, *outs):
    core, rank = tab[CORE], tab[RANK]
    low = pl.multiple_of(core * half, half)
    high = pl.multiple_of(res.shape[0] // 2 + core * half, half)
    for k in range(ranks):
        target = rank + k
        target = jnp.where(target >= ranks, target - ranks, target)

        def put(columns, k=k):
            outs[k][:half] = res[pl.ds(low, half), columns]
            outs[k][half:] = res[pl.ds(high, half), columns]

        if features % 128 == 0:
            put(pl.ds(pl.multiple_of(target * features, 128), features))
        else:
            for t in range(ranks):
                pl.when(target == t)(functools.partial(put, slice(t * features, (t + 1) * features)))


def pack(tab, residual, ranks, cores):
    rows, width = residual.shape
    half, features = rows // 2 // cores, width // ranks
    return pl.pallas_call(
        functools.partial(pack_kernel, ranks, features, half),
        in_specs=[smem(), whole()],
        out_specs=[whole()] * ranks,
        out_shape=[jax.ShapeDtypeStruct((2 * half, features), bf16)] * ranks,
        compiler_params=params(),
        cost_estimate=cost(0, 4 * residual.size),
        name="pack",
    )(tab, residual)


def route_kernel(tab, *refs):
    count = len(refs) // 3
    busy = tab[BUSY] == 1
    for i in range(count):
        special, usual, out = refs[2 * i], refs[2 * i + 1], refs[2 * count + i]

        @pl.when(busy)
        def _(special=special, out=out):
            out[...] = special[...]

        @pl.when(jnp.logical_not(busy))
        def _(usual=usual, out=out):
            out[...] = usual[...]


def route(tab, *choices):
    flat = [x for pair in choices for x in pair]
    return pl.pallas_call(
        route_kernel,
        in_specs=[smem()] + [whole()] * len(flat),
        out_specs=[whole()] * len(choices),
        out_shape=[jax.ShapeDtypeStruct(b.shape, b.dtype) for _, b in choices],
        compiler_params=params(),
        cost_estimate=cost(0, 3 * sum(2 * b.size for _, b in choices)),
        name="route",
    )(tab, *flat)


def project_kernel(source, nodes, block, half, first, tab, *refs):
    blocks, refs = refs[: nodes + 1], refs[nodes + 1 :]
    before = None if first else refs[0]
    weight, kept, given, acc = refs[-4:]
    step = pl.program_id(0)
    depth = weight.shape[0]
    columns = pl.ds(pl.multiple_of(step * depth, 128), depth)
    last = jnp.where(tab[BUSY] == 1, blocks[nodes][:, columns], blocks[nodes - 1][:, columns])
    lhs = jnp.concatenate([b[:, columns] for b in blocks[: nodes - 1]] + [last], 0)
    got = mm(lhs, weight[...])

    @pl.when(step == 0)
    def _():
        acc[...] = got if first else got + before[...]

    @pl.when(step > 0)
    def _():
        acc[...] += got

    @pl.when(step == pl.num_programs(0) - 1)
    def _():
        core = tab[CORE]
        for k in range(nodes):
            at = tab[source + k] * block
            kept[k * half : (k + 1) * half] = acc[pl.ds(pl.multiple_of(at + core * half, half), half)]
            other = acc[pl.ds(pl.multiple_of(at + (1 - core) * half, half), half)]
            given[k * half : (k + 1) * half] = other.astype(bf16)


def project_part_kernel(nodes, first, tab, *refs):
    blocks, refs = refs[: nodes + 1], refs[nodes + 1 :]
    weight, out = refs[-2:]
    step = pl.program_id(0)
    depth = weight.shape[0]
    columns = pl.ds(pl.multiple_of(step * depth, 128), depth)
    last = jnp.where(tab[BUSY] == 1, blocks[nodes][:, columns], blocks[nodes - 1][:, columns])
    lhs = jnp.concatenate([b[:, columns] for b in blocks[: nodes - 1]] + [last], 0)
    got = mm(lhs, weight[...])

    @pl.when(step == 0)
    def _():
        out[...] = got if first else got + refs[0][...]

    @pl.when(step > 0)
    def _():
        out[...] += got


def project(tab, table, blocks, before, weight, part, parts, cores):
    block, width = blocks[0].shape
    nodes = len(blocks) - 1
    half = block // cores
    features = weight.shape[1]
    depth = 1024 if width % 1024 == 0 else width
    steps = width // depth
    total = jax.ShapeDtypeStruct((nodes * block, features), f32)
    final = part == parts - 1
    first = before is None
    ins = [smem()] + [whole()] * (nodes + 1 + (not first))
    ins += [pl.BlockSpec((depth, features), lambda i: (part * steps + i, 0))]
    args = [tab, *blocks] + ([] if first else [before]) + [weight]
    estimate = cost(
        2 * nodes * block * width * features, 2 * (nodes * block * width + width * features)
    )
    if not final:
        return pl.pallas_call(
            functools.partial(project_part_kernel, nodes, first),
            grid=(steps,),
            in_specs=ins,
            out_specs=pl.BlockSpec(total.shape, lambda i: (0, 0)),
            out_shape=total,
            compiler_params=params(),
            cost_estimate=estimate,
            name="project",
        )(*args)
    return pl.pallas_call(
        functools.partial(project_kernel, table.source, nodes, block, half, first),
        grid=(steps,),
        in_specs=ins,
        out_specs=[pl.BlockSpec((nodes * half, features), lambda i: (0, 0))] * 2,
        out_shape=[
            jax.ShapeDtypeStruct((nodes * half, features), f32),
            jax.ShapeDtypeStruct((nodes * half, features), bf16),
        ],
        scratch_shapes=[pltpu.VMEM(total.shape, f32)],
        compiler_params=params(),
        cost_estimate=estimate,
        name="project",
    )(*args)


def stream_kernel(ranks, half, tab, kept, other, *refs):
    res, out = refs[:-1], refs[-1]
    rank, busy_rank = tab[RANK], tab[BUSY_RANK]

    def put(slot, extra):
        rows = pl.ds(pl.multiple_of(slot * half, half), half)
        total = kept[rows] + other[rows].astype(f32) + extra.astype(f32)
        out[rows] = total.astype(bf16)

    for k in range(ranks):
        owner = rank - k
        owner = jnp.where(owner < 0, owner + ranks, owner)
        put(owner, res[k][:half])

        @pl.when(owner == busy_rank)
        def _(k=k):
            put(ranks, res[k][half:])


def stream_of(tab, kept, other, res):
    half = res[0].shape[0] // 2
    return pl.pallas_call(
        functools.partial(stream_kernel, len(res), half),
        in_specs=[smem()] + [whole()] * (2 + len(res)),
        out_specs=whole(),
        out_shape=jax.ShapeDtypeStruct(other.shape, bf16),
        compiler_params=params(),
        cost_estimate=cost(0, 10 * other.size),
        name="stream",
    )(tab, kept, other, *res)


def expand_kernel(count, first, final, width, tab, *refs):
    mines, theirs = refs[:count], refs[count : 2 * count]
    refs = refs[2 * count :]
    gain, gate, up = refs[:3]
    refs = refs[3:]
    if not first:
        before, refs = refs[:3], refs[3:]
    if final:
        hidden, refs = refs[0], refs[1:]
    gates, ups, squares = refs
    step = pl.program_id(0)
    for i in range(count):

        @pl.when(step == i)
        def _(i=i):
            both = jnp.concatenate([mines[i][...], theirs[i][...]], 0).astype(f32)
            scaled = (both * gain[0]).astype(bf16)
            values = (
                mm(scaled, gate[...]),
                mm(scaled, up[...]),
                jnp.sum(both * both, axis=1, keepdims=True),
            )
            for n, (ref, value) in enumerate(zip((gates, ups, squares), values)):
                if i == 0:
                    ref[...] = value if first else value + before[n][...]
                else:
                    ref[...] += value

    if final:

        @pl.when(step == count - 1)
        def _():
            scale = lax.rsqrt(squares[...] / width + norm_eps)
            g = gates[...] * scale
            hidden[...] = (g / (1.0 + jnp.exp(-g)) * (ups[...] * scale)).astype(bf16)


def expand(tab, mines, theirs, owners, gain, gate, up, before, final):
    count = len(mines)
    rows, features = mines[0].shape
    units = gate.shape[1]
    first = before is None

    def owner(i, tab):
        index = tab[owners[0]]
        for n in range(1, count):
            index = jnp.where(i == n, tab[owners[n]], index)
        return index

    def full(shape):
        return pl.BlockSpec(shape, lambda i, tab: (0,) * len(shape))

    sums = [(2 * rows, units), (2 * rows, units), (2 * rows, 1)]
    ins = [full((rows, features))] * (2 * count)
    ins += [pl.BlockSpec((1, 1, features), lambda i, tab: (owner(i, tab), 0, 0))]
    ins += [pl.BlockSpec((features, units), lambda i, tab: (owner(i, tab), 0))] * 2
    if not first:
        ins += [full(s) for s in sums]
    shapes = [jax.ShapeDtypeStruct(s, f32) for s in sums]
    out_shapes = [jax.ShapeDtypeStruct((2 * rows, units), bf16)] if final else shapes
    return pl.pallas_call(
        functools.partial(expand_kernel, count, first, final, gate.shape[0]),
        grid_spec=pltpu.PrefetchScalarGridSpec(
            num_scalar_prefetch=1,
            grid=(count,),
            in_specs=ins,
            out_specs=[full(s.shape) for s in out_shapes],
            scratch_shapes=[pltpu.VMEM(s, f32) for s in sums] if final else [],
        ),
        out_shape=out_shapes,
        compiler_params=params(),
        cost_estimate=cost(
            8 * count * rows * features * units, count * (4 * features * units + 4 * rows * features)
        ),
        name="expand",
    )(tab, *mines, *theirs, gain, gate, up, *([] if first else before))


def collect_kernel(owners, tab, *refs):
    out = refs[-1]
    half = out.shape[1] // 2
    for i, at in enumerate(owners):
        out[tab[at], :half] = refs[2 * i][...]
        out[tab[at], half:] = refs[2 * i + 1][...]


def collect(tab, blocks, owners, half):
    ranks = len(blocks)
    features = blocks[0].shape[1]
    ins, args = [], []
    for x in blocks:
        ins += [
            pl.BlockSpec((half, features), lambda i, tab: (tab[RANK], 0)),
            pl.BlockSpec((half, features), lambda i, tab: (ranks, 0)),
        ]
        args += [x, x]
    shape = (ranks, 2 * half, features)
    return pl.pallas_call(
        functools.partial(collect_kernel, owners),
        grid_spec=pltpu.PrefetchScalarGridSpec(
            num_scalar_prefetch=1,
            grid=(1,),
            in_specs=ins,
            out_specs=pl.BlockSpec(shape, lambda i, tab: (0, 0, 0)),
        ),
        out_shape=jax.ShapeDtypeStruct(shape, bf16),
        compiler_params=params(),
        cost_estimate=cost(0, 8 * ranks * half * features),
        name="collect",
    )(tab, *args)


def contract_kernel(hidden, weight, mine, given):
    got = mm(hidden[...], weight[...]).astype(bf16)
    rows = mine.shape[0]
    mine[...] = got[:rows]
    given[...] = got[rows:]


def contract(hidden, weight, part, parts):
    rows, units = hidden.shape
    columns = weight.shape[1] // parts
    wide = columns // 2 if columns % 256 == 0 else columns
    steps = columns // wide
    out = jax.ShapeDtypeStruct((rows // 2, columns), bf16)
    return pl.pallas_call(
        contract_kernel,
        grid=(steps,),
        in_specs=[
            pl.BlockSpec((rows, units), lambda i: (0, 0)),
            pl.BlockSpec((units, wide), lambda i: (0, part * steps + i)),
        ],
        out_specs=[pl.BlockSpec((rows // 2, wide), lambda i: (0, i))] * 2,
        out_shape=[out, out],
        compiler_params=params(),
        cost_estimate=cost(2 * rows * units * columns, 2 * (units + rows) * columns),
        name="contract",
    )(hidden, weight)


def add_kernel(step, tab, mine_f, theirs_f, mine_b, theirs_b, *refs):
    got, (out_f, out_b) = refs[:-2], refs[-2:]
    busy = tab[BUSY] == 1
    own_f = mine_f[...].astype(f32) + theirs_f[...].astype(f32)
    own_b = mine_b[...].astype(f32) + theirs_b[...].astype(f32)
    if step == 1:
        out_f[...] = jnp.where(busy, 0.0, own_f).astype(bf16)
        out_b[...] = own_b.astype(bf16)
    elif step == 2:
        out_f[...] = (own_f + jnp.where(busy, 0.0, got[0][...].astype(f32))).astype(bf16)
        out_b[...] = (own_b + jnp.where(busy, 0.0, got[1][...].astype(f32))).astype(bf16)
    else:
        from_f = jnp.where(busy, got[0][...], got[1][...]).astype(f32)
        from_b = jnp.where(busy, got[2][...], got[3][...]).astype(f32)
        out_f[...] = (own_f + from_f).astype(bf16)
        out_b[...] = (own_b + from_b).astype(bf16)


def add(tab, table, step, mine, theirs, got, half):
    columns = mine.shape[1]
    far = table.reach + 1 - step

    def at(where):
        return pl.BlockSpec((half, columns), lambda i, tab: (tab[where + far], 0))

    full = pl.BlockSpec((half, columns), lambda i, tab: (0, 0))
    out = jax.ShapeDtypeStruct((half, columns), bf16)
    return pl.pallas_call(
        functools.partial(add_kernel, step),
        grid_spec=pltpu.PrefetchScalarGridSpec(
            num_scalar_prefetch=1,
            grid=(1,),
            in_specs=[at(table.ahead)] * 2 + [at(table.behind)] * 2 + [full] * len(got),
            out_specs=[full, full],
        ),
        out_shape=[out, out],
        compiler_params=params(),
        cost_estimate=cost(0, 16 * half * columns),
        name="add",
    )(tab, mine, theirs, mine, theirs, *got)


def close_kernel(begin, tab, mm_, tm, me, te, f_last, f_prev, b_last, b_prev, own, kept, given):
    busy, first = tab[BUSY] == 1, tab[CORE] == 0
    half, columns = kept.shape
    features = own.shape[2]

    def total(*refs):
        out = refs[0][...].astype(f32)
        for r in refs[1:]:
            out = out + r[...].astype(f32)
        return out

    main = total(mm_, tm, f_last) + jnp.where(busy, b_prev[...], b_last[...]).astype(f32)
    extra = total(me, te, f_prev, b_last)
    for c in range(columns // features):
        cols = slice(c * features, (c + 1) * features)
        m = (main[:, cols] + own[begin + c, :half].astype(f32)).astype(bf16)
        e = (extra[:, cols] + own[begin + c, half:].astype(f32)).astype(bf16)
        kept[:, cols] = jnp.where(first, m, e)
        given[:, cols] = jnp.where(first, e, m)


def close(tab, mine, theirs, got_f, got_b, own, begin, half):
    columns = mine.shape[1]
    nodes = mine.shape[0] // half
    own_at = pl.BlockSpec((half, columns), lambda i, tab: (tab[RANK], 0))
    extra_at = pl.BlockSpec((half, columns), lambda i, tab: (nodes - 1, 0))
    full = pl.BlockSpec((half, columns), lambda i, tab: (0, 0))
    out = jax.ShapeDtypeStruct((half, columns), bf16)
    return pl.pallas_call(
        functools.partial(close_kernel, begin),
        grid_spec=pltpu.PrefetchScalarGridSpec(
            num_scalar_prefetch=1,
            grid=(1,),
            in_specs=[own_at, own_at, extra_at, extra_at]
            + [full] * 4
            + [pl.BlockSpec(own.shape, lambda i, tab: (0, 0, 0))],
            out_specs=[full, full],
        ),
        out_shape=[out, out],
        compiler_params=params(),
        cost_estimate=cost(0, 24 * half * columns),
        name="close",
    )(tab, mine, theirs, mine, theirs, got_f[-1], got_f[-2], got_b[-1], got_b[-2], own)


def finish_kernel(parts, tab, *refs):
    kept, got, out = refs[:parts], refs[parts : 2 * parts], refs[-1]
    half, columns = kept[0].shape
    first = tab[CORE] == 0
    row = tab[CORE] * (2 * half) + lax.broadcasted_iota(i32, (half, 1), 0)
    for p in range(parts):
        cols = slice(p * columns, (p + 1) * columns)
        low = jnp.where(first, kept[p][...], got[p][...])
        high = jnp.where(first, got[p][...], kept[p][...])
        zero = jnp.zeros_like(low)
        out[:half, cols] = jnp.where(row < tab[LIVE], low, zero)
        out[half:, cols] = jnp.where(row + half < tab[LIVE], high, zero)


def finish(tab, kept, got):
    half, columns = kept[0].shape
    return pl.pallas_call(
        functools.partial(finish_kernel, len(kept)),
        in_specs=[smem()] + [whole()] * (2 * len(kept)),
        out_specs=whole(),
        out_shape=jax.ShapeDtypeStruct((2 * half, columns * len(kept)), bf16),
        compiler_params=params(),
        cost_estimate=cost(0, 8 * half * columns * len(kept)),
        name="finish",
    )(tab, *kept, *got)


attention_parts = 2
contract_parts = 2


def on_device(
    order,
    queries,
    latent_cache,
    new_latent,
    span_len,
    dec_count,
    span_start,
    cache_len,
    value_weight,
    out_weight,
    residual,
    norm_gain,
    gate_weight,
    up_weight,
    down_weight,
):
    ranks = len(order)
    reach = ranks // 2
    cores = lax.axis_size("head")
    rows_dev, width = residual.shape
    half = rows_dev // 2 // cores
    features = out_weight.shape[1]
    table = Table(ranks, cache_len.shape[1])

    forward = [(order[i], order[(i + 1) % ranks]) for i in range(ranks)]
    backward = [(b, a) for a, b in forward]
    exchange = [(c, cores - 1 - c) for c in range(cores)]

    def send_next(x):
        return lax.ppermute(x, "blk", forward)

    def send_prev(x):
        return lax.ppermute(x, "blk", backward)

    def swap(x):
        return lax.ppermute(x, "head", exchange)

    ids = jnp.stack([lax.axis_index("blk"), lax.axis_index("head")]).astype(i32)
    at = jnp.asarray([order.index(i) for i in range(ranks)], i32)
    who = jnp.asarray(order, i32)
    tab = pl.pallas_call(
        functools.partial(table_kernel, table, ranks),
        in_specs=[smem()] * 7,
        out_specs=smem(),
        out_shape=jax.ShapeDtypeStruct((table.size,), i32),
        name="table",
    )(ids, span_len, dec_count, span_start, cache_len, at, who)

    packed = pack(tab, residual, ranks, cores)
    res = [packed[0]]
    for shift in range(1, ranks):
        pairs = [(i, (i + shift) % ranks) for i in range(ranks)]
        res.append(lax.ppermute(packed[shift], "blk", pairs))

    total, halves = None, None
    gathered = []
    for part in range(attention_parts):
        main, extra = attend(
            tab, queries, latent_cache, new_latent, value_weight, part, attention_parts
        )
        behind, ahead = [], []
        for step in range(reach):
            if step == 0:
                (out_f,), out_b = route(tab, (extra, main)), main
            elif step == 1:
                out_f, out_b = route(tab, (main, behind[0]), (extra, ahead[0]))
            else:
                out_f, out_b = route(
                    tab,
                    (behind[step - 2], behind[step - 1]),
                    (ahead[step - 2], ahead[step - 1]),
                )
            behind.append(send_next(out_f))
            ahead.append(send_prev(out_b))
        gathered.append([main] + behind + ahead + [extra])
    for part in range(attention_parts):
        total = project(
            tab, table, gathered[part], total, out_weight, part, attention_parts, cores
        )
    kept, given = total
    stream = stream_of(tab, kept, swap(given), res)

    gain = norm_gain.reshape(ranks, 1, features)
    sums = expand(tab, [stream], [swap(stream)], [RANK], gain, gate_weight, up_weight, None, False)
    blocks, owners = [stream], [RANK]
    fore, back = stream, stream
    for step in range(1, reach + 1):
        back = send_next(back)
        arrived, from_owner = [back], [table.owner_back + step]
        if step < reach:
            fore = send_prev(fore)
            arrived, from_owner = [back, fore], from_owner + [table.owner_fore + step]
        others = [swap(x) for x in arrived]
        sums = expand(
            tab, arrived, others, from_owner, gain, gate_weight, up_weight, sums, step == reach
        )
        blocks += arrived
        owners += from_owner
    (hidden,) = sums
    own = collect(tab, blocks, owners, half)

    parts = contract_parts
    mine, theirs = [], []
    for part in range(parts):
        a, b = contract(hidden, down_weight, part, parts)
        mine.append(a)
        theirs.append(swap(b))
    kept_out, got_out = [], []
    for part in range(parts):
        got_f, got_b = [], []
        for step in range(1, reach + 1):
            if step == 1:
                got = []
            elif step == 2:
                got = [got_f[0], got_b[0]]
            else:
                got = [got_f[step - 3], got_f[step - 2], got_b[step - 3], got_b[step - 2]]
            out_f, out_b = add(tab, table, step, mine[part], theirs[part], got, half)
            got_f.append(send_next(out_f))
            got_b.append(send_prev(out_b))
        a, b = close(
            tab, mine[part], theirs[part], got_f, got_b, own, part * (ranks // parts), half
        )
        kept_out.append(a)
        got_out.append(swap(b))
    return finish(tab, kept_out, got_out)


def solution(mesh):
    placed = (
        P(("groups", "blk"), "head"),
        P(("groups", "blk"), None, None),
        P(None, ("groups", "blk")),
        P("groups"),
        P("groups"),
        P(("groups", "blk")),
        P(("groups", "blk"), None),
        P("head", None, None),
        P("head", "blk"),
        P(("groups", "blk"), None),
        P(),
        P(None, ("blk", "head")),
        P(None, ("blk", "head")),
        P(("blk", "head"), None),
    )
    order = ring_order(mesh)
    return jax.shard_map(
        lambda *args: on_device(order, *args),
        mesh=mesh,
        in_specs=placed,
        out_specs=P(("groups", "blk", "head"), None),
        check_vma=False,
    )
```

time: 422 us -> 199 us (0.47)
  waiting for transfers between devices: 294 us -> 43.8 us
  matrix products: 62 us -> 0 us
  Pallas kernels: 0 us -> 52.2 us
  starting transfers between devices: 0.31 us -> 49.5 us
  local copies, waits for them, and re-layouts: 9.72 us -> 51.1 us
  blocking collectives: 29.5 us -> 0 us
  between operations: 14 us -> 1.14 us
  other arithmetic: 12.1 us -> 0.57 us
    all_gather x2 -> x0, waiting for transfers between devices: 187 us -> none  [the longest x1 111 us: on_device(): row_piece = lax.all_gather(normed, 'blk', axis=0, tiled=True)]
    reduce_scatter x1 -> x0, waiting for transfers between devices: 89.4 us -> none  [on_device(): lax.psum_scatter(padded_term(hidden, down_weight).astype(jnp.bfloat16), (...]
    dot_general x11 -> x0, matrix products: 62 us -> none  [the longest x1 27.8 us: padded_term(): return jnp.dot(hidden, down_weight, preferred_element_type=jnp.float32)]
    pallas_call x0 -> x34, Pallas kernels: none -> 52.2 us  [the longest x5 14.3 us: expand(): pl.pallas_call(functools.partial(expand_kernel, count, first, final, gate...]
    ppermute x0 -> x59, starting transfers between devices: none -> 49.5 us  [the longest x20 25.7 us: send_next(): return lax.ppermute(x, 'blk', forward)]
    unnamed x14 -> x43, local copies, waits for them, and re-layouts: 3 us -> 51.1 us
    ppermute x0 -> x59, waiting for transfers between devices: none -> 43.8 us  [the longest x20 20.2 us: send_next(): return lax.ppermute(x, 'blk', forward)]
    all_to_all x1 -> x0, blocking collectives: 29.5 us -> none  [on_device(): lax.all_to_all(summed_out.astype(jnp.bfloat16), 'blk', split_axis=0, conc...]
  transfers between devices with their start and end apart: 4 -> 59, of which waited for: 4 -> 23; matrix products, arithmetic and copies ran while one was open for 0% -> 12% of each run, Pallas kernels for 0% -> 18%
where the time goes in v2:
time: 199 us; the launch traced here: 198 us
  Pallas kernels  52.2 us (26%)
  local copies, waits for them, and re-layouts  51.1 us (26%)
  starting transfers between devices  49.5 us (25%)
  waiting for transfers between devices  43.8 us (22%)
    unnamed x43, local copies, waits for them, and re-layouts  51.1 us
    ppermute x20, starting transfers between devices, send_next(): return lax.ppermute(x, 'blk', forward)  25.7 us
    ppermute x20, waiting for transfers between devices, send_next(): return lax.ppermute(x, 'blk', forward)  20.2 us
    ppermute x19, starting transfers between devices, send_prev(): return lax.ppermute(x, 'blk', backward)  14.8 us
    pallas_call x5, Pallas kernels, expand(): pl.pallas_call(functools.partial(expand_kernel, count, first, final, gate...  14.3 us
    ppermute x19, waiting for transfers between devices, send_prev(): return lax.ppermute(x, 'blk', backward)  12.4 us
    pallas_call x2, Pallas kernels, attend(): pl.pallas_call(functools.partial(attend_kernel, heads, group, rows, lat,...  12 us
    ppermute x7, waiting for transfers between devices, on_device(): res.append(lax.ppermute(packed[shift], 'blk', pairs))  9.83 us
  transfers between devices with their start and end apart: 59, of which 23 were waited for; matrix products, arithmetic and copies ran while one was open for 12% of the time, Pallas kernels for 18%

profile of v2, /device:TPU:0, one launch (start us, length us, event | category | flops | bytes accessed | tf_op | source)
XLA Modules:
  0.0 198.3 jit_solution(3032723957955625433)
XLA Ops:
  0.7 1.0 copy.17.fresh
  2.2 1.3 table.1.tab
  3.6 2.2 %copy-done.5 = bf16[32,512,128]{2,1,0:T(8,128)(2,1)S(1)} copy-done((bf16[32,512,128]{2,1,0:T(8,128)(2,1)S(1)}, bf16[32,512,128]{2,1,0:T(8,128)(2,1)}, u32[]{:S(2)}) %copy-start.5) | copy-done | bytes 4194328
  5.8 1.7 copy-done.6
  7.4 1.7 copy-done.7
  9.7 6.0 %attend.3 = (bf16[32,2048]{1,0:T(8,128)(2,1)S(1)}, bf16[32,2048]{1,0:T(8,128)(2,1)S(1)}) custom-call(s32[44]{0:T(128)S(1)} %copy-done.10, bf16[64,18432]{1,0:T(8,128)(2,1)S(1)} %copy-done.6, bf16[8,576,256]{2,1,0:T(8,128)(2,1)S(1)} %copy-done.7, bf16[576,64]{1,0:T(8,128)(2,1)S(1)} %copy.17.fresh, bf16[32,512,128]{2,1,0:T(8,128)(2,1)S(1)} %copy-done.5), custom_call_target="tpu_custom_call" | custom-call | flops 713031680 | bytes 5636096 | tf_op jit(solution)/shard_map/attend/pallas_call | solution.py:233
  16.3 3.1 %collective-permute-start.8 = (bf16[32,2048]{1,0:T(8,128)(2,1)S(1)}, bf16[32,2048]{1,0:T(8,128)(2,1)S(1)}, u32[]{:S(2)}, u32[]{:S(2)}) collective-permute-start(bf16[32,2048]{1,0:T(8,128)(2,1)S(1)} %route.12), channel_id=1, source_target_pairs={{0,4},{4,8},{8,12},{12,14},{14,10},{10,6},{6,2},{2,0},{1,5},{5,9},... | collective-permute-start | bytes 393224 | tf_op jit(solution)/shard_map/ppermute | solution.py:734
  19.4 6.0 %attend.2 = (bf16[32,2048]{1,0:T(8,128)(2,1)S(1)}, bf16[32,2048]{1,0:T(8,128)(2,1)S(1)}) custom-call(s32[44]{0:T(128)S(1)} %copy-done.10, bf16[64,18432]{1,0:T(8,128)(2,1)S(1)} %copy-done.6, bf16[8,576,256]{2,1,0:T(8,128)(2,1)S(1)} %copy-done.7, bf16[576,64]{1,0:T(8,128)(2,1)S(1)} %copy.17.fresh, bf16[32,512,128]{2,1,0:T(8,128)(2,1)S(1)} %copy-done.5), custom_call_target="tpu_custom_call" | custom-call | flops 713031680 | bytes 5636096 | tf_op jit(solution)/shard_map/attend/pallas_call | solution.py:233
  25.9 2.1 %collective-permute-start = (bf16[32,2048]{1,0:T(8,128)(2,1)S(1)}, bf16[32,2048]{1,0:T(8,128)(2,1)S(1)}, u32[]{:S(2)}, u32[]{:S(2)}) collective-permute-start(bf16[32,2048]{1,0:T(8,128)(2,1)S(1)} %route.8), channel_id=1, source_target_pairs={{0,4},{4,8},{8,12},{12,14},{14,10},{10,6},{6,2},{2,0},{1,5},{5,9},... | collective-permute-start | bytes 393224 | tf_op jit(solution)/shard_map/ppermute | solution.py:734
  28.6 2.1 %collective-permute-start.10 = (bf16[32,2048]{1,0:T(8,128)(2,1)S(1)}, bf16[32,2048]{1,0:T(8,128)(2,1)S(1)}, u32[]{:S(2)}, u32[]{:S(2)}) collective-permute-start(bf16[32,2048]{1,0:T(8,128)(2,1)S(1)} %get-tuple-element.77), channel_id=1, source_target_pairs={{0,4},{4,8},{8,12},{12,14},{14,10},{10,6},{6,2},{2,0},{1,5},{5,9},... | collective-permute-start | bytes 393224 | tf_op jit(solution)/shard_map/ppermute | solution.py:734
  30.7 1.0 collective-permute-done.refs_1_.refs_0_
  31.7 2.5 %collective-permute-done.1.refs_3_.refs_2_.refs_5_ = bf16[32,2048]{1,0:T(8,128)(2,1)S(1)} collective-permute-done((bf16[32,2048]{1,0:T(8,128)(2,1)S(1)}, bf16[32,2048]{1,0:T(8,128)(2,1)S(1)}, u32[]{:S(2)}, u32[]{:S(2)}) %collective-permute-start.1) | collective-permute-done | bytes 131104 | tf_op jit(solution)/shard_map/ppermute | solution.py:737
  34.8 1.6 collective-permute-start.2
  37.5 1.6 collective-permute-start.12
  39.6 1.4 collective-permute-done.2.refs_1_.refs_0_.refs_2_
  41.0 1.3 collective-permute-done.3.refs_3_.refs_2_.refs_6_
  42.9 1.6 collective-permute-start.4
  45.5 1.6 collective-permute-start.14
  48.5 1.9 collective-permute-done.5.refs_3_.refs_7_
  51.0 1.4 collective-permute-start.6
  53.1 2.3 %project.2.refs_10_ = f32[288,896]{1,0:T(8,128)S(1)} custom-call(s32[44]{0:T(128)S(1)} %copy-done.10, bf16[32,2048]{1,0:T(8,128)(2,1)S(1)} %get-tuple-element.75.refs_1_.refs_0_, bf16[32,2048]{1,0:T(8,128)(2,1)S(1)} %collective-permute-done.8.refs_1_.refs_0_, bf16[32,2048]{1,0:T(8,128)(2,1)S(1)} %collective-permute-done.10.refs_1_.refs_0_.refs_2_, ...), custom_call_target="tpu_custom_call" | custom-call | flops 1056964608 | bytes 4849664 | tf_op jit(solution)/shard_map/project/pallas_call | solution.py:388
  56.0 1.3 collective-permute-done.7.refs_8_
  57.3 2.4 %project.3 = (f32[144,896]{1,0:T(8,128)S(1)}, bf16[144,896]{1,0:T(8,128)(2,1)S(1)}) custom-call(s32[44]{0:T(128)S(1)} %copy-done.10, bf16[32,2048]{1,0:T(8,128)(2,1)S(1)} %get-tuple-element.67.refs_1_.refs_0_, bf16[32,2048]{1,0:T(8,128)(2,1)S(1)} %collective-permute-done.refs_1_.refs_0_, bf16[32,2048]{1,0:T(8,128)(2,1)S(1)} %collective-permute-done.2.refs_1_.refs_0_.refs_2_, ...), custom_call_target="tpu_custom_call" | custom-call | flops 1056964608 | bytes 4849664 | tf_op jit(solution)/shard_map/project/pallas_call | solution.py:398
  61.6 0.9 collective-permute-start.19
  62.5 3.5 %collective-permute-start.20 = (bf16[32,896]{1,0:T(8,128)(2,1)S(1)}, bf16[32,896]{1,0:T(8,128)(2,1)S(1)}, u32[]{:S(2)}, u32[]{:S(2)}) collective-permute-start(bf16[32,896]{1,0:T(8,128)(2,1)S(1)} %get-tuple-element.89), channel_id=1, source_target_pairs={{0,8},{2,10},{4,12},{6,14},{8,0},{10,2},{12,4},{14,6},{1,9},{3,11}... | collective-permute-start | bytes 172040 | tf_op jit(solution)/shard_map/ppermute | solution.py:757
  66.0 2.0 collective-permute-done.17.refs_1_
  68.9 3.7 %collective-permute-done.19.refs_3_ = bf16[32,896]{1,0:T(8,128)(2,1)S(1)} collective-permute-done((bf16[32,896]{1,0:T(8,128)(2,1)S(1)}, bf16[32,896]{1,0:T(8,128)(2,1)S(1)}, u32[]{:S(2)}, u32[]{:S(2)}) %collective-permute-start.19) | collective-permute-done | bytes 57376 | tf_op jit(solution)/shard_map/ppermute | solution.py:757
  72.6 2.3 %collective-permute-done.21.refs_5_ = bf16[32,896]{1,0:T(8,128)(2,1)S(1)} collective-permute-done((bf16[32,896]{1,0:T(8,128)(2,1)S(1)}, bf16[32,896]{1,0:T(8,128)(2,1)S(1)}, u32[]{:S(2)}, u32[]{:S(2)}) %collective-permute-start.21) | collective-permute-done | bytes 57376 | tf_op jit(solution)/shard_map/ppermute | solution.py:757
  74.9 1.9 collective-permute-done.23.refs_7_
  77.5 2.0 %collective-permute-start.29 = (bf16[144,896]{1,0:T(8,128)(2,1)S(1)}, bf16[144,896]{1,0:T(8,128)(2,1)S(1)}, u32[]{:S(2)}, u32[]{:S(2)}) collective-permute-start(bf16[144,896]{1,0:T(8,128)(2,1)S(1)} %stream.1.refs_0_.refs_1_), channel_id=1, source_target_pairs={{4,0},{8,4},{12,8},{14,12},{10,14},{6,10},{2,6},{0,2},{5,1},{9,5},... | collective-permute-start | bytes 774152 | tf_op jit(solution)/shard_map/ppermute | solution.py:737
  79.5 4.8 %collective-permute-done.24.refs_0_.refs_2_.refs_3_ = bf16[144,896]{1,0:T(8,128)(2,1)S(1)} collective-permute-done((bf16[144,896]{1,0:T(8,128)(2,1)S(1)}, bf16[144,896]{1,0:T(8,128)(2,1)S(1)}, u32[]{:S(2)}, u32[]{:S(2)}) %collective-permute-start.24) | collective-permute-done | bytes 258080 | tf_op jit(solution)/shard_map/ppermute | solution.py:734
  84.6 1.7 collective-permute-start.30
  86.4 5.0 %collective-permute-done.25.refs_0_.refs_6_.refs_7_ = bf16[144,896]{1,0:T(8,128)(2,1)S(1)} collective-permute-done((bf16[144,896]{1,0:T(8,128)(2,1)S(1)}, bf16[144,896]{1,0:T(8,128)(2,1)S(1)}, u32[]{:S(2)}, u32[]{:S(2)}) %collective-permute-start.25) | collective-permute-done | bytes 258080 | tf_op jit(solution)/shard_map/ppermute | solution.py:734
  91.9 2.0 %collective-permute-start.31 = (bf16[144,896]{1,0:T(8,128)(2,1)S(1)}, bf16[144,896]{1,0:T(8,128)(2,1)}, u32[]{:S(2)}, u32[]{:S(2)}) collective-permute-start(bf16[144,896]{1,0:T(8,128)(2,1)S(1)} %collective-permute-done.30.refs_1_.refs_8_.refs_9_), channel_id=1, source_target_pairs={{4,0},{8,4},{12,8},{14,12},{10,14},{6,10},{2,6},{0,2},{5,1},{9,5},... | collective-permute-start | bytes 774152 | tf_op jit(solution)/shard_map/ppermute | solution.py:737
  93.9 4.7 %collective-permute-done.26.refs_0_.refs_10_.refs_11_ = bf16[144,896]{1,0:T(8,128)(2,1)S(1)} collective-permute-done((bf16[144,896]{1,0:T(8,128)(2,1)S(1)}, bf16[144,896]{1,0:T(8,128)(2,1)S(1)}, u32[]{:S(2)}, u32[]{:S(2)}) %collective-permute-start.26) | collective-permute-done | bytes 258080 | tf_op jit(solution)/shard_map/ppermute | solution.py:734
  100.5 12.4 %copy.27.refs_3_.refs_5_ = bf16[7168,576]{1,0:T(8,128)(2,1)} copy(bf16[7168,576]{0,1:T(8,128)(2,1)} %param.27) | data formatting | bytes 16515072 | tf_op args[11]
  112.8 12.4 %copy.28.refs_4_.refs_6_ = bf16[7168,576]{1,0:T(8,128)(2,1)} copy(bf16[7168,576]{0,1:T(8,128)(2,1)} %param.28) | data formatting | bytes 16515072 | tf_op args[12]
  126.5 3.6 %copy-done = bf16[7168,576]{1,0:T(8,128)(2,1)S(1)} copy-done((bf16[7168,576]{1,0:T(8,128)(2,1)S(1)}, bf16[7168,576]{1,0:T(8,128)(2,1)}, u32[]{:S(2)}) %copy-start) | copy-done | bytes 8257560
  130.1 3.6 %copy-done.2 = bf16[7168,576]{1,0:T(8,128)(2,1)S(1)} copy-done((bf16[7168,576]{1,0:T(8,128)(2,1)S(1)}, bf16[7168,576]{1,0:T(8,128)(2,1)}, u32[]{:S(2)}) %copy-start.2) | copy-done | bytes 8257560
  133.7 0.9 copy-done.17
  134.7 1.6 expand.5
  136.3 1.9 copy-done.1
  138.3 3.6 %copy-done.3 = bf16[7168,576]{1,0:T(8,128)(2,1)S(1)} copy-done((bf16[7168,576]{1,0:T(8,128)(2,1)S(1)}, bf16[7168,576]{1,0:T(8,128)(2,1)}, u32[]{:S(2)}) %copy-start.3) | copy-done | bytes 8257560
  141.9 2.7 %expand.6 = (f32[288,576]{1,0:T(8,128)S(1)}, f32[288,576]{1,0:T(8,128)S(1)}, f32[288,1]{1,0:T(8,128)S(1)}) custom-call(s32[44]{0:T(128)S(1)} %copy-done.11, bf16[144,896]{1,0:T(8,128)(2,1)S(1)} %collective-permute-done.24.refs_0_.refs_2_.refs_3_, bf16[144,896]{1,0:T(8,128)(2,1)S(1)} %collective-permute-done.29.refs_1_.refs_4_.refs_5_, ...), custom_call_target="tpu_custom_call" | custom-call | flops 1189085184 | bytes 5160960 | tf_op jit(solution)/shard_map/expand/pallas_call | solution.py:506
  144.6 3.8 %expand.7 = (f32[288,576]{1,0:T(8,128)S(1)}, f32[288,576]{1,0:T(8,128)S(1)}, f32[288,1]{1,0:T(8,128)S(1)}) custom-call(s32[44]{0:T(128)S(1)} %copy-done.11, bf16[144,896]{1,0:T(8,128)(2,1)S(1)} %collective-permute-done.25.refs_0_.refs_6_.refs_7_, bf16[144,896]{1,0:T(8,128)(2,1)S(1)} %collective-permute-done.30.refs_1_.refs_8_.refs_9_, ...), custom_call_target="tpu_custom_call" | custom-call | flops 1189085184 | bytes 5160960 | tf_op jit(solution)/shard_map/expand/pallas_call | solution.py:506
  148.4 3.7 %expand.8 = (f32[288,576]{1,0:T(8,128)S(1)}, f32[288,576]{1,0:T(8,128)S(1)}, f32[288,1]{1,0:T(8,128)S(1)}) custom-call(s32[44]{0:T(128)S(1)} %copy-done.11, bf16[144,896]{1,0:T(8,128)(2,1)S(1)} %collective-permute-done.26.refs_0_.refs_10_.refs_11_, bf16[144,896]{1,0:T(8,128)(2,1)} %collective-permute-done.31.refs_1_.refs_12_.refs_13_, ...), custom_call_target="tpu_custom_call" | custom-call | flops 1189085184 | bytes 5160960 | tf_op jit(solution)/shard_map/expand/pallas_call | solution.py:506
  152.1 2.6 %expand.9.hidden = bf16[288,576]{1,0:T(8,128)(2,1)S(1)} custom-call(s32[44]{0:T(128)S(1)} %copy-done.11, bf16[144,896]{1,0:T(8,128)(2,1)} %collective-permute-done.27.refs_0_.refs_14_.refs_15_, bf16[144,896]{1,0:T(8,128)(2,1)S(1)} %collective-permute-done.28.refs_1_, f32[8,1,896]{2,1,0:T(1,128)S(1)} %bitcast.9, bf16[7168,576]{1,0:T(8,128)(2,1)S(1)} %copy-done.1, ...), custom_call_target="tpu_custom_call" | custom-call | flops 594542592 | bytes 2580480 | tf_op jit(solution)/shard_map/expand/pallas_call | solution.py:506
  154.7 3.3 %copy-done.4 = bf16[576,7168]{1,0:T(8,128)(2,1)S(1)} copy-done((bf16[576,7168]{1,0:T(8,128)(2,1)S(1)}, bf16[576,7168]{1,0:T(8,128)(2,1)}, u32[]{:S(2)}) %copy-start.4) | copy-done | bytes 8257560
  158.1 2.4 %contract.3 = (bf16[144,3584]{1,0:T(8,128)(2,1)S(1)}, bf16[144,3584]{1,0:T(8,128)(2,1)S(1)}) custom-call(bf16[288,576]{1,0:T(8,128)(2,1)S(1)} %expand.9.hidden, bf16[576,7168]{1,0:T(8,128)(2,1)S(1)} %copy-done.4), custom_call_target="tpu_custom_call" | custom-call | flops 1189085184 | bytes 6193152 | tf_op jit(solution)/shard_map/contract/pallas_call | solution.py:571
  160.6 2.4 %contract.2 = (bf16[144,3584]{1,0:T(8,128)(2,1)S(1)}, bf16[144,3584]{1,0:T(8,128)(2,1)S(1)}) custom-call(bf16[288,576]{1,0:T(8,128)(2,1)S(1)} %expand.9.hidden, bf16[576,7168]{1,0:T(8,128)(2,1)S(1)} %copy-done.4), custom_call_target="tpu_custom_call" | custom-call | flops 1189085184 | bytes 6193152 | tf_op jit(solution)/shard_map/contract/pallas_call | solution.py:571
  164.2 2.1 %collective-permute-start.50 = (bf16[16,3584]{1,0:T(8,128)(2,1)S(1)}, bf16[16,3584]{1,0:T(8,128)(2,1)S(1)}, u32[]{:S(2)}, u32[]{:S(2)}) collective-permute-start(bf16[16,3584]{1,0:T(8,128)(2,1)S(1)} %get-tuple-element.119), channel_id=1, source_target_pairs={{4,0},{8,4},{12,8},{14,12},{10,14},{6,10},{2,6},{0,2},{5,1},{9,5},... | collective-permute-start | bytes 344072 | tf_op jit(solution)/shard_map/ppermute | solution.py:737
  167.0 2.0 %collective-permute-start.41 = (bf16[16,3584]{1,0:T(8,128)(2,1)S(1)}, bf16[16,3584]{1,0:T(8,128)(2,1)S(1)}, u32[]{:S(2)}, u32[]{:S(2)}) collective-permute-start(bf16[16,3584]{1,0:T(8,128)(2,1)S(1)} %get-tuple-element.108), channel_id=1, source_target_pairs={{4,0},{8,4},{12,8},{14,12},{10,14},{6,10},{2,6},{0,2},{5,1},{9,5},... | collective-permute-start | bytes 344072 | tf_op jit(solution)/shard_map/ppermute | solution.py:737
  170.2 2.1 %collective-permute-start.51 = (bf16[16,3584]{1,0:T(8,128)(2,1)S(1)}, bf16[16,3584]{1,0:T(8,128)(2,1)S(1)}, u32[]{:S(2)}, u32[]{:S(2)}) collective-permute-start(bf16[16,3584]{1,0:T(8,128)(2,1)S(1)} %get-tuple-element.120), channel_id=1, source_target_pairs={{0,4},{4,8},{8,12},{12,14},{14,10},{10,6},{6,2},{2,0},{1,5},{5,9},... | collective-permute-start | bytes 344072 | tf_op jit(solution)/shard_map/ppermute | solution.py:734
  173.0 2.1 %collective-permute-start.42 = (bf16[16,3584]{1,0:T(8,128)(2,1)S(1)}, bf16[16,3584]{1,0:T(8,128)(2,1)S(1)}, u32[]{:S(2)}, u32[]{:S(2)}) collective-permute-start(bf16[16,3584]{1,0:T(8,128)(2,1)S(1)} %get-tuple-element.109), channel_id=1, source_target_pairs={{0,4},{4,8},{8,12},{12,14},{14,10},{10,6},{6,2},{2,0},{1,5},{5,9},... | collective-permute-start | bytes 344072 | tf_op jit(solution)/shard_map/ppermute | solution.py:734
  175.3 2.7 %collective-permute-done.52.refs_3_.refs_2_ = bf16[16,3584]{1,0:T(8,128)(2,1)S(1)} collective-permute-done((bf16[16,3584]{1,0:T(8,128)(2,1)S(1)}, bf16[16,3584]{1,0:T(8,128)(2,1)S(1)}, u32[]{:S(2)}, u32[]{:S(2)}) %collective-permute-start.52) | collective-permute-done | bytes 114720 | tf_op jit(solution)/shard_map/ppermute | solution.py:737
  178.7 2.1 %collective-permute-start.53 = (bf16[16,3584]{1,0:T(8,128)(2,1)S(1)}, bf16[16,3584]{1,0:T(8,128)(2,1)S(1)}, u32[]{:S(2)}, u32[]{:S(2)}) collective-permute-start(bf16[16,3584]{1,0:T(8,128)(2,1)S(1)} %get-tuple-element.122), channel_id=1, source_target_pairs={{0,4},{4,8},{8,12},{12,14},{14,10},{10,6},{6,2},{2,0},{1,5},{5,9},... | collective-permute-start | bytes 344072 | tf_op jit(solution)/shard_map/ppermute | solution.py:734
  181.4 2.1 %collective-permute-start.44 = (bf16[16,3584]{1,0:T(8,128)(2,1)S(1)}, bf16[16,3584]{1,0:T(8,128)(2,1)S(1)}, u32[]{:S(2)}, u32[]{:S(2)}) collective-permute-start(bf16[16,3584]{1,0:T(8,128)(2,1)S(1)} %get-tuple-element.111), channel_id=1, source_target_pairs={{0,4},{4,8},{8,12},{12,14},{14,10},{10,6},{6,2},{2,0},{1,5},{5,9},... | collective-permute-start | bytes 344072 | tf_op jit(solution)/shard_map/ppermute | solution.py:734
  183.9 1.8 collective-permute-done.54.refs_3_.b_prev
  186.4 0.9 collective-permute-start.55
  187.3 1.2 collective-permute-start.56
  190.0 1.2 collective-permute-start.47
  191.2 1.4 collect.1.own
  195.6 1.3 collective-permute-done.57.refs_2_
  196.9 1.4 finish.1
  (133 shorter events, 28.3 us)
Async XLA Ops:
  9.7 43.4 %slice-start = ((s8[7340032]{0:T(1024)(128)(4,1)}), s8[4194304]{0:T(1024)(128)(4,1)S(1)}, s32[]{:S(2)}) async-start(s8[7340032]{0:T(1024)(128)(4,1)} %bitcast.3), calls=%async_computation | async-start | bytes 8388608
  16.3 36.8 %slice-start.1 = ((s8[7340032]{0:T(1024)(128)(4,1)}), s8[3145728]{0:T(1024)(128)(4,1)S(1)}, s32[]{:S(2)}) async-start(s8[7340032]{0:T(1024)(128)(4,1)} %bitcast.3), calls=%async_computation.1 | async-start | bytes 6291456
  16.3 11.7 %collective-permute-start.8 = (bf16[32,2048]{1,0:T(8,128)(2,1)S(1)}, bf16[32,2048]{1,0:T(8,128)(2,1)S(1)}, u32[]{:S(2)}, u32[]{:S(2)}) collective-permute-start(bf16[32,2048]{1,0:T(8,128)(2,1)S(1)} %route.12), channel_id=1, source_target_pairs={{0,4},{4,8},{8,12},{12,14},{14,10},{10,6},{6,2},{2,0},{1,5},{5,9},... | collective-permute-start | bytes 393224 | tf_op jit(solution)/shard_map/ppermute | solution.py:734
  19.3 8.7 %collective-permute-start.9 = (bf16[32,2048]{1,0:T(8,128)(2,1)S(1)}, bf16[32,2048]{1,0:T(8,128)(2,1)S(1)}, u32[]{:S(2)}, u32[]{:S(2)}) collective-permute-start(bf16[32,2048]{1,0:T(8,128)(2,1)S(1)} %get-tuple-element.75.refs_1_.refs_0_), channel_id=1, source_target_pairs={{4,0},{8,4},{12,8},{14,12},{10,14},{6,10},{2,6},{0,2},{5,1},{9,5},... | collective-permute-start | bytes 393224 | tf_op jit(solution)/shard_map/ppermute | solution.py:737
  25.9 5.8 %collective-permute-start = (bf16[32,2048]{1,0:T(8,128)(2,1)S(1)}, bf16[32,2048]{1,0:T(8,128)(2,1)S(1)}, u32[]{:S(2)}, u32[]{:S(2)}) collective-permute-start(bf16[32,2048]{1,0:T(8,128)(2,1)S(1)} %route.8), channel_id=1, source_target_pairs={{0,4},{4,8},{8,12},{12,14},{14,10},{10,6},{6,2},{2,0},{1,5},{5,9},... | collective-permute-start | bytes 393224 | tf_op jit(solution)/shard_map/ppermute | solution.py:734
  28.0 6.2 %collective-permute-start.1 = (bf16[32,2048]{1,0:T(8,128)(2,1)S(1)}, bf16[32,2048]{1,0:T(8,128)(2,1)S(1)}, u32[]{:S(2)}, u32[]{:S(2)}) collective-permute-start(bf16[32,2048]{1,0:T(8,128)(2,1)S(1)} %get-tuple-element.67.refs_1_.refs_0_), channel_id=1, source_target_pairs={{4,0},{8,4},{12,8},{14,12},{10,14},{6,10},{2,6},{0,2},{5,1},{9,5},... | collective-permute-start | bytes 393224 | tf_op jit(solution)/shard_map/ppermute | solution.py:737
  28.6 8.3 %collective-permute-start.10 = (bf16[32,2048]{1,0:T(8,128)(2,1)S(1)}, bf16[32,2048]{1,0:T(8,128)(2,1)S(1)}, u32[]{:S(2)}, u32[]{:S(2)}) collective-permute-start(bf16[32,2048]{1,0:T(8,128)(2,1)S(1)} %get-tuple-element.77), channel_id=1, source_target_pairs={{0,4},{4,8},{8,12},{12,14},{14,10},{10,6},{6,2},{2,0},{1,5},{5,9},... | collective-permute-start | bytes 393224 | tf_op jit(solution)/shard_map/ppermute | solution.py:734
  30.7 6.3 %collective-permute-start.11 = (bf16[32,2048]{1,0:T(8,128)(2,1)S(1)}, bf16[32,2048]{1,0:T(8,128)(2,1)S(1)}, u32[]{:S(2)}, u32[]{:S(2)}) collective-permute-start(bf16[32,2048]{1,0:T(8,128)(2,1)S(1)} %get-tuple-element.78), channel_id=1, source_target_pairs={{4,0},{8,4},{12,8},{14,12},{10,14},{6,10},{2,6},{0,2},{5,1},{9,5},... | collective-permute-start | bytes 393224 | tf_op jit(solution)/shard_map/ppermute | solution.py:737
  34.8 6.2 %collective-permute-start.2 = (bf16[32,2048]{1,0:T(8,128)(2,1)S(1)}, bf16[32,2048]{1,0:T(8,128)(2,1)S(1)}, u32[]{:S(2)}, u32[]{:S(2)}) collective-permute-start(bf16[32,2048]{1,0:T(8,128)(2,1)S(1)} %get-tuple-element.69), channel_id=1, source_target_pairs={{0,4},{4,8},{8,12},{12,14},{14,10},{10,6},{6,2},{2,0},{1,5},{5,9},... | collective-permute-start | bytes 393224 | tf_op jit(solution)/shard_map/ppermute | solution.py:734
  36.4 5.8 %collective-permute-start.3 = (bf16[32,2048]{1,0:T(8,128)(2,1)S(1)}, bf16[32,2048]{1,0:T(8,128)(2,1)S(1)}, u32[]{:S(2)}, u32[]{:S(2)}) collective-permute-start(bf16[32,2048]{1,0:T(8,128)(2,1)S(1)} %get-tuple-element.70), channel_id=1, source_target_pairs={{4,0},{8,4},{12,8},{14,12},{10,14},{6,10},{2,6},{0,2},{5,1},{9,5},... | collective-permute-start | bytes 393224 | tf_op jit(solution)/shard_map/ppermute | solution.py:737
  37.5 7.5 %collective-permute-start.12 = (bf16[32,2048]{1,0:T(8,128)(2,1)S(1)}, bf16[32,2048]{1,0:T(8,128)(2,1)S(1)}, u32[]{:S(2)}, u32[]{:S(2)}) collective-permute-start(bf16[32,2048]{1,0:T(8,128)(2,1)S(1)} %get-tuple-element.79), channel_id=1, source_target_pairs={{0,4},{4,8},{8,12},{12,14},{14,10},{10,6},{6,2},{2,0},{1,5},{5,9},... | collective-permute-start | bytes 393224 | tf_op jit(solution)/shard_map/ppermute | solution.py:734
  39.1 5.8 %collective-permute-start.13 = (bf16[32,2048]{1,0:T(8,128)(2,1)S(1)}, bf16[32,2048]{1,0:T(8,128)(2,1)S(1)}, u32[]{:S(2)}, u32[]{:S(2)}) collective-permute-start(bf16[32,2048]{1,0:T(8,128)(2,1)S(1)} %get-tuple-element.80), channel_id=1, source_target_pairs={{4,0},{8,4},{12,8},{14,12},{10,14},{6,10},{2,6},{0,2},{5,1},{9,5},... | collective-permute-start | bytes 393224 | tf_op jit(solution)/shard_map/ppermute | solution.py:737
  42.9 5.6 %collective-permute-start.4 = (bf16[32,2048]{1,0:T(8,128)(2,1)S(1)}, bf16[32,2048]{1,0:T(8,128)(2,1)S(1)}, u32[]{:S(2)}, u32[]{:S(2)}) collective-permute-start(bf16[32,2048]{1,0:T(8,128)(2,1)S(1)} %get-tuple-element.71), channel_id=1, source_target_pairs={{0,4},{4,8},{8,12},{12,14},{14,10},{10,6},{6,2},{2,0},{1,5},{5,9},... | collective-permute-start | bytes 393224 | tf_op jit(solution)/shard_map/ppermute | solution.py:734
  44.5 5.9 %collective-permute-start.5 = (bf16[32,2048]{1,0:T(8,128)(2,1)S(1)}, bf16[32,2048]{1,0:T(8,128)(2,1)S(1)}, u32[]{:S(2)}, u32[]{:S(2)}) collective-permute-start(bf16[32,2048]{1,0:T(8,128)(2,1)S(1)} %get-tuple-element.72), channel_id=1, source_target_pairs={{4,0},{8,4},{12,8},{14,12},{10,14},{6,10},{2,6},{0,2},{5,1},{9,5},... | collective-permute-start | bytes 393224 | tf_op jit(solution)/shard_map/ppermute | solution.py:737
  45.5 7.5 %collective-permute-start.14 = (bf16[32,2048]{1,0:T(8,128)(2,1)S(1)}, bf16[32,2048]{1,0:T(8,128)(2,1)S(1)}, u32[]{:S(2)}, u32[]{:S(2)}) collective-permute-start(bf16[32,2048]{1,0:T(8,128)(2,1)S(1)} %get-tuple-element.81), channel_id=1, source_target_pairs={{0,4},{4,8},{8,12},{12,14},{14,10},{10,6},{6,2},{2,0},{1,5},{5,9},... | collective-permute-start | bytes 393224 | tf_op jit(solution)/shard_map/ppermute | solution.py:734
  47.2 5.9 %collective-permute-start.15 = (bf16[32,2048]{1,0:T(8,128)(2,1)S(1)}, bf16[32,2048]{1,0:T(8,128)(2,1)S(1)}, u32[]{:S(2)}, u32[]{:S(2)}) collective-permute-start(bf16[32,2048]{1,0:T(8,128)(2,1)S(1)} %get-tuple-element.82), channel_id=1, source_target_pairs={{4,0},{8,4},{12,8},{14,12},{10,14},{6,10},{2,6},{0,2},{5,1},{9,5},... | collective-permute-start | bytes 393224 | tf_op jit(solution)/shard_map/ppermute | solution.py:737
  51.0 5.0 %collective-permute-start.6 = (bf16[32,2048]{1,0:T(8,128)(2,1)S(1)}, bf16[32,2048]{1,0:T(8,128)(2,1)S(1)}, u32[]{:S(2)}, u32[]{:S(2)}) collective-permute-start(bf16[32,2048]{1,0:T(8,128)(2,1)S(1)} %get-tuple-element.73), channel_id=1, source_target_pairs={{0,4},{4,8},{8,12},{12,14},{14,10},{10,6},{6,2},{2,0},{1,5},{5,9},... | collective-permute-start | bytes 393224 | tf_op jit(solution)/shard_map/ppermute | solution.py:734
  52.3 7.5 %copy-start.8 = (bf16[64,7168]{1,0:T(8,128)(2,1)S(1)}, bf16[64,7168]{1,0:T(8,128)(2,1)}, u32[]{:S(2)}) copy-start(bf16[64,7168]{1,0:T(8,128)(2,1)} %res.1) | copy-start | bytes 2752516
  52.3 5.0 %collective-permute-start.7 = (bf16[32,2048]{1,0:T(8,128)(2,1)S(1)}, bf16[32,2048]{1,0:T(8,128)(2,1)S(1)}, u32[]{:S(2)}, u32[]{:S(2)}) collective-permute-start(bf16[32,2048]{1,0:T(8,128)(2,1)S(1)} %get-tuple-element.74), channel_id=1, source_target_pairs={{4,0},{8,4},{12,8},{14,12},{10,14},{6,10},{2,6},{0,2},{5,1},{9,5},... | collective-permute-start | bytes 393224 | tf_op jit(solution)/shard_map/ppermute | solution.py:737
  59.7 17.0 %collective-permute-start.16 = (bf16[144,896]{1,0:T(8,128)(2,1)S(1)}, bf16[144,896]{1,0:T(8,128)(2,1)S(1)}, u32[]{:S(2)}, u32[]{:S(2)}) collective-permute-start(bf16[144,896]{1,0:T(8,128)(2,1)S(1)} %get-tuple-element.84), channel_id=1, source_target_pairs={{0,1},{1,0},{2,3},{3,2},{4,5},{5,4},{6,7},{7,6},{8,9},{9,8},{10,11... | collective-permute-start | bytes 774152 | tf_op jit(solution)/shard_map/ppermute | solution.py:740
  60.4 7.6 %collective-permute-start.17 = (bf16[32,896]{1,0:T(8,128)(2,1)S(1)}, bf16[32,896]{1,0:T(8,128)(2,1)S(1)}, u32[]{:S(2)}, u32[]{:S(2)}) collective-permute-start(bf16[32,896]{1,0:T(8,128)(2,1)S(1)} %get-tuple-element.86), channel_id=1, source_target_pairs={{0,2},{2,4},{4,6},{6,8},{8,10},{10,12},{12,14},{14,0},{1,3},{3,5},... | collective-permute-start | bytes 172040 | tf_op jit(solution)/shard_map/ppermute | solution.py:757
  61.2 6.8 %collective-permute-start.18 = (bf16[32,896]{1,0:T(8,128)(2,1)S(1)}, bf16[32,896]{1,0:T(8,128)(2,1)S(1)}, u32[]{:S(2)}, u32[]{:S(2)}) collective-permute-start(bf16[32,896]{1,0:T(8,128)(2,1)S(1)} %get-tuple-element.87), channel_id=1, source_target_pairs={{0,4},{2,6},{4,8},{6,10},{8,12},{10,14},{12,0},{14,2},{1,5},{3,7},... | collective-permute-start | bytes 172040 | tf_op jit(solution)/shard_map/ppermute | solution.py:757
  61.6 10.9 %collective-permute-start.19 = (bf16[32,896]{1,0:T(8,128)(2,1)S(1)}, bf16[32,896]{1,0:T(8,128)(2,1)S(1)}, u32[]{:S(2)}, u32[]{:S(2)}) collective-permute-start(bf16[32,896]{1,0:T(8,128)(2,1)S(1)} %get-tuple-element.88), channel_id=1, source_target_pairs={{0,6},{2,8},{4,10},{6,12},{8,14},{10,0},{12,2},{14,4},{1,7},{3,9},... | collective-permute-start | bytes 172040 | tf_op jit(solution)/shard_map/ppermute | solution.py:757
  62.5 10.0 %collective-permute-start.20 = (bf16[32,896]{1,0:T(8,128)(2,1)S(1)}, bf16[32,896]{1,0:T(8,128)(2,1)S(1)}, u32[]{:S(2)}, u32[]{:S(2)}) collective-permute-start(bf16[32,896]{1,0:T(8,128)(2,1)S(1)} %get-tuple-element.89), channel_id=1, source_target_pairs={{0,8},{2,10},{4,12},{6,14},{8,0},{10,2},{12,4},{14,6},{1,9},{3,11}... | collective-permute-start | bytes 172040 | tf_op jit(solution)/shard_map/ppermute | solution.py:757
  68.0 6.9 %collective-permute-start.21 = (bf16[32,896]{1,0:T(8,128)(2,1)S(1)}, bf16[32,896]{1,0:T(8,128)(2,1)S(1)}, u32[]{:S(2)}, u32[]{:S(2)}) collective-permute-start(bf16[32,896]{1,0:T(8,128)(2,1)S(1)} %get-tuple-element.90), channel_id=1, source_target_pairs={{0,10},{2,12},{4,14},{6,0},{8,2},{10,4},{12,6},{14,8},{1,11},{3,13... | collective-permute-start | bytes 172040 | tf_op jit(solution)/shard_map/ppermute | solution.py:757
  68.0 6.9 %collective-permute-start.22 = (bf16[32,896]{1,0:T(8,128)(2,1)S(1)}, bf16[32,896]{1,0:T(8,128)(2,1)S(1)}, u32[]{:S(2)}, u32[]{:S(2)}) collective-permute-start(bf16[32,896]{1,0:T(8,128)(2,1)S(1)} %get-tuple-element.91), channel_id=1, source_target_pairs={{0,12},{2,14},{4,0},{6,2},{8,4},{10,6},{12,8},{14,10},{1,13},{3,15... | collective-permute-start | bytes 172040 | tf_op jit(solution)/shard_map/ppermute | solution.py:757
  72.6 4.2 %collective-permute-start.23 = (bf16[32,896]{1,0:T(8,128)(2,1)S(1)}, bf16[32,896]{1,0:T(8,128)(2,1)S(1)}, u32[]{:S(2)}, u32[]{:S(2)}) collective-permute-start(bf16[32,896]{1,0:T(8,128)(2,1)S(1)} %get-tuple-element.92), channel_id=1, source_target_pairs={{0,14},{2,0},{4,2},{6,4},{8,6},{10,8},{12,10},{14,12},{1,15},{3,1}... | collective-permute-start | bytes 172040 | tf_op jit(solution)/shard_map/ppermute | solution.py:757
  77.4 6.9 %collective-permute-start.24 = (bf16[144,896]{1,0:T(8,128)(2,1)S(1)}, bf16[144,896]{1,0:T(8,128)(2,1)S(1)}, u32[]{:S(2)}, u32[]{:S(2)}) collective-permute-start(bf16[144,896]{1,0:T(8,128)(2,1)S(1)} %stream.1.refs_0_.refs_1_), channel_id=1, source_target_pairs={{0,4},{4,8},{8,12},{12,14},{14,10},{10,6},{6,2},{2,0},{1,5},{5,9},... | collective-permute-start | bytes 774152 | tf_op jit(solution)/shard_map/ppermute | solution.py:734
  77.5 7.1 %collective-permute-start.29 = (bf16[144,896]{1,0:T(8,128)(2,1)S(1)}, bf16[144,896]{1,0:T(8,128)(2,1)S(1)}, u32[]{:S(2)}, u32[]{:S(2)}) collective-permute-start(bf16[144,896]{1,0:T(8,128)(2,1)S(1)} %stream.1.refs_0_.refs_1_), channel_id=1, source_target_pairs={{4,0},{8,4},{12,8},{14,12},{10,14},{6,10},{2,6},{0,2},{5,1},{9,5},... | collective-permute-start | bytes 774152 | tf_op jit(solution)/shard_map/ppermute | solution.py:737
  84.3 7.0 %collective-permute-start.25 = (bf16[144,896]{1,0:T(8,128)(2,1)S(1)}, bf16[144,896]{1,0:T(8,128)(2,1)S(1)}, u32[]{:S(2)}, u32[]{:S(2)}) collective-permute-start(bf16[144,896]{1,0:T(8,128)(2,1)S(1)} %collective-permute-done.24.refs_0_.refs_2_.refs_3_), channel_id=1, source_target_pairs={{0,4},{4,8},{8,12},{12,14},{14,10},{10,6},{6,2},{2,0},{1,5},{5,9},... | collective-permute-start | bytes 774152 | tf_op jit(solution)/shard_map/ppermute | solution.py:734
  84.6 7.2 %collective-permute-start.30 = (bf16[144,896]{1,0:T(8,128)(2,1)S(1)}, bf16[144,896]{1,0:T(8,128)(2,1)S(1)}, u32[]{:S(2)}, u32[]{:S(2)}) collective-permute-start(bf16[144,896]{1,0:T(8,128)(2,1)S(1)} %collective-permute-done.29.refs_1_.refs_4_.refs_5_), channel_id=1, source_target_pairs={{4,0},{8,4},{12,8},{14,12},{10,14},{6,10},{2,6},{0,2},{5,1},{9,5},... | collective-permute-start | bytes 774152 | tf_op jit(solution)/shard_map/ppermute | solution.py:737
  91.3 7.2 %collective-permute-start.26 = (bf16[144,896]{1,0:T(8,128)(2,1)S(1)}, bf16[144,896]{1,0:T(8,128)(2,1)S(1)}, u32[]{:S(2)}, u32[]{:S(2)}) collective-permute-start(bf16[144,896]{1,0:T(8,128)(2,1)S(1)} %collective-permute-done.25.refs_0_.refs_6_.refs_7_), channel_id=1, source_target_pairs={{0,4},{4,8},{8,12},{12,14},{14,10},{10,6},{6,2},{2,0},{1,5},{5,9},... | collective-permute-start | bytes 774152 | tf_op jit(solution)/shard_map/ppermute | solution.py:734
  91.3 7.2 %collective-permute-start.38 = (bf16[144,896]{1,0:T(8,128)(2,1)S(1)}, bf16[144,896]{1,0:T(8,128)(2,1)S(1)}, u32[]{:S(2)}, u32[]{:S(2)}) collective-permute-start(bf16[144,896]{1,0:T(8,128)(2,1)S(1)} %stream.1.refs_0_.refs_1_), channel_id=1, source_target_pairs={{0,1},{1,0},{2,3},{3,2},{4,5},{5,4},{6,7},{7,6},{8,9},{9,8},{10,11... | collective-permute-start | bytes 774152 | tf_op jit(solution)/shard_map/ppermute | solution.py:740
  91.3 7.9 %collective-permute-start.36 = (bf16[144,896]{1,0:T(8,128)(2,1)S(1)}, bf16[144,896]{1,0:T(8,128)(2,1)S(1)}, u32[]{:S(2)}, u32[]{:S(2)}) collective-permute-start(bf16[144,896]{1,0:T(8,128)(2,1)S(1)} %collective-permute-done.24.refs_0_.refs_2_.refs_3_), channel_id=1, source_target_pairs={{0,1},{1,0},{2,3},{3,2},{4,5},{5,4},{6,7},{7,6},{8,9},{9,8},{10,11... | collective-permute-start | bytes 774152 | tf_op jit(solution)/shard_map/ppermute | solution.py:740
  91.9 33.4 %collective-permute-start.37 = (bf16[144,896]{1,0:T(8,128)(2,1)S(1)}, bf16[144,896]{1,0:T(8,128)(2,1)S(1)}, u32[]{:S(2)}, u32[]{:S(2)}) collective-permute-start(bf16[144,896]{1,0:T(8,128)(2,1)S(1)} %collective-permute-done.29.refs_1_.refs_4_.refs_5_), channel_id=1, source_target_pairs={{0,1},{1,0},{2,3},{3,2},{4,5},{5,4},{6,7},{7,6},{8,9},{9,8},{10,11... | collective-permute-start | bytes 774152 | tf_op jit(solution)/shard_map/ppermute | solution.py:740
  91.9 34.1 %collective-permute-start.31 = (bf16[144,896]{1,0:T(8,128)(2,1)S(1)}, bf16[144,896]{1,0:T(8,128)(2,1)}, u32[]{:S(2)}, u32[]{:S(2)}) collective-permute-start(bf16[144,896]{1,0:T(8,128)(2,1)S(1)} %collective-permute-done.30.refs_1_.refs_8_.refs_9_), channel_id=1, source_target_pairs={{4,0},{8,4},{12,8},{14,12},{10,14},{6,10},{2,6},{0,2},{5,1},{9,5},... | collective-permute-start | bytes 774152 | tf_op jit(solution)/shard_map/ppermute | solution.py:737
  98.6 37.7 %collective-permute-start.27 = (bf16[144,896]{1,0:T(8,128)(2,1)S(1)}, bf16[144,896]{1,0:T(8,128)(2,1)}, u32[]{:S(2)}, u32[]{:S(2)}) collective-permute-start(bf16[144,896]{1,0:T(8,128)(2,1)S(1)} %collective-permute-done.26.refs_0_.refs_10_.refs_11_), channel_id=1, source_target_pairs={{0,4},{4,8},{8,12},{12,14},{14,10},{10,6},{6,2},{2,0},{1,5},{5,9},... | collective-permute-start | bytes 774152 | tf_op jit(solution)/shard_map/ppermute | solution.py:734
  99.3 45.4 %collective-permute-start.34 = (bf16[144,896]{1,0:T(8,128)(2,1)S(1)}, bf16[144,896]{1,0:T(8,128)(2,1)}, u32[]{:S(2)}, u32[]{:S(2)}) collective-permute-start(bf16[144,896]{1,0:T(8,128)(2,1)S(1)} %collective-permute-done.25.refs_0_.refs_6_.refs_7_), channel_id=1, source_target_pairs={{0,1},{1,0},{2,3},{3,2},{4,5},{5,4},{6,7},{7,6},{8,9},{9,8},{10,11... | collective-permute-start | bytes 774152 | tf_op jit(solution)/shard_map/ppermute | solution.py:740
  100.0 44.7 %collective-permute-start.35 = (bf16[144,896]{1,0:T(8,128)(2,1)S(1)}, bf16[144,896]{1,0:T(8,128)(2,1)}, u32[]{:S(2)}, u32[]{:S(2)}) collective-permute-start(bf16[144,896]{1,0:T(8,128)(2,1)S(1)} %collective-permute-done.30.refs_1_.refs_8_.refs_9_), channel_id=1, source_target_pairs={{0,1},{1,0},{2,3},{3,2},{4,5},{5,4},{6,7},{7,6},{8,9},{9,8},{10,11... | collective-permute-start | bytes 774152 | tf_op jit(solution)/shard_map/ppermute | solution.py:740
  112.8 13.6 %copy-start.9 = (f32[7168]{0:T(1024)S(1)}, f32[7168]{0:T(1024)}, u32[]{:S(2)}) copy-start(f32[7168]{0:T(1024)} %param.26) | copy-start | bytes 86020
  112.8 13.6 %copy-start.11 = (s32[44]{0:T(128)S(1)}, s32[44]{0:T(128)}, u32[]{:S(2)}) copy-start(s32[44]{0:T(128)} %table.1.tab) | copy-start | bytes 532
  126.0 22.4 %collective-permute-start.32 = (bf16[144,896]{1,0:T(8,128)(2,1)S(1)}, bf16[144,896]{1,0:T(8,128)(2,1)S(1)}, u32[]{:S(2)}, u32[]{:S(2)}) collective-permute-start(bf16[144,896]{1,0:T(8,128)(2,1)S(1)} %collective-permute-done.26.refs_0_.refs_10_.refs_11_), channel_id=1, source_target_pairs={{0,1},{1,0},{2,3},{3,2},{4,5},{5,4},{6,7},{7,6},{8,9},{9,8},{10,11... | collective-permute-start | bytes 774152 | tf_op jit(solution)/shard_map/ppermute | solution.py:740
  126.0 22.5 %collective-permute-start.33 = (bf16[144,896]{1,0:T(8,128)(2,1)}, bf16[144,896]{1,0:T(8,128)(2,1)S(1)}, u32[]{:S(2)}, u32[]{:S(2)}) collective-permute-start(bf16[144,896]{1,0:T(8,128)(2,1)} %collective-permute-done.31.refs_1_.refs_12_.refs_13_), channel_id=1, source_target_pairs={{0,1},{1,0},{2,3},{3,2},{4,5},{5,4},{6,7},{7,6},{8,9},{9,8},{10,11... | collective-permute-start | bytes 774152 | tf_op jit(solution)/shard_map/ppermute | solution.py:740
  136.3 15.8 %collective-permute-start.28 = (bf16[144,896]{1,0:T(8,128)(2,1)}, bf16[144,896]{1,0:T(8,128)(2,1)S(1)}, u32[]{:S(2)}, u32[]{:S(2)}) collective-permute-start(bf16[144,896]{1,0:T(8,128)(2,1)} %collective-permute-done.27.refs_0_.refs_14_.refs_15_), channel_id=1, source_target_pairs={{0,1},{1,0},{2,3},{3,2},{4,5},{5,4},{6,7},{7,6},{8,9},{9,8},{10,11... | collective-permute-start | bytes 774152 | tf_op jit(solution)/shard_map/ppermute | solution.py:740
  160.5 3.0 %collective-permute-start.48 = (bf16[144,3584]{1,0:T(8,128)(2,1)S(1)}, bf16[144,3584]{1,0:T(8,128)(2,1)S(1)}, u32[]{:S(2)}, u32[]{:S(2)}) collective-permute-start(bf16[144,3584]{1,0:T(8,128)(2,1)S(1)} %get-tuple-element.117), channel_id=1, source_target_pairs={{0,1},{1,0},{2,3},{3,2},{4,5},{5,4},{6,7},{7,6},{8,9},{9,8},{10,11... | collective-permute-start | bytes 3096584 | tf_op jit(solution)/shard_map/ppermute | solution.py:740
  163.0 3.3 %collective-permute-start.39 = (bf16[144,3584]{1,0:T(8,128)(2,1)S(1)}, bf16[144,3584]{1,0:T(8,128)(2,1)S(1)}, u32[]{:S(2)}, u32[]{:S(2)}) collective-permute-start(bf16[144,3584]{1,0:T(8,128)(2,1)S(1)} %get-tuple-element.106), channel_id=1, source_target_pairs={{0,1},{1,0},{2,3},{3,2},{4,5},{5,4},{6,7},{7,6},{8,9},{9,8},{10,11... | collective-permute-start | bytes 3096584 | tf_op jit(solution)/shard_map/ppermute | solution.py:740
  164.1 5.4 %collective-permute-start.49 = (bf16[16,3584]{1,0:T(8,128)(2,1)S(1)}, bf16[16,3584]{1,0:T(8,128)(2,1)S(1)}, u32[]{:S(2)}, u32[]{:S(2)}) collective-permute-start(bf16[16,3584]{1,0:T(8,128)(2,1)S(1)} %get-tuple-element.118), channel_id=1, source_target_pairs={{0,4},{4,8},{8,12},{12,14},{14,10},{10,6},{6,2},{2,0},{1,5},{5,9},... | collective-permute-start | bytes 344072 | tf_op jit(solution)/shard_map/ppermute | solution.py:734
  164.2 5.4 %collective-permute-start.50 = (bf16[16,3584]{1,0:T(8,128)(2,1)S(1)}, bf16[16,3584]{1,0:T(8,128)(2,1)S(1)}, u32[]{:S(2)}, u32[]{:S(2)}) collective-permute-start(bf16[16,3584]{1,0:T(8,128)(2,1)S(1)} %get-tuple-element.119), channel_id=1, source_target_pairs={{4,0},{8,4},{12,8},{14,12},{10,14},{6,10},{2,6},{0,2},{5,1},{9,5},... | collective-permute-start | bytes 344072 | tf_op jit(solution)/shard_map/ppermute | solution.py:737
  166.9 5.5 %collective-permute-start.40 = (bf16[16,3584]{1,0:T(8,128)(2,1)S(1)}, bf16[16,3584]{1,0:T(8,128)(2,1)S(1)}, u32[]{:S(2)}, u32[]{:S(2)}) collective-permute-start(bf16[16,3584]{1,0:T(8,128)(2,1)S(1)} %get-tuple-element.107), channel_id=1, source_target_pairs={{0,4},{4,8},{8,12},{12,14},{14,10},{10,6},{6,2},{2,0},{1,5},{5,9},... | collective-permute-start | bytes 344072 | tf_op jit(solution)/shard_map/ppermute | solution.py:734
  167.0 5.4 %collective-permute-start.41 = (bf16[16,3584]{1,0:T(8,128)(2,1)S(1)}, bf16[16,3584]{1,0:T(8,128)(2,1)S(1)}, u32[]{:S(2)}, u32[]{:S(2)}) collective-permute-start(bf16[16,3584]{1,0:T(8,128)(2,1)S(1)} %get-tuple-element.108), channel_id=1, source_target_pairs={{4,0},{8,4},{12,8},{14,12},{10,14},{6,10},{2,6},{0,2},{5,1},{9,5},... | collective-permute-start | bytes 344072 | tf_op jit(solution)/shard_map/ppermute | solution.py:737
  170.2 5.1 %collective-permute-start.51 = (bf16[16,3584]{1,0:T(8,128)(2,1)S(1)}, bf16[16,3584]{1,0:T(8,128)(2,1)S(1)}, u32[]{:S(2)}, u32[]{:S(2)}) collective-permute-start(bf16[16,3584]{1,0:T(8,128)(2,1)S(1)} %get-tuple-element.120), channel_id=1, source_target_pairs={{0,4},{4,8},{8,12},{12,14},{14,10},{10,6},{6,2},{2,0},{1,5},{5,9},... | collective-permute-start | bytes 344072 | tf_op jit(solution)/shard_map/ppermute | solution.py:734
  172.4 5.7 %collective-permute-start.52 = (bf16[16,3584]{1,0:T(8,128)(2,1)S(1)}, bf16[16,3584]{1,0:T(8,128)(2,1)S(1)}, u32[]{:S(2)}, u32[]{:S(2)}) collective-permute-start(bf16[16,3584]{1,0:T(8,128)(2,1)S(1)} %get-tuple-element.121), channel_id=1, source_target_pairs={{4,0},{8,4},{12,8},{14,12},{10,14},{6,10},{2,6},{0,2},{5,1},{9,5},... | collective-permute-start | bytes 344072 | tf_op jit(solution)/shard_map/ppermute | solution.py:737
  173.0 7.7 %collective-permute-start.42 = (bf16[16,3584]{1,0:T(8,128)(2,1)S(1)}, bf16[16,3584]{1,0:T(8,128)(2,1)S(1)}, u32[]{:S(2)}, u32[]{:S(2)}) collective-permute-start(bf16[16,3584]{1,0:T(8,128)(2,1)S(1)} %get-tuple-element.109), channel_id=1, source_target_pairs={{0,4},{4,8},{8,12},{12,14},{14,10},{10,6},{6,2},{2,0},{1,5},{5,9},... | collective-permute-start | bytes 344072 | tf_op jit(solution)/shard_map/ppermute | solution.py:734
  175.1 5.7 %collective-permute-start.43 = (bf16[16,3584]{1,0:T(8,128)(2,1)S(1)}, bf16[16,3584]{1,0:T(8,128)(2,1)S(1)}, u32[]{:S(2)}, u32[]{:S(2)}) collective-permute-start(bf16[16,3584]{1,0:T(8,128)(2,1)S(1)} %get-tuple-element.110), channel_id=1, source_target_pairs={{4,0},{8,4},{12,8},{14,12},{10,14},{6,10},{2,6},{0,2},{5,1},{9,5},... | collective-permute-start | bytes 344072 | tf_op jit(solution)/shard_map/ppermute | solution.py:737
  178.7 5.3 %collective-permute-start.53 = (bf16[16,3584]{1,0:T(8,128)(2,1)S(1)}, bf16[16,3584]{1,0:T(8,128)(2,1)S(1)}, u32[]{:S(2)}, u32[]{:S(2)}) collective-permute-start(bf16[16,3584]{1,0:T(8,128)(2,1)S(1)} %get-tuple-element.122), channel_id=1, source_target_pairs={{0,4},{4,8},{8,12},{12,14},{14,10},{10,6},{6,2},{2,0},{1,5},{5,9},... | collective-permute-start | bytes 344072 | tf_op jit(solution)/shard_map/ppermute | solution.py:734
  180.8 5.0 %collective-permute-start.54 = (bf16[16,3584]{1,0:T(8,128)(2,1)S(1)}, bf16[16,3584]{1,0:T(8,128)(2,1)S(1)}, u32[]{:S(2)}, u32[]{:S(2)}) collective-permute-start(bf16[16,3584]{1,0:T(8,128)(2,1)S(1)} %get-tuple-element.123), channel_id=1, source_target_pairs={{4,0},{8,4},{12,8},{14,12},{10,14},{6,10},{2,6},{0,2},{5,1},{9,5},... | collective-permute-start | bytes 344072 | tf_op jit(solution)/shard_map/ppermute | solution.py:737
  181.4 7.1 %collective-permute-start.44 = (bf16[16,3584]{1,0:T(8,128)(2,1)S(1)}, bf16[16,3584]{1,0:T(8,128)(2,1)S(1)}, u32[]{:S(2)}, u32[]{:S(2)}) collective-permute-start(bf16[16,3584]{1,0:T(8,128)(2,1)S(1)} %get-tuple-element.111), channel_id=1, source_target_pairs={{0,4},{4,8},{8,12},{12,14},{14,10},{10,6},{6,2},{2,0},{1,5},{5,9},... | collective-permute-start | bytes 344072 | tf_op jit(solution)/shard_map/ppermute | solution.py:734
  183.5 5.0 %collective-permute-start.45 = (bf16[16,3584]{1,0:T(8,128)(2,1)S(1)}, bf16[16,3584]{1,0:T(8,128)(2,1)S(1)}, u32[]{:S(2)}, u32[]{:S(2)}) collective-permute-start(bf16[16,3584]{1,0:T(8,128)(2,1)S(1)} %get-tuple-element.112), channel_id=1, source_target_pairs={{4,0},{8,4},{12,8},{14,12},{10,14},{6,10},{2,6},{0,2},{5,1},{9,5},... | collective-permute-start | bytes 344072 | tf_op jit(solution)/shard_map/ppermute | solution.py:737
  186.4 6.2 %collective-permute-start.55 = (bf16[16,3584]{1,0:T(8,128)(2,1)S(1)}, bf16[16,3584]{1,0:T(8,128)(2,1)S(1)}, u32[]{:S(2)}, u32[]{:S(2)}) collective-permute-start(bf16[16,3584]{1,0:T(8,128)(2,1)S(1)} %get-tuple-element.124), channel_id=1, source_target_pairs={{0,4},{4,8},{8,12},{12,14},{14,10},{10,6},{6,2},{2,0},{1,5},{5,9},... | collective-permute-start | bytes 344072 | tf_op jit(solution)/shard_map/ppermute | solution.py:734
  187.3 5.3 %collective-permute-start.56 = (bf16[16,3584]{1,0:T(8,128)(2,1)S(1)}, bf16[16,3584]{1,0:T(8,128)(2,1)S(1)}, u32[]{:S(2)}, u32[]{:S(2)}) collective-permute-start(bf16[16,3584]{1,0:T(8,128)(2,1)S(1)} %get-tuple-element.125), channel_id=1, source_target_pairs={{4,0},{8,4},{12,8},{14,12},{10,14},{6,10},{2,6},{0,2},{5,1},{9,5},... | collective-permute-start | bytes 344072 | tf_op jit(solution)/shard_map/ppermute | solution.py:737
  189.1 4.8 %collective-permute-start.46 = (bf16[16,3584]{1,0:T(8,128)(2,1)S(1)}, bf16[16,3584]{1,0:T(8,128)(2,1)S(1)}, u32[]{:S(2)}, u32[]{:S(2)}) collective-permute-start(bf16[16,3584]{1,0:T(8,128)(2,1)S(1)} %get-tuple-element.113), channel_id=1, source_target_pairs={{0,4},{4,8},{8,12},{12,14},{14,10},{10,6},{6,2},{2,0},{1,5},{5,9},... | collective-permute-start | bytes 344072 | tf_op jit(solution)/shard_map/ppermute | solution.py:734
  190.0 4.8 %collective-permute-start.47 = (bf16[16,3584]{1,0:T(8,128)(2,1)S(1)}, bf16[16,3584]{1,0:T(8,128)(2,1)S(1)}, u32[]{:S(2)}, u32[]{:S(2)}) collective-permute-start(bf16[16,3584]{1,0:T(8,128)(2,1)S(1)} %get-tuple-element.114), channel_id=1, source_target_pairs={{4,0},{8,4},{12,8},{14,12},{10,14},{6,10},{2,6},{0,2},{5,1},{9,5},... | collective-permute-start | bytes 344072 | tf_op jit(solution)/shard_map/ppermute | solution.py:737
  193.3 2.3 %collective-permute-start.58 = (bf16[16,3584]{1,0:T(8,128)(2,1)S(1)}, bf16[16,3584]{1,0:T(8,128)(2,1)S(1)}, u32[]{:S(2)}, u32[]{:S(2)}) collective-permute-start(bf16[16,3584]{1,0:T(8,128)(2,1)S(1)} %get-tuple-element.128), channel_id=1, source_target_pairs={{0,1},{1,0},{2,3},{3,2},{4,5},{5,4},{6,7},{7,6},{8,9},{9,8},{10,11... | collective-permute-start | bytes 344072 | tf_op jit(solution)/shard_map/ppermute | solution.py:740
  195.5 1.4 collective-permute-start.57
  (15 other events, 34.2 us)

commit v3 on v2

--- a/solution.py
+++ b/solution.py
@@ -123,7 +123,7 @@
 
 def attend_kernel(
     heads, group, rows, lat, cached, value, start_step,
-    tab, q, cache, fresh, vw, main, extra, k0, k1, kpad, dq, dec,
+    tab, q, cache, fresh, vw, main, extra, k0, k1, kpad, dq, dec, turn,
 ):
     pair = 2 * lat
     wide = -(-lat // 128) * 128
@@ -141,11 +141,14 @@
 
     @pl.when(pl.program_id(0) == 0)
     def _():
+        turn[...] = jnp.zeros_like(turn)
+        turn[:rows, :lat] = fresh[...].astype(f32)
+        turned = turn[...].T.astype(bf16)[:lat]
         k0[...] = jnp.zeros_like(k0)
         k1[...] = jnp.zeros_like(k1)
         for ref, off in ((k0, 0), (k1, shift)):
             ref[off : off + lat, :cached] = cache[0]
-            ref[off : off + lat, cached:keys] = fresh[...]
+            ref[off : off + lat, cached:] = turned
         kpad[...] = jnp.zeros_like(kpad)
         for s in range(slots):
             kpad[s, :lat] = cache[s + 1]
@@ -176,7 +179,7 @@
         acc = jnp.zeros((n, value), f32)
         for s in range(slots):
             acc = acc + mm_nt(jnp.where(slot == s, w, 0.0).astype(bf16), cache[s + 1, :value])
-        own_value = mm_nt(pick, fresh[:value])[:dr]
+        own_value = mm(pick, fresh[:, :value])[:dr]
         own_value = jnp.broadcast_to(own_value[None], (heads, dr, value)).reshape(n, value)
         dec[...] = acc + (e_own / total).astype(bf16).astype(f32) * own_value
 
@@ -237,7 +240,7 @@
             smem(),
             pl.BlockSpec((rows, heads * lat), lambda i: (0, part)),
             pl.BlockSpec(cache.shape, lambda i: (0, 0, 0)),
-            pl.BlockSpec(fresh.shape, lambda i: (0, 0)),
+            pl.BlockSpec(fresh.shape[::-1], lambda i: (0, 0)),
             pl.BlockSpec((group, value, vh), lambda i: (part * steps + i, 0, 0)),
         ],
         out_specs=[pl.BlockSpec((rows // 2, group * vh), lambda i: (0, i))] * 2,
@@ -248,15 +251,16 @@
             pltpu.VMEM((slots - 1, wide, cached), bf16),
             pltpu.VMEM((heads * 8, wide), f32),
             pltpu.VMEM((heads * 8, value), f32),
+            pltpu.VMEM((cols - cached, wide), f32),
         ],
-        compiler_params=params(40),
+        compiler_params=params(56),
         cost_estimate=cost(
             2 * rows * heads * (cached + rows) * (lat + value),
             2 * (queries.size // parts + cache.size + vw.size // parts),
             rows * heads * (cached + rows),
         ),
         name="attend",
-    )(tab, queries, cache, fresh, vw)
+    )(tab, queries, cache, fresh.T, vw)
 
 
 def pack_kernel(ranks, features, half, tab, res, *outs):
@@ -443,7 +447,7 @@
     )(tab, kept, other, *res)
 
 
-def expand_kernel(count, first, final, width, tab, *refs):
+def expand_kernel(count, first, final, width, turned, tab, *refs):
     mines, theirs = refs[:count], refs[count : 2 * count]
     refs = refs[2 * count :]
     gain, gate, up = refs[:3]
@@ -460,9 +464,10 @@
         def _(i=i):
             both = jnp.concatenate([mines[i][...], theirs[i][...]], 0).astype(f32)
             scaled = (both * gain[0]).astype(bf16)
+            times = mm_nt if turned else mm
             values = (
-                mm(scaled, gate[...]),
-                mm(scaled, up[...]),
+                times(scaled, gate[...]),
+                times(scaled, up[...]),
                 jnp.sum(both * both, axis=1, keepdims=True),
             )
             for n, (ref, value) in enumerate(zip((gates, ups, squares), values)):
@@ -485,6 +490,7 @@
     rows, features = mines[0].shape
     units = gate.shape[1]
     first = before is None
+    width = gate.shape[0]
 
     def owner(i, tab):
         index = tab[owners[0]]
@@ -498,13 +504,18 @@
     sums = [(2 * rows, units), (2 * rows, units), (2 * rows, 1)]
     ins = [full((rows, features))] * (2 * count)
     ins += [pl.BlockSpec((1, 1, features), lambda i, tab: (owner(i, tab), 0, 0))]
-    ins += [pl.BlockSpec((features, units), lambda i, tab: (owner(i, tab), 0))] * 2
+    turned = features % 128 == 0
+    if turned:
+        gate, up = gate.T, up.T
+        ins += [pl.BlockSpec((units, features), lambda i, tab: (0, owner(i, tab)))] * 2
+    else:
+        ins += [pl.BlockSpec((features, units), lambda i, tab: (owner(i, tab), 0))] * 2
     if not first:
         ins += [full(s) for s in sums]
     shapes = [jax.ShapeDtypeStruct(s, f32) for s in sums]
     out_shapes = [jax.ShapeDtypeStruct((2 * rows, units), bf16)] if final else shapes
     return pl.pallas_call(
-        functools.partial(expand_kernel, count, first, final, gate.shape[0]),
+        functools.partial(expand_kernel, count, first, final, width, turned),
         grid_spec=pltpu.PrefetchScalarGridSpec(
             num_scalar_prefetch=1,
             grid=(count,),
@@ -513,7 +524,7 @@
             scratch_shapes=[pltpu.VMEM(s, f32) for s in sums] if final else [],
         ),
         out_shape=out_shapes,
-        compiler_params=params(),
+        compiler_params=params(56),
         cost_estimate=cost(
             8 * count * rows * features * units, count * (4 * features * units + 4 * rows * features)
         ),
@@ -777,6 +788,8 @@
             behind.append(send_next(out_f))
             ahead.append(send_prev(out_b))
         gathered.append([main] + behind + ahead + [extra])
+    tied = lax.optimization_barrier((gathered[0], res))
+    gathered[0], res = tied
     for part in range(attention_parts):
         total = project(
             tab, table, gathered[part], total, out_weight, part, attention_parts, cores
@@ -788,12 +801,16 @@
     sums = expand(tab, [stream], [swap(stream)], [RANK], gain, gate_weight, up_weight, None, False)
     blocks, owners = [stream], [RANK]
     fore, back = stream, stream
+    cut = -(-stream.shape[0] // 32) * 16
     for step in range(1, reach + 1):
-        back = send_next(back)
-        arrived, from_owner = [back], [table.owner_back + step]
         if step < reach:
-            fore = send_prev(fore)
-            arrived, from_owner = [back, fore], from_owner + [table.owner_fore + step]
+            back, fore = send_next(back), send_prev(fore)
+            arrived = [back, fore]
+            from_owner = [table.owner_back + step, table.owner_fore + step]
+        else:
+            last = [send_next(back[:cut]), send_prev(fore[cut:])]
+            arrived = [jnp.concatenate(last, 0)]
+            from_owner = [table.owner_back + step]
         others = [swap(x) for x in arrived]
         sums = expand(
             tab, arrived, others, from_owner, gain, gate_weight, up_weight, sums, step == reach

time: 199 us -> 183 us (0.920)
  local copies, waits for them, and re-layouts: 51.1 us -> 9.52 us
  Pallas kernels: 52.2 us -> 75.7 us
  starting transfers between devices: 49.5 us -> 55.5 us
  waiting for transfers between devices: 43.8 us -> 40.1 us
    unnamed x43 -> x71, local copies, waits for them, and re-layouts: 51.1 us -> 8.85 us
    pallas_call x5, Pallas kernels: 14.3 us -> 30.6 us  [expand(): pl.pallas_call(functools.partial(expand_kernel, count, first, final, widt...]
    ppermute x20, starting transfers between devices: 25.7 us -> 30.9 us  [send_next(): return lax.ppermute(x, 'blk', forward)]
    pallas_call x2, Pallas kernels: 12 us -> 16.8 us  [attend(): pl.pallas_call(functools.partial(attend_kernel, heads, group, rows, lat,...]
    ppermute x7, waiting for transfers between devices: 9.83 us -> 5.48 us  [on_device(): res.append(lax.ppermute(packed[shift], 'blk', pairs))]
    ppermute x7, starting transfers between devices: 6.49 us -> 9.49 us  [on_device(): res.append(lax.ppermute(packed[shift], 'blk', pairs))]
    ppermute x19 -> x20, starting transfers between devices: 14.8 us -> 12.6 us  [send_prev(): return lax.ppermute(x, 'blk', backward)]
    ppermute x19 -> x20, waiting for transfers between devices: 12.4 us -> 12.6 us  [send_prev(): return lax.ppermute(x, 'blk', backward)]
  transfers between devices with their start and end apart: 59 -> 60, of which waited for: 23 -> 22; matrix products, arithmetic and copies ran while one was open for 12% -> 1% of each run, Pallas kernels for 18% -> 29%
where the time goes in v3:
time: 183 us
  Pallas kernels  75.7 us (41%)
  starting transfers between devices  55.5 us (30%)
  waiting for transfers between devices  40.1 us (22%)
  local copies, waits for them, and re-layouts  9.52 us (5%)
    ppermute x20, starting transfers between devices, send_next(): return lax.ppermute(x, 'blk', forward)  30.9 us
    pallas_call x5, Pallas kernels, expand(): pl.pallas_call(functools.partial(expand_kernel, count, first, final, widt...  30.6 us
    ppermute x20, waiting for transfers between devices, send_next(): return lax.ppermute(x, 'blk', forward)  19.1 us
    pallas_call x2, Pallas kernels, attend(): pl.pallas_call(functools.partial(attend_kernel, heads, group, rows, lat,...  16.8 us
    ppermute x20, waiting for transfers between devices, send_prev(): return lax.ppermute(x, 'blk', backward)  12.6 us
    ppermute x20, starting transfers between devices, send_prev(): return lax.ppermute(x, 'blk', backward)  12.6 us
    ppermute x7, starting transfers between devices, on_device(): res.append(lax.ppermute(packed[shift], 'blk', pairs))  9.49 us
    unnamed x71, local copies, waits for them, and re-layouts  8.85 us
  transfers between devices with their start and end apart: 60, of which 22 were waited for; matrix products, arithmetic and copies ran while one was open for 1% of the time, Pallas kernels for 29%

profile of v3, /device:TPU:0, one launch (start us, length us, event | category | flops | bytes accessed | tf_op | source)
XLA Modules:
  0.0 182.7 jit_solution(11450512803471913018)
XLA Ops:
  1.2 1.3 table.1.tab
  2.6 8.4 %attend.3 = (bf16[32,2048]{1,0:T(8,128)(2,1)}, bf16[32,2048]{1,0:T(8,128)(2,1)}) custom-call(s32[44]{0:T(128)} %table.1.tab, bf16[64,18432]{1,0:T(8,128)(2,1)} %q.3, bf16[8,576,256]{2,1,0:T(8,128)(2,1)} %cache.3, bf16[64,576]{1,0:T(8,128)(2,1)} %bitcast.25, bf16[32,512,128]{2,1,0:T(8,128)(2,1)} %vw.3), custom_call_target="tpu_custom_call" | custom-call | flops 713031680 | bytes 5636096 | tf_op jit(solution)/shard_map/attend/pallas_call | solution.py:236
  11.0 1.0 copy-done.18
  12.0 1.2 route.12
  13.2 3.1 %collective-permute-start.8 = (bf16[32,2048]{1,0:T(8,128)(2,1)S(1)}, bf16[32,2048]{1,0:T(8,128)(2,1)S(1)}, u32[]{:S(2)}, u32[]{:S(2)}) collective-permute-start(bf16[32,2048]{1,0:T(8,128)(2,1)S(1)} %route.12), channel_id=1, source_target_pairs={{0,4},{4,8},{8,12},{12,14},{14,10},{10,6},{6,2},{2,0},{1,5},{5,9},... | collective-permute-start | bytes 393224 | tf_op jit(solution)/shard_map/ppermute | solution.py:745
  16.3 8.4 %attend.2 = (bf16[32,2048]{1,0:T(8,128)(2,1)}, bf16[32,2048]{1,0:T(8,128)(2,1)}) custom-call(s32[44]{0:T(128)} %table.1.tab, bf16[64,18432]{1,0:T(8,128)(2,1)} %q.3, bf16[8,576,256]{2,1,0:T(8,128)(2,1)} %cache.3, bf16[64,576]{1,0:T(8,128)(2,1)} %bitcast.26, bf16[32,512,128]{2,1,0:T(8,128)(2,1)} %vw.3), custom_call_target="tpu_custom_call" | custom-call | flops 713031680 | bytes 5636096 | tf_op jit(solution)/shard_map/attend/pallas_call | solution.py:236
  24.7 0.9 copy-done.15
  25.6 1.0 route.8
  26.6 2.1 %collective-permute-start = (bf16[32,2048]{1,0:T(8,128)(2,1)S(1)}, bf16[32,2048]{1,0:T(8,128)(2,1)S(1)}, u32[]{:S(2)}, u32[]{:S(2)}) collective-permute-start(bf16[32,2048]{1,0:T(8,128)(2,1)S(1)} %route.8), channel_id=1, source_target_pairs={{0,4},{4,8},{8,12},{12,14},{14,10},{10,6},{6,2},{2,0},{1,5},{5,9},... | collective-permute-start | bytes 393224 | tf_op jit(solution)/shard_map/ppermute | solution.py:745
  28.7 0.9 route.13
  29.7 2.1 %collective-permute-start.10 = (bf16[32,2048]{1,0:T(8,128)(2,1)S(1)}, bf16[32,2048]{1,0:T(8,128)(2,1)S(1)}, u32[]{:S(2)}, u32[]{:S(2)}) collective-permute-start(bf16[32,2048]{1,0:T(8,128)(2,1)S(1)} %get-tuple-element.95), channel_id=1, source_target_pairs={{0,4},{4,8},{8,12},{12,14},{14,10},{10,6},{6,2},{2,0},{1,5},{5,9},... | collective-permute-start | bytes 393224 | tf_op jit(solution)/shard_map/ppermute | solution.py:745
  32.0 3.0 %collective-permute-done.1.refs_3_.refs_2_.refs_5_ = bf16[32,2048]{1,0:T(8,128)(2,1)S(1)} collective-permute-done((bf16[32,2048]{1,0:T(8,128)(2,1)}, bf16[32,2048]{1,0:T(8,128)(2,1)S(1)}, u32[]{:S(2)}, u32[]{:S(2)}) %collective-permute-start.1) | collective-permute-done | bytes 131104 | tf_op jit(solution)/shard_map/ppermute | solution.py:748
  35.0 0.9 copy-done.16
  35.9 0.9 route.9
  36.8 1.6 collective-permute-start.2
  39.5 1.6 collective-permute-start.12
  41.5 1.2 copy-done.20
  44.0 2.0 %collective-permute-start.4 = (bf16[32,2048]{1,0:T(8,128)(2,1)S(1)}, bf16[32,2048]{1,0:T(8,128)(2,1)S(1)}, u32[]{:S(2)}, u32[]{:S(2)}) collective-permute-start(bf16[32,2048]{1,0:T(8,128)(2,1)S(1)} %get-tuple-element.89), channel_id=1, source_target_pairs={{0,4},{4,8},{8,12},{12,14},{14,10},{10,6},{6,2},{2,0},{1,5},{5,9},... | collective-permute-start | bytes 393224 | tf_op jit(solution)/shard_map/ppermute | solution.py:745
  46.0 1.6 collective-permute-start.17
  47.5 2.9 %collective-permute-done.16.refs_1_ = bf16[32,896]{1,0:T(8,128)(2,1)S(1)} collective-permute-done((bf16[32,896]{1,0:T(8,128)(2,1)S(1)}, bf16[32,896]{1,0:T(8,128)(2,1)S(1)}, u32[]{:S(2)}, u32[]{:S(2)}) %collective-permute-start.16) | collective-permute-done | bytes 57376 | tf_op jit(solution)/shard_map/ppermute | solution.py:768
  50.4 1.2 collective-permute-start.18
  51.6 2.6 %collective-permute-start.19 = (bf16[32,896]{1,0:T(8,128)(2,1)S(1)}, bf16[32,896]{1,0:T(8,128)(2,1)S(1)}, u32[]{:S(2)}, u32[]{:S(2)}) collective-permute-start(bf16[32,896]{1,0:T(8,128)(2,1)S(1)} %get-tuple-element.105), channel_id=1, source_target_pairs={{0,8},{2,10},{4,12},{6,14},{8,0},{10,2},{12,4},{14,6},{1,9},{3,11}... | collective-permute-start | bytes 172040 | tf_op jit(solution)/shard_map/ppermute | solution.py:768
  55.1 1.9 %collective-permute-done.18.refs_3_ = bf16[32,896]{1,0:T(8,128)(2,1)S(1)} collective-permute-done((bf16[32,896]{1,0:T(8,128)(2,1)S(1)}, bf16[32,896]{1,0:T(8,128)(2,1)S(1)}, u32[]{:S(2)}, u32[]{:S(2)}) %collective-permute-start.18) | collective-permute-done | bytes 57376 | tf_op jit(solution)/shard_map/ppermute | solution.py:768
  57.1 2.5 %collective-permute-start.15 = (bf16[32,2048]{1,0:T(8,128)(2,1)S(1)}, bf16[32,2048]{1,0:T(8,128)(2,1)S(1)}, u32[]{:S(2)}, u32[]{:S(2)}) collective-permute-start(bf16[32,2048]{1,0:T(8,128)(2,1)S(1)} %get-tuple-element.100), channel_id=1, source_target_pairs={{4,0},{8,4},{12,8},{14,12},{10,14},{6,10},{2,6},{0,2},{5,1},{9,5},... | collective-permute-start | bytes 393224 | tf_op jit(solution)/shard_map/ppermute | solution.py:748
  59.9 2.6 %collective-permute-start.21 = (bf16[32,896]{1,0:T(8,128)(2,1)S(1)}, bf16[32,896]{1,0:T(8,128)(2,1)S(1)}, u32[]{:S(2)}, u32[]{:S(2)}) collective-permute-start(bf16[32,896]{1,0:T(8,128)(2,1)S(1)} %get-tuple-element.107), channel_id=1, source_target_pairs={{0,12},{2,14},{4,0},{6,2},{8,4},{10,6},{12,8},{14,10},{1,13},{3,15... | collective-permute-start | bytes 172040 | tf_op jit(solution)/shard_map/ppermute | solution.py:768
  62.5 1.1 collective-permute-start.22
  65.7 1.3 collective-permute-start.7
  67.1 2.7 %project.2.refs_10_ = f32[288,896]{1,0:T(8,128)S(1)} custom-call(s32[44]{0:T(128)S(1)} %copy-done.22, bf16[32,2048]{1,0:T(8,128)(2,1)} %get-tuple-element.109.refs_1_.refs_0_, bf16[32,2048]{1,0:T(8,128)(2,1)S(1)} %collective-permute-done.8.refs_1_.refs_0_, bf16[32,2048]{1,0:T(8,128)(2,1)S(1)} %collective-permute-done.10.refs_1_.refs_0_.refs_2_, ...), custom_call_target="tpu_custom_call" | custom-call | flops 1056964608 | bytes 4849664 | tf_op jit(solution)/shard_map/project/pallas_call | solution.py:392
  70.7 2.8 %project.3 = (f32[144,896]{1,0:T(8,128)S(1)}, bf16[144,896]{1,0:T(8,128)(2,1)S(1)}) custom-call(s32[44]{0:T(128)S(1)} %copy-done.22, bf16[32,2048]{1,0:T(8,128)(2,1)} %get-tuple-element.85.refs_1_.refs_0_, bf16[32,2048]{1,0:T(8,128)(2,1)S(1)} %collective-permute-done.refs_1_.refs_0_, bf16[32,2048]{1,0:T(8,128)(2,1)S(1)} %collective-permute-done.2.refs_1_.refs_0_.refs_2_, ...), custom_call_target="tpu_custom_call" | custom-call | flops 1056964608 | bytes 4849664 | tf_op jit(solution)/shard_map/project/pallas_call | solution.py:402
  73.6 1.5 collective-permute-done.23.other
  75.8 2.0 %collective-permute-start.24 = (bf16[144,896]{1,0:T(8,128)(2,1)S(1)}, bf16[144,896]{1,0:T(8,128)(2,1)S(1)}, u32[]{:S(2)}, u32[]{:S(2)}) collective-permute-start(bf16[144,896]{1,0:T(8,128)(2,1)S(1)} %stream.1.refs_0_.refs_1_), channel_id=1, source_target_pairs={{0,4},{4,8},{8,12},{12,14},{14,10},{10,6},{6,2},{2,0},{1,5},{5,9},... | collective-permute-start | bytes 774152 | tf_op jit(solution)/shard_map/ppermute | solution.py:745
  77.8 6.2 %collective-permute-done.24.refs_0_.refs_2_.refs_3_ = bf16[144,896]{1,0:T(8,128)(2,1)S(1)} collective-permute-done((bf16[144,896]{1,0:T(8,128)(2,1)S(1)}, bf16[144,896]{1,0:T(8,128)(2,1)S(1)}, u32[]{:S(2)}, u32[]{:S(2)}) %collective-permute-start.24) | collective-permute-done | bytes 258080 | tf_op jit(solution)/shard_map/ppermute | solution.py:745
  84.1 1.9 %collective-permute-start.25 = (bf16[144,896]{1,0:T(8,128)(2,1)S(1)}, bf16[144,896]{1,0:T(8,128)(2,1)S(1)}, u32[]{:S(2)}, u32[]{:S(2)}) collective-permute-start(bf16[144,896]{1,0:T(8,128)(2,1)S(1)} %collective-permute-done.24.refs_0_.refs_2_.refs_3_), channel_id=1, source_target_pairs={{0,4},{4,8},{8,12},{12,14},{14,10},{10,6},{6,2},{2,0},{1,5},{5,9},... | collective-permute-start | bytes 774152 | tf_op jit(solution)/shard_map/ppermute | solution.py:745
  86.1 5.4 %collective-permute-done.25.refs_0_.refs_6_.refs_7_ = bf16[144,896]{1,0:T(8,128)(2,1)S(1)} collective-permute-done((bf16[144,896]{1,0:T(8,128)(2,1)S(1)}, bf16[144,896]{1,0:T(8,128)(2,1)S(1)}, u32[]{:S(2)}, u32[]{:S(2)}) %collective-permute-start.25) | collective-permute-done | bytes 258080 | tf_op jit(solution)/shard_map/ppermute | solution.py:745
  91.5 1.9 %collective-permute-start.26 = (bf16[144,896]{1,0:T(8,128)(2,1)S(1)}, bf16[144,896]{1,0:T(8,128)(2,1)S(1)}, u32[]{:S(2)}, u32[]{:S(2)}) collective-permute-start(bf16[144,896]{1,0:T(8,128)(2,1)S(1)} %collective-permute-done.25.refs_0_.refs_6_.refs_7_), channel_id=1, source_target_pairs={{0,4},{4,8},{8,12},{12,14},{14,10},{10,6},{6,2},{2,0},{1,5},{5,9},... | collective-permute-start | bytes 774152 | tf_op jit(solution)/shard_map/ppermute | solution.py:745
  93.6 4.4 %collective-permute-done.26.refs_0_.refs_10_.refs_11_ = bf16[144,896]{1,0:T(8,128)(2,1)S(1)} collective-permute-done((bf16[144,896]{1,0:T(8,128)(2,1)S(1)}, bf16[144,896]{1,0:T(8,128)(2,1)S(1)}, u32[]{:S(2)}, u32[]{:S(2)}) %collective-permute-start.26) | collective-permute-done | bytes 258080 | tf_op jit(solution)/shard_map/ppermute | solution.py:745
  98.0 2.0 %collective-permute-start.27 = (bf16[80,896]{1,0:T(8,128)(2,1)S(1)}, bf16[80,896]{1,0:T(8,128)(2,1)S(1)}, u32[]{:S(2)}, u32[]{:S(2)}) collective-permute-start(bf16[80,896]{1,0:T(8,128)(2,1)S(1)} %slice.8), channel_id=1, source_target_pairs={{0,4},{4,8},{8,12},{12,14},{14,10},{10,6},{6,2},{2,0},{1,5},{5,9},... | collective-permute-start | bytes 430088 | tf_op jit(solution)/shard_map/ppermute | solution.py:745
  101.2 4.5 %expand.5 = (f32[288,576]{1,0:T(8,128)}, f32[288,576]{1,0:T(8,128)}, f32[288,1]{1,0:T(8,128)}) custom-call(s32[44]{0:T(128)} %table.1.tab, bf16[144,896]{1,0:T(8,128)(2,1)} %copy-done, bf16[144,896]{1,0:T(8,128)(2,1)} %copy-done.30, f32[8,1,896]{2,1,0:T(1,128)} %bitcast.20, bf16[576,7168]{1,0:T(8,128)(2,1)} %bitcast.10, bf16[576,7168]{1,0:T(8,128)(2,1)} %bitcast.15), custom_call_target="tpu_custom_call" | custom-call | flops 594542592 | bytes 2580480 | tf_op jit(solution)/shard_map/expand/pallas_call | solution.py:517
  107.5 4.4 %collective-permute-done.31 = bf16[64,896]{1,0:T(8,128)(2,1)S(1)} collective-permute-done((bf16[64,896]{1,0:T(8,128)(2,1)S(1)}, bf16[64,896]{1,0:T(8,128)(2,1)S(1)}, u32[]{:S(2)}, u32[]{:S(2)}) %collective-permute-start.31) | collective-permute-done | bytes 114720 | tf_op jit(solution)/shard_map/ppermute | solution.py:748
  113.2 6.8 %expand.6 = (f32[288,576]{1,0:T(8,128)}, f32[288,576]{1,0:T(8,128)}, f32[288,1]{1,0:T(8,128)}) custom-call(s32[44]{0:T(128)} %table.1.tab, bf16[144,896]{1,0:T(8,128)(2,1)} %copy-done.7, bf16[144,896]{1,0:T(8,128)(2,1)} %copy-done.9, bf16[144,896]{1,0:T(8,128)(2,1)} %copy-done.24, bf16[144,896]{1,0:T(8,128)(2,1)} %copy-done.26, f32[8,1,896]{2,1,0:T(1,128)} %bitcast.21, ...), custom_call_target="tpu_custom_call" | custom-call | flops 1189085184 | bytes 5160960 | tf_op jit(solution)/shard_map/expand/pallas_call | solution.py:517
  120.8 7.3 %expand.7 = (f32[288,576]{1,0:T(8,128)}, f32[288,576]{1,0:T(8,128)}, f32[288,1]{1,0:T(8,128)}) custom-call(s32[44]{0:T(128)} %table.1.tab, bf16[144,896]{1,0:T(8,128)(2,1)} %copy-done.11, bf16[144,896]{1,0:T(8,128)(2,1)} %copy-done.13, bf16[144,896]{1,0:T(8,128)(2,1)} %copy-done.25, bf16[144,896]{1,0:T(8,128)(2,1)} %copy-done.27, f32[8,1,896]{2,1,0:T(1,128)} %bitcast.22, ...), custom_call_target="tpu_custom_call" | custom-call | flops 1189085184 | bytes 5160960 | tf_op jit(solution)/shard_map/expand/pallas_call | solution.py:517
  129.5 7.3 %expand.8 = (f32[288,576]{1,0:T(8,128)}, f32[288,576]{1,0:T(8,128)}, f32[288,1]{1,0:T(8,128)}) custom-call(s32[44]{0:T(128)} %table.1.tab, bf16[144,896]{1,0:T(8,128)(2,1)} %copy-done.3, bf16[144,896]{1,0:T(8,128)(2,1)} %copy-done.5, bf16[144,896]{1,0:T(8,128)(2,1)} %copy-done.28, bf16[144,896]{1,0:T(8,128)(2,1)} %copy-done.29, f32[8,1,896]{2,1,0:T(1,128)} %bitcast.23, ...), custom_call_target="tpu_custom_call" | custom-call | flops 1189085184 | bytes 5160960 | tf_op jit(solution)/shard_map/expand/pallas_call | solution.py:517
  136.8 4.8 %expand.9.hidden = bf16[288,576]{1,0:T(8,128)(2,1)} custom-call(s32[44]{0:T(128)} %table.1.tab, bf16[144,896]{1,0:T(8,128)(2,1)} %constant_dynamic-update-slice_fusion.refs_0_.refs_14_.refs_15_, bf16[144,896]{1,0:T(8,128)(2,1)} %collective-permute-done.32.refs_1_, f32[8,1,896]{2,1,0:T(1,128)} %bitcast.24, bf16[576,7168]{1,0:T(8,128)(2,1)} %bitcast.14, ...), custom_call_target="tpu_custom_call" | custom-call | flops 594542592 | bytes 2580480 | tf_op jit(solution)/shard_map/expand/pallas_call | solution.py:517
  141.6 1.0 copy-done.2
  142.6 2.4 %contract.3 = (bf16[144,3584]{1,0:T(8,128)(2,1)S(1)}, bf16[144,3584]{1,0:T(8,128)(2,1)S(1)}) custom-call(bf16[288,576]{1,0:T(8,128)(2,1)S(1)} %copy-done.2, bf16[576,7168]{1,0:T(8,128)(2,1)S(1)} %bitcast.7), custom_call_target="tpu_custom_call" | custom-call | flops 1189085184 | bytes 6193152 | tf_op jit(solution)/shard_map/contract/pallas_call | solution.py:582
  145.6 2.4 %contract.2 = (bf16[144,3584]{1,0:T(8,128)(2,1)S(1)}, bf16[144,3584]{1,0:T(8,128)(2,1)S(1)}) custom-call(bf16[288,576]{1,0:T(8,128)(2,1)S(1)} %copy-done.2, bf16[576,7168]{1,0:T(8,128)(2,1)S(1)} %bitcast.7), custom_call_target="tpu_custom_call" | custom-call | flops 1189085184 | bytes 6193152 | tf_op jit(solution)/shard_map/contract/pallas_call | solution.py:582
  148.7 1.8 collective-permute-start.50
  151.3 1.8 collective-permute-start.41
  153.4 0.9 collective-permute-done.50.refs_0_
  154.4 1.5 collective-permute-done.51.refs_1_.refs_2_
  156.5 1.1 collective-permute-start.52
  157.5 1.0 collective-permute-start.53
  159.2 1.1 collective-permute-start.43
  160.3 1.0 collective-permute-start.44
  161.3 0.9 collective-permute-done.52.refs_1_.refs_0_
  162.2 1.2 collective-permute-done.53.refs_3_.refs_2_
  164.8 1.4 collective-permute-start.55
  167.5 1.5 collective-permute-start.46
  170.4 1.3 collective-permute-start.56
  173.2 1.3 collective-permute-start.47
  175.3 1.4 collect.1.own
  178.0 1.3 collective-permute-done.48.b_last
  180.1 1.3 collective-permute-done.58.refs_2_
  181.4 1.4 finish.1
  (167 shorter events, 27.6 us)
Async XLA Ops:
  10.9 56.1 %slice-start.2 = ((s8[7340032]{0:T(1024)(128)(4,1)}), s8[4194304]{0:T(1024)(128)(4,1)S(1)}, s32[]{:S(2)}) async-start(s8[7340032]{0:T(1024)(128)(4,1)} %bitcast.8), calls=%async_computation.2 | async-start | bytes 8388608
  13.2 53.9 %slice-start.3 = ((s8[7340032]{0:T(1024)(128)(4,1)}), s8[3145728]{0:T(1024)(128)(4,1)S(1)}, s32[]{:S(2)}) async-start(s8[7340032]{0:T(1024)(128)(4,1)} %bitcast.8), calls=%async_computation.3 | async-start | bytes 6291456
  13.2 15.5 %collective-permute-start.8 = (bf16[32,2048]{1,0:T(8,128)(2,1)S(1)}, bf16[32,2048]{1,0:T(8,128)(2,1)S(1)}, u32[]{:S(2)}, u32[]{:S(2)}) collective-permute-start(bf16[32,2048]{1,0:T(8,128)(2,1)S(1)} %route.12), channel_id=1, source_target_pairs={{0,4},{4,8},{8,12},{12,14},{14,10},{10,6},{6,2},{2,0},{1,5},{5,9},... | collective-permute-start | bytes 393224 | tf_op jit(solution)/shard_map/ppermute | solution.py:745
  16.3 12.4 %collective-permute-start.9 = (bf16[32,2048]{1,0:T(8,128)(2,1)}, bf16[32,2048]{1,0:T(8,128)(2,1)S(1)}, u32[]{:S(2)}, u32[]{:S(2)}) collective-permute-start(bf16[32,2048]{1,0:T(8,128)(2,1)} %get-tuple-element.109.refs_1_.refs_0_), channel_id=1, source_target_pairs={{4,0},{8,4},{12,8},{14,12},{10,14},{6,10},{2,6},{0,2},{5,1},{9,5},... | collective-permute-start | bytes 393224 | tf_op jit(solution)/shard_map/ppermute | solution.py:748
  25.6 45.0 %copy-start.17 = (bf16[32,2048]{1,0:T(8,128)(2,1)S(1)}, bf16[32,2048]{1,0:T(8,128)(2,1)}, u32[]{:S(2)}) copy-start(bf16[32,2048]{1,0:T(8,128)(2,1)} %get-tuple-element.86.refs_0_.refs_2_.refs_9_) | copy-start | bytes 393220
  26.6 5.3 %collective-permute-start = (bf16[32,2048]{1,0:T(8,128)(2,1)S(1)}, bf16[32,2048]{1,0:T(8,128)(2,1)S(1)}, u32[]{:S(2)}, u32[]{:S(2)}) collective-permute-start(bf16[32,2048]{1,0:T(8,128)(2,1)S(1)} %route.8), channel_id=1, source_target_pairs={{0,4},{4,8},{8,12},{12,14},{14,10},{10,6},{6,2},{2,0},{1,5},{5,9},... | collective-permute-start | bytes 393224 | tf_op jit(solution)/shard_map/ppermute | solution.py:745
  28.7 6.3 %collective-permute-start.1 = (bf16[32,2048]{1,0:T(8,128)(2,1)}, bf16[32,2048]{1,0:T(8,128)(2,1)S(1)}, u32[]{:S(2)}, u32[]{:S(2)}) collective-permute-start(bf16[32,2048]{1,0:T(8,128)(2,1)} %get-tuple-element.85.refs_1_.refs_0_), channel_id=1, source_target_pairs={{4,0},{8,4},{12,8},{14,12},{10,14},{6,10},{2,6},{0,2},{5,1},{9,5},... | collective-permute-start | bytes 393224 | tf_op jit(solution)/shard_map/ppermute | solution.py:748
  29.7 9.2 %collective-permute-start.10 = (bf16[32,2048]{1,0:T(8,128)(2,1)S(1)}, bf16[32,2048]{1,0:T(8,128)(2,1)S(1)}, u32[]{:S(2)}, u32[]{:S(2)}) collective-permute-start(bf16[32,2048]{1,0:T(8,128)(2,1)S(1)} %get-tuple-element.95), channel_id=1, source_target_pairs={{0,4},{4,8},{8,12},{12,14},{14,10},{10,6},{6,2},{2,0},{1,5},{5,9},... | collective-permute-start | bytes 393224 | tf_op jit(solution)/shard_map/ppermute | solution.py:745
  31.7 7.2 %collective-permute-start.11 = (bf16[32,2048]{1,0:T(8,128)(2,1)S(1)}, bf16[32,2048]{1,0:T(8,128)(2,1)S(1)}, u32[]{:S(2)}, u32[]{:S(2)}) collective-permute-start(bf16[32,2048]{1,0:T(8,128)(2,1)S(1)} %get-tuple-element.96), channel_id=1, source_target_pairs={{4,0},{8,4},{12,8},{14,12},{10,14},{6,10},{2,6},{0,2},{5,1},{9,5},... | collective-permute-start | bytes 393224 | tf_op jit(solution)/shard_map/ppermute | solution.py:748
  36.8 6.6 %collective-permute-start.2 = (bf16[32,2048]{1,0:T(8,128)(2,1)S(1)}, bf16[32,2048]{1,0:T(8,128)(2,1)S(1)}, u32[]{:S(2)}, u32[]{:S(2)}) collective-permute-start(bf16[32,2048]{1,0:T(8,128)(2,1)S(1)} %get-tuple-element.87), channel_id=1, source_target_pairs={{0,4},{4,8},{8,12},{12,14},{14,10},{10,6},{6,2},{2,0},{1,5},{5,9},... | collective-permute-start | bytes 393224 | tf_op jit(solution)/shard_map/ppermute | solution.py:745
  38.4 5.0 %collective-permute-start.3 = (bf16[32,2048]{1,0:T(8,128)(2,1)S(1)}, bf16[32,2048]{1,0:T(8,128)(2,1)S(1)}, u32[]{:S(2)}, u32[]{:S(2)}) collective-permute-start(bf16[32,2048]{1,0:T(8,128)(2,1)S(1)} %get-tuple-element.88), channel_id=1, source_target_pairs={{4,0},{8,4},{12,8},{14,12},{10,14},{6,10},{2,6},{0,2},{5,1},{9,5},... | collective-permute-start | bytes 393224 | tf_op jit(solution)/shard_map/ppermute | solution.py:748
  39.5 10.9 %collective-permute-start.12 = (bf16[32,2048]{1,0:T(8,128)(2,1)S(1)}, bf16[32,2048]{1,0:T(8,128)(2,1)S(1)}, u32[]{:S(2)}, u32[]{:S(2)}) collective-permute-start(bf16[32,2048]{1,0:T(8,128)(2,1)S(1)} %get-tuple-element.97), channel_id=1, source_target_pairs={{0,4},{4,8},{8,12},{12,14},{14,10},{10,6},{6,2},{2,0},{1,5},{5,9},... | collective-permute-start | bytes 393224 | tf_op jit(solution)/shard_map/ppermute | solution.py:745
  41.1 10.5 %collective-permute-start.13 = (bf16[32,2048]{1,0:T(8,128)(2,1)S(1)}, bf16[32,2048]{1,0:T(8,128)(2,1)S(1)}, u32[]{:S(2)}, u32[]{:S(2)}) collective-permute-start(bf16[32,2048]{1,0:T(8,128)(2,1)S(1)} %get-tuple-element.98), channel_id=1, source_target_pairs={{4,0},{8,4},{12,8},{14,12},{10,14},{6,10},{2,6},{0,2},{5,1},{9,5},... | collective-permute-start | bytes 393224 | tf_op jit(solution)/shard_map/ppermute | solution.py:748
  43.3 7.1 %collective-permute-start.16 = (bf16[32,896]{1,0:T(8,128)(2,1)S(1)}, bf16[32,896]{1,0:T(8,128)(2,1)S(1)}, u32[]{:S(2)}, u32[]{:S(2)}) collective-permute-start(bf16[32,896]{1,0:T(8,128)(2,1)S(1)} %get-tuple-element.102), channel_id=1, source_target_pairs={{0,2},{2,4},{4,6},{6,8},{8,10},{10,12},{12,14},{14,0},{1,3},{3,5},... | collective-permute-start | bytes 172040 | tf_op jit(solution)/shard_map/ppermute | solution.py:768
  44.0 15.9 %collective-permute-start.4 = (bf16[32,2048]{1,0:T(8,128)(2,1)S(1)}, bf16[32,2048]{1,0:T(8,128)(2,1)S(1)}, u32[]{:S(2)}, u32[]{:S(2)}) collective-permute-start(bf16[32,2048]{1,0:T(8,128)(2,1)S(1)} %get-tuple-element.89), channel_id=1, source_target_pairs={{0,4},{4,8},{8,12},{12,14},{14,10},{10,6},{6,2},{2,0},{1,5},{5,9},... | collective-permute-start | bytes 393224 | tf_op jit(solution)/shard_map/ppermute | solution.py:745
  46.0 8.8 %collective-permute-start.17 = (bf16[32,896]{1,0:T(8,128)(2,1)S(1)}, bf16[32,896]{1,0:T(8,128)(2,1)S(1)}, u32[]{:S(2)}, u32[]{:S(2)}) collective-permute-start(bf16[32,896]{1,0:T(8,128)(2,1)S(1)} %get-tuple-element.103), channel_id=1, source_target_pairs={{0,4},{2,6},{4,8},{6,10},{8,12},{10,14},{12,0},{14,2},{1,5},{3,7},... | collective-permute-start | bytes 172040 | tf_op jit(solution)/shard_map/ppermute | solution.py:768
  50.4 12.1 %collective-permute-start.5 = (bf16[32,2048]{1,0:T(8,128)(2,1)S(1)}, bf16[32,2048]{1,0:T(8,128)(2,1)S(1)}, u32[]{:S(2)}, u32[]{:S(2)}) collective-permute-start(bf16[32,2048]{1,0:T(8,128)(2,1)S(1)} %get-tuple-element.90), channel_id=1, source_target_pairs={{4,0},{8,4},{12,8},{14,12},{10,14},{6,10},{2,6},{0,2},{5,1},{9,5},... | collective-permute-start | bytes 393224 | tf_op jit(solution)/shard_map/ppermute | solution.py:748
  50.4 6.7 %collective-permute-start.18 = (bf16[32,896]{1,0:T(8,128)(2,1)S(1)}, bf16[32,896]{1,0:T(8,128)(2,1)S(1)}, u32[]{:S(2)}, u32[]{:S(2)}) collective-permute-start(bf16[32,896]{1,0:T(8,128)(2,1)S(1)} %get-tuple-element.104), channel_id=1, source_target_pairs={{0,6},{2,8},{4,10},{6,12},{8,14},{10,0},{12,2},{14,4},{1,7},{3,9},... | collective-permute-start | bytes 172040 | tf_op jit(solution)/shard_map/ppermute | solution.py:768
  51.6 8.0 %collective-permute-start.19 = (bf16[32,896]{1,0:T(8,128)(2,1)S(1)}, bf16[32,896]{1,0:T(8,128)(2,1)S(1)}, u32[]{:S(2)}, u32[]{:S(2)}) collective-permute-start(bf16[32,896]{1,0:T(8,128)(2,1)S(1)} %get-tuple-element.105), channel_id=1, source_target_pairs={{0,8},{2,10},{4,12},{6,14},{8,0},{10,2},{12,4},{14,6},{1,9},{3,11}... | collective-permute-start | bytes 172040 | tf_op jit(solution)/shard_map/ppermute | solution.py:768
  54.7 12.3 %collective-permute-start.14 = (bf16[32,2048]{1,0:T(8,128)(2,1)S(1)}, bf16[32,2048]{1,0:T(8,128)(2,1)S(1)}, u32[]{:S(2)}, u32[]{:S(2)}) collective-permute-start(bf16[32,2048]{1,0:T(8,128)(2,1)S(1)} %get-tuple-element.99), channel_id=1, source_target_pairs={{0,4},{4,8},{8,12},{12,14},{14,10},{10,6},{6,2},{2,0},{1,5},{5,9},... | collective-permute-start | bytes 393224 | tf_op jit(solution)/shard_map/ppermute | solution.py:745
  57.1 10.0 %collective-permute-start.15 = (bf16[32,2048]{1,0:T(8,128)(2,1)S(1)}, bf16[32,2048]{1,0:T(8,128)(2,1)S(1)}, u32[]{:S(2)}, u32[]{:S(2)}) collective-permute-start(bf16[32,2048]{1,0:T(8,128)(2,1)S(1)} %get-tuple-element.100), channel_id=1, source_target_pairs={{4,0},{8,4},{12,8},{14,12},{10,14},{6,10},{2,6},{0,2},{5,1},{9,5},... | collective-permute-start | bytes 393224 | tf_op jit(solution)/shard_map/ppermute | solution.py:748
  59.6 5.2 %collective-permute-start.20 = (bf16[32,896]{1,0:T(8,128)(2,1)S(1)}, bf16[32,896]{1,0:T(8,128)(2,1)S(1)}, u32[]{:S(2)}, u32[]{:S(2)}) collective-permute-start(bf16[32,896]{1,0:T(8,128)(2,1)S(1)} %get-tuple-element.106), channel_id=1, source_target_pairs={{0,10},{2,12},{4,14},{6,0},{8,2},{10,4},{12,6},{14,8},{1,11},{3,13... | collective-permute-start | bytes 172040 | tf_op jit(solution)/shard_map/ppermute | solution.py:768
  59.9 5.8 %collective-permute-start.21 = (bf16[32,896]{1,0:T(8,128)(2,1)S(1)}, bf16[32,896]{1,0:T(8,128)(2,1)S(1)}, u32[]{:S(2)}, u32[]{:S(2)}) collective-permute-start(bf16[32,896]{1,0:T(8,128)(2,1)S(1)} %get-tuple-element.107), channel_id=1, source_target_pairs={{0,12},{2,14},{4,0},{6,2},{8,4},{10,6},{12,8},{14,10},{1,13},{3,15... | collective-permute-start | bytes 172040 | tf_op jit(solution)/shard_map/ppermute | solution.py:768
  62.5 4.5 %collective-permute-start.22 = (bf16[32,896]{1,0:T(8,128)(2,1)S(1)}, bf16[32,896]{1,0:T(8,128)(2,1)S(1)}, u32[]{:S(2)}, u32[]{:S(2)}) collective-permute-start(bf16[32,896]{1,0:T(8,128)(2,1)S(1)} %get-tuple-element.108), channel_id=1, source_target_pairs={{0,14},{2,0},{4,2},{6,4},{8,6},{10,8},{12,10},{14,12},{1,15},{3,1}... | collective-permute-start | bytes 172040 | tf_op jit(solution)/shard_map/ppermute | solution.py:768
  64.8 5.0 %collective-permute-start.6 = (bf16[32,2048]{1,0:T(8,128)(2,1)S(1)}, bf16[32,2048]{1,0:T(8,128)(2,1)S(1)}, u32[]{:S(2)}, u32[]{:S(2)}) collective-permute-start(bf16[32,2048]{1,0:T(8,128)(2,1)S(1)} %get-tuple-element.91), channel_id=1, source_target_pairs={{0,4},{4,8},{8,12},{12,14},{14,10},{10,6},{6,2},{2,0},{1,5},{5,9},... | collective-permute-start | bytes 393224 | tf_op jit(solution)/shard_map/ppermute | solution.py:745
  65.7 5.0 %collective-permute-start.7 = (bf16[32,2048]{1,0:T(8,128)(2,1)S(1)}, bf16[32,2048]{1,0:T(8,128)(2,1)S(1)}, u32[]{:S(2)}, u32[]{:S(2)}) collective-permute-start(bf16[32,2048]{1,0:T(8,128)(2,1)S(1)} %get-tuple-element.92), channel_id=1, source_target_pairs={{4,0},{8,4},{12,8},{14,12},{10,14},{6,10},{2,6},{0,2},{5,1},{9,5},... | collective-permute-start | bytes 393224 | tf_op jit(solution)/shard_map/ppermute | solution.py:748
  73.5 1.6 collective-permute-start.23
  75.8 24.8 %copy-start = (bf16[144,896]{1,0:T(8,128)(2,1)}, bf16[144,896]{1,0:T(8,128)(2,1)S(1)}, u32[]{:S(2)}) copy-start(bf16[144,896]{1,0:T(8,128)(2,1)S(1)} %stream.1.refs_0_.refs_1_) | copy-start | bytes 774148
  75.8 8.3 %collective-permute-start.24 = (bf16[144,896]{1,0:T(8,128)(2,1)S(1)}, bf16[144,896]{1,0:T(8,128)(2,1)S(1)}, u32[]{:S(2)}, u32[]{:S(2)}) collective-permute-start(bf16[144,896]{1,0:T(8,128)(2,1)S(1)} %stream.1.refs_0_.refs_1_), channel_id=1, source_target_pairs={{0,4},{4,8},{8,12},{12,14},{14,10},{10,6},{6,2},{2,0},{1,5},{5,9},... | collective-permute-start | bytes 774152 | tf_op jit(solution)/shard_map/ppermute | solution.py:745
  77.7 8.3 %collective-permute-start.28 = (bf16[144,896]{1,0:T(8,128)(2,1)S(1)}, bf16[144,896]{1,0:T(8,128)(2,1)S(1)}, u32[]{:S(2)}, u32[]{:S(2)}) collective-permute-start(bf16[144,896]{1,0:T(8,128)(2,1)S(1)} %stream.1.refs_0_.refs_1_), channel_id=1, source_target_pairs={{4,0},{8,4},{12,8},{14,12},{10,14},{6,10},{2,6},{0,2},{5,1},{9,5},... | collective-permute-start | bytes 774152 | tf_op jit(solution)/shard_map/ppermute | solution.py:748
  84.1 7.4 %collective-permute-start.25 = (bf16[144,896]{1,0:T(8,128)(2,1)S(1)}, bf16[144,896]{1,0:T(8,128)(2,1)S(1)}, u32[]{:S(2)}, u32[]{:S(2)}) collective-permute-start(bf16[144,896]{1,0:T(8,128)(2,1)S(1)} %collective-permute-done.24.refs_0_.refs_2_.refs_3_), channel_id=1, source_target_pairs={{0,4},{4,8},{8,12},{12,14},{14,10},{10,6},{6,2},{2,0},{1,5},{5,9},... | collective-permute-start | bytes 774152 | tf_op jit(solution)/shard_map/ppermute | solution.py:745
  86.0 7.4 %collective-permute-start.29 = (bf16[144,896]{1,0:T(8,128)(2,1)S(1)}, bf16[144,896]{1,0:T(8,128)(2,1)S(1)}, u32[]{:S(2)}, u32[]{:S(2)}) collective-permute-start(bf16[144,896]{1,0:T(8,128)(2,1)S(1)} %collective-permute-done.28.refs_1_.refs_4_.refs_5_), channel_id=1, source_target_pairs={{4,0},{8,4},{12,8},{14,12},{10,14},{6,10},{2,6},{0,2},{5,1},{9,5},... | collective-permute-start | bytes 774152 | tf_op jit(solution)/shard_map/ppermute | solution.py:748
  91.5 6.5 %collective-permute-start.26 = (bf16[144,896]{1,0:T(8,128)(2,1)S(1)}, bf16[144,896]{1,0:T(8,128)(2,1)S(1)}, u32[]{:S(2)}, u32[]{:S(2)}) collective-permute-start(bf16[144,896]{1,0:T(8,128)(2,1)S(1)} %collective-permute-done.25.refs_0_.refs_6_.refs_7_), channel_id=1, source_target_pairs={{0,4},{4,8},{8,12},{12,14},{14,10},{10,6},{6,2},{2,0},{1,5},{5,9},... | collective-permute-start | bytes 774152 | tf_op jit(solution)/shard_map/ppermute | solution.py:745
  93.4 7.1 %collective-permute-start.39 = (bf16[144,896]{1,0:T(8,128)(2,1)S(1)}, bf16[144,896]{1,0:T(8,128)(2,1)S(1)}, u32[]{:S(2)}, u32[]{:S(2)}) collective-permute-start(bf16[144,896]{1,0:T(8,128)(2,1)S(1)} %stream.1.refs_0_.refs_1_), channel_id=1, source_target_pairs={{0,1},{1,0},{2,3},{3,2},{4,5},{5,4},{6,7},{7,6},{8,9},{9,8},{10,11... | collective-permute-start | bytes 774152 | tf_op jit(solution)/shard_map/ppermute | solution.py:751
  93.4 12.3 %collective-permute-start.30 = (bf16[144,896]{1,0:T(8,128)(2,1)S(1)}, bf16[144,896]{1,0:T(8,128)(2,1)S(1)}, u32[]{:S(2)}, u32[]{:S(2)}) collective-permute-start(bf16[144,896]{1,0:T(8,128)(2,1)S(1)} %collective-permute-done.29.refs_1_.refs_8_.refs_9_), channel_id=1, source_target_pairs={{4,0},{8,4},{12,8},{14,12},{10,14},{6,10},{2,6},{0,2},{5,1},{9,5},... | collective-permute-start | bytes 774152 | tf_op jit(solution)/shard_map/ppermute | solution.py:748
  98.0 8.3 %collective-permute-start.27 = (bf16[80,896]{1,0:T(8,128)(2,1)S(1)}, bf16[80,896]{1,0:T(8,128)(2,1)S(1)}, u32[]{:S(2)}, u32[]{:S(2)}) collective-permute-start(bf16[80,896]{1,0:T(8,128)(2,1)S(1)} %slice.8), channel_id=1, source_target_pairs={{0,4},{4,8},{8,12},{12,14},{14,10},{10,6},{6,2},{2,0},{1,5},{5,9},... | collective-permute-start | bytes 430088 | tf_op jit(solution)/shard_map/ppermute | solution.py:745
  100.0 7.4 %collective-permute-start.37 = (bf16[144,896]{1,0:T(8,128)(2,1)S(1)}, bf16[144,896]{1,0:T(8,128)(2,1)S(1)}, u32[]{:S(2)}, u32[]{:S(2)}) collective-permute-start(bf16[144,896]{1,0:T(8,128)(2,1)S(1)} %collective-permute-done.24.refs_0_.refs_2_.refs_3_), channel_id=1, source_target_pairs={{0,1},{1,0},{2,3},{3,2},{4,5},{5,4},{6,7},{7,6},{8,9},{9,8},{10,11... | collective-permute-start | bytes 774152 | tf_op jit(solution)/shard_map/ppermute | solution.py:751
  100.0 12.5 %collective-permute-start.38 = (bf16[144,896]{1,0:T(8,128)(2,1)S(1)}, bf16[144,896]{1,0:T(8,128)(2,1)S(1)}, u32[]{:S(2)}, u32[]{:S(2)}) collective-permute-start(bf16[144,896]{1,0:T(8,128)(2,1)S(1)} %collective-permute-done.28.refs_1_.refs_4_.refs_5_), channel_id=1, source_target_pairs={{0,1},{1,0},{2,3},{3,2},{4,5},{5,4},{6,7},{7,6},{8,9},{9,8},{10,11... | collective-permute-start | bytes 774152 | tf_op jit(solution)/shard_map/ppermute | solution.py:751
  105.7 14.3 %collective-permute-start.35 = (bf16[144,896]{1,0:T(8,128)(2,1)S(1)}, bf16[144,896]{1,0:T(8,128)(2,1)S(1)}, u32[]{:S(2)}, u32[]{:S(2)}) collective-permute-start(bf16[144,896]{1,0:T(8,128)(2,1)S(1)} %collective-permute-done.25.refs_0_.refs_6_.refs_7_), channel_id=1, source_target_pairs={{0,1},{1,0},{2,3},{3,2},{4,5},{5,4},{6,7},{7,6},{8,9},{9,8},{10,11... | collective-permute-start | bytes 774152 | tf_op jit(solution)/shard_map/ppermute | solution.py:751
  105.8 14.2 %collective-permute-start.36 = (bf16[144,896]{1,0:T(8,128)(2,1)S(1)}, bf16[144,896]{1,0:T(8,128)(2,1)S(1)}, u32[]{:S(2)}, u32[]{:S(2)}) collective-permute-start(bf16[144,896]{1,0:T(8,128)(2,1)S(1)} %collective-permute-done.29.refs_1_.refs_8_.refs_9_), channel_id=1, source_target_pairs={{0,1},{1,0},{2,3},{3,2},{4,5},{5,4},{6,7},{7,6},{8,9},{9,8},{10,11... | collective-permute-start | bytes 774152 | tf_op jit(solution)/shard_map/ppermute | solution.py:751
  106.4 5.5 %collective-permute-start.31 = (bf16[64,896]{1,0:T(8,128)(2,1)S(1)}, bf16[64,896]{1,0:T(8,128)(2,1)S(1)}, u32[]{:S(2)}, u32[]{:S(2)}) collective-permute-start(bf16[64,896]{1,0:T(8,128)(2,1)S(1)} %slice.9), channel_id=1, source_target_pairs={{4,0},{8,4},{12,8},{14,12},{10,14},{6,10},{2,6},{0,2},{5,1},{9,5},... | collective-permute-start | bytes 344072 | tf_op jit(solution)/shard_map/ppermute | solution.py:748
  107.4 20.7 %collective-permute-start.33 = (bf16[144,896]{1,0:T(8,128)(2,1)S(1)}, bf16[144,896]{1,0:T(8,128)(2,1)S(1)}, u32[]{:S(2)}, u32[]{:S(2)}) collective-permute-start(bf16[144,896]{1,0:T(8,128)(2,1)S(1)} %collective-permute-done.26.refs_0_.refs_10_.refs_11_), channel_id=1, source_target_pairs={{0,1},{1,0},{2,3},{3,2},{4,5},{5,4},{6,7},{7,6},{8,9},{9,8},{10,11... | collective-permute-start | bytes 774152 | tf_op jit(solution)/shard_map/ppermute | solution.py:751
  111.9 16.2 %collective-permute-start.34 = (bf16[144,896]{1,0:T(8,128)(2,1)S(1)}, bf16[144,896]{1,0:T(8,128)(2,1)S(1)}, u32[]{:S(2)}, u32[]{:S(2)}) collective-permute-start(bf16[144,896]{1,0:T(8,128)(2,1)S(1)} %collective-permute-done.30.refs_1_.refs_12_.refs_13_), channel_id=1, source_target_pairs={{0,1},{1,0},{2,3},{3,2},{4,5},{5,4},{6,7},{7,6},{8,9},{9,8},{10,11... | collective-permute-start | bytes 774152 | tf_op jit(solution)/shard_map/ppermute | solution.py:751
  112.5 24.3 %collective-permute-start.32 = (bf16[144,896]{1,0:T(8,128)(2,1)}, bf16[144,896]{1,0:T(8,128)(2,1)}, u32[]{:S(2)}, u32[]{:S(2)}) collective-permute-start(bf16[144,896]{1,0:T(8,128)(2,1)} %constant_dynamic-update-slice_fusion.refs_0_.refs_14_.refs_15_), channel_id=1, source_target_pairs={{0,1},{1,0},{2,3},{3,2},{4,5},{5,4},{6,7},{7,6},{8,9},{9,8},{10,11... | collective-permute-start | bytes 774152 | tf_op jit(solution)/shard_map/ppermute | solution.py:751
  145.0 3.0 %collective-permute-start.49 = (bf16[144,3584]{1,0:T(8,128)(2,1)S(1)}, bf16[144,3584]{1,0:T(8,128)(2,1)S(1)}, u32[]{:S(2)}, u32[]{:S(2)}) collective-permute-start(bf16[144,3584]{1,0:T(8,128)(2,1)S(1)} %get-tuple-element.153), channel_id=1, source_target_pairs={{0,1},{1,0},{2,3},{3,2},{4,5},{5,4},{6,7},{7,6},{8,9},{9,8},{10,11... | collective-permute-start | bytes 3096584 | tf_op jit(solution)/shard_map/ppermute | solution.py:751
  147.9 2.8 %collective-permute-start.40 = (bf16[144,3584]{1,0:T(8,128)(2,1)S(1)}, bf16[144,3584]{1,0:T(8,128)(2,1)S(1)}, u32[]{:S(2)}, u32[]{:S(2)}) collective-permute-start(bf16[144,3584]{1,0:T(8,128)(2,1)S(1)} %get-tuple-element.142), channel_id=1, source_target_pairs={{0,1},{1,0},{2,3},{3,2},{4,5},{5,4},{6,7},{7,6},{8,9},{9,8},{10,11... | collective-permute-start | bytes 3096584 | tf_op jit(solution)/shard_map/ppermute | solution.py:751
  148.7 5.7 %collective-permute-start.50 = (bf16[16,3584]{1,0:T(8,128)(2,1)S(1)}, bf16[16,3584]{1,0:T(8,128)(2,1)S(1)}, u32[]{:S(2)}, u32[]{:S(2)}) collective-permute-start(bf16[16,3584]{1,0:T(8,128)(2,1)S(1)} %get-tuple-element.154), channel_id=1, source_target_pairs={{0,4},{4,8},{8,12},{12,14},{14,10},{10,6},{6,2},{2,0},{1,5},{5,9},... | collective-permute-start | bytes 344072 | tf_op jit(solution)/shard_map/ppermute | solution.py:745
  150.4 5.4 %collective-permute-start.51 = (bf16[16,3584]{1,0:T(8,128)(2,1)S(1)}, bf16[16,3584]{1,0:T(8,128)(2,1)S(1)}, u32[]{:S(2)}, u32[]{:S(2)}) collective-permute-start(bf16[16,3584]{1,0:T(8,128)(2,1)S(1)} %get-tuple-element.155), channel_id=1, source_target_pairs={{4,0},{8,4},{12,8},{14,12},{10,14},{6,10},{2,6},{0,2},{5,1},{9,5},... | collective-permute-start | bytes 344072 | tf_op jit(solution)/shard_map/ppermute | solution.py:748
  151.3 7.2 %collective-permute-start.41 = (bf16[16,3584]{1,0:T(8,128)(2,1)S(1)}, bf16[16,3584]{1,0:T(8,128)(2,1)S(1)}, u32[]{:S(2)}, u32[]{:S(2)}) collective-permute-start(bf16[16,3584]{1,0:T(8,128)(2,1)S(1)} %get-tuple-element.143), channel_id=1, source_target_pairs={{0,4},{4,8},{8,12},{12,14},{14,10},{10,6},{6,2},{2,0},{1,5},{5,9},... | collective-permute-start | bytes 344072 | tf_op jit(solution)/shard_map/ppermute | solution.py:745
  153.1 5.4 %collective-permute-start.42 = (bf16[16,3584]{1,0:T(8,128)(2,1)S(1)}, bf16[16,3584]{1,0:T(8,128)(2,1)S(1)}, u32[]{:S(2)}, u32[]{:S(2)}) collective-permute-start(bf16[16,3584]{1,0:T(8,128)(2,1)S(1)} %get-tuple-element.144), channel_id=1, source_target_pairs={{4,0},{8,4},{12,8},{14,12},{10,14},{6,10},{2,6},{0,2},{5,1},{9,5},... | collective-permute-start | bytes 344072 | tf_op jit(solution)/shard_map/ppermute | solution.py:748
  156.5 5.7 %collective-permute-start.52 = (bf16[16,3584]{1,0:T(8,128)(2,1)S(1)}, bf16[16,3584]{1,0:T(8,128)(2,1)S(1)}, u32[]{:S(2)}, u32[]{:S(2)}) collective-permute-start(bf16[16,3584]{1,0:T(8,128)(2,1)S(1)} %get-tuple-element.156), channel_id=1, source_target_pairs={{0,4},{4,8},{8,12},{12,14},{14,10},{10,6},{6,2},{2,0},{1,5},{5,9},... | collective-permute-start | bytes 344072 | tf_op jit(solution)/shard_map/ppermute | solution.py:745
  157.5 5.9 %collective-permute-start.53 = (bf16[16,3584]{1,0:T(8,128)(2,1)S(1)}, bf16[16,3584]{1,0:T(8,128)(2,1)S(1)}, u32[]{:S(2)}, u32[]{:S(2)}) collective-permute-start(bf16[16,3584]{1,0:T(8,128)(2,1)S(1)} %get-tuple-element.157), channel_id=1, source_target_pairs={{4,0},{8,4},{12,8},{14,12},{10,14},{6,10},{2,6},{0,2},{5,1},{9,5},... | collective-permute-start | bytes 344072 | tf_op jit(solution)/shard_map/ppermute | solution.py:748
  159.2 7.0 %collective-permute-start.43 = (bf16[16,3584]{1,0:T(8,128)(2,1)S(1)}, bf16[16,3584]{1,0:T(8,128)(2,1)S(1)}, u32[]{:S(2)}, u32[]{:S(2)}) collective-permute-start(bf16[16,3584]{1,0:T(8,128)(2,1)S(1)} %get-tuple-element.145), channel_id=1, source_target_pairs={{0,4},{4,8},{8,12},{12,14},{14,10},{10,6},{6,2},{2,0},{1,5},{5,9},... | collective-permute-start | bytes 344072 | tf_op jit(solution)/shard_map/ppermute | solution.py:745
  160.3 6.0 %collective-permute-start.44 = (bf16[16,3584]{1,0:T(8,128)(2,1)S(1)}, bf16[16,3584]{1,0:T(8,128)(2,1)S(1)}, u32[]{:S(2)}, u32[]{:S(2)}) collective-permute-start(bf16[16,3584]{1,0:T(8,128)(2,1)S(1)} %get-tuple-element.146), channel_id=1, source_target_pairs={{4,0},{8,4},{12,8},{14,12},{10,14},{6,10},{2,6},{0,2},{5,1},{9,5},... | collective-permute-start | bytes 344072 | tf_op jit(solution)/shard_map/ppermute | solution.py:748
  164.1 5.3 %collective-permute-start.54 = (bf16[16,3584]{1,0:T(8,128)(2,1)S(1)}, bf16[16,3584]{1,0:T(8,128)(2,1)S(1)}, u32[]{:S(2)}, u32[]{:S(2)}) collective-permute-start(bf16[16,3584]{1,0:T(8,128)(2,1)S(1)} %get-tuple-element.158), channel_id=1, source_target_pairs={{0,4},{4,8},{8,12},{12,14},{14,10},{10,6},{6,2},{2,0},{1,5},{5,9},... | collective-permute-start | bytes 344072 | tf_op jit(solution)/shard_map/ppermute | solution.py:745
  164.8 5.0 %collective-permute-start.55 = (bf16[16,3584]{1,0:T(8,128)(2,1)S(1)}, bf16[16,3584]{1,0:T(8,128)(2,1)S(1)}, u32[]{:S(2)}, u32[]{:S(2)}) collective-permute-start(bf16[16,3584]{1,0:T(8,128)(2,1)S(1)} %get-tuple-element.159), channel_id=1, source_target_pairs={{4,0},{8,4},{12,8},{14,12},{10,14},{6,10},{2,6},{0,2},{5,1},{9,5},... | collective-permute-start | bytes 344072 | tf_op jit(solution)/shard_map/ppermute | solution.py:748
  166.9 5.6 %collective-permute-start.45 = (bf16[16,3584]{1,0:T(8,128)(2,1)S(1)}, bf16[16,3584]{1,0:T(8,128)(2,1)S(1)}, u32[]{:S(2)}, u32[]{:S(2)}) collective-permute-start(bf16[16,3584]{1,0:T(8,128)(2,1)S(1)} %get-tuple-element.147), channel_id=1, source_target_pairs={{0,4},{4,8},{8,12},{12,14},{14,10},{10,6},{6,2},{2,0},{1,5},{5,9},... | collective-permute-start | bytes 344072 | tf_op jit(solution)/shard_map/ppermute | solution.py:745
  167.5 5.0 %collective-permute-start.46 = (bf16[16,3584]{1,0:T(8,128)(2,1)S(1)}, bf16[16,3584]{1,0:T(8,128)(2,1)S(1)}, u32[]{:S(2)}, u32[]{:S(2)}) collective-permute-start(bf16[16,3584]{1,0:T(8,128)(2,1)S(1)} %get-tuple-element.148), channel_id=1, source_target_pairs={{4,0},{8,4},{12,8},{14,12},{10,14},{6,10},{2,6},{0,2},{5,1},{9,5},... | collective-permute-start | bytes 344072 | tf_op jit(solution)/shard_map/ppermute | solution.py:748
  170.4 6.2 %collective-permute-start.56 = (bf16[16,3584]{1,0:T(8,128)(2,1)S(1)}, bf16[16,3584]{1,0:T(8,128)(2,1)S(1)}, u32[]{:S(2)}, u32[]{:S(2)}) collective-permute-start(bf16[16,3584]{1,0:T(8,128)(2,1)S(1)} %get-tuple-element.160), channel_id=1, source_target_pairs={{0,4},{4,8},{8,12},{12,14},{14,10},{10,6},{6,2},{2,0},{1,5},{5,9},... | collective-permute-start | bytes 344072 | tf_op jit(solution)/shard_map/ppermute | solution.py:745
  171.7 4.9 %collective-permute-start.57 = (bf16[16,3584]{1,0:T(8,128)(2,1)S(1)}, bf16[16,3584]{1,0:T(8,128)(2,1)S(1)}, u32[]{:S(2)}, u32[]{:S(2)}) collective-permute-start(bf16[16,3584]{1,0:T(8,128)(2,1)S(1)} %get-tuple-element.161), channel_id=1, source_target_pairs={{4,0},{8,4},{12,8},{14,12},{10,14},{6,10},{2,6},{0,2},{5,1},{9,5},... | collective-permute-start | bytes 344072 | tf_op jit(solution)/shard_map/ppermute | solution.py:748
  173.2 4.8 %collective-permute-start.47 = (bf16[16,3584]{1,0:T(8,128)(2,1)S(1)}, bf16[16,3584]{1,0:T(8,128)(2,1)S(1)}, u32[]{:S(2)}, u32[]{:S(2)}) collective-permute-start(bf16[16,3584]{1,0:T(8,128)(2,1)S(1)} %get-tuple-element.149), channel_id=1, source_target_pairs={{0,4},{4,8},{8,12},{12,14},{14,10},{10,6},{6,2},{2,0},{1,5},{5,9},... | collective-permute-start | bytes 344072 | tf_op jit(solution)/shard_map/ppermute | solution.py:745
  174.5 4.8 %collective-permute-start.48 = (bf16[16,3584]{1,0:T(8,128)(2,1)S(1)}, bf16[16,3584]{1,0:T(8,128)(2,1)S(1)}, u32[]{:S(2)}, u32[]{:S(2)}) collective-permute-start(bf16[16,3584]{1,0:T(8,128)(2,1)S(1)} %get-tuple-element.150), channel_id=1, source_target_pairs={{4,0},{8,4},{12,8},{14,12},{10,14},{6,10},{2,6},{0,2},{5,1},{9,5},... | collective-permute-start | bytes 344072 | tf_op jit(solution)/shard_map/ppermute | solution.py:748
  177.4 2.7 %collective-permute-start.59 = (bf16[16,3584]{1,0:T(8,128)(2,1)S(1)}, bf16[16,3584]{1,0:T(8,128)(2,1)S(1)}, u32[]{:S(2)}, u32[]{:S(2)}) collective-permute-start(bf16[16,3584]{1,0:T(8,128)(2,1)S(1)} %get-tuple-element.164), channel_id=1, source_target_pairs={{0,1},{1,0},{2,3},{3,2},{4,5},{5,4},{6,7},{7,6},{8,9},{9,8},{10,11... | collective-permute-start | bytes 344072 | tf_op jit(solution)/shard_map/ppermute | solution.py:751
  180.0 1.4 collective-permute-start.58
  (31 other events, 270.3 us)

commit v4 on v3

--- a/solution.py
+++ b/solution.py
@@ -220,8 +220,9 @@
     decoded = jnp.concatenate([decoded, jnp.zeros_like(decoded)], 0).astype(bf16)
     out = jnp.concatenate(outs, 1) + mm(onehot((rows, 16), 0, 1), decoded)
     out = out.astype(bf16)
-    main[...] = out[: rows // 2]
-    extra[...] = out[rows // 2 :]
+    at = pl.ds(pl.multiple_of(step * out.shape[1], out.shape[1]), out.shape[1])
+    main[:, at] = out[: rows // 2]
+    extra[:, at] = out[rows // 2 :]
 
 
 def attend(tab, queries, cache, fresh, vw, part, parts):
@@ -243,7 +244,7 @@
             pl.BlockSpec(fresh.shape[::-1], lambda i: (0, 0)),
             pl.BlockSpec((group, value, vh), lambda i: (part * steps + i, 0, 0)),
         ],
-        out_specs=[pl.BlockSpec((rows // 2, group * vh), lambda i: (0, i))] * 2,
+        out_specs=[whole()] * 2,
         out_shape=[half, half],
         scratch_shapes=[
             pltpu.VMEM((wide, cols), bf16),
@@ -290,7 +291,7 @@
         in_specs=[smem(), whole()],
         out_specs=[whole()] * ranks,
         out_shape=[jax.ShapeDtypeStruct((2 * half, features), bf16)] * ranks,
-        compiler_params=params(),
+        compiler_params=params(8),
         cost_estimate=cost(0, 4 * residual.size),
         name="pack",
     )(tab, residual)
@@ -318,22 +319,22 @@
         in_specs=[smem()] + [whole()] * len(flat),
         out_specs=[whole()] * len(choices),
         out_shape=[jax.ShapeDtypeStruct(b.shape, b.dtype) for _, b in choices],
-        compiler_params=params(),
+        compiler_params=params(6),
         cost_estimate=cost(0, 3 * sum(2 * b.size for _, b in choices)),
         name="route",
     )(tab, *flat)
 
 
-def project_kernel(source, nodes, block, half, first, tab, *refs):
+def project_kernel(source, nodes, block, half, part, first, tab, *refs):
     blocks, refs = refs[: nodes + 1], refs[nodes + 1 :]
     before = None if first else refs[0]
     weight, kept, given, acc = refs[-4:]
     step = pl.program_id(0)
-    depth = weight.shape[0]
+    depth = blocks[0].shape[1] // pl.num_programs(0)
     columns = pl.ds(pl.multiple_of(step * depth, 128), depth)
     last = jnp.where(tab[BUSY] == 1, blocks[nodes][:, columns], blocks[nodes - 1][:, columns])
     lhs = jnp.concatenate([b[:, columns] for b in blocks[: nodes - 1]] + [last], 0)
-    got = mm(lhs, weight[...])
+    got = mm(lhs, weight[pl.ds(pl.multiple_of(part * blocks[0].shape[1] + step * depth, 128), depth)])
 
     @pl.when(step == 0)
     def _():
@@ -353,15 +354,15 @@
             given[k * half : (k + 1) * half] = other.astype(bf16)
 
 
-def project_part_kernel(nodes, first, tab, *refs):
+def project_part_kernel(nodes, part, first, tab, *refs):
     blocks, refs = refs[: nodes + 1], refs[nodes + 1 :]
     weight, out = refs[-2:]
     step = pl.program_id(0)
-    depth = weight.shape[0]
+    depth = blocks[0].shape[1] // pl.num_programs(0)
     columns = pl.ds(pl.multiple_of(step * depth, 128), depth)
     last = jnp.where(tab[BUSY] == 1, blocks[nodes][:, columns], blocks[nodes - 1][:, columns])
     lhs = jnp.concatenate([b[:, columns] for b in blocks[: nodes - 1]] + [last], 0)
-    got = mm(lhs, weight[...])
+    got = mm(lhs, weight[pl.ds(pl.multiple_of(part * blocks[0].shape[1] + step * depth, 128), depth)])
 
     @pl.when(step == 0)
     def _():
@@ -382,25 +383,24 @@
     total = jax.ShapeDtypeStruct((nodes * block, features), f32)
     final = part == parts - 1
     first = before is None
-    ins = [smem()] + [whole()] * (nodes + 1 + (not first))
-    ins += [pl.BlockSpec((depth, features), lambda i: (part * steps + i, 0))]
+    ins = [smem()] + [whole()] * (nodes + 2 + (not first))
     args = [tab, *blocks] + ([] if first else [before]) + [weight]
     estimate = cost(
         2 * nodes * block * width * features, 2 * (nodes * block * width + width * features)
     )
     if not final:
         return pl.pallas_call(
-            functools.partial(project_part_kernel, nodes, first),
+            functools.partial(project_part_kernel, nodes, part, first),
             grid=(steps,),
             in_specs=ins,
             out_specs=pl.BlockSpec(total.shape, lambda i: (0, 0)),
             out_shape=total,
-            compiler_params=params(),
+            compiler_params=params(16),
             cost_estimate=estimate,
             name="project",
         )(*args)
     return pl.pallas_call(
-        functools.partial(project_kernel, table.source, nodes, block, half, first),
+        functools.partial(project_kernel, table.source, nodes, block, half, part, first),
         grid=(steps,),
         in_specs=ins,
         out_specs=[pl.BlockSpec((nodes * half, features), lambda i: (0, 0))] * 2,
@@ -409,7 +409,7 @@
             jax.ShapeDtypeStruct((nodes * half, features), bf16),
         ],
         scratch_shapes=[pltpu.VMEM(total.shape, f32)],
-        compiler_params=params(),
+        compiler_params=params(16),
         cost_estimate=estimate,
         name="project",
     )(*args)
@@ -441,15 +441,18 @@
         in_specs=[smem()] + [whole()] * (2 + len(res)),
         out_specs=whole(),
         out_shape=jax.ShapeDtypeStruct(other.shape, bf16),
-        compiler_params=params(),
+        compiler_params=params(8),
         cost_estimate=cost(0, 10 * other.size),
         name="stream",
     )(tab, kept, other, *res)
 
 
-def expand_kernel(count, first, final, width, turned, tab, *refs):
-    mines, theirs = refs[:count], refs[count : 2 * count]
-    refs = refs[2 * count :]
+def expand_kernel(pieces, first, final, width, turned, owners, tab, *refs):
+    count = len(pieces)
+    blocks = []
+    for number in pieces:
+        blocks.append(refs[: 2 * number])
+        refs = refs[2 * number :]
     gain, gate, up = refs[:3]
     refs = refs[3:]
     if not first:
@@ -462,12 +465,16 @@
 
         @pl.when(step == i)
         def _(i=i):
-            both = jnp.concatenate([mines[i][...], theirs[i][...]], 0).astype(f32)
+            both = jnp.concatenate([x[...] for x in blocks[i]], 0).astype(f32)
+            rows_of = both.shape[1]
             scaled = (both * gain[0]).astype(bf16)
-            times = mm_nt if turned else mm
+            if turned:
+                at = pl.ds(pl.multiple_of(tab[owners[i]] * rows_of, 128), rows_of)
+                products = mm_nt(scaled, gate[:, at]), mm_nt(scaled, up[:, at])
+            else:
+                products = mm(scaled, gate[...]), mm(scaled, up[...])
             values = (
-                times(scaled, gate[...]),
-                times(scaled, up[...]),
+                *products,
                 jnp.sum(both * both, axis=1, keepdims=True),
             )
             for n, (ref, value) in enumerate(zip((gates, ups, squares), values)):
@@ -487,7 +494,9 @@
 
 def expand(tab, mines, theirs, owners, gain, gate, up, before, final):
     count = len(mines)
-    rows, features = mines[0].shape
+    pieces = tuple(len(x) for x in mines)
+    rows, features = sum(x.shape[0] for x in mines[0]), mines[0][0].shape[1]
+    arrays = [x for own, other in zip(mines, theirs) for x in (*own, *other)]
     units = gate.shape[1]
     first = before is None
     width = gate.shape[0]
@@ -502,12 +511,12 @@
         return pl.BlockSpec(shape, lambda i, tab: (0,) * len(shape))
 
     sums = [(2 * rows, units), (2 * rows, units), (2 * rows, 1)]
-    ins = [full((rows, features))] * (2 * count)
+    ins = [full(x.shape) for x in arrays]
     ins += [pl.BlockSpec((1, 1, features), lambda i, tab: (owner(i, tab), 0, 0))]
     turned = features % 128 == 0
     if turned:
         gate, up = gate.T, up.T
-        ins += [pl.BlockSpec((units, features), lambda i, tab: (0, owner(i, tab)))] * 2
+        ins += [pl.BlockSpec(memory_space=pltpu.VMEM)] * 2
     else:
         ins += [pl.BlockSpec((features, units), lambda i, tab: (owner(i, tab), 0))] * 2
     if not first:
@@ -515,7 +524,7 @@
     shapes = [jax.ShapeDtypeStruct(s, f32) for s in sums]
     out_shapes = [jax.ShapeDtypeStruct((2 * rows, units), bf16)] if final else shapes
     return pl.pallas_call(
-        functools.partial(expand_kernel, count, first, final, width, turned),
+        functools.partial(expand_kernel, pieces, first, final, width, turned, owners),
         grid_spec=pltpu.PrefetchScalarGridSpec(
             num_scalar_prefetch=1,
             grid=(count,),
@@ -524,12 +533,12 @@
             scratch_shapes=[pltpu.VMEM(s, f32) for s in sums] if final else [],
         ),
         out_shape=out_shapes,
-        compiler_params=params(56),
+        compiler_params=params(20),
         cost_estimate=cost(
             8 * count * rows * features * units, count * (4 * features * units + 4 * rows * features)
         ),
         name="expand",
-    )(tab, *mines, *theirs, gain, gate, up, *([] if first else before))
+    )(tab, *arrays, gain, gate, up, *([] if first else before))
 
 
 def collect_kernel(owners, tab, *refs):
@@ -560,15 +569,16 @@
             out_specs=pl.BlockSpec(shape, lambda i, tab: (0, 0, 0)),
         ),
         out_shape=jax.ShapeDtypeStruct(shape, bf16),
-        compiler_params=params(),
+        compiler_params=params(10),
         cost_estimate=cost(0, 8 * ranks * half * features),
         name="collect",
     )(tab, *args)
 
 
-def contract_kernel(hidden, weight, mine, given):
-    got = mm(hidden[...], weight[...]).astype(bf16)
-    rows = mine.shape[0]
+def contract_kernel(begin, hidden, weight, mine, given):
+    rows, wide = mine.shape
+    at = pl.ds(pl.multiple_of(begin + pl.program_id(0) * wide, 128), wide)
+    got = mm(hidden[...], weight[:, at]).astype(bf16)
     mine[...] = got[:rows]
     given[...] = got[rows:]
 
@@ -580,15 +590,15 @@
     steps = columns // wide
     out = jax.ShapeDtypeStruct((rows // 2, columns), bf16)
     return pl.pallas_call(
-        contract_kernel,
+        functools.partial(contract_kernel, part * columns),
         grid=(steps,),
         in_specs=[
             pl.BlockSpec((rows, units), lambda i: (0, 0)),
-            pl.BlockSpec((units, wide), lambda i: (0, part * steps + i)),
+            whole(),
         ],
         out_specs=[pl.BlockSpec((rows // 2, wide), lambda i: (0, i))] * 2,
         out_shape=[out, out],
-        compiler_params=params(),
+        compiler_params=params(16),
         cost_estimate=cost(2 * rows * units * columns, 2 * (units + rows) * columns),
         name="contract",
     )(hidden, weight)
@@ -630,7 +640,7 @@
             out_specs=[full, full],
         ),
         out_shape=[out, out],
-        compiler_params=params(),
+        compiler_params=params(8),
         cost_estimate=cost(0, 16 * half * columns),
         name="add",
     )(tab, mine, theirs, mine, theirs, *got)
@@ -675,7 +685,7 @@
             out_specs=[full, full],
         ),
         out_shape=[out, out],
-        compiler_params=params(),
+        compiler_params=params(12),
         cost_estimate=cost(0, 24 * half * columns),
         name="close",
     )(tab, mine, theirs, mine, theirs, got_f[-1], got_f[-2], got_b[-1], got_b[-2], own)
@@ -702,7 +712,7 @@
         in_specs=[smem()] + [whole()] * (2 * len(kept)),
         out_specs=whole(),
         out_shape=jax.ShapeDtypeStruct((2 * half, columns * len(kept)), bf16),
-        compiler_params=params(),
+        compiler_params=params(8),
         cost_estimate=cost(0, 8 * half * columns * len(kept)),
         name="finish",
     )(tab, *kept, *got)
@@ -773,6 +783,8 @@
         main, extra = attend(
             tab, queries, latent_cache, new_latent, value_weight, part, attention_parts
         )
+        if part == attention_parts - 1:
+            main, extra, res = lax.optimization_barrier((main, extra, res))
         behind, ahead = [], []
         for step in range(reach):
             if step == 0:
@@ -788,8 +800,6 @@
             behind.append(send_next(out_f))
             ahead.append(send_prev(out_b))
         gathered.append([main] + behind + ahead + [extra])
-    tied = lax.optimization_barrier((gathered[0], res))
-    gathered[0], res = tied
     for part in range(attention_parts):
         total = project(
             tab, table, gathered[part], total, out_weight, part, attention_parts, cores
@@ -798,24 +808,28 @@
     stream = stream_of(tab, kept, swap(given), res)
 
     gain = norm_gain.reshape(ranks, 1, features)
-    sums = expand(tab, [stream], [swap(stream)], [RANK], gain, gate_weight, up_weight, None, False)
+    sums = expand(tab, [[stream]], [[swap(stream)]], [RANK], gain, gate_weight, up_weight, None, False)
     blocks, owners = [stream], [RANK]
     fore, back = stream, stream
     cut = -(-stream.shape[0] // 32) * 16
+    done = None
     for step in range(1, reach + 1):
+        if done is not None:
+            back, fore, done = lax.optimization_barrier((back, fore, done))
+        done = sums
         if step < reach:
             back, fore = send_next(back), send_prev(fore)
-            arrived = [back, fore]
+            arrived = [[back], [fore]]
             from_owner = [table.owner_back + step, table.owner_fore + step]
         else:
-            last = [send_next(back[:cut]), send_prev(fore[cut:])]
-            arrived = [jnp.concatenate(last, 0)]
+            arrived = [[send_next(back[:cut]), send_prev(fore[cut:])]]
             from_owner = [table.owner_back + step]
-        others = [swap(x) for x in arrived]
+        tied, sums = lax.optimization_barrier((arrived, sums))
+        others = [[swap(x) for x in pieces] for pieces in tied]
         sums = expand(
             tab, arrived, others, from_owner, gain, gate_weight, up_weight, sums, step == reach
         )
-        blocks += arrived
+        blocks += [x[0] if len(x) == 1 else jnp.concatenate(x, 0) for x in arrived]
         owners += from_owner
     (hidden,) = sums
     own = collect(tab, blocks, owners, half)

time: 183 us -> 154 us (0.84)
  Pallas kernels: 75.7 us -> 57.6 us
  waiting for transfers between devices: 40.1 us -> 31.2 us
  local copies, waits for them, and re-layouts: 9.52 us -> 4.37 us
  starting transfers between devices: 55.5 us -> 58.3 us
    pallas_call x8, Pallas kernels: 38 us -> 19.2 us  [the longest x5 12.1 us: expand(): pl.pallas_call(functools.partial(expand_kernel, pieces, first, final, wid...]
    ppermute x20, starting transfers between devices: 30.9 us -> 19.5 us  [send_next(): return lax.ppermute(x, 'blk', forward)]
    ppermute x20, starting transfers between devices: 12.6 us -> 22 us  [send_prev(): return lax.ppermute(x, 'blk', backward)]
    ppermute x20, waiting for transfers between devices: 19.1 us -> 12.6 us  [send_next(): return lax.ppermute(x, 'blk', forward)]
    ppermute x7, waiting for transfers between devices: 5.48 us -> 0.02 us  [on_device(): res.append(lax.ppermute(packed[shift], 'blk', pairs))]
    unnamed x71 -> x36, local copies, waits for them, and re-layouts: 8.85 us -> 4.34 us
    ppermute x7, starting transfers between devices: 9.49 us -> 13.7 us  [on_device(): res.append(lax.ppermute(packed[shift], 'blk', pairs))]
    ppermute x20, waiting for transfers between devices: 12.6 us -> 14.8 us  [send_prev(): return lax.ppermute(x, 'blk', backward)]
  transfers between devices with their start and end apart: 60 -> 61, of which waited for: 22 -> 28; matrix products, arithmetic and copies ran while one was open for 1% -> 0% of each run, Pallas kernels for 29% -> 30%
where the time goes in v4:
time: 154 us; the launch traced here: 153 us
  starting transfers between devices  58.3 us (38%)
  Pallas kernels  57.6 us (37%)
  waiting for transfers between devices  31.2 us (20%)
  local copies, waits for them, and re-layouts  4.37 us (3%)
    ppermute x20, starting transfers between devices, send_prev(): return lax.ppermute(x, 'blk', backward)  22 us
    ppermute x20, starting transfers between devices, send_next(): return lax.ppermute(x, 'blk', forward)  19.5 us
    pallas_call x2, Pallas kernels, attend(): pl.pallas_call(functools.partial(attend_kernel, heads, group, rows, lat,...  17 us
    ppermute x20, waiting for transfers between devices, send_prev(): return lax.ppermute(x, 'blk', backward)  14.8 us
    ppermute x7, starting transfers between devices, on_device(): res.append(lax.ppermute(packed[shift], 'blk', pairs))  13.7 us
    ppermute x20, waiting for transfers between devices, send_next(): return lax.ppermute(x, 'blk', forward)  12.6 us
    pallas_call x5, Pallas kernels, expand(): pl.pallas_call(functools.partial(expand_kernel, pieces, first, final, wid...  12.1 us
    pallas_call x8, Pallas kernels, route(): pl.pallas_call(route_kernel, in_specs=[smem()] + [whole()] * len(flat), o...  6.25 us
  transfers between devices with their start and end apart: 61, of which 28 were waited for; matrix products, arithmetic and copies ran while one was open for 0% of the time, Pallas kernels for 30%

profile of v4, /device:TPU:0, one launch (start us, length us, event | category | flops | bytes accessed | tf_op | source)
XLA Modules:
  0.0 153.3 jit_solution(14534507756669231383)
XLA Ops:
  1.3 1.3 table.1.tab
  2.6 1.2 copy-done.4
  4.5 1.2 pack.1
  6.4 3.0 %collective-permute-start = (bf16[32,896]{1,0:T(8,128)(2,1)S(1)}, bf16[32,896]{1,0:T(8,128)(2,1)S(1)}, u32[]{:S(2)}, u32[]{:S(2)}) collective-permute-start(bf16[32,896]{1,0:T(8,128)(2,1)S(1)} %get-tuple-element.100), channel_id=1, source_target_pairs={{0,2},{2,4},{4,6},{6,8},{8,10},{10,12},{12,14},{14,0},{1,3},{3,5},... | collective-permute-start | bytes 172040 | tf_op jit(solution)/shard_map/ppermute | solution.py:778
  9.3 1.6 %collective-permute-start.1 = (bf16[32,896]{1,0:T(8,128)(2,1)S(1)}, bf16[32,896]{1,0:T(8,128)(2,1)S(1)}, u32[]{:S(2)}, u32[]{:S(2)}) collective-permute-start(bf16[32,896]{1,0:T(8,128)(2,1)S(1)} %get-tuple-element.101), channel_id=1, source_target_pairs={{0,4},{2,6},{4,8},{6,10},{8,12},{10,14},{12,0},{14,2},{1,5},{3,7},... | collective-permute-start | bytes 172040 | tf_op jit(solution)/shard_map/ppermute | solution.py:778
  10.9 2.5 %collective-permute-start.2 = (bf16[32,896]{1,0:T(8,128)(2,1)S(1)}, bf16[32,896]{1,0:T(8,128)(2,1)S(1)}, u32[]{:S(2)}, u32[]{:S(2)}) collective-permute-start(bf16[32,896]{1,0:T(8,128)(2,1)S(1)} %get-tuple-element.102), channel_id=1, source_target_pairs={{0,6},{2,8},{4,10},{6,12},{8,14},{10,0},{12,2},{14,4},{1,7},{3,9},... | collective-permute-start | bytes 172040 | tf_op jit(solution)/shard_map/ppermute | solution.py:778
  13.4 1.2 collective-permute-start.3
  14.7 8.6 %attend.3 = (bf16[32,2048]{1,0:T(8,128)(2,1)}, bf16[32,2048]{1,0:T(8,128)(2,1)}) custom-call(s32[44]{0:T(128)} %table.1.tab, bf16[64,18432]{1,0:T(8,128)(2,1)} %q.3, bf16[8,576,256]{2,1,0:T(8,128)(2,1)} %cache.3, bf16[64,576]{1,0:T(8,128)(2,1)} %bitcast.29, bf16[32,512,128]{2,1,0:T(8,128)(2,1)} %vw.3), custom_call_target="tpu_custom_call" | custom-call | flops 713031680 | bytes 5636096 | tf_op jit(solution)/shard_map/attend/pallas_call | solution.py:237
  23.3 0.9 copy-done
  24.2 1.0 route.12
  25.1 1.6 %collective-permute-start.15 = (bf16[32,2048]{1,0:T(8,128)(2,1)S(1)}, bf16[32,2048]{1,0:T(8,128)(2,1)S(1)}, u32[]{:S(2)}, u32[]{:S(2)}) collective-permute-start(bf16[32,2048]{1,0:T(8,128)(2,1)S(1)} %route.12), channel_id=1, source_target_pairs={{0,4},{4,8},{8,12},{12,14},{14,10},{10,6},{6,2},{2,0},{1,5},{5,9},... | collective-permute-start | bytes 393224 | tf_op jit(solution)/shard_map/ppermute | solution.py:755
  27.2 2.6 %collective-permute-start.4 = (bf16[32,896]{1,0:T(8,128)(2,1)}, bf16[32,896]{1,0:T(8,128)(2,1)S(1)}, u32[]{:S(2)}, u32[]{:S(2)}) collective-permute-start(bf16[32,896]{1,0:T(8,128)(2,1)} %get-tuple-element.104), channel_id=1, source_target_pairs={{0,10},{2,12},{4,14},{6,0},{8,2},{10,4},{12,6},{14,8},{1,11},{3,13... | collective-permute-start | bytes 172040 | tf_op jit(solution)/shard_map/ppermute | solution.py:778
  29.9 1.3 collective-permute-start.5
  31.2 1.4 collective-permute-start.6
  32.6 8.4 %attend.2 = (bf16[32,2048]{1,0:T(8,128)(2,1)}, bf16[32,2048]{1,0:T(8,128)(2,1)}) custom-call(s32[44]{0:T(128)} %table.1.tab, bf16[64,18432]{1,0:T(8,128)(2,1)} %q.3, bf16[8,576,256]{2,1,0:T(8,128)(2,1)} %cache.3, bf16[64,576]{1,0:T(8,128)(2,1)} %bitcast.30, bf16[32,512,128]{2,1,0:T(8,128)(2,1)} %vw.3), custom_call_target="tpu_custom_call" | custom-call | flops 713031680 | bytes 5636096 | tf_op jit(solution)/shard_map/attend/pallas_call | solution.py:237
  42.0 1.0 route.8
  43.7 1.4 collective-permute-start.8
  45.0 0.9 route.13
  46.7 1.4 collective-permute-start.18
  48.2 0.9 collective-permute-done.8.refs_3_.refs_2_.refs_5_
  49.1 1.1 route.9
  50.3 2.0 %collective-permute-start.10 = (bf16[32,2048]{1,0:T(8,128)(2,1)S(1)}, bf16[32,2048]{1,0:T(8,128)(2,1)S(1)}, u32[]{:S(2)}, u32[]{:S(2)}) collective-permute-start(bf16[32,2048]{1,0:T(8,128)(2,1)S(1)} %get-tuple-element.110), channel_id=1, source_target_pairs={{4,0},{8,4},{12,8},{14,12},{10,14},{6,10},{2,6},{0,2},{5,1},{9,5},... | collective-permute-start | bytes 393224 | tf_op jit(solution)/shard_map/ppermute | solution.py:758
  53.3 2.0 %collective-permute-start.20 = (bf16[32,2048]{1,0:T(8,128)(2,1)S(1)}, bf16[32,2048]{1,0:T(8,128)(2,1)S(1)}, u32[]{:S(2)}, u32[]{:S(2)}) collective-permute-start(bf16[32,2048]{1,0:T(8,128)(2,1)S(1)} %get-tuple-element.120), channel_id=1, source_target_pairs={{4,0},{8,4},{12,8},{14,12},{10,14},{6,10},{2,6},{0,2},{5,1},{9,5},... | collective-permute-start | bytes 393224 | tf_op jit(solution)/shard_map/ppermute | solution.py:758
  55.4 1.2 collective-permute-done.9.refs_1_.refs_0_.refs_2_
  57.8 1.5 %collective-permute-start.12 = (bf16[32,2048]{1,0:T(8,128)(2,1)S(1)}, bf16[32,2048]{1,0:T(8,128)(2,1)S(1)}, u32[]{:S(2)}, u32[]{:S(2)}) collective-permute-start(bf16[32,2048]{1,0:T(8,128)(2,1)S(1)} %get-tuple-element.112), channel_id=1, source_target_pairs={{4,0},{8,4},{12,8},{14,12},{10,14},{6,10},{2,6},{0,2},{5,1},{9,5},... | collective-permute-start | bytes 393224 | tf_op jit(solution)/shard_map/ppermute | solution.py:758
  60.7 1.4 collective-permute-start.22
  63.7 0.9 collective-permute-start.13
  64.6 1.2 collective-permute-start.14
  65.9 2.9 %project.2.refs_10_ = f32[288,896]{1,0:T(8,128)S(1)} custom-call(s32[44]{0:T(128)S(1)} %copy-done.8, bf16[32,2048]{1,0:T(8,128)(2,1)} %get-tuple-element.115.refs_1_.refs_0_, bf16[32,2048]{1,0:T(8,128)(2,1)S(1)} %collective-permute-done.15.refs_1_.refs_0_, bf16[32,2048]{1,0:T(8,128)(2,1)S(1)} %collective-permute-done.17.refs_1_.refs_0_.refs_2_, ...), custom_call_target="tpu_custom_call" | custom-call | flops 1056964608 | bytes 4849664 | tf_op jit(solution)/shard_map/project/pallas_call | solution.py:392
  69.6 3.2 %project.3 = (f32[144,896]{1,0:T(8,128)S(1)}, bf16[144,896]{1,0:T(8,128)(2,1)S(1)}) custom-call(s32[44]{0:T(128)S(1)} %copy-done.8, bf16[32,2048]{1,0:T(8,128)(2,1)} %get-tuple-element.107.refs_1_.refs_0_, bf16[32,2048]{1,0:T(8,128)(2,1)S(1)} %collective-permute-done.7.refs_1_.refs_0_, bf16[32,2048]{1,0:T(8,128)(2,1)S(1)} %collective-permute-done.9.refs_1_.refs_0_.refs_2_, ...), custom_call_target="tpu_custom_call" | custom-call | flops 1056964608 | bytes 4849664 | tf_op jit(solution)/shard_map/project/pallas_call | solution.py:402
  72.8 1.5 collective-permute-done.23.other
  74.4 1.0 stream.1.refs_0_.refs_1_
  75.5 1.1 collective-permute-start.25
  76.6 0.9 collective-permute-start.24
  77.6 1.7 %expand.5 = (f32[288,576]{1,0:T(8,128)S(1)}, f32[288,576]{1,0:T(8,128)S(1)}, f32[288,1]{1,0:T(8,128)S(1)}) custom-call(s32[44]{0:T(128)S(1)} %copy-done.8, bf16[144,896]{1,0:T(8,128)(2,1)S(1)} %stream.1.refs_0_.refs_1_, bf16[144,896]{1,0:T(8,128)(2,1)S(1)} %collective-permute-done.26.refs_1_, f32[8,1,896]{2,1,0:T(1,128)S(1)} %bitcast.24, ...), custom_call_target="tpu_custom_call" | custom-call | flops 594542592 | bytes 2580480 | tf_op jit(solution)/shard_map/expand/pallas_call | solution.py:526
  79.3 4.7 %collective-permute-done.25.refs_2_.refs_4_.refs_5_ = bf16[144,896]{1,0:T(8,128)(2,1)S(1)} collective-permute-done((bf16[144,896]{1,0:T(8,128)(2,1)S(1)}, bf16[144,896]{1,0:T(8,128)(2,1)S(1)}, u32[]{:S(2)}, u32[]{:S(2)}) %collective-permute-start.25) | collective-permute-done | bytes 258080 | tf_op jit(solution)/shard_map/ppermute | solution.py:758
  85.3 0.9 collective-permute-start.27
  86.3 1.1 collective-permute-start.28
  87.4 2.9 %expand.6 = (f32[288,576]{1,0:T(8,128)S(1)}, f32[288,576]{1,0:T(8,128)S(1)}, f32[288,1]{1,0:T(8,128)S(1)}) custom-call(s32[44]{0:T(128)S(1)} %copy-done.8, bf16[144,896]{1,0:T(8,128)(2,1)S(1)} %collective-permute-done.24.refs_0_.refs_2_.refs_3_, bf16[144,896]{1,0:T(8,128)(2,1)S(1)} %collective-permute-done.29.refs_1_, ...), custom_call_target="tpu_custom_call" | custom-call | flops 1189085184 | bytes 5160960 | tf_op jit(solution)/shard_map/expand/pallas_call | solution.py:526
  90.2 3.2 %collective-permute-done.27.refs_0_.refs_6_.refs_7_ = bf16[144,896]{1,0:T(8,128)(2,1)S(1)} collective-permute-done((bf16[144,896]{1,0:T(8,128)(2,1)S(1)}, bf16[144,896]{1,0:T(8,128)(2,1)S(1)}, u32[]{:S(2)}, u32[]{:S(2)}) %collective-permute-start.27) | collective-permute-done | bytes 258080 | tf_op jit(solution)/shard_map/ppermute | solution.py:755
  95.5 1.2 collective-permute-start.32
  96.7 2.9 %expand.7 = (f32[288,576]{1,0:T(8,128)S(1)}, f32[288,576]{1,0:T(8,128)S(1)}, f32[288,1]{1,0:T(8,128)S(1)}) custom-call(s32[44]{0:T(128)S(1)} %copy-done.8, bf16[144,896]{1,0:T(8,128)(2,1)S(1)} %collective-permute-done.27.refs_0_.refs_6_.refs_7_, bf16[144,896]{1,0:T(8,128)(2,1)S(1)} %collective-permute-done.33.refs_1_, ...), custom_call_target="tpu_custom_call" | custom-call | flops 1189085184 | bytes 5160960 | tf_op jit(solution)/shard_map/expand/pallas_call | solution.py:526
  99.6 3.2 %collective-permute-done.31.refs_0_.refs_10_.refs_11_ = bf16[144,896]{1,0:T(8,128)(2,1)S(1)} collective-permute-done((bf16[144,896]{1,0:T(8,128)(2,1)S(1)}, bf16[144,896]{1,0:T(8,128)(2,1)S(1)}, u32[]{:S(2)}, u32[]{:S(2)}) %collective-permute-start.31) | collective-permute-done | bytes 258080 | tf_op jit(solution)/shard_map/ppermute | solution.py:755
  103.9 1.8 %collective-permute-start.35 = (bf16[80,896]{1,0:T(8,128)(2,1)S(1)}, bf16[80,896]{1,0:T(8,128)(2,1)S(1)}, u32[]{:S(2)}, u32[]{:S(2)}) collective-permute-start(bf16[80,896]{1,0:T(8,128)(2,1)S(1)} %slice.6), channel_id=1, source_target_pairs={{0,4},{4,8},{8,12},{12,14},{14,10},{10,6},{6,2},{2,0},{1,5},{5,9},... | collective-permute-start | bytes 430088 | tf_op jit(solution)/shard_map/ppermute | solution.py:755
  106.0 2.9 %expand.8 = (f32[288,576]{1,0:T(8,128)S(1)}, f32[288,576]{1,0:T(8,128)S(1)}, f32[288,1]{1,0:T(8,128)S(1)}) custom-call(s32[44]{0:T(128)S(1)} %copy-done.8, bf16[144,896]{1,0:T(8,128)(2,1)S(1)} %collective-permute-done.31.refs_0_.refs_10_.refs_11_, bf16[144,896]{1,0:T(8,128)(2,1)S(1)} %collective-permute-done.37.refs_1_, ...), custom_call_target="tpu_custom_call" | custom-call | flops 1189085184 | bytes 5160960 | tf_op jit(solution)/shard_map/expand/pallas_call | solution.py:526
  108.9 1.6 %collective-permute-done.36.refs_1_ = bf16[64,896]{1,0:T(8,128)(2,1)S(1)} collective-permute-done((bf16[64,896]{1,0:T(8,128)(2,1)S(1)}, bf16[64,896]{1,0:T(8,128)(2,1)S(1)}, u32[]{:S(2)}, u32[]{:S(2)}) %collective-permute-start.36) | collective-permute-done | bytes 114720 | tf_op jit(solution)/shard_map/ppermute | solution.py:758
  111.1 1.0 collective-permute-done.40.refs_3_
  112.1 1.8 %expand.9.hidden = bf16[288,576]{1,0:T(8,128)(2,1)S(1)} custom-call(s32[44]{0:T(128)S(1)} %copy-done.8, bf16[80,896]{1,0:T(8,128)(2,1)S(1)} %collective-permute-done.35.refs_0_, bf16[64,896]{1,0:T(8,128)(2,1)S(1)} %collective-permute-done.36.refs_1_, bf16[80,896]{1,0:T(8,128)(2,1)S(1)} %collective-permute-done.39.refs_2_, ...), custom_call_target="tpu_custom_call" | custom-call | flops 594542592 | bytes 2580480 | tf_op jit(solution)/shard_map/expand/pallas_call | solution.py:526
  114.0 2.1 %contract.3 = (bf16[144,3584]{1,0:T(8,128)(2,1)S(1)}, bf16[144,3584]{1,0:T(8,128)(2,1)S(1)}) custom-call(bf16[288,576]{1,0:T(8,128)(2,1)S(1)} %expand.9.hidden, bf16[576,7168]{1,0:T(8,128)(2,1)S(1)} %bitcast.21), custom_call_target="tpu_custom_call" | custom-call | flops 1189085184 | bytes 6193152 | tf_op jit(solution)/shard_map/contract/pallas_call | solution.py:592
  116.5 2.1 %contract.2 = (bf16[144,3584]{1,0:T(8,128)(2,1)S(1)}, bf16[144,3584]{1,0:T(8,128)(2,1)S(1)}) custom-call(bf16[288,576]{1,0:T(8,128)(2,1)S(1)} %expand.9.hidden, bf16[576,7168]{1,0:T(8,128)(2,1)S(1)} %bitcast.21), custom_call_target="tpu_custom_call" | custom-call | flops 1189085184 | bytes 6193152 | tf_op jit(solution)/shard_map/contract/pallas_call | solution.py:592
  119.5 1.6 %collective-permute-start.51 = (bf16[16,3584]{1,0:T(8,128)(2,1)S(1)}, bf16[16,3584]{1,0:T(8,128)(2,1)S(1)}, u32[]{:S(2)}, u32[]{:S(2)}) collective-permute-start(bf16[16,3584]{1,0:T(8,128)(2,1)S(1)} %get-tuple-element.178), channel_id=1, source_target_pairs={{0,4},{4,8},{8,12},{12,14},{14,10},{10,6},{6,2},{2,0},{1,5},{5,9},... | collective-permute-start | bytes 344072 | tf_op jit(solution)/shard_map/ppermute | solution.py:755
  122.1 1.6 %collective-permute-start.42 = (bf16[16,3584]{1,0:T(8,128)(2,1)S(1)}, bf16[16,3584]{1,0:T(8,128)(2,1)S(1)}, u32[]{:S(2)}, u32[]{:S(2)}) collective-permute-start(bf16[16,3584]{1,0:T(8,128)(2,1)S(1)} %get-tuple-element.167), channel_id=1, source_target_pairs={{0,4},{4,8},{8,12},{12,14},{14,10},{10,6},{6,2},{2,0},{1,5},{5,9},... | collective-permute-start | bytes 344072 | tf_op jit(solution)/shard_map/ppermute | solution.py:755
  124.9 1.3 collective-permute-done.52.refs_1_.refs_2_
  126.8 1.5 collective-permute-start.53
  129.6 1.5 collective-permute-start.44
  131.7 0.9 collective-permute-done.53.refs_1_.refs_0_
  132.6 1.7 %collective-permute-done.54.refs_3_.refs_2_ = bf16[16,3584]{1,0:T(8,128)(2,1)S(1)} collective-permute-done((bf16[16,3584]{1,0:T(8,128)(2,1)S(1)}, bf16[16,3584]{1,0:T(8,128)(2,1)S(1)}, u32[]{:S(2)}, u32[]{:S(2)}) %collective-permute-start.54) | collective-permute-done | bytes 114720 | tf_op jit(solution)/shard_map/ppermute | solution.py:758
  135.8 1.2 collective-permute-start.56
  138.6 1.2 collective-permute-start.47
  142.3 1.2 collective-permute-start.58
  145.1 1.2 collective-permute-start.49
  147.9 1.1 collective-permute-done.48.f_last
  150.7 1.3 collective-permute-done.59.refs_2_
  152.0 1.4 finish.1
  (136 shorter events, 32.9 us)
Async XLA Ops:
  6.4 20.4 %collective-permute-start = (bf16[32,896]{1,0:T(8,128)(2,1)S(1)}, bf16[32,896]{1,0:T(8,128)(2,1)S(1)}, u32[]{:S(2)}, u32[]{:S(2)}) collective-permute-start(bf16[32,896]{1,0:T(8,128)(2,1)S(1)} %get-tuple-element.100), channel_id=1, source_target_pairs={{0,2},{2,4},{4,6},{6,8},{8,10},{10,12},{12,14},{14,0},{1,3},{3,5},... | collective-permute-start | bytes 172040 | tf_op jit(solution)/shard_map/ppermute | solution.py:778
  9.3 17.9 %collective-permute-start.1 = (bf16[32,896]{1,0:T(8,128)(2,1)S(1)}, bf16[32,896]{1,0:T(8,128)(2,1)S(1)}, u32[]{:S(2)}, u32[]{:S(2)}) collective-permute-start(bf16[32,896]{1,0:T(8,128)(2,1)S(1)} %get-tuple-element.101), channel_id=1, source_target_pairs={{0,4},{2,6},{4,8},{6,10},{8,12},{10,14},{12,0},{14,2},{1,5},{3,7},... | collective-permute-start | bytes 172040 | tf_op jit(solution)/shard_map/ppermute | solution.py:778
  10.9 19.0 %collective-permute-start.2 = (bf16[32,896]{1,0:T(8,128)(2,1)S(1)}, bf16[32,896]{1,0:T(8,128)(2,1)S(1)}, u32[]{:S(2)}, u32[]{:S(2)}) collective-permute-start(bf16[32,896]{1,0:T(8,128)(2,1)S(1)} %get-tuple-element.102), channel_id=1, source_target_pairs={{0,6},{2,8},{4,10},{6,12},{8,14},{10,0},{12,2},{14,4},{1,7},{3,9},... | collective-permute-start | bytes 172040 | tf_op jit(solution)/shard_map/ppermute | solution.py:778
  13.4 17.8 %collective-permute-start.3 = (bf16[32,896]{1,0:T(8,128)(2,1)S(1)}, bf16[32,896]{1,0:T(8,128)(2,1)S(1)}, u32[]{:S(2)}, u32[]{:S(2)}) collective-permute-start(bf16[32,896]{1,0:T(8,128)(2,1)S(1)} %get-tuple-element.103), channel_id=1, source_target_pairs={{0,8},{2,10},{4,12},{6,14},{8,0},{10,2},{12,4},{14,6},{1,9},{3,11}... | collective-permute-start | bytes 172040 | tf_op jit(solution)/shard_map/ppermute | solution.py:778
  14.7 51.1 %slice-start.6 = ((s8[7340032]{0:T(1024)(128)(4,1)}), s8[4194304]{0:T(1024)(128)(4,1)S(1)}, s32[]{:S(2)}) async-start(s8[7340032]{0:T(1024)(128)(4,1)} %bitcast.22), calls=%async_computation.6 | async-start | bytes 8388608
  25.1 19.9 %collective-permute-start.15 = (bf16[32,2048]{1,0:T(8,128)(2,1)S(1)}, bf16[32,2048]{1,0:T(8,128)(2,1)S(1)}, u32[]{:S(2)}, u32[]{:S(2)}) collective-permute-start(bf16[32,2048]{1,0:T(8,128)(2,1)S(1)} %route.12), channel_id=1, source_target_pairs={{0,4},{4,8},{8,12},{12,14},{14,10},{10,6},{6,2},{2,0},{1,5},{5,9},... | collective-permute-start | bytes 393224 | tf_op jit(solution)/shard_map/ppermute | solution.py:755
  26.8 18.3 %collective-permute-start.16 = (bf16[32,2048]{1,0:T(8,128)(2,1)}, bf16[32,2048]{1,0:T(8,128)(2,1)S(1)}, u32[]{:S(2)}, u32[]{:S(2)}) collective-permute-start(bf16[32,2048]{1,0:T(8,128)(2,1)} %get-tuple-element.115.refs_1_.refs_0_), channel_id=1, source_target_pairs={{4,0},{8,4},{12,8},{14,12},{10,14},{6,10},{2,6},{0,2},{5,1},{9,5},... | collective-permute-start | bytes 393224 | tf_op jit(solution)/shard_map/ppermute | solution.py:758
  27.2 13.8 %collective-permute-start.4 = (bf16[32,896]{1,0:T(8,128)(2,1)}, bf16[32,896]{1,0:T(8,128)(2,1)S(1)}, u32[]{:S(2)}, u32[]{:S(2)}) collective-permute-start(bf16[32,896]{1,0:T(8,128)(2,1)} %get-tuple-element.104), channel_id=1, source_target_pairs={{0,10},{2,12},{4,14},{6,0},{8,2},{10,4},{12,6},{14,8},{1,11},{3,13... | collective-permute-start | bytes 172040 | tf_op jit(solution)/shard_map/ppermute | solution.py:778
  29.9 11.2 %collective-permute-start.5 = (bf16[32,896]{1,0:T(8,128)(2,1)}, bf16[32,896]{1,0:T(8,128)(2,1)S(1)}, u32[]{:S(2)}, u32[]{:S(2)}) collective-permute-start(bf16[32,896]{1,0:T(8,128)(2,1)} %get-tuple-element.105), channel_id=1, source_target_pairs={{0,12},{2,14},{4,0},{6,2},{8,4},{10,6},{12,8},{14,10},{1,13},{3,15... | collective-permute-start | bytes 172040 | tf_op jit(solution)/shard_map/ppermute | solution.py:778
  31.2 34.6 %slice-start.7 = ((s8[7340032]{0:T(1024)(128)(4,1)}), s8[3145728]{0:T(1024)(128)(4,1)S(1)}, s32[]{:S(2)}) async-start(s8[7340032]{0:T(1024)(128)(4,1)} %bitcast.22), calls=%async_computation.7 | async-start | bytes 6291456
  31.2 9.8 %collective-permute-start.6 = (bf16[32,896]{1,0:T(8,128)(2,1)}, bf16[32,896]{1,0:T(8,128)(2,1)}, u32[]{:S(2)}, u32[]{:S(2)}) collective-permute-start(bf16[32,896]{1,0:T(8,128)(2,1)} %copy-done.9), channel_id=1, source_target_pairs={{0,14},{2,0},{4,2},{6,4},{8,6},{10,8},{12,10},{14,12},{1,15},{3,1}... | collective-permute-start | bytes 172040 | tf_op jit(solution)/shard_map/ppermute | solution.py:778
  42.9 5.2 %collective-permute-start.7 = (bf16[32,2048]{1,0:T(8,128)(2,1)S(1)}, bf16[32,2048]{1,0:T(8,128)(2,1)S(1)}, u32[]{:S(2)}, u32[]{:S(2)}) collective-permute-start(bf16[32,2048]{1,0:T(8,128)(2,1)S(1)} %route.8), channel_id=1, source_target_pairs={{0,4},{4,8},{8,12},{12,14},{14,10},{10,6},{6,2},{2,0},{1,5},{5,9},... | collective-permute-start | bytes 393224 | tf_op jit(solution)/shard_map/ppermute | solution.py:755
  43.7 5.5 %collective-permute-start.8 = (bf16[32,2048]{1,0:T(8,128)(2,1)}, bf16[32,2048]{1,0:T(8,128)(2,1)S(1)}, u32[]{:S(2)}, u32[]{:S(2)}) collective-permute-start(bf16[32,2048]{1,0:T(8,128)(2,1)} %get-tuple-element.107.refs_1_.refs_0_), channel_id=1, source_target_pairs={{4,0},{8,4},{12,8},{14,12},{10,14},{6,10},{2,6},{0,2},{5,1},{9,5},... | collective-permute-start | bytes 393224 | tf_op jit(solution)/shard_map/ppermute | solution.py:758
  46.0 6.3 %collective-permute-start.17 = (bf16[32,2048]{1,0:T(8,128)(2,1)S(1)}, bf16[32,2048]{1,0:T(8,128)(2,1)S(1)}, u32[]{:S(2)}, u32[]{:S(2)}) collective-permute-start(bf16[32,2048]{1,0:T(8,128)(2,1)S(1)} %get-tuple-element.117), channel_id=1, source_target_pairs={{0,4},{4,8},{8,12},{12,14},{14,10},{10,6},{6,2},{2,0},{1,5},{5,9},... | collective-permute-start | bytes 393224 | tf_op jit(solution)/shard_map/ppermute | solution.py:755
  46.7 6.0 %collective-permute-start.18 = (bf16[32,2048]{1,0:T(8,128)(2,1)S(1)}, bf16[32,2048]{1,0:T(8,128)(2,1)S(1)}, u32[]{:S(2)}, u32[]{:S(2)}) collective-permute-start(bf16[32,2048]{1,0:T(8,128)(2,1)S(1)} %get-tuple-element.118), channel_id=1, source_target_pairs={{4,0},{8,4},{12,8},{14,12},{10,14},{6,10},{2,6},{0,2},{5,1},{9,5},... | collective-permute-start | bytes 393224 | tf_op jit(solution)/shard_map/ppermute | solution.py:758
  49.1 28.4 %slice-start.2 = ((s8[8257536]{0:T(1024)(128)(4,1)}), s8[4194304]{0:T(1024)(128)(4,1)S(1)}, s32[]{:S(2)}) async-start(s8[8257536]{0:T(1024)(128)(4,1)} %bitcast.13), calls=%async_computation.2 | async-start | bytes 8388608
  50.2 6.3 %collective-permute-start.9 = (bf16[32,2048]{1,0:T(8,128)(2,1)S(1)}, bf16[32,2048]{1,0:T(8,128)(2,1)S(1)}, u32[]{:S(2)}, u32[]{:S(2)}) collective-permute-start(bf16[32,2048]{1,0:T(8,128)(2,1)S(1)} %get-tuple-element.109), channel_id=1, source_target_pairs={{0,4},{4,8},{8,12},{12,14},{14,10},{10,6},{6,2},{2,0},{1,5},{5,9},... | collective-permute-start | bytes 393224 | tf_op jit(solution)/shard_map/ppermute | solution.py:755
  50.3 6.4 %collective-permute-start.10 = (bf16[32,2048]{1,0:T(8,128)(2,1)S(1)}, bf16[32,2048]{1,0:T(8,128)(2,1)S(1)}, u32[]{:S(2)}, u32[]{:S(2)}) collective-permute-start(bf16[32,2048]{1,0:T(8,128)(2,1)S(1)} %get-tuple-element.110), channel_id=1, source_target_pairs={{4,0},{8,4},{12,8},{14,12},{10,14},{6,10},{2,6},{0,2},{5,1},{9,5},... | collective-permute-start | bytes 393224 | tf_op jit(solution)/shard_map/ppermute | solution.py:758
  53.3 6.2 %collective-permute-start.19 = (bf16[32,2048]{1,0:T(8,128)(2,1)S(1)}, bf16[32,2048]{1,0:T(8,128)(2,1)S(1)}, u32[]{:S(2)}, u32[]{:S(2)}) collective-permute-start(bf16[32,2048]{1,0:T(8,128)(2,1)S(1)} %get-tuple-element.119), channel_id=1, source_target_pairs={{0,4},{4,8},{8,12},{12,14},{14,10},{10,6},{6,2},{2,0},{1,5},{5,9},... | collective-permute-start | bytes 393224 | tf_op jit(solution)/shard_map/ppermute | solution.py:755
  53.3 6.1 %collective-permute-start.20 = (bf16[32,2048]{1,0:T(8,128)(2,1)S(1)}, bf16[32,2048]{1,0:T(8,128)(2,1)S(1)}, u32[]{:S(2)}, u32[]{:S(2)}) collective-permute-start(bf16[32,2048]{1,0:T(8,128)(2,1)S(1)} %get-tuple-element.120), channel_id=1, source_target_pairs={{4,0},{8,4},{12,8},{14,12},{10,14},{6,10},{2,6},{0,2},{5,1},{9,5},... | collective-permute-start | bytes 393224 | tf_op jit(solution)/shard_map/ppermute | solution.py:758
  57.3 5.5 %collective-permute-start.11 = (bf16[32,2048]{1,0:T(8,128)(2,1)S(1)}, bf16[32,2048]{1,0:T(8,128)(2,1)S(1)}, u32[]{:S(2)}, u32[]{:S(2)}) collective-permute-start(bf16[32,2048]{1,0:T(8,128)(2,1)S(1)} %get-tuple-element.111), channel_id=1, source_target_pairs={{0,4},{4,8},{8,12},{12,14},{14,10},{10,6},{6,2},{2,0},{1,5},{5,9},... | collective-permute-start | bytes 393224 | tf_op jit(solution)/shard_map/ppermute | solution.py:755
  57.8 5.3 %collective-permute-start.12 = (bf16[32,2048]{1,0:T(8,128)(2,1)S(1)}, bf16[32,2048]{1,0:T(8,128)(2,1)S(1)}, u32[]{:S(2)}, u32[]{:S(2)}) collective-permute-start(bf16[32,2048]{1,0:T(8,128)(2,1)S(1)} %get-tuple-element.112), channel_id=1, source_target_pairs={{4,0},{8,4},{12,8},{14,12},{10,14},{6,10},{2,6},{0,2},{5,1},{9,5},... | collective-permute-start | bytes 393224 | tf_op jit(solution)/shard_map/ppermute | solution.py:758
  60.1 5.8 %collective-permute-start.21 = (bf16[32,2048]{1,0:T(8,128)(2,1)S(1)}, bf16[32,2048]{1,0:T(8,128)(2,1)S(1)}, u32[]{:S(2)}, u32[]{:S(2)}) collective-permute-start(bf16[32,2048]{1,0:T(8,128)(2,1)S(1)} %get-tuple-element.121), channel_id=1, source_target_pairs={{0,4},{4,8},{8,12},{12,14},{14,10},{10,6},{6,2},{2,0},{1,5},{5,9},... | collective-permute-start | bytes 393224 | tf_op jit(solution)/shard_map/ppermute | solution.py:755
  60.7 5.1 %collective-permute-start.22 = (bf16[32,2048]{1,0:T(8,128)(2,1)S(1)}, bf16[32,2048]{1,0:T(8,128)(2,1)S(1)}, u32[]{:S(2)}, u32[]{:S(2)}) collective-permute-start(bf16[32,2048]{1,0:T(8,128)(2,1)S(1)} %get-tuple-element.122), channel_id=1, source_target_pairs={{4,0},{8,4},{12,8},{14,12},{10,14},{6,10},{2,6},{0,2},{5,1},{9,5},... | collective-permute-start | bytes 393224 | tf_op jit(solution)/shard_map/ppermute | solution.py:758
  63.7 5.0 %collective-permute-start.13 = (bf16[32,2048]{1,0:T(8,128)(2,1)S(1)}, bf16[32,2048]{1,0:T(8,128)(2,1)S(1)}, u32[]{:S(2)}, u32[]{:S(2)}) collective-permute-start(bf16[32,2048]{1,0:T(8,128)(2,1)S(1)} %get-tuple-element.113), channel_id=1, source_target_pairs={{0,4},{4,8},{8,12},{12,14},{14,10},{10,6},{6,2},{2,0},{1,5},{5,9},... | collective-permute-start | bytes 393224 | tf_op jit(solution)/shard_map/ppermute | solution.py:755
  64.6 5.0 %collective-permute-start.14 = (bf16[32,2048]{1,0:T(8,128)(2,1)S(1)}, bf16[32,2048]{1,0:T(8,128)(2,1)S(1)}, u32[]{:S(2)}, u32[]{:S(2)}) collective-permute-start(bf16[32,2048]{1,0:T(8,128)(2,1)S(1)} %get-tuple-element.114), channel_id=1, source_target_pairs={{4,0},{8,4},{12,8},{14,12},{10,14},{6,10},{2,6},{0,2},{5,1},{9,5},... | collective-permute-start | bytes 393224 | tf_op jit(solution)/shard_map/ppermute | solution.py:758
  72.8 1.6 %collective-permute-start.23 = (bf16[144,896]{1,0:T(8,128)(2,1)S(1)}, bf16[144,896]{1,0:T(8,128)(2,1)S(1)}, u32[]{:S(2)}, u32[]{:S(2)}) collective-permute-start(bf16[144,896]{1,0:T(8,128)(2,1)S(1)} %get-tuple-element.124), channel_id=1, source_target_pairs={{0,1},{1,0},{2,3},{3,2},{4,5},{5,4},{6,7},{7,6},{8,9},{9,8},{10,11... | collective-permute-start | bytes 774152 | tf_op jit(solution)/shard_map/ppermute | solution.py:761
  75.3 2.2 %collective-permute-start.26 = (bf16[144,896]{1,0:T(8,128)(2,1)S(1)}, bf16[144,896]{1,0:T(8,128)(2,1)S(1)}, u32[]{:S(2)}, u32[]{:S(2)}) collective-permute-start(bf16[144,896]{1,0:T(8,128)(2,1)S(1)} %stream.1.refs_0_.refs_1_), channel_id=1, source_target_pairs={{0,1},{1,0},{2,3},{3,2},{4,5},{5,4},{6,7},{7,6},{8,9},{9,8},{10,11... | collective-permute-start | bytes 774152 | tf_op jit(solution)/shard_map/ppermute | solution.py:761
  75.5 8.5 %collective-permute-start.25 = (bf16[144,896]{1,0:T(8,128)(2,1)S(1)}, bf16[144,896]{1,0:T(8,128)(2,1)S(1)}, u32[]{:S(2)}, u32[]{:S(2)}) collective-permute-start(bf16[144,896]{1,0:T(8,128)(2,1)S(1)} %stream.1.refs_0_.refs_1_), channel_id=1, source_target_pairs={{4,0},{8,4},{12,8},{14,12},{10,14},{6,10},{2,6},{0,2},{5,1},{9,5},... | collective-permute-start | bytes 774152 | tf_op jit(solution)/shard_map/ppermute | solution.py:758
  76.6 8.2 %collective-permute-start.24 = (bf16[144,896]{1,0:T(8,128)(2,1)S(1)}, bf16[144,896]{1,0:T(8,128)(2,1)S(1)}, u32[]{:S(2)}, u32[]{:S(2)}) collective-permute-start(bf16[144,896]{1,0:T(8,128)(2,1)S(1)} %stream.1.refs_0_.refs_1_), channel_id=1, source_target_pairs={{0,4},{4,8},{8,12},{12,14},{14,10},{10,6},{6,2},{2,0},{1,5},{5,9},... | collective-permute-start | bytes 774152 | tf_op jit(solution)/shard_map/ppermute | solution.py:755
  84.8 2.5 %collective-permute-start.29 = (bf16[144,896]{1,0:T(8,128)(2,1)S(1)}, bf16[144,896]{1,0:T(8,128)(2,1)S(1)}, u32[]{:S(2)}, u32[]{:S(2)}) collective-permute-start(bf16[144,896]{1,0:T(8,128)(2,1)S(1)} %collective-permute-done.24.refs_0_.refs_2_.refs_3_), channel_id=1, source_target_pairs={{0,1},{1,0},{2,3},{3,2},{4,5},{5,4},{6,7},{7,6},{8,9},{9,8},{10,11... | collective-permute-start | bytes 774152 | tf_op jit(solution)/shard_map/ppermute | solution.py:761
  84.8 2.5 %collective-permute-start.30 = (bf16[144,896]{1,0:T(8,128)(2,1)S(1)}, bf16[144,896]{1,0:T(8,128)(2,1)S(1)}, u32[]{:S(2)}, u32[]{:S(2)}) collective-permute-start(bf16[144,896]{1,0:T(8,128)(2,1)S(1)} %collective-permute-done.25.refs_2_.refs_4_.refs_5_), channel_id=1, source_target_pairs={{0,1},{1,0},{2,3},{3,2},{4,5},{5,4},{6,7},{7,6},{8,9},{9,8},{10,11... | collective-permute-start | bytes 774152 | tf_op jit(solution)/shard_map/ppermute | solution.py:761
  85.3 8.1 %collective-permute-start.27 = (bf16[144,896]{1,0:T(8,128)(2,1)S(1)}, bf16[144,896]{1,0:T(8,128)(2,1)S(1)}, u32[]{:S(2)}, u32[]{:S(2)}) collective-permute-start(bf16[144,896]{1,0:T(8,128)(2,1)S(1)} %collective-permute-done.24.refs_0_.refs_2_.refs_3_), channel_id=1, source_target_pairs={{0,4},{4,8},{8,12},{12,14},{14,10},{10,6},{6,2},{2,0},{1,5},{5,9},... | collective-permute-start | bytes 774152 | tf_op jit(solution)/shard_map/ppermute | solution.py:755
  86.3 7.8 %collective-permute-start.28 = (bf16[144,896]{1,0:T(8,128)(2,1)S(1)}, bf16[144,896]{1,0:T(8,128)(2,1)S(1)}, u32[]{:S(2)}, u32[]{:S(2)}) collective-permute-start(bf16[144,896]{1,0:T(8,128)(2,1)S(1)} %collective-permute-done.25.refs_2_.refs_4_.refs_5_), channel_id=1, source_target_pairs={{4,0},{8,4},{12,8},{14,12},{10,14},{6,10},{2,6},{0,2},{5,1},{9,5},... | collective-permute-start | bytes 774152 | tf_op jit(solution)/shard_map/ppermute | solution.py:758
  94.1 2.5 %collective-permute-start.33 = (bf16[144,896]{1,0:T(8,128)(2,1)S(1)}, bf16[144,896]{1,0:T(8,128)(2,1)S(1)}, u32[]{:S(2)}, u32[]{:S(2)}) collective-permute-start(bf16[144,896]{1,0:T(8,128)(2,1)S(1)} %collective-permute-done.27.refs_0_.refs_6_.refs_7_), channel_id=1, source_target_pairs={{0,1},{1,0},{2,3},{3,2},{4,5},{5,4},{6,7},{7,6},{8,9},{9,8},{10,11... | collective-permute-start | bytes 774152 | tf_op jit(solution)/shard_map/ppermute | solution.py:761
  94.1 2.5 %collective-permute-start.34 = (bf16[144,896]{1,0:T(8,128)(2,1)S(1)}, bf16[144,896]{1,0:T(8,128)(2,1)S(1)}, u32[]{:S(2)}, u32[]{:S(2)}) collective-permute-start(bf16[144,896]{1,0:T(8,128)(2,1)S(1)} %collective-permute-done.28.refs_2_.refs_8_.refs_9_), channel_id=1, source_target_pairs={{0,1},{1,0},{2,3},{3,2},{4,5},{5,4},{6,7},{7,6},{8,9},{9,8},{10,11... | collective-permute-start | bytes 774152 | tf_op jit(solution)/shard_map/ppermute | solution.py:761
  94.6 8.1 %collective-permute-start.31 = (bf16[144,896]{1,0:T(8,128)(2,1)S(1)}, bf16[144,896]{1,0:T(8,128)(2,1)S(1)}, u32[]{:S(2)}, u32[]{:S(2)}) collective-permute-start(bf16[144,896]{1,0:T(8,128)(2,1)S(1)} %collective-permute-done.27.refs_0_.refs_6_.refs_7_), channel_id=1, source_target_pairs={{0,4},{4,8},{8,12},{12,14},{14,10},{10,6},{6,2},{2,0},{1,5},{5,9},... | collective-permute-start | bytes 774152 | tf_op jit(solution)/shard_map/ppermute | solution.py:755
  95.5 7.8 %collective-permute-start.32 = (bf16[144,896]{1,0:T(8,128)(2,1)S(1)}, bf16[144,896]{1,0:T(8,128)(2,1)S(1)}, u32[]{:S(2)}, u32[]{:S(2)}) collective-permute-start(bf16[144,896]{1,0:T(8,128)(2,1)S(1)} %collective-permute-done.28.refs_2_.refs_8_.refs_9_), channel_id=1, source_target_pairs={{4,0},{8,4},{12,8},{14,12},{10,14},{6,10},{2,6},{0,2},{5,1},{9,5},... | collective-permute-start | bytes 774152 | tf_op jit(solution)/shard_map/ppermute | solution.py:758
  103.4 2.7 %collective-permute-start.37 = (bf16[144,896]{1,0:T(8,128)(2,1)S(1)}, bf16[144,896]{1,0:T(8,128)(2,1)S(1)}, u32[]{:S(2)}, u32[]{:S(2)}) collective-permute-start(bf16[144,896]{1,0:T(8,128)(2,1)S(1)} %collective-permute-done.31.refs_0_.refs_10_.refs_11_), channel_id=1, source_target_pairs={{0,1},{1,0},{2,3},{3,2},{4,5},{5,4},{6,7},{7,6},{8,9},{9,8},{10,11... | collective-permute-start | bytes 774152 | tf_op jit(solution)/shard_map/ppermute | solution.py:761
  103.4 2.7 %collective-permute-start.38 = (bf16[144,896]{1,0:T(8,128)(2,1)S(1)}, bf16[144,896]{1,0:T(8,128)(2,1)S(1)}, u32[]{:S(2)}, u32[]{:S(2)}) collective-permute-start(bf16[144,896]{1,0:T(8,128)(2,1)S(1)} %collective-permute-done.32.refs_2_.refs_12_.refs_13_), channel_id=1, source_target_pairs={{0,1},{1,0},{2,3},{3,2},{4,5},{5,4},{6,7},{7,6},{8,9},{9,8},{10,11... | collective-permute-start | bytes 774152 | tf_op jit(solution)/shard_map/ppermute | solution.py:761
  103.9 6.7 %collective-permute-start.35 = (bf16[80,896]{1,0:T(8,128)(2,1)S(1)}, bf16[80,896]{1,0:T(8,128)(2,1)S(1)}, u32[]{:S(2)}, u32[]{:S(2)}) collective-permute-start(bf16[80,896]{1,0:T(8,128)(2,1)S(1)} %slice.6), channel_id=1, source_target_pairs={{0,4},{4,8},{8,12},{12,14},{14,10},{10,6},{6,2},{2,0},{1,5},{5,9},... | collective-permute-start | bytes 430088 | tf_op jit(solution)/shard_map/ppermute | solution.py:755
  105.7 4.8 %collective-permute-start.36 = (bf16[64,896]{1,0:T(8,128)(2,1)S(1)}, bf16[64,896]{1,0:T(8,128)(2,1)S(1)}, u32[]{:S(2)}, u32[]{:S(2)}) collective-permute-start(bf16[64,896]{1,0:T(8,128)(2,1)S(1)} %slice.7), channel_id=1, source_target_pairs={{4,0},{8,4},{12,8},{14,12},{10,14},{6,10},{2,6},{0,2},{5,1},{9,5},... | collective-permute-start | bytes 344072 | tf_op jit(solution)/shard_map/ppermute | solution.py:758
  110.5 1.6 %collective-permute-start.39 = (bf16[80,896]{1,0:T(8,128)(2,1)S(1)}, bf16[80,896]{1,0:T(8,128)(2,1)S(1)}, u32[]{:S(2)}, u32[]{:S(2)}) collective-permute-start(bf16[80,896]{1,0:T(8,128)(2,1)S(1)} %collective-permute-done.35.refs_0_), channel_id=1, source_target_pairs={{0,1},{1,0},{2,3},{3,2},{4,5},{5,4},{6,7},{7,6},{8,9},{9,8},{10,11... | collective-permute-start | bytes 430088 | tf_op jit(solution)/shard_map/ppermute | solution.py:761
  110.6 1.5 collective-permute-start.40
  116.1 2.7 %collective-permute-start.50 = (bf16[144,3584]{1,0:T(8,128)(2,1)S(1)}, bf16[144,3584]{1,0:T(8,128)(2,1)S(1)}, u32[]{:S(2)}, u32[]{:S(2)}) collective-permute-start(bf16[144,3584]{1,0:T(8,128)(2,1)S(1)} %get-tuple-element.177), channel_id=1, source_target_pairs={{0,1},{1,0},{2,3},{3,2},{4,5},{5,4},{6,7},{7,6},{8,9},{9,8},{10,11... | collective-permute-start | bytes 3096584 | tf_op jit(solution)/shard_map/ppermute | solution.py:761
  118.6 3.0 %collective-permute-start.41 = (bf16[144,3584]{1,0:T(8,128)(2,1)S(1)}, bf16[144,3584]{1,0:T(8,128)(2,1)S(1)}, u32[]{:S(2)}, u32[]{:S(2)}) collective-permute-start(bf16[144,3584]{1,0:T(8,128)(2,1)S(1)} %get-tuple-element.166), channel_id=1, source_target_pairs={{0,1},{1,0},{2,3},{3,2},{4,5},{5,4},{6,7},{7,6},{8,9},{9,8},{10,11... | collective-permute-start | bytes 3096584 | tf_op jit(solution)/shard_map/ppermute | solution.py:761
  119.5 5.5 %collective-permute-start.51 = (bf16[16,3584]{1,0:T(8,128)(2,1)S(1)}, bf16[16,3584]{1,0:T(8,128)(2,1)S(1)}, u32[]{:S(2)}, u32[]{:S(2)}) collective-permute-start(bf16[16,3584]{1,0:T(8,128)(2,1)S(1)} %get-tuple-element.178), channel_id=1, source_target_pairs={{0,4},{4,8},{8,12},{12,14},{14,10},{10,6},{6,2},{2,0},{1,5},{5,9},... | collective-permute-start | bytes 344072 | tf_op jit(solution)/shard_map/ppermute | solution.py:755
  121.0 5.1 %collective-permute-start.52 = (bf16[16,3584]{1,0:T(8,128)(2,1)S(1)}, bf16[16,3584]{1,0:T(8,128)(2,1)S(1)}, u32[]{:S(2)}, u32[]{:S(2)}) collective-permute-start(bf16[16,3584]{1,0:T(8,128)(2,1)S(1)} %get-tuple-element.179), channel_id=1, source_target_pairs={{4,0},{8,4},{12,8},{14,12},{10,14},{6,10},{2,6},{0,2},{5,1},{9,5},... | collective-permute-start | bytes 344072 | tf_op jit(solution)/shard_map/ppermute | solution.py:758
  122.1 6.8 %collective-permute-start.42 = (bf16[16,3584]{1,0:T(8,128)(2,1)S(1)}, bf16[16,3584]{1,0:T(8,128)(2,1)S(1)}, u32[]{:S(2)}, u32[]{:S(2)}) collective-permute-start(bf16[16,3584]{1,0:T(8,128)(2,1)S(1)} %get-tuple-element.167), channel_id=1, source_target_pairs={{0,4},{4,8},{8,12},{12,14},{14,10},{10,6},{6,2},{2,0},{1,5},{5,9},... | collective-permute-start | bytes 344072 | tf_op jit(solution)/shard_map/ppermute | solution.py:755
  123.7 5.2 %collective-permute-start.43 = (bf16[16,3584]{1,0:T(8,128)(2,1)S(1)}, bf16[16,3584]{1,0:T(8,128)(2,1)S(1)}, u32[]{:S(2)}, u32[]{:S(2)}) collective-permute-start(bf16[16,3584]{1,0:T(8,128)(2,1)S(1)} %get-tuple-element.168), channel_id=1, source_target_pairs={{4,0},{8,4},{12,8},{14,12},{10,14},{6,10},{2,6},{0,2},{5,1},{9,5},... | collective-permute-start | bytes 344072 | tf_op jit(solution)/shard_map/ppermute | solution.py:758
  126.8 5.8 %collective-permute-start.53 = (bf16[16,3584]{1,0:T(8,128)(2,1)S(1)}, bf16[16,3584]{1,0:T(8,128)(2,1)S(1)}, u32[]{:S(2)}, u32[]{:S(2)}) collective-permute-start(bf16[16,3584]{1,0:T(8,128)(2,1)S(1)} %get-tuple-element.180), channel_id=1, source_target_pairs={{0,4},{4,8},{8,12},{12,14},{14,10},{10,6},{6,2},{2,0},{1,5},{5,9},... | collective-permute-start | bytes 344072 | tf_op jit(solution)/shard_map/ppermute | solution.py:755
  128.3 6.0 %collective-permute-start.54 = (bf16[16,3584]{1,0:T(8,128)(2,1)S(1)}, bf16[16,3584]{1,0:T(8,128)(2,1)S(1)}, u32[]{:S(2)}, u32[]{:S(2)}) collective-permute-start(bf16[16,3584]{1,0:T(8,128)(2,1)S(1)} %get-tuple-element.181), channel_id=1, source_target_pairs={{4,0},{8,4},{12,8},{14,12},{10,14},{6,10},{2,6},{0,2},{5,1},{9,5},... | collective-permute-start | bytes 344072 | tf_op jit(solution)/shard_map/ppermute | solution.py:758
  129.6 7.5 %collective-permute-start.44 = (bf16[16,3584]{1,0:T(8,128)(2,1)S(1)}, bf16[16,3584]{1,0:T(8,128)(2,1)S(1)}, u32[]{:S(2)}, u32[]{:S(2)}) collective-permute-start(bf16[16,3584]{1,0:T(8,128)(2,1)S(1)} %get-tuple-element.169), channel_id=1, source_target_pairs={{0,4},{4,8},{8,12},{12,14},{14,10},{10,6},{6,2},{2,0},{1,5},{5,9},... | collective-permute-start | bytes 344072 | tf_op jit(solution)/shard_map/ppermute | solution.py:755
  131.1 6.0 %collective-permute-start.45 = (bf16[16,3584]{1,0:T(8,128)(2,1)S(1)}, bf16[16,3584]{1,0:T(8,128)(2,1)S(1)}, u32[]{:S(2)}, u32[]{:S(2)}) collective-permute-start(bf16[16,3584]{1,0:T(8,128)(2,1)S(1)} %get-tuple-element.170), channel_id=1, source_target_pairs={{4,0},{8,4},{12,8},{14,12},{10,14},{6,10},{2,6},{0,2},{5,1},{9,5},... | collective-permute-start | bytes 344072 | tf_op jit(solution)/shard_map/ppermute | solution.py:758
  135.0 5.3 %collective-permute-start.55 = (bf16[16,3584]{1,0:T(8,128)(2,1)S(1)}, bf16[16,3584]{1,0:T(8,128)(2,1)S(1)}, u32[]{:S(2)}, u32[]{:S(2)}) collective-permute-start(bf16[16,3584]{1,0:T(8,128)(2,1)S(1)} %get-tuple-element.182), channel_id=1, source_target_pairs={{0,4},{4,8},{8,12},{12,14},{14,10},{10,6},{6,2},{2,0},{1,5},{5,9},... | collective-permute-start | bytes 344072 | tf_op jit(solution)/shard_map/ppermute | solution.py:755
  135.8 4.9 %collective-permute-start.56 = (bf16[16,3584]{1,0:T(8,128)(2,1)S(1)}, bf16[16,3584]{1,0:T(8,128)(2,1)S(1)}, u32[]{:S(2)}, u32[]{:S(2)}) collective-permute-start(bf16[16,3584]{1,0:T(8,128)(2,1)S(1)} %get-tuple-element.183), channel_id=1, source_target_pairs={{4,0},{8,4},{12,8},{14,12},{10,14},{6,10},{2,6},{0,2},{5,1},{9,5},... | collective-permute-start | bytes 344072 | tf_op jit(solution)/shard_map/ppermute | solution.py:758
  137.8 5.8 %collective-permute-start.46 = (bf16[16,3584]{1,0:T(8,128)(2,1)S(1)}, bf16[16,3584]{1,0:T(8,128)(2,1)S(1)}, u32[]{:S(2)}, u32[]{:S(2)}) collective-permute-start(bf16[16,3584]{1,0:T(8,128)(2,1)S(1)} %get-tuple-element.171), channel_id=1, source_target_pairs={{0,4},{4,8},{8,12},{12,14},{14,10},{10,6},{6,2},{2,0},{1,5},{5,9},... | collective-permute-start | bytes 344072 | tf_op jit(solution)/shard_map/ppermute | solution.py:755
  138.6 4.9 %collective-permute-start.47 = (bf16[16,3584]{1,0:T(8,128)(2,1)S(1)}, bf16[16,3584]{1,0:T(8,128)(2,1)S(1)}, u32[]{:S(2)}, u32[]{:S(2)}) collective-permute-start(bf16[16,3584]{1,0:T(8,128)(2,1)S(1)} %get-tuple-element.172), channel_id=1, source_target_pairs={{4,0},{8,4},{12,8},{14,12},{10,14},{6,10},{2,6},{0,2},{5,1},{9,5},... | collective-permute-start | bytes 344072 | tf_op jit(solution)/shard_map/ppermute | solution.py:758
  141.4 5.5 %collective-permute-start.57 = (bf16[16,3584]{1,0:T(8,128)(2,1)S(1)}, bf16[16,3584]{1,0:T(8,128)(2,1)S(1)}, u32[]{:S(2)}, u32[]{:S(2)}) collective-permute-start(bf16[16,3584]{1,0:T(8,128)(2,1)S(1)} %get-tuple-element.184), channel_id=1, source_target_pairs={{0,4},{4,8},{8,12},{12,14},{14,10},{10,6},{6,2},{2,0},{1,5},{5,9},... | collective-permute-start | bytes 344072 | tf_op jit(solution)/shard_map/ppermute | solution.py:755
  142.3 4.8 %collective-permute-start.58 = (bf16[16,3584]{1,0:T(8,128)(2,1)S(1)}, bf16[16,3584]{1,0:T(8,128)(2,1)S(1)}, u32[]{:S(2)}, u32[]{:S(2)}) collective-permute-start(bf16[16,3584]{1,0:T(8,128)(2,1)S(1)} %get-tuple-element.185), channel_id=1, source_target_pairs={{4,0},{8,4},{12,8},{14,12},{10,14},{6,10},{2,6},{0,2},{5,1},{9,5},... | collective-permute-start | bytes 344072 | tf_op jit(solution)/shard_map/ppermute | solution.py:758
  144.2 4.8 %collective-permute-start.48 = (bf16[16,3584]{1,0:T(8,128)(2,1)S(1)}, bf16[16,3584]{1,0:T(8,128)(2,1)S(1)}, u32[]{:S(2)}, u32[]{:S(2)}) collective-permute-start(bf16[16,3584]{1,0:T(8,128)(2,1)S(1)} %get-tuple-element.173), channel_id=1, source_target_pairs={{0,4},{4,8},{8,12},{12,14},{14,10},{10,6},{6,2},{2,0},{1,5},{5,9},... | collective-permute-start | bytes 344072 | tf_op jit(solution)/shard_map/ppermute | solution.py:755
  145.1 4.8 %collective-permute-start.49 = (bf16[16,3584]{1,0:T(8,128)(2,1)S(1)}, bf16[16,3584]{1,0:T(8,128)(2,1)S(1)}, u32[]{:S(2)}, u32[]{:S(2)}) collective-permute-start(bf16[16,3584]{1,0:T(8,128)(2,1)S(1)} %get-tuple-element.174), channel_id=1, source_target_pairs={{4,0},{8,4},{12,8},{14,12},{10,14},{6,10},{2,6},{0,2},{5,1},{9,5},... | collective-permute-start | bytes 344072 | tf_op jit(solution)/shard_map/ppermute | solution.py:758
  147.8 2.8 %collective-permute-start.60 = (bf16[16,3584]{1,0:T(8,128)(2,1)S(1)}, bf16[16,3584]{1,0:T(8,128)(2,1)S(1)}, u32[]{:S(2)}, u32[]{:S(2)}) collective-permute-start(bf16[16,3584]{1,0:T(8,128)(2,1)S(1)} %get-tuple-element.188), channel_id=1, source_target_pairs={{0,1},{1,0},{2,3},{3,2},{4,5},{5,4},{6,7},{7,6},{8,9},{9,8},{10,11... | collective-permute-start | bytes 344072 | tf_op jit(solution)/shard_map/ppermute | solution.py:761
  150.6 1.4 collective-permute-start.59
  (15 other events, 147.3 us)

commit v5 on v4

--- a/solution.py
+++ b/solution.py
@@ -23,6 +23,10 @@
 
 def mm_nt(a, b):
     return lax.dot_general(a, b, (((1,), (1,)), ((), ())), preferred_element_type=f32)
+
+
+def in_hbm(x):
+    return pltpu.with_memory_space_constraint(x, pltpu.HBM)
 
 
 def smem():
@@ -69,11 +73,16 @@
         self.behind = self.ahead + self.reach + 1
         self.owner_back = self.behind + self.reach + 1
         self.owner_fore = self.owner_back + self.reach + 1
-        self.size = self.owner_fore + self.reach + 1
-
-
-def table_kernel(table, ranks, ids, span, dec, start, lengths, at, who, out):
-    reach = table.reach
+        self.who = self.owner_fore + self.reach + 1
+        self.at = self.who + ranks
+        self.size = self.at + ranks
+
+
+def table_kernel(table, order, ids, span, dec, start, lengths, out):
+    reach, ranks = table.reach, len(order)
+    for i, r in enumerate(order):
+        out[table.who + i] = r
+        out[table.at + r] = i
     rank, core = ids[0], ids[1]
     most, busy_rank = span[0] + dec[0], jnp.int32(0)
     for i in range(1, ranks):
@@ -86,18 +95,18 @@
         x = jnp.where(x < 0, x + ranks, x)
         return jnp.where(x >= ranks, x - ranks, x)
 
-    place, busy_place = at[rank], at[busy_rank]
+    place, busy_place = out[table.at + rank], out[table.at + busy_rank]
     to_busy = wrap(busy_place - place)
     from_busy = wrap(place - busy_place)
 
     def node_ahead(k):
         far = (to_busy > 0) & (k > to_busy + 1)
-        slot = who[wrap(place + k - jnp.where(far, 1, 0))]
+        slot = out[table.who + wrap(place + k - jnp.where(far, 1, 0))]
         return jnp.where((to_busy > 0) & (k == to_busy + 1), ranks, slot)
 
     def node_behind(k):
         far = (from_busy > 0) & (k > from_busy)
-        slot = who[wrap(place - k + jnp.where(far, 1, 0))]
+        slot = out[table.who + wrap(place - k + jnp.where(far, 1, 0))]
         return jnp.where((from_busy > 0) & (k == from_busy), ranks, slot)
 
     out[RANK] = rank
@@ -114,167 +123,192 @@
     for k in range(1, reach + 1):
         out[table.ahead + k] = node_ahead(k)
         out[table.behind + k] = node_behind(k)
-        out[table.owner_back + k] = who[wrap(place - k)]
-        out[table.owner_fore + k] = who[wrap(place + k)]
+        out[table.owner_back + k] = out[table.who + wrap(place - k)]
+        out[table.owner_fore + k] = out[table.who + wrap(place + k)]
         out[table.source + node_behind(k)] = k
         last = jnp.where(busy, ranks, node_ahead(k)) if k == reach else node_ahead(k)
         out[table.source + last] = reach + k
 
 
 def attend_kernel(
-    heads, group, rows, lat, cached, value, start_step,
-    tab, q, cache, fresh, vw, main, extra, k0, k1, kpad, dq, dec, turn,
+    heads, group, rows, lat, value, parts, tab, q_hbm, cache_hbm, fresh, vw_hbm, *refs
 ):
-    pair = 2 * lat
-    wide = -(-lat // 128) * 128
-    shift = wide - lat
-    keys = cached + rows
-    cols = -(-keys // 128) * 128
-    slots = cache.shape[0] - 1
-    dr = 8
+    outs, refs = refs[: 2 * parts], refs[2 * parts :]
+    q, keys, vw, dq, latent, fz, q_sem, key_sem, vw_sem = refs
+    slots = keys.shape[0] - 2
+    cached = keys.shape[2]
+    wide = keys.shape[1]
+    shift, pair, dr = wide - lat, 2 * lat, 8
+    groups, pairs = heads // group, group // 2
     span, decs = tab[SPAN], tab[DEC]
+
+    def q_copy(g):
+        at = pl.ds(g * group * lat, group * lat)
+        return pltpu.make_async_copy(q_hbm.at[:, at], q.at[:, at], q_sem.at[g])
+
+    def vw_copy(g):
+        at = pl.ds(g * group, group)
+        return pltpu.make_async_copy(vw_hbm.at[at], vw.at[at], vw_sem.at[g])
+
+    even_copy = pltpu.make_async_copy(cache_hbm.at[0], keys.at[0, pl.ds(0, lat)], key_sem.at[0])
+    odd_copy = pltpu.make_async_copy(
+        cache_hbm.at[0], keys.at[slots + 1, pl.ds(shift, lat)], key_sem.at[1]
+    )
+    rest_copy = pltpu.make_async_copy(
+        cache_hbm.at[pl.ds(1, slots)], keys.at[pl.ds(1, slots), pl.ds(0, lat)], key_sem.at[2]
+    )
+    even_copy.start()
+    odd_copy.start()
+    for g in range(groups):
+        q_copy(g).start()
+    rest_copy.start()
+    for g in range(groups):
+        vw_copy(g).start()
 
     def onehot(shape, row_dim, slot_dim):
         r = lax.broadcasted_iota(i32, shape, row_dim)
         j = lax.broadcasted_iota(i32, shape, slot_dim)
         return jnp.where((r == span + j) & (j < decs), 1.0, 0.0).astype(bf16)
 
-    @pl.when(pl.program_id(0) == 0)
-    def _():
-        turn[...] = jnp.zeros_like(turn)
-        turn[:rows, :lat] = fresh[...].astype(f32)
-        turned = turn[...].T.astype(bf16)[:lat]
-        k0[...] = jnp.zeros_like(k0)
-        k1[...] = jnp.zeros_like(k1)
-        for ref, off in ((k0, 0), (k1, shift)):
-            ref[off : off + lat, :cached] = cache[0]
-            ref[off : off + lat, cached:] = turned
-        kpad[...] = jnp.zeros_like(kpad)
-        for s in range(slots):
-            kpad[s, :lat] = cache[s + 1]
-        pick = onehot((16, rows), 1, 0)
-        for p in range(heads // 2):
-            got = mm(pick, q[:, pair * p : pair * (p + 1)])[:dr]
-            dq[2 * p * dr : (2 * p + 1) * dr] = got[:, :wide]
-            dq[(2 * p + 1) * dr : (2 * p + 2) * dr] = pltpu.roll(got[:, pair - wide :], wide - shift, 1)
-        n = heads * dr
-        queries = dq[...].astype(bf16)
-        slot = lax.broadcasted_iota(i32, (n, 1), 0) % dr
-        length = jnp.zeros((n, 1), i32)
-        scores = jnp.zeros((n, cached), f32)
-        for s in range(slots):
-            scores = jnp.where(slot == s, mm(queries, kpad[s]), scores)
-            length = jnp.where(slot == s, tab[LENGTHS + s], length)
-        seen = lax.broadcasted_iota(i32, (n, cached), 1) < length
-        scores = jnp.where(seen, scores * score_scale, masked_score)
-        own = mm(queries, k0[:, cached:])
-        column = lax.broadcasted_iota(i32, own.shape, 1)
-        own = jnp.sum(jnp.where(column == span + slot, own, 0.0), axis=1, keepdims=True)
-        own = own * score_scale
-        peak = jnp.maximum(jnp.max(scores, axis=1, keepdims=True), own)
-        e = jnp.where(seen, jnp.exp(scores - peak), 0.0)
-        e_own = jnp.exp(own - peak)
-        total = jnp.sum(e, axis=1, keepdims=True) + e_own
-        w = e / total
-        acc = jnp.zeros((n, value), f32)
-        for s in range(slots):
-            acc = acc + mm_nt(jnp.where(slot == s, w, 0.0).astype(bf16), cache[s + 1, :value])
-        own_value = mm(pick, fresh[:, :value])[:dr]
-        own_value = jnp.broadcast_to(own_value[None], (heads, dr, value)).reshape(n, value)
-        dec[...] = acc + (e_own / total).astype(bf16).astype(f32) * own_value
-
-    step = pl.program_id(0)
-    start = step * (group * lat)
-    pairs = group // 2
-
-    def stacked(off):
-        return jnp.concatenate(
-            [q[:, pl.ds(pl.multiple_of(start + pair * p + off, 128), wide)] for p in range(pairs)], 0
-        )
+    tail = jnp.zeros((shift, cached), bf16)
+    for s in range(slots + 1):
+        keys[s, lat:] = tail
+    keys[slots + 1, :shift] = tail
+    fz[...] = jnp.zeros_like(fz)
+    fz[:rows, :lat] = fresh[...].astype(f32)
+    fresh_even = fz[...].astype(bf16)
+    fresh_odd = pltpu.roll(fz[...], shift, 1).astype(bf16)
 
     m = pairs * rows
+    cols = cached + fz.shape[0]
     row = lax.broadcasted_iota(i32, (m, 1), 0) % rows
     col = lax.broadcasted_iota(i32, (m, cols), 1)
-    seen = (col < jnp.where(col < cached, tab[START], cached + 1 + row)) & (col < keys)
-    values = k0[:value]
-
-    def latent(lhs, ref):
-        s = jnp.where(seen, mm(lhs, ref[...]) * score_scale, masked_score)
+    seen = col < jnp.where(col < cached, tab[START], cached + 1 + row)
+
+    def span_latent(lhs, slot, fresh_keys):
+        s = jnp.concatenate([mm(lhs, keys[slot]), mm_nt(lhs, fresh_keys)], 1)
+        s = jnp.where(seen, s * score_scale, masked_score)
         e = jnp.where(seen, jnp.exp(s - jnp.max(s, axis=1, keepdims=True)), 0.0)
         w = (e * (1.0 / jnp.sum(e, axis=1, keepdims=True))).astype(bf16)
-        o = mm_nt(w, values)
+        o = mm_nt(w[:, :cached], keys[0, :value]) + mm(w[:, cached:], fresh_even[:, :value])
         return jnp.where(row < span, o, 0.0).astype(bf16)
 
-    even, odd = latent(stacked(0), k0), latent(stacked(pair - wide), k1)
-    outs, decoded = [], []
-    for p in range(pairs):
-        at = pl.multiple_of((step * group + 2 * p) * dr, 16)
-        lhs = jnp.concatenate(
-            [even[p * rows : (p + 1) * rows], odd[p * rows : (p + 1) * rows], dec[pl.ds(at, 16)].astype(bf16)], 0
-        )
-        vh = vw.shape[2]
-        r = mm(lhs, jnp.concatenate([vw[2 * p], vw[2 * p + 1]], 1))
-        outs += [r[:rows, :vh], r[rows : 2 * rows, vh:]]
-        decoded += [r[2 * rows : 2 * rows + dr, :vh], r[2 * rows + dr :, vh:]]
-    decoded = jnp.concatenate(decoded, 1)
-    decoded = jnp.concatenate([decoded, jnp.zeros_like(decoded)], 0).astype(bf16)
-    out = jnp.concatenate(outs, 1) + mm(onehot((rows, 16), 0, 1), decoded)
-    out = out.astype(bf16)
-    at = pl.ds(pl.multiple_of(step * out.shape[1], out.shape[1]), out.shape[1])
-    main[:, at] = out[: rows // 2]
-    extra[:, at] = out[rows // 2 :]
-
-
-def attend(tab, queries, cache, fresh, vw, part, parts):
-    rows, heads = queries.shape[0], vw.shape[0] // parts
-    lat = queries.shape[1] // vw.shape[0]
+    even_copy.wait()
+    odd_copy.wait()
+    for g in range(groups):
+        q_copy(g).wait()
+        start = g * group * lat
+        for odd in range(2):
+            off = start + odd * (pair - wide)
+            lhs = jnp.concatenate(
+                [q[:, off + pair * p : off + pair * p + wide] for p in range(pairs)], 0
+            )
+            o = span_latent(lhs, (slots + 1) * odd, fresh_odd if odd else fresh_even)
+            latent[g, odd] = o
+
+    pick = onehot((16, rows), 1, 0)
+    for p in range(heads // 2):
+        got = mm(pick, q[:, pair * p : pair * (p + 1)])[:dr]
+        dq[2 * p * dr : (2 * p + 1) * dr] = got[:, :wide]
+        dq[(2 * p + 1) * dr : (2 * p + 2) * dr] = pltpu.roll(got[:, pair - wide :], wide - shift, 1)
+    n = heads * dr
+    queries = dq[...].astype(bf16)
+    slot = lax.broadcasted_iota(i32, (n, 1), 0) % dr
+    rest_copy.wait()
+    length = jnp.zeros((n, 1), i32)
+    scores = jnp.zeros((n, cached), f32)
+    for s in range(slots):
+        scores = jnp.where(slot == s, mm(queries, keys[s + 1]), scores)
+        length = jnp.where(slot == s, tab[LENGTHS + s], length)
+    unmasked = lax.broadcasted_iota(i32, (n, cached), 1) < length
+    scores = jnp.where(unmasked, scores * score_scale, masked_score)
+    own = mm_nt(queries, fresh_even)
+    column = lax.broadcasted_iota(i32, own.shape, 1)
+    own = jnp.sum(jnp.where(column == span + slot, own, 0.0), axis=1, keepdims=True)
+    own = own * score_scale
+    peak = jnp.maximum(jnp.max(scores, axis=1, keepdims=True), own)
+    e = jnp.where(unmasked, jnp.exp(scores - peak), 0.0)
+    e_own = jnp.exp(own - peak)
+    total = jnp.sum(e, axis=1, keepdims=True) + e_own
+    w = e / total
+    acc = jnp.zeros((n, value), f32)
+    for s in range(slots):
+        acc = acc + mm_nt(jnp.where(slot == s, w, 0.0).astype(bf16), keys[s + 1, :value])
+    own_value = mm(pick, fresh[:, :value])[:dr]
+    own_value = jnp.broadcast_to(own_value[None], (heads, dr, value)).reshape(n, value)
+    dec = (acc + (e_own / total).astype(bf16).astype(f32) * own_value).astype(bf16)
+
+    place = onehot((rows, 16), 0, 1)
+    vh = vw.shape[2]
+    block = rows // 2
+    per_part = groups // parts
+    for g in range(groups):
+        vw_copy(g).wait()
+        values, decoded = [], []
+        for p in range(pairs):
+            h = g * group + 2 * p
+            lhs = jnp.concatenate(
+                [
+                    latent[g, 0, p * rows : (p + 1) * rows],
+                    latent[g, 1, p * rows : (p + 1) * rows],
+                    dec[h * dr : (h + 2) * dr],
+                ],
+                0,
+            )
+            r = mm(lhs, jnp.concatenate([vw[h], vw[h + 1]], 1))
+            values += [r[:rows, :vh], r[rows : 2 * rows, vh:]]
+            decoded += [r[2 * rows : 2 * rows + dr, :vh], r[2 * rows + dr :, vh:]]
+        decoded = jnp.concatenate(decoded, 1)
+        decoded = jnp.concatenate([decoded, jnp.zeros_like(decoded)], 0).astype(bf16)
+        out = (jnp.concatenate(values, 1) + mm(place, decoded)).astype(bf16)
+        part, at = g // per_part, (g % per_part) * group * vh
+        outs[2 * part][:, at : at + group * vh] = out[:block]
+        outs[2 * part + 1][:, at : at + group * vh] = out[block:]
+
+
+def attend(tab, queries, cache, fresh, vw, parts):
+    rows, heads = queries.shape[0], vw.shape[0]
+    lat = queries.shape[1] // heads
     slots, _, cached = cache.shape
     value, vh = vw.shape[1:]
-    group = min(8, heads)
-    wide, cols = -(-lat // 128) * 128, -(-(cached + rows) // 128) * 128
-    steps = heads // group
-    half = jax.ShapeDtypeStruct((rows // 2, heads * vh), bf16)
-    return pl.pallas_call(
-        functools.partial(attend_kernel, heads, group, rows, lat, cached, value, part),
-        grid=(steps,),
-        in_specs=[
-            smem(),
-            pl.BlockSpec((rows, heads * lat), lambda i: (0, part)),
-            pl.BlockSpec(cache.shape, lambda i: (0, 0, 0)),
-            pl.BlockSpec(fresh.shape[::-1], lambda i: (0, 0)),
-            pl.BlockSpec((group, value, vh), lambda i: (part * steps + i, 0, 0)),
+    group = min(8, heads // parts)
+    groups = heads // group
+    wide = -(-lat // 128) * 128
+    half = jax.ShapeDtypeStruct((rows // 2, heads // parts * vh), bf16)
+    hbm = pl.BlockSpec(memory_space=pltpu.HBM)
+    return pl.pallas_call(
+        functools.partial(attend_kernel, heads, group, rows, lat, value, parts),
+        in_specs=[smem(), hbm, hbm, whole(), hbm],
+        out_specs=[whole()] * (2 * parts),
+        out_shape=[half] * (2 * parts),
+        scratch_shapes=[
+            pltpu.VMEM(queries.shape, bf16),
+            pltpu.VMEM((slots + 1, wide, cached), bf16),
+            pltpu.VMEM(vw.shape, bf16),
+            pltpu.VMEM((heads * 8, wide), f32),
+            pltpu.VMEM((groups, 2, group // 2 * rows, value), bf16),
+            pltpu.VMEM((-(-rows // 128) * 128, wide), f32),
+            pltpu.SemaphoreType.DMA((groups,)),
+            pltpu.SemaphoreType.DMA((3,)),
+            pltpu.SemaphoreType.DMA((groups,)),
         ],
-        out_specs=[whole()] * 2,
-        out_shape=[half, half],
-        scratch_shapes=[
-            pltpu.VMEM((wide, cols), bf16),
-            pltpu.VMEM((wide, cols), bf16),
-            pltpu.VMEM((slots - 1, wide, cached), bf16),
-            pltpu.VMEM((heads * 8, wide), f32),
-            pltpu.VMEM((heads * 8, value), f32),
-            pltpu.VMEM((cols - cached, wide), f32),
-        ],
-        compiler_params=params(56),
+        compiler_params=params(28),
         cost_estimate=cost(
             2 * rows * heads * (cached + rows) * (lat + value),
-            2 * (queries.size // parts + cache.size + vw.size // parts),
+            2 * (queries.size + cache.size + vw.size),
             rows * heads * (cached + rows),
         ),
         name="attend",
-    )(tab, queries, cache, fresh.T, vw)
-
-
-def pack_kernel(ranks, features, half, tab, res, *outs):
-    core, rank = tab[CORE], tab[RANK]
-    low = pl.multiple_of(core * half, half)
-    high = pl.multiple_of(res.shape[0] // 2 + core * half, half)
-    for k in range(ranks):
-        target = rank + k
+    )(tab, in_hbm(queries), in_hbm(cache), fresh.T, in_hbm(vw))
+
+
+def pack_kernel(ranks, cores, features, tab, res, *outs):
+    for k in range(ranks // cores):
+        target = tab[RANK] + k + (ranks // cores) * tab[CORE]
         target = jnp.where(target >= ranks, target - ranks, target)
 
         def put(columns, k=k):
-            outs[k][:half] = res[pl.ds(low, half), columns]
-            outs[k][half:] = res[pl.ds(high, half), columns]
+            outs[k][...] = res[:, columns]
 
         if features % 128 == 0:
             put(pl.ds(pl.multiple_of(target * features, 128), features))
@@ -285,16 +319,50 @@
 
 def pack(tab, residual, ranks, cores):
     rows, width = residual.shape
-    half, features = rows // 2 // cores, width // ranks
-    return pl.pallas_call(
-        functools.partial(pack_kernel, ranks, features, half),
+    features = width // ranks
+    count = ranks // cores
+    return pl.pallas_call(
+        functools.partial(pack_kernel, ranks, cores, features),
         in_specs=[smem(), whole()],
-        out_specs=[whole()] * ranks,
-        out_shape=[jax.ShapeDtypeStruct((2 * half, features), bf16)] * ranks,
+        out_specs=[whole()] * count,
+        out_shape=[jax.ShapeDtypeStruct((rows, features), bf16)] * count,
         compiler_params=params(8),
         cost_estimate=cost(0, 4 * residual.size),
         name="pack",
     )(tab, residual)
+
+
+def share_kernel(half, tab, own, *refs):
+    pieces, out = refs[:-1], refs[-1]
+    other = 1 - tab[CORE]
+    block = own.shape[0] // 2
+    low = pl.multiple_of(other * half, half)
+    high = pl.multiple_of(block + other * half, half)
+
+    def put(k, piece):
+        out[2 * k * half : (2 * k + 1) * half] = piece[pl.ds(low, half)]
+        out[(2 * k + 1) * half : (2 * k + 2) * half] = piece[pl.ds(high, half)]
+
+    for k, piece in enumerate(pieces):
+        if k > 0:
+            put(k, piece)
+        else:
+            pl.when(tab[CORE] == 0)(functools.partial(put, k, own))
+            pl.when(tab[CORE] != 0)(functools.partial(put, k, piece))
+
+
+def share(tab, own, pieces, cores):
+    rows, features = own.shape
+    half = rows // 2 // cores
+    return pl.pallas_call(
+        functools.partial(share_kernel, half),
+        in_specs=[smem()] + [whole()] * (1 + len(pieces)),
+        out_specs=whole(),
+        out_shape=jax.ShapeDtypeStruct((2 * half * len(pieces), features), bf16),
+        compiler_params=params(8),
+        cost_estimate=cost(0, 4 * own.size * len(pieces)),
+        name="share",
+    )(tab, own, *pieces)
 
 
 def route_kernel(tab, *refs):
@@ -378,7 +446,7 @@
     nodes = len(blocks) - 1
     half = block // cores
     features = weight.shape[1]
-    depth = 1024 if width % 1024 == 0 else width
+    depth = width
     steps = width // depth
     total = jax.ShapeDtypeStruct((nodes * block, features), f32)
     final = part == parts - 1
@@ -415,36 +483,59 @@
     )(*args)
 
 
-def stream_kernel(ranks, half, tab, kept, other, *refs):
-    res, out = refs[:-1], refs[-1]
-    rank, busy_rank = tab[RANK], tab[BUSY_RANK]
+def stream_kernel(ranks, half, tab, kept, other, own, shared, *refs):
+    pieces, out = refs[:-1], refs[-1]
+    rank, core, busy_rank = tab[RANK], tab[CORE], tab[BUSY_RANK]
+    count = len(pieces)
+    block = own.shape[0] // 2
 
     def put(slot, extra):
         rows = pl.ds(pl.multiple_of(slot * half, half), half)
         total = kept[rows] + other[rows].astype(f32) + extra.astype(f32)
         out[rows] = total.astype(bf16)
 
-    for k in range(ranks):
-        owner = rank - k
-        owner = jnp.where(owner < 0, owner + ranks, owner)
-        put(owner, res[k][:half])
+    def put_both(owner, main, extra):
+        put(owner, main())
 
         @pl.when(owner == busy_rank)
-        def _(k=k):
-            put(ranks, res[k][half:])
-
-
-def stream_of(tab, kept, other, res):
-    half = res[0].shape[0] // 2
-    return pl.pallas_call(
-        functools.partial(stream_kernel, len(res), half),
-        in_specs=[smem()] + [whole()] * (2 + len(res)),
+        def _():
+            put(ranks, extra())
+
+    def owner_of(k, c):
+        owner = rank - k - count * c
+        return jnp.where(owner < 0, owner + ranks, owner)
+
+    low = pl.ds(pl.multiple_of(core * half, half), half)
+    high = pl.ds(pl.multiple_of(block + core * half, half), half)
+    for k, piece in enumerate(pieces):
+
+        def received(piece=piece, k=k):
+            put_both(owner_of(k, core), lambda: piece[low], lambda: piece[high])
+
+        if k > 0:
+            received()
+        else:
+            pl.when(core == 0)(functools.partial(received, own))
+            pl.when(core != 0)(received)
+        at = 2 * k * half
+        put_both(
+            owner_of(k, 1 - core),
+            lambda at=at: shared[at : at + half],
+            lambda at=at: shared[at + half : at + 2 * half],
+        )
+
+
+def stream_of(tab, kept, other, own, shared, pieces, cores):
+    half = own.shape[0] // 2 // cores
+    return pl.pallas_call(
+        functools.partial(stream_kernel, cores * len(pieces), half),
+        in_specs=[smem()] + [whole()] * (4 + len(pieces)),
         out_specs=whole(),
         out_shape=jax.ShapeDtypeStruct(other.shape, bf16),
         compiler_params=params(8),
         cost_estimate=cost(0, 10 * other.size),
         name="stream",
-    )(tab, kept, other, *res)
+    )(tab, kept, other, own, shared, *pieces)
 
 
 def expand_kernel(pieces, first, final, width, turned, owners, tab, *refs):
@@ -761,30 +852,32 @@
         return lax.ppermute(x, "head", exchange)
 
     ids = jnp.stack([lax.axis_index("blk"), lax.axis_index("head")]).astype(i32)
-    at = jnp.asarray([order.index(i) for i in range(ranks)], i32)
-    who = jnp.asarray(order, i32)
     tab = pl.pallas_call(
-        functools.partial(table_kernel, table, ranks),
-        in_specs=[smem()] * 7,
+        functools.partial(table_kernel, table, order),
+        in_specs=[smem()] * 5,
         out_specs=smem(),
         out_shape=jax.ShapeDtypeStruct((table.size,), i32),
         name="table",
-    )(ids, span_len, dec_count, span_start, cache_len, at, who)
+    )(ids, span_len, dec_count, span_start, cache_len)
 
     packed = pack(tab, residual, ranks, cores)
-    res = [packed[0]]
-    for shift in range(1, ranks):
-        pairs = [(i, (i + shift) % ranks) for i in range(ranks)]
-        res.append(lax.ppermute(packed[shift], "blk", pairs))
-
-    total, halves = None, None
+    pieces = []
+    for k, x in enumerate(packed):
+        pairs = [
+            (i * cores + c, (i + k + len(packed) * c) % ranks * cores + c)
+            for i in range(ranks)
+            for c in range(cores)
+            if k + c > 0
+        ]
+        pieces.append(lax.ppermute(x, ("blk", "head"), pairs))
+
+    values = attend(tab, queries, latent_cache, new_latent, value_weight, attention_parts)
+    values, pieces = lax.optimization_barrier((values, pieces))
+    shared = swap(share(tab, packed[0], pieces, cores))
+    total = None
     gathered = []
     for part in range(attention_parts):
-        main, extra = attend(
-            tab, queries, latent_cache, new_latent, value_weight, part, attention_parts
-        )
-        if part == attention_parts - 1:
-            main, extra, res = lax.optimization_barrier((main, extra, res))
+        main, extra = values[2 * part], values[2 * part + 1]
         behind, ahead = [], []
         for step in range(reach):
             if step == 0:
@@ -800,12 +893,13 @@
             behind.append(send_next(out_f))
             ahead.append(send_prev(out_b))
         gathered.append([main] + behind + ahead + [extra])
+    gathered[0], shared = lax.optimization_barrier((gathered[0], shared))
     for part in range(attention_parts):
         total = project(
             tab, table, gathered[part], total, out_weight, part, attention_parts, cores
         )
     kept, given = total
-    stream = stream_of(tab, kept, swap(given), res)
+    stream = stream_of(tab, kept, swap(given), packed[0], shared, pieces, cores)
 
     gain = norm_gain.reshape(ranks, 1, features)
     sums = expand(tab, [[stream]], [[swap(stream)]], [RANK], gain, gate_weight, up_weight, None, False)

time: 154 us -> 141 us (0.916)
  Pallas kernels: 57.6 us -> 48.8 us
  starting transfers between devices: 58.3 us -> 53.5 us
  waiting for transfers between devices: 31.2 us -> 33.1 us
    ppermute x7 -> x4, starting transfers between devices: 13.7 us -> 7.78 us  [on_device(): pieces.append(lax.ppermute(x, ('blk', 'head'), pairs))]
    pallas_call x2 -> x1, Pallas kernels: 17 us -> 12.4 us  [attend(): pl.pallas_call(functools.partial(attend_kernel, heads, group, rows, lat,...]
    pallas_call x8, Pallas kernels: 6.25 us -> 4.54 us  [route(): pl.pallas_call(route_kernel, in_specs=[smem()] + [whole()] * len(flat), o...]
    ppermute x20, starting transfers between devices: 19.5 us -> 21.2 us  [send_next(): return lax.ppermute(x, 'blk', forward)]
    unnamed x36 -> x28, local copies, waits for them, and re-layouts: 4.34 us -> 3.43 us
    pallas_call x3 -> x4, Pallas kernels: 3.51 us -> 3.19 us  [the longest x1 1.35 us: on_device(): pl.pallas_call(functools.partial(table_kernel, table, order), in_specs=[s...]
    ppermute x14 -> x15, starting transfers between devices: 3.15 us -> 3.22 us  [swap(): return lax.ppermute(x, 'head', exchange)]
    ppermute x14 -> x15, waiting for transfers between devices: 3.86 us -> 3.87 us  [swap(): return lax.ppermute(x, 'head', exchange)]
  transfers between devices with their start and end apart: 61 -> 59, of which waited for: 28 -> 29; matrix products, arithmetic and copies ran while one was open for 0% -> 0% of each run, Pallas kernels for 30% -> 27%
where the time goes in v5:
time: 141 us
  starting transfers between devices  53.5 us (38%)
  Pallas kernels  48.8 us (35%)
  waiting for transfers between devices  33.1 us (23%)
  local copies, waits for them, and re-layouts  3.45 us (2%)
    ppermute x20, starting transfers between devices, send_prev(): return lax.ppermute(x, 'blk', backward)  21.3 us
    ppermute x20, starting transfers between devices, send_next(): return lax.ppermute(x, 'blk', forward)  21.2 us
    ppermute x20, waiting for transfers between devices, send_prev(): return lax.ppermute(x, 'blk', backward)  16.1 us
    ppermute x20, waiting for transfers between devices, send_next(): return lax.ppermute(x, 'blk', forward)  13.2 us
    pallas_call x1, Pallas kernels, attend(): pl.pallas_call(functools.partial(attend_kernel, heads, group, rows, lat,...  12.4 us
    pallas_call x5, Pallas kernels, expand(): pl.pallas_call(functools.partial(expand_kernel, pieces, first, final, wid...  12.1 us
    ppermute x4, starting transfers between devices, on_device(): pieces.append(lax.ppermute(x, ('blk', 'head'), pairs))  7.78 us
    pallas_call x8, Pallas kernels, add(): pl.pallas_call(functools.partial(add_kernel, step), grid_spec=pltpu.Prefe...  5.07 us
  transfers between devices with their start and end apart: 59, of which 29 were waited for; matrix products, arithmetic and copies ran while one was open for 0% of the time, Pallas kernels for 27%

profile of v5, /device:TPU:0, one launch (start us, length us, event | category | flops | bytes accessed | tf_op | source)
XLA Modules:
  0.0 140.6 jit_solution(8892718017761904474)
XLA Ops:
  1.2 1.3 table.1.tab
  2.6 1.2 copy-done
  5.0 3.0 %collective-permute-start.1 = (bf16[64,896]{1,0:T(8,128)(2,1)S(1)}, bf16[64,896]{1,0:T(8,128)(2,1)S(1)}, u32[]{:S(2)}, u32[]{:S(2)}) collective-permute-start(bf16[64,896]{1,0:T(8,128)(2,1)S(1)} %get-tuple-element.107), channel_id=1, source_target_pairs={{0,2},{1,11},{2,4},{3,13},{4,6},{5,15},{6,8},{7,1},{8,10},{9,3},{1... | collective-permute-start | bytes 344072 | tf_op jit(solution)/shard_map/ppermute | solution.py:872
  8.0 1.6 %collective-permute-start.2 = (bf16[64,896]{1,0:T(8,128)(2,1)S(1)}, bf16[64,896]{1,0:T(8,128)(2,1)S(1)}, u32[]{:S(2)}, u32[]{:S(2)}) collective-permute-start(bf16[64,896]{1,0:T(8,128)(2,1)S(1)} %get-tuple-element.108), channel_id=1, source_target_pairs={{0,4},{1,13},{2,6},{3,15},{4,8},{5,1},{6,10},{7,3},{8,12},{9,5},{1... | collective-permute-start | bytes 344072 | tf_op jit(solution)/shard_map/ppermute | solution.py:872
  9.6 2.5 %collective-permute-start.3 = (bf16[64,896]{1,0:T(8,128)(2,1)S(1)}, bf16[64,896]{1,0:T(8,128)(2,1)S(1)}, u32[]{:S(2)}, u32[]{:S(2)}) collective-permute-start(bf16[64,896]{1,0:T(8,128)(2,1)S(1)} %get-tuple-element.109), channel_id=1, source_target_pairs={{0,6},{1,15},{2,8},{3,1},{4,10},{5,3},{6,12},{7,5},{8,14},{9,7},{1... | collective-permute-start | bytes 344072 | tf_op jit(solution)/shard_map/ppermute | solution.py:872
  12.1 0.7 collective-permute-start
  13.4 0.9 copy-done.5
  14.3 12.4 %attend.1 = (bf16[32,2048]{1,0:T(8,128)(2,1)S(1)}, bf16[32,2048]{1,0:T(8,128)(2,1)S(1)}, bf16[32,2048]{1,0:T(8,128)(2,1)S(1)}, bf16[32,2048]{1,0:T(8,128)(2,1)S(1)}) custom-call(s32[60]{0:T(128)S(1)} %copy-done.3, bf16[64,18432]{1,0:T(8,128)(2,1)} %q_hbm.1, bf16[8,576,256]{2,1,0:T(8,128)(2,1)} %cache_hbm.1, bf16[64,576]{1,0:T(8,128)(2,1)S(1)} %bitcast.29, ...), custom_call_target="tpu_custom_call" | custom-call | flops 1426063360 | bytes 8912896 | tf_op jit(solution)/shard_map/attend/pallas_call | solution.py:279
  27.5 1.9 %collective-permute-start.13 = (bf16[32,2048]{1,0:T(8,128)(2,1)S(1)}, bf16[32,2048]{1,0:T(8,128)(2,1)S(1)}, u32[]{:S(2)}, u32[]{:S(2)}) collective-permute-start(bf16[32,2048]{1,0:T(8,128)(2,1)S(1)} %get-tuple-element.130.refs_1_.refs_0_), channel_id=1, source_target_pairs={{4,0},{8,4},{12,8},{14,12},{10,14},{6,10},{2,6},{0,2},{5,1},{9,5},... | collective-permute-start | bytes 393224 | tf_op jit(solution)/shard_map/ppermute | solution.py:849
  30.2 1.9 %collective-permute-start.5 = (bf16[32,2048]{1,0:T(8,128)(2,1)S(1)}, bf16[32,2048]{1,0:T(8,128)(2,1)S(1)}, u32[]{:S(2)}, u32[]{:S(2)}) collective-permute-start(bf16[32,2048]{1,0:T(8,128)(2,1)S(1)} %get-tuple-element.110.refs_1_.refs_0_), channel_id=1, source_target_pairs={{4,0},{8,4},{12,8},{14,12},{10,14},{6,10},{2,6},{0,2},{5,1},{9,5},... | collective-permute-start | bytes 393224 | tf_op jit(solution)/shard_map/ppermute | solution.py:849
  33.2 2.9 %collective-permute-start.14 = (bf16[32,2048]{1,0:T(8,128)(2,1)S(1)}, bf16[32,2048]{1,0:T(8,128)(2,1)S(1)}, u32[]{:S(2)}, u32[]{:S(2)}) collective-permute-start(bf16[32,2048]{1,0:T(8,128)(2,1)S(1)} %get-tuple-element.120), channel_id=1, source_target_pairs={{0,4},{4,8},{8,12},{12,14},{14,10},{10,6},{6,2},{2,0},{1,5},{5,9},... | collective-permute-start | bytes 393224 | tf_op jit(solution)/shard_map/ppermute | solution.py:846
  36.8 2.2 %collective-permute-start.6 = (bf16[32,2048]{1,0:T(8,128)(2,1)S(1)}, bf16[32,2048]{1,0:T(8,128)(2,1)S(1)}, u32[]{:S(2)}, u32[]{:S(2)}) collective-permute-start(bf16[32,2048]{1,0:T(8,128)(2,1)S(1)} %get-tuple-element.112), channel_id=1, source_target_pairs={{0,4},{4,8},{8,12},{12,14},{14,10},{10,6},{6,2},{2,0},{1,5},{5,9},... | collective-permute-start | bytes 393224 | tf_op jit(solution)/shard_map/ppermute | solution.py:846
  39.0 0.7 collective-permute-done.14.refs_1_.refs_0_.refs_2_
  39.7 2.0 %collective-permute-done.15.refs_3_.refs_2_.refs_6_ = bf16[32,2048]{1,0:T(8,128)(2,1)S(1)} collective-permute-done((bf16[32,2048]{1,0:T(8,128)(2,1)S(1)}, bf16[32,2048]{1,0:T(8,128)(2,1)S(1)}, u32[]{:S(2)}, u32[]{:S(2)}) %collective-permute-start.15) | collective-permute-done | bytes 131104 | tf_op jit(solution)/shard_map/ppermute | solution.py:849
  42.3 1.7 %collective-permute-start.16 = (bf16[32,2048]{1,0:T(8,128)(2,1)S(1)}, bf16[32,2048]{1,0:T(8,128)(2,1)S(1)}, u32[]{:S(2)}, u32[]{:S(2)}) collective-permute-start(bf16[32,2048]{1,0:T(8,128)(2,1)S(1)} %get-tuple-element.122), channel_id=1, source_target_pairs={{0,4},{4,8},{8,12},{12,14},{14,10},{10,6},{6,2},{2,0},{1,5},{5,9},... | collective-permute-start | bytes 393224 | tf_op jit(solution)/shard_map/ppermute | solution.py:846
  45.6 1.7 %collective-permute-start.8 = (bf16[32,2048]{1,0:T(8,128)(2,1)S(1)}, bf16[32,2048]{1,0:T(8,128)(2,1)S(1)}, u32[]{:S(2)}, u32[]{:S(2)}) collective-permute-start(bf16[32,2048]{1,0:T(8,128)(2,1)S(1)} %get-tuple-element.114), channel_id=1, source_target_pairs={{0,4},{4,8},{8,12},{12,14},{14,10},{10,6},{6,2},{2,0},{1,5},{5,9},... | collective-permute-start | bytes 393224 | tf_op jit(solution)/shard_map/ppermute | solution.py:846
  47.7 1.2 collective-permute-done.17.refs_3_.refs_7_
  50.1 1.5 %collective-permute-start.19 = (bf16[32,2048]{1,0:T(8,128)(2,1)S(1)}, bf16[32,2048]{1,0:T(8,128)(2,1)S(1)}, u32[]{:S(2)}, u32[]{:S(2)}) collective-permute-start(bf16[32,2048]{1,0:T(8,128)(2,1)S(1)} %get-tuple-element.125), channel_id=1, source_target_pairs={{4,0},{8,4},{12,8},{14,12},{10,14},{6,10},{2,6},{0,2},{5,1},{9,5},... | collective-permute-start | bytes 393224 | tf_op jit(solution)/shard_map/ppermute | solution.py:849
  52.0 1.6 %collective-permute-done.9.refs_3_.refs_7_ = bf16[32,2048]{1,0:T(8,128)(2,1)S(1)} collective-permute-done((bf16[32,2048]{1,0:T(8,128)(2,1)S(1)}, bf16[32,2048]{1,0:T(8,128)(2,1)S(1)}, u32[]{:S(2)}, u32[]{:S(2)}) %collective-permute-start.9) | collective-permute-done | bytes 131104 | tf_op jit(solution)/shard_map/ppermute | solution.py:849
  54.8 1.5 %collective-permute-start.11 = (bf16[32,2048]{1,0:T(8,128)(2,1)S(1)}, bf16[32,2048]{1,0:T(8,128)(2,1)S(1)}, u32[]{:S(2)}, u32[]{:S(2)}) collective-permute-start(bf16[32,2048]{1,0:T(8,128)(2,1)S(1)} %get-tuple-element.117), channel_id=1, source_target_pairs={{4,0},{8,4},{12,8},{14,12},{10,14},{6,10},{2,6},{0,2},{5,1},{9,5},... | collective-permute-start | bytes 393224 | tf_op jit(solution)/shard_map/ppermute | solution.py:849
  56.3 1.9 %project.2.refs_10_ = f32[288,896]{1,0:T(8,128)S(1)} custom-call(s32[60]{0:T(128)S(1)} %copy-done.3, bf16[32,2048]{1,0:T(8,128)(2,1)S(1)} %get-tuple-element.130.refs_1_.refs_0_, bf16[32,2048]{1,0:T(8,128)(2,1)S(1)} %collective-permute-done.12.refs_1_.refs_0_, bf16[32,2048]{1,0:T(8,128)(2,1)S(1)} %collective-permute-done.14.refs_1_.refs_0_.refs_2_, ...), custom_call_target="tpu_custom_call" | custom-call | flops 1056964608 | bytes 4849664 | tf_op jit(solution)/shard_map/project/pallas_call | solution.py:460
  58.3 0.9 collective-permute-done.10.refs_4_
  59.7 2.0 %project.3 = (f32[144,896]{1,0:T(8,128)S(1)}, bf16[144,896]{1,0:T(8,128)(2,1)S(1)}) custom-call(s32[60]{0:T(128)S(1)} %copy-done.3, bf16[32,2048]{1,0:T(8,128)(2,1)S(1)} %get-tuple-element.110.refs_1_.refs_0_, bf16[32,2048]{1,0:T(8,128)(2,1)S(1)} %collective-permute-done.4.refs_1_.refs_0_, ...), custom_call_target="tpu_custom_call" | custom-call | flops 1056964608 | bytes 4849664 | tf_op jit(solution)/shard_map/project/pallas_call | solution.py:470
  61.8 1.5 %collective-permute-done.21.other = bf16[144,896]{1,0:T(8,128)(2,1)S(1)} collective-permute-done((bf16[144,896]{1,0:T(8,128)(2,1)S(1)}, bf16[144,896]{1,0:T(8,128)(2,1)S(1)}, u32[]{:S(2)}, u32[]{:S(2)}) %collective-permute-start.21) | collective-permute-done | bytes 258080 | tf_op jit(solution)/shard_map/ppermute | solution.py:852
  63.4 0.7 stream.1.refs_0_.refs_1_
  64.2 1.5 %collective-permute-start.23 = (bf16[144,896]{1,0:T(8,128)(2,1)S(1)}, bf16[144,896]{1,0:T(8,128)(2,1)S(1)}, u32[]{:S(2)}, u32[]{:S(2)}) collective-permute-start(bf16[144,896]{1,0:T(8,128)(2,1)S(1)} %stream.1.refs_0_.refs_1_), channel_id=1, source_target_pairs={{4,0},{8,4},{12,8},{14,12},{10,14},{6,10},{2,6},{0,2},{5,1},{9,5},... | collective-permute-start | bytes 774152 | tf_op jit(solution)/shard_map/ppermute | solution.py:849
  66.3 1.7 %expand.5 = (f32[288,576]{1,0:T(8,128)S(1)}, f32[288,576]{1,0:T(8,128)S(1)}, f32[288,1]{1,0:T(8,128)S(1)}) custom-call(s32[60]{0:T(128)S(1)} %copy-done.3, bf16[144,896]{1,0:T(8,128)(2,1)S(1)} %stream.1.refs_0_.refs_1_, bf16[144,896]{1,0:T(8,128)(2,1)S(1)} %collective-permute-done.24.refs_1_, f32[8,1,896]{2,1,0:T(1,128)S(1)} %bitcast.24, ...), custom_call_target="tpu_custom_call" | custom-call | flops 594542592 | bytes 2580480 | tf_op jit(solution)/shard_map/expand/pallas_call | solution.py:617
  68.0 4.7 %collective-permute-done.23.refs_2_.refs_4_.refs_5_ = bf16[144,896]{1,0:T(8,128)(2,1)S(1)} collective-permute-done((bf16[144,896]{1,0:T(8,128)(2,1)S(1)}, bf16[144,896]{1,0:T(8,128)(2,1)S(1)}, u32[]{:S(2)}, u32[]{:S(2)}) %collective-permute-start.23) | collective-permute-done | bytes 258080 | tf_op jit(solution)/shard_map/ppermute | solution.py:849
  72.7 1.2 collective-permute-done.22.refs_0_.refs_2_.refs_3_
  75.0 1.5 %collective-permute-start.26 = (bf16[144,896]{1,0:T(8,128)(2,1)S(1)}, bf16[144,896]{1,0:T(8,128)(2,1)S(1)}, u32[]{:S(2)}, u32[]{:S(2)}) collective-permute-start(bf16[144,896]{1,0:T(8,128)(2,1)S(1)} %collective-permute-done.23.refs_2_.refs_4_.refs_5_), channel_id=1, source_target_pairs={{4,0},{8,4},{12,8},{14,12},{10,14},{6,10},{2,6},{0,2},{5,1},{9,5},... | collective-permute-start | bytes 774152 | tf_op jit(solution)/shard_map/ppermute | solution.py:849
  76.5 2.9 %expand.6 = (f32[288,576]{1,0:T(8,128)S(1)}, f32[288,576]{1,0:T(8,128)S(1)}, f32[288,1]{1,0:T(8,128)S(1)}) custom-call(s32[60]{0:T(128)S(1)} %copy-done.3, bf16[144,896]{1,0:T(8,128)(2,1)S(1)} %collective-permute-done.22.refs_0_.refs_2_.refs_3_, bf16[144,896]{1,0:T(8,128)(2,1)S(1)} %collective-permute-done.27.refs_1_, ...), custom_call_target="tpu_custom_call" | custom-call | flops 1189085184 | bytes 5160960 | tf_op jit(solution)/shard_map/expand/pallas_call | solution.py:617
  79.4 3.2 %collective-permute-done.25.refs_0_.refs_6_.refs_7_ = bf16[144,896]{1,0:T(8,128)(2,1)S(1)} collective-permute-done((bf16[144,896]{1,0:T(8,128)(2,1)S(1)}, bf16[144,896]{1,0:T(8,128)(2,1)S(1)}, u32[]{:S(2)}, u32[]{:S(2)}) %collective-permute-start.25) | collective-permute-done | bytes 258080 | tf_op jit(solution)/shard_map/ppermute | solution.py:846
  83.9 1.5 %collective-permute-start.30 = (bf16[144,896]{1,0:T(8,128)(2,1)S(1)}, bf16[144,896]{1,0:T(8,128)(2,1)S(1)}, u32[]{:S(2)}, u32[]{:S(2)}) collective-permute-start(bf16[144,896]{1,0:T(8,128)(2,1)S(1)} %collective-permute-done.26.refs_2_.refs_8_.refs_9_), channel_id=1, source_target_pairs={{4,0},{8,4},{12,8},{14,12},{10,14},{6,10},{2,6},{0,2},{5,1},{9,5},... | collective-permute-start | bytes 774152 | tf_op jit(solution)/shard_map/ppermute | solution.py:849
  85.4 2.9 %expand.7 = (f32[288,576]{1,0:T(8,128)S(1)}, f32[288,576]{1,0:T(8,128)S(1)}, f32[288,1]{1,0:T(8,128)S(1)}) custom-call(s32[60]{0:T(128)S(1)} %copy-done.3, bf16[144,896]{1,0:T(8,128)(2,1)S(1)} %collective-permute-done.25.refs_0_.refs_6_.refs_7_, bf16[144,896]{1,0:T(8,128)(2,1)S(1)} %collective-permute-done.31.refs_1_, ...), custom_call_target="tpu_custom_call" | custom-call | flops 1189085184 | bytes 5160960 | tf_op jit(solution)/shard_map/expand/pallas_call | solution.py:617
  88.3 3.2 %collective-permute-done.29.refs_0_.refs_10_.refs_11_ = bf16[144,896]{1,0:T(8,128)(2,1)S(1)} collective-permute-done((bf16[144,896]{1,0:T(8,128)(2,1)S(1)}, bf16[144,896]{1,0:T(8,128)(2,1)S(1)}, u32[]{:S(2)}, u32[]{:S(2)}) %collective-permute-start.29) | collective-permute-done | bytes 258080 | tf_op jit(solution)/shard_map/ppermute | solution.py:846
  92.3 1.6 %collective-permute-start.33 = (bf16[80,896]{1,0:T(8,128)(2,1)S(1)}, bf16[80,896]{1,0:T(8,128)(2,1)S(1)}, u32[]{:S(2)}, u32[]{:S(2)}) collective-permute-start(bf16[80,896]{1,0:T(8,128)(2,1)S(1)} %slice.6), channel_id=1, source_target_pairs={{0,4},{4,8},{8,12},{12,14},{14,10},{10,6},{6,2},{2,0},{1,5},{5,9},... | collective-permute-start | bytes 430088 | tf_op jit(solution)/shard_map/ppermute | solution.py:846
  94.4 2.9 %expand.8 = (f32[288,576]{1,0:T(8,128)S(1)}, f32[288,576]{1,0:T(8,128)S(1)}, f32[288,1]{1,0:T(8,128)S(1)}) custom-call(s32[60]{0:T(128)S(1)} %copy-done.3, bf16[144,896]{1,0:T(8,128)(2,1)S(1)} %collective-permute-done.29.refs_0_.refs_10_.refs_11_, bf16[144,896]{1,0:T(8,128)(2,1)S(1)} %collective-permute-done.35.refs_1_, ...), custom_call_target="tpu_custom_call" | custom-call | flops 1189085184 | bytes 5160960 | tf_op jit(solution)/shard_map/expand/pallas_call | solution.py:617
  97.3 1.4 collective-permute-done.34.refs_1_
  99.3 1.0 collective-permute-done.38.refs_3_
  100.3 1.8 %expand.9.hidden = bf16[288,576]{1,0:T(8,128)(2,1)S(1)} custom-call(s32[60]{0:T(128)S(1)} %copy-done.3, bf16[80,896]{1,0:T(8,128)(2,1)S(1)} %collective-permute-done.33.refs_0_, bf16[64,896]{1,0:T(8,128)(2,1)S(1)} %collective-permute-done.34.refs_1_, bf16[80,896]{1,0:T(8,128)(2,1)S(1)} %collective-permute-done.37.refs_2_, ...), custom_call_target="tpu_custom_call" | custom-call | flops 594542592 | bytes 2580480 | tf_op jit(solution)/shard_map/expand/pallas_call | solution.py:617
  102.1 2.1 %contract.3 = (bf16[144,3584]{1,0:T(8,128)(2,1)S(1)}, bf16[144,3584]{1,0:T(8,128)(2,1)S(1)}) custom-call(bf16[288,576]{1,0:T(8,128)(2,1)S(1)} %expand.9.hidden, bf16[576,7168]{1,0:T(8,128)(2,1)S(1)} %bitcast.21), custom_call_target="tpu_custom_call" | custom-call | flops 1189085184 | bytes 6193152 | tf_op jit(solution)/shard_map/contract/pallas_call | solution.py:683
  104.6 2.1 %contract.2 = (bf16[144,3584]{1,0:T(8,128)(2,1)S(1)}, bf16[144,3584]{1,0:T(8,128)(2,1)S(1)}) custom-call(bf16[288,576]{1,0:T(8,128)(2,1)S(1)} %expand.9.hidden, bf16[576,7168]{1,0:T(8,128)(2,1)S(1)} %bitcast.21), custom_call_target="tpu_custom_call" | custom-call | flops 1189085184 | bytes 6193152 | tf_op jit(solution)/shard_map/contract/pallas_call | solution.py:683
  107.6 1.8 %collective-permute-start.49 = (bf16[16,3584]{1,0:T(8,128)(2,1)S(1)}, bf16[16,3584]{1,0:T(8,128)(2,1)S(1)}, u32[]{:S(2)}, u32[]{:S(2)}) collective-permute-start(bf16[16,3584]{1,0:T(8,128)(2,1)S(1)} %get-tuple-element.188), channel_id=1, source_target_pairs={{0,4},{4,8},{8,12},{12,14},{14,10},{10,6},{6,2},{2,0},{1,5},{5,9},... | collective-permute-start | bytes 344072 | tf_op jit(solution)/shard_map/ppermute | solution.py:846
  110.3 1.8 %collective-permute-start.40 = (bf16[16,3584]{1,0:T(8,128)(2,1)S(1)}, bf16[16,3584]{1,0:T(8,128)(2,1)S(1)}, u32[]{:S(2)}, u32[]{:S(2)}) collective-permute-start(bf16[16,3584]{1,0:T(8,128)(2,1)S(1)} %get-tuple-element.177), channel_id=1, source_target_pairs={{0,4},{4,8},{8,12},{12,14},{14,10},{10,6},{6,2},{2,0},{1,5},{5,9},... | collective-permute-start | bytes 344072 | tf_op jit(solution)/shard_map/ppermute | solution.py:846
  112.4 0.7 collective-permute-done.49.refs_0_
  113.1 1.5 %collective-permute-done.50.refs_1_.refs_2_ = bf16[16,3584]{1,0:T(8,128)(2,1)S(1)} collective-permute-done((bf16[16,3584]{1,0:T(8,128)(2,1)S(1)}, bf16[16,3584]{1,0:T(8,128)(2,1)S(1)}, u32[]{:S(2)}, u32[]{:S(2)}) %collective-permute-start.50) | collective-permute-done | bytes 114720 | tf_op jit(solution)/shard_map/ppermute | solution.py:849
  115.2 0.8 collective-permute-start.51
  116.0 1.3 collective-permute-start.52
  118.0 0.8 collective-permute-start.42
  118.7 1.3 collective-permute-start.43
  120.0 0.9 collective-permute-done.51.refs_1_.refs_0_
  121.0 1.0 collective-permute-done.52.refs_3_.refs_2_
  123.1 1.6 %collective-permute-start.54 = (bf16[16,3584]{1,0:T(8,128)(2,1)S(1)}, bf16[16,3584]{1,0:T(8,128)(2,1)S(1)}, u32[]{:S(2)}, u32[]{:S(2)}) collective-permute-start(bf16[16,3584]{1,0:T(8,128)(2,1)S(1)} %get-tuple-element.193), channel_id=1, source_target_pairs={{4,0},{8,4},{12,8},{14,12},{10,14},{6,10},{2,6},{0,2},{5,1},{9,5},... | collective-permute-start | bytes 344072 | tf_op jit(solution)/shard_map/ppermute | solution.py:849
  125.8 1.6 %collective-permute-start.45 = (bf16[16,3584]{1,0:T(8,128)(2,1)S(1)}, bf16[16,3584]{1,0:T(8,128)(2,1)S(1)}, u32[]{:S(2)}, u32[]{:S(2)}) collective-permute-start(bf16[16,3584]{1,0:T(8,128)(2,1)S(1)} %get-tuple-element.182), channel_id=1, source_target_pairs={{4,0},{8,4},{12,8},{14,12},{10,14},{6,10},{2,6},{0,2},{5,1},{9,5},... | collective-permute-start | bytes 344072 | tf_op jit(solution)/shard_map/ppermute | solution.py:849
  128.8 0.9 collective-permute-start.55
  129.6 1.2 collective-permute-start.56
  131.5 0.9 collective-permute-start.46
  132.4 1.2 collective-permute-start.47
  134.4 0.7 close.3
  135.2 1.1 collective-permute-done.46.f_last
  136.3 0.8 collective-permute-done.47.b_last
  137.2 0.7 close.2
  138.0 1.3 collective-permute-done.57.refs_2_
  139.3 1.4 finish.1
  (124 shorter events, 25.7 us)
Async XLA Ops:
  4.4 51.9 %slice-start.6 = ((s8[7340032]{0:T(1024)(128)(4,1)}), s8[4194304]{0:T(1024)(128)(4,1)S(1)}, s32[]{:S(2)}) async-start(s8[7340032]{0:T(1024)(128)(4,1)} %bitcast.22), calls=%async_computation.6 | async-start | bytes 8388608
  5.0 21.8 %collective-permute-start.1 = (bf16[64,896]{1,0:T(8,128)(2,1)S(1)}, bf16[64,896]{1,0:T(8,128)(2,1)S(1)}, u32[]{:S(2)}, u32[]{:S(2)}) collective-permute-start(bf16[64,896]{1,0:T(8,128)(2,1)S(1)} %get-tuple-element.107), channel_id=1, source_target_pairs={{0,2},{1,11},{2,4},{3,13},{4,6},{5,15},{6,8},{7,1},{8,10},{9,3},{1... | collective-permute-start | bytes 344072 | tf_op jit(solution)/shard_map/ppermute | solution.py:872
  8.0 18.8 %collective-permute-start.2 = (bf16[64,896]{1,0:T(8,128)(2,1)S(1)}, bf16[64,896]{1,0:T(8,128)(2,1)S(1)}, u32[]{:S(2)}, u32[]{:S(2)}) collective-permute-start(bf16[64,896]{1,0:T(8,128)(2,1)S(1)} %get-tuple-element.108), channel_id=1, source_target_pairs={{0,4},{1,13},{2,6},{3,15},{4,8},{5,1},{6,10},{7,3},{8,12},{9,5},{1... | collective-permute-start | bytes 344072 | tf_op jit(solution)/shard_map/ppermute | solution.py:872
  9.6 17.2 %collective-permute-start.3 = (bf16[64,896]{1,0:T(8,128)(2,1)S(1)}, bf16[64,896]{1,0:T(8,128)(2,1)S(1)}, u32[]{:S(2)}, u32[]{:S(2)}) collective-permute-start(bf16[64,896]{1,0:T(8,128)(2,1)S(1)} %get-tuple-element.109), channel_id=1, source_target_pairs={{0,6},{1,15},{2,8},{3,1},{4,10},{5,3},{6,12},{7,5},{8,14},{9,7},{1... | collective-permute-start | bytes 344072 | tf_op jit(solution)/shard_map/ppermute | solution.py:872
  12.1 14.7 %collective-permute-start = (bf16[64,896]{1,0:T(8,128)(2,1)S(1)}, bf16[64,896]{1,0:T(8,128)(2,1)S(1)}, u32[]{:S(2)}, u32[]{:S(2)}) collective-permute-start(bf16[64,896]{1,0:T(8,128)(2,1)S(1)} %get-tuple-element.106.own), channel_id=1, source_target_pairs={{1,9},{3,11},{5,13},{7,15},{9,1},{11,3},{13,5},{15,7},{17,25},{19,... | collective-permute-start | bytes 344072 | tf_op jit(solution)/shard_map/ppermute | solution.py:872
  14.3 41.9 %slice-start.7 = ((s8[7340032]{0:T(1024)(128)(4,1)}), s8[3145728]{0:T(1024)(128)(4,1)S(1)}, s32[]{:S(2)}) async-start(s8[7340032]{0:T(1024)(128)(4,1)} %bitcast.22), calls=%async_computation.7 | async-start | bytes 6291456
  27.4 5.0 %collective-permute-start.12 = (bf16[32,2048]{1,0:T(8,128)(2,1)S(1)}, bf16[32,2048]{1,0:T(8,128)(2,1)S(1)}, u32[]{:S(2)}, u32[]{:S(2)}) collective-permute-start(bf16[32,2048]{1,0:T(8,128)(2,1)S(1)} %route.12), channel_id=1, source_target_pairs={{0,4},{4,8},{8,12},{12,14},{14,10},{10,6},{6,2},{2,0},{1,5},{5,9},... | collective-permute-start | bytes 393224 | tf_op jit(solution)/shard_map/ppermute | solution.py:846
  27.5 5.0 %collective-permute-start.13 = (bf16[32,2048]{1,0:T(8,128)(2,1)S(1)}, bf16[32,2048]{1,0:T(8,128)(2,1)S(1)}, u32[]{:S(2)}, u32[]{:S(2)}) collective-permute-start(bf16[32,2048]{1,0:T(8,128)(2,1)S(1)} %get-tuple-element.130.refs_1_.refs_0_), channel_id=1, source_target_pairs={{4,0},{8,4},{12,8},{14,12},{10,14},{6,10},{2,6},{0,2},{5,1},{9,5},... | collective-permute-start | bytes 393224 | tf_op jit(solution)/shard_map/ppermute | solution.py:849
  30.0 6.1 %collective-permute-start.4 = (bf16[32,2048]{1,0:T(8,128)(2,1)S(1)}, bf16[32,2048]{1,0:T(8,128)(2,1)S(1)}, u32[]{:S(2)}, u32[]{:S(2)}) collective-permute-start(bf16[32,2048]{1,0:T(8,128)(2,1)S(1)} %route.8), channel_id=1, source_target_pairs={{0,4},{4,8},{8,12},{12,14},{14,10},{10,6},{6,2},{2,0},{1,5},{5,9},... | collective-permute-start | bytes 393224 | tf_op jit(solution)/shard_map/ppermute | solution.py:846
  30.2 6.0 %collective-permute-start.5 = (bf16[32,2048]{1,0:T(8,128)(2,1)S(1)}, bf16[32,2048]{1,0:T(8,128)(2,1)S(1)}, u32[]{:S(2)}, u32[]{:S(2)}) collective-permute-start(bf16[32,2048]{1,0:T(8,128)(2,1)S(1)} %get-tuple-element.110.refs_1_.refs_0_), channel_id=1, source_target_pairs={{4,0},{8,4},{12,8},{14,12},{10,14},{6,10},{2,6},{0,2},{5,1},{9,5},... | collective-permute-start | bytes 393224 | tf_op jit(solution)/shard_map/ppermute | solution.py:849
  33.2 6.5 %collective-permute-start.14 = (bf16[32,2048]{1,0:T(8,128)(2,1)S(1)}, bf16[32,2048]{1,0:T(8,128)(2,1)S(1)}, u32[]{:S(2)}, u32[]{:S(2)}) collective-permute-start(bf16[32,2048]{1,0:T(8,128)(2,1)S(1)} %get-tuple-element.120), channel_id=1, source_target_pairs={{0,4},{4,8},{8,12},{12,14},{14,10},{10,6},{6,2},{2,0},{1,5},{5,9},... | collective-permute-start | bytes 393224 | tf_op jit(solution)/shard_map/ppermute | solution.py:846
  36.1 5.6 %collective-permute-start.15 = (bf16[32,2048]{1,0:T(8,128)(2,1)S(1)}, bf16[32,2048]{1,0:T(8,128)(2,1)S(1)}, u32[]{:S(2)}, u32[]{:S(2)}) collective-permute-start(bf16[32,2048]{1,0:T(8,128)(2,1)S(1)} %get-tuple-element.121), channel_id=1, source_target_pairs={{4,0},{8,4},{12,8},{14,12},{10,14},{6,10},{2,6},{0,2},{5,1},{9,5},... | collective-permute-start | bytes 393224 | tf_op jit(solution)/shard_map/ppermute | solution.py:849
  36.8 8.3 %collective-permute-start.6 = (bf16[32,2048]{1,0:T(8,128)(2,1)S(1)}, bf16[32,2048]{1,0:T(8,128)(2,1)S(1)}, u32[]{:S(2)}, u32[]{:S(2)}) collective-permute-start(bf16[32,2048]{1,0:T(8,128)(2,1)S(1)} %get-tuple-element.112), channel_id=1, source_target_pairs={{0,4},{4,8},{8,12},{12,14},{14,10},{10,6},{6,2},{2,0},{1,5},{5,9},... | collective-permute-start | bytes 393224 | tf_op jit(solution)/shard_map/ppermute | solution.py:846
  38.9 6.1 %collective-permute-start.7 = (bf16[32,2048]{1,0:T(8,128)(2,1)S(1)}, bf16[32,2048]{1,0:T(8,128)(2,1)S(1)}, u32[]{:S(2)}, u32[]{:S(2)}) collective-permute-start(bf16[32,2048]{1,0:T(8,128)(2,1)S(1)} %get-tuple-element.113), channel_id=1, source_target_pairs={{4,0},{8,4},{12,8},{14,12},{10,14},{6,10},{2,6},{0,2},{5,1},{9,5},... | collective-permute-start | bytes 393224 | tf_op jit(solution)/shard_map/ppermute | solution.py:849
  42.3 5.4 %collective-permute-start.16 = (bf16[32,2048]{1,0:T(8,128)(2,1)S(1)}, bf16[32,2048]{1,0:T(8,128)(2,1)S(1)}, u32[]{:S(2)}, u32[]{:S(2)}) collective-permute-start(bf16[32,2048]{1,0:T(8,128)(2,1)S(1)} %get-tuple-element.122), channel_id=1, source_target_pairs={{0,4},{4,8},{8,12},{12,14},{14,10},{10,6},{6,2},{2,0},{1,5},{5,9},... | collective-permute-start | bytes 393224 | tf_op jit(solution)/shard_map/ppermute | solution.py:846
  44.0 5.0 %collective-permute-start.17 = (bf16[32,2048]{1,0:T(8,128)(2,1)S(1)}, bf16[32,2048]{1,0:T(8,128)(2,1)S(1)}, u32[]{:S(2)}, u32[]{:S(2)}) collective-permute-start(bf16[32,2048]{1,0:T(8,128)(2,1)S(1)} %get-tuple-element.123), channel_id=1, source_target_pairs={{4,0},{8,4},{12,8},{14,12},{10,14},{6,10},{2,6},{0,2},{5,1},{9,5},... | collective-permute-start | bytes 393224 | tf_op jit(solution)/shard_map/ppermute | solution.py:849
  44.4 21.9 %slice-start.2 = ((s8[8257536]{0:T(1024)(128)(4,1)}), s8[4194304]{0:T(1024)(128)(4,1)S(1)}, s32[]{:S(2)}) async-start(s8[8257536]{0:T(1024)(128)(4,1)} %bitcast.13), calls=%async_computation.2 | async-start | bytes 8388608
  44.9 11.3 %collective-permute-start.20 = (bf16[128,896]{1,0:T(8,128)(2,1)S(1)}, bf16[128,896]{1,0:T(8,128)(2,1)S(1)}, u32[]{:S(2)}, u32[]{:S(2)}) collective-permute-start(bf16[128,896]{1,0:T(8,128)(2,1)S(1)} %share.1), channel_id=1, source_target_pairs={{0,1},{1,0},{2,3},{3,2},{4,5},{5,4},{6,7},{7,6},{8,9},{9,8},{10,11... | collective-permute-start | bytes 688136 | tf_op jit(solution)/shard_map/ppermute | solution.py:852
  45.6 6.4 %collective-permute-start.8 = (bf16[32,2048]{1,0:T(8,128)(2,1)S(1)}, bf16[32,2048]{1,0:T(8,128)(2,1)S(1)}, u32[]{:S(2)}, u32[]{:S(2)}) collective-permute-start(bf16[32,2048]{1,0:T(8,128)(2,1)S(1)} %get-tuple-element.114), channel_id=1, source_target_pairs={{0,4},{4,8},{8,12},{12,14},{14,10},{10,6},{6,2},{2,0},{1,5},{5,9},... | collective-permute-start | bytes 393224 | tf_op jit(solution)/shard_map/ppermute | solution.py:846
  47.3 6.3 %collective-permute-start.9 = (bf16[32,2048]{1,0:T(8,128)(2,1)S(1)}, bf16[32,2048]{1,0:T(8,128)(2,1)S(1)}, u32[]{:S(2)}, u32[]{:S(2)}) collective-permute-start(bf16[32,2048]{1,0:T(8,128)(2,1)S(1)} %get-tuple-element.115), channel_id=1, source_target_pairs={{4,0},{8,4},{12,8},{14,12},{10,14},{6,10},{2,6},{0,2},{5,1},{9,5},... | collective-permute-start | bytes 393224 | tf_op jit(solution)/shard_map/ppermute | solution.py:849
  49.5 6.7 %collective-permute-start.18 = (bf16[32,2048]{1,0:T(8,128)(2,1)S(1)}, bf16[32,2048]{1,0:T(8,128)(2,1)S(1)}, u32[]{:S(2)}, u32[]{:S(2)}) collective-permute-start(bf16[32,2048]{1,0:T(8,128)(2,1)S(1)} %get-tuple-element.124), channel_id=1, source_target_pairs={{0,4},{4,8},{8,12},{12,14},{14,10},{10,6},{6,2},{2,0},{1,5},{5,9},... | collective-permute-start | bytes 393224 | tf_op jit(solution)/shard_map/ppermute | solution.py:846
  50.1 6.1 %collective-permute-start.19 = (bf16[32,2048]{1,0:T(8,128)(2,1)S(1)}, bf16[32,2048]{1,0:T(8,128)(2,1)S(1)}, u32[]{:S(2)}, u32[]{:S(2)}) collective-permute-start(bf16[32,2048]{1,0:T(8,128)(2,1)S(1)} %get-tuple-element.125), channel_id=1, source_target_pairs={{4,0},{8,4},{12,8},{14,12},{10,14},{6,10},{2,6},{0,2},{5,1},{9,5},... | collective-permute-start | bytes 393224 | tf_op jit(solution)/shard_map/ppermute | solution.py:849
  54.2 5.0 %collective-permute-start.10 = (bf16[32,2048]{1,0:T(8,128)(2,1)S(1)}, bf16[32,2048]{1,0:T(8,128)(2,1)S(1)}, u32[]{:S(2)}, u32[]{:S(2)}) collective-permute-start(bf16[32,2048]{1,0:T(8,128)(2,1)S(1)} %get-tuple-element.116), channel_id=1, source_target_pairs={{0,4},{4,8},{8,12},{12,14},{14,10},{10,6},{6,2},{2,0},{1,5},{5,9},... | collective-permute-start | bytes 393224 | tf_op jit(solution)/shard_map/ppermute | solution.py:846
  54.8 11.5 %slice-start.3 = ((s8[8257536]{0:T(1024)(128)(4,1)}), s8[4063232]{0:T(1024)(128)(4,1)S(1)}, s32[]{:S(2)}) async-start(s8[8257536]{0:T(1024)(128)(4,1)} %bitcast.13), calls=%async_computation.3 | async-start | bytes 8126464
  54.8 5.0 %collective-permute-start.11 = (bf16[32,2048]{1,0:T(8,128)(2,1)S(1)}, bf16[32,2048]{1,0:T(8,128)(2,1)S(1)}, u32[]{:S(2)}, u32[]{:S(2)}) collective-permute-start(bf16[32,2048]{1,0:T(8,128)(2,1)S(1)} %get-tuple-element.117), channel_id=1, source_target_pairs={{4,0},{8,4},{12,8},{14,12},{10,14},{6,10},{2,6},{0,2},{5,1},{9,5},... | collective-permute-start | bytes 393224 | tf_op jit(solution)/shard_map/ppermute | solution.py:849
  56.3 10.0 %slice-start = ((s8[8257536]{0:T(1024)(128)(4,1)}), s8[4194304]{0:T(1024)(128)(4,1)S(1)}, s32[]{:S(2)}) async-start(s8[8257536]{0:T(1024)(128)(4,1)} %bitcast.6), calls=%async_computation | async-start | bytes 8388608
  61.8 1.6 %collective-permute-start.21 = (bf16[144,896]{1,0:T(8,128)(2,1)S(1)}, bf16[144,896]{1,0:T(8,128)(2,1)S(1)}, u32[]{:S(2)}, u32[]{:S(2)}) collective-permute-start(bf16[144,896]{1,0:T(8,128)(2,1)S(1)} %get-tuple-element.141), channel_id=1, source_target_pairs={{0,1},{1,0},{2,3},{3,2},{4,5},{5,4},{6,7},{7,6},{8,9},{9,8},{10,11... | collective-permute-start | bytes 774152 | tf_op jit(solution)/shard_map/ppermute | solution.py:852
  64.0 2.2 %collective-permute-start.24 = (bf16[144,896]{1,0:T(8,128)(2,1)S(1)}, bf16[144,896]{1,0:T(8,128)(2,1)S(1)}, u32[]{:S(2)}, u32[]{:S(2)}) collective-permute-start(bf16[144,896]{1,0:T(8,128)(2,1)S(1)} %stream.1.refs_0_.refs_1_), channel_id=1, source_target_pairs={{0,1},{1,0},{2,3},{3,2},{4,5},{5,4},{6,7},{7,6},{8,9},{9,8},{10,11... | collective-permute-start | bytes 774152 | tf_op jit(solution)/shard_map/ppermute | solution.py:852
  64.2 8.5 %collective-permute-start.23 = (bf16[144,896]{1,0:T(8,128)(2,1)S(1)}, bf16[144,896]{1,0:T(8,128)(2,1)S(1)}, u32[]{:S(2)}, u32[]{:S(2)}) collective-permute-start(bf16[144,896]{1,0:T(8,128)(2,1)S(1)} %stream.1.refs_0_.refs_1_), channel_id=1, source_target_pairs={{4,0},{8,4},{12,8},{14,12},{10,14},{6,10},{2,6},{0,2},{5,1},{9,5},... | collective-permute-start | bytes 774152 | tf_op jit(solution)/shard_map/ppermute | solution.py:849
  65.7 8.2 %collective-permute-start.22 = (bf16[144,896]{1,0:T(8,128)(2,1)S(1)}, bf16[144,896]{1,0:T(8,128)(2,1)S(1)}, u32[]{:S(2)}, u32[]{:S(2)}) collective-permute-start(bf16[144,896]{1,0:T(8,128)(2,1)S(1)} %stream.1.refs_0_.refs_1_), channel_id=1, source_target_pairs={{0,4},{4,8},{8,12},{12,14},{14,10},{10,6},{6,2},{2,0},{1,5},{5,9},... | collective-permute-start | bytes 774152 | tf_op jit(solution)/shard_map/ppermute | solution.py:846
  73.9 2.5 %collective-permute-start.27 = (bf16[144,896]{1,0:T(8,128)(2,1)S(1)}, bf16[144,896]{1,0:T(8,128)(2,1)S(1)}, u32[]{:S(2)}, u32[]{:S(2)}) collective-permute-start(bf16[144,896]{1,0:T(8,128)(2,1)S(1)} %collective-permute-done.22.refs_0_.refs_2_.refs_3_), channel_id=1, source_target_pairs={{0,1},{1,0},{2,3},{3,2},{4,5},{5,4},{6,7},{7,6},{8,9},{9,8},{10,11... | collective-permute-start | bytes 774152 | tf_op jit(solution)/shard_map/ppermute | solution.py:852
  73.9 2.5 %collective-permute-start.28 = (bf16[144,896]{1,0:T(8,128)(2,1)S(1)}, bf16[144,896]{1,0:T(8,128)(2,1)S(1)}, u32[]{:S(2)}, u32[]{:S(2)}) collective-permute-start(bf16[144,896]{1,0:T(8,128)(2,1)S(1)} %collective-permute-done.23.refs_2_.refs_4_.refs_5_), channel_id=1, source_target_pairs={{0,1},{1,0},{2,3},{3,2},{4,5},{5,4},{6,7},{7,6},{8,9},{9,8},{10,11... | collective-permute-start | bytes 774152 | tf_op jit(solution)/shard_map/ppermute | solution.py:852
  74.4 8.1 %collective-permute-start.25 = (bf16[144,896]{1,0:T(8,128)(2,1)S(1)}, bf16[144,896]{1,0:T(8,128)(2,1)S(1)}, u32[]{:S(2)}, u32[]{:S(2)}) collective-permute-start(bf16[144,896]{1,0:T(8,128)(2,1)S(1)} %collective-permute-done.22.refs_0_.refs_2_.refs_3_), channel_id=1, source_target_pairs={{0,4},{4,8},{8,12},{12,14},{14,10},{10,6},{6,2},{2,0},{1,5},{5,9},... | collective-permute-start | bytes 774152 | tf_op jit(solution)/shard_map/ppermute | solution.py:846
  75.0 7.8 %collective-permute-start.26 = (bf16[144,896]{1,0:T(8,128)(2,1)S(1)}, bf16[144,896]{1,0:T(8,128)(2,1)S(1)}, u32[]{:S(2)}, u32[]{:S(2)}) collective-permute-start(bf16[144,896]{1,0:T(8,128)(2,1)S(1)} %collective-permute-done.23.refs_2_.refs_4_.refs_5_), channel_id=1, source_target_pairs={{4,0},{8,4},{12,8},{14,12},{10,14},{6,10},{2,6},{0,2},{5,1},{9,5},... | collective-permute-start | bytes 774152 | tf_op jit(solution)/shard_map/ppermute | solution.py:849
  82.9 2.5 %collective-permute-start.31 = (bf16[144,896]{1,0:T(8,128)(2,1)S(1)}, bf16[144,896]{1,0:T(8,128)(2,1)S(1)}, u32[]{:S(2)}, u32[]{:S(2)}) collective-permute-start(bf16[144,896]{1,0:T(8,128)(2,1)S(1)} %collective-permute-done.25.refs_0_.refs_6_.refs_7_), channel_id=1, source_target_pairs={{0,1},{1,0},{2,3},{3,2},{4,5},{5,4},{6,7},{7,6},{8,9},{9,8},{10,11... | collective-permute-start | bytes 774152 | tf_op jit(solution)/shard_map/ppermute | solution.py:852
  82.9 2.5 %collective-permute-start.32 = (bf16[144,896]{1,0:T(8,128)(2,1)S(1)}, bf16[144,896]{1,0:T(8,128)(2,1)S(1)}, u32[]{:S(2)}, u32[]{:S(2)}) collective-permute-start(bf16[144,896]{1,0:T(8,128)(2,1)S(1)} %collective-permute-done.26.refs_2_.refs_8_.refs_9_), channel_id=1, source_target_pairs={{0,1},{1,0},{2,3},{3,2},{4,5},{5,4},{6,7},{7,6},{8,9},{9,8},{10,11... | collective-permute-start | bytes 774152 | tf_op jit(solution)/shard_map/ppermute | solution.py:852
  83.4 8.1 %collective-permute-start.29 = (bf16[144,896]{1,0:T(8,128)(2,1)S(1)}, bf16[144,896]{1,0:T(8,128)(2,1)S(1)}, u32[]{:S(2)}, u32[]{:S(2)}) collective-permute-start(bf16[144,896]{1,0:T(8,128)(2,1)S(1)} %collective-permute-done.25.refs_0_.refs_6_.refs_7_), channel_id=1, source_target_pairs={{0,4},{4,8},{8,12},{12,14},{14,10},{10,6},{6,2},{2,0},{1,5},{5,9},... | collective-permute-start | bytes 774152 | tf_op jit(solution)/shard_map/ppermute | solution.py:846
  83.9 7.8 %collective-permute-start.30 = (bf16[144,896]{1,0:T(8,128)(2,1)S(1)}, bf16[144,896]{1,0:T(8,128)(2,1)S(1)}, u32[]{:S(2)}, u32[]{:S(2)}) collective-permute-start(bf16[144,896]{1,0:T(8,128)(2,1)S(1)} %collective-permute-done.26.refs_2_.refs_8_.refs_9_), channel_id=1, source_target_pairs={{4,0},{8,4},{12,8},{14,12},{10,14},{6,10},{2,6},{0,2},{5,1},{9,5},... | collective-permute-start | bytes 774152 | tf_op jit(solution)/shard_map/ppermute | solution.py:849
  91.7 2.7 %collective-permute-start.35 = (bf16[144,896]{1,0:T(8,128)(2,1)S(1)}, bf16[144,896]{1,0:T(8,128)(2,1)S(1)}, u32[]{:S(2)}, u32[]{:S(2)}) collective-permute-start(bf16[144,896]{1,0:T(8,128)(2,1)S(1)} %collective-permute-done.29.refs_0_.refs_10_.refs_11_), channel_id=1, source_target_pairs={{0,1},{1,0},{2,3},{3,2},{4,5},{5,4},{6,7},{7,6},{8,9},{9,8},{10,11... | collective-permute-start | bytes 774152 | tf_op jit(solution)/shard_map/ppermute | solution.py:852
  91.7 2.7 %collective-permute-start.36 = (bf16[144,896]{1,0:T(8,128)(2,1)S(1)}, bf16[144,896]{1,0:T(8,128)(2,1)S(1)}, u32[]{:S(2)}, u32[]{:S(2)}) collective-permute-start(bf16[144,896]{1,0:T(8,128)(2,1)S(1)} %collective-permute-done.30.refs_2_.refs_12_.refs_13_), channel_id=1, source_target_pairs={{0,1},{1,0},{2,3},{3,2},{4,5},{5,4},{6,7},{7,6},{8,9},{9,8},{10,11... | collective-permute-start | bytes 774152 | tf_op jit(solution)/shard_map/ppermute | solution.py:852
  92.3 6.4 %collective-permute-start.33 = (bf16[80,896]{1,0:T(8,128)(2,1)S(1)}, bf16[80,896]{1,0:T(8,128)(2,1)S(1)}, u32[]{:S(2)}, u32[]{:S(2)}) collective-permute-start(bf16[80,896]{1,0:T(8,128)(2,1)S(1)} %slice.6), channel_id=1, source_target_pairs={{0,4},{4,8},{8,12},{12,14},{14,10},{10,6},{6,2},{2,0},{1,5},{5,9},... | collective-permute-start | bytes 430088 | tf_op jit(solution)/shard_map/ppermute | solution.py:846
  93.8 4.8 %collective-permute-start.34 = (bf16[64,896]{1,0:T(8,128)(2,1)S(1)}, bf16[64,896]{1,0:T(8,128)(2,1)S(1)}, u32[]{:S(2)}, u32[]{:S(2)}) collective-permute-start(bf16[64,896]{1,0:T(8,128)(2,1)S(1)} %slice.7), channel_id=1, source_target_pairs={{4,0},{8,4},{12,8},{14,12},{10,14},{6,10},{2,6},{0,2},{5,1},{9,5},... | collective-permute-start | bytes 344072 | tf_op jit(solution)/shard_map/ppermute | solution.py:849
  98.7 1.6 %collective-permute-start.37 = (bf16[80,896]{1,0:T(8,128)(2,1)S(1)}, bf16[80,896]{1,0:T(8,128)(2,1)S(1)}, u32[]{:S(2)}, u32[]{:S(2)}) collective-permute-start(bf16[80,896]{1,0:T(8,128)(2,1)S(1)} %collective-permute-done.33.refs_0_), channel_id=1, source_target_pairs={{0,1},{1,0},{2,3},{3,2},{4,5},{5,4},{6,7},{7,6},{8,9},{9,8},{10,11... | collective-permute-start | bytes 430088 | tf_op jit(solution)/shard_map/ppermute | solution.py:852
  98.8 1.5 %collective-permute-start.38 = (bf16[64,896]{1,0:T(8,128)(2,1)S(1)}, bf16[64,896]{1,0:T(8,128)(2,1)S(1)}, u32[]{:S(2)}, u32[]{:S(2)}) collective-permute-start(bf16[64,896]{1,0:T(8,128)(2,1)S(1)} %collective-permute-done.34.refs_1_), channel_id=1, source_target_pairs={{0,1},{1,0},{2,3},{3,2},{4,5},{5,4},{6,7},{7,6},{8,9},{9,8},{10,11... | collective-permute-start | bytes 344072 | tf_op jit(solution)/shard_map/ppermute | solution.py:852
  104.2 2.7 %collective-permute-start.48 = (bf16[144,3584]{1,0:T(8,128)(2,1)S(1)}, bf16[144,3584]{1,0:T(8,128)(2,1)S(1)}, u32[]{:S(2)}, u32[]{:S(2)}) collective-permute-start(bf16[144,3584]{1,0:T(8,128)(2,1)S(1)} %get-tuple-element.187), channel_id=1, source_target_pairs={{0,1},{1,0},{2,3},{3,2},{4,5},{5,4},{6,7},{7,6},{8,9},{9,8},{10,11... | collective-permute-start | bytes 3096584 | tf_op jit(solution)/shard_map/ppermute | solution.py:852
  106.7 3.0 %collective-permute-start.39 = (bf16[144,3584]{1,0:T(8,128)(2,1)S(1)}, bf16[144,3584]{1,0:T(8,128)(2,1)S(1)}, u32[]{:S(2)}, u32[]{:S(2)}) collective-permute-start(bf16[144,3584]{1,0:T(8,128)(2,1)S(1)} %get-tuple-element.176), channel_id=1, source_target_pairs={{0,1},{1,0},{2,3},{3,2},{4,5},{5,4},{6,7},{7,6},{8,9},{9,8},{10,11... | collective-permute-start | bytes 3096584 | tf_op jit(solution)/shard_map/ppermute | solution.py:852
  107.6 5.5 %collective-permute-start.49 = (bf16[16,3584]{1,0:T(8,128)(2,1)S(1)}, bf16[16,3584]{1,0:T(8,128)(2,1)S(1)}, u32[]{:S(2)}, u32[]{:S(2)}) collective-permute-start(bf16[16,3584]{1,0:T(8,128)(2,1)S(1)} %get-tuple-element.188), channel_id=1, source_target_pairs={{0,4},{4,8},{8,12},{12,14},{14,10},{10,6},{6,2},{2,0},{1,5},{5,9},... | collective-permute-start | bytes 344072 | tf_op jit(solution)/shard_map/ppermute | solution.py:846
  109.4 5.2 %collective-permute-start.50 = (bf16[16,3584]{1,0:T(8,128)(2,1)S(1)}, bf16[16,3584]{1,0:T(8,128)(2,1)S(1)}, u32[]{:S(2)}, u32[]{:S(2)}) collective-permute-start(bf16[16,3584]{1,0:T(8,128)(2,1)S(1)} %get-tuple-element.189), channel_id=1, source_target_pairs={{4,0},{8,4},{12,8},{14,12},{10,14},{6,10},{2,6},{0,2},{5,1},{9,5},... | collective-permute-start | bytes 344072 | tf_op jit(solution)/shard_map/ppermute | solution.py:849
  110.3 7.0 %collective-permute-start.40 = (bf16[16,3584]{1,0:T(8,128)(2,1)S(1)}, bf16[16,3584]{1,0:T(8,128)(2,1)S(1)}, u32[]{:S(2)}, u32[]{:S(2)}) collective-permute-start(bf16[16,3584]{1,0:T(8,128)(2,1)S(1)} %get-tuple-element.177), channel_id=1, source_target_pairs={{0,4},{4,8},{8,12},{12,14},{14,10},{10,6},{6,2},{2,0},{1,5},{5,9},... | collective-permute-start | bytes 344072 | tf_op jit(solution)/shard_map/ppermute | solution.py:846
  112.1 5.2 %collective-permute-start.41 = (bf16[16,3584]{1,0:T(8,128)(2,1)S(1)}, bf16[16,3584]{1,0:T(8,128)(2,1)S(1)}, u32[]{:S(2)}, u32[]{:S(2)}) collective-permute-start(bf16[16,3584]{1,0:T(8,128)(2,1)S(1)} %get-tuple-element.178), channel_id=1, source_target_pairs={{4,0},{8,4},{12,8},{14,12},{10,14},{6,10},{2,6},{0,2},{5,1},{9,5},... | collective-permute-start | bytes 344072 | tf_op jit(solution)/shard_map/ppermute | solution.py:849
  115.2 5.8 %collective-permute-start.51 = (bf16[16,3584]{1,0:T(8,128)(2,1)S(1)}, bf16[16,3584]{1,0:T(8,128)(2,1)S(1)}, u32[]{:S(2)}, u32[]{:S(2)}) collective-permute-start(bf16[16,3584]{1,0:T(8,128)(2,1)S(1)} %get-tuple-element.190), channel_id=1, source_target_pairs={{0,4},{4,8},{8,12},{12,14},{14,10},{10,6},{6,2},{2,0},{1,5},{5,9},... | collective-permute-start | bytes 344072 | tf_op jit(solution)/shard_map/ppermute | solution.py:846
  116.0 6.0 %collective-permute-start.52 = (bf16[16,3584]{1,0:T(8,128)(2,1)S(1)}, bf16[16,3584]{1,0:T(8,128)(2,1)S(1)}, u32[]{:S(2)}, u32[]{:S(2)}) collective-permute-start(bf16[16,3584]{1,0:T(8,128)(2,1)S(1)} %get-tuple-element.191), channel_id=1, source_target_pairs={{4,0},{8,4},{12,8},{14,12},{10,14},{6,10},{2,6},{0,2},{5,1},{9,5},... | collective-permute-start | bytes 344072 | tf_op jit(solution)/shard_map/ppermute | solution.py:849
  118.0 6.7 %collective-permute-start.42 = (bf16[16,3584]{1,0:T(8,128)(2,1)S(1)}, bf16[16,3584]{1,0:T(8,128)(2,1)S(1)}, u32[]{:S(2)}, u32[]{:S(2)}) collective-permute-start(bf16[16,3584]{1,0:T(8,128)(2,1)S(1)} %get-tuple-element.179), channel_id=1, source_target_pairs={{0,4},{4,8},{8,12},{12,14},{14,10},{10,6},{6,2},{2,0},{1,5},{5,9},... | collective-permute-start | bytes 344072 | tf_op jit(solution)/shard_map/ppermute | solution.py:846
  118.7 6.0 %collective-permute-start.43 = (bf16[16,3584]{1,0:T(8,128)(2,1)S(1)}, bf16[16,3584]{1,0:T(8,128)(2,1)S(1)}, u32[]{:S(2)}, u32[]{:S(2)}) collective-permute-start(bf16[16,3584]{1,0:T(8,128)(2,1)S(1)} %get-tuple-element.180), channel_id=1, source_target_pairs={{4,0},{8,4},{12,8},{14,12},{10,14},{6,10},{2,6},{0,2},{5,1},{9,5},... | collective-permute-start | bytes 344072 | tf_op jit(solution)/shard_map/ppermute | solution.py:849
  122.6 5.4 %collective-permute-start.53 = (bf16[16,3584]{1,0:T(8,128)(2,1)S(1)}, bf16[16,3584]{1,0:T(8,128)(2,1)S(1)}, u32[]{:S(2)}, u32[]{:S(2)}) collective-permute-start(bf16[16,3584]{1,0:T(8,128)(2,1)S(1)} %get-tuple-element.192), channel_id=1, source_target_pairs={{0,4},{4,8},{8,12},{12,14},{14,10},{10,6},{6,2},{2,0},{1,5},{5,9},... | collective-permute-start | bytes 344072 | tf_op jit(solution)/shard_map/ppermute | solution.py:846
  123.1 5.0 %collective-permute-start.54 = (bf16[16,3584]{1,0:T(8,128)(2,1)S(1)}, bf16[16,3584]{1,0:T(8,128)(2,1)S(1)}, u32[]{:S(2)}, u32[]{:S(2)}) collective-permute-start(bf16[16,3584]{1,0:T(8,128)(2,1)S(1)} %get-tuple-element.193), channel_id=1, source_target_pairs={{4,0},{8,4},{12,8},{14,12},{10,14},{6,10},{2,6},{0,2},{5,1},{9,5},... | collective-permute-start | bytes 344072 | tf_op jit(solution)/shard_map/ppermute | solution.py:849
  125.4 5.5 %collective-permute-start.44 = (bf16[16,3584]{1,0:T(8,128)(2,1)S(1)}, bf16[16,3584]{1,0:T(8,128)(2,1)S(1)}, u32[]{:S(2)}, u32[]{:S(2)}) collective-permute-start(bf16[16,3584]{1,0:T(8,128)(2,1)S(1)} %get-tuple-element.181), channel_id=1, source_target_pairs={{0,4},{4,8},{8,12},{12,14},{14,10},{10,6},{6,2},{2,0},{1,5},{5,9},... | collective-permute-start | bytes 344072 | tf_op jit(solution)/shard_map/ppermute | solution.py:846
  125.8 5.0 %collective-permute-start.45 = (bf16[16,3584]{1,0:T(8,128)(2,1)S(1)}, bf16[16,3584]{1,0:T(8,128)(2,1)S(1)}, u32[]{:S(2)}, u32[]{:S(2)}) collective-permute-start(bf16[16,3584]{1,0:T(8,128)(2,1)S(1)} %get-tuple-element.182), channel_id=1, source_target_pairs={{4,0},{8,4},{12,8},{14,12},{10,14},{6,10},{2,6},{0,2},{5,1},{9,5},... | collective-permute-start | bytes 344072 | tf_op jit(solution)/shard_map/ppermute | solution.py:849
  128.8 5.4 %collective-permute-start.55 = (bf16[16,3584]{1,0:T(8,128)(2,1)S(1)}, bf16[16,3584]{1,0:T(8,128)(2,1)S(1)}, u32[]{:S(2)}, u32[]{:S(2)}) collective-permute-start(bf16[16,3584]{1,0:T(8,128)(2,1)S(1)} %get-tuple-element.194), channel_id=1, source_target_pairs={{0,4},{4,8},{8,12},{12,14},{14,10},{10,6},{6,2},{2,0},{1,5},{5,9},... | collective-permute-start | bytes 344072 | tf_op jit(solution)/shard_map/ppermute | solution.py:846
  129.6 4.8 %collective-permute-start.56 = (bf16[16,3584]{1,0:T(8,128)(2,1)S(1)}, bf16[16,3584]{1,0:T(8,128)(2,1)S(1)}, u32[]{:S(2)}, u32[]{:S(2)}) collective-permute-start(bf16[16,3584]{1,0:T(8,128)(2,1)S(1)} %get-tuple-element.195), channel_id=1, source_target_pairs={{4,0},{8,4},{12,8},{14,12},{10,14},{6,10},{2,6},{0,2},{5,1},{9,5},... | collective-permute-start | bytes 344072 | tf_op jit(solution)/shard_map/ppermute | solution.py:849
  131.5 4.8 %collective-permute-start.46 = (bf16[16,3584]{1,0:T(8,128)(2,1)S(1)}, bf16[16,3584]{1,0:T(8,128)(2,1)S(1)}, u32[]{:S(2)}, u32[]{:S(2)}) collective-permute-start(bf16[16,3584]{1,0:T(8,128)(2,1)S(1)} %get-tuple-element.183), channel_id=1, source_target_pairs={{0,4},{4,8},{8,12},{12,14},{14,10},{10,6},{6,2},{2,0},{1,5},{5,9},... | collective-permute-start | bytes 344072 | tf_op jit(solution)/shard_map/ppermute | solution.py:846
  132.4 4.8 %collective-permute-start.47 = (bf16[16,3584]{1,0:T(8,128)(2,1)S(1)}, bf16[16,3584]{1,0:T(8,128)(2,1)S(1)}, u32[]{:S(2)}, u32[]{:S(2)}) collective-permute-start(bf16[16,3584]{1,0:T(8,128)(2,1)S(1)} %get-tuple-element.184), channel_id=1, source_target_pairs={{4,0},{8,4},{12,8},{14,12},{10,14},{6,10},{2,6},{0,2},{5,1},{9,5},... | collective-permute-start | bytes 344072 | tf_op jit(solution)/shard_map/ppermute | solution.py:849
  135.2 2.8 %collective-permute-start.58 = (bf16[16,3584]{1,0:T(8,128)(2,1)S(1)}, bf16[16,3584]{1,0:T(8,128)(2,1)S(1)}, u32[]{:S(2)}, u32[]{:S(2)}) collective-permute-start(bf16[16,3584]{1,0:T(8,128)(2,1)S(1)} %get-tuple-element.198), channel_id=1, source_target_pairs={{0,1},{1,0},{2,3},{3,2},{4,5},{5,4},{6,7},{7,6},{8,9},{9,8},{10,11... | collective-permute-start | bytes 344072 | tf_op jit(solution)/shard_map/ppermute | solution.py:852
  137.9 1.4 collective-permute-start.57
  (9 other events, 31.2 us)

commit v6 on v5

--- a/solution.py
+++ b/solution.py
@@ -131,39 +131,58 @@
 
 
 def attend_kernel(
-    heads, group, rows, lat, value, parts, tab, q_hbm, cache_hbm, fresh, vw_hbm, *refs
+    table, order, heads, first, count, group, rows, lat, value, lead, *refs
 ):
-    outs, refs = refs[: 2 * parts], refs[2 * parts :]
-    q, keys, vw, dq, latent, fz, q_sem, key_sem, vw_sem = refs
-    slots = keys.shape[0] - 2
-    cached = keys.shape[2]
-    wide = keys.shape[1]
+    if lead:
+        scalars, refs = refs[:5], refs[5:]
+        q_hbm, cache_hbm, fresh, vw_hbm, tab, head, main, extra, later = refs[:9]
+        refs = refs[9:]
+        q, keys, vw, latent, fz, q_sem, key_sem, vw_sem, dq = refs
+        loaded, base = heads, 0
+    else:
+        tab, q_hbm, cache_hbm, fresh, vw_hbm, decoded_here, head, main, extra = refs[:9]
+        q, keys, vw, latent, fz, q_sem, key_sem, vw_sem = refs[9:]
+        loaded, base = count, first
+    cached, wide = keys.shape[2], keys.shape[1]
+    slots = cache_hbm.shape[0] - 1
+    odd_slot = keys.shape[0] - 1
     shift, pair, dr = wide - lat, 2 * lat, 8
-    groups, pairs = heads // group, group // 2
-    span, decs = tab[SPAN], tab[DEC]
+    groups, pairs = count // group, group // 2
+    loads = loaded // group
 
     def q_copy(g):
-        at = pl.ds(g * group * lat, group * lat)
-        return pltpu.make_async_copy(q_hbm.at[:, at], q.at[:, at], q_sem.at[g])
+        source = pl.ds((base + g * group) * lat, group * lat)
+        return pltpu.make_async_copy(
+            q_hbm.at[:, source], q.at[:, pl.ds(g * group * lat, group * lat)], q_sem.at[g]
+        )
 
     def vw_copy(g):
-        at = pl.ds(g * group, group)
-        return pltpu.make_async_copy(vw_hbm.at[at], vw.at[at], vw_sem.at[g])
+        source = pl.ds(first + g * group, group)
+        return pltpu.make_async_copy(vw_hbm.at[source], vw.at[pl.ds(g * group, group)], vw_sem.at[g])
 
     even_copy = pltpu.make_async_copy(cache_hbm.at[0], keys.at[0, pl.ds(0, lat)], key_sem.at[0])
     odd_copy = pltpu.make_async_copy(
-        cache_hbm.at[0], keys.at[slots + 1, pl.ds(shift, lat)], key_sem.at[1]
+        cache_hbm.at[0], keys.at[odd_slot, pl.ds(shift, lat)], key_sem.at[1]
     )
-    rest_copy = pltpu.make_async_copy(
-        cache_hbm.at[pl.ds(1, slots)], keys.at[pl.ds(1, slots), pl.ds(0, lat)], key_sem.at[2]
-    )
+    waiting = [q_copy(g) for g in range(1, loads)]
+    if lead:
+        rest_copy = pltpu.make_async_copy(
+            cache_hbm.at[pl.ds(1, slots)], keys.at[pl.ds(1, slots), pl.ds(0, lat)], key_sem.at[2]
+        )
+        waiting.append(rest_copy)
+    waiting += [vw_copy(g) for g in range(groups)]
+
+    def start_next(number):
+        for _ in range(min(number, len(waiting))):
+            waiting.pop(0).start()
+
     even_copy.start()
+    q_copy(0).start()
     odd_copy.start()
-    for g in range(groups):
-        q_copy(g).start()
-    rest_copy.start()
-    for g in range(groups):
-        vw_copy(g).start()
+    start_next(1)
+    if lead:
+        table_kernel(table, order, *scalars, tab)
+    span, decs = tab[SPAN], tab[DEC]
 
     def onehot(shape, row_dim, slot_dim):
         r = lax.broadcasted_iota(i32, shape, row_dim)
@@ -171,9 +190,9 @@
         return jnp.where((r == span + j) & (j < decs), 1.0, 0.0).astype(bf16)
 
     tail = jnp.zeros((shift, cached), bf16)
-    for s in range(slots + 1):
+    for s in range(odd_slot):
         keys[s, lat:] = tail
-    keys[slots + 1, :shift] = tail
+    keys[odd_slot, :shift] = tail
     fz[...] = jnp.zeros_like(fz)
     fz[:rows, :lat] = fresh[...].astype(f32)
     fresh_even = fz[...].astype(bf16)
@@ -197,51 +216,60 @@
     odd_copy.wait()
     for g in range(groups):
         q_copy(g).wait()
+        start_next(2)
         start = g * group * lat
         for odd in range(2):
             off = start + odd * (pair - wide)
             lhs = jnp.concatenate(
                 [q[:, off + pair * p : off + pair * p + wide] for p in range(pairs)], 0
             )
-            o = span_latent(lhs, (slots + 1) * odd, fresh_odd if odd else fresh_even)
-            latent[g, odd] = o
-
-    pick = onehot((16, rows), 1, 0)
-    for p in range(heads // 2):
-        got = mm(pick, q[:, pair * p : pair * (p + 1)])[:dr]
-        dq[2 * p * dr : (2 * p + 1) * dr] = got[:, :wide]
-        dq[(2 * p + 1) * dr : (2 * p + 2) * dr] = pltpu.roll(got[:, pair - wide :], wide - shift, 1)
-    n = heads * dr
-    queries = dq[...].astype(bf16)
-    slot = lax.broadcasted_iota(i32, (n, 1), 0) % dr
-    rest_copy.wait()
-    length = jnp.zeros((n, 1), i32)
-    scores = jnp.zeros((n, cached), f32)
-    for s in range(slots):
-        scores = jnp.where(slot == s, mm(queries, keys[s + 1]), scores)
-        length = jnp.where(slot == s, tab[LENGTHS + s], length)
-    unmasked = lax.broadcasted_iota(i32, (n, cached), 1) < length
-    scores = jnp.where(unmasked, scores * score_scale, masked_score)
-    own = mm_nt(queries, fresh_even)
-    column = lax.broadcasted_iota(i32, own.shape, 1)
-    own = jnp.sum(jnp.where(column == span + slot, own, 0.0), axis=1, keepdims=True)
-    own = own * score_scale
-    peak = jnp.maximum(jnp.max(scores, axis=1, keepdims=True), own)
-    e = jnp.where(unmasked, jnp.exp(scores - peak), 0.0)
-    e_own = jnp.exp(own - peak)
-    total = jnp.sum(e, axis=1, keepdims=True) + e_own
-    w = e / total
-    acc = jnp.zeros((n, value), f32)
-    for s in range(slots):
-        acc = acc + mm_nt(jnp.where(slot == s, w, 0.0).astype(bf16), keys[s + 1, :value])
-    own_value = mm(pick, fresh[:, :value])[:dr]
-    own_value = jnp.broadcast_to(own_value[None], (heads, dr, value)).reshape(n, value)
-    dec = (acc + (e_own / total).astype(bf16).astype(f32) * own_value).astype(bf16)
+            latent[g, odd] = span_latent(lhs, odd_slot * odd, fresh_odd if odd else fresh_even)
+    start_next(len(waiting))
+
+    if lead:
+        for g in range(groups, loads):
+            q_copy(g).wait()
+        pick = onehot((16, rows), 1, 0)
+        for p in range(heads // 2):
+            got = mm(pick, q[:, pair * p : pair * (p + 1)])[:dr]
+            dq[2 * p * dr : (2 * p + 1) * dr] = got[:, :wide]
+            dq[(2 * p + 1) * dr : (2 * p + 2) * dr] = pltpu.roll(
+                got[:, pair - wide :], wide - shift, 1
+            )
+        n = heads * dr
+        queries = dq[...].astype(bf16)
+        slot = lax.broadcasted_iota(i32, (n, 1), 0) % dr
+        rest_copy.wait()
+        length = jnp.zeros((n, 1), i32)
+        scores = jnp.zeros((n, cached), f32)
+        for s in range(slots):
+            scores = jnp.where(slot == s, mm(queries, keys[s + 1]), scores)
+            length = jnp.where(slot == s, tab[LENGTHS + s], length)
+        unmasked = lax.broadcasted_iota(i32, (n, cached), 1) < length
+        scores = jnp.where(unmasked, scores * score_scale, masked_score)
+        own = mm_nt(queries, fresh_even)
+        column = lax.broadcasted_iota(i32, own.shape, 1)
+        own = jnp.sum(jnp.where(column == span + slot, own, 0.0), axis=1, keepdims=True)
+        own = own * score_scale
+        peak = jnp.maximum(jnp.max(scores, axis=1, keepdims=True), own)
+        e = jnp.where(unmasked, jnp.exp(scores - peak), 0.0)
+        e_own = jnp.exp(own - peak)
+        total = jnp.sum(e, axis=1, keepdims=True) + e_own
+        w = e / total
+        acc = jnp.zeros((n, value), f32)
+        for s in range(slots):
+            acc = acc + mm_nt(jnp.where(slot == s, w, 0.0).astype(bf16), keys[s + 1, :value])
+        own_value = mm(pick, fresh[:, :value])[:dr]
+        own_value = jnp.broadcast_to(own_value[None], (heads, dr, value)).reshape(n, value)
+        dec = (acc + (e_own / total).astype(bf16).astype(f32) * own_value).astype(bf16)
+        later[...] = dec[count * dr :]
+        dec = dec[: count * dr]
+    else:
+        dec = decoded_here[...]
 
     place = onehot((rows, 16), 0, 1)
     vh = vw.shape[2]
     block = rows // 2
-    per_part = groups // parts
     for g in range(groups):
         vw_copy(g).wait()
         values, decoded = [], []
@@ -261,45 +289,61 @@
         decoded = jnp.concatenate(decoded, 1)
         decoded = jnp.concatenate([decoded, jnp.zeros_like(decoded)], 0).astype(bf16)
         out = (jnp.concatenate(values, 1) + mm(place, decoded)).astype(bf16)
-        part, at = g // per_part, (g % per_part) * group * vh
-        outs[2 * part][:, at : at + group * vh] = out[:block]
-        outs[2 * part + 1][:, at : at + group * vh] = out[block:]
-
-
-def attend(tab, queries, cache, fresh, vw, parts):
+        at = slice(g * group * vh, (g + 1) * group * vh)
+        main[:, at] = out[:block]
+        extra[:, at] = out[block:]
+        head[:, at] = jnp.where(tab[BUSY] == 1, out[block:], out[:block])
+
+
+def attend(table, order, scalars, queries, cache, fresh, vw, part, parts, decoded):
     rows, heads = queries.shape[0], vw.shape[0]
     lat = queries.shape[1] // heads
     slots, _, cached = cache.shape
     value, vh = vw.shape[1:]
-    group = min(8, heads // parts)
-    groups = heads // group
+    count = heads // parts
+    group = min(8, count)
+    lead = decoded is None
+    loaded = heads if lead else count
     wide = -(-lat // 128) * 128
-    half = jax.ShapeDtypeStruct((rows // 2, heads // parts * vh), bf16)
+    half = jax.ShapeDtypeStruct((rows // 2, count * vh), bf16)
     hbm = pl.BlockSpec(memory_space=pltpu.HBM)
-    return pl.pallas_call(
-        functools.partial(attend_kernel, heads, group, rows, lat, value, parts),
-        in_specs=[smem(), hbm, hbm, whole(), hbm],
-        out_specs=[whole()] * (2 * parts),
-        out_shape=[half] * (2 * parts),
-        scratch_shapes=[
-            pltpu.VMEM(queries.shape, bf16),
-            pltpu.VMEM((slots + 1, wide, cached), bf16),
-            pltpu.VMEM(vw.shape, bf16),
-            pltpu.VMEM((heads * 8, wide), f32),
-            pltpu.VMEM((groups, 2, group // 2 * rows, value), bf16),
-            pltpu.VMEM((-(-rows // 128) * 128, wide), f32),
-            pltpu.SemaphoreType.DMA((groups,)),
-            pltpu.SemaphoreType.DMA((3,)),
-            pltpu.SemaphoreType.DMA((groups,)),
-        ],
-        compiler_params=params(28),
+    scratch = [
+        pltpu.VMEM((rows, loaded * lat), bf16),
+        pltpu.VMEM((slots + 1 if lead else 2, wide, cached), bf16),
+        pltpu.VMEM((count, value, vh), bf16),
+        pltpu.VMEM((count // group, 2, group // 2 * rows, value), bf16),
+        pltpu.VMEM((-(-rows // 128) * 128, wide), f32),
+        pltpu.SemaphoreType.DMA((loaded // group,)),
+        pltpu.SemaphoreType.DMA((3,)),
+        pltpu.SemaphoreType.DMA((count // group,)),
+    ]
+    out_shape, out_specs = [half] * 3, [whole()] * 3
+    ins = [smem()] * len(scalars) + [hbm, hbm, whole(), hbm]
+    args = [*scalars, in_hbm(queries), in_hbm(cache), fresh.T, in_hbm(vw)]
+    if lead:
+        scratch.append(pltpu.VMEM((heads * 8, wide), f32))
+        out_shape = [jax.ShapeDtypeStruct((table.size,), i32)] + out_shape
+        out_shape += [jax.ShapeDtypeStruct(((heads - count) * 8, value), bf16)]
+        out_specs = [smem()] + out_specs + [whole()]
+    else:
+        ins.append(whole())
+        args.append(decoded)
+    return pl.pallas_call(
+        functools.partial(
+            attend_kernel, table, order, heads, part * count, count, group, rows, lat, value, lead
+        ),
+        in_specs=ins,
+        out_specs=out_specs,
+        out_shape=out_shape,
+        scratch_shapes=scratch,
+        compiler_params=params(24),
         cost_estimate=cost(
-            2 * rows * heads * (cached + rows) * (lat + value),
-            2 * (queries.size + cache.size + vw.size),
-            rows * heads * (cached + rows),
+            2 * rows * count * (cached + rows) * (lat + value),
+            2 * (queries.size + cache.size + vw.size) // parts,
+            rows * count * (cached + rows),
         ),
         name="attend",
-    )(tab, in_hbm(queries), in_hbm(cache), fresh.T, in_hbm(vw))
+    )(*args)
 
 
 def pack_kernel(ranks, cores, features, tab, res, *outs):
@@ -809,7 +853,6 @@
     )(tab, *kept, *got)
 
 
-attention_parts = 2
 contract_parts = 2
 
 
@@ -852,13 +895,9 @@
         return lax.ppermute(x, "head", exchange)
 
     ids = jnp.stack([lax.axis_index("blk"), lax.axis_index("head")]).astype(i32)
-    tab = pl.pallas_call(
-        functools.partial(table_kernel, table, order),
-        in_specs=[smem()] * 5,
-        out_specs=smem(),
-        out_shape=jax.ShapeDtypeStruct((table.size,), i32),
-        name="table",
-    )(ids, span_len, dec_count, span_start, cache_len)
+    scalars = [ids, span_len, dec_count, span_start, cache_len]
+    caches = (queries, latent_cache, new_latent, value_weight)
+    tab, *lead, decoded = attend(table, order, scalars, *caches, 0, 2, None)
 
     packed = pack(tab, residual, ranks, cores)
     pieces = []
@@ -871,17 +910,18 @@
         ]
         pieces.append(lax.ppermute(x, ("blk", "head"), pairs))
 
-    values = attend(tab, queries, latent_cache, new_latent, value_weight, attention_parts)
-    values, pieces = lax.optimization_barrier((values, pieces))
+    decoded, packed = lax.optimization_barrier((decoded, packed))
+    follow = attend(table, order, [tab], *caches, 1, 2, decoded)
+    follow, pieces = lax.optimization_barrier((follow, pieces))
     shared = swap(share(tab, packed[0], pieces, cores))
+
     total = None
     gathered = []
-    for part in range(attention_parts):
-        main, extra = values[2 * part], values[2 * part + 1]
+    for head, main, extra in (lead, follow):
         behind, ahead = [], []
         for step in range(reach):
             if step == 0:
-                (out_f,), out_b = route(tab, (extra, main)), main
+                out_f, out_b = head, main
             elif step == 1:
                 out_f, out_b = route(tab, (main, behind[0]), (extra, ahead[0]))
             else:
@@ -894,10 +934,8 @@
             ahead.append(send_prev(out_b))
         gathered.append([main] + behind + ahead + [extra])
     gathered[0], shared = lax.optimization_barrier((gathered[0], shared))
-    for part in range(attention_parts):
-        total = project(
-            tab, table, gathered[part], total, out_weight, part, attention_parts, cores
-        )
+    for part in range(2):
+        total = project(tab, table, gathered[part], total, out_weight, part, 2, cores)
     kept, given = total
     stream = stream_of(tab, kept, swap(given), packed[0], shared, pieces, cores)
 

time: 141 us -> 140 us (level)
    ppermute x20, starting transfers between devices: 21.2 us -> 23 us  [send_next(): return lax.ppermute(x, 'blk', forward)]
    pallas_call x8 -> x6, Pallas kernels: 4.54 us -> 3.42 us  [route(): pl.pallas_call(route_kernel, in_specs=[smem()] + [whole()] * len(flat), o...]
    unnamed x28 -> x30, local copies, waits for them, and re-layouts: 3.43 us -> 2.92 us
  transfers between devices with their start and end apart: 59 -> 59, of which waited for: 29 -> 27; matrix products, arithmetic and copies ran while one was open for 0% -> 0% of each run, Pallas kernels for 27% -> 22%
where the time goes in v6:
time: 140 us
  starting transfers between devices  54.8 us (39%)
  Pallas kernels  48.1 us (34%)
  waiting for transfers between devices  33 us (24%)
  local copies, waits for them, and re-layouts  2.95 us (2%)
    ppermute x20, starting transfers between devices, send_next(): return lax.ppermute(x, 'blk', forward)  23 us
    ppermute x20, starting transfers between devices, send_prev(): return lax.ppermute(x, 'blk', backward)  20.2 us
    ppermute x20, waiting for transfers between devices, send_prev(): return lax.ppermute(x, 'blk', backward)  16.7 us
    pallas_call x2, Pallas kernels, attend(): pl.pallas_call(functools.partial(attend_kernel, table, order, heads, part...  14.2 us
    ppermute x20, waiting for transfers between devices, send_next(): return lax.ppermute(x, 'blk', forward)  12.4 us
    pallas_call x5, Pallas kernels, expand(): pl.pallas_call(functools.partial(expand_kernel, pieces, first, final, wid...  12.1 us
    ppermute x4, starting transfers between devices, on_device(): pieces.append(lax.ppermute(x, ('blk', 'head'), pairs))  7.91 us
    pallas_call x8, Pallas kernels, add(): pl.pallas_call(functools.partial(add_kernel, step), grid_spec=pltpu.Prefe...  5.06 us
  transfers between devices with their start and end apart: 59, of which 27 were waited for; matrix products, arithmetic and copies ran while one was open for 0% of the time, Pallas kernels for 22%

profile of v6, /device:TPU:0, one launch (start us, length us, event | category | flops | bytes accessed | tf_op | source)
XLA Modules:
  0.0 140.2 jit_solution(8748906806120803345)
XLA Ops:
  0.8 0.9 copy-done.2
  3.7 8.3 %attend.2 = (s32[60]{0:T(128)S(1)}, bf16[32,2048]{1,0:T(8,128)(2,1)S(1)}, bf16[32,2048]{1,0:T(8,128)(2,1)S(1)}, bf16[32,2048]{1,0:T(8,128)(2,1)S(1)}, bf16[128,512]{1,0:T(8,128)(2,1)S(1)}) custom-call(s32[2]{0:T(128)S(1)} %pad_add_fusion.refs_0_, s32[8]{0:T(128)S(1)} %copy-done.4, s32[8]{0:T(128)S(1)} %copy-done.5, s32[1]{0:T(128)S(6)} %copy.15.refs_3_, ...), custom_call_target="tpu_custom_call" | custom-call | flops 713031680 | bytes 4456448 | tf_op jit(solution)/shard_map/attend/pallas_call | solution.py:331
  12.6 0.8 collective-permute-start
  13.4 3.0 %collective-permute-start.1 = (bf16[64,896]{1,0:T(8,128)(2,1)S(1)}, bf16[64,896]{1,0:T(8,128)(2,1)S(1)}, u32[]{:S(2)}, u32[]{:S(2)}) collective-permute-start(bf16[64,896]{1,0:T(8,128)(2,1)S(1)} %get-tuple-element.110), channel_id=1, source_target_pairs={{0,2},{1,11},{2,4},{3,13},{4,6},{5,15},{6,8},{7,1},{8,10},{9,3},{1... | collective-permute-start | bytes 344072 | tf_op jit(solution)/shard_map/ppermute | solution.py:911
  16.4 1.6 %collective-permute-start.2 = (bf16[64,896]{1,0:T(8,128)(2,1)S(1)}, bf16[64,896]{1,0:T(8,128)(2,1)S(1)}, u32[]{:S(2)}, u32[]{:S(2)}) collective-permute-start(bf16[64,896]{1,0:T(8,128)(2,1)S(1)} %get-tuple-element.111), channel_id=1, source_target_pairs={{0,4},{1,13},{2,6},{3,15},{4,8},{5,1},{6,10},{7,3},{8,12},{9,5},{1... | collective-permute-start | bytes 344072 | tf_op jit(solution)/shard_map/ppermute | solution.py:911
  18.0 2.5 %collective-permute-start.3 = (bf16[64,896]{1,0:T(8,128)(2,1)S(1)}, bf16[64,896]{1,0:T(8,128)(2,1)S(1)}, u32[]{:S(2)}, u32[]{:S(2)}) collective-permute-start(bf16[64,896]{1,0:T(8,128)(2,1)S(1)} %get-tuple-element.112), channel_id=1, source_target_pairs={{0,6},{1,15},{2,8},{3,1},{4,10},{5,3},{6,12},{7,5},{8,14},{9,7},{1... | collective-permute-start | bytes 344072 | tf_op jit(solution)/shard_map/ppermute | solution.py:911
  20.6 1.9 %collective-permute-start.13 = (bf16[32,2048]{1,0:T(8,128)(2,1)S(1)}, bf16[32,2048]{1,0:T(8,128)(2,1)S(1)}, u32[]{:S(2)}, u32[]{:S(2)}) collective-permute-start(bf16[32,2048]{1,0:T(8,128)(2,1)S(1)} %get-tuple-element.140.refs_0_), channel_id=1, source_target_pairs={{4,0},{8,4},{12,8},{14,12},{10,14},{6,10},{2,6},{0,2},{5,1},{9,5},... | collective-permute-start | bytes 393224 | tf_op jit(solution)/shard_map/ppermute | solution.py:892
  22.5 5.9 %attend.3 = (bf16[32,2048]{1,0:T(8,128)(2,1)S(1)}, bf16[32,2048]{1,0:T(8,128)(2,1)S(1)}, bf16[32,2048]{1,0:T(8,128)(2,1)S(1)}) custom-call(s32[60]{0:T(128)S(1)} %get-tuple-element.107.tab.refs_0_, bf16[64,18432]{1,0:T(8,128)(2,1)} %refs_1_.3, bf16[8,576,256]{2,1,0:T(8,128)(2,1)} %refs_2_.3, bf16[64,576]{1,0:T(8,128)(2,1)S(1)} %bitcast.30, ...), custom_call_target="tpu_custom_call" | custom-call | flops 713031680 | bytes 4456448 | tf_op jit(solution)/shard_map/attend/pallas_call | solution.py:331
  28.5 1.4 %collective-permute-start.4 = (bf16[32,2048]{1,0:T(8,128)(2,1)S(1)}, bf16[32,2048]{1,0:T(8,128)(2,1)S(1)}, u32[]{:S(2)}, u32[]{:S(2)}) collective-permute-start(bf16[32,2048]{1,0:T(8,128)(2,1)S(1)} %get-tuple-element.118), channel_id=1, source_target_pairs={{0,4},{4,8},{8,12},{12,14},{14,10},{10,6},{6,2},{2,0},{1,5},{5,9},... | collective-permute-start | bytes 393224 | tf_op jit(solution)/shard_map/ppermute | solution.py:889
  31.2 2.1 %collective-permute-start.14 = (bf16[32,2048]{1,0:T(8,128)(2,1)S(1)}, bf16[32,2048]{1,0:T(8,128)(2,1)S(1)}, u32[]{:S(2)}, u32[]{:S(2)}) collective-permute-start(bf16[32,2048]{1,0:T(8,128)(2,1)S(1)} %get-tuple-element.129), channel_id=1, source_target_pairs={{0,4},{4,8},{8,12},{12,14},{14,10},{10,6},{6,2},{2,0},{1,5},{5,9},... | collective-permute-start | bytes 393224 | tf_op jit(solution)/shard_map/ppermute | solution.py:889
  33.5 1.4 collective-permute-done.5.refs_3_.refs_2_.refs_5_
  35.5 3.5 %collective-permute-start.6 = (bf16[32,2048]{1,0:T(8,128)(2,1)S(1)}, bf16[32,2048]{1,0:T(8,128)(2,1)S(1)}, u32[]{:S(2)}, u32[]{:S(2)}) collective-permute-start(bf16[32,2048]{1,0:T(8,128)(2,1)S(1)} %get-tuple-element.120), channel_id=1, source_target_pairs={{0,4},{4,8},{8,12},{12,14},{14,10},{10,6},{6,2},{2,0},{1,5},{5,9},... | collective-permute-start | bytes 393224 | tf_op jit(solution)/shard_map/ppermute | solution.py:889
  40.3 2.2 %collective-permute-start.16 = (bf16[32,2048]{1,0:T(8,128)(2,1)S(1)}, bf16[32,2048]{1,0:T(8,128)(2,1)S(1)}, u32[]{:S(2)}, u32[]{:S(2)}) collective-permute-start(bf16[32,2048]{1,0:T(8,128)(2,1)S(1)} %get-tuple-element.131), channel_id=1, source_target_pairs={{0,4},{4,8},{8,12},{12,14},{14,10},{10,6},{6,2},{2,0},{1,5},{5,9},... | collective-permute-start | bytes 393224 | tf_op jit(solution)/shard_map/ppermute | solution.py:889
  43.7 1.6 %collective-permute-done.7.refs_3_.refs_2_.refs_6_ = bf16[32,2048]{1,0:T(8,128)(2,1)S(1)} collective-permute-done((bf16[32,2048]{1,0:T(8,128)(2,1)S(1)}, bf16[32,2048]{1,0:T(8,128)(2,1)S(1)}, u32[]{:S(2)}, u32[]{:S(2)}) %collective-permute-start.7) | collective-permute-done | bytes 131104 | tf_op jit(solution)/shard_map/ppermute | solution.py:892
  45.9 0.9 collective-permute-start.8
  46.8 1.2 collective-permute-start.9
  48.8 1.8 %collective-permute-start.18 = (bf16[32,2048]{1,0:T(8,128)(2,1)S(1)}, bf16[32,2048]{1,0:T(8,128)(2,1)S(1)}, u32[]{:S(2)}, u32[]{:S(2)}) collective-permute-start(bf16[32,2048]{1,0:T(8,128)(2,1)S(1)} %get-tuple-element.133), channel_id=1, source_target_pairs={{0,4},{4,8},{8,12},{12,14},{14,10},{10,6},{6,2},{2,0},{1,5},{5,9},... | collective-permute-start | bytes 393224 | tf_op jit(solution)/shard_map/ppermute | solution.py:889
  50.8 0.8 collective-permute-done.8.refs_1_.refs_3_
  51.6 1.5 %collective-permute-done.9.refs_3_.refs_7_ = bf16[32,2048]{1,0:T(8,128)(2,1)S(1)} collective-permute-done((bf16[32,2048]{1,0:T(8,128)(2,1)S(1)}, bf16[32,2048]{1,0:T(8,128)(2,1)S(1)}, u32[]{:S(2)}, u32[]{:S(2)}) %collective-permute-start.9) | collective-permute-done | bytes 131104 | tf_op jit(solution)/shard_map/ppermute | solution.py:892
  54.3 1.5 %collective-permute-start.11 = (bf16[32,2048]{1,0:T(8,128)(2,1)S(1)}, bf16[32,2048]{1,0:T(8,128)(2,1)S(1)}, u32[]{:S(2)}, u32[]{:S(2)}) collective-permute-start(bf16[32,2048]{1,0:T(8,128)(2,1)S(1)} %get-tuple-element.125), channel_id=1, source_target_pairs={{4,0},{8,4},{12,8},{14,12},{10,14},{6,10},{2,6},{0,2},{5,1},{9,5},... | collective-permute-start | bytes 393224 | tf_op jit(solution)/shard_map/ppermute | solution.py:892
  55.9 1.9 %project.2.refs_10_ = f32[288,896]{1,0:T(8,128)S(1)} custom-call(s32[60]{0:T(128)S(1)} %get-tuple-element.107.tab.refs_0_, bf16[32,2048]{1,0:T(8,128)(2,1)S(1)} %get-tuple-element.140.refs_0_, bf16[32,2048]{1,0:T(8,128)(2,1)S(1)} %collective-permute-done.12.refs_1_.refs_0_, bf16[32,2048]{1,0:T(8,128)(2,1)S(1)} %collective-permute-done.14.refs_1_.refs_0_.refs_2_, ...), custom_call_target="tpu_custom_call" | custom-call | flops 1056964608 | bytes 4849664 | tf_op jit(solution)/shard_map/project/pallas_call | solution.py:504
  57.8 0.9 collective-permute-done.10.refs_4_
  58.7 1.0 collective-permute-done.11.refs_8_
  59.7 2.0 %project.3 = (f32[144,896]{1,0:T(8,128)S(1)}, bf16[144,896]{1,0:T(8,128)(2,1)S(1)}) custom-call(s32[60]{0:T(128)S(1)} %get-tuple-element.107.tab.refs_0_, bf16[32,2048]{1,0:T(8,128)(2,1)S(1)} %get-tuple-element.117.refs_0_, bf16[32,2048]{1,0:T(8,128)(2,1)S(1)} %collective-permute-done.4.refs_1_.refs_0_, ...), custom_call_target="tpu_custom_call" | custom-call | flops 1056964608 | bytes 4849664 | tf_op jit(solution)/shard_map/project/pallas_call | solution.py:514
  61.8 1.5 %collective-permute-done.21.other = bf16[144,896]{1,0:T(8,128)(2,1)S(1)} collective-permute-done((bf16[144,896]{1,0:T(8,128)(2,1)S(1)}, bf16[144,896]{1,0:T(8,128)(2,1)S(1)}, u32[]{:S(2)}, u32[]{:S(2)}) %collective-permute-start.21) | collective-permute-done | bytes 258080 | tf_op jit(solution)/shard_map/ppermute | solution.py:895
  64.2 1.2 collective-permute-start.23
  65.4 1.0 collective-permute-start.22
  66.4 1.7 %expand.5 = (f32[288,576]{1,0:T(8,128)S(1)}, f32[288,576]{1,0:T(8,128)S(1)}, f32[288,1]{1,0:T(8,128)S(1)}) custom-call(s32[60]{0:T(128)S(1)} %get-tuple-element.107.tab.refs_0_, bf16[144,896]{1,0:T(8,128)(2,1)S(1)} %stream.1.refs_0_.refs_1_, bf16[144,896]{1,0:T(8,128)(2,1)S(1)} %collective-permute-done.24.refs_1_, f32[8,1,896]{2,1,0:T(1,128)S(1)} %bitcast.24, ...), custom_call_target="tpu_custom_call" | custom-call | flops 594542592 | bytes 2580480 | tf_op jit(solution)/shard_map/expand/pallas_call | solution.py:661
  68.1 4.6 %collective-permute-done.23.refs_2_.refs_4_.refs_5_ = bf16[144,896]{1,0:T(8,128)(2,1)S(1)} collective-permute-done((bf16[144,896]{1,0:T(8,128)(2,1)S(1)}, bf16[144,896]{1,0:T(8,128)(2,1)S(1)}, u32[]{:S(2)}, u32[]{:S(2)}) %collective-permute-start.23) | collective-permute-done | bytes 258080 | tf_op jit(solution)/shard_map/ppermute | solution.py:892
  72.7 0.8 collective-permute-done.22.refs_0_.refs_2_.refs_3_
  74.0 1.0 collective-permute-start.25
  75.0 1.1 collective-permute-start.26
  76.0 2.9 %expand.6 = (f32[288,576]{1,0:T(8,128)S(1)}, f32[288,576]{1,0:T(8,128)S(1)}, f32[288,1]{1,0:T(8,128)S(1)}) custom-call(s32[60]{0:T(128)S(1)} %get-tuple-element.107.tab.refs_0_, bf16[144,896]{1,0:T(8,128)(2,1)S(1)} %collective-permute-done.22.refs_0_.refs_2_.refs_3_, bf16[144,896]{1,0:T(8,128)(2,1)S(1)} %collective-permute-done.27.refs_1_, ...), custom_call_target="tpu_custom_call" | custom-call | flops 1189085184 | bytes 5160960 | tf_op jit(solution)/shard_map/expand/pallas_call | solution.py:661
  78.9 3.2 %collective-permute-done.25.refs_0_.refs_6_.refs_7_ = bf16[144,896]{1,0:T(8,128)(2,1)S(1)} collective-permute-done((bf16[144,896]{1,0:T(8,128)(2,1)S(1)}, bf16[144,896]{1,0:T(8,128)(2,1)S(1)}, u32[]{:S(2)}, u32[]{:S(2)}) %collective-permute-start.25) | collective-permute-done | bytes 258080 | tf_op jit(solution)/shard_map/ppermute | solution.py:889
  83.3 1.7 %collective-permute-start.29 = (bf16[144,896]{1,0:T(8,128)(2,1)S(1)}, bf16[144,896]{1,0:T(8,128)(2,1)S(1)}, u32[]{:S(2)}, u32[]{:S(2)}) collective-permute-start(bf16[144,896]{1,0:T(8,128)(2,1)S(1)} %collective-permute-done.25.refs_0_.refs_6_.refs_7_), channel_id=1, source_target_pairs={{0,4},{4,8},{8,12},{12,14},{14,10},{10,6},{6,2},{2,0},{1,5},{5,9},... | collective-permute-start | bytes 774152 | tf_op jit(solution)/shard_map/ppermute | solution.py:889
  85.4 2.9 %expand.7 = (f32[288,576]{1,0:T(8,128)S(1)}, f32[288,576]{1,0:T(8,128)S(1)}, f32[288,1]{1,0:T(8,128)S(1)}) custom-call(s32[60]{0:T(128)S(1)} %get-tuple-element.107.tab.refs_0_, bf16[144,896]{1,0:T(8,128)(2,1)S(1)} %collective-permute-done.25.refs_0_.refs_6_.refs_7_, bf16[144,896]{1,0:T(8,128)(2,1)S(1)} %collective-permute-done.31.refs_1_, ...), custom_call_target="tpu_custom_call" | custom-call | flops 1189085184 | bytes 5160960 | tf_op jit(solution)/shard_map/expand/pallas_call | solution.py:661
  88.2 3.2 %collective-permute-done.29.refs_0_.refs_10_.refs_11_ = bf16[144,896]{1,0:T(8,128)(2,1)S(1)} collective-permute-done((bf16[144,896]{1,0:T(8,128)(2,1)S(1)}, bf16[144,896]{1,0:T(8,128)(2,1)S(1)}, u32[]{:S(2)}, u32[]{:S(2)}) %collective-permute-start.29) | collective-permute-done | bytes 258080 | tf_op jit(solution)/shard_map/ppermute | solution.py:889
  91.5 1.5 %collective-permute-done.30.refs_2_.refs_12_.refs_13_ = bf16[144,896]{1,0:T(8,128)(2,1)S(1)} collective-permute-done((bf16[144,896]{1,0:T(8,128)(2,1)S(1)}, bf16[144,896]{1,0:T(8,128)(2,1)S(1)}, u32[]{:S(2)}, u32[]{:S(2)}) %collective-permute-start.30) | collective-permute-done | bytes 258080 | tf_op jit(solution)/shard_map/ppermute | solution.py:892
  93.5 1.2 collective-permute-start.33
  94.7 0.9 collective-permute-start.34
  95.6 2.9 %expand.8 = (f32[288,576]{1,0:T(8,128)S(1)}, f32[288,576]{1,0:T(8,128)S(1)}, f32[288,1]{1,0:T(8,128)S(1)}) custom-call(s32[60]{0:T(128)S(1)} %get-tuple-element.107.tab.refs_0_, bf16[144,896]{1,0:T(8,128)(2,1)S(1)} %collective-permute-done.29.refs_0_.refs_10_.refs_11_, bf16[144,896]{1,0:T(8,128)(2,1)S(1)} %collective-permute-done.35.refs_1_, ...), custom_call_target="tpu_custom_call" | custom-call | flops 1189085184 | bytes 5160960 | tf_op jit(solution)/shard_map/expand/pallas_call | solution.py:661
  98.5 1.0 collective-permute-done.34.refs_1_
  100.1 1.0 collective-permute-done.38.refs_3_
  101.1 1.8 %expand.9.hidden = bf16[288,576]{1,0:T(8,128)(2,1)S(1)} custom-call(s32[60]{0:T(128)S(1)} %get-tuple-element.107.tab.refs_0_, bf16[80,896]{1,0:T(8,128)(2,1)S(1)} %collective-permute-done.33.refs_0_, bf16[64,896]{1,0:T(8,128)(2,1)S(1)} %collective-permute-done.34.refs_1_, bf16[80,896]{1,0:T(8,128)(2,1)S(1)} %collective-permute-done.37.refs_2_, ...), custom_call_target="tpu_custom_call" | custom-call | flops 594542592 | bytes 2580480 | tf_op jit(solution)/shard_map/expand/pallas_call | solution.py:661
  102.9 2.1 %contract.3 = (bf16[144,3584]{1,0:T(8,128)(2,1)S(1)}, bf16[144,3584]{1,0:T(8,128)(2,1)S(1)}) custom-call(bf16[288,576]{1,0:T(8,128)(2,1)S(1)} %expand.9.hidden, bf16[576,7168]{1,0:T(8,128)(2,1)S(1)} %bitcast.21), custom_call_target="tpu_custom_call" | custom-call | flops 1189085184 | bytes 6193152 | tf_op jit(solution)/shard_map/contract/pallas_call | solution.py:727
  105.4 2.1 %contract.2 = (bf16[144,3584]{1,0:T(8,128)(2,1)S(1)}, bf16[144,3584]{1,0:T(8,128)(2,1)S(1)}) custom-call(bf16[288,576]{1,0:T(8,128)(2,1)S(1)} %expand.9.hidden, bf16[576,7168]{1,0:T(8,128)(2,1)S(1)} %bitcast.21), custom_call_target="tpu_custom_call" | custom-call | flops 1189085184 | bytes 6193152 | tf_op jit(solution)/shard_map/contract/pallas_call | solution.py:727
  108.4 0.8 collective-permute-start.49
  109.2 1.2 collective-permute-start.50
  111.1 0.8 collective-permute-start.40
  111.9 1.2 collective-permute-start.41
  115.5 1.6 %collective-permute-start.52 = (bf16[16,3584]{1,0:T(8,128)(2,1)S(1)}, bf16[16,3584]{1,0:T(8,128)(2,1)S(1)}, u32[]{:S(2)}, u32[]{:S(2)}) collective-permute-start(bf16[16,3584]{1,0:T(8,128)(2,1)S(1)} %get-tuple-element.201), channel_id=1, source_target_pairs={{4,0},{8,4},{12,8},{14,12},{10,14},{6,10},{2,6},{0,2},{5,1},{9,5},... | collective-permute-start | bytes 344072 | tf_op jit(solution)/shard_map/ppermute | solution.py:892
  118.2 1.6 %collective-permute-start.43 = (bf16[16,3584]{1,0:T(8,128)(2,1)S(1)}, bf16[16,3584]{1,0:T(8,128)(2,1)S(1)}, u32[]{:S(2)}, u32[]{:S(2)}) collective-permute-start(bf16[16,3584]{1,0:T(8,128)(2,1)S(1)} %get-tuple-element.190), channel_id=1, source_target_pairs={{4,0},{8,4},{12,8},{14,12},{10,14},{6,10},{2,6},{0,2},{5,1},{9,5},... | collective-permute-start | bytes 344072 | tf_op jit(solution)/shard_map/ppermute | solution.py:892
  119.8 0.9 collective-permute-done.51.refs_1_.refs_0_
  122.3 1.8 %collective-permute-start.54 = (bf16[16,3584]{1,0:T(8,128)(2,1)S(1)}, bf16[16,3584]{1,0:T(8,128)(2,1)S(1)}, u32[]{:S(2)}, u32[]{:S(2)}) collective-permute-start(bf16[16,3584]{1,0:T(8,128)(2,1)S(1)} %get-tuple-element.203), channel_id=1, source_target_pairs={{4,0},{8,4},{12,8},{14,12},{10,14},{6,10},{2,6},{0,2},{5,1},{9,5},... | collective-permute-start | bytes 344072 | tf_op jit(solution)/shard_map/ppermute | solution.py:892
  125.0 1.8 %collective-permute-start.45 = (bf16[16,3584]{1,0:T(8,128)(2,1)S(1)}, bf16[16,3584]{1,0:T(8,128)(2,1)S(1)}, u32[]{:S(2)}, u32[]{:S(2)}) collective-permute-start(bf16[16,3584]{1,0:T(8,128)(2,1)S(1)} %get-tuple-element.192), channel_id=1, source_target_pairs={{4,0},{8,4},{12,8},{14,12},{10,14},{6,10},{2,6},{0,2},{5,1},{9,5},... | collective-permute-start | bytes 344072 | tf_op jit(solution)/shard_map/ppermute | solution.py:892
  128.1 1.1 collective-permute-start.55
  129.2 1.0 collective-permute-start.56
  130.9 1.1 collective-permute-start.46
  131.9 1.0 collective-permute-start.47
  134.0 0.7 close.3
  134.8 0.9 collective-permute-done.46.f_last
  135.7 1.0 collective-permute-done.47.b_last
  137.5 1.3 collective-permute-done.57.refs_2_
  138.8 1.4 finish.1
  (124 shorter events, 26.0 us)
Async XLA Ops:
  3.7 18.8 %copy-start.3 = (bf16[576,64]{0,1:T(8,128)(2,1)S(1)}, bf16[576,64]{0,1:T(8,128)(2,1)}, u32[]{:S(2)}) copy-start(bf16[576,64]{0,1:T(8,128)(2,1)} %param.16) | copy-start | bytes 221188
  11.9 43.9 %slice-start.6 = ((s8[7340032]{0:T(1024)(128)(4,1)}), s8[4194304]{0:T(1024)(128)(4,1)S(1)}, s32[]{:S(2)}) async-start(s8[7340032]{0:T(1024)(128)(4,1)} %bitcast.22), calls=%async_computation.6 | async-start | bytes 8388608
  12.6 8.0 %collective-permute-start = (bf16[64,896]{1,0:T(8,128)(2,1)S(1)}, bf16[64,896]{1,0:T(8,128)(2,1)S(1)}, u32[]{:S(2)}, u32[]{:S(2)}) collective-permute-start(bf16[64,896]{1,0:T(8,128)(2,1)S(1)} %get-tuple-element.135.own), channel_id=1, source_target_pairs={{1,9},{3,11},{5,13},{7,15},{9,1},{11,3},{13,5},{15,7},{17,25},{19,... | collective-permute-start | bytes 344072 | tf_op jit(solution)/shard_map/ppermute | solution.py:911
  13.4 15.1 %collective-permute-start.1 = (bf16[64,896]{1,0:T(8,128)(2,1)S(1)}, bf16[64,896]{1,0:T(8,128)(2,1)S(1)}, u32[]{:S(2)}, u32[]{:S(2)}) collective-permute-start(bf16[64,896]{1,0:T(8,128)(2,1)S(1)} %get-tuple-element.110), channel_id=1, source_target_pairs={{0,2},{1,11},{2,4},{3,13},{4,6},{5,15},{6,8},{7,1},{8,10},{9,3},{1... | collective-permute-start | bytes 344072 | tf_op jit(solution)/shard_map/ppermute | solution.py:911
  16.4 12.1 %collective-permute-start.2 = (bf16[64,896]{1,0:T(8,128)(2,1)S(1)}, bf16[64,896]{1,0:T(8,128)(2,1)S(1)}, u32[]{:S(2)}, u32[]{:S(2)}) collective-permute-start(bf16[64,896]{1,0:T(8,128)(2,1)S(1)} %get-tuple-element.111), channel_id=1, source_target_pairs={{0,4},{1,13},{2,6},{3,15},{4,8},{5,1},{6,10},{7,3},{8,12},{9,5},{1... | collective-permute-start | bytes 344072 | tf_op jit(solution)/shard_map/ppermute | solution.py:911
  18.0 10.6 %collective-permute-start.3 = (bf16[64,896]{1,0:T(8,128)(2,1)S(1)}, bf16[64,896]{1,0:T(8,128)(2,1)S(1)}, u32[]{:S(2)}, u32[]{:S(2)}) collective-permute-start(bf16[64,896]{1,0:T(8,128)(2,1)S(1)} %get-tuple-element.112), channel_id=1, source_target_pairs={{0,6},{1,15},{2,8},{3,1},{4,10},{5,3},{6,12},{7,5},{8,14},{9,7},{1... | collective-permute-start | bytes 344072 | tf_op jit(solution)/shard_map/ppermute | solution.py:911
  20.5 10.1 %collective-permute-start.12 = (bf16[32,2048]{1,0:T(8,128)(2,1)S(1)}, bf16[32,2048]{1,0:T(8,128)(2,1)S(1)}, u32[]{:S(2)}, u32[]{:S(2)}) collective-permute-start(bf16[32,2048]{1,0:T(8,128)(2,1)S(1)} %get-tuple-element.127), channel_id=1, source_target_pairs={{0,4},{4,8},{8,12},{12,14},{14,10},{10,6},{6,2},{2,0},{1,5},{5,9},... | collective-permute-start | bytes 393224 | tf_op jit(solution)/shard_map/ppermute | solution.py:889
  20.6 10.0 %collective-permute-start.13 = (bf16[32,2048]{1,0:T(8,128)(2,1)S(1)}, bf16[32,2048]{1,0:T(8,128)(2,1)S(1)}, u32[]{:S(2)}, u32[]{:S(2)}) collective-permute-start(bf16[32,2048]{1,0:T(8,128)(2,1)S(1)} %get-tuple-element.140.refs_0_), channel_id=1, source_target_pairs={{4,0},{8,4},{12,8},{14,12},{10,14},{6,10},{2,6},{0,2},{5,1},{9,5},... | collective-permute-start | bytes 393224 | tf_op jit(solution)/shard_map/ppermute | solution.py:892
  22.5 33.3 %slice-start.7 = ((s8[7340032]{0:T(1024)(128)(4,1)}), s8[3145728]{0:T(1024)(128)(4,1)S(1)}, s32[]{:S(2)}) async-start(s8[7340032]{0:T(1024)(128)(4,1)} %bitcast.22), calls=%async_computation.7 | async-start | bytes 6291456
  28.5 5.0 %collective-permute-start.4 = (bf16[32,2048]{1,0:T(8,128)(2,1)S(1)}, bf16[32,2048]{1,0:T(8,128)(2,1)S(1)}, u32[]{:S(2)}, u32[]{:S(2)}) collective-permute-start(bf16[32,2048]{1,0:T(8,128)(2,1)S(1)} %get-tuple-element.118), channel_id=1, source_target_pairs={{0,4},{4,8},{8,12},{12,14},{14,10},{10,6},{6,2},{2,0},{1,5},{5,9},... | collective-permute-start | bytes 393224 | tf_op jit(solution)/shard_map/ppermute | solution.py:889
  29.9 5.0 %collective-permute-start.5 = (bf16[32,2048]{1,0:T(8,128)(2,1)S(1)}, bf16[32,2048]{1,0:T(8,128)(2,1)S(1)}, u32[]{:S(2)}, u32[]{:S(2)}) collective-permute-start(bf16[32,2048]{1,0:T(8,128)(2,1)S(1)} %get-tuple-element.117.refs_0_), channel_id=1, source_target_pairs={{4,0},{8,4},{12,8},{14,12},{10,14},{6,10},{2,6},{0,2},{5,1},{9,5},... | collective-permute-start | bytes 393224 | tf_op jit(solution)/shard_map/ppermute | solution.py:892
  31.2 7.9 %collective-permute-start.14 = (bf16[32,2048]{1,0:T(8,128)(2,1)S(1)}, bf16[32,2048]{1,0:T(8,128)(2,1)S(1)}, u32[]{:S(2)}, u32[]{:S(2)}) collective-permute-start(bf16[32,2048]{1,0:T(8,128)(2,1)S(1)} %get-tuple-element.129), channel_id=1, source_target_pairs={{0,4},{4,8},{8,12},{12,14},{14,10},{10,6},{6,2},{2,0},{1,5},{5,9},... | collective-permute-start | bytes 393224 | tf_op jit(solution)/shard_map/ppermute | solution.py:889
  33.3 6.4 %collective-permute-start.15 = (bf16[32,2048]{1,0:T(8,128)(2,1)S(1)}, bf16[32,2048]{1,0:T(8,128)(2,1)S(1)}, u32[]{:S(2)}, u32[]{:S(2)}) collective-permute-start(bf16[32,2048]{1,0:T(8,128)(2,1)S(1)} %get-tuple-element.130), channel_id=1, source_target_pairs={{4,0},{8,4},{12,8},{14,12},{10,14},{6,10},{2,6},{0,2},{5,1},{9,5},... | collective-permute-start | bytes 393224 | tf_op jit(solution)/shard_map/ppermute | solution.py:892
  35.5 8.2 %collective-permute-start.6 = (bf16[32,2048]{1,0:T(8,128)(2,1)S(1)}, bf16[32,2048]{1,0:T(8,128)(2,1)S(1)}, u32[]{:S(2)}, u32[]{:S(2)}) collective-permute-start(bf16[32,2048]{1,0:T(8,128)(2,1)S(1)} %get-tuple-element.120), channel_id=1, source_target_pairs={{0,4},{4,8},{8,12},{12,14},{14,10},{10,6},{6,2},{2,0},{1,5},{5,9},... | collective-permute-start | bytes 393224 | tf_op jit(solution)/shard_map/ppermute | solution.py:889
  39.0 6.2 %collective-permute-start.7 = (bf16[32,2048]{1,0:T(8,128)(2,1)S(1)}, bf16[32,2048]{1,0:T(8,128)(2,1)S(1)}, u32[]{:S(2)}, u32[]{:S(2)}) collective-permute-start(bf16[32,2048]{1,0:T(8,128)(2,1)S(1)} %get-tuple-element.121), channel_id=1, source_target_pairs={{4,0},{8,4},{12,8},{14,12},{10,14},{6,10},{2,6},{0,2},{5,1},{9,5},... | collective-permute-start | bytes 393224 | tf_op jit(solution)/shard_map/ppermute | solution.py:892
  40.3 7.6 %collective-permute-start.16 = (bf16[32,2048]{1,0:T(8,128)(2,1)S(1)}, bf16[32,2048]{1,0:T(8,128)(2,1)S(1)}, u32[]{:S(2)}, u32[]{:S(2)}) collective-permute-start(bf16[32,2048]{1,0:T(8,128)(2,1)S(1)} %get-tuple-element.131), channel_id=1, source_target_pairs={{0,4},{4,8},{8,12},{12,14},{14,10},{10,6},{6,2},{2,0},{1,5},{5,9},... | collective-permute-start | bytes 393224 | tf_op jit(solution)/shard_map/ppermute | solution.py:889
  42.5 5.7 %collective-permute-start.17 = (bf16[32,2048]{1,0:T(8,128)(2,1)S(1)}, bf16[32,2048]{1,0:T(8,128)(2,1)S(1)}, u32[]{:S(2)}, u32[]{:S(2)}) collective-permute-start(bf16[32,2048]{1,0:T(8,128)(2,1)S(1)} %get-tuple-element.132), channel_id=1, source_target_pairs={{4,0},{8,4},{12,8},{14,12},{10,14},{6,10},{2,6},{0,2},{5,1},{9,5},... | collective-permute-start | bytes 393224 | tf_op jit(solution)/shard_map/ppermute | solution.py:892
  42.5 23.9 %slice-start.2 = ((s8[8257536]{0:T(1024)(128)(4,1)}), s8[4194304]{0:T(1024)(128)(4,1)S(1)}, s32[]{:S(2)}) async-start(s8[8257536]{0:T(1024)(128)(4,1)} %bitcast.13), calls=%async_computation.2 | async-start | bytes 8388608
  43.1 12.7 %collective-permute-start.20 = (bf16[128,896]{1,0:T(8,128)(2,1)S(1)}, bf16[128,896]{1,0:T(8,128)(2,1)S(1)}, u32[]{:S(2)}, u32[]{:S(2)}) collective-permute-start(bf16[128,896]{1,0:T(8,128)(2,1)S(1)} %share.1), channel_id=1, source_target_pairs={{0,1},{1,0},{2,3},{3,2},{4,5},{5,4},{6,7},{7,6},{8,9},{9,8},{10,11... | collective-permute-start | bytes 688136 | tf_op jit(solution)/shard_map/ppermute | solution.py:895
  45.9 5.8 %collective-permute-start.8 = (bf16[32,2048]{1,0:T(8,128)(2,1)S(1)}, bf16[32,2048]{1,0:T(8,128)(2,1)S(1)}, u32[]{:S(2)}, u32[]{:S(2)}) collective-permute-start(bf16[32,2048]{1,0:T(8,128)(2,1)S(1)} %get-tuple-element.122), channel_id=1, source_target_pairs={{0,4},{4,8},{8,12},{12,14},{14,10},{10,6},{6,2},{2,0},{1,5},{5,9},... | collective-permute-start | bytes 393224 | tf_op jit(solution)/shard_map/ppermute | solution.py:889
  46.8 6.4 %collective-permute-start.9 = (bf16[32,2048]{1,0:T(8,128)(2,1)S(1)}, bf16[32,2048]{1,0:T(8,128)(2,1)S(1)}, u32[]{:S(2)}, u32[]{:S(2)}) collective-permute-start(bf16[32,2048]{1,0:T(8,128)(2,1)S(1)} %get-tuple-element.123), channel_id=1, source_target_pairs={{4,0},{8,4},{12,8},{14,12},{10,14},{6,10},{2,6},{0,2},{5,1},{9,5},... | collective-permute-start | bytes 393224 | tf_op jit(solution)/shard_map/ppermute | solution.py:892
  48.8 7.0 %collective-permute-start.18 = (bf16[32,2048]{1,0:T(8,128)(2,1)S(1)}, bf16[32,2048]{1,0:T(8,128)(2,1)S(1)}, u32[]{:S(2)}, u32[]{:S(2)}) collective-permute-start(bf16[32,2048]{1,0:T(8,128)(2,1)S(1)} %get-tuple-element.133), channel_id=1, source_target_pairs={{0,4},{4,8},{8,12},{12,14},{14,10},{10,6},{6,2},{2,0},{1,5},{5,9},... | collective-permute-start | bytes 393224 | tf_op jit(solution)/shard_map/ppermute | solution.py:889
  50.6 5.2 %collective-permute-start.19 = (bf16[32,2048]{1,0:T(8,128)(2,1)S(1)}, bf16[32,2048]{1,0:T(8,128)(2,1)S(1)}, u32[]{:S(2)}, u32[]{:S(2)}) collective-permute-start(bf16[32,2048]{1,0:T(8,128)(2,1)S(1)} %get-tuple-element.134), channel_id=1, source_target_pairs={{4,0},{8,4},{12,8},{14,12},{10,14},{6,10},{2,6},{0,2},{5,1},{9,5},... | collective-permute-start | bytes 393224 | tf_op jit(solution)/shard_map/ppermute | solution.py:892
  53.7 5.0 %collective-permute-start.10 = (bf16[32,2048]{1,0:T(8,128)(2,1)S(1)}, bf16[32,2048]{1,0:T(8,128)(2,1)S(1)}, u32[]{:S(2)}, u32[]{:S(2)}) collective-permute-start(bf16[32,2048]{1,0:T(8,128)(2,1)S(1)} %get-tuple-element.124), channel_id=1, source_target_pairs={{0,4},{4,8},{8,12},{12,14},{14,10},{10,6},{6,2},{2,0},{1,5},{5,9},... | collective-permute-start | bytes 393224 | tf_op jit(solution)/shard_map/ppermute | solution.py:889
  54.3 12.1 %slice-start.3 = ((s8[8257536]{0:T(1024)(128)(4,1)}), s8[4063232]{0:T(1024)(128)(4,1)S(1)}, s32[]{:S(2)}) async-start(s8[8257536]{0:T(1024)(128)(4,1)} %bitcast.13), calls=%async_computation.3 | async-start | bytes 8126464
  54.3 5.4 %collective-permute-start.11 = (bf16[32,2048]{1,0:T(8,128)(2,1)S(1)}, bf16[32,2048]{1,0:T(8,128)(2,1)S(1)}, u32[]{:S(2)}, u32[]{:S(2)}) collective-permute-start(bf16[32,2048]{1,0:T(8,128)(2,1)S(1)} %get-tuple-element.125), channel_id=1, source_target_pairs={{4,0},{8,4},{12,8},{14,12},{10,14},{6,10},{2,6},{0,2},{5,1},{9,5},... | collective-permute-start | bytes 393224 | tf_op jit(solution)/shard_map/ppermute | solution.py:892
  61.7 1.6 %collective-permute-start.21 = (bf16[144,896]{1,0:T(8,128)(2,1)S(1)}, bf16[144,896]{1,0:T(8,128)(2,1)S(1)}, u32[]{:S(2)}, u32[]{:S(2)}) collective-permute-start(bf16[144,896]{1,0:T(8,128)(2,1)S(1)} %get-tuple-element.151), channel_id=1, source_target_pairs={{0,1},{1,0},{2,3},{3,2},{4,5},{5,4},{6,7},{7,6},{8,9},{9,8},{10,11... | collective-permute-start | bytes 774152 | tf_op jit(solution)/shard_map/ppermute | solution.py:895
  64.0 2.3 %collective-permute-start.24 = (bf16[144,896]{1,0:T(8,128)(2,1)S(1)}, bf16[144,896]{1,0:T(8,128)(2,1)S(1)}, u32[]{:S(2)}, u32[]{:S(2)}) collective-permute-start(bf16[144,896]{1,0:T(8,128)(2,1)S(1)} %stream.1.refs_0_.refs_1_), channel_id=1, source_target_pairs={{0,1},{1,0},{2,3},{3,2},{4,5},{5,4},{6,7},{7,6},{8,9},{9,8},{10,11... | collective-permute-start | bytes 774152 | tf_op jit(solution)/shard_map/ppermute | solution.py:895
  64.2 8.5 %collective-permute-start.23 = (bf16[144,896]{1,0:T(8,128)(2,1)S(1)}, bf16[144,896]{1,0:T(8,128)(2,1)S(1)}, u32[]{:S(2)}, u32[]{:S(2)}) collective-permute-start(bf16[144,896]{1,0:T(8,128)(2,1)S(1)} %stream.1.refs_0_.refs_1_), channel_id=1, source_target_pairs={{4,0},{8,4},{12,8},{14,12},{10,14},{6,10},{2,6},{0,2},{5,1},{9,5},... | collective-permute-start | bytes 774152 | tf_op jit(solution)/shard_map/ppermute | solution.py:892
  65.4 8.1 %collective-permute-start.22 = (bf16[144,896]{1,0:T(8,128)(2,1)S(1)}, bf16[144,896]{1,0:T(8,128)(2,1)S(1)}, u32[]{:S(2)}, u32[]{:S(2)}) collective-permute-start(bf16[144,896]{1,0:T(8,128)(2,1)S(1)} %stream.1.refs_0_.refs_1_), channel_id=1, source_target_pairs={{0,4},{4,8},{8,12},{12,14},{14,10},{10,6},{6,2},{2,0},{1,5},{5,9},... | collective-permute-start | bytes 774152 | tf_op jit(solution)/shard_map/ppermute | solution.py:889
  73.5 2.5 %collective-permute-start.27 = (bf16[144,896]{1,0:T(8,128)(2,1)S(1)}, bf16[144,896]{1,0:T(8,128)(2,1)S(1)}, u32[]{:S(2)}, u32[]{:S(2)}) collective-permute-start(bf16[144,896]{1,0:T(8,128)(2,1)S(1)} %collective-permute-done.22.refs_0_.refs_2_.refs_3_), channel_id=1, source_target_pairs={{0,1},{1,0},{2,3},{3,2},{4,5},{5,4},{6,7},{7,6},{8,9},{9,8},{10,11... | collective-permute-start | bytes 774152 | tf_op jit(solution)/shard_map/ppermute | solution.py:895
  73.5 2.5 %collective-permute-start.28 = (bf16[144,896]{1,0:T(8,128)(2,1)S(1)}, bf16[144,896]{1,0:T(8,128)(2,1)S(1)}, u32[]{:S(2)}, u32[]{:S(2)}) collective-permute-start(bf16[144,896]{1,0:T(8,128)(2,1)S(1)} %collective-permute-done.23.refs_2_.refs_4_.refs_5_), channel_id=1, source_target_pairs={{0,1},{1,0},{2,3},{3,2},{4,5},{5,4},{6,7},{7,6},{8,9},{9,8},{10,11... | collective-permute-start | bytes 774152 | tf_op jit(solution)/shard_map/ppermute | solution.py:895
  74.0 8.1 %collective-permute-start.25 = (bf16[144,896]{1,0:T(8,128)(2,1)S(1)}, bf16[144,896]{1,0:T(8,128)(2,1)S(1)}, u32[]{:S(2)}, u32[]{:S(2)}) collective-permute-start(bf16[144,896]{1,0:T(8,128)(2,1)S(1)} %collective-permute-done.22.refs_0_.refs_2_.refs_3_), channel_id=1, source_target_pairs={{0,4},{4,8},{8,12},{12,14},{14,10},{10,6},{6,2},{2,0},{1,5},{5,9},... | collective-permute-start | bytes 774152 | tf_op jit(solution)/shard_map/ppermute | solution.py:889
  75.0 7.8 %collective-permute-start.26 = (bf16[144,896]{1,0:T(8,128)(2,1)S(1)}, bf16[144,896]{1,0:T(8,128)(2,1)S(1)}, u32[]{:S(2)}, u32[]{:S(2)}) collective-permute-start(bf16[144,896]{1,0:T(8,128)(2,1)S(1)} %collective-permute-done.23.refs_2_.refs_4_.refs_5_), channel_id=1, source_target_pairs={{4,0},{8,4},{12,8},{14,12},{10,14},{6,10},{2,6},{0,2},{5,1},{9,5},... | collective-permute-start | bytes 774152 | tf_op jit(solution)/shard_map/ppermute | solution.py:892
  82.8 2.5 %collective-permute-start.31 = (bf16[144,896]{1,0:T(8,128)(2,1)S(1)}, bf16[144,896]{1,0:T(8,128)(2,1)S(1)}, u32[]{:S(2)}, u32[]{:S(2)}) collective-permute-start(bf16[144,896]{1,0:T(8,128)(2,1)S(1)} %collective-permute-done.25.refs_0_.refs_6_.refs_7_), channel_id=1, source_target_pairs={{0,1},{1,0},{2,3},{3,2},{4,5},{5,4},{6,7},{7,6},{8,9},{9,8},{10,11... | collective-permute-start | bytes 774152 | tf_op jit(solution)/shard_map/ppermute | solution.py:895
  82.8 2.5 %collective-permute-start.32 = (bf16[144,896]{1,0:T(8,128)(2,1)S(1)}, bf16[144,896]{1,0:T(8,128)(2,1)S(1)}, u32[]{:S(2)}, u32[]{:S(2)}) collective-permute-start(bf16[144,896]{1,0:T(8,128)(2,1)S(1)} %collective-permute-done.26.refs_2_.refs_8_.refs_9_), channel_id=1, source_target_pairs={{0,1},{1,0},{2,3},{3,2},{4,5},{5,4},{6,7},{7,6},{8,9},{9,8},{10,11... | collective-permute-start | bytes 774152 | tf_op jit(solution)/shard_map/ppermute | solution.py:895
  83.3 8.1 %collective-permute-start.29 = (bf16[144,896]{1,0:T(8,128)(2,1)S(1)}, bf16[144,896]{1,0:T(8,128)(2,1)S(1)}, u32[]{:S(2)}, u32[]{:S(2)}) collective-permute-start(bf16[144,896]{1,0:T(8,128)(2,1)S(1)} %collective-permute-done.25.refs_0_.refs_6_.refs_7_), channel_id=1, source_target_pairs={{0,4},{4,8},{8,12},{12,14},{14,10},{10,6},{6,2},{2,0},{1,5},{5,9},... | collective-permute-start | bytes 774152 | tf_op jit(solution)/shard_map/ppermute | solution.py:889
  85.1 7.8 %collective-permute-start.30 = (bf16[144,896]{1,0:T(8,128)(2,1)S(1)}, bf16[144,896]{1,0:T(8,128)(2,1)S(1)}, u32[]{:S(2)}, u32[]{:S(2)}) collective-permute-start(bf16[144,896]{1,0:T(8,128)(2,1)S(1)} %collective-permute-done.26.refs_2_.refs_8_.refs_9_), channel_id=1, source_target_pairs={{4,0},{8,4},{12,8},{14,12},{10,14},{6,10},{2,6},{0,2},{5,1},{9,5},... | collective-permute-start | bytes 774152 | tf_op jit(solution)/shard_map/ppermute | solution.py:892
  92.9 2.7 %collective-permute-start.35 = (bf16[144,896]{1,0:T(8,128)(2,1)S(1)}, bf16[144,896]{1,0:T(8,128)(2,1)S(1)}, u32[]{:S(2)}, u32[]{:S(2)}) collective-permute-start(bf16[144,896]{1,0:T(8,128)(2,1)S(1)} %collective-permute-done.29.refs_0_.refs_10_.refs_11_), channel_id=1, source_target_pairs={{0,1},{1,0},{2,3},{3,2},{4,5},{5,4},{6,7},{7,6},{8,9},{9,8},{10,11... | collective-permute-start | bytes 774152 | tf_op jit(solution)/shard_map/ppermute | solution.py:895
  92.9 2.7 %collective-permute-start.36 = (bf16[144,896]{1,0:T(8,128)(2,1)S(1)}, bf16[144,896]{1,0:T(8,128)(2,1)S(1)}, u32[]{:S(2)}, u32[]{:S(2)}) collective-permute-start(bf16[144,896]{1,0:T(8,128)(2,1)S(1)} %collective-permute-done.30.refs_2_.refs_12_.refs_13_), channel_id=1, source_target_pairs={{0,1},{1,0},{2,3},{3,2},{4,5},{5,4},{6,7},{7,6},{8,9},{9,8},{10,11... | collective-permute-start | bytes 774152 | tf_op jit(solution)/shard_map/ppermute | solution.py:895
  93.5 6.1 %collective-permute-start.33 = (bf16[80,896]{1,0:T(8,128)(2,1)S(1)}, bf16[80,896]{1,0:T(8,128)(2,1)S(1)}, u32[]{:S(2)}, u32[]{:S(2)}) collective-permute-start(bf16[80,896]{1,0:T(8,128)(2,1)S(1)} %slice.6), channel_id=1, source_target_pairs={{0,4},{4,8},{8,12},{12,14},{14,10},{10,6},{6,2},{2,0},{1,5},{5,9},... | collective-permute-start | bytes 430088 | tf_op jit(solution)/shard_map/ppermute | solution.py:889
  94.7 4.8 %collective-permute-start.34 = (bf16[64,896]{1,0:T(8,128)(2,1)S(1)}, bf16[64,896]{1,0:T(8,128)(2,1)S(1)}, u32[]{:S(2)}, u32[]{:S(2)}) collective-permute-start(bf16[64,896]{1,0:T(8,128)(2,1)S(1)} %slice.7), channel_id=1, source_target_pairs={{4,0},{8,4},{12,8},{14,12},{10,14},{6,10},{2,6},{0,2},{5,1},{9,5},... | collective-permute-start | bytes 344072 | tf_op jit(solution)/shard_map/ppermute | solution.py:892
  99.5 1.6 %collective-permute-start.37 = (bf16[80,896]{1,0:T(8,128)(2,1)S(1)}, bf16[80,896]{1,0:T(8,128)(2,1)S(1)}, u32[]{:S(2)}, u32[]{:S(2)}) collective-permute-start(bf16[80,896]{1,0:T(8,128)(2,1)S(1)} %collective-permute-done.33.refs_0_), channel_id=1, source_target_pairs={{0,1},{1,0},{2,3},{3,2},{4,5},{5,4},{6,7},{7,6},{8,9},{9,8},{10,11... | collective-permute-start | bytes 430088 | tf_op jit(solution)/shard_map/ppermute | solution.py:895
  99.6 1.5 %collective-permute-start.38 = (bf16[64,896]{1,0:T(8,128)(2,1)S(1)}, bf16[64,896]{1,0:T(8,128)(2,1)S(1)}, u32[]{:S(2)}, u32[]{:S(2)}) collective-permute-start(bf16[64,896]{1,0:T(8,128)(2,1)S(1)} %collective-permute-done.34.refs_1_), channel_id=1, source_target_pairs={{0,1},{1,0},{2,3},{3,2},{4,5},{5,4},{6,7},{7,6},{8,9},{9,8},{10,11... | collective-permute-start | bytes 344072 | tf_op jit(solution)/shard_map/ppermute | solution.py:895
  105.0 2.7 %collective-permute-start.48 = (bf16[144,3584]{1,0:T(8,128)(2,1)S(1)}, bf16[144,3584]{1,0:T(8,128)(2,1)S(1)}, u32[]{:S(2)}, u32[]{:S(2)}) collective-permute-start(bf16[144,3584]{1,0:T(8,128)(2,1)S(1)} %get-tuple-element.197), channel_id=1, source_target_pairs={{0,1},{1,0},{2,3},{3,2},{4,5},{5,4},{6,7},{7,6},{8,9},{9,8},{10,11... | collective-permute-start | bytes 3096584 | tf_op jit(solution)/shard_map/ppermute | solution.py:895
  107.5 3.0 %collective-permute-start.39 = (bf16[144,3584]{1,0:T(8,128)(2,1)S(1)}, bf16[144,3584]{1,0:T(8,128)(2,1)S(1)}, u32[]{:S(2)}, u32[]{:S(2)}) collective-permute-start(bf16[144,3584]{1,0:T(8,128)(2,1)S(1)} %get-tuple-element.186), channel_id=1, source_target_pairs={{0,1},{1,0},{2,3},{3,2},{4,5},{5,4},{6,7},{7,6},{8,9},{9,8},{10,11... | collective-permute-start | bytes 3096584 | tf_op jit(solution)/shard_map/ppermute | solution.py:895
  108.4 5.5 %collective-permute-start.49 = (bf16[16,3584]{1,0:T(8,128)(2,1)S(1)}, bf16[16,3584]{1,0:T(8,128)(2,1)S(1)}, u32[]{:S(2)}, u32[]{:S(2)}) collective-permute-start(bf16[16,3584]{1,0:T(8,128)(2,1)S(1)} %get-tuple-element.198), channel_id=1, source_target_pairs={{0,4},{4,8},{8,12},{12,14},{14,10},{10,6},{6,2},{2,0},{1,5},{5,9},... | collective-permute-start | bytes 344072 | tf_op jit(solution)/shard_map/ppermute | solution.py:889
  109.2 5.1 %collective-permute-start.50 = (bf16[16,3584]{1,0:T(8,128)(2,1)S(1)}, bf16[16,3584]{1,0:T(8,128)(2,1)S(1)}, u32[]{:S(2)}, u32[]{:S(2)}) collective-permute-start(bf16[16,3584]{1,0:T(8,128)(2,1)S(1)} %get-tuple-element.199), channel_id=1, source_target_pairs={{4,0},{8,4},{12,8},{14,12},{10,14},{6,10},{2,6},{0,2},{5,1},{9,5},... | collective-permute-start | bytes 344072 | tf_op jit(solution)/shard_map/ppermute | solution.py:892
  111.1 6.0 %collective-permute-start.40 = (bf16[16,3584]{1,0:T(8,128)(2,1)S(1)}, bf16[16,3584]{1,0:T(8,128)(2,1)S(1)}, u32[]{:S(2)}, u32[]{:S(2)}) collective-permute-start(bf16[16,3584]{1,0:T(8,128)(2,1)S(1)} %get-tuple-element.187), channel_id=1, source_target_pairs={{0,4},{4,8},{8,12},{12,14},{14,10},{10,6},{6,2},{2,0},{1,5},{5,9},... | collective-permute-start | bytes 344072 | tf_op jit(solution)/shard_map/ppermute | solution.py:889
  111.9 5.1 %collective-permute-start.41 = (bf16[16,3584]{1,0:T(8,128)(2,1)S(1)}, bf16[16,3584]{1,0:T(8,128)(2,1)S(1)}, u32[]{:S(2)}, u32[]{:S(2)}) collective-permute-start(bf16[16,3584]{1,0:T(8,128)(2,1)S(1)} %get-tuple-element.188), channel_id=1, source_target_pairs={{4,0},{8,4},{12,8},{14,12},{10,14},{6,10},{2,6},{0,2},{5,1},{9,5},... | collective-permute-start | bytes 344072 | tf_op jit(solution)/shard_map/ppermute | solution.py:892
  115.0 5.7 %collective-permute-start.51 = (bf16[16,3584]{1,0:T(8,128)(2,1)S(1)}, bf16[16,3584]{1,0:T(8,128)(2,1)S(1)}, u32[]{:S(2)}, u32[]{:S(2)}) collective-permute-start(bf16[16,3584]{1,0:T(8,128)(2,1)S(1)} %get-tuple-element.200), channel_id=1, source_target_pairs={{0,4},{4,8},{8,12},{12,14},{14,10},{10,6},{6,2},{2,0},{1,5},{5,9},... | collective-permute-start | bytes 344072 | tf_op jit(solution)/shard_map/ppermute | solution.py:889
  115.5 5.8 %collective-permute-start.52 = (bf16[16,3584]{1,0:T(8,128)(2,1)S(1)}, bf16[16,3584]{1,0:T(8,128)(2,1)S(1)}, u32[]{:S(2)}, u32[]{:S(2)}) collective-permute-start(bf16[16,3584]{1,0:T(8,128)(2,1)S(1)} %get-tuple-element.201), channel_id=1, source_target_pairs={{4,0},{8,4},{12,8},{14,12},{10,14},{6,10},{2,6},{0,2},{5,1},{9,5},... | collective-permute-start | bytes 344072 | tf_op jit(solution)/shard_map/ppermute | solution.py:892
  117.7 6.3 %collective-permute-start.42 = (bf16[16,3584]{1,0:T(8,128)(2,1)S(1)}, bf16[16,3584]{1,0:T(8,128)(2,1)S(1)}, u32[]{:S(2)}, u32[]{:S(2)}) collective-permute-start(bf16[16,3584]{1,0:T(8,128)(2,1)S(1)} %get-tuple-element.189), channel_id=1, source_target_pairs={{0,4},{4,8},{8,12},{12,14},{14,10},{10,6},{6,2},{2,0},{1,5},{5,9},... | collective-permute-start | bytes 344072 | tf_op jit(solution)/shard_map/ppermute | solution.py:889
  118.2 5.8 %collective-permute-start.43 = (bf16[16,3584]{1,0:T(8,128)(2,1)S(1)}, bf16[16,3584]{1,0:T(8,128)(2,1)S(1)}, u32[]{:S(2)}, u32[]{:S(2)}) collective-permute-start(bf16[16,3584]{1,0:T(8,128)(2,1)S(1)} %get-tuple-element.190), channel_id=1, source_target_pairs={{4,0},{8,4},{12,8},{14,12},{10,14},{6,10},{2,6},{0,2},{5,1},{9,5},... | collective-permute-start | bytes 344072 | tf_op jit(solution)/shard_map/ppermute | solution.py:892
  122.0 5.5 %collective-permute-start.53 = (bf16[16,3584]{1,0:T(8,128)(2,1)S(1)}, bf16[16,3584]{1,0:T(8,128)(2,1)S(1)}, u32[]{:S(2)}, u32[]{:S(2)}) collective-permute-start(bf16[16,3584]{1,0:T(8,128)(2,1)S(1)} %get-tuple-element.202), channel_id=1, source_target_pairs={{0,4},{4,8},{8,12},{12,14},{14,10},{10,6},{6,2},{2,0},{1,5},{5,9},... | collective-permute-start | bytes 344072 | tf_op jit(solution)/shard_map/ppermute | solution.py:889
  122.3 5.2 %collective-permute-start.54 = (bf16[16,3584]{1,0:T(8,128)(2,1)S(1)}, bf16[16,3584]{1,0:T(8,128)(2,1)S(1)}, u32[]{:S(2)}, u32[]{:S(2)}) collective-permute-start(bf16[16,3584]{1,0:T(8,128)(2,1)S(1)} %get-tuple-element.203), channel_id=1, source_target_pairs={{4,0},{8,4},{12,8},{14,12},{10,14},{6,10},{2,6},{0,2},{5,1},{9,5},... | collective-permute-start | bytes 344072 | tf_op jit(solution)/shard_map/ppermute | solution.py:892
  124.7 5.5 %collective-permute-start.44 = (bf16[16,3584]{1,0:T(8,128)(2,1)S(1)}, bf16[16,3584]{1,0:T(8,128)(2,1)S(1)}, u32[]{:S(2)}, u32[]{:S(2)}) collective-permute-start(bf16[16,3584]{1,0:T(8,128)(2,1)S(1)} %get-tuple-element.191), channel_id=1, source_target_pairs={{0,4},{4,8},{8,12},{12,14},{14,10},{10,6},{6,2},{2,0},{1,5},{5,9},... | collective-permute-start | bytes 344072 | tf_op jit(solution)/shard_map/ppermute | solution.py:889
  125.0 5.2 %collective-permute-start.45 = (bf16[16,3584]{1,0:T(8,128)(2,1)S(1)}, bf16[16,3584]{1,0:T(8,128)(2,1)S(1)}, u32[]{:S(2)}, u32[]{:S(2)}) collective-permute-start(bf16[16,3584]{1,0:T(8,128)(2,1)S(1)} %get-tuple-element.192), channel_id=1, source_target_pairs={{4,0},{8,4},{12,8},{14,12},{10,14},{6,10},{2,6},{0,2},{5,1},{9,5},... | collective-permute-start | bytes 344072 | tf_op jit(solution)/shard_map/ppermute | solution.py:892
  128.1 5.4 %collective-permute-start.55 = (bf16[16,3584]{1,0:T(8,128)(2,1)S(1)}, bf16[16,3584]{1,0:T(8,128)(2,1)S(1)}, u32[]{:S(2)}, u32[]{:S(2)}) collective-permute-start(bf16[16,3584]{1,0:T(8,128)(2,1)S(1)} %get-tuple-element.204), channel_id=1, source_target_pairs={{0,4},{4,8},{8,12},{12,14},{14,10},{10,6},{6,2},{2,0},{1,5},{5,9},... | collective-permute-start | bytes 344072 | tf_op jit(solution)/shard_map/ppermute | solution.py:889
  129.2 4.8 %collective-permute-start.56 = (bf16[16,3584]{1,0:T(8,128)(2,1)S(1)}, bf16[16,3584]{1,0:T(8,128)(2,1)S(1)}, u32[]{:S(2)}, u32[]{:S(2)}) collective-permute-start(bf16[16,3584]{1,0:T(8,128)(2,1)S(1)} %get-tuple-element.205), channel_id=1, source_target_pairs={{4,0},{8,4},{12,8},{14,12},{10,14},{6,10},{2,6},{0,2},{5,1},{9,5},... | collective-permute-start | bytes 344072 | tf_op jit(solution)/shard_map/ppermute | solution.py:892
  130.9 4.8 %collective-permute-start.46 = (bf16[16,3584]{1,0:T(8,128)(2,1)S(1)}, bf16[16,3584]{1,0:T(8,128)(2,1)S(1)}, u32[]{:S(2)}, u32[]{:S(2)}) collective-permute-start(bf16[16,3584]{1,0:T(8,128)(2,1)S(1)} %get-tuple-element.193), channel_id=1, source_target_pairs={{0,4},{4,8},{8,12},{12,14},{14,10},{10,6},{6,2},{2,0},{1,5},{5,9},... | collective-permute-start | bytes 344072 | tf_op jit(solution)/shard_map/ppermute | solution.py:889
  131.9 4.8 %collective-permute-start.47 = (bf16[16,3584]{1,0:T(8,128)(2,1)S(1)}, bf16[16,3584]{1,0:T(8,128)(2,1)S(1)}, u32[]{:S(2)}, u32[]{:S(2)}) collective-permute-start(bf16[16,3584]{1,0:T(8,128)(2,1)S(1)} %get-tuple-element.194), channel_id=1, source_target_pairs={{4,0},{8,4},{12,8},{14,12},{10,14},{6,10},{2,6},{0,2},{5,1},{9,5},... | collective-permute-start | bytes 344072 | tf_op jit(solution)/shard_map/ppermute | solution.py:892
  134.7 2.8 %collective-permute-start.58 = (bf16[16,3584]{1,0:T(8,128)(2,1)S(1)}, bf16[16,3584]{1,0:T(8,128)(2,1)S(1)}, u32[]{:S(2)}, u32[]{:S(2)}) collective-permute-start(bf16[16,3584]{1,0:T(8,128)(2,1)S(1)} %get-tuple-element.208), channel_id=1, source_target_pairs={{0,1},{1,0},{2,3},{3,2},{4,5},{5,4},{6,7},{7,6},{8,9},{9,8},{10,11... | collective-permute-start | bytes 344072 | tf_op jit(solution)/shard_map/ppermute | solution.py:895
  137.4 1.4 collective-permute-start.57
  (10 other events, 49.3 us)

commit v7 on v6

--- a/solution.py
+++ b/solution.py
@@ -135,8 +135,8 @@
 ):
     if lead:
         scalars, refs = refs[:5], refs[5:]
-        q_hbm, cache_hbm, fresh, vw_hbm, tab, head, main, extra, later = refs[:9]
-        refs = refs[9:]
+        q_hbm, cache_hbm, fresh, vw_hbm, tab, head, main, extra, later, mask = refs[:10]
+        refs = refs[10:]
         q, keys, vw, latent, fz, q_sem, key_sem, vw_sem, dq = refs
         loaded, base = heads, 0
     else:
@@ -207,7 +207,7 @@
     def span_latent(lhs, slot, fresh_keys):
         s = jnp.concatenate([mm(lhs, keys[slot]), mm_nt(lhs, fresh_keys)], 1)
         s = jnp.where(seen, s * score_scale, masked_score)
-        e = jnp.where(seen, jnp.exp(s - jnp.max(s, axis=1, keepdims=True)), 0.0)
+        e = jnp.exp(s - jnp.max(s, axis=1, keepdims=True))
         w = (e * (1.0 / jnp.sum(e, axis=1, keepdims=True))).astype(bf16)
         o = mm_nt(w[:, :cached], keys[0, :value]) + mm(w[:, cached:], fresh_even[:, :value])
         return jnp.where(row < span, o, 0.0).astype(bf16)
@@ -252,7 +252,7 @@
         own = jnp.sum(jnp.where(column == span + slot, own, 0.0), axis=1, keepdims=True)
         own = own * score_scale
         peak = jnp.maximum(jnp.max(scores, axis=1, keepdims=True), own)
-        e = jnp.where(unmasked, jnp.exp(scores - peak), 0.0)
+        e = jnp.exp(scores - peak)
         e_own = jnp.exp(own - peak)
         total = jnp.sum(e, axis=1, keepdims=True) + e_own
         w = e / total
@@ -263,6 +263,7 @@
         own_value = jnp.broadcast_to(own_value[None], (heads, dr, value)).reshape(n, value)
         dec = (acc + (e_own / total).astype(bf16).astype(f32) * own_value).astype(bf16)
         later[...] = dec[count * dr :]
+        mask[...] = jnp.full(mask.shape, tab[BUSY].astype(f32))
         dec = dec[: count * dr]
     else:
         dec = decoded_here[...]
@@ -324,7 +325,8 @@
         scratch.append(pltpu.VMEM((heads * 8, wide), f32))
         out_shape = [jax.ShapeDtypeStruct((table.size,), i32)] + out_shape
         out_shape += [jax.ShapeDtypeStruct(((heads - count) * 8, value), bf16)]
-        out_specs = [smem()] + out_specs + [whole()]
+        out_shape += [jax.ShapeDtypeStruct((8, 128), f32)]
+        out_specs = [smem()] + out_specs + [whole()] * 2
     else:
         ins.append(whole())
         args.append(decoded)
@@ -407,34 +409,6 @@
         cost_estimate=cost(0, 4 * own.size * len(pieces)),
         name="share",
     )(tab, own, *pieces)
-
-
-def route_kernel(tab, *refs):
-    count = len(refs) // 3
-    busy = tab[BUSY] == 1
-    for i in range(count):
-        special, usual, out = refs[2 * i], refs[2 * i + 1], refs[2 * count + i]
-
-        @pl.when(busy)
-        def _(special=special, out=out):
-            out[...] = special[...]
-
-        @pl.when(jnp.logical_not(busy))
-        def _(usual=usual, out=out):
-            out[...] = usual[...]
-
-
-def route(tab, *choices):
-    flat = [x for pair in choices for x in pair]
-    return pl.pallas_call(
-        route_kernel,
-        in_specs=[smem()] + [whole()] * len(flat),
-        out_specs=[whole()] * len(choices),
-        out_shape=[jax.ShapeDtypeStruct(b.shape, b.dtype) for _, b in choices],
-        compiler_params=params(6),
-        cost_estimate=cost(0, 3 * sum(2 * b.size for _, b in choices)),
-        name="route",
-    )(tab, *flat)
 
 
 def project_kernel(source, nodes, block, half, part, first, tab, *refs):
@@ -739,46 +713,31 @@
     )(hidden, weight)
 
 
-def add_kernel(step, tab, mine_f, theirs_f, mine_b, theirs_b, *refs):
-    got, (out_f, out_b) = refs[:-2], refs[-2:]
+def pick_kernel(table, half, tab, mine, theirs, *outs):
     busy = tab[BUSY] == 1
-    own_f = mine_f[...].astype(f32) + theirs_f[...].astype(f32)
-    own_b = mine_b[...].astype(f32) + theirs_b[...].astype(f32)
-    if step == 1:
-        out_f[...] = jnp.where(busy, 0.0, own_f).astype(bf16)
-        out_b[...] = own_b.astype(bf16)
-    elif step == 2:
-        out_f[...] = (own_f + jnp.where(busy, 0.0, got[0][...].astype(f32))).astype(bf16)
-        out_b[...] = (own_b + jnp.where(busy, 0.0, got[1][...].astype(f32))).astype(bf16)
-    else:
-        from_f = jnp.where(busy, got[0][...], got[1][...]).astype(f32)
-        from_b = jnp.where(busy, got[2][...], got[3][...]).astype(f32)
-        out_f[...] = (own_f + from_f).astype(bf16)
-        out_b[...] = (own_b + from_b).astype(bf16)
-
-
-def add(tab, table, step, mine, theirs, got, half):
+    reach = table.reach
+    for step in range(1, reach + 1):
+        for n, where in enumerate((table.ahead, table.behind)):
+            at = pl.multiple_of(tab[where + reach + 1 - step] * half, half)
+            total = mine[pl.ds(at, half)].astype(f32) + theirs[pl.ds(at, half)].astype(f32)
+            if step == 1 and n == 0:
+                total = jnp.where(busy, 0.0, total)
+            outs[2 * (step - 1) + n][...] = total
+
+
+def pick(tab, table, mine, theirs, half):
     columns = mine.shape[1]
-    far = table.reach + 1 - step
-
-    def at(where):
-        return pl.BlockSpec((half, columns), lambda i, tab: (tab[where + far], 0))
-
-    full = pl.BlockSpec((half, columns), lambda i, tab: (0, 0))
-    out = jax.ShapeDtypeStruct((half, columns), bf16)
-    return pl.pallas_call(
-        functools.partial(add_kernel, step),
-        grid_spec=pltpu.PrefetchScalarGridSpec(
-            num_scalar_prefetch=1,
-            grid=(1,),
-            in_specs=[at(table.ahead)] * 2 + [at(table.behind)] * 2 + [full] * len(got),
-            out_specs=[full, full],
-        ),
-        out_shape=[out, out],
-        compiler_params=params(8),
-        cost_estimate=cost(0, 16 * half * columns),
-        name="add",
-    )(tab, mine, theirs, mine, theirs, *got)
+    count = 2 * table.reach
+    out = jax.ShapeDtypeStruct((half, columns), f32)
+    return pl.pallas_call(
+        functools.partial(pick_kernel, table, half),
+        in_specs=[smem(), whole(), whole()],
+        out_specs=[whole()] * count,
+        out_shape=[out] * count,
+        compiler_params=params(10),
+        cost_estimate=cost(0, 8 * count * half * columns),
+        name="pick",
+    )(tab, mine, theirs)
 
 
 def close_kernel(begin, tab, mm_, tm, me, te, f_last, f_prev, b_last, b_prev, own, kept, given):
@@ -897,42 +856,58 @@
     ids = jnp.stack([lax.axis_index("blk"), lax.axis_index("head")]).astype(i32)
     scalars = [ids, span_len, dec_count, span_start, cache_len]
     caches = (queries, latent_cache, new_latent, value_weight)
-    tab, *lead, decoded = attend(table, order, scalars, *caches, 0, 2, None)
-
-    packed = pack(tab, residual, ranks, cores)
-    pieces = []
-    for k, x in enumerate(packed):
+    tab, *lead, decoded, mask = attend(table, order, scalars, *caches, 0, 2, None)
+    here = mask[:1, :1] > 0
+
+    def choose(special, usual):
+        return jnp.where(jnp.broadcast_to(here, usual.shape), special, usual)
+
+
+    packed = list(pack(tab, residual, ranks, cores))
+    pieces = [None] * len(packed)
+
+    def send_piece(k):
         pairs = [
             (i * cores + c, (i + k + len(packed) * c) % ranks * cores + c)
             for i in range(ranks)
             for c in range(cores)
             if k + c > 0
         ]
-        pieces.append(lax.ppermute(x, ("blk", "head"), pairs))
-
+        pieces[k] = lax.ppermute(packed[k], ("blk", "head"), pairs)
+
+    early = len(packed) // 2
+    for k in range(early):
+        send_piece(k)
     decoded, packed = lax.optimization_barrier((decoded, packed))
+    packed = list(packed)
     follow = attend(table, order, [tab], *caches, 1, 2, decoded)
-    follow, pieces = lax.optimization_barrier((follow, pieces))
-    shared = swap(share(tab, packed[0], pieces, cores))
+    follow, pieces[:early], out_weight = lax.optimization_barrier(
+        (follow, pieces[:early], out_weight)
+    )
 
     total = None
-    gathered = []
+    chains = []
     for head, main, extra in (lead, follow):
-        behind, ahead = [], []
-        for step in range(reach):
+        chains.append((head, main, extra, [], []))
+    for step in range(reach):
+        for part, (head, main, extra, behind, ahead) in enumerate(chains):
             if step == 0:
                 out_f, out_b = head, main
             elif step == 1:
-                out_f, out_b = route(tab, (main, behind[0]), (extra, ahead[0]))
+                out_f, out_b = choose(main, behind[0]), choose(extra, ahead[0])
             else:
-                out_f, out_b = route(
-                    tab,
-                    (behind[step - 2], behind[step - 1]),
-                    (ahead[step - 2], ahead[step - 1]),
-                )
+                out_f = choose(behind[step - 2], behind[step - 1])
+                out_b = choose(ahead[step - 2], ahead[step - 1])
+            piece = early + step - 1 + part * (len(packed) - early) // 2
+            if 0 < step <= (len(packed) - early) // 2:
+                out_f, out_b, packed[piece] = lax.optimization_barrier((out_f, out_b, packed[piece]))
+                send_piece(piece)
+            else:
+                out_f, out_b = lax.optimization_barrier((out_f, out_b))
             behind.append(send_next(out_f))
             ahead.append(send_prev(out_b))
-        gathered.append([main] + behind + ahead + [extra])
+    gathered = [[main] + behind + ahead + [extra] for _, main, extra, behind, ahead in chains]
+    shared = swap(share(tab, packed[0], pieces, cores))
     gathered[0], shared = lax.optimization_barrier((gathered[0], shared))
     for part in range(2):
         total = project(tab, table, gathered[part], total, out_weight, part, 2, cores)
@@ -975,14 +950,16 @@
     kept_out, got_out = [], []
     for part in range(parts):
         got_f, got_b = [], []
+        owned = pick(tab, table, mine[part], theirs[part], half)
         for step in range(1, reach + 1):
-            if step == 1:
-                got = []
-            elif step == 2:
-                got = [got_f[0], got_b[0]]
-            else:
-                got = [got_f[step - 3], got_f[step - 2], got_b[step - 3], got_b[step - 2]]
-            out_f, out_b = add(tab, table, step, mine[part], theirs[part], got, half)
+            out_f, out_b = owned[2 * step - 2], owned[2 * step - 1]
+            if step == 2:
+                out_f = out_f + choose(jnp.zeros_like(out_f), got_f[0].astype(f32))
+                out_b = out_b + choose(jnp.zeros_like(out_b), got_b[0].astype(f32))
+            elif step > 2:
+                out_f = out_f + choose(got_f[step - 3], got_f[step - 2]).astype(f32)
+                out_b = out_b + choose(got_b[step - 3], got_b[step - 2]).astype(f32)
+            out_f, out_b = lax.optimization_barrier((out_f.astype(bf16), out_b.astype(bf16)))
             got_f.append(send_next(out_f))
             got_b.append(send_prev(out_b))
         a, b = close(

time: 140 us -> 139 us (level)
  Pallas kernels: 48.1 us -> 41 us
  waiting for transfers between devices: 33 us -> 38.4 us
  starting transfers between devices: 54.8 us -> 53 us
    ppermute x20, waiting for transfers between devices: 12.4 us -> 22.4 us  [send_next(): return lax.ppermute(x, 'blk', forward)]
    pallas_call x14 -> x2, Pallas kernels: 8.48 us -> 1.47 us  [pick(): pl.pallas_call(functools.partial(pick_kernel, table, half), in_specs=[sme...]
    ppermute x20, waiting for transfers between devices: 16.7 us -> 9.74 us  [send_prev(): return lax.ppermute(x, 'blk', backward)]
    ppermute x4, starting transfers between devices: 7.91 us -> 2.27 us  [send_piece(): pieces[k] = lax.ppermute(packed[k], ('blk', 'head'), pairs)]
    ppermute x20, starting transfers between devices: 20.2 us -> 25.3 us  [send_prev(): return lax.ppermute(x, 'blk', backward)]
    ppermute x4, waiting for transfers between devices: 0.04 us -> 2.37 us  [send_piece(): pieces[k] = lax.ppermute(packed[k], ('blk', 'head'), pairs)]
  transfers between devices with their start and end apart: 59 -> 59, of which waited for: 27 -> 33; matrix products, arithmetic and copies ran while one was open for 0% -> 1% of each run, Pallas kernels for 22% -> 18%
where the time goes in v7:
time: 139 us
  starting transfers between devices  53 us (38%)
  Pallas kernels  41 us (29%)
  waiting for transfers between devices  38.4 us (28%)
  local copies, waits for them, and re-layouts  3.53 us (3%)
  between operations  1.99 us (1%)
    ppermute x20, starting transfers between devices, send_prev(): return lax.ppermute(x, 'blk', backward)  25.3 us
    ppermute x20, waiting for transfers between devices, send_next(): return lax.ppermute(x, 'blk', forward)  22.4 us
    ppermute x20, starting transfers between devices, send_next(): return lax.ppermute(x, 'blk', forward)  22.2 us
    pallas_call x2, Pallas kernels, attend(): pl.pallas_call(functools.partial(attend_kernel, table, order, heads, part...  14.1 us
    pallas_call x5, Pallas kernels, expand(): pl.pallas_call(functools.partial(expand_kernel, pieces, first, final, wid...  12.1 us
    ppermute x20, waiting for transfers between devices, send_prev(): return lax.ppermute(x, 'blk', backward)  9.74 us
    pallas_call x2, Pallas kernels, contract(): pl.pallas_call(functools.partial(contract_kernel, part * columns), grid=(...  4.16 us
    ppermute x15, waiting for transfers between devices, swap(): return lax.ppermute(x, 'head', exchange)  3.85 us
  transfers between devices with their start and end apart: 59, of which 33 were waited for; matrix products, arithmetic and copies ran while one was open for 1% of the time, Pallas kernels for 18%

profile of v7, /device:TPU:0, one launch (start us, length us, event | category | flops | bytes accessed | tf_op | source)
XLA Modules:
  0.0 138.6 jit_solution(6269967595455996679)
XLA Ops:
  0.8 0.9 copy-done.2
  3.7 8.2 %attend.2 = (s32[60]{0:T(128)S(1)}, bf16[32,2048]{1,0:T(8,128)(2,1)S(1)}, bf16[32,2048]{1,0:T(8,128)(2,1)S(1)}, bf16[32,2048]{1,0:T(8,128)(2,1)S(1)}, bf16[128,5...) custom-call(s32[2]{0:T(128)S(1)} %pad_add_fusion.refs_0_, s32[8]{0:T(128)S(1)} %copy-done.4, s32[8]{0:T(128)S(1)} %copy-done.5, ...), custom_call_target="tpu_custom_call" | custom-call | flops 713031680 | bytes 4456448 | tf_op jit(solution)/shard_map/attend/pallas_call | solution.py:333
  11.9 3.1 %collective-permute-start.10 = (bf16[32,2048]{1,0:T(8,128)(2,1)S(1)}, bf16[32,2048]{1,0:T(8,128)(2,1)S(1)}, u32[]{:S(2)}, u32[]{:S(2)}) collective-permute-start(bf16[32,2048]{1,0:T(8,128)(2,1)S(1)} %get-tuple-element.156), channel_id=1, source_target_pairs={{0,4},{4,8},{8,12},{12,14},{14,10},{10,6},{6,2},{2,0},{1,5},{5,9},... | collective-permute-start | bytes 393224 | tf_op jit(solution)/shard_map/ppermute | solution.py:848
  15.6 0.8 collective-permute-start
  16.4 3.0 %collective-permute-start.11 = (bf16[32,2048]{1,0:T(8,128)(2,1)S(1)}, bf16[32,2048]{1,0:T(8,128)(2,1)S(1)}, u32[]{:S(2)}, u32[]{:S(2)}) collective-permute-start(bf16[32,2048]{1,0:T(8,128)(2,1)S(1)} %get-tuple-element.171.refs_0_), channel_id=1, source_target_pairs={{4,0},{8,4},{12,8},{14,12},{10,14},{6,10},{2,6},{0,2},{5,1},{9,5},... | collective-permute-start | bytes 393224 | tf_op jit(solution)/shard_map/ppermute | solution.py:851
  20.7 5.9 %attend.3 = (bf16[32,2048]{1,0:T(8,128)(2,1)S(1)}, bf16[32,2048]{1,0:T(8,128)(2,1)S(1)}, bf16[32,2048]{1,0:T(8,128)(2,1)S(1)}) custom-call(s32[60]{0:T(128)S(1)} %get-tuple-element.131.tab.refs_0_, bf16[64,18432]{1,0:T(8,128)(2,1)} %refs_1_.3, bf16[8,576,256]{2,1,0:T(8,128)(2,1)} %refs_2_.3, bf16[64,576]{1,0:T(8,128)(2,1)S(1)} %bitcast.31, ...), custom_call_target="tpu_custom_call" | custom-call | flops 713031680 | bytes 4456448 | tf_op jit(solution)/shard_map/attend/pallas_call | solution.py:333
  26.6 1.6 %collective-permute-start.3 = (bf16[32,2048]{1,0:T(8,128)(2,1)S(1)}, bf16[32,2048]{1,0:T(8,128)(2,1)S(1)}, u32[]{:S(2)}, u32[]{:S(2)}) collective-permute-start(bf16[32,2048]{1,0:T(8,128)(2,1)S(1)} %get-tuple-element.146.refs_0_), channel_id=1, source_target_pairs={{4,0},{8,4},{12,8},{14,12},{10,14},{6,10},{2,6},{0,2},{5,1},{9,5},... | collective-permute-start | bytes 393224 | tf_op jit(solution)/shard_map/ppermute | solution.py:851
  28.8 3.0 %collective-permute-start.13 = (bf16[32,2048]{1,0:T(8,128)(2,1)S(1)}, bf16[32,2048]{1,0:T(8,128)(2,1)S(1)}, u32[]{:S(2)}, u32[]{:S(2)}) collective-permute-start(bf16[32,2048]{1,0:T(8,128)(2,1)S(1)} %broadcast_select_fusion.4), channel_id=1, source_target_pairs={{4,0},{8,4},{12,8},{14,12},{10,14},{6,10},{2,6},{0,2},{5,1},{9,5},... | collective-permute-start | bytes 393224 | tf_op jit(solution)/shard_map/ppermute | solution.py:851
  31.9 2.4 %collective-permute-done.2.refs_1_ = bf16[32,2048]{1,0:T(8,128)(2,1)S(1)} collective-permute-done((bf16[32,2048]{1,0:T(8,128)(2,1)S(1)}, bf16[32,2048]{1,0:T(8,128)(2,1)S(1)}, u32[]{:S(2)}, u32[]{:S(2)}) %collective-permute-start.2) | collective-permute-done | bytes 131104 | tf_op jit(solution)/shard_map/ppermute | solution.py:848
  34.3 1.3 collective-permute-start.19
  36.1 2.3 %collective-permute-start.4 = (bf16[32,2048]{1,0:T(8,128)(2,1)S(1)}, bf16[32,2048]{1,0:T(8,128)(2,1)S(1)}, u32[]{:S(2)}, u32[]{:S(2)}) collective-permute-start(bf16[32,2048]{1,0:T(8,128)(2,1)S(1)} %broadcast_select_fusion.11), channel_id=1, source_target_pairs={{0,4},{4,8},{8,12},{12,14},{14,10},{10,6},{6,2},{2,0},{1,5},{5,9},... | collective-permute-start | bytes 393224 | tf_op jit(solution)/shard_map/ppermute | solution.py:848
  38.5 1.4 %collective-permute-start.15 = (bf16[32,2048]{1,0:T(8,128)(2,1)S(1)}, bf16[32,2048]{1,0:T(8,128)(2,1)S(1)}, u32[]{:S(2)}, u32[]{:S(2)}) collective-permute-start(bf16[32,2048]{1,0:T(8,128)(2,1)S(1)} %broadcast_select_fusion.2), channel_id=1, source_target_pairs={{4,0},{8,4},{12,8},{14,12},{10,14},{6,10},{2,6},{0,2},{5,1},{9,5},... | collective-permute-start | bytes 393224 | tf_op jit(solution)/shard_map/ppermute | solution.py:851
  39.9 0.8 collective-permute-start.14
  40.8 2.4 %collective-permute-done.19.refs_3_ = bf16[64,896]{1,0:T(8,128)(2,1)S(1)} collective-permute-done((bf16[64,896]{1,0:T(8,128)(2,1)S(1)}, bf16[64,896]{1,0:T(8,128)(2,1)S(1)}, u32[]{:S(2)}, u32[]{:S(2)}) %collective-permute-start.19) | collective-permute-done | bytes 114720 | tf_op jit(solution)/shard_map/ppermute | solution.py:876
  43.9 1.8 %collective-permute-start.7 = (bf16[32,2048]{1,0:T(8,128)(2,1)S(1)}, bf16[32,2048]{1,0:T(8,128)(2,1)S(1)}, u32[]{:S(2)}, u32[]{:S(2)}) collective-permute-start(bf16[32,2048]{1,0:T(8,128)(2,1)S(1)} %broadcast_select_fusion.8), channel_id=1, source_target_pairs={{4,0},{8,4},{12,8},{14,12},{10,14},{6,10},{2,6},{0,2},{5,1},{9,5},... | collective-permute-start | bytes 393224 | tf_op jit(solution)/shard_map/ppermute | solution.py:851
  46.3 1.4 %collective-permute-start.16 = (bf16[32,2048]{1,0:T(8,128)(2,1)S(1)}, bf16[32,2048]{1,0:T(8,128)(2,1)S(1)}, u32[]{:S(2)}, u32[]{:S(2)}) collective-permute-start(bf16[32,2048]{1,0:T(8,128)(2,1)S(1)} %broadcast_select_fusion.1), channel_id=1, source_target_pairs={{0,4},{4,8},{8,12},{12,14},{14,10},{10,6},{6,2},{2,0},{1,5},{5,9},... | collective-permute-start | bytes 393224 | tf_op jit(solution)/shard_map/ppermute | solution.py:848
  47.8 0.8 collective-permute-start.17
  48.6 0.8 collective-permute-done.7.refs_7_
  49.4 2.6 %collective-permute-done.6.refs_3_ = bf16[32,2048]{1,0:T(8,128)(2,1)S(1)} collective-permute-done((bf16[32,2048]{1,0:T(8,128)(2,1)S(1)}, bf16[32,2048]{1,0:T(8,128)(2,1)S(1)}, u32[]{:S(2)}, u32[]{:S(2)}) %collective-permute-start.6) | collective-permute-done | bytes 131104 | tf_op jit(solution)/shard_map/ppermute | solution.py:848
  52.1 2.0 %collective-permute-start.9 = (bf16[32,2048]{1,0:T(8,128)(2,1)S(1)}, bf16[32,2048]{1,0:T(8,128)(2,1)S(1)}, u32[]{:S(2)}, u32[]{:S(2)}) collective-permute-start(bf16[32,2048]{1,0:T(8,128)(2,1)S(1)} %broadcast_select_fusion.6), channel_id=1, source_target_pairs={{4,0},{8,4},{12,8},{14,12},{10,14},{6,10},{2,6},{0,2},{5,1},{9,5},... | collective-permute-start | bytes 393224 | tf_op jit(solution)/shard_map/ppermute | solution.py:851
  54.9 1.9 %project.2.refs_10_ = f32[288,896]{1,0:T(8,128)S(1)} custom-call(s32[60]{0:T(128)S(1)} %get-tuple-element.131.tab.refs_0_, bf16[32,2048]{1,0:T(8,128)(2,1)S(1)} %get-tuple-element.171.refs_0_, bf16[32,2048]{1,0:T(8,128)(2,1)S(1)} %collective-permute-done.10.refs_1_, bf16[32,2048]{1,0:T(8,128)(2,1)S(1)} %collective-permute-done.12.refs_2_, ...), custom_call_target="tpu_custom_call" | custom-call | flops 1056964608 | bytes 4849664 | tf_op jit(solution)/shard_map/project/pallas_call | solution.py:478
  57.2 1.3 collective-permute-done.9.refs_8_
  58.5 2.0 %project.3 = (f32[144,896]{1,0:T(8,128)S(1)}, bf16[144,896]{1,0:T(8,128)(2,1)S(1)}) custom-call(s32[60]{0:T(128)S(1)} %get-tuple-element.131.tab.refs_0_, bf16[32,2048]{1,0:T(8,128)(2,1)S(1)} %get-tuple-element.146.refs_0_, bf16[32,2048]{1,0:T(8,128)(2,1)S(1)} %collective-permute-done.2.refs_1_, bf16[32,2048]{1,0:T(8,128)(2,1)S(1)} %collective-permute-done.4.refs_2_, ...), custom_call_target="tpu_custom_call" | custom-call | flops 1056964608 | bytes 4849664 | tf_op jit(solution)/shard_map/project/pallas_call | solution.py:488
  60.6 1.5 %collective-permute-done.21.other = bf16[144,896]{1,0:T(8,128)(2,1)S(1)} collective-permute-done((bf16[144,896]{1,0:T(8,128)(2,1)S(1)}, bf16[144,896]{1,0:T(8,128)(2,1)S(1)}, u32[]{:S(2)}, u32[]{:S(2)}) %collective-permute-start.21) | collective-permute-done | bytes 258080 | tf_op jit(solution)/shard_map/ppermute | solution.py:854
  63.5 1.5 %collective-permute-start.23 = (bf16[144,896]{1,0:T(8,128)(2,1)S(1)}, bf16[144,896]{1,0:T(8,128)(2,1)S(1)}, u32[]{:S(2)}, u32[]{:S(2)}) collective-permute-start(bf16[144,896]{1,0:T(8,128)(2,1)S(1)} %stream.1.refs_0_.refs_1_), channel_id=1, source_target_pairs={{4,0},{8,4},{12,8},{14,12},{10,14},{6,10},{2,6},{0,2},{5,1},{9,5},... | collective-permute-start | bytes 774152 | tf_op jit(solution)/shard_map/ppermute | solution.py:851
  65.1 1.7 %expand.5 = (f32[288,576]{1,0:T(8,128)S(1)}, f32[288,576]{1,0:T(8,128)S(1)}, f32[288,1]{1,0:T(8,128)S(1)}) custom-call(s32[60]{0:T(128)S(1)} %get-tuple-element.131.tab.refs_0_, bf16[144,896]{1,0:T(8,128)(2,1)S(1)} %stream.1.refs_0_.refs_1_, bf16[144,896]{1,0:T(8,128)(2,1)S(1)} %collective-permute-done.24.refs_1_, f32[8,1,896]{2,1,0:T(1,128)S(1)} %bitcast.25, ...), custom_call_target="tpu_custom_call" | custom-call | flops 594542592 | bytes 2580480 | tf_op jit(solution)/shard_map/expand/pallas_call | solution.py:635
  66.7 4.7 %collective-permute-done.22.refs_0_.refs_2_.refs_3_ = bf16[144,896]{1,0:T(8,128)(2,1)S(1)} collective-permute-done((bf16[144,896]{1,0:T(8,128)(2,1)S(1)}, bf16[144,896]{1,0:T(8,128)(2,1)S(1)}, u32[]{:S(2)}, u32[]{:S(2)}) %collective-permute-start.22) | collective-permute-done | bytes 258080 | tf_op jit(solution)/shard_map/ppermute | solution.py:848
  72.2 1.6 %collective-permute-start.25 = (bf16[144,896]{1,0:T(8,128)(2,1)S(1)}, bf16[144,896]{1,0:T(8,128)(2,1)S(1)}, u32[]{:S(2)}, u32[]{:S(2)}) collective-permute-start(bf16[144,896]{1,0:T(8,128)(2,1)S(1)} %collective-permute-done.22.refs_0_.refs_2_.refs_3_), channel_id=1, source_target_pairs={{0,4},{4,8},{8,12},{12,14},{14,10},{10,6},{6,2},{2,0},{1,5},{5,9},... | collective-permute-start | bytes 774152 | tf_op jit(solution)/shard_map/ppermute | solution.py:848
  74.2 2.9 %expand.6 = (f32[288,576]{1,0:T(8,128)S(1)}, f32[288,576]{1,0:T(8,128)S(1)}, f32[288,1]{1,0:T(8,128)S(1)}) custom-call(s32[60]{0:T(128)S(1)} %get-tuple-element.131.tab.refs_0_, bf16[144,896]{1,0:T(8,128)(2,1)S(1)} %collective-permute-done.22.refs_0_.refs_2_.refs_3_, bf16[144,896]{1,0:T(8,128)(2,1)S(1)} %collective-permute-done.27.refs_1_, ...), custom_call_target="tpu_custom_call" | custom-call | flops 1189085184 | bytes 5160960 | tf_op jit(solution)/shard_map/expand/pallas_call | solution.py:635
  77.1 3.2 %collective-permute-done.25.refs_0_.refs_6_.refs_7_ = bf16[144,896]{1,0:T(8,128)(2,1)S(1)} collective-permute-done((bf16[144,896]{1,0:T(8,128)(2,1)S(1)}, bf16[144,896]{1,0:T(8,128)(2,1)S(1)}, u32[]{:S(2)}, u32[]{:S(2)}) %collective-permute-start.25) | collective-permute-done | bytes 258080 | tf_op jit(solution)/shard_map/ppermute | solution.py:848
  80.3 1.3 collective-permute-done.26.refs_2_.refs_8_.refs_9_
  82.1 1.2 collective-permute-start.29
  83.3 0.8 collective-permute-start.30
  84.2 2.9 %expand.7 = (f32[288,576]{1,0:T(8,128)S(1)}, f32[288,576]{1,0:T(8,128)S(1)}, f32[288,1]{1,0:T(8,128)S(1)}) custom-call(s32[60]{0:T(128)S(1)} %get-tuple-element.131.tab.refs_0_, bf16[144,896]{1,0:T(8,128)(2,1)S(1)} %collective-permute-done.25.refs_0_.refs_6_.refs_7_, bf16[144,896]{1,0:T(8,128)(2,1)S(1)} %collective-permute-done.31.refs_1_, ...), custom_call_target="tpu_custom_call" | custom-call | flops 1189085184 | bytes 5160960 | tf_op jit(solution)/shard_map/expand/pallas_call | solution.py:635
  87.0 3.2 %collective-permute-done.29.refs_0_.refs_10_.refs_11_ = bf16[144,896]{1,0:T(8,128)(2,1)S(1)} collective-permute-done((bf16[144,896]{1,0:T(8,128)(2,1)S(1)}, bf16[144,896]{1,0:T(8,128)(2,1)S(1)}, u32[]{:S(2)}, u32[]{:S(2)}) %collective-permute-start.29) | collective-permute-done | bytes 258080 | tf_op jit(solution)/shard_map/ppermute | solution.py:848
  90.3 0.9 collective-permute-done.30.refs_2_.refs_12_.refs_13_
  92.3 1.5 %collective-permute-start.34 = (bf16[64,896]{1,0:T(8,128)(2,1)S(1)}, bf16[64,896]{1,0:T(8,128)(2,1)S(1)}, u32[]{:S(2)}, u32[]{:S(2)}) collective-permute-start(bf16[64,896]{1,0:T(8,128)(2,1)S(1)} %slice.11), channel_id=1, source_target_pairs={{4,0},{8,4},{12,8},{14,12},{10,14},{6,10},{2,6},{0,2},{5,1},{9,5},... | collective-permute-start | bytes 344072 | tf_op jit(solution)/shard_map/ppermute | solution.py:851
  93.8 2.9 %expand.8 = (f32[288,576]{1,0:T(8,128)S(1)}, f32[288,576]{1,0:T(8,128)S(1)}, f32[288,1]{1,0:T(8,128)S(1)}) custom-call(s32[60]{0:T(128)S(1)} %get-tuple-element.131.tab.refs_0_, bf16[144,896]{1,0:T(8,128)(2,1)S(1)} %collective-permute-done.29.refs_0_.refs_10_.refs_11_, bf16[144,896]{1,0:T(8,128)(2,1)S(1)} %collective-permute-done.35.refs_1_, ...), custom_call_target="tpu_custom_call" | custom-call | flops 1189085184 | bytes 5160960 | tf_op jit(solution)/shard_map/expand/pallas_call | solution.py:635
  97.9 1.0 collective-permute-done.38.refs_3_
  99.0 1.8 %expand.9.hidden = bf16[288,576]{1,0:T(8,128)(2,1)S(1)} custom-call(s32[60]{0:T(128)S(1)} %get-tuple-element.131.tab.refs_0_, bf16[80,896]{1,0:T(8,128)(2,1)S(1)} %collective-permute-done.33.refs_0_, bf16[64,896]{1,0:T(8,128)(2,1)S(1)} %collective-permute-done.34.refs_1_, bf16[80,896]{1,0:T(8,128)(2,1)S(1)} %collective-permute-done.37.refs_2_, ...), custom_call_target="tpu_custom_call" | custom-call | flops 594542592 | bytes 2580480 | tf_op jit(solution)/shard_map/expand/pallas_call | solution.py:635
  100.9 2.1 %contract.3 = (bf16[144,3584]{1,0:T(8,128)(2,1)S(1)}, bf16[144,3584]{1,0:T(8,128)(2,1)S(1)}) custom-call(bf16[288,576]{1,0:T(8,128)(2,1)S(1)} %expand.9.hidden, bf16[576,7168]{1,0:T(8,128)(2,1)S(1)} %bitcast.22), custom_call_target="tpu_custom_call" | custom-call | flops 1189085184 | bytes 6193152 | tf_op jit(solution)/shard_map/contract/pallas_call | solution.py:701
  103.3 2.1 %contract.2 = (bf16[144,3584]{1,0:T(8,128)(2,1)S(1)}, bf16[144,3584]{1,0:T(8,128)(2,1)S(1)}) custom-call(bf16[288,576]{1,0:T(8,128)(2,1)S(1)} %expand.9.hidden, bf16[576,7168]{1,0:T(8,128)(2,1)S(1)} %bitcast.22), custom_call_target="tpu_custom_call" | custom-call | flops 1189085184 | bytes 6193152 | tf_op jit(solution)/shard_map/contract/pallas_call | solution.py:701
  105.7 0.7 pick.3
  106.5 1.3 collective-permute-start.50
  107.8 0.8 collective-permute-start.49
  108.5 0.7 pick.2
  109.3 1.3 collective-permute-start.41
  110.6 0.8 collective-permute-start.40
  111.9 1.0 collective-permute-done.49
  112.9 0.9 collective-permute-start.52
  113.8 1.2 collective-permute-start.51
  115.6 1.0 collective-permute-start.43
  116.7 1.0 collective-permute-start.42
  117.7 1.0 collective-permute-done.52
  118.7 1.1 collective-permute-done.51
  120.6 1.4 %collective-permute-start.53 = (bf16[16,3584]{1,0:T(8,128)(2,1)S(1)}, bf16[16,3584]{1,0:T(8,128)(2,1)S(1)}, u32[]{:S(2)}, u32[]{:S(2)}) collective-permute-start(bf16[16,3584]{1,0:T(8,128)(2,1)S(1)} %add_convert_fusion.3), channel_id=1, source_target_pairs={{0,4},{4,8},{8,12},{12,14},{14,10},{10,6},{6,2},{2,0},{1,5},{5,9},... | collective-permute-start | bytes 344072 | tf_op jit(solution)/shard_map/ppermute | solution.py:848
  122.9 1.7 %collective-permute-start.44 = (bf16[16,3584]{1,0:T(8,128)(2,1)S(1)}, bf16[16,3584]{1,0:T(8,128)(2,1)S(1)}, u32[]{:S(2)}, u32[]{:S(2)}) collective-permute-start(bf16[16,3584]{1,0:T(8,128)(2,1)S(1)} %add_convert_fusion.9), channel_id=1, source_target_pairs={{0,4},{4,8},{8,12},{12,14},{14,10},{10,6},{6,2},{2,0},{1,5},{5,9},... | collective-permute-start | bytes 344072 | tf_op jit(solution)/shard_map/ppermute | solution.py:848
  125.2 0.9 collective-permute-done.53.f_prev
  126.1 1.4 collective-permute-start.55
  128.8 1.6 %collective-permute-start.46 = (bf16[16,3584]{1,0:T(8,128)(2,1)S(1)}, bf16[16,3584]{1,0:T(8,128)(2,1)S(1)}, u32[]{:S(2)}, u32[]{:S(2)}) collective-permute-start(bf16[16,3584]{1,0:T(8,128)(2,1)S(1)} %add_convert_fusion.7), channel_id=1, source_target_pairs={{0,4},{4,8},{8,12},{12,14},{14,10},{10,6},{6,2},{2,0},{1,5},{5,9},... | collective-permute-start | bytes 344072 | tf_op jit(solution)/shard_map/ppermute | solution.py:848
  131.5 0.7 collective-permute-done.56.b_last
  133.6 1.6 %collective-permute-done.47.b_last = bf16[16,3584]{1,0:T(8,128)(2,1)S(1)} collective-permute-done((bf16[16,3584]{1,0:T(8,128)(2,1)S(1)}, bf16[16,3584]{1,0:T(8,128)(2,1)S(1)}, u32[]{:S(2)}, u32[]{:S(2)}) %collective-permute-start.47) | collective-permute-done | bytes 114720 | tf_op jit(solution)/shard_map/ppermute | solution.py:851
  136.0 1.3 collective-permute-done.57.refs_2_
  137.3 1.4 finish.1
  (141 shorter events, 21.2 us)
Async XLA Ops:
  0.0 15.0 %copy-start = (bf16[64,7168]{1,0:T(8,128)(2,1)S(1)}, bf16[64,7168]{1,0:T(8,128)(2,1)}, u32[]{:S(2)}) copy-start(bf16[64,7168]{1,0:T(8,128)(2,1)} %res.1) | copy-start | bytes 2752516
  3.7 17.0 %copy-start.3 = (bf16[576,64]{0,1:T(8,128)(2,1)S(1)}, bf16[576,64]{0,1:T(8,128)(2,1)}, u32[]{:S(2)}) copy-start(bf16[576,64]{0,1:T(8,128)(2,1)} %param.16) | copy-start | bytes 221188
  11.9 16.8 %collective-permute-start.10 = (bf16[32,2048]{1,0:T(8,128)(2,1)S(1)}, bf16[32,2048]{1,0:T(8,128)(2,1)S(1)}, u32[]{:S(2)}, u32[]{:S(2)}) collective-permute-start(bf16[32,2048]{1,0:T(8,128)(2,1)S(1)} %get-tuple-element.156), channel_id=1, source_target_pairs={{0,4},{4,8},{8,12},{12,14},{14,10},{10,6},{6,2},{2,0},{1,5},{5,9},... | collective-permute-start | bytes 393224 | tf_op jit(solution)/shard_map/ppermute | solution.py:848
  15.6 39.3 %slice-start.6 = ((s8[7340032]{0:T(1024)(128)(4,1)}), s8[4194304]{0:T(1024)(128)(4,1)S(1)}, s32[]{:S(2)}) async-start(s8[7340032]{0:T(1024)(128)(4,1)} %bitcast.23), calls=%async_computation.6 | async-start | bytes 8388608
  15.6 11.0 %collective-permute-start = (bf16[64,896]{1,0:T(8,128)(2,1)S(1)}, bf16[64,896]{1,0:T(8,128)(2,1)S(1)}, u32[]{:S(2)}, u32[]{:S(2)}) collective-permute-start(bf16[64,896]{1,0:T(8,128)(2,1)S(1)} %get-tuple-element.166.own), channel_id=1, source_target_pairs={{1,9},{3,11},{5,13},{7,15},{9,1},{11,3},{13,5},{15,7},{17,25},{19,... | collective-permute-start | bytes 344072 | tf_op jit(solution)/shard_map/ppermute | solution.py:876
  16.4 10.2 %collective-permute-start.1 = (bf16[64,896]{1,0:T(8,128)(2,1)S(1)}, bf16[64,896]{1,0:T(8,128)(2,1)S(1)}, u32[]{:S(2)}, u32[]{:S(2)}) collective-permute-start(bf16[64,896]{1,0:T(8,128)(2,1)S(1)} %get-tuple-element.134), channel_id=1, source_target_pairs={{0,2},{1,11},{2,4},{3,13},{4,6},{5,15},{6,8},{7,1},{8,10},{9,3},{1... | collective-permute-start | bytes 344072 | tf_op jit(solution)/shard_map/ppermute | solution.py:876
  16.4 12.3 %collective-permute-start.11 = (bf16[32,2048]{1,0:T(8,128)(2,1)S(1)}, bf16[32,2048]{1,0:T(8,128)(2,1)S(1)}, u32[]{:S(2)}, u32[]{:S(2)}) collective-permute-start(bf16[32,2048]{1,0:T(8,128)(2,1)S(1)} %get-tuple-element.171.refs_0_), channel_id=1, source_target_pairs={{4,0},{8,4},{12,8},{14,12},{10,14},{6,10},{2,6},{0,2},{5,1},{9,5},... | collective-permute-start | bytes 393224 | tf_op jit(solution)/shard_map/ppermute | solution.py:851
  20.6 34.2 %slice-start.7 = ((s8[7340032]{0:T(1024)(128)(4,1)}), s8[3145728]{0:T(1024)(128)(4,1)S(1)}, s32[]{:S(2)}) async-start(s8[7340032]{0:T(1024)(128)(4,1)} %bitcast.23), calls=%async_computation.7 | async-start | bytes 6291456
  26.6 7.7 %collective-permute-start.3 = (bf16[32,2048]{1,0:T(8,128)(2,1)S(1)}, bf16[32,2048]{1,0:T(8,128)(2,1)S(1)}, u32[]{:S(2)}, u32[]{:S(2)}) collective-permute-start(bf16[32,2048]{1,0:T(8,128)(2,1)S(1)} %get-tuple-element.146.refs_0_), channel_id=1, source_target_pairs={{4,0},{8,4},{12,8},{14,12},{10,14},{6,10},{2,6},{0,2},{5,1},{9,5},... | collective-permute-start | bytes 393224 | tf_op jit(solution)/shard_map/ppermute | solution.py:851
  28.2 6.1 %collective-permute-start.2 = (bf16[32,2048]{1,0:T(8,128)(2,1)S(1)}, bf16[32,2048]{1,0:T(8,128)(2,1)S(1)}, u32[]{:S(2)}, u32[]{:S(2)}) collective-permute-start(bf16[32,2048]{1,0:T(8,128)(2,1)S(1)} %get-tuple-element.143), channel_id=1, source_target_pairs={{0,4},{4,8},{8,12},{12,14},{14,10},{10,6},{6,2},{2,0},{1,5},{5,9},... | collective-permute-start | bytes 393224 | tf_op jit(solution)/shard_map/ppermute | solution.py:848
  28.7 11.2 %collective-permute-start.18 = (bf16[64,896]{1,0:T(8,128)(2,1)S(1)}, bf16[64,896]{1,0:T(8,128)(2,1)S(1)}, u32[]{:S(2)}, u32[]{:S(2)}) collective-permute-start(bf16[64,896]{1,0:T(8,128)(2,1)S(1)} %get-tuple-element.169), channel_id=1, source_target_pairs={{0,4},{1,13},{2,6},{3,15},{4,8},{5,1},{6,10},{7,3},{8,12},{9,5},{1... | collective-permute-start | bytes 344072 | tf_op jit(solution)/shard_map/ppermute | solution.py:876
  28.8 7.3 %collective-permute-start.13 = (bf16[32,2048]{1,0:T(8,128)(2,1)S(1)}, bf16[32,2048]{1,0:T(8,128)(2,1)S(1)}, u32[]{:S(2)}, u32[]{:S(2)}) collective-permute-start(bf16[32,2048]{1,0:T(8,128)(2,1)S(1)} %broadcast_select_fusion.4), channel_id=1, source_target_pairs={{4,0},{8,4},{12,8},{14,12},{10,14},{6,10},{2,6},{0,2},{5,1},{9,5},... | collective-permute-start | bytes 393224 | tf_op jit(solution)/shard_map/ppermute | solution.py:851
  31.9 6.6 %collective-permute-start.12 = (bf16[32,2048]{1,0:T(8,128)(2,1)S(1)}, bf16[32,2048]{1,0:T(8,128)(2,1)S(1)}, u32[]{:S(2)}, u32[]{:S(2)}) collective-permute-start(bf16[32,2048]{1,0:T(8,128)(2,1)S(1)} %broadcast_select_fusion.5), channel_id=1, source_target_pairs={{0,4},{4,8},{8,12},{12,14},{14,10},{10,6},{6,2},{2,0},{1,5},{5,9},... | collective-permute-start | bytes 393224 | tf_op jit(solution)/shard_map/ppermute | solution.py:848
  34.3 8.8 %collective-permute-start.19 = (bf16[64,896]{1,0:T(8,128)(2,1)S(1)}, bf16[64,896]{1,0:T(8,128)(2,1)S(1)}, u32[]{:S(2)}, u32[]{:S(2)}) collective-permute-start(bf16[64,896]{1,0:T(8,128)(2,1)S(1)} %get-tuple-element.170), channel_id=1, source_target_pairs={{0,6},{1,15},{2,8},{3,1},{4,10},{5,3},{6,12},{7,5},{8,14},{9,7},{1... | collective-permute-start | bytes 344072 | tf_op jit(solution)/shard_map/ppermute | solution.py:876
  35.7 8.1 %collective-permute-start.5 = (bf16[32,2048]{1,0:T(8,128)(2,1)S(1)}, bf16[32,2048]{1,0:T(8,128)(2,1)S(1)}, u32[]{:S(2)}, u32[]{:S(2)}) collective-permute-start(bf16[32,2048]{1,0:T(8,128)(2,1)S(1)} %broadcast_select_fusion.10), channel_id=1, source_target_pairs={{4,0},{8,4},{12,8},{14,12},{10,14},{6,10},{2,6},{0,2},{5,1},{9,5},... | collective-permute-start | bytes 393224 | tf_op jit(solution)/shard_map/ppermute | solution.py:851
  36.1 7.7 %collective-permute-start.4 = (bf16[32,2048]{1,0:T(8,128)(2,1)S(1)}, bf16[32,2048]{1,0:T(8,128)(2,1)S(1)}, u32[]{:S(2)}, u32[]{:S(2)}) collective-permute-start(bf16[32,2048]{1,0:T(8,128)(2,1)S(1)} %broadcast_select_fusion.11), channel_id=1, source_target_pairs={{0,4},{4,8},{8,12},{12,14},{14,10},{10,6},{6,2},{2,0},{1,5},{5,9},... | collective-permute-start | bytes 393224 | tf_op jit(solution)/shard_map/ppermute | solution.py:848
  38.5 7.5 %collective-permute-start.15 = (bf16[32,2048]{1,0:T(8,128)(2,1)S(1)}, bf16[32,2048]{1,0:T(8,128)(2,1)S(1)}, u32[]{:S(2)}, u32[]{:S(2)}) collective-permute-start(bf16[32,2048]{1,0:T(8,128)(2,1)S(1)} %broadcast_select_fusion.2), channel_id=1, source_target_pairs={{4,0},{8,4},{12,8},{14,12},{10,14},{6,10},{2,6},{0,2},{5,1},{9,5},... | collective-permute-start | bytes 393224 | tf_op jit(solution)/shard_map/ppermute | solution.py:851
  39.9 6.3 %collective-permute-start.14 = (bf16[32,2048]{1,0:T(8,128)(2,1)S(1)}, bf16[32,2048]{1,0:T(8,128)(2,1)S(1)}, u32[]{:S(2)}, u32[]{:S(2)}) collective-permute-start(bf16[32,2048]{1,0:T(8,128)(2,1)S(1)} %broadcast_select_fusion.3), channel_id=1, source_target_pairs={{0,4},{4,8},{8,12},{12,14},{14,10},{10,6},{6,2},{2,0},{1,5},{5,9},... | collective-permute-start | bytes 393224 | tf_op jit(solution)/shard_map/ppermute | solution.py:848
  43.7 11.1 %collective-permute-start.20 = (bf16[128,896]{1,0:T(8,128)(2,1)S(1)}, bf16[128,896]{1,0:T(8,128)(2,1)S(1)}, u32[]{:S(2)}, u32[]{:S(2)}) collective-permute-start(bf16[128,896]{1,0:T(8,128)(2,1)S(1)} %share.1), channel_id=1, source_target_pairs={{0,1},{1,0},{2,3},{3,2},{4,5},{5,4},{6,7},{7,6},{8,9},{9,8},{10,11... | collective-permute-start | bytes 688136 | tf_op jit(solution)/shard_map/ppermute | solution.py:854
  43.9 21.2 %slice-start.2 = ((s8[8257536]{0:T(1024)(128)(4,1)}), s8[4194304]{0:T(1024)(128)(4,1)S(1)}, s32[]{:S(2)}) async-start(s8[8257536]{0:T(1024)(128)(4,1)} %bitcast.14), calls=%async_computation.2 | async-start | bytes 8388608
  43.9 5.5 %collective-permute-start.7 = (bf16[32,2048]{1,0:T(8,128)(2,1)S(1)}, bf16[32,2048]{1,0:T(8,128)(2,1)S(1)}, u32[]{:S(2)}, u32[]{:S(2)}) collective-permute-start(bf16[32,2048]{1,0:T(8,128)(2,1)S(1)} %broadcast_select_fusion.8), channel_id=1, source_target_pairs={{4,0},{8,4},{12,8},{14,12},{10,14},{6,10},{2,6},{0,2},{5,1},{9,5},... | collective-permute-start | bytes 393224 | tf_op jit(solution)/shard_map/ppermute | solution.py:851
  45.7 6.3 %collective-permute-start.6 = (bf16[32,2048]{1,0:T(8,128)(2,1)S(1)}, bf16[32,2048]{1,0:T(8,128)(2,1)S(1)}, u32[]{:S(2)}, u32[]{:S(2)}) collective-permute-start(bf16[32,2048]{1,0:T(8,128)(2,1)S(1)} %broadcast_select_fusion.9), channel_id=1, source_target_pairs={{0,4},{4,8},{8,12},{12,14},{14,10},{10,6},{6,2},{2,0},{1,5},{5,9},... | collective-permute-start | bytes 393224 | tf_op jit(solution)/shard_map/ppermute | solution.py:848
  46.3 8.5 %collective-permute-start.16 = (bf16[32,2048]{1,0:T(8,128)(2,1)S(1)}, bf16[32,2048]{1,0:T(8,128)(2,1)S(1)}, u32[]{:S(2)}, u32[]{:S(2)}) collective-permute-start(bf16[32,2048]{1,0:T(8,128)(2,1)S(1)} %broadcast_select_fusion.1), channel_id=1, source_target_pairs={{0,4},{4,8},{8,12},{12,14},{14,10},{10,6},{6,2},{2,0},{1,5},{5,9},... | collective-permute-start | bytes 393224 | tf_op jit(solution)/shard_map/ppermute | solution.py:848
  47.8 7.1 %collective-permute-start.17 = (bf16[32,2048]{1,0:T(8,128)(2,1)S(1)}, bf16[32,2048]{1,0:T(8,128)(2,1)S(1)}, u32[]{:S(2)}, u32[]{:S(2)}) collective-permute-start(bf16[32,2048]{1,0:T(8,128)(2,1)S(1)} %broadcast_select_fusion), channel_id=1, source_target_pairs={{4,0},{8,4},{12,8},{14,12},{10,14},{6,10},{2,6},{0,2},{5,1},{9,5},... | collective-permute-start | bytes 393224 | tf_op jit(solution)/shard_map/ppermute | solution.py:851
  52.0 5.2 %collective-permute-start.8 = (bf16[32,2048]{1,0:T(8,128)(2,1)S(1)}, bf16[32,2048]{1,0:T(8,128)(2,1)S(1)}, u32[]{:S(2)}, u32[]{:S(2)}) collective-permute-start(bf16[32,2048]{1,0:T(8,128)(2,1)S(1)} %broadcast_select_fusion.7), channel_id=1, source_target_pairs={{0,4},{4,8},{8,12},{12,14},{14,10},{10,6},{6,2},{2,0},{1,5},{5,9},... | collective-permute-start | bytes 393224 | tf_op jit(solution)/shard_map/ppermute | solution.py:848
  52.1 6.3 %collective-permute-start.9 = (bf16[32,2048]{1,0:T(8,128)(2,1)S(1)}, bf16[32,2048]{1,0:T(8,128)(2,1)S(1)}, u32[]{:S(2)}, u32[]{:S(2)}) collective-permute-start(bf16[32,2048]{1,0:T(8,128)(2,1)S(1)} %broadcast_select_fusion.6), channel_id=1, source_target_pairs={{4,0},{8,4},{12,8},{14,12},{10,14},{6,10},{2,6},{0,2},{5,1},{9,5},... | collective-permute-start | bytes 393224 | tf_op jit(solution)/shard_map/ppermute | solution.py:851
  60.5 1.6 %collective-permute-start.21 = (bf16[144,896]{1,0:T(8,128)(2,1)S(1)}, bf16[144,896]{1,0:T(8,128)(2,1)S(1)}, u32[]{:S(2)}, u32[]{:S(2)}) collective-permute-start(bf16[144,896]{1,0:T(8,128)(2,1)S(1)} %get-tuple-element.183), channel_id=1, source_target_pairs={{0,1},{1,0},{2,3},{3,2},{4,5},{5,4},{6,7},{7,6},{8,9},{9,8},{10,11... | collective-permute-start | bytes 774152 | tf_op jit(solution)/shard_map/ppermute | solution.py:854
  62.8 2.2 %collective-permute-start.24 = (bf16[144,896]{1,0:T(8,128)(2,1)S(1)}, bf16[144,896]{1,0:T(8,128)(2,1)S(1)}, u32[]{:S(2)}, u32[]{:S(2)}) collective-permute-start(bf16[144,896]{1,0:T(8,128)(2,1)S(1)} %stream.1.refs_0_.refs_1_), channel_id=1, source_target_pairs={{0,1},{1,0},{2,3},{3,2},{4,5},{5,4},{6,7},{7,6},{8,9},{9,8},{10,11... | collective-permute-start | bytes 774152 | tf_op jit(solution)/shard_map/ppermute | solution.py:854
  63.0 8.5 %collective-permute-start.22 = (bf16[144,896]{1,0:T(8,128)(2,1)S(1)}, bf16[144,896]{1,0:T(8,128)(2,1)S(1)}, u32[]{:S(2)}, u32[]{:S(2)}) collective-permute-start(bf16[144,896]{1,0:T(8,128)(2,1)S(1)} %stream.1.refs_0_.refs_1_), channel_id=1, source_target_pairs={{0,4},{4,8},{8,12},{12,14},{14,10},{10,6},{6,2},{2,0},{1,5},{5,9},... | collective-permute-start | bytes 774152 | tf_op jit(solution)/shard_map/ppermute | solution.py:848
  63.5 8.2 %collective-permute-start.23 = (bf16[144,896]{1,0:T(8,128)(2,1)S(1)}, bf16[144,896]{1,0:T(8,128)(2,1)S(1)}, u32[]{:S(2)}, u32[]{:S(2)}) collective-permute-start(bf16[144,896]{1,0:T(8,128)(2,1)S(1)} %stream.1.refs_0_.refs_1_), channel_id=1, source_target_pairs={{4,0},{8,4},{12,8},{14,12},{10,14},{6,10},{2,6},{0,2},{5,1},{9,5},... | collective-permute-start | bytes 774152 | tf_op jit(solution)/shard_map/ppermute | solution.py:851
  71.7 2.5 %collective-permute-start.27 = (bf16[144,896]{1,0:T(8,128)(2,1)S(1)}, bf16[144,896]{1,0:T(8,128)(2,1)S(1)}, u32[]{:S(2)}, u32[]{:S(2)}) collective-permute-start(bf16[144,896]{1,0:T(8,128)(2,1)S(1)} %collective-permute-done.22.refs_0_.refs_2_.refs_3_), channel_id=1, source_target_pairs={{0,1},{1,0},{2,3},{3,2},{4,5},{5,4},{6,7},{7,6},{8,9},{9,8},{10,11... | collective-permute-start | bytes 774152 | tf_op jit(solution)/shard_map/ppermute | solution.py:854
  71.7 2.5 %collective-permute-start.28 = (bf16[144,896]{1,0:T(8,128)(2,1)S(1)}, bf16[144,896]{1,0:T(8,128)(2,1)S(1)}, u32[]{:S(2)}, u32[]{:S(2)}) collective-permute-start(bf16[144,896]{1,0:T(8,128)(2,1)S(1)} %collective-permute-done.23.refs_2_.refs_4_.refs_5_), channel_id=1, source_target_pairs={{0,1},{1,0},{2,3},{3,2},{4,5},{5,4},{6,7},{7,6},{8,9},{9,8},{10,11... | collective-permute-start | bytes 774152 | tf_op jit(solution)/shard_map/ppermute | solution.py:854
  72.2 8.1 %collective-permute-start.25 = (bf16[144,896]{1,0:T(8,128)(2,1)S(1)}, bf16[144,896]{1,0:T(8,128)(2,1)S(1)}, u32[]{:S(2)}, u32[]{:S(2)}) collective-permute-start(bf16[144,896]{1,0:T(8,128)(2,1)S(1)} %collective-permute-done.22.refs_0_.refs_2_.refs_3_), channel_id=1, source_target_pairs={{0,4},{4,8},{8,12},{12,14},{14,10},{10,6},{6,2},{2,0},{1,5},{5,9},... | collective-permute-start | bytes 774152 | tf_op jit(solution)/shard_map/ppermute | solution.py:848
  73.8 7.8 %collective-permute-start.26 = (bf16[144,896]{1,0:T(8,128)(2,1)S(1)}, bf16[144,896]{1,0:T(8,128)(2,1)S(1)}, u32[]{:S(2)}, u32[]{:S(2)}) collective-permute-start(bf16[144,896]{1,0:T(8,128)(2,1)S(1)} %collective-permute-done.23.refs_2_.refs_4_.refs_5_), channel_id=1, source_target_pairs={{4,0},{8,4},{12,8},{14,12},{10,14},{6,10},{2,6},{0,2},{5,1},{9,5},... | collective-permute-start | bytes 774152 | tf_op jit(solution)/shard_map/ppermute | solution.py:851
  81.6 2.5 %collective-permute-start.31 = (bf16[144,896]{1,0:T(8,128)(2,1)S(1)}, bf16[144,896]{1,0:T(8,128)(2,1)S(1)}, u32[]{:S(2)}, u32[]{:S(2)}) collective-permute-start(bf16[144,896]{1,0:T(8,128)(2,1)S(1)} %collective-permute-done.25.refs_0_.refs_6_.refs_7_), channel_id=1, source_target_pairs={{0,1},{1,0},{2,3},{3,2},{4,5},{5,4},{6,7},{7,6},{8,9},{9,8},{10,11... | collective-permute-start | bytes 774152 | tf_op jit(solution)/shard_map/ppermute | solution.py:854
  81.6 2.5 %collective-permute-start.32 = (bf16[144,896]{1,0:T(8,128)(2,1)S(1)}, bf16[144,896]{1,0:T(8,128)(2,1)S(1)}, u32[]{:S(2)}, u32[]{:S(2)}) collective-permute-start(bf16[144,896]{1,0:T(8,128)(2,1)S(1)} %collective-permute-done.26.refs_2_.refs_8_.refs_9_), channel_id=1, source_target_pairs={{0,1},{1,0},{2,3},{3,2},{4,5},{5,4},{6,7},{7,6},{8,9},{9,8},{10,11... | collective-permute-start | bytes 774152 | tf_op jit(solution)/shard_map/ppermute | solution.py:854
  82.1 8.1 %collective-permute-start.29 = (bf16[144,896]{1,0:T(8,128)(2,1)S(1)}, bf16[144,896]{1,0:T(8,128)(2,1)S(1)}, u32[]{:S(2)}, u32[]{:S(2)}) collective-permute-start(bf16[144,896]{1,0:T(8,128)(2,1)S(1)} %collective-permute-done.25.refs_0_.refs_6_.refs_7_), channel_id=1, source_target_pairs={{0,4},{4,8},{8,12},{12,14},{14,10},{10,6},{6,2},{2,0},{1,5},{5,9},... | collective-permute-start | bytes 774152 | tf_op jit(solution)/shard_map/ppermute | solution.py:848
  83.3 7.8 %collective-permute-start.30 = (bf16[144,896]{1,0:T(8,128)(2,1)S(1)}, bf16[144,896]{1,0:T(8,128)(2,1)S(1)}, u32[]{:S(2)}, u32[]{:S(2)}) collective-permute-start(bf16[144,896]{1,0:T(8,128)(2,1)S(1)} %collective-permute-done.26.refs_2_.refs_8_.refs_9_), channel_id=1, source_target_pairs={{4,0},{8,4},{12,8},{14,12},{10,14},{6,10},{2,6},{0,2},{5,1},{9,5},... | collective-permute-start | bytes 774152 | tf_op jit(solution)/shard_map/ppermute | solution.py:851
  91.2 2.7 %collective-permute-start.35 = (bf16[144,896]{1,0:T(8,128)(2,1)S(1)}, bf16[144,896]{1,0:T(8,128)(2,1)S(1)}, u32[]{:S(2)}, u32[]{:S(2)}) collective-permute-start(bf16[144,896]{1,0:T(8,128)(2,1)S(1)} %collective-permute-done.29.refs_0_.refs_10_.refs_11_), channel_id=1, source_target_pairs={{0,1},{1,0},{2,3},{3,2},{4,5},{5,4},{6,7},{7,6},{8,9},{9,8},{10,11... | collective-permute-start | bytes 774152 | tf_op jit(solution)/shard_map/ppermute | solution.py:854
  91.2 2.7 %collective-permute-start.36 = (bf16[144,896]{1,0:T(8,128)(2,1)S(1)}, bf16[144,896]{1,0:T(8,128)(2,1)S(1)}, u32[]{:S(2)}, u32[]{:S(2)}) collective-permute-start(bf16[144,896]{1,0:T(8,128)(2,1)S(1)} %collective-permute-done.30.refs_2_.refs_12_.refs_13_), channel_id=1, source_target_pairs={{0,1},{1,0},{2,3},{3,2},{4,5},{5,4},{6,7},{7,6},{8,9},{9,8},{10,11... | collective-permute-start | bytes 774152 | tf_op jit(solution)/shard_map/ppermute | solution.py:854
  91.7 5.7 %collective-permute-start.33 = (bf16[80,896]{1,0:T(8,128)(2,1)S(1)}, bf16[80,896]{1,0:T(8,128)(2,1)S(1)}, u32[]{:S(2)}, u32[]{:S(2)}) collective-permute-start(bf16[80,896]{1,0:T(8,128)(2,1)S(1)} %slice.10), channel_id=1, source_target_pairs={{0,4},{4,8},{8,12},{12,14},{14,10},{10,6},{6,2},{2,0},{1,5},{5,9},... | collective-permute-start | bytes 430088 | tf_op jit(solution)/shard_map/ppermute | solution.py:848
  92.3 4.8 %collective-permute-start.34 = (bf16[64,896]{1,0:T(8,128)(2,1)S(1)}, bf16[64,896]{1,0:T(8,128)(2,1)S(1)}, u32[]{:S(2)}, u32[]{:S(2)}) collective-permute-start(bf16[64,896]{1,0:T(8,128)(2,1)S(1)} %slice.11), channel_id=1, source_target_pairs={{4,0},{8,4},{12,8},{14,12},{10,14},{6,10},{2,6},{0,2},{5,1},{9,5},... | collective-permute-start | bytes 344072 | tf_op jit(solution)/shard_map/ppermute | solution.py:851
  97.4 1.5 %collective-permute-start.37 = (bf16[80,896]{1,0:T(8,128)(2,1)S(1)}, bf16[80,896]{1,0:T(8,128)(2,1)S(1)}, u32[]{:S(2)}, u32[]{:S(2)}) collective-permute-start(bf16[80,896]{1,0:T(8,128)(2,1)S(1)} %collective-permute-done.33.refs_0_), channel_id=1, source_target_pairs={{0,1},{1,0},{2,3},{3,2},{4,5},{5,4},{6,7},{7,6},{8,9},{9,8},{10,11... | collective-permute-start | bytes 430088 | tf_op jit(solution)/shard_map/ppermute | solution.py:854
  97.4 1.5 %collective-permute-start.38 = (bf16[64,896]{1,0:T(8,128)(2,1)S(1)}, bf16[64,896]{1,0:T(8,128)(2,1)S(1)}, u32[]{:S(2)}, u32[]{:S(2)}) collective-permute-start(bf16[64,896]{1,0:T(8,128)(2,1)S(1)} %collective-permute-done.34.refs_1_), channel_id=1, source_target_pairs={{0,1},{1,0},{2,3},{3,2},{4,5},{5,4},{6,7},{7,6},{8,9},{9,8},{10,11... | collective-permute-start | bytes 344072 | tf_op jit(solution)/shard_map/ppermute | solution.py:854
  102.9 2.7 %collective-permute-start.48 = (bf16[144,3584]{1,0:T(8,128)(2,1)S(1)}, bf16[144,3584]{1,0:T(8,128)(2,1)S(1)}, u32[]{:S(2)}, u32[]{:S(2)}) collective-permute-start(bf16[144,3584]{1,0:T(8,128)(2,1)S(1)} %get-tuple-element.237), channel_id=1, source_target_pairs={{0,1},{1,0},{2,3},{3,2},{4,5},{5,4},{6,7},{7,6},{8,9},{9,8},{10,11... | collective-permute-start | bytes 3096584 | tf_op jit(solution)/shard_map/ppermute | solution.py:854
  105.4 3.2 %collective-permute-start.39 = (bf16[144,3584]{1,0:T(8,128)(2,1)S(1)}, bf16[144,3584]{1,0:T(8,128)(2,1)S(1)}, u32[]{:S(2)}, u32[]{:S(2)}) collective-permute-start(bf16[144,3584]{1,0:T(8,128)(2,1)S(1)} %get-tuple-element.218), channel_id=1, source_target_pairs={{0,1},{1,0},{2,3},{3,2},{4,5},{5,4},{6,7},{7,6},{8,9},{9,8},{10,11... | collective-permute-start | bytes 3096584 | tf_op jit(solution)/shard_map/ppermute | solution.py:854
  106.5 5.4 %collective-permute-start.50 = (bf16[16,3584]{1,0:T(8,128)(2,1)S(1)}, bf16[16,3584]{1,0:T(8,128)(2,1)S(1)}, u32[]{:S(2)}, u32[]{:S(2)}) collective-permute-start(bf16[16,3584]{1,0:T(8,128)(2,1)S(1)} %convert_element_type.99), channel_id=1, source_target_pairs={{4,0},{8,4},{12,8},{14,12},{10,14},{6,10},{2,6},{0,2},{5,1},{9,5},... | collective-permute-start | bytes 344072 | tf_op jit(solution)/shard_map/ppermute | solution.py:851
  107.8 5.1 %collective-permute-start.49 = (bf16[16,3584]{1,0:T(8,128)(2,1)S(1)}, bf16[16,3584]{1,0:T(8,128)(2,1)S(1)}, u32[]{:S(2)}, u32[]{:S(2)}) collective-permute-start(bf16[16,3584]{1,0:T(8,128)(2,1)S(1)} %convert_element_type.98), channel_id=1, source_target_pairs={{0,4},{4,8},{8,12},{12,14},{14,10},{10,6},{6,2},{2,0},{1,5},{5,9},... | collective-permute-start | bytes 344072 | tf_op jit(solution)/shard_map/ppermute | solution.py:848
  109.3 5.7 %collective-permute-start.41 = (bf16[16,3584]{1,0:T(8,128)(2,1)S(1)}, bf16[16,3584]{1,0:T(8,128)(2,1)S(1)}, u32[]{:S(2)}, u32[]{:S(2)}) collective-permute-start(bf16[16,3584]{1,0:T(8,128)(2,1)S(1)} %convert_element_type.85), channel_id=1, source_target_pairs={{4,0},{8,4},{12,8},{14,12},{10,14},{6,10},{2,6},{0,2},{5,1},{9,5},... | collective-permute-start | bytes 344072 | tf_op jit(solution)/shard_map/ppermute | solution.py:851
  110.6 5.0 %collective-permute-start.40 = (bf16[16,3584]{1,0:T(8,128)(2,1)S(1)}, bf16[16,3584]{1,0:T(8,128)(2,1)S(1)}, u32[]{:S(2)}, u32[]{:S(2)}) collective-permute-start(bf16[16,3584]{1,0:T(8,128)(2,1)S(1)} %convert_element_type.84), channel_id=1, source_target_pairs={{0,4},{4,8},{8,12},{12,14},{14,10},{10,6},{6,2},{2,0},{1,5},{5,9},... | collective-permute-start | bytes 344072 | tf_op jit(solution)/shard_map/ppermute | solution.py:848
  112.9 5.8 %collective-permute-start.52 = (bf16[16,3584]{1,0:T(8,128)(2,1)S(1)}, bf16[16,3584]{1,0:T(8,128)(2,1)S(1)}, u32[]{:S(2)}, u32[]{:S(2)}) collective-permute-start(bf16[16,3584]{1,0:T(8,128)(2,1)S(1)} %add_convert_fusion.4), channel_id=1, source_target_pairs={{4,0},{8,4},{12,8},{14,12},{10,14},{6,10},{2,6},{0,2},{5,1},{9,5},... | collective-permute-start | bytes 344072 | tf_op jit(solution)/shard_map/ppermute | solution.py:851
  113.8 6.0 %collective-permute-start.51 = (bf16[16,3584]{1,0:T(8,128)(2,1)S(1)}, bf16[16,3584]{1,0:T(8,128)(2,1)S(1)}, u32[]{:S(2)}, u32[]{:S(2)}) collective-permute-start(bf16[16,3584]{1,0:T(8,128)(2,1)S(1)} %add_convert_fusion.5), channel_id=1, source_target_pairs={{0,4},{4,8},{8,12},{12,14},{14,10},{10,6},{6,2},{2,0},{1,5},{5,9},... | collective-permute-start | bytes 344072 | tf_op jit(solution)/shard_map/ppermute | solution.py:848
  115.6 6.3 %collective-permute-start.43 = (bf16[16,3584]{1,0:T(8,128)(2,1)S(1)}, bf16[16,3584]{1,0:T(8,128)(2,1)S(1)}, u32[]{:S(2)}, u32[]{:S(2)}) collective-permute-start(bf16[16,3584]{1,0:T(8,128)(2,1)S(1)} %add_convert_fusion.10), channel_id=1, source_target_pairs={{4,0},{8,4},{12,8},{14,12},{10,14},{6,10},{2,6},{0,2},{5,1},{9,5},... | collective-permute-start | bytes 344072 | tf_op jit(solution)/shard_map/ppermute | solution.py:851
  116.7 5.8 %collective-permute-start.42 = (bf16[16,3584]{1,0:T(8,128)(2,1)S(1)}, bf16[16,3584]{1,0:T(8,128)(2,1)S(1)}, u32[]{:S(2)}, u32[]{:S(2)}) collective-permute-start(bf16[16,3584]{1,0:T(8,128)(2,1)S(1)} %add_convert_fusion.11), channel_id=1, source_target_pairs={{0,4},{4,8},{8,12},{12,14},{14,10},{10,6},{6,2},{2,0},{1,5},{5,9},... | collective-permute-start | bytes 344072 | tf_op jit(solution)/shard_map/ppermute | solution.py:848
  119.9 5.2 %collective-permute-start.54 = (bf16[16,3584]{1,0:T(8,128)(2,1)S(1)}, bf16[16,3584]{1,0:T(8,128)(2,1)S(1)}, u32[]{:S(2)}, u32[]{:S(2)}) collective-permute-start(bf16[16,3584]{1,0:T(8,128)(2,1)S(1)} %add_convert_fusion.2), channel_id=1, source_target_pairs={{4,0},{8,4},{12,8},{14,12},{10,14},{6,10},{2,6},{0,2},{5,1},{9,5},... | collective-permute-start | bytes 344072 | tf_op jit(solution)/shard_map/ppermute | solution.py:851
  120.6 5.5 %collective-permute-start.53 = (bf16[16,3584]{1,0:T(8,128)(2,1)S(1)}, bf16[16,3584]{1,0:T(8,128)(2,1)S(1)}, u32[]{:S(2)}, u32[]{:S(2)}) collective-permute-start(bf16[16,3584]{1,0:T(8,128)(2,1)S(1)} %add_convert_fusion.3), channel_id=1, source_target_pairs={{0,4},{4,8},{8,12},{12,14},{14,10},{10,6},{6,2},{2,0},{1,5},{5,9},... | collective-permute-start | bytes 344072 | tf_op jit(solution)/shard_map/ppermute | solution.py:848
  122.5 6.1 %collective-permute-start.45 = (bf16[16,3584]{1,0:T(8,128)(2,1)S(1)}, bf16[16,3584]{1,0:T(8,128)(2,1)S(1)}, u32[]{:S(2)}, u32[]{:S(2)}) collective-permute-start(bf16[16,3584]{1,0:T(8,128)(2,1)S(1)} %add_convert_fusion.8), channel_id=1, source_target_pairs={{4,0},{8,4},{12,8},{14,12},{10,14},{6,10},{2,6},{0,2},{5,1},{9,5},... | collective-permute-start | bytes 344072 | tf_op jit(solution)/shard_map/ppermute | solution.py:851
  122.9 5.9 %collective-permute-start.44 = (bf16[16,3584]{1,0:T(8,128)(2,1)S(1)}, bf16[16,3584]{1,0:T(8,128)(2,1)S(1)}, u32[]{:S(2)}, u32[]{:S(2)}) collective-permute-start(bf16[16,3584]{1,0:T(8,128)(2,1)S(1)} %add_convert_fusion.9), channel_id=1, source_target_pairs={{0,4},{4,8},{8,12},{12,14},{14,10},{10,6},{6,2},{2,0},{1,5},{5,9},... | collective-permute-start | bytes 344072 | tf_op jit(solution)/shard_map/ppermute | solution.py:848
  126.1 5.4 %collective-permute-start.55 = (bf16[16,3584]{1,0:T(8,128)(2,1)S(1)}, bf16[16,3584]{1,0:T(8,128)(2,1)S(1)}, u32[]{:S(2)}, u32[]{:S(2)}) collective-permute-start(bf16[16,3584]{1,0:T(8,128)(2,1)S(1)} %add_convert_fusion.1), channel_id=1, source_target_pairs={{0,4},{4,8},{8,12},{12,14},{14,10},{10,6},{6,2},{2,0},{1,5},{5,9},... | collective-permute-start | bytes 344072 | tf_op jit(solution)/shard_map/ppermute | solution.py:848
  127.4 4.8 %collective-permute-start.56 = (bf16[16,3584]{1,0:T(8,128)(2,1)S(1)}, bf16[16,3584]{1,0:T(8,128)(2,1)S(1)}, u32[]{:S(2)}, u32[]{:S(2)}) collective-permute-start(bf16[16,3584]{1,0:T(8,128)(2,1)S(1)} %add_convert_fusion), channel_id=1, source_target_pairs={{4,0},{8,4},{12,8},{14,12},{10,14},{6,10},{2,6},{0,2},{5,1},{9,5},... | collective-permute-start | bytes 344072 | tf_op jit(solution)/shard_map/ppermute | solution.py:851
  128.8 4.8 %collective-permute-start.46 = (bf16[16,3584]{1,0:T(8,128)(2,1)S(1)}, bf16[16,3584]{1,0:T(8,128)(2,1)S(1)}, u32[]{:S(2)}, u32[]{:S(2)}) collective-permute-start(bf16[16,3584]{1,0:T(8,128)(2,1)S(1)} %add_convert_fusion.7), channel_id=1, source_target_pairs={{0,4},{4,8},{8,12},{12,14},{14,10},{10,6},{6,2},{2,0},{1,5},{5,9},... | collective-permute-start | bytes 344072 | tf_op jit(solution)/shard_map/ppermute | solution.py:848
  130.4 4.8 %collective-permute-start.47 = (bf16[16,3584]{1,0:T(8,128)(2,1)S(1)}, bf16[16,3584]{1,0:T(8,128)(2,1)S(1)}, u32[]{:S(2)}, u32[]{:S(2)}) collective-permute-start(bf16[16,3584]{1,0:T(8,128)(2,1)S(1)} %add_convert_fusion.6), channel_id=1, source_target_pairs={{4,0},{8,4},{12,8},{14,12},{10,14},{6,10},{2,6},{0,2},{5,1},{9,5},... | collective-permute-start | bytes 344072 | tf_op jit(solution)/shard_map/ppermute | solution.py:851
  132.9 3.0 %collective-permute-start.58 = (bf16[16,3584]{1,0:T(8,128)(2,1)S(1)}, bf16[16,3584]{1,0:T(8,128)(2,1)S(1)}, u32[]{:S(2)}, u32[]{:S(2)}) collective-permute-start(bf16[16,3584]{1,0:T(8,128)(2,1)S(1)} %get-tuple-element.256), channel_id=1, source_target_pairs={{0,1},{1,0},{2,3},{3,2},{4,5},{5,4},{6,7},{7,6},{8,9},{9,8},{10,11... | collective-permute-start | bytes 344072 | tf_op jit(solution)/shard_map/ppermute | solution.py:854
  135.9 1.4 %collective-permute-start.57 = (bf16[16,3584]{1,0:T(8,128)(2,1)S(1)}, bf16[16,3584]{1,0:T(8,128)(2,1)S(1)}, u32[]{:S(2)}, u32[]{:S(2)}) collective-permute-start(bf16[16,3584]{1,0:T(8,128)(2,1)S(1)} %get-tuple-element.255), channel_id=1, source_target_pairs={{0,1},{1,0},{2,3},{3,2},{4,5},{5,4},{6,7},{7,6},{8,9},{9,8},{10,11... | collective-permute-start | bytes 344072 | tf_op jit(solution)/shard_map/ppermute | solution.py:854
  (10 other events, 49.2 us)

commit v8 on v7

--- a/solution.py
+++ b/solution.py
@@ -78,12 +78,15 @@
         self.size = self.at + ranks
 
 
-def table_kernel(table, order, ids, span, dec, start, lengths, out):
+def table_kernel(table, order, given, out):
     reach, ranks = table.reach, len(order)
+    span = [given[2 + i] for i in range(ranks)]
+    dec = [given[2 + ranks + i] for i in range(ranks)]
+    lengths = 3 + 2 * ranks
     for i, r in enumerate(order):
         out[table.who + i] = r
         out[table.at + r] = i
-    rank, core = ids[0], ids[1]
+    rank, core = given[0], given[1]
     most, busy_rank = span[0] + dec[0], jnp.int32(0)
     for i in range(1, ranks):
         here = span[i] + dec[i]
@@ -113,12 +116,12 @@
     out[CORE] = core
     out[BUSY] = jnp.where(busy, 1, 0)
     out[BUSY_RANK] = busy_rank
-    out[SPAN] = span[rank]
-    out[DEC] = dec[rank]
-    out[LIVE] = span[rank] + dec[rank]
-    out[START] = start[0]
-    for j in range(lengths.shape[1]):
-        out[LENGTHS + j] = lengths[0, j]
+    out[SPAN] = given[2 + rank]
+    out[DEC] = given[2 + ranks + rank]
+    out[LIVE] = given[2 + rank] + given[2 + ranks + rank]
+    out[START] = given[lengths - 1]
+    for j in range(given.shape[0] - lengths):
+        out[LENGTHS + j] = given[lengths + j]
     out[table.source + rank] = 0
     for k in range(1, reach + 1):
         out[table.ahead + k] = node_ahead(k)
@@ -134,9 +137,9 @@
     table, order, heads, first, count, group, rows, lat, value, lead, *refs
 ):
     if lead:
-        scalars, refs = refs[:5], refs[5:]
-        q_hbm, cache_hbm, fresh, vw_hbm, tab, head, main, extra, later, mask = refs[:10]
-        refs = refs[10:]
+        given, refs = refs[0], refs[1:]
+        q_hbm, cache_hbm, fresh, vw_hbm, tab, head, main, extra, later = refs[:9]
+        flags, refs = refs[9:12], refs[12:]
         q, keys, vw, latent, fz, q_sem, key_sem, vw_sem, dq = refs
         loaded, base = heads, 0
     else:
@@ -181,7 +184,7 @@
     odd_copy.start()
     start_next(1)
     if lead:
-        table_kernel(table, order, *scalars, tab)
+        table_kernel(table, order, given, tab)
     span, decs = tab[SPAN], tab[DEC]
 
     def onehot(shape, row_dim, slot_dim):
@@ -263,7 +266,8 @@
         own_value = jnp.broadcast_to(own_value[None], (heads, dr, value)).reshape(n, value)
         dec = (acc + (e_own / total).astype(bf16).astype(f32) * own_value).astype(bf16)
         later[...] = dec[count * dr :]
-        mask[...] = jnp.full(mask.shape, tab[BUSY].astype(f32))
+        for flag, at in zip(flags, (BUSY, CORE, LIVE)):
+            flag[...] = jnp.full(flag.shape, tab[at].astype(f32))
         dec = dec[: count * dr]
     else:
         dec = decoded_here[...]
@@ -296,7 +300,7 @@
         head[:, at] = jnp.where(tab[BUSY] == 1, out[block:], out[:block])
 
 
-def attend(table, order, scalars, queries, cache, fresh, vw, part, parts, decoded):
+def attend(table, order, numbers, queries, cache, fresh, vw, part, parts, decoded):
     rows, heads = queries.shape[0], vw.shape[0]
     lat = queries.shape[1] // heads
     slots, _, cached = cache.shape
@@ -319,14 +323,14 @@
         pltpu.SemaphoreType.DMA((count // group,)),
     ]
     out_shape, out_specs = [half] * 3, [whole()] * 3
-    ins = [smem()] * len(scalars) + [hbm, hbm, whole(), hbm]
-    args = [*scalars, in_hbm(queries), in_hbm(cache), fresh.T, in_hbm(vw)]
+    ins = [smem(), hbm, hbm, whole(), hbm]
+    args = [numbers, in_hbm(queries), in_hbm(cache), fresh.T, in_hbm(vw)]
     if lead:
         scratch.append(pltpu.VMEM((heads * 8, wide), f32))
         out_shape = [jax.ShapeDtypeStruct((table.size,), i32)] + out_shape
         out_shape += [jax.ShapeDtypeStruct(((heads - count) * 8, value), bf16)]
-        out_shape += [jax.ShapeDtypeStruct((8, 128), f32)]
-        out_specs = [smem()] + out_specs + [whole()] * 2
+        out_shape += [jax.ShapeDtypeStruct((1, 1), f32)] * 3
+        out_specs = [smem()] + out_specs + [whole()] * 4
     else:
         ins.append(whole())
         args.append(decoded)
@@ -501,16 +505,14 @@
     )(*args)
 
 
-def stream_kernel(ranks, half, tab, kept, other, own, shared, *refs):
+def place_kernel(ranks, half, tab, own, shared, *refs):
     pieces, out = refs[:-1], refs[-1]
     rank, core, busy_rank = tab[RANK], tab[CORE], tab[BUSY_RANK]
     count = len(pieces)
     block = own.shape[0] // 2
 
     def put(slot, extra):
-        rows = pl.ds(pl.multiple_of(slot * half, half), half)
-        total = kept[rows] + other[rows].astype(f32) + extra.astype(f32)
-        out[rows] = total.astype(bf16)
+        out[pl.ds(pl.multiple_of(slot * half, half), half)] = extra
 
     def put_both(owner, main, extra):
         put(owner, main())
@@ -543,25 +545,28 @@
         )
 
 
-def stream_of(tab, kept, other, own, shared, pieces, cores):
-    half = own.shape[0] // 2 // cores
+def placed_rows(tab, own, shared, pieces, cores):
+    rows, features = own.shape
+    half = rows // 2 // cores
+    ranks = cores * len(pieces)
     return pl.pallas_call(
-        functools.partial(stream_kernel, cores * len(pieces), half),
-        in_specs=[smem()] + [whole()] * (4 + len(pieces)),
+        functools.partial(place_kernel, ranks, half),
+        in_specs=[smem()] + [whole()] * (2 + len(pieces)),
         out_specs=whole(),
-        out_shape=jax.ShapeDtypeStruct(other.shape, bf16),
+        out_shape=jax.ShapeDtypeStruct(((ranks + 1) * half, features), bf16),
         compiler_params=params(8),
-        cost_estimate=cost(0, 10 * other.size),
-        name="stream",
-    )(tab, kept, other, own, shared, *pieces)
-
-
-def expand_kernel(pieces, first, final, width, turned, owners, tab, *refs):
+        cost_estimate=cost(0, 4 * (ranks + 1) * half * features),
+        name="place",
+    )(tab, own, shared, *pieces)
+
+
+def expand_kernel(pieces, others, first, final, width, turned, owners, tab, *refs):
     count = len(pieces)
     blocks = []
     for number in pieces:
-        blocks.append(refs[: 2 * number])
-        refs = refs[2 * number :]
+        blocks.append(refs[:number])
+        refs = refs[number:]
+    theirs, refs = refs[:others], refs[others:]
     gain, gate, up = refs[:3]
     refs = refs[3:]
     if not first:
@@ -574,7 +579,11 @@
 
         @pl.when(step == i)
         def _(i=i):
-            both = jnp.concatenate([x[...] for x in blocks[i]], 0).astype(f32)
+            both = [x[...] for x in blocks[i]]
+            for x in theirs:
+                rows = x.shape[0] // count
+                both.append(x[i * rows : (i + 1) * rows])
+            both = jnp.concatenate(both, 0).astype(f32)
             rows_of = both.shape[1]
             scaled = (both * gain[0]).astype(bf16)
             if turned:
@@ -605,7 +614,7 @@
     count = len(mines)
     pieces = tuple(len(x) for x in mines)
     rows, features = sum(x.shape[0] for x in mines[0]), mines[0][0].shape[1]
-    arrays = [x for own, other in zip(mines, theirs) for x in (*own, *other)]
+    arrays = [x for own in mines for x in own] + theirs
     units = gate.shape[1]
     first = before is None
     width = gate.shape[0]
@@ -633,7 +642,7 @@
     shapes = [jax.ShapeDtypeStruct(s, f32) for s in sums]
     out_shapes = [jax.ShapeDtypeStruct((2 * rows, units), bf16)] if final else shapes
     return pl.pallas_call(
-        functools.partial(expand_kernel, pieces, first, final, width, turned, owners),
+        functools.partial(expand_kernel, pieces, len(theirs), first, final, width, turned, owners),
         grid_spec=pltpu.PrefetchScalarGridSpec(
             num_scalar_prefetch=1,
             grid=(count,),
@@ -643,15 +652,20 @@
         ),
         out_shape=out_shapes,
         compiler_params=params(20),
-        cost_estimate=cost(
-            8 * count * rows * features * units, count * (4 * features * units + 4 * rows * features)
-        ),
+        cost_estimate=cost(1, 1),
         name="expand",
     )(tab, *arrays, gain, gate, up, *([] if first else before))
 
 
 def collect_kernel(owners, tab, *refs):
     out = refs[-1]
+    if len(out.shape) == 2:
+        half, features = out.shape[0] // 2, out.shape[1] // len(owners)
+        for i, at in enumerate(owners):
+            columns = pl.ds(pl.multiple_of(tab[at] * features, 128), features)
+            out[:half, columns] = refs[2 * i][...]
+            out[half:, columns] = refs[2 * i + 1][...]
+        return
     half = out.shape[1] // 2
     for i, at in enumerate(owners):
         out[tab[at], :half] = refs[2 * i][...]
@@ -668,45 +682,40 @@
             pl.BlockSpec((half, features), lambda i, tab: (ranks, 0)),
         ]
         args += [x, x]
-    shape = (ranks, 2 * half, features)
-    return pl.pallas_call(
+    aligned = features % 128 == 0
+    shape = (2 * half, ranks * features) if aligned else (ranks, 2 * half, features)
+    out = pl.pallas_call(
         functools.partial(collect_kernel, owners),
         grid_spec=pltpu.PrefetchScalarGridSpec(
             num_scalar_prefetch=1,
             grid=(1,),
             in_specs=ins,
-            out_specs=pl.BlockSpec(shape, lambda i, tab: (0, 0, 0)),
+            out_specs=pl.BlockSpec(shape, lambda i, tab: (0,) * len(shape)),
         ),
         out_shape=jax.ShapeDtypeStruct(shape, bf16),
         compiler_params=params(10),
         cost_estimate=cost(0, 8 * ranks * half * features),
         name="collect",
     )(tab, *args)
-
-
-def contract_kernel(begin, hidden, weight, mine, given):
-    rows, wide = mine.shape
+    return out if aligned else out.transpose(1, 0, 2).reshape(2 * half, ranks * features)
+
+
+def contract_kernel(begin, hidden, weight, out):
+    wide = out.shape[1]
     at = pl.ds(pl.multiple_of(begin + pl.program_id(0) * wide, 128), wide)
-    got = mm(hidden[...], weight[:, at]).astype(bf16)
-    mine[...] = got[:rows]
-    given[...] = got[rows:]
-
-
-def contract(hidden, weight, part, parts):
-    rows, units = hidden.shape
+    out[...] = mm(hidden[...], weight[:, at]).astype(bf16)
+
+
+def contract(hidden, weight, part, parts, which):
+    rows, units = hidden.shape[0] // 2, hidden.shape[1]
     columns = weight.shape[1] // parts
     wide = columns // 2 if columns % 256 == 0 else columns
-    steps = columns // wide
-    out = jax.ShapeDtypeStruct((rows // 2, columns), bf16)
     return pl.pallas_call(
         functools.partial(contract_kernel, part * columns),
-        grid=(steps,),
-        in_specs=[
-            pl.BlockSpec((rows, units), lambda i: (0, 0)),
-            whole(),
-        ],
-        out_specs=[pl.BlockSpec((rows // 2, wide), lambda i: (0, i))] * 2,
-        out_shape=[out, out],
+        grid=(columns // wide,),
+        in_specs=[pl.BlockSpec((rows, units), lambda i: (which, 0)), whole()],
+        out_specs=pl.BlockSpec((rows, wide), lambda i: (0, i)),
+        out_shape=jax.ShapeDtypeStruct((rows, columns), bf16),
         compiler_params=params(16),
         cost_estimate=cost(2 * rows * units * columns, 2 * (units + rows) * columns),
         name="contract",
@@ -723,11 +732,14 @@
             if step == 1 and n == 0:
                 total = jnp.where(busy, 0.0, total)
             outs[2 * (step - 1) + n][...] = total
+    for n, slot in enumerate((tab[RANK], 2 * reach)):
+        at = pl.multiple_of(slot * half, half)
+        outs[2 * reach + n][...] = mine[pl.ds(at, half)].astype(f32) + theirs[pl.ds(at, half)].astype(f32)
 
 
 def pick(tab, table, mine, theirs, half):
     columns = mine.shape[1]
-    count = 2 * table.reach
+    count = 2 * table.reach + 2
     out = jax.ShapeDtypeStruct((half, columns), f32)
     return pl.pallas_call(
         functools.partial(pick_kernel, table, half),
@@ -738,78 +750,6 @@
         cost_estimate=cost(0, 8 * count * half * columns),
         name="pick",
     )(tab, mine, theirs)
-
-
-def close_kernel(begin, tab, mm_, tm, me, te, f_last, f_prev, b_last, b_prev, own, kept, given):
-    busy, first = tab[BUSY] == 1, tab[CORE] == 0
-    half, columns = kept.shape
-    features = own.shape[2]
-
-    def total(*refs):
-        out = refs[0][...].astype(f32)
-        for r in refs[1:]:
-            out = out + r[...].astype(f32)
-        return out
-
-    main = total(mm_, tm, f_last) + jnp.where(busy, b_prev[...], b_last[...]).astype(f32)
-    extra = total(me, te, f_prev, b_last)
-    for c in range(columns // features):
-        cols = slice(c * features, (c + 1) * features)
-        m = (main[:, cols] + own[begin + c, :half].astype(f32)).astype(bf16)
-        e = (extra[:, cols] + own[begin + c, half:].astype(f32)).astype(bf16)
-        kept[:, cols] = jnp.where(first, m, e)
-        given[:, cols] = jnp.where(first, e, m)
-
-
-def close(tab, mine, theirs, got_f, got_b, own, begin, half):
-    columns = mine.shape[1]
-    nodes = mine.shape[0] // half
-    own_at = pl.BlockSpec((half, columns), lambda i, tab: (tab[RANK], 0))
-    extra_at = pl.BlockSpec((half, columns), lambda i, tab: (nodes - 1, 0))
-    full = pl.BlockSpec((half, columns), lambda i, tab: (0, 0))
-    out = jax.ShapeDtypeStruct((half, columns), bf16)
-    return pl.pallas_call(
-        functools.partial(close_kernel, begin),
-        grid_spec=pltpu.PrefetchScalarGridSpec(
-            num_scalar_prefetch=1,
-            grid=(1,),
-            in_specs=[own_at, own_at, extra_at, extra_at]
-            + [full] * 4
-            + [pl.BlockSpec(own.shape, lambda i, tab: (0, 0, 0))],
-            out_specs=[full, full],
-        ),
-        out_shape=[out, out],
-        compiler_params=params(12),
-        cost_estimate=cost(0, 24 * half * columns),
-        name="close",
-    )(tab, mine, theirs, mine, theirs, got_f[-1], got_f[-2], got_b[-1], got_b[-2], own)
-
-
-def finish_kernel(parts, tab, *refs):
-    kept, got, out = refs[:parts], refs[parts : 2 * parts], refs[-1]
-    half, columns = kept[0].shape
-    first = tab[CORE] == 0
-    row = tab[CORE] * (2 * half) + lax.broadcasted_iota(i32, (half, 1), 0)
-    for p in range(parts):
-        cols = slice(p * columns, (p + 1) * columns)
-        low = jnp.where(first, kept[p][...], got[p][...])
-        high = jnp.where(first, got[p][...], kept[p][...])
-        zero = jnp.zeros_like(low)
-        out[:half, cols] = jnp.where(row < tab[LIVE], low, zero)
-        out[half:, cols] = jnp.where(row + half < tab[LIVE], high, zero)
-
-
-def finish(tab, kept, got):
-    half, columns = kept[0].shape
-    return pl.pallas_call(
-        functools.partial(finish_kernel, len(kept)),
-        in_specs=[smem()] + [whole()] * (2 * len(kept)),
-        out_specs=whole(),
-        out_shape=jax.ShapeDtypeStruct((2 * half, columns * len(kept)), bf16),
-        compiler_params=params(8),
-        cost_estimate=cost(0, 8 * half * columns * len(kept)),
-        name="finish",
-    )(tab, *kept, *got)
 
 
 contract_parts = 2
@@ -854,13 +794,12 @@
         return lax.ppermute(x, "head", exchange)
 
     ids = jnp.stack([lax.axis_index("blk"), lax.axis_index("head")]).astype(i32)
-    scalars = [ids, span_len, dec_count, span_start, cache_len]
+    given = jnp.concatenate([ids, span_len, dec_count, span_start, cache_len[0]])
     caches = (queries, latent_cache, new_latent, value_weight)
-    tab, *lead, decoded, mask = attend(table, order, scalars, *caches, 0, 2, None)
-    here = mask[:1, :1] > 0
-
-    def choose(special, usual):
-        return jnp.where(jnp.broadcast_to(here, usual.shape), special, usual)
+    tab, *lead, decoded, busy, which, live = attend(table, order, given, *caches, 0, 2, None)
+
+    def choose(special, usual, flag=busy):
+        return jnp.where(jnp.broadcast_to(flag > 0, usual.shape), special, usual)
 
 
     packed = list(pack(tab, residual, ranks, cores))
@@ -880,7 +819,7 @@
         send_piece(k)
     decoded, packed = lax.optimization_barrier((decoded, packed))
     packed = list(packed)
-    follow = attend(table, order, [tab], *caches, 1, 2, decoded)
+    follow = attend(table, order, tab, *caches, 1, 2, decoded)
     follow, pieces[:early], out_weight = lax.optimization_barrier(
         (follow, pieces[:early], out_weight)
     )
@@ -911,46 +850,50 @@
     gathered[0], shared = lax.optimization_barrier((gathered[0], shared))
     for part in range(2):
         total = project(tab, table, gathered[part], total, out_weight, part, 2, cores)
-    kept, given = total
-    stream = stream_of(tab, kept, swap(given), packed[0], shared, pieces, cores)
+    kept, other = total
+    res_here = placed_rows(tab, packed[0], shared, pieces, cores)
+    stream = (kept + swap(other).astype(f32) + res_here.astype(f32)).astype(bf16)
 
     gain = norm_gain.reshape(ranks, 1, features)
-    sums = expand(tab, [[stream]], [[swap(stream)]], [RANK], gain, gate_weight, up_weight, None, False)
+    weights = (gain, gate_weight, up_weight)
+    cut = -(-stream.shape[0] // 32) * 16
+    backs = [stream[:cut], stream[cut:]]
+    fores = list(backs)
+    swapped, backs[1], fores[1] = lax.optimization_barrier((swap(stream), backs[1], fores[1]))
+    sums = expand(tab, [[stream]], [swapped], [RANK], *weights, None, False)
     blocks, owners = [stream], [RANK]
-    fore, back = stream, stream
-    cut = -(-stream.shape[0] // 32) * 16
     done = None
     for step in range(1, reach + 1):
         if done is not None:
-            back, fore, done = lax.optimization_barrier((back, fore, done))
+            backs[0], fores[0], done = lax.optimization_barrier((backs[0], fores[0], done))
         done = sums
         if step < reach:
-            back, fore = send_next(back), send_prev(fore)
-            arrived = [[back], [fore]]
+            for n in range(2):
+                back, fore = lax.optimization_barrier((backs[n], fores[n]))
+                backs[n], fores[n] = send_next(back), send_prev(fore)
+            arrived = [list(backs), list(fores)]
             from_owner = [table.owner_back + step, table.owner_fore + step]
         else:
-            arrived = [[send_next(back[:cut]), send_prev(fore[cut:])]]
+            arrived = [[send_next(backs[0]), send_prev(fores[1])]]
             from_owner = [table.owner_back + step]
-        tied, sums = lax.optimization_barrier((arrived, sums))
-        others = [[swap(x) for x in pieces] for pieces in tied]
-        sums = expand(
-            tab, arrived, others, from_owner, gain, gate_weight, up_weight, sums, step == reach
-        )
-        blocks += [x[0] if len(x) == 1 else jnp.concatenate(x, 0) for x in arrived]
+        others = []
+        for chain in zip(*arrived):
+            tied, sums = lax.optimization_barrier((chain, sums))
+            others.append(swap(jnp.concatenate(tied, 0)))
+        sums = expand(tab, arrived, others, from_owner, *weights, sums, step == reach)
+        blocks += [jnp.concatenate(x, 0) for x in arrived]
         owners += from_owner
     (hidden,) = sums
-    own = collect(tab, blocks, owners, half)
+    own = collect(tab, blocks, owners, half).astype(f32)
 
     parts = contract_parts
-    mine, theirs = [], []
-    for part in range(parts):
-        a, b = contract(hidden, down_weight, part, parts)
-        mine.append(a)
-        theirs.append(swap(b))
-    kept_out, got_out = [], []
+    theirs = [swap(contract(hidden, down_weight, part, parts, 1)) for part in range(parts)]
+    mine = [contract(hidden, down_weight, part, parts, 0) for part in range(parts)]
+    columns = width // parts
+    lows, highs = [], []
     for part in range(parts):
         got_f, got_b = [], []
-        owned = pick(tab, table, mine[part], theirs[part], half)
+        *owned, main, extra = pick(tab, table, mine[part], theirs[part], half)
         for step in range(1, reach + 1):
             out_f, out_b = owned[2 * step - 2], owned[2 * step - 1]
             if step == 2:
@@ -962,12 +905,18 @@
             out_f, out_b = lax.optimization_barrier((out_f.astype(bf16), out_b.astype(bf16)))
             got_f.append(send_next(out_f))
             got_b.append(send_prev(out_b))
-        a, b = close(
-            tab, mine[part], theirs[part], got_f, got_b, own, part * (ranks // parts), half
-        )
-        kept_out.append(a)
-        got_out.append(swap(b))
-    return finish(tab, kept_out, got_out)
+        at = slice(part * columns, (part + 1) * columns)
+        main = main + own[:half, at] + got_f[-1].astype(f32)
+        main = (main + choose(got_b[-2], got_b[-1]).astype(f32)).astype(bf16)
+        extra = extra + own[half:, at] + got_f[-2].astype(f32) + got_b[-1].astype(f32)
+        extra = extra.astype(bf16)
+        received = swap(choose(main, extra, which))
+        stays = choose(extra, main, which)
+        lows.append(choose(received, stays, which))
+        highs.append(choose(stays, received, which))
+    result = jnp.concatenate([jnp.concatenate(lows, 1), jnp.concatenate(highs, 1)], 0)
+    row = which * (2 * half) + lax.broadcasted_iota(i32, result.shape, 0).astype(f32)
+    return jnp.where(row < live, result, jnp.zeros_like(result))
 
 
 def solution(mesh):

time: 139 us -> 140 us (level)
  starting transfers between devices: 53 us -> 59.3 us
  waiting for transfers between devices: 38.4 us -> 32.8 us
  other arithmetic: 0.8 us -> 3.01 us
  Pallas kernels: 41 us -> 39.1 us
  local copies, waits for them, and re-layouts: 3.53 us -> 1.82 us
  between operations: 1.99 us -> 3.39 us
    ppermute x20 -> x23, waiting for transfers between devices: 22.4 us -> 14 us  [send_next(): return lax.ppermute(x, 'blk', forward)]
    ppermute x20 -> x23, starting transfers between devices: 22.2 us -> 28.9 us  [send_next(): return lax.ppermute(x, 'blk', forward)]
    ppermute x20 -> x23, waiting for transfers between devices: 9.74 us -> 13.8 us  [send_prev(): return lax.ppermute(x, 'blk', backward)]
    pallas_call x9 -> x6, Pallas kernels: 15.5 us -> 12.7 us  [the longest x5 12.1 us: expand(): pl.pallas_call(functools.partial(expand_kernel, pieces, len(theirs), firs...]
    unnamed x30 -> x24, local copies, waits for them, and re-layouts: 2.99 us -> 1.03 us
    ppermute x20 -> x23, starting transfers between devices: 25.3 us -> 24 us  [send_prev(): return lax.ppermute(x, 'blk', backward)]
    pallas_call x2 -> x4, Pallas kernels: 4.16 us -> 5.01 us  [contract(): pl.pallas_call(functools.partial(contract_kernel, part * columns), grid=(...]
  transfers between devices with their start and end apart: 59 -> 65, of which waited for: 33 -> 35; matrix products, arithmetic and copies ran while one was open for 1% -> 1% of each run, Pallas kernels for 18% -> 19%
where the time goes in v8:
time: 140 us; the launch traced here: 139 us
  starting transfers between devices  59.3 us (42%)
  Pallas kernels  39.1 us (28%)
  waiting for transfers between devices  32.8 us (23%)
  between operations  3.39 us (2%)
  other arithmetic  3.01 us (2%)
  local copies, waits for them, and re-layouts  1.82 us (1%)
    ppermute x23, starting transfers between devices, send_next(): return lax.ppermute(x, 'blk', forward)  28.9 us
    ppermute x23, starting transfers between devices, send_prev(): return lax.ppermute(x, 'blk', backward)  24 us
    pallas_call x2, Pallas kernels, attend(): pl.pallas_call(functools.partial(attend_kernel, table, order, heads, part...  14.1 us
    ppermute x23, waiting for transfers between devices, send_next(): return lax.ppermute(x, 'blk', forward)  14 us
    ppermute x23, waiting for transfers between devices, send_prev(): return lax.ppermute(x, 'blk', backward)  13.8 us
    pallas_call x5, Pallas kernels, expand(): pl.pallas_call(functools.partial(expand_kernel, pieces, len(theirs), firs...  12.1 us
    pallas_call x4, Pallas kernels, contract(): pl.pallas_call(functools.partial(contract_kernel, part * columns), grid=(...  5.01 us
    ppermute x15, starting transfers between devices, swap(): return lax.ppermute(x, 'head', exchange)  3.52 us
  transfers between devices with their start and end apart: 65, of which 35 were waited for; matrix products, arithmetic and copies ran while one was open for 1% of the time, Pallas kernels for 19%

profile of v8, /device:TPU:0, one launch (start us, length us, event | category | flops | bytes accessed | tf_op | source)
XLA Modules:
  0.0 139.3 jit_solution(7290843920562220595)
XLA Ops:
  2.4 8.2 %attend.2 = (s32[60]{0:T(128)S(1)}, bf16[32,2048]{1,0:T(8,128)(2,1)S(1)}, bf16[32,2048]{1,0:T(8,128)(2,1)S(1)}, bf16[32,2048]{1,0:T(8,128)(2,1)S(1)}, bf16[128,5...) custom-call(s32[26]{0:T(128)S(1)} %concatenate.51.refs_0_, bf16[64,18432]{1,0:T(8,128)(2,1)} %refs_1_.3, ...), custom_call_target="tpu_custom_call" | custom-call | flops 713031680 | bytes 4456448 | tf_op jit(solution)/shard_map/attend/pallas_call | solution.py:337
  10.6 3.1 %collective-permute-start.10 = (bf16[32,2048]{1,0:T(8,128)(2,1)S(1)}, bf16[32,2048]{1,0:T(8,128)(2,1)S(1)}, u32[]{:S(2)}, u32[]{:S(2)}) collective-permute-start(bf16[32,2048]{1,0:T(8,128)(2,1)S(1)} %get-tuple-element.189), channel_id=1, source_target_pairs={{0,4},{4,8},{8,12},{12,14},{14,10},{10,6},{6,2},{2,0},{1,5},{5,9},... | collective-permute-start | bytes 393224 | tf_op jit(solution)/shard_map/ppermute | solution.py:788
  15.2 3.0 %collective-permute-start.11 = (bf16[32,2048]{1,0:T(8,128)(2,1)S(1)}, bf16[32,2048]{1,0:T(8,128)(2,1)S(1)}, u32[]{:S(2)}, u32[]{:S(2)}) collective-permute-start(bf16[32,2048]{1,0:T(8,128)(2,1)S(1)} %get-tuple-element.204.refs_0_), channel_id=1, source_target_pairs={{4,0},{8,4},{12,8},{14,12},{10,14},{6,10},{2,6},{0,2},{5,1},{9,5},... | collective-permute-start | bytes 393224 | tf_op jit(solution)/shard_map/ppermute | solution.py:791
  18.9 5.9 %attend.3 = (bf16[32,2048]{1,0:T(8,128)(2,1)S(1)}, bf16[32,2048]{1,0:T(8,128)(2,1)S(1)}, bf16[32,2048]{1,0:T(8,128)(2,1)S(1)}) custom-call(s32[60]{0:T(128)S(1)} %get-tuple-element.164.tab.refs_0_, bf16[64,18432]{1,0:T(8,128)(2,1)} %refs_1_.3, bf16[8,576,256]{2,1,0:T(8,128)(2,1)} %refs_2_.3, bf16[64,576]{1,0:T(8,128)(2,1)S(1)} %bitcast.35, ...), custom_call_target="tpu_custom_call" | custom-call | flops 713031680 | bytes 4456448 | tf_op jit(solution)/shard_map/attend/pallas_call | solution.py:337
  24.8 1.6 %collective-permute-start.3 = (bf16[32,2048]{1,0:T(8,128)(2,1)S(1)}, bf16[32,2048]{1,0:T(8,128)(2,1)S(1)}, u32[]{:S(2)}, u32[]{:S(2)}) collective-permute-start(bf16[32,2048]{1,0:T(8,128)(2,1)S(1)} %get-tuple-element.179.refs_0_), channel_id=1, source_target_pairs={{4,0},{8,4},{12,8},{14,12},{10,14},{6,10},{2,6},{0,2},{5,1},{9,5},... | collective-permute-start | bytes 393224 | tf_op jit(solution)/shard_map/ppermute | solution.py:791
  27.5 2.5 %collective-permute-start.13 = (bf16[32,2048]{1,0:T(8,128)(2,1)S(1)}, bf16[32,2048]{1,0:T(8,128)(2,1)S(1)}, u32[]{:S(2)}, u32[]{:S(2)}) collective-permute-start(bf16[32,2048]{1,0:T(8,128)(2,1)S(1)} %broadcast_select_fusion.4), channel_id=1, source_target_pairs={{4,0},{8,4},{12,8},{14,12},{10,14},{6,10},{2,6},{0,2},{5,1},{9,5},... | collective-permute-start | bytes 393224 | tf_op jit(solution)/shard_map/ppermute | solution.py:791
  30.1 2.4 %collective-permute-done.2.refs_1_ = bf16[32,2048]{1,0:T(8,128)(2,1)S(1)} collective-permute-done((bf16[32,2048]{1,0:T(8,128)(2,1)S(1)}, bf16[32,2048]{1,0:T(8,128)(2,1)S(1)}, u32[]{:S(2)}, u32[]{:S(2)}) %collective-permute-start.2) | collective-permute-done | bytes 131104 | tf_op jit(solution)/shard_map/ppermute | solution.py:788
  32.5 1.4 collective-permute-start.19
  33.9 0.9 collective-permute-start.5
  35.1 2.0 %collective-permute-start.4 = (bf16[32,2048]{1,0:T(8,128)(2,1)S(1)}, bf16[32,2048]{1,0:T(8,128)(2,1)S(1)}, u32[]{:S(2)}, u32[]{:S(2)}) collective-permute-start(bf16[32,2048]{1,0:T(8,128)(2,1)S(1)} %broadcast_select_fusion.11), channel_id=1, source_target_pairs={{0,4},{4,8},{8,12},{12,14},{14,10},{10,6},{6,2},{2,0},{1,5},{5,9},... | collective-permute-start | bytes 393224 | tf_op jit(solution)/shard_map/ppermute | solution.py:788
  37.2 1.2 collective-permute-start.15
  38.4 0.9 collective-permute-start.14
  39.3 2.1 %collective-permute-done.19.refs_3_ = bf16[64,896]{1,0:T(8,128)(2,1)S(1)} collective-permute-done((bf16[64,896]{1,0:T(8,128)(2,1)S(1)}, bf16[64,896]{1,0:T(8,128)(2,1)S(1)}, u32[]{:S(2)}, u32[]{:S(2)}) %collective-permute-start.19) | collective-permute-done | bytes 114720 | tf_op jit(solution)/shard_map/ppermute | solution.py:815
  42.2 1.7 %collective-permute-start.7 = (bf16[32,2048]{1,0:T(8,128)(2,1)S(1)}, bf16[32,2048]{1,0:T(8,128)(2,1)S(1)}, u32[]{:S(2)}, u32[]{:S(2)}) collective-permute-start(bf16[32,2048]{1,0:T(8,128)(2,1)S(1)} %broadcast_select_fusion.8), channel_id=1, source_target_pairs={{4,0},{8,4},{12,8},{14,12},{10,14},{6,10},{2,6},{0,2},{5,1},{9,5},... | collective-permute-start | bytes 393224 | tf_op jit(solution)/shard_map/ppermute | solution.py:791
  45.0 1.4 collective-permute-start.16
  47.1 1.3 collective-permute-done.7.refs_7_
  48.4 1.8 %collective-permute-done.6.refs_3_ = bf16[32,2048]{1,0:T(8,128)(2,1)S(1)} collective-permute-done((bf16[32,2048]{1,0:T(8,128)(2,1)S(1)}, bf16[32,2048]{1,0:T(8,128)(2,1)S(1)}, u32[]{:S(2)}, u32[]{:S(2)}) %collective-permute-start.6) | collective-permute-done | bytes 131104 | tf_op jit(solution)/shard_map/ppermute | solution.py:788
  50.8 1.6 %collective-permute-start.9 = (bf16[32,2048]{1,0:T(8,128)(2,1)S(1)}, bf16[32,2048]{1,0:T(8,128)(2,1)S(1)}, u32[]{:S(2)}, u32[]{:S(2)}) collective-permute-start(bf16[32,2048]{1,0:T(8,128)(2,1)S(1)} %broadcast_select_fusion.6), channel_id=1, source_target_pairs={{4,0},{8,4},{12,8},{14,12},{10,14},{6,10},{2,6},{0,2},{5,1},{9,5},... | collective-permute-start | bytes 393224 | tf_op jit(solution)/shard_map/ppermute | solution.py:791
  53.1 1.9 %project.2.refs_10_ = f32[288,896]{1,0:T(8,128)S(1)} custom-call(s32[60]{0:T(128)S(1)} %get-tuple-element.164.tab.refs_0_, bf16[32,2048]{1,0:T(8,128)(2,1)S(1)} %get-tuple-element.204.refs_0_, bf16[32,2048]{1,0:T(8,128)(2,1)S(1)} %collective-permute-done.10.refs_1_, bf16[32,2048]{1,0:T(8,128)(2,1)S(1)} %collective-permute-done.12.refs_2_, ...), custom_call_target="tpu_custom_call" | custom-call | flops 1056964608 | bytes 4849664 | tf_op jit(solution)/shard_map/project/pallas_call | solution.py:482
  56.0 2.0 %project.3 = (f32[144,896]{1,0:T(8,128)S(1)}, bf16[144,896]{1,0:T(8,128)(2,1)S(1)}) custom-call(s32[60]{0:T(128)S(1)} %get-tuple-element.164.tab.refs_0_, bf16[32,2048]{1,0:T(8,128)(2,1)S(1)} %get-tuple-element.179.refs_0_, bf16[32,2048]{1,0:T(8,128)(2,1)S(1)} %collective-permute-done.2.refs_1_, bf16[32,2048]{1,0:T(8,128)(2,1)S(1)} %collective-permute-done.4.refs_2_, ...), custom_call_target="tpu_custom_call" | custom-call | flops 1056964608 | bytes 4849664 | tf_op jit(solution)/shard_map/project/pallas_call | solution.py:492
  58.7 0.9 collective-permute-done.21
  59.9 1.2 collective-permute-start.22
  61.0 0.9 collective-permute-start.23
  62.0 1.1 collective-permute-start.27
  63.1 0.9 collective-permute-start.28
  64.1 1.7 %expand.5 = (f32[288,576]{1,0:T(8,128)S(1)}, f32[288,576]{1,0:T(8,128)S(1)}, f32[288,1]{1,0:T(8,128)S(1)}) custom-call(s32[60]{0:T(128)S(1)} %get-tuple-element.164.tab.refs_0_, bf16[144,896]{1,0:T(8,128)(2,1)S(1)} %add_convert_fusion.refs_0_.refs_1_, bf16[144,896]{1,0:T(8,128)(2,1)S(1)} %collective-permute-done.24.refs_1_, f32[8,1,896]{2,1,0:T(1,128)S(1)} %bitcast.29, ...), custom_call_target="tpu_custom_call" | custom-call | flops 1 | bytes 1 | tf_op jit(solution)/shard_map/expand/pallas_call | solution.py:644
  66.5 1.1 collective-permute-done.23.refs_2_
  68.4 1.1 collective-permute-done.28.refs_3_
  69.6 1.8 %collective-permute-start.25 = (bf16[80,896]{1,0:T(8,128)(2,1)S(1)}, bf16[80,896]{1,0:T(8,128)(2,1)S(1)}, u32[]{:S(2)}, u32[]{:S(2)}) collective-permute-start(bf16[80,896]{1,0:T(8,128)(2,1)S(1)} %collective-permute-done.22.refs_0_), channel_id=1, source_target_pairs={{0,4},{4,8},{8,12},{12,14},{14,10},{10,6},{6,2},{2,0},{1,5},{5,9},... | collective-permute-start | bytes 430088 | tf_op jit(solution)/shard_map/ppermute | solution.py:788
  71.7 1.7 %collective-permute-start.33 = (bf16[64,896]{1,0:T(8,128)(2,1)S(1)}, bf16[64,896]{1,0:T(8,128)(2,1)S(1)}, u32[]{:S(2)}, u32[]{:S(2)}) collective-permute-start(bf16[64,896]{1,0:T(8,128)(2,1)S(1)} %collective-permute-done.27.refs_1_), channel_id=1, source_target_pairs={{0,4},{4,8},{8,12},{12,14},{14,10},{10,6},{6,2},{2,0},{1,5},{5,9},... | collective-permute-start | bytes 344072 | tf_op jit(solution)/shard_map/ppermute | solution.py:788
  73.7 2.9 %expand.6 = (f32[288,576]{1,0:T(8,128)S(1)}, f32[288,576]{1,0:T(8,128)S(1)}, f32[288,1]{1,0:T(8,128)S(1)}) custom-call(s32[60]{0:T(128)S(1)} %get-tuple-element.164.tab.refs_0_, bf16[80,896]{1,0:T(8,128)(2,1)S(1)} %collective-permute-done.22.refs_0_, bf16[64,896]{1,0:T(8,128)(2,1)S(1)} %collective-permute-done.27.refs_1_, ...), custom_call_target="tpu_custom_call" | custom-call | flops 1 | bytes 1 | tf_op jit(solution)/shard_map/expand/pallas_call | solution.py:644
  76.6 1.4 %collective-permute-done.26.refs_2_ = bf16[80,896]{1,0:T(8,128)(2,1)S(1)} collective-permute-done((bf16[80,896]{1,0:T(8,128)(2,1)S(1)}, bf16[80,896]{1,0:T(8,128)(2,1)S(1)}, u32[]{:S(2)}, u32[]{:S(2)}) %collective-permute-start.26) | collective-permute-done | bytes 143392 | tf_op jit(solution)/shard_map/ppermute | solution.py:791
  78.2 1.5 %collective-permute-done.34.refs_3_ = bf16[64,896]{1,0:T(8,128)(2,1)S(1)} collective-permute-done((bf16[64,896]{1,0:T(8,128)(2,1)S(1)}, bf16[64,896]{1,0:T(8,128)(2,1)S(1)}, u32[]{:S(2)}, u32[]{:S(2)}) %collective-permute-start.34) | collective-permute-done | bytes 114720 | tf_op jit(solution)/shard_map/ppermute | solution.py:791
  80.4 0.9 collective-permute-start.31
  81.3 1.1 collective-permute-start.32
  82.7 1.7 %collective-permute-start.40 = (bf16[64,896]{1,0:T(8,128)(2,1)S(1)}, bf16[64,896]{1,0:T(8,128)(2,1)S(1)}, u32[]{:S(2)}, u32[]{:S(2)}) collective-permute-start(bf16[64,896]{1,0:T(8,128)(2,1)S(1)} %collective-permute-done.33.refs_1_), channel_id=1, source_target_pairs={{0,4},{4,8},{8,12},{12,14},{14,10},{10,6},{6,2},{2,0},{1,5},{5,9},... | collective-permute-start | bytes 344072 | tf_op jit(solution)/shard_map/ppermute | solution.py:788
  84.4 2.9 %expand.7 = (f32[288,576]{1,0:T(8,128)S(1)}, f32[288,576]{1,0:T(8,128)S(1)}, f32[288,1]{1,0:T(8,128)S(1)}) custom-call(s32[60]{0:T(128)S(1)} %get-tuple-element.164.tab.refs_0_, bf16[80,896]{1,0:T(8,128)(2,1)S(1)} %collective-permute-done.25.refs_0_, bf16[64,896]{1,0:T(8,128)(2,1)S(1)} %collective-permute-done.33.refs_1_, ...), custom_call_target="tpu_custom_call" | custom-call | flops 1 | bytes 1 | tf_op jit(solution)/shard_map/expand/pallas_call | solution.py:644
  88.0 1.3 collective-permute-done.38.refs_3_
  90.4 1.5 %collective-permute-start.39 = (bf16[64,896]{1,0:T(8,128)(2,1)S(1)}, bf16[64,896]{1,0:T(8,128)(2,1)S(1)}, u32[]{:S(2)}, u32[]{:S(2)}) collective-permute-start(bf16[64,896]{1,0:T(8,128)(2,1)S(1)} %collective-permute-done.38.refs_3_), channel_id=1, source_target_pairs={{4,0},{8,4},{12,8},{14,12},{10,14},{6,10},{2,6},{0,2},{5,1},{9,5},... | collective-permute-start | bytes 344072 | tf_op jit(solution)/shard_map/ppermute | solution.py:791
  91.9 2.9 %expand.8 = (f32[288,576]{1,0:T(8,128)S(1)}, f32[288,576]{1,0:T(8,128)S(1)}, f32[288,1]{1,0:T(8,128)S(1)}) custom-call(s32[60]{0:T(128)S(1)} %get-tuple-element.164.tab.refs_0_, bf16[80,896]{1,0:T(8,128)(2,1)S(1)} %collective-permute-done.31.refs_0_, bf16[64,896]{1,0:T(8,128)(2,1)S(1)} %collective-permute-done.40.refs_1_, ...), custom_call_target="tpu_custom_call" | custom-call | flops 1 | bytes 1 | tf_op jit(solution)/shard_map/expand/pallas_call | solution.py:644
  96.2 1.0 collective-permute-done.44.refs_3_
  97.2 1.8 %expand.9.hidden = bf16[288,576]{1,0:T(8,128)(2,1)S(1)} custom-call(s32[60]{0:T(128)S(1)} %get-tuple-element.164.tab.refs_0_, bf16[80,896]{1,0:T(8,128)(2,1)S(1)} %collective-permute-done.37.refs_0_, bf16[64,896]{1,0:T(8,128)(2,1)S(1)} %collective-permute-done.39.refs_1_, bf16[80,896]{1,0:T(8,128)(2,1)S(1)} %collective-permute-done.43.refs_2_, ...), custom_call_target="tpu_custom_call" | custom-call | flops 1 | bytes 1 | tf_op jit(solution)/shard_map/expand/pallas_call | solution.py:644
  99.1 1.2 contract.7
  100.7 1.2 contract.5
  103.0 1.3 contract.6.mine
  105.1 1.2 collective-permute-start.57
  106.3 1.3 contract.4.mine
  107.6 1.0 collective-permute-start.56
  109.4 1.2 collective-permute-start.47
  110.5 0.9 collective-permute-start.46
  111.5 1.2 collective-permute-done.56
  113.6 1.2 collective-permute-start.58
  114.9 0.9 collective-permute-done.46
  115.9 1.5 %collective-permute-start.49 = (bf16[16,3584]{1,0:T(8,128)(2,1)S(1)}, bf16[16,3584]{1,0:T(8,128)(2,1)S(1)}, u32[]{:S(2)}, u32[]{:S(2)}) collective-permute-start(bf16[16,3584]{1,0:T(8,128)(2,1)S(1)} %add_convert_fusion.11), channel_id=1, source_target_pairs={{4,0},{8,4},{12,8},{14,12},{10,14},{6,10},{2,6},{0,2},{5,1},{9,5},... | collective-permute-start | bytes 344072 | tf_op jit(solution)/shard_map/ppermute | solution.py:791
  118.6 1.0 collective-permute-done.58
  119.9 1.8 %collective-permute-start.60 = (bf16[16,3584]{1,0:T(8,128)(2,1)S(1)}, bf16[16,3584]{1,0:T(8,128)(2,1)S(1)}, u32[]{:S(2)}, u32[]{:S(2)}) collective-permute-start(bf16[16,3584]{1,0:T(8,128)(2,1)S(1)} %add_convert_fusion.4), channel_id=1, source_target_pairs={{0,4},{4,8},{8,12},{12,14},{14,10},{10,6},{6,2},{2,0},{1,5},{5,9},... | collective-permute-start | bytes 344072 | tf_op jit(solution)/shard_map/ppermute | solution.py:788
  122.9 1.7 %collective-permute-start.50 = (bf16[16,3584]{1,0:T(8,128)(2,1)S(1)}, bf16[16,3584]{1,0:T(8,128)(2,1)S(1)}, u32[]{:S(2)}, u32[]{:S(2)}) collective-permute-start(bf16[16,3584]{1,0:T(8,128)(2,1)S(1)} %add_convert_fusion.10), channel_id=1, source_target_pairs={{0,4},{4,8},{8,12},{12,14},{14,10},{10,6},{6,2},{2,0},{1,5},{5,9},... | collective-permute-start | bytes 344072 | tf_op jit(solution)/shard_map/ppermute | solution.py:788
  125.4 2.0 %collective-permute-start.62 = (bf16[16,3584]{1,0:T(8,128)(2,1)S(1)}, bf16[16,3584]{1,0:T(8,128)(2,1)S(1)}, u32[]{:S(2)}, u32[]{:S(2)}) collective-permute-start(bf16[16,3584]{1,0:T(8,128)(2,1)S(1)} %add_convert_fusion.2), channel_id=1, source_target_pairs={{0,4},{4,8},{8,12},{12,14},{14,10},{10,6},{6,2},{2,0},{1,5},{5,9},... | collective-permute-start | bytes 344072 | tf_op jit(solution)/shard_map/ppermute | solution.py:788
  127.5 1.0 collective-permute-done.51
  128.5 2.0 %collective-permute-start.52 = (bf16[16,3584]{1,0:T(8,128)(2,1)S(1)}, bf16[16,3584]{1,0:T(8,128)(2,1)S(1)}, u32[]{:S(2)}, u32[]{:S(2)}) collective-permute-start(bf16[16,3584]{1,0:T(8,128)(2,1)S(1)} %add_convert_fusion.8), channel_id=1, source_target_pairs={{0,4},{4,8},{8,12},{12,14},{14,10},{10,6},{6,2},{2,0},{1,5},{5,9},... | collective-permute-start | bytes 344072 | tf_op jit(solution)/shard_map/ppermute | solution.py:788
  132.1 1.2 collective-permute-done.52
  133.4 1.9 %collective-permute-done.53 = bf16[16,3584]{1,0:T(8,128)(2,1)S(1)} collective-permute-done((bf16[16,3584]{1,0:T(8,128)(2,1)S(1)}, bf16[16,3584]{1,0:T(8,128)(2,1)S(1)}, u32[]{:S(2)}, u32[]{:S(2)}) %collective-permute-start.53) | collective-permute-done | bytes 114720 | tf_op jit(solution)/shard_map/ppermute | solution.py:791
  137.5 0.9 collective-permute-done.64
  138.4 0.9 maximum_select_fusion
  (164 shorter events, 27.4 us)
Async XLA Ops:
  10.6 16.3 %collective-permute-start.10 = (bf16[32,2048]{1,0:T(8,128)(2,1)S(1)}, bf16[32,2048]{1,0:T(8,128)(2,1)S(1)}, u32[]{:S(2)}, u32[]{:S(2)}) collective-permute-start(bf16[32,2048]{1,0:T(8,128)(2,1)S(1)} %get-tuple-element.189), channel_id=1, source_target_pairs={{0,4},{4,8},{8,12},{12,14},{14,10},{10,6},{6,2},{2,0},{1,5},{5,9},... | collective-permute-start | bytes 393224 | tf_op jit(solution)/shard_map/ppermute | solution.py:788
  14.3 10.5 %collective-permute-start = (bf16[64,896]{1,0:T(8,128)(2,1)S(1)}, bf16[64,896]{1,0:T(8,128)(2,1)S(1)}, u32[]{:S(2)}, u32[]{:S(2)}) collective-permute-start(bf16[64,896]{1,0:T(8,128)(2,1)S(1)} %get-tuple-element.199.own), channel_id=1, source_target_pairs={{1,9},{3,11},{5,13},{7,15},{9,1},{11,3},{13,5},{15,7},{17,25},{19,... | collective-permute-start | bytes 344072 | tf_op jit(solution)/shard_map/ppermute | solution.py:815
  15.1 9.7 %collective-permute-start.1 = (bf16[64,896]{1,0:T(8,128)(2,1)S(1)}, bf16[64,896]{1,0:T(8,128)(2,1)S(1)}, u32[]{:S(2)}, u32[]{:S(2)}) collective-permute-start(bf16[64,896]{1,0:T(8,128)(2,1)S(1)} %get-tuple-element.167), channel_id=1, source_target_pairs={{0,2},{1,11},{2,4},{3,13},{4,6},{5,15},{6,8},{7,1},{8,10},{9,3},{1... | collective-permute-start | bytes 344072 | tf_op jit(solution)/shard_map/ppermute | solution.py:815
  15.2 11.7 %collective-permute-start.11 = (bf16[32,2048]{1,0:T(8,128)(2,1)S(1)}, bf16[32,2048]{1,0:T(8,128)(2,1)S(1)}, u32[]{:S(2)}, u32[]{:S(2)}) collective-permute-start(bf16[32,2048]{1,0:T(8,128)(2,1)S(1)} %get-tuple-element.204.refs_0_), channel_id=1, source_target_pairs={{4,0},{8,4},{12,8},{14,12},{10,14},{6,10},{2,6},{0,2},{5,1},{9,5},... | collective-permute-start | bytes 393224 | tf_op jit(solution)/shard_map/ppermute | solution.py:791
  24.8 7.7 %collective-permute-start.3 = (bf16[32,2048]{1,0:T(8,128)(2,1)S(1)}, bf16[32,2048]{1,0:T(8,128)(2,1)S(1)}, u32[]{:S(2)}, u32[]{:S(2)}) collective-permute-start(bf16[32,2048]{1,0:T(8,128)(2,1)S(1)} %get-tuple-element.179.refs_0_), channel_id=1, source_target_pairs={{4,0},{8,4},{12,8},{14,12},{10,14},{6,10},{2,6},{0,2},{5,1},{9,5},... | collective-permute-start | bytes 393224 | tf_op jit(solution)/shard_map/ppermute | solution.py:791
  26.4 6.1 %collective-permute-start.2 = (bf16[32,2048]{1,0:T(8,128)(2,1)S(1)}, bf16[32,2048]{1,0:T(8,128)(2,1)S(1)}, u32[]{:S(2)}, u32[]{:S(2)}) collective-permute-start(bf16[32,2048]{1,0:T(8,128)(2,1)S(1)} %get-tuple-element.176), channel_id=1, source_target_pairs={{0,4},{4,8},{8,12},{12,14},{14,10},{10,6},{6,2},{2,0},{1,5},{5,9},... | collective-permute-start | bytes 393224 | tf_op jit(solution)/shard_map/ppermute | solution.py:788
  26.9 11.4 %collective-permute-start.18 = (bf16[64,896]{1,0:T(8,128)(2,1)S(1)}, bf16[64,896]{1,0:T(8,128)(2,1)S(1)}, u32[]{:S(2)}, u32[]{:S(2)}) collective-permute-start(bf16[64,896]{1,0:T(8,128)(2,1)S(1)} %get-tuple-element.202), channel_id=1, source_target_pairs={{0,4},{1,13},{2,6},{3,15},{4,8},{5,1},{6,10},{7,3},{8,12},{9,5},{1... | collective-permute-start | bytes 344072 | tf_op jit(solution)/shard_map/ppermute | solution.py:815
  27.5 7.6 %collective-permute-start.13 = (bf16[32,2048]{1,0:T(8,128)(2,1)S(1)}, bf16[32,2048]{1,0:T(8,128)(2,1)S(1)}, u32[]{:S(2)}, u32[]{:S(2)}) collective-permute-start(bf16[32,2048]{1,0:T(8,128)(2,1)S(1)} %broadcast_select_fusion.4), channel_id=1, source_target_pairs={{4,0},{8,4},{12,8},{14,12},{10,14},{6,10},{2,6},{0,2},{5,1},{9,5},... | collective-permute-start | bytes 393224 | tf_op jit(solution)/shard_map/ppermute | solution.py:791
  30.1 7.0 %collective-permute-start.12 = (bf16[32,2048]{1,0:T(8,128)(2,1)S(1)}, bf16[32,2048]{1,0:T(8,128)(2,1)S(1)}, u32[]{:S(2)}, u32[]{:S(2)}) collective-permute-start(bf16[32,2048]{1,0:T(8,128)(2,1)S(1)} %broadcast_select_fusion.5), channel_id=1, source_target_pairs={{0,4},{4,8},{8,12},{12,14},{14,10},{10,6},{6,2},{2,0},{1,5},{5,9},... | collective-permute-start | bytes 393224 | tf_op jit(solution)/shard_map/ppermute | solution.py:788
  32.5 8.8 %collective-permute-start.19 = (bf16[64,896]{1,0:T(8,128)(2,1)S(1)}, bf16[64,896]{1,0:T(8,128)(2,1)S(1)}, u32[]{:S(2)}, u32[]{:S(2)}) collective-permute-start(bf16[64,896]{1,0:T(8,128)(2,1)S(1)} %get-tuple-element.203), channel_id=1, source_target_pairs={{0,6},{1,15},{2,8},{3,1},{4,10},{5,3},{6,12},{7,5},{8,14},{9,7},{1... | collective-permute-start | bytes 344072 | tf_op jit(solution)/shard_map/ppermute | solution.py:815
  33.9 8.1 %collective-permute-start.5 = (bf16[32,2048]{1,0:T(8,128)(2,1)S(1)}, bf16[32,2048]{1,0:T(8,128)(2,1)S(1)}, u32[]{:S(2)}, u32[]{:S(2)}) collective-permute-start(bf16[32,2048]{1,0:T(8,128)(2,1)S(1)} %broadcast_select_fusion.10), channel_id=1, source_target_pairs={{4,0},{8,4},{12,8},{14,12},{10,14},{6,10},{2,6},{0,2},{5,1},{9,5},... | collective-permute-start | bytes 393224 | tf_op jit(solution)/shard_map/ppermute | solution.py:791
  35.1 7.1 %collective-permute-start.4 = (bf16[32,2048]{1,0:T(8,128)(2,1)S(1)}, bf16[32,2048]{1,0:T(8,128)(2,1)S(1)}, u32[]{:S(2)}, u32[]{:S(2)}) collective-permute-start(bf16[32,2048]{1,0:T(8,128)(2,1)S(1)} %broadcast_select_fusion.11), channel_id=1, source_target_pairs={{0,4},{4,8},{8,12},{12,14},{14,10},{10,6},{6,2},{2,0},{1,5},{5,9},... | collective-permute-start | bytes 393224 | tf_op jit(solution)/shard_map/ppermute | solution.py:788
  37.2 7.2 %collective-permute-start.15 = (bf16[32,2048]{1,0:T(8,128)(2,1)S(1)}, bf16[32,2048]{1,0:T(8,128)(2,1)S(1)}, u32[]{:S(2)}, u32[]{:S(2)}) collective-permute-start(bf16[32,2048]{1,0:T(8,128)(2,1)S(1)} %broadcast_select_fusion.2), channel_id=1, source_target_pairs={{4,0},{8,4},{12,8},{14,12},{10,14},{6,10},{2,6},{0,2},{5,1},{9,5},... | collective-permute-start | bytes 393224 | tf_op jit(solution)/shard_map/ppermute | solution.py:791
  38.4 6.7 %collective-permute-start.14 = (bf16[32,2048]{1,0:T(8,128)(2,1)S(1)}, bf16[32,2048]{1,0:T(8,128)(2,1)S(1)}, u32[]{:S(2)}, u32[]{:S(2)}) collective-permute-start(bf16[32,2048]{1,0:T(8,128)(2,1)S(1)} %broadcast_select_fusion.3), channel_id=1, source_target_pairs={{0,4},{4,8},{8,12},{12,14},{14,10},{10,6},{6,2},{2,0},{1,5},{5,9},... | collective-permute-start | bytes 393224 | tf_op jit(solution)/shard_map/ppermute | solution.py:788
  41.9 11.1 %collective-permute-start.20 = (bf16[128,896]{1,0:T(8,128)(2,1)S(1)}, bf16[128,896]{1,0:T(8,128)(2,1)S(1)}, u32[]{:S(2)}, u32[]{:S(2)}) collective-permute-start(bf16[128,896]{1,0:T(8,128)(2,1)S(1)} %share.1), channel_id=1, source_target_pairs={{0,1},{1,0},{2,3},{3,2},{4,5},{5,4},{6,7},{7,6},{8,9},{9,8},{10,11... | collective-permute-start | bytes 688136 | tf_op jit(solution)/shard_map/ppermute | solution.py:794
  42.2 6.2 %collective-permute-start.7 = (bf16[32,2048]{1,0:T(8,128)(2,1)S(1)}, bf16[32,2048]{1,0:T(8,128)(2,1)S(1)}, u32[]{:S(2)}, u32[]{:S(2)}) collective-permute-start(bf16[32,2048]{1,0:T(8,128)(2,1)S(1)} %broadcast_select_fusion.8), channel_id=1, source_target_pairs={{4,0},{8,4},{12,8},{14,12},{10,14},{6,10},{2,6},{0,2},{5,1},{9,5},... | collective-permute-start | bytes 393224 | tf_op jit(solution)/shard_map/ppermute | solution.py:791
  43.9 6.3 %collective-permute-start.6 = (bf16[32,2048]{1,0:T(8,128)(2,1)S(1)}, bf16[32,2048]{1,0:T(8,128)(2,1)S(1)}, u32[]{:S(2)}, u32[]{:S(2)}) collective-permute-start(bf16[32,2048]{1,0:T(8,128)(2,1)S(1)} %broadcast_select_fusion.9), channel_id=1, source_target_pairs={{0,4},{4,8},{8,12},{12,14},{14,10},{10,6},{6,2},{2,0},{1,5},{5,9},... | collective-permute-start | bytes 393224 | tf_op jit(solution)/shard_map/ppermute | solution.py:788
  45.0 8.0 %collective-permute-start.16 = (bf16[32,2048]{1,0:T(8,128)(2,1)S(1)}, bf16[32,2048]{1,0:T(8,128)(2,1)S(1)}, u32[]{:S(2)}, u32[]{:S(2)}) collective-permute-start(bf16[32,2048]{1,0:T(8,128)(2,1)S(1)} %broadcast_select_fusion.1), channel_id=1, source_target_pairs={{0,4},{4,8},{8,12},{12,14},{14,10},{10,6},{6,2},{2,0},{1,5},{5,9},... | collective-permute-start | bytes 393224 | tf_op jit(solution)/shard_map/ppermute | solution.py:788
  46.4 6.6 %collective-permute-start.17 = (bf16[32,2048]{1,0:T(8,128)(2,1)S(1)}, bf16[32,2048]{1,0:T(8,128)(2,1)S(1)}, u32[]{:S(2)}, u32[]{:S(2)}) collective-permute-start(bf16[32,2048]{1,0:T(8,128)(2,1)S(1)} %broadcast_select_fusion), channel_id=1, source_target_pairs={{4,0},{8,4},{12,8},{14,12},{10,14},{6,10},{2,6},{0,2},{5,1},{9,5},... | collective-permute-start | bytes 393224 | tf_op jit(solution)/shard_map/ppermute | solution.py:791
  50.2 5.2 %collective-permute-start.8 = (bf16[32,2048]{1,0:T(8,128)(2,1)S(1)}, bf16[32,2048]{1,0:T(8,128)(2,1)S(1)}, u32[]{:S(2)}, u32[]{:S(2)}) collective-permute-start(bf16[32,2048]{1,0:T(8,128)(2,1)S(1)} %broadcast_select_fusion.7), channel_id=1, source_target_pairs={{0,4},{4,8},{8,12},{12,14},{14,10},{10,6},{6,2},{2,0},{1,5},{5,9},... | collective-permute-start | bytes 393224 | tf_op jit(solution)/shard_map/ppermute | solution.py:788
  50.8 5.2 %collective-permute-start.9 = (bf16[32,2048]{1,0:T(8,128)(2,1)S(1)}, bf16[32,2048]{1,0:T(8,128)(2,1)S(1)}, u32[]{:S(2)}, u32[]{:S(2)}) collective-permute-start(bf16[32,2048]{1,0:T(8,128)(2,1)S(1)} %broadcast_select_fusion.6), channel_id=1, source_target_pairs={{4,0},{8,4},{12,8},{14,12},{10,14},{6,10},{2,6},{0,2},{5,1},{9,5},... | collective-permute-start | bytes 393224 | tf_op jit(solution)/shard_map/ppermute | solution.py:791
  58.0 1.6 %collective-permute-start.21 = (bf16[144,896]{1,0:T(8,128)(2,1)S(1)}, bf16[144,896]{1,0:T(8,128)(2,1)S(1)}, u32[]{:S(2)}, u32[]{:S(2)}) collective-permute-start(bf16[144,896]{1,0:T(8,128)(2,1)S(1)} %get-tuple-element.216), channel_id=1, source_target_pairs={{0,1},{1,0},{2,3},{3,2},{4,5},{5,4},{6,7},{7,6},{8,9},{9,8},{10,11... | collective-permute-start | bytes 774152 | tf_op jit(solution)/shard_map/ppermute | solution.py:794
  59.7 2.3 %collective-permute-start.24 = (bf16[144,896]{1,0:T(8,128)(2,1)S(1)}, bf16[144,896]{1,0:T(8,128)(2,1)S(1)}, u32[]{:S(2)}, u32[]{:S(2)}) collective-permute-start(bf16[144,896]{1,0:T(8,128)(2,1)S(1)} %add_convert_fusion.refs_0_.refs_1_), channel_id=1, source_target_pairs={{0,1},{1,0},{2,3},{3,2},{4,5},{5,4},{6,7},{7,6},{8,9},{9,8},{10,11... | collective-permute-start | bytes 774152 | tf_op jit(solution)/shard_map/ppermute | solution.py:794
  59.9 6.6 %collective-permute-start.22 = (bf16[80,896]{1,0:T(8,128)(2,1)S(1)}, bf16[80,896]{1,0:T(8,128)(2,1)S(1)}, u32[]{:S(2)}, u32[]{:S(2)}) collective-permute-start(bf16[80,896]{1,0:T(8,128)(2,1)S(1)} %slice.24), channel_id=1, source_target_pairs={{0,4},{4,8},{8,12},{12,14},{14,10},{10,6},{6,2},{2,0},{1,5},{5,9},... | collective-permute-start | bytes 430088 | tf_op jit(solution)/shard_map/ppermute | solution.py:788
  61.0 6.6 %collective-permute-start.23 = (bf16[80,896]{1,0:T(8,128)(2,1)S(1)}, bf16[80,896]{1,0:T(8,128)(2,1)S(1)}, u32[]{:S(2)}, u32[]{:S(2)}) collective-permute-start(bf16[80,896]{1,0:T(8,128)(2,1)S(1)} %slice.24), channel_id=1, source_target_pairs={{4,0},{8,4},{12,8},{14,12},{10,14},{6,10},{2,6},{0,2},{5,1},{9,5},... | collective-permute-start | bytes 430088 | tf_op jit(solution)/shard_map/ppermute | solution.py:791
  62.0 6.4 %collective-permute-start.27 = (bf16[64,896]{1,0:T(8,128)(2,1)S(1)}, bf16[64,896]{1,0:T(8,128)(2,1)S(1)}, u32[]{:S(2)}, u32[]{:S(2)}) collective-permute-start(bf16[64,896]{1,0:T(8,128)(2,1)S(1)} %slice.25), channel_id=1, source_target_pairs={{0,4},{4,8},{8,12},{12,14},{14,10},{10,6},{6,2},{2,0},{1,5},{5,9},... | collective-permute-start | bytes 344072 | tf_op jit(solution)/shard_map/ppermute | solution.py:788
  63.1 6.4 %collective-permute-start.28 = (bf16[64,896]{1,0:T(8,128)(2,1)S(1)}, bf16[64,896]{1,0:T(8,128)(2,1)S(1)}, u32[]{:S(2)}, u32[]{:S(2)}) collective-permute-start(bf16[64,896]{1,0:T(8,128)(2,1)S(1)} %slice.25), channel_id=1, source_target_pairs={{4,0},{8,4},{12,8},{14,12},{10,14},{6,10},{2,6},{0,2},{5,1},{9,5},... | collective-permute-start | bytes 344072 | tf_op jit(solution)/shard_map/ppermute | solution.py:791
  67.6 5.8 %collective-permute-start.29 = (bf16[160,896]{1,0:T(8,128)(2,1)S(1)}, bf16[160,896]{1,0:T(8,128)(2,1)S(1)}, u32[]{:S(2)}, u32[]{:S(2)}) collective-permute-start(bf16[160,896]{1,0:T(8,128)(2,1)S(1)} %pad_maximum_fusion), channel_id=1, source_target_pairs={{0,1},{1,0},{2,3},{3,2},{4,5},{5,4},{6,7},{7,6},{8,9},{9,8},{10,11... | collective-permute-start | bytes 860168 | tf_op jit(solution)/shard_map/ppermute | solution.py:794
  69.5 4.2 %collective-permute-start.30 = (bf16[128,896]{1,0:T(8,128)(2,1)S(1)}, bf16[128,896]{1,0:T(8,128)(2,1)S(1)}, u32[]{:S(2)}, u32[]{:S(2)}) collective-permute-start(bf16[128,896]{1,0:T(8,128)(2,1)S(1)} %pad_maximum_fusion.10), channel_id=1, source_target_pairs={{0,1},{1,0},{2,3},{3,2},{4,5},{5,4},{6,7},{7,6},{8,9},{9,8},{10,11... | collective-permute-start | bytes 688136 | tf_op jit(solution)/shard_map/ppermute | solution.py:794
  69.6 7.0 %collective-permute-start.25 = (bf16[80,896]{1,0:T(8,128)(2,1)S(1)}, bf16[80,896]{1,0:T(8,128)(2,1)S(1)}, u32[]{:S(2)}, u32[]{:S(2)}) collective-permute-start(bf16[80,896]{1,0:T(8,128)(2,1)S(1)} %collective-permute-done.22.refs_0_), channel_id=1, source_target_pairs={{0,4},{4,8},{8,12},{12,14},{14,10},{10,6},{6,2},{2,0},{1,5},{5,9},... | collective-permute-start | bytes 430088 | tf_op jit(solution)/shard_map/ppermute | solution.py:788
  71.4 6.6 %collective-permute-start.26 = (bf16[80,896]{1,0:T(8,128)(2,1)S(1)}, bf16[80,896]{1,0:T(8,128)(2,1)S(1)}, u32[]{:S(2)}, u32[]{:S(2)}) collective-permute-start(bf16[80,896]{1,0:T(8,128)(2,1)S(1)} %collective-permute-done.23.refs_2_), channel_id=1, source_target_pairs={{4,0},{8,4},{12,8},{14,12},{10,14},{6,10},{2,6},{0,2},{5,1},{9,5},... | collective-permute-start | bytes 430088 | tf_op jit(solution)/shard_map/ppermute | solution.py:791
  71.7 6.5 %collective-permute-start.33 = (bf16[64,896]{1,0:T(8,128)(2,1)S(1)}, bf16[64,896]{1,0:T(8,128)(2,1)S(1)}, u32[]{:S(2)}, u32[]{:S(2)}) collective-permute-start(bf16[64,896]{1,0:T(8,128)(2,1)S(1)} %collective-permute-done.27.refs_1_), channel_id=1, source_target_pairs={{0,4},{4,8},{8,12},{12,14},{14,10},{10,6},{6,2},{2,0},{1,5},{5,9},... | collective-permute-start | bytes 344072 | tf_op jit(solution)/shard_map/ppermute | solution.py:788
  73.4 6.3 %collective-permute-start.34 = (bf16[64,896]{1,0:T(8,128)(2,1)S(1)}, bf16[64,896]{1,0:T(8,128)(2,1)S(1)}, u32[]{:S(2)}, u32[]{:S(2)}) collective-permute-start(bf16[64,896]{1,0:T(8,128)(2,1)S(1)} %collective-permute-done.28.refs_3_), channel_id=1, source_target_pairs={{4,0},{8,4},{12,8},{14,12},{10,14},{6,10},{2,6},{0,2},{5,1},{9,5},... | collective-permute-start | bytes 344072 | tf_op jit(solution)/shard_map/ppermute | solution.py:791
  79.7 3.0 %collective-permute-start.36 = (bf16[128,896]{1,0:T(8,128)(2,1)S(1)}, bf16[128,896]{1,0:T(8,128)(2,1)S(1)}, u32[]{:S(2)}, u32[]{:S(2)}) collective-permute-start(bf16[128,896]{1,0:T(8,128)(2,1)S(1)} %pad_maximum_fusion.11), channel_id=1, source_target_pairs={{0,1},{1,0},{2,3},{3,2},{4,5},{5,4},{6,7},{7,6},{8,9},{9,8},{10,11... | collective-permute-start | bytes 688136 | tf_op jit(solution)/shard_map/ppermute | solution.py:794
  79.8 4.6 %collective-permute-start.35 = (bf16[160,896]{1,0:T(8,128)(2,1)S(1)}, bf16[160,896]{1,0:T(8,128)(2,1)S(1)}, u32[]{:S(2)}, u32[]{:S(2)}) collective-permute-start(bf16[160,896]{1,0:T(8,128)(2,1)S(1)} %pad_maximum_fusion.1), channel_id=1, source_target_pairs={{0,1},{1,0},{2,3},{3,2},{4,5},{5,4},{6,7},{7,6},{8,9},{9,8},{10,11... | collective-permute-start | bytes 860168 | tf_op jit(solution)/shard_map/ppermute | solution.py:794
  80.4 7.0 %collective-permute-start.31 = (bf16[80,896]{1,0:T(8,128)(2,1)S(1)}, bf16[80,896]{1,0:T(8,128)(2,1)S(1)}, u32[]{:S(2)}, u32[]{:S(2)}) collective-permute-start(bf16[80,896]{1,0:T(8,128)(2,1)S(1)} %collective-permute-done.25.refs_0_), channel_id=1, source_target_pairs={{0,4},{4,8},{8,12},{12,14},{14,10},{10,6},{6,2},{2,0},{1,5},{5,9},... | collective-permute-start | bytes 430088 | tf_op jit(solution)/shard_map/ppermute | solution.py:788
  81.3 6.7 %collective-permute-start.32 = (bf16[80,896]{1,0:T(8,128)(2,1)S(1)}, bf16[80,896]{1,0:T(8,128)(2,1)S(1)}, u32[]{:S(2)}, u32[]{:S(2)}) collective-permute-start(bf16[80,896]{1,0:T(8,128)(2,1)S(1)} %collective-permute-done.26.refs_2_), channel_id=1, source_target_pairs={{4,0},{8,4},{12,8},{14,12},{10,14},{6,10},{2,6},{0,2},{5,1},{9,5},... | collective-permute-start | bytes 430088 | tf_op jit(solution)/shard_map/ppermute | solution.py:791
  82.4 6.8 %collective-permute-start.38 = (bf16[64,896]{1,0:T(8,128)(2,1)S(1)}, bf16[64,896]{1,0:T(8,128)(2,1)S(1)}, u32[]{:S(2)}, u32[]{:S(2)}) collective-permute-start(bf16[64,896]{1,0:T(8,128)(2,1)S(1)} %collective-permute-done.34.refs_3_), channel_id=1, source_target_pairs={{4,0},{8,4},{12,8},{14,12},{10,14},{6,10},{2,6},{0,2},{5,1},{9,5},... | collective-permute-start | bytes 344072 | tf_op jit(solution)/shard_map/ppermute | solution.py:791
  82.7 6.5 %collective-permute-start.40 = (bf16[64,896]{1,0:T(8,128)(2,1)S(1)}, bf16[64,896]{1,0:T(8,128)(2,1)S(1)}, u32[]{:S(2)}, u32[]{:S(2)}) collective-permute-start(bf16[64,896]{1,0:T(8,128)(2,1)S(1)} %collective-permute-done.33.refs_1_), channel_id=1, source_target_pairs={{0,4},{4,8},{8,12},{12,14},{14,10},{10,6},{6,2},{2,0},{1,5},{5,9},... | collective-permute-start | bytes 344072 | tf_op jit(solution)/shard_map/ppermute | solution.py:788
  89.2 2.7 %collective-permute-start.41 = (bf16[160,896]{1,0:T(8,128)(2,1)S(1)}, bf16[160,896]{1,0:T(8,128)(2,1)S(1)}, u32[]{:S(2)}, u32[]{:S(2)}) collective-permute-start(bf16[160,896]{1,0:T(8,128)(2,1)S(1)} %pad_maximum_fusion.2), channel_id=1, source_target_pairs={{0,1},{1,0},{2,3},{3,2},{4,5},{5,4},{6,7},{7,6},{8,9},{9,8},{10,11... | collective-permute-start | bytes 860168 | tf_op jit(solution)/shard_map/ppermute | solution.py:794
  89.4 2.6 %collective-permute-start.42 = (bf16[128,896]{1,0:T(8,128)(2,1)S(1)}, bf16[128,896]{1,0:T(8,128)(2,1)S(1)}, u32[]{:S(2)}, u32[]{:S(2)}) collective-permute-start(bf16[128,896]{1,0:T(8,128)(2,1)S(1)} %pad_maximum_fusion.12), channel_id=1, source_target_pairs={{0,1},{1,0},{2,3},{3,2},{4,5},{5,4},{6,7},{7,6},{8,9},{9,8},{10,11... | collective-permute-start | bytes 688136 | tf_op jit(solution)/shard_map/ppermute | solution.py:794
  89.9 5.7 %collective-permute-start.37 = (bf16[80,896]{1,0:T(8,128)(2,1)S(1)}, bf16[80,896]{1,0:T(8,128)(2,1)S(1)}, u32[]{:S(2)}, u32[]{:S(2)}) collective-permute-start(bf16[80,896]{1,0:T(8,128)(2,1)S(1)} %collective-permute-done.31.refs_0_), channel_id=1, source_target_pairs={{0,4},{4,8},{8,12},{12,14},{14,10},{10,6},{6,2},{2,0},{1,5},{5,9},... | collective-permute-start | bytes 430088 | tf_op jit(solution)/shard_map/ppermute | solution.py:788
  90.4 5.2 %collective-permute-start.39 = (bf16[64,896]{1,0:T(8,128)(2,1)S(1)}, bf16[64,896]{1,0:T(8,128)(2,1)S(1)}, u32[]{:S(2)}, u32[]{:S(2)}) collective-permute-start(bf16[64,896]{1,0:T(8,128)(2,1)S(1)} %collective-permute-done.38.refs_3_), channel_id=1, source_target_pairs={{4,0},{8,4},{12,8},{14,12},{10,14},{6,10},{2,6},{0,2},{5,1},{9,5},... | collective-permute-start | bytes 344072 | tf_op jit(solution)/shard_map/ppermute | solution.py:791
  95.6 1.5 %collective-permute-start.43 = (bf16[80,896]{1,0:T(8,128)(2,1)S(1)}, bf16[80,896]{1,0:T(8,128)(2,1)S(1)}, u32[]{:S(2)}, u32[]{:S(2)}) collective-permute-start(bf16[80,896]{1,0:T(8,128)(2,1)S(1)} %collective-permute-done.37.refs_0_), channel_id=1, source_target_pairs={{0,1},{1,0},{2,3},{3,2},{4,5},{5,4},{6,7},{7,6},{8,9},{9,8},{10,11... | collective-permute-start | bytes 430088 | tf_op jit(solution)/shard_map/ppermute | solution.py:794
  100.3 4.0 %collective-permute-start.55 = (bf16[144,3584]{1,0:T(8,128)(2,1)S(1)}, bf16[144,3584]{1,0:T(8,128)(2,1)S(1)}, u32[]{:S(2)}, u32[]{:S(2)}) collective-permute-start(bf16[144,3584]{1,0:T(8,128)(2,1)S(1)} %contract.7), channel_id=1, source_target_pairs={{0,1},{1,0},{2,3},{3,2},{4,5},{5,4},{6,7},{7,6},{8,9},{9,8},{10,11... | collective-permute-start | bytes 3096584 | tf_op jit(solution)/shard_map/ppermute | solution.py:794
  101.9 6.7 %collective-permute-start.45 = (bf16[144,3584]{1,0:T(8,128)(2,1)S(1)}, bf16[144,3584]{1,0:T(8,128)(2,1)S(1)}, u32[]{:S(2)}, u32[]{:S(2)}) collective-permute-start(bf16[144,3584]{1,0:T(8,128)(2,1)S(1)} %contract.5), channel_id=1, source_target_pairs={{0,1},{1,0},{2,3},{3,2},{4,5},{5,4},{6,7},{7,6},{8,9},{9,8},{10,11... | collective-permute-start | bytes 3096584 | tf_op jit(solution)/shard_map/ppermute | solution.py:794
  105.1 6.3 %collective-permute-start.57 = (bf16[16,3584]{1,0:T(8,128)(2,1)S(1)}, bf16[16,3584]{1,0:T(8,128)(2,1)S(1)}, u32[]{:S(2)}, u32[]{:S(2)}) collective-permute-start(bf16[16,3584]{1,0:T(8,128)(2,1)S(1)} %convert_element_type.162), channel_id=1, source_target_pairs={{4,0},{8,4},{12,8},{14,12},{10,14},{6,10},{2,6},{0,2},{5,1},{9,5},... | collective-permute-start | bytes 344072 | tf_op jit(solution)/shard_map/ppermute | solution.py:791
  107.6 5.2 %collective-permute-start.56 = (bf16[16,3584]{1,0:T(8,128)(2,1)S(1)}, bf16[16,3584]{1,0:T(8,128)(2,1)S(1)}, u32[]{:S(2)}, u32[]{:S(2)}) collective-permute-start(bf16[16,3584]{1,0:T(8,128)(2,1)S(1)} %convert_element_type.161), channel_id=1, source_target_pairs={{0,4},{4,8},{8,12},{12,14},{14,10},{10,6},{6,2},{2,0},{1,5},{5,9},... | collective-permute-start | bytes 344072 | tf_op jit(solution)/shard_map/ppermute | solution.py:788
  109.4 5.5 %collective-permute-start.47 = (bf16[16,3584]{1,0:T(8,128)(2,1)S(1)}, bf16[16,3584]{1,0:T(8,128)(2,1)S(1)}, u32[]{:S(2)}, u32[]{:S(2)}) collective-permute-start(bf16[16,3584]{1,0:T(8,128)(2,1)S(1)} %convert_element_type.142), channel_id=1, source_target_pairs={{4,0},{8,4},{12,8},{14,12},{10,14},{6,10},{2,6},{0,2},{5,1},{9,5},... | collective-permute-start | bytes 344072 | tf_op jit(solution)/shard_map/ppermute | solution.py:791
  110.5 5.3 %collective-permute-start.46 = (bf16[16,3584]{1,0:T(8,128)(2,1)S(1)}, bf16[16,3584]{1,0:T(8,128)(2,1)S(1)}, u32[]{:S(2)}, u32[]{:S(2)}) collective-permute-start(bf16[16,3584]{1,0:T(8,128)(2,1)S(1)} %convert_element_type.141), channel_id=1, source_target_pairs={{0,4},{4,8},{8,12},{12,14},{14,10},{10,6},{6,2},{2,0},{1,5},{5,9},... | collective-permute-start | bytes 344072 | tf_op jit(solution)/shard_map/ppermute | solution.py:788
  112.8 5.7 %collective-permute-start.59 = (bf16[16,3584]{1,0:T(8,128)(2,1)S(1)}, bf16[16,3584]{1,0:T(8,128)(2,1)S(1)}, u32[]{:S(2)}, u32[]{:S(2)}) collective-permute-start(bf16[16,3584]{1,0:T(8,128)(2,1)S(1)} %add_convert_fusion.5), channel_id=1, source_target_pairs={{4,0},{8,4},{12,8},{14,12},{10,14},{6,10},{2,6},{0,2},{5,1},{9,5},... | collective-permute-start | bytes 344072 | tf_op jit(solution)/shard_map/ppermute | solution.py:791
  113.6 6.0 %collective-permute-start.58 = (bf16[16,3584]{1,0:T(8,128)(2,1)S(1)}, bf16[16,3584]{1,0:T(8,128)(2,1)S(1)}, u32[]{:S(2)}, u32[]{:S(2)}) collective-permute-start(bf16[16,3584]{1,0:T(8,128)(2,1)S(1)} %add_convert_fusion.6), channel_id=1, source_target_pairs={{0,4},{4,8},{8,12},{12,14},{14,10},{10,6},{6,2},{2,0},{1,5},{5,9},... | collective-permute-start | bytes 344072 | tf_op jit(solution)/shard_map/ppermute | solution.py:788
  115.9 6.0 %collective-permute-start.49 = (bf16[16,3584]{1,0:T(8,128)(2,1)S(1)}, bf16[16,3584]{1,0:T(8,128)(2,1)S(1)}, u32[]{:S(2)}, u32[]{:S(2)}) collective-permute-start(bf16[16,3584]{1,0:T(8,128)(2,1)S(1)} %add_convert_fusion.11), channel_id=1, source_target_pairs={{4,0},{8,4},{12,8},{14,12},{10,14},{6,10},{2,6},{0,2},{5,1},{9,5},... | collective-permute-start | bytes 344072 | tf_op jit(solution)/shard_map/ppermute | solution.py:791
  117.3 5.1 %collective-permute-start.48 = (bf16[16,3584]{1,0:T(8,128)(2,1)S(1)}, bf16[16,3584]{1,0:T(8,128)(2,1)S(1)}, u32[]{:S(2)}, u32[]{:S(2)}) collective-permute-start(bf16[16,3584]{1,0:T(8,128)(2,1)S(1)} %add_convert_fusion.12), channel_id=1, source_target_pairs={{0,4},{4,8},{8,12},{12,14},{14,10},{10,6},{6,2},{2,0},{1,5},{5,9},... | collective-permute-start | bytes 344072 | tf_op jit(solution)/shard_map/ppermute | solution.py:788
  119.7 5.2 %collective-permute-start.61 = (bf16[16,3584]{1,0:T(8,128)(2,1)S(1)}, bf16[16,3584]{1,0:T(8,128)(2,1)S(1)}, u32[]{:S(2)}, u32[]{:S(2)}) collective-permute-start(bf16[16,3584]{1,0:T(8,128)(2,1)S(1)} %add_convert_fusion.3), channel_id=1, source_target_pairs={{4,0},{8,4},{12,8},{14,12},{10,14},{6,10},{2,6},{0,2},{5,1},{9,5},... | collective-permute-start | bytes 344072 | tf_op jit(solution)/shard_map/ppermute | solution.py:791
  119.9 5.4 %collective-permute-start.60 = (bf16[16,3584]{1,0:T(8,128)(2,1)S(1)}, bf16[16,3584]{1,0:T(8,128)(2,1)S(1)}, u32[]{:S(2)}, u32[]{:S(2)}) collective-permute-start(bf16[16,3584]{1,0:T(8,128)(2,1)S(1)} %add_convert_fusion.4), channel_id=1, source_target_pairs={{0,4},{4,8},{8,12},{12,14},{14,10},{10,6},{6,2},{2,0},{1,5},{5,9},... | collective-permute-start | bytes 344072 | tf_op jit(solution)/shard_map/ppermute | solution.py:788
  122.5 5.9 %collective-permute-start.51 = (bf16[16,3584]{1,0:T(8,128)(2,1)S(1)}, bf16[16,3584]{1,0:T(8,128)(2,1)S(1)}, u32[]{:S(2)}, u32[]{:S(2)}) collective-permute-start(bf16[16,3584]{1,0:T(8,128)(2,1)S(1)} %add_convert_fusion.9), channel_id=1, source_target_pairs={{4,0},{8,4},{12,8},{14,12},{10,14},{6,10},{2,6},{0,2},{5,1},{9,5},... | collective-permute-start | bytes 344072 | tf_op jit(solution)/shard_map/ppermute | solution.py:791
  122.9 5.6 %collective-permute-start.50 = (bf16[16,3584]{1,0:T(8,128)(2,1)S(1)}, bf16[16,3584]{1,0:T(8,128)(2,1)S(1)}, u32[]{:S(2)}, u32[]{:S(2)}) collective-permute-start(bf16[16,3584]{1,0:T(8,128)(2,1)S(1)} %add_convert_fusion.10), channel_id=1, source_target_pairs={{0,4},{4,8},{8,12},{12,14},{14,10},{10,6},{6,2},{2,0},{1,5},{5,9},... | collective-permute-start | bytes 344072 | tf_op jit(solution)/shard_map/ppermute | solution.py:788
  125.4 5.9 %collective-permute-start.62 = (bf16[16,3584]{1,0:T(8,128)(2,1)S(1)}, bf16[16,3584]{1,0:T(8,128)(2,1)S(1)}, u32[]{:S(2)}, u32[]{:S(2)}) collective-permute-start(bf16[16,3584]{1,0:T(8,128)(2,1)S(1)} %add_convert_fusion.2), channel_id=1, source_target_pairs={{0,4},{4,8},{8,12},{12,14},{14,10},{10,6},{6,2},{2,0},{1,5},{5,9},... | collective-permute-start | bytes 344072 | tf_op jit(solution)/shard_map/ppermute | solution.py:788
  127.4 4.8 %collective-permute-start.63 = (bf16[16,3584]{1,0:T(8,128)(2,1)S(1)}, bf16[16,3584]{1,0:T(8,128)(2,1)S(1)}, u32[]{:S(2)}, u32[]{:S(2)}) collective-permute-start(bf16[16,3584]{1,0:T(8,128)(2,1)S(1)} %add_convert_fusion.1), channel_id=1, source_target_pairs={{4,0},{8,4},{12,8},{14,12},{10,14},{6,10},{2,6},{0,2},{5,1},{9,5},... | collective-permute-start | bytes 344072 | tf_op jit(solution)/shard_map/ppermute | solution.py:791
  128.5 4.8 %collective-permute-start.52 = (bf16[16,3584]{1,0:T(8,128)(2,1)S(1)}, bf16[16,3584]{1,0:T(8,128)(2,1)S(1)}, u32[]{:S(2)}, u32[]{:S(2)}) collective-permute-start(bf16[16,3584]{1,0:T(8,128)(2,1)S(1)} %add_convert_fusion.8), channel_id=1, source_target_pairs={{0,4},{4,8},{8,12},{12,14},{14,10},{10,6},{6,2},{2,0},{1,5},{5,9},... | collective-permute-start | bytes 344072 | tf_op jit(solution)/shard_map/ppermute | solution.py:788
  130.5 4.8 %collective-permute-start.53 = (bf16[16,3584]{1,0:T(8,128)(2,1)S(1)}, bf16[16,3584]{1,0:T(8,128)(2,1)S(1)}, u32[]{:S(2)}, u32[]{:S(2)}) collective-permute-start(bf16[16,3584]{1,0:T(8,128)(2,1)S(1)} %add_convert_fusion.7), channel_id=1, source_target_pairs={{4,0},{8,4},{12,8},{14,12},{10,14},{6,10},{2,6},{0,2},{5,1},{9,5},... | collective-permute-start | bytes 344072 | tf_op jit(solution)/shard_map/ppermute | solution.py:791
  135.5 1.9 %collective-permute-start.54 = (bf16[16,3584]{1,0:T(8,128)(2,1)S(1)}, bf16[16,3584]{1,0:T(8,128)(2,1)S(1)}, u32[]{:S(2)}, u32[]{:S(2)}) collective-permute-start(bf16[16,3584]{1,0:T(8,128)(2,1)S(1)} %get-tuple-element.319), channel_id=1, source_target_pairs={{0,1},{1,0},{2,3},{3,2},{4,5},{5,4},{6,7},{7,6},{8,9},{9,8},{10,11... | collective-permute-start | bytes 344072 | tf_op jit(solution)/shard_map/ppermute | solution.py:794
  136.9 1.5 %collective-permute-start.64 = (bf16[16,3584]{1,0:T(8,128)(2,1)S(1)}, bf16[16,3584]{1,0:T(8,128)(2,1)S(1)}, u32[]{:S(2)}, u32[]{:S(2)}) collective-permute-start(bf16[16,3584]{1,0:T(8,128)(2,1)S(1)} %get-tuple-element.325), channel_id=1, source_target_pairs={{0,1},{1,0},{2,3},{3,2},{4,5},{5,4},{6,7},{7,6},{8,9},{9,8},{10,11... | collective-permute-start | bytes 344072 | tf_op jit(solution)/shard_map/ppermute | solution.py:794
  (13 other events, 169.5 us)

commit v9 on v8

--- a/solution.py
+++ b/solution.py
@@ -138,13 +138,13 @@
 ):
     if lead:
         given, refs = refs[0], refs[1:]
-        q_hbm, cache_hbm, fresh, vw_hbm, tab, head, main, extra, later = refs[:9]
+        q_hbm, cache_hbm, fresh_hbm, vw_hbm, tab, head, main, extra, later = refs[:9]
         flags, refs = refs[9:12], refs[12:]
-        q, keys, vw, latent, fz, q_sem, key_sem, vw_sem, dq = refs
+        q, keys, vw, latent, fz, fresh, q_sem, key_sem, vw_sem, dq = refs
         loaded, base = heads, 0
     else:
-        tab, q_hbm, cache_hbm, fresh, vw_hbm, decoded_here, head, main, extra = refs[:9]
-        q, keys, vw, latent, fz, q_sem, key_sem, vw_sem = refs[9:]
+        tab, q_hbm, cache_hbm, fresh_hbm, vw_hbm, decoded_here, head, main, extra = refs[:9]
+        q, keys, vw, latent, fz, fresh, q_sem, key_sem, vw_sem = refs[9:]
         loaded, base = count, first
     cached, wide = keys.shape[2], keys.shape[1]
     slots = cache_hbm.shape[0] - 1
@@ -179,6 +179,8 @@
         for _ in range(min(number, len(waiting))):
             waiting.pop(0).start()
 
+    fresh_copy = pltpu.make_async_copy(fresh_hbm, fresh, key_sem.at[3])
+    fresh_copy.start()
     even_copy.start()
     q_copy(0).start()
     odd_copy.start()
@@ -197,6 +199,7 @@
         keys[s, lat:] = tail
     keys[odd_slot, :shift] = tail
     fz[...] = jnp.zeros_like(fz)
+    fresh_copy.wait()
     fz[:rows, :lat] = fresh[...].astype(f32)
     fresh_even = fz[...].astype(bf16)
     fresh_odd = pltpu.roll(fz[...], shift, 1).astype(bf16)
@@ -318,13 +321,14 @@
         pltpu.VMEM((count, value, vh), bf16),
         pltpu.VMEM((count // group, 2, group // 2 * rows, value), bf16),
         pltpu.VMEM((-(-rows // 128) * 128, wide), f32),
+        pltpu.VMEM(fresh.shape[::-1], bf16),
         pltpu.SemaphoreType.DMA((loaded // group,)),
-        pltpu.SemaphoreType.DMA((3,)),
+        pltpu.SemaphoreType.DMA((4,)),
         pltpu.SemaphoreType.DMA((count // group,)),
     ]
     out_shape, out_specs = [half] * 3, [whole()] * 3
-    ins = [smem(), hbm, hbm, whole(), hbm]
-    args = [numbers, in_hbm(queries), in_hbm(cache), fresh.T, in_hbm(vw)]
+    ins = [smem()] + [hbm] * 4
+    args = [numbers, in_hbm(queries), in_hbm(cache), in_hbm(fresh.T), in_hbm(vw)]
     if lead:
         scratch.append(pltpu.VMEM((heads * 8, wide), f32))
         out_shape = [jax.ShapeDtypeStruct((table.size,), i32)] + out_shape
@@ -560,7 +564,7 @@
     )(tab, own, shared, *pieces)
 
 
-def expand_kernel(pieces, others, first, final, width, turned, owners, tab, *refs):
+def expand_kernel(pieces, others, first, turned, owners, tab, *refs):
     count = len(pieces)
     blocks = []
     for number in pieces:
@@ -571,8 +575,6 @@
     refs = refs[3:]
     if not first:
         before, refs = refs[:3], refs[3:]
-    if final:
-        hidden, refs = refs[0], refs[1:]
     gates, ups, squares = refs
     step = pl.program_id(0)
     for i in range(count):
@@ -601,23 +603,64 @@
                 else:
                     ref[...] += value
 
-    if final:
-
-        @pl.when(step == count - 1)
-        def _():
-            scale = lax.rsqrt(squares[...] / width + norm_eps)
-            g = gates[...] * scale
-            hidden[...] = (g / (1.0 + jnp.exp(-g)) * (ups[...] * scale)).astype(bf16)
-
-
-def expand(tab, mines, theirs, owners, gain, gate, up, before, final):
+
+def last_kernel(count, width, turned, owner, tab, *refs):
+    block = jnp.concatenate([x[...] for x in refs[:count]], 0).astype(f32)
+    gain, gate, up, gates, ups, squares, hidden = refs[count:]
+    features = block.shape[1]
+    scaled = (block * gain[0]).astype(bf16)
+    if turned:
+        at = pl.ds(pl.multiple_of(tab[owner] * features, 128), features)
+        g, u = mm_nt(scaled, gate[:, at]), mm_nt(scaled, up[:, at])
+    else:
+        g, u = mm(scaled, gate[...]), mm(scaled, up[...])
+    total = squares[...] + jnp.sum(block * block, axis=1, keepdims=True)
+    scale = lax.rsqrt(total / width + norm_eps)
+    g = (g + gates[...]) * scale
+    hidden[...] = (g / (1.0 + jnp.exp(-g)) * ((u + ups[...]) * scale)).astype(bf16)
+
+
+def expand_last(tab, pieces, owner, gain, gate, up, before, which):
+    rows, features = sum(x.shape[0] for x in pieces), pieces[0].shape[1]
+    units, width = gate.shape[1], gate.shape[0]
+    turned = features % 128 == 0
+
+    def full(shape):
+        return pl.BlockSpec(shape, lambda i, tab: (0,) * len(shape))
+
+    def half(columns):
+        return pl.BlockSpec((rows, columns), lambda i, tab: (which, 0))
+
+    if turned:
+        gate, up = gate.T, up.T
+        weights = [pl.BlockSpec(memory_space=pltpu.VMEM)] * 2
+    else:
+        weights = [pl.BlockSpec((features, units), lambda i, tab: (tab[owner], 0))] * 2
+    return pl.pallas_call(
+        functools.partial(last_kernel, len(pieces), width, turned, owner),
+        grid_spec=pltpu.PrefetchScalarGridSpec(
+            num_scalar_prefetch=1,
+            grid=(1,),
+            in_specs=[full(x.shape) for x in pieces]
+            + [pl.BlockSpec((1, 1, features), lambda i, tab: (tab[owner], 0, 0))]
+            + weights
+            + [half(units), half(units), half(1)],
+            out_specs=full((rows, units)),
+        ),
+        out_shape=jax.ShapeDtypeStruct((rows, units), bf16),
+        compiler_params=params(20),
+        cost_estimate=cost(4 * rows * features * units, 4 * features * units),
+        name="last",
+    )(tab, *pieces, gain, gate, up, *before)
+
+
+def expand(tab, mines, theirs, owners, gain, gate, up, before):
     count = len(mines)
     pieces = tuple(len(x) for x in mines)
     rows, features = sum(x.shape[0] for x in mines[0]), mines[0][0].shape[1]
     arrays = [x for own in mines for x in own] + theirs
     units = gate.shape[1]
     first = before is None
-    width = gate.shape[0]
 
     def owner(i, tab):
         index = tab[owners[0]]
@@ -640,17 +683,15 @@
     if not first:
         ins += [full(s) for s in sums]
     shapes = [jax.ShapeDtypeStruct(s, f32) for s in sums]
-    out_shapes = [jax.ShapeDtypeStruct((2 * rows, units), bf16)] if final else shapes
     return pl.pallas_call(
-        functools.partial(expand_kernel, pieces, len(theirs), first, final, width, turned, owners),
+        functools.partial(expand_kernel, pieces, len(theirs), first, turned, owners),
         grid_spec=pltpu.PrefetchScalarGridSpec(
             num_scalar_prefetch=1,
             grid=(count,),
             in_specs=ins,
-            out_specs=[full(s.shape) for s in out_shapes],
-            scratch_shapes=[pltpu.VMEM(s, f32) for s in sums] if final else [],
+            out_specs=[full(s) for s in sums],
         ),
-        out_shape=out_shapes,
+        out_shape=shapes,
         compiler_params=params(20),
         cost_estimate=cost(1, 1),
         name="expand",
@@ -706,14 +747,14 @@
     out[...] = mm(hidden[...], weight[:, at]).astype(bf16)
 
 
-def contract(hidden, weight, part, parts, which):
-    rows, units = hidden.shape[0] // 2, hidden.shape[1]
+def contract(hidden, weight, part, parts):
+    rows, units = hidden.shape
     columns = weight.shape[1] // parts
     wide = columns // 2 if columns % 256 == 0 else columns
     return pl.pallas_call(
         functools.partial(contract_kernel, part * columns),
         grid=(columns // wide,),
-        in_specs=[pl.BlockSpec((rows, units), lambda i: (which, 0)), whole()],
+        in_specs=[pl.BlockSpec((rows, units), lambda i: (0, 0)), whole()],
         out_specs=pl.BlockSpec((rows, wide), lambda i: (0, i)),
         out_shape=jax.ShapeDtypeStruct((rows, columns), bf16),
         compiler_params=params(16),
@@ -846,6 +887,8 @@
             behind.append(send_next(out_f))
             ahead.append(send_prev(out_b))
     gathered = [[main] + behind + ahead + [extra] for _, main, extra, behind, ahead in chains]
+    chains[0][3][-1], pieces = lax.optimization_barrier((chains[0][3][-1], pieces))
+    gathered[0][reach] = chains[0][3][-1]
     shared = swap(share(tab, packed[0], pieces, cores))
     gathered[0], shared = lax.optimization_barrier((gathered[0], shared))
     for part in range(2):
@@ -857,38 +900,34 @@
     gain = norm_gain.reshape(ranks, 1, features)
     weights = (gain, gate_weight, up_weight)
     cut = -(-stream.shape[0] // 32) * 16
-    backs = [stream[:cut], stream[cut:]]
-    fores = list(backs)
-    swapped, backs[1], fores[1] = lax.optimization_barrier((swap(stream), backs[1], fores[1]))
-    sums = expand(tab, [[stream]], [swapped], [RANK], *weights, None, False)
+    back, fore = stream, stream
+    sums = expand(tab, [[stream]], [swap(stream)], [RANK], *weights, None)
     blocks, owners = [stream], [RANK]
     done = None
-    for step in range(1, reach + 1):
+    for step in range(1, reach):
         if done is not None:
-            backs[0], fores[0], done = lax.optimization_barrier((backs[0], fores[0], done))
+            back, fore, done = lax.optimization_barrier((back, fore, done))
         done = sums
-        if step < reach:
-            for n in range(2):
-                back, fore = lax.optimization_barrier((backs[n], fores[n]))
-                backs[n], fores[n] = send_next(back), send_prev(fore)
-            arrived = [list(backs), list(fores)]
-            from_owner = [table.owner_back + step, table.owner_fore + step]
-        else:
-            arrived = [[send_next(backs[0]), send_prev(fores[1])]]
-            from_owner = [table.owner_back + step]
-        others = []
-        for chain in zip(*arrived):
-            tied, sums = lax.optimization_barrier((chain, sums))
-            others.append(swap(jnp.concatenate(tied, 0)))
-        sums = expand(tab, arrived, others, from_owner, *weights, sums, step == reach)
-        blocks += [jnp.concatenate(x, 0) for x in arrived]
+        back, fore = send_next(back), send_prev(fore)
+        from_owner = [table.owner_back + step, table.owner_fore + step]
+        tied, sums = lax.optimization_barrier(((back, fore), sums))
+        others = swap(jnp.concatenate(tied, 0))
+        sums = expand(tab, [[back], [fore]], [others], from_owner, *weights, sums)
+        blocks += [back, fore]
         owners += from_owner
-    (hidden,) = sums
+    back, fore, done = lax.optimization_barrier((back, fore, done))
+    last = [send_next(back[:cut]), send_prev(fore[cut:])]
+    owner = table.owner_back + reach
+    tied, sums = lax.optimization_barrier((last, sums))
+    others = [swap(x) for x in tied]
+    hidden = [expand_last(tab, x, owner, *weights, sums, n) for n, x in enumerate((last, others))]
+    blocks.append(jnp.concatenate(last, 0))
+    owners.append(owner)
     own = collect(tab, blocks, owners, half).astype(f32)
 
     parts = contract_parts
-    theirs = [swap(contract(hidden, down_weight, part, parts, 1)) for part in range(parts)]
-    mine = [contract(hidden, down_weight, part, parts, 0) for part in range(parts)]
+    theirs = [swap(contract(hidden[1], down_weight, part, parts)) for part in range(parts)]
+    mine = [contract(hidden[0], down_weight, part, parts) for part in range(parts)]
     columns = width // parts
     lows, highs = [], []
     for part in range(parts):

time: 140 us -> 145 us (1.036)
  waiting for transfers between devices: 32.8 us -> 46 us
  starting transfers between devices: 59.3 us -> 51.5 us
    ppermute x23 -> x20, waiting for transfers between devices: 14 us -> 28 us  [send_next(): return lax.ppermute(x, 'blk', forward)]
    ppermute x23 -> x20, starting transfers between devices: 28.9 us -> 23.9 us  [send_next(): return lax.ppermute(x, 'blk', forward)]
    pallas_call x0 -> x2, Pallas kernels: none -> 2.85 us  [expand_last(): pl.pallas_call(functools.partial(last_kernel, len(pieces), width, turned,...]
    ppermute x4, waiting for transfers between devices: 2.11 us -> 0.01 us  [send_piece(): pieces[k] = lax.ppermute(packed[k], ('blk', 'head'), pairs)]
    pallas_call x5 -> x4, Pallas kernels: 12.1 us -> 10.3 us  [expand(): pl.pallas_call(functools.partial(expand_kernel, pieces, len(theirs), firs...]
    ppermute x23 -> x20, starting transfers between devices: 24 us -> 22.2 us  [send_prev(): return lax.ppermute(x, 'blk', backward)]
    ppermute x23 -> x20, waiting for transfers between devices: 13.8 us -> 15 us  [send_prev(): return lax.ppermute(x, 'blk', backward)]
    ppermute x15 -> x12, starting transfers between devices: 3.52 us -> 2.59 us  [swap(): return lax.ppermute(x, 'head', exchange)]
  transfers between devices with their start and end apart: 65 -> 56, of which waited for: 35 -> 29; matrix products, arithmetic and copies ran while one was open for 1% -> 1% of each run, Pallas kernels for 19% -> 19%
where the time goes in v9:
time: 145 us
  starting transfers between devices  51.5 us (36%)
  waiting for transfers between devices  46 us (32%)
  Pallas kernels  40.1 us (28%)
  between operations  3.4 us (2%)
  other arithmetic  2.89 us (2%)
    ppermute x20, waiting for transfers between devices, send_next(): return lax.ppermute(x, 'blk', forward)  28 us
    ppermute x20, starting transfers between devices, send_next(): return lax.ppermute(x, 'blk', forward)  23.9 us
    ppermute x20, starting transfers between devices, send_prev(): return lax.ppermute(x, 'blk', backward)  22.2 us
    ppermute x20, waiting for transfers between devices, send_prev(): return lax.ppermute(x, 'blk', backward)  15 us
    pallas_call x2, Pallas kernels, attend(): pl.pallas_call(functools.partial(attend_kernel, table, order, heads, part...  14.1 us
    pallas_call x4, Pallas kernels, expand(): pl.pallas_call(functools.partial(expand_kernel, pieces, len(theirs), firs...  10.3 us
    pallas_call x4, Pallas kernels, contract(): pl.pallas_call(functools.partial(contract_kernel, part * columns), grid=(...  5.03 us
  transfers between devices with their start and end apart: 56, of which 29 were waited for; matrix products, arithmetic and copies ran while one was open for 1% of the time, Pallas kernels for 19%

profile of v9, /device:TPU:0, one launch (start us, length us, event | category | flops | bytes accessed | tf_op | source)
XLA Modules:
  0.0 145.1 jit_solution(15138435484623937884)
XLA Ops:
  1.5 8.2 %attend.2 = (s32[60]{0:T(128)S(1)}, bf16[32,2048]{1,0:T(8,128)(2,1)S(1)}, bf16[32,2048]{1,0:T(8,128)(2,1)S(1)}, bf16[32,2048]{1,0:T(8,128)(2,1)S(1)}, bf16[128,5...) custom-call(s32[26]{0:T(128)S(1)} %concatenate.24.refs_0_, bf16[64,18432]{1,0:T(8,128)(2,1)} %refs_1_.3, ...), custom_call_target="tpu_custom_call" | custom-call | flops 713031680 | bytes 4456448 | tf_op jit(solution)/shard_map/attend/pallas_call | solution.py:341
  9.7 3.1 %collective-permute-start.10 = (bf16[32,2048]{1,0:T(8,128)(2,1)S(1)}, bf16[32,2048]{1,0:T(8,128)(2,1)S(1)}, u32[]{:S(2)}, u32[]{:S(2)}) collective-permute-start(bf16[32,2048]{1,0:T(8,128)(2,1)S(1)} %get-tuple-element.161), channel_id=1, source_target_pairs={{0,4},{4,8},{8,12},{12,14},{14,10},{10,6},{6,2},{2,0},{1,5},{5,9},... | collective-permute-start | bytes 393224 | tf_op jit(solution)/shard_map/ppermute | solution.py:829
  14.2 3.0 %collective-permute-start.11 = (bf16[32,2048]{1,0:T(8,128)(2,1)S(1)}, bf16[32,2048]{1,0:T(8,128)(2,1)S(1)}, u32[]{:S(2)}, u32[]{:S(2)}) collective-permute-start(bf16[32,2048]{1,0:T(8,128)(2,1)S(1)} %get-tuple-element.181.refs_0_), channel_id=1, source_target_pairs={{4,0},{8,4},{12,8},{14,12},{10,14},{6,10},{2,6},{0,2},{5,1},{9,5},... | collective-permute-start | bytes 393224 | tf_op jit(solution)/shard_map/ppermute | solution.py:832
  17.9 5.9 %attend.3 = (bf16[32,2048]{1,0:T(8,128)(2,1)S(1)}, bf16[32,2048]{1,0:T(8,128)(2,1)S(1)}, bf16[32,2048]{1,0:T(8,128)(2,1)S(1)}) custom-call(s32[60]{0:T(128)S(1)} %get-tuple-element.136.tab.refs_0_, bf16[64,18432]{1,0:T(8,128)(2,1)} %refs_1_.3, bf16[8,576,256]{2,1,0:T(8,128)(2,1)} %refs_2_.3, bf16[64,576]{1,0:T(8,128)(2,1)} %bitcast.38, ...), custom_call_target="tpu_custom_call" | custom-call | flops 713031680 | bytes 4456448 | tf_op jit(solution)/shard_map/attend/pallas_call | solution.py:341
  23.9 1.6 %collective-permute-start.3 = (bf16[32,2048]{1,0:T(8,128)(2,1)S(1)}, bf16[32,2048]{1,0:T(8,128)(2,1)S(1)}, u32[]{:S(2)}, u32[]{:S(2)}) collective-permute-start(bf16[32,2048]{1,0:T(8,128)(2,1)S(1)} %get-tuple-element.151.refs_0_), channel_id=1, source_target_pairs={{4,0},{8,4},{12,8},{14,12},{10,14},{6,10},{2,6},{0,2},{5,1},{9,5},... | collective-permute-start | bytes 393224 | tf_op jit(solution)/shard_map/ppermute | solution.py:832
  26.0 1.6 %collective-permute-start.13 = (bf16[32,2048]{1,0:T(8,128)(2,1)S(1)}, bf16[32,2048]{1,0:T(8,128)(2,1)S(1)}, u32[]{:S(2)}, u32[]{:S(2)}) collective-permute-start(bf16[32,2048]{1,0:T(8,128)(2,1)S(1)} %broadcast_select_fusion.4), channel_id=1, source_target_pairs={{4,0},{8,4},{12,8},{14,12},{10,14},{6,10},{2,6},{0,2},{5,1},{9,5},... | collective-permute-start | bytes 393224 | tf_op jit(solution)/shard_map/ppermute | solution.py:832
  28.7 2.9 %collective-permute-done.2.refs_1_ = bf16[32,2048]{1,0:T(8,128)(2,1)S(1)} collective-permute-done((bf16[32,2048]{1,0:T(8,128)(2,1)S(1)}, bf16[32,2048]{1,0:T(8,128)(2,1)S(1)}, u32[]{:S(2)}, u32[]{:S(2)}) %collective-permute-start.2) | collective-permute-done | bytes 131104 | tf_op jit(solution)/shard_map/ppermute | solution.py:829
  31.6 1.3 collective-permute-start.18
  33.0 0.9 collective-permute-start.5
  33.8 1.1 collective-permute-start.4
  35.1 1.2 collective-permute-start.15
  36.2 4.6 %collective-permute-done.5.refs_6_ = bf16[32,2048]{1,0:T(8,128)(2,1)S(1)} collective-permute-done((bf16[32,2048]{1,0:T(8,128)(2,1)S(1)}, bf16[32,2048]{1,0:T(8,128)(2,1)S(1)}, u32[]{:S(2)}, u32[]{:S(2)}) %collective-permute-start.5) | collective-permute-done | bytes 131104 | tf_op jit(solution)/shard_map/ppermute | solution.py:832
  40.9 2.0 %collective-permute-start.7 = (bf16[32,2048]{1,0:T(8,128)(2,1)S(1)}, bf16[32,2048]{1,0:T(8,128)(2,1)S(1)}, u32[]{:S(2)}, u32[]{:S(2)}) collective-permute-start(bf16[32,2048]{1,0:T(8,128)(2,1)S(1)} %broadcast_select_fusion.8), channel_id=1, source_target_pairs={{4,0},{8,4},{12,8},{14,12},{10,14},{6,10},{2,6},{0,2},{5,1},{9,5},... | collective-permute-start | bytes 393224 | tf_op jit(solution)/shard_map/ppermute | solution.py:832
  43.6 1.0 collective-permute-start.6
  44.7 1.5 %collective-permute-done.14.refs_3_ = bf16[32,2048]{1,0:T(8,128)(2,1)S(1)} collective-permute-done((bf16[32,2048]{1,0:T(8,128)(2,1)S(1)}, bf16[32,2048]{1,0:T(8,128)(2,1)S(1)}, u32[]{:S(2)}, u32[]{:S(2)}) %collective-permute-start.14) | collective-permute-done | bytes 131104 | tf_op jit(solution)/shard_map/ppermute | solution.py:829
  46.1 2.3 %collective-permute-start.16 = (bf16[32,2048]{1,0:T(8,128)(2,1)S(1)}, bf16[32,2048]{1,0:T(8,128)(2,1)S(1)}, u32[]{:S(2)}, u32[]{:S(2)}) collective-permute-start(bf16[32,2048]{1,0:T(8,128)(2,1)S(1)} %broadcast_select_fusion.1), channel_id=1, source_target_pairs={{0,4},{4,8},{8,12},{12,14},{14,10},{10,6},{6,2},{2,0},{1,5},{5,9},... | collective-permute-start | bytes 393224 | tf_op jit(solution)/shard_map/ppermute | solution.py:829
  48.7 4.0 %collective-permute-done.16.refs_4_ = bf16[32,2048]{1,0:T(8,128)(2,1)S(1)} collective-permute-done((bf16[32,2048]{1,0:T(8,128)(2,1)S(1)}, bf16[32,2048]{1,0:T(8,128)(2,1)S(1)}, u32[]{:S(2)}, u32[]{:S(2)}) %collective-permute-start.16) | collective-permute-done | bytes 131104 | tf_op jit(solution)/shard_map/ppermute | solution.py:829
  54.2 1.5 %collective-permute-start.9 = (bf16[32,2048]{1,0:T(8,128)(2,1)S(1)}, bf16[32,2048]{1,0:T(8,128)(2,1)S(1)}, u32[]{:S(2)}, u32[]{:S(2)}) collective-permute-start(bf16[32,2048]{1,0:T(8,128)(2,1)S(1)} %broadcast_select_fusion.6), channel_id=1, source_target_pairs={{4,0},{8,4},{12,8},{14,12},{10,14},{6,10},{2,6},{0,2},{5,1},{9,5},... | collective-permute-start | bytes 393224 | tf_op jit(solution)/shard_map/ppermute | solution.py:832
  55.7 1.9 %project.2.refs_10_ = f32[288,896]{1,0:T(8,128)S(1)} custom-call(s32[60]{0:T(128)S(1)} %get-tuple-element.136.tab.refs_0_, bf16[32,2048]{1,0:T(8,128)(2,1)S(1)} %get-tuple-element.181.refs_0_, bf16[32,2048]{1,0:T(8,128)(2,1)S(1)} %collective-permute-done.10.refs_1_, bf16[32,2048]{1,0:T(8,128)(2,1)S(1)} %collective-permute-done.12.refs_2_, ...), custom_call_target="tpu_custom_call" | custom-call | flops 1056964608 | bytes 4849664 | tf_op jit(solution)/shard_map/project/pallas_call | solution.py:486
  57.7 1.6 %collective-permute-done.8.refs_4_ = bf16[32,2048]{1,0:T(8,128)(2,1)S(1)} collective-permute-done((bf16[32,2048]{1,0:T(8,128)(2,1)S(1)}, bf16[32,2048]{1,0:T(8,128)(2,1)S(1)}, u32[]{:S(2)}, u32[]{:S(2)}) %collective-permute-start.8) | collective-permute-done | bytes 131104 | tf_op jit(solution)/shard_map/ppermute | solution.py:829
  59.3 1.2 collective-permute-done.9.refs_8_
  60.5 2.0 %project.3 = (f32[144,896]{1,0:T(8,128)S(1)}, bf16[144,896]{1,0:T(8,128)(2,1)S(1)}) custom-call(s32[60]{0:T(128)S(1)} %get-tuple-element.136.tab.refs_0_, bf16[32,2048]{1,0:T(8,128)(2,1)S(1)} %get-tuple-element.151.refs_0_, bf16[32,2048]{1,0:T(8,128)(2,1)S(1)} %collective-permute-done.2.refs_1_, bf16[32,2048]{1,0:T(8,128)(2,1)S(1)} %collective-permute-done.4.refs_2_, ...), custom_call_target="tpu_custom_call" | custom-call | flops 1056964608 | bytes 4849664 | tf_op jit(solution)/shard_map/project/pallas_call | solution.py:496
  63.2 0.9 collective-permute-done.21
  64.4 1.8 %collective-permute-start.22 = (bf16[144,896]{1,0:T(8,128)(2,1)S(1)}, bf16[144,896]{1,0:T(8,128)(2,1)S(1)}, u32[]{:S(2)}, u32[]{:S(2)}) collective-permute-start(bf16[144,896]{1,0:T(8,128)(2,1)S(1)} %add_convert_fusion.refs_0_.refs_1_), channel_id=1, source_target_pairs={{0,4},{4,8},{8,12},{12,14},{14,10},{10,6},{6,2},{2,0},{1,5},{5,9},... | collective-permute-start | bytes 774152 | tf_op jit(solution)/shard_map/ppermute | solution.py:829
  66.5 1.7 %expand.4 = (f32[288,576]{1,0:T(8,128)S(1)}, f32[288,576]{1,0:T(8,128)S(1)}, f32[288,1]{1,0:T(8,128)S(1)}) custom-call(s32[60]{0:T(128)S(1)} %get-tuple-element.136.tab.refs_0_, bf16[144,896]{1,0:T(8,128)(2,1)S(1)} %add_convert_fusion.refs_0_.refs_1_, bf16[144,896]{1,0:T(8,128)(2,1)S(1)} %collective-permute-done.24.refs_1_, f32[8,1,896]{2,1,0:T(1,128)S(1)} %bitcast.31, ...), custom_call_target="tpu_custom_call" | custom-call | flops 1 | bytes 1 | tf_op jit(solution)/shard_map/expand/pallas_call | solution.py:686
  68.2 4.7 %collective-permute-done.22.refs_0_.refs_2_.refs_3_ = bf16[144,896]{1,0:T(8,128)(2,1)S(1)} collective-permute-done((bf16[144,896]{1,0:T(8,128)(2,1)S(1)}, bf16[144,896]{1,0:T(8,128)(2,1)S(1)}, u32[]{:S(2)}, u32[]{:S(2)}) %collective-permute-start.22) | collective-permute-done | bytes 258080 | tf_op jit(solution)/shard_map/ppermute | solution.py:829
  72.9 1.5 %collective-permute-done.23.refs_1_.refs_4_.refs_5_ = bf16[144,896]{1,0:T(8,128)(2,1)S(1)} collective-permute-done((bf16[144,896]{1,0:T(8,128)(2,1)S(1)}, bf16[144,896]{1,0:T(8,128)(2,1)S(1)}, u32[]{:S(2)}, u32[]{:S(2)}) %collective-permute-start.23) | collective-permute-done | bytes 258080 | tf_op jit(solution)/shard_map/ppermute | solution.py:832
  74.9 1.7 %collective-permute-start.26 = (bf16[144,896]{1,0:T(8,128)(2,1)S(1)}, bf16[144,896]{1,0:T(8,128)(2,1)S(1)}, u32[]{:S(2)}, u32[]{:S(2)}) collective-permute-start(bf16[144,896]{1,0:T(8,128)(2,1)S(1)} %collective-permute-done.23.refs_1_.refs_4_.refs_5_), channel_id=1, source_target_pairs={{4,0},{8,4},{12,8},{14,12},{10,14},{6,10},{2,6},{0,2},{5,1},{9,5},... | collective-permute-start | bytes 774152 | tf_op jit(solution)/shard_map/ppermute | solution.py:832
  76.6 2.9 %expand.5 = (f32[288,576]{1,0:T(8,128)S(1)}, f32[288,576]{1,0:T(8,128)S(1)}, f32[288,1]{1,0:T(8,128)S(1)}) custom-call(s32[60]{0:T(128)S(1)} %get-tuple-element.136.tab.refs_0_, bf16[144,896]{1,0:T(8,128)(2,1)S(1)} %collective-permute-done.22.refs_0_.refs_2_.refs_3_, bf16[144,896]{1,0:T(8,128)(2,1)S(1)} %collective-permute-done.23.refs_1_.refs_4_.refs_5_, ...), custom_call_target="tpu_custom_call" | custom-call | flops 1 | bytes 1 | tf_op jit(solution)/shard_map/expand/pallas_call | solution.py:686
  79.4 3.7 %collective-permute-done.25.refs_0_.refs_6_.refs_7_ = bf16[144,896]{1,0:T(8,128)(2,1)S(1)} collective-permute-done((bf16[144,896]{1,0:T(8,128)(2,1)S(1)}, bf16[144,896]{1,0:T(8,128)(2,1)S(1)}, u32[]{:S(2)}, u32[]{:S(2)}) %collective-permute-start.25) | collective-permute-done | bytes 258080 | tf_op jit(solution)/shard_map/ppermute | solution.py:829
  83.3 1.4 collective-permute-start.28
  85.4 2.9 %expand.6 = (f32[288,576]{1,0:T(8,128)S(1)}, f32[288,576]{1,0:T(8,128)S(1)}, f32[288,1]{1,0:T(8,128)S(1)}) custom-call(s32[60]{0:T(128)S(1)} %get-tuple-element.136.tab.refs_0_, bf16[144,896]{1,0:T(8,128)(2,1)S(1)} %collective-permute-done.25.refs_0_.refs_6_.refs_7_, bf16[144,896]{1,0:T(8,128)(2,1)S(1)} %collective-permute-done.26.refs_1_.refs_8_.refs_9_, ...), custom_call_target="tpu_custom_call" | custom-call | flops 1 | bytes 1 | tf_op jit(solution)/shard_map/expand/pallas_call | solution.py:686
  88.3 3.7 %collective-permute-done.28.refs_0_.refs_10_.refs_11_ = bf16[144,896]{1,0:T(8,128)(2,1)S(1)} collective-permute-done((bf16[144,896]{1,0:T(8,128)(2,1)S(1)}, bf16[144,896]{1,0:T(8,128)(2,1)S(1)}, u32[]{:S(2)}, u32[]{:S(2)}) %collective-permute-start.28) | collective-permute-done | bytes 258080 | tf_op jit(solution)/shard_map/ppermute | solution.py:829
  91.9 1.1 collective-permute-done.29.refs_1_.refs_12_.refs_13_
  93.1 1.8 %collective-permute-start.31 = (bf16[80,896]{1,0:T(8,128)(2,1)S(1)}, bf16[80,896]{1,0:T(8,128)(2,1)S(1)}, u32[]{:S(2)}, u32[]{:S(2)}) collective-permute-start(bf16[80,896]{1,0:T(8,128)(2,1)S(1)} %slice.18), channel_id=1, source_target_pairs={{0,4},{4,8},{8,12},{12,14},{14,10},{10,6},{6,2},{2,0},{1,5},{5,9},... | collective-permute-start | bytes 430088 | tf_op jit(solution)/shard_map/ppermute | solution.py:829
  95.3 2.9 %expand.7 = (f32[288,576]{1,0:T(8,128)S(1)}, f32[288,576]{1,0:T(8,128)S(1)}, f32[288,1]{1,0:T(8,128)S(1)}) custom-call(s32[60]{0:T(128)S(1)} %get-tuple-element.136.tab.refs_0_, bf16[144,896]{1,0:T(8,128)(2,1)S(1)} %collective-permute-done.28.refs_0_.refs_10_.refs_11_, bf16[144,896]{1,0:T(8,128)(2,1)S(1)} %collective-permute-done.29.refs_1_.refs_12_.refs_13_, ...), custom_call_target="tpu_custom_call" | custom-call | flops 1 | bytes 1 | tf_op jit(solution)/shard_map/expand/pallas_call | solution.py:686
  98.2 2.1 %collective-permute-done.32.refs_1_ = bf16[64,896]{1,0:T(8,128)(2,1)S(1)} collective-permute-done((bf16[64,896]{1,0:T(8,128)(2,1)S(1)}, bf16[64,896]{1,0:T(8,128)(2,1)S(1)}, u32[]{:S(2)}, u32[]{:S(2)}) %collective-permute-start.32) | collective-permute-done | bytes 114720 | tf_op jit(solution)/shard_map/ppermute | solution.py:832
  100.8 1.0 collective-permute-done.35.refs_1_
  101.9 1.4 last.3.hidden
  103.7 1.2 contract.7
  105.0 1.3 contract.5
  106.8 1.4 last.2.hidden
  108.3 1.3 contract.6.mine
  111.6 1.3 contract.4.mine
  112.9 1.8 %collective-permute-start.47 = (bf16[16,3584]{1,0:T(8,128)(2,1)S(1)}, bf16[16,3584]{1,0:T(8,128)(2,1)S(1)}, u32[]{:S(2)}, u32[]{:S(2)}) collective-permute-start(bf16[16,3584]{1,0:T(8,128)(2,1)S(1)} %convert_element_type.161), channel_id=1, source_target_pairs={{0,4},{4,8},{8,12},{12,14},{14,10},{10,6},{6,2},{2,0},{1,5},{5,9},... | collective-permute-start | bytes 344072 | tf_op jit(solution)/shard_map/ppermute | solution.py:829
  115.9 1.7 %collective-permute-start.37 = (bf16[16,3584]{1,0:T(8,128)(2,1)S(1)}, bf16[16,3584]{1,0:T(8,128)(2,1)S(1)}, u32[]{:S(2)}, u32[]{:S(2)}) collective-permute-start(bf16[16,3584]{1,0:T(8,128)(2,1)S(1)} %convert_element_type.141), channel_id=1, source_target_pairs={{0,4},{4,8},{8,12},{12,14},{14,10},{10,6},{6,2},{2,0},{1,5},{5,9},... | collective-permute-start | bytes 344072 | tf_op jit(solution)/shard_map/ppermute | solution.py:829
  117.8 1.2 collective-permute-start.50
  119.1 0.8 collective-permute-start.49
  119.9 1.6 %collective-permute-done.38 = bf16[16,3584]{1,0:T(8,128)(2,1)S(1)} collective-permute-done((bf16[16,3584]{1,0:T(8,128)(2,1)S(1)}, bf16[16,3584]{1,0:T(8,128)(2,1)S(1)}, u32[]{:S(2)}, u32[]{:S(2)}) %collective-permute-start.38) | collective-permute-done | bytes 114720 | tf_op jit(solution)/shard_map/ppermute | solution.py:832
  121.6 1.1 collective-permute-start.40
  122.7 1.0 collective-permute-start.39
  123.8 1.2 collective-permute-done.49
  125.1 1.3 collective-permute-start.52
  126.4 0.8 collective-permute-start.51
  128.1 1.0 collective-permute-start.42
  129.1 1.1 collective-permute-start.41
  130.4 2.0 %collective-permute-done.51 = bf16[16,3584]{1,0:T(8,128)(2,1)S(1)} collective-permute-done((bf16[16,3584]{1,0:T(8,128)(2,1)S(1)}, bf16[16,3584]{1,0:T(8,128)(2,1)S(1)}, u32[]{:S(2)}, u32[]{:S(2)}) %collective-permute-start.51) | collective-permute-done | bytes 114720 | tf_op jit(solution)/shard_map/ppermute | solution.py:829
  132.4 0.9 collective-permute-start.53
  133.3 1.2 collective-permute-start.54
  134.9 1.3 collective-permute-start.43
  138.1 1.6 %collective-permute-done.43 = bf16[16,3584]{1,0:T(8,128)(2,1)S(1)} collective-permute-done((bf16[16,3584]{1,0:T(8,128)(2,1)S(1)}, bf16[16,3584]{1,0:T(8,128)(2,1)S(1)}, u32[]{:S(2)}, u32[]{:S(2)}) %collective-permute-start.43) | collective-permute-done | bytes 114720 | tf_op jit(solution)/shard_map/ppermute | solution.py:829
  139.7 1.3 collective-permute-done.44
  143.2 0.9 collective-permute-done.55
  144.2 0.9 maximum_select_fusion
  (134 shorter events, 19.1 us)
Async XLA Ops:
  0.0 12.8 %copy-start.1 = (bf16[64,7168]{1,0:T(8,128)(2,1)S(1)}, bf16[64,7168]{1,0:T(8,128)(2,1)}, u32[]{:S(2)}) copy-start(bf16[64,7168]{1,0:T(8,128)(2,1)} %res.1) | copy-start | bytes 2752516
  9.7 16.3 %collective-permute-start.10 = (bf16[32,2048]{1,0:T(8,128)(2,1)S(1)}, bf16[32,2048]{1,0:T(8,128)(2,1)S(1)}, u32[]{:S(2)}, u32[]{:S(2)}) collective-permute-start(bf16[32,2048]{1,0:T(8,128)(2,1)S(1)} %get-tuple-element.161), channel_id=1, source_target_pairs={{0,4},{4,8},{8,12},{12,14},{14,10},{10,6},{6,2},{2,0},{1,5},{5,9},... | collective-permute-start | bytes 393224 | tf_op jit(solution)/shard_map/ppermute | solution.py:829
  13.3 42.3 %slice-start.6 = ((s8[7340032]{0:T(1024)(128)(4,1)}), s8[4194304]{0:T(1024)(128)(4,1)S(1)}, s32[]{:S(2)}) async-start(s8[7340032]{0:T(1024)(128)(4,1)} %bitcast.29), calls=%async_computation.6 | async-start | bytes 8388608
  13.4 10.5 %collective-permute-start = (bf16[64,896]{1,0:T(8,128)(2,1)S(1)}, bf16[64,896]{1,0:T(8,128)(2,1)S(1)}, u32[]{:S(2)}, u32[]{:S(2)}) collective-permute-start(bf16[64,896]{1,0:T(8,128)(2,1)S(1)} %get-tuple-element.176.own), channel_id=1, source_target_pairs={{1,9},{3,11},{5,13},{7,15},{9,1},{11,3},{13,5},{15,7},{17,25},{19,... | collective-permute-start | bytes 344072 | tf_op jit(solution)/shard_map/ppermute | solution.py:856
  14.2 9.7 %collective-permute-start.1 = (bf16[64,896]{1,0:T(8,128)(2,1)S(1)}, bf16[64,896]{1,0:T(8,128)(2,1)S(1)}, u32[]{:S(2)}, u32[]{:S(2)}) collective-permute-start(bf16[64,896]{1,0:T(8,128)(2,1)S(1)} %get-tuple-element.139), channel_id=1, source_target_pairs={{0,2},{1,11},{2,4},{3,13},{4,6},{5,15},{6,8},{7,1},{8,10},{9,3},{1... | collective-permute-start | bytes 344072 | tf_op jit(solution)/shard_map/ppermute | solution.py:856
  14.2 11.8 %collective-permute-start.11 = (bf16[32,2048]{1,0:T(8,128)(2,1)S(1)}, bf16[32,2048]{1,0:T(8,128)(2,1)S(1)}, u32[]{:S(2)}, u32[]{:S(2)}) collective-permute-start(bf16[32,2048]{1,0:T(8,128)(2,1)S(1)} %get-tuple-element.181.refs_0_), channel_id=1, source_target_pairs={{4,0},{8,4},{12,8},{14,12},{10,14},{6,10},{2,6},{0,2},{5,1},{9,5},... | collective-permute-start | bytes 393224 | tf_op jit(solution)/shard_map/ppermute | solution.py:832
  17.9 37.8 %slice-start.7 = ((s8[7340032]{0:T(1024)(128)(4,1)}), s8[3145728]{0:T(1024)(128)(4,1)S(1)}, s32[]{:S(2)}) async-start(s8[7340032]{0:T(1024)(128)(4,1)} %bitcast.29), calls=%async_computation.7 | async-start | bytes 6291456
  23.9 7.7 %collective-permute-start.3 = (bf16[32,2048]{1,0:T(8,128)(2,1)S(1)}, bf16[32,2048]{1,0:T(8,128)(2,1)S(1)}, u32[]{:S(2)}, u32[]{:S(2)}) collective-permute-start(bf16[32,2048]{1,0:T(8,128)(2,1)S(1)} %get-tuple-element.151.refs_0_), channel_id=1, source_target_pairs={{4,0},{8,4},{12,8},{14,12},{10,14},{6,10},{2,6},{0,2},{5,1},{9,5},... | collective-permute-start | bytes 393224 | tf_op jit(solution)/shard_map/ppermute | solution.py:832
  25.5 6.1 %collective-permute-start.2 = (bf16[32,2048]{1,0:T(8,128)(2,1)S(1)}, bf16[32,2048]{1,0:T(8,128)(2,1)S(1)}, u32[]{:S(2)}, u32[]{:S(2)}) collective-permute-start(bf16[32,2048]{1,0:T(8,128)(2,1)S(1)} %get-tuple-element.148), channel_id=1, source_target_pairs={{0,4},{4,8},{8,12},{12,14},{14,10},{10,6},{6,2},{2,0},{1,5},{5,9},... | collective-permute-start | bytes 393224 | tf_op jit(solution)/shard_map/ppermute | solution.py:829
  26.0 7.8 %collective-permute-start.13 = (bf16[32,2048]{1,0:T(8,128)(2,1)S(1)}, bf16[32,2048]{1,0:T(8,128)(2,1)S(1)}, u32[]{:S(2)}, u32[]{:S(2)}) collective-permute-start(bf16[32,2048]{1,0:T(8,128)(2,1)S(1)} %broadcast_select_fusion.4), channel_id=1, source_target_pairs={{4,0},{8,4},{12,8},{14,12},{10,14},{6,10},{2,6},{0,2},{5,1},{9,5},... | collective-permute-start | bytes 393224 | tf_op jit(solution)/shard_map/ppermute | solution.py:832
  27.7 7.4 %collective-permute-start.12 = (bf16[32,2048]{1,0:T(8,128)(2,1)S(1)}, bf16[32,2048]{1,0:T(8,128)(2,1)S(1)}, u32[]{:S(2)}, u32[]{:S(2)}) collective-permute-start(bf16[32,2048]{1,0:T(8,128)(2,1)S(1)} %broadcast_select_fusion.5), channel_id=1, source_target_pairs={{0,4},{4,8},{8,12},{12,14},{14,10},{10,6},{6,2},{2,0},{1,5},{5,9},... | collective-permute-start | bytes 393224 | tf_op jit(solution)/shard_map/ppermute | solution.py:829
  28.1 20.5 %collective-permute-start.17 = (bf16[64,896]{1,0:T(8,128)(2,1)S(1)}, bf16[64,896]{1,0:T(8,128)(2,1)S(1)}, u32[]{:S(2)}, u32[]{:S(2)}) collective-permute-start(bf16[64,896]{1,0:T(8,128)(2,1)S(1)} %get-tuple-element.172), channel_id=1, source_target_pairs={{0,4},{1,13},{2,6},{3,15},{4,8},{5,1},{6,10},{7,3},{8,12},{9,5},{1... | collective-permute-start | bytes 344072 | tf_op jit(solution)/shard_map/ppermute | solution.py:856
  31.6 17.0 %collective-permute-start.18 = (bf16[64,896]{1,0:T(8,128)(2,1)S(1)}, bf16[64,896]{1,0:T(8,128)(2,1)S(1)}, u32[]{:S(2)}, u32[]{:S(2)}) collective-permute-start(bf16[64,896]{1,0:T(8,128)(2,1)S(1)} %get-tuple-element.173), channel_id=1, source_target_pairs={{0,6},{1,15},{2,8},{3,1},{4,10},{5,3},{6,12},{7,5},{8,14},{9,7},{1... | collective-permute-start | bytes 344072 | tf_op jit(solution)/shard_map/ppermute | solution.py:856
  33.0 7.8 %collective-permute-start.5 = (bf16[32,2048]{1,0:T(8,128)(2,1)S(1)}, bf16[32,2048]{1,0:T(8,128)(2,1)S(1)}, u32[]{:S(2)}, u32[]{:S(2)}) collective-permute-start(bf16[32,2048]{1,0:T(8,128)(2,1)S(1)} %broadcast_select_fusion.10), channel_id=1, source_target_pairs={{4,0},{8,4},{12,8},{14,12},{10,14},{6,10},{2,6},{0,2},{5,1},{9,5},... | collective-permute-start | bytes 393224 | tf_op jit(solution)/shard_map/ppermute | solution.py:832
  33.8 7.0 %collective-permute-start.4 = (bf16[32,2048]{1,0:T(8,128)(2,1)S(1)}, bf16[32,2048]{1,0:T(8,128)(2,1)S(1)}, u32[]{:S(2)}, u32[]{:S(2)}) collective-permute-start(bf16[32,2048]{1,0:T(8,128)(2,1)S(1)} %broadcast_select_fusion.11), channel_id=1, source_target_pairs={{0,4},{4,8},{8,12},{12,14},{14,10},{10,6},{6,2},{2,0},{1,5},{5,9},... | collective-permute-start | bytes 393224 | tf_op jit(solution)/shard_map/ppermute | solution.py:829
  35.1 8.6 %collective-permute-start.15 = (bf16[32,2048]{1,0:T(8,128)(2,1)S(1)}, bf16[32,2048]{1,0:T(8,128)(2,1)S(1)}, u32[]{:S(2)}, u32[]{:S(2)}) collective-permute-start(bf16[32,2048]{1,0:T(8,128)(2,1)S(1)} %broadcast_select_fusion.2), channel_id=1, source_target_pairs={{4,0},{8,4},{12,8},{14,12},{10,14},{6,10},{2,6},{0,2},{5,1},{9,5},... | collective-permute-start | bytes 393224 | tf_op jit(solution)/shard_map/ppermute | solution.py:832
  40.8 5.3 %collective-permute-start.14 = (bf16[32,2048]{1,0:T(8,128)(2,1)S(1)}, bf16[32,2048]{1,0:T(8,128)(2,1)S(1)}, u32[]{:S(2)}, u32[]{:S(2)}) collective-permute-start(bf16[32,2048]{1,0:T(8,128)(2,1)S(1)} %broadcast_select_fusion.3), channel_id=1, source_target_pairs={{0,4},{4,8},{8,12},{12,14},{14,10},{10,6},{6,2},{2,0},{1,5},{5,9},... | collective-permute-start | bytes 393224 | tf_op jit(solution)/shard_map/ppermute | solution.py:829
  40.9 7.7 %collective-permute-start.7 = (bf16[32,2048]{1,0:T(8,128)(2,1)S(1)}, bf16[32,2048]{1,0:T(8,128)(2,1)S(1)}, u32[]{:S(2)}, u32[]{:S(2)}) collective-permute-start(bf16[32,2048]{1,0:T(8,128)(2,1)S(1)} %broadcast_select_fusion.8), channel_id=1, source_target_pairs={{4,0},{8,4},{12,8},{14,12},{10,14},{6,10},{2,6},{0,2},{5,1},{9,5},... | collective-permute-start | bytes 393224 | tf_op jit(solution)/shard_map/ppermute | solution.py:832
  43.6 9.9 %collective-permute-start.6 = (bf16[32,2048]{1,0:T(8,128)(2,1)S(1)}, bf16[32,2048]{1,0:T(8,128)(2,1)S(1)}, u32[]{:S(2)}, u32[]{:S(2)}) collective-permute-start(bf16[32,2048]{1,0:T(8,128)(2,1)S(1)} %broadcast_select_fusion.9), channel_id=1, source_target_pairs={{0,4},{4,8},{8,12},{12,14},{14,10},{10,6},{6,2},{2,0},{1,5},{5,9},... | collective-permute-start | bytes 393224 | tf_op jit(solution)/shard_map/ppermute | solution.py:829
  46.1 20.3 %slice-start.2 = ((s8[8257536]{0:T(1024)(128)(4,1)}), s8[4194304]{0:T(1024)(128)(4,1)S(1)}, s32[]{:S(2)}) async-start(s8[8257536]{0:T(1024)(128)(4,1)} %bitcast.19), calls=%async_computation.2 | async-start | bytes 8388608
  46.1 6.6 %collective-permute-start.16 = (bf16[32,2048]{1,0:T(8,128)(2,1)S(1)}, bf16[32,2048]{1,0:T(8,128)(2,1)S(1)}, u32[]{:S(2)}, u32[]{:S(2)}) collective-permute-start(bf16[32,2048]{1,0:T(8,128)(2,1)S(1)} %broadcast_select_fusion.1), channel_id=1, source_target_pairs={{0,4},{4,8},{8,12},{12,14},{14,10},{10,6},{6,2},{2,0},{1,5},{5,9},... | collective-permute-start | bytes 393224 | tf_op jit(solution)/shard_map/ppermute | solution.py:829
  48.6 7.0 %collective-permute-start.19 = (bf16[32,2048]{1,0:T(8,128)(2,1)S(1)}, bf16[32,2048]{1,0:T(8,128)(2,1)S(1)}, u32[]{:S(2)}, u32[]{:S(2)}) collective-permute-start(bf16[32,2048]{1,0:T(8,128)(2,1)S(1)} %broadcast_select_fusion), channel_id=1, source_target_pairs={{4,0},{8,4},{12,8},{14,12},{10,14},{6,10},{2,6},{0,2},{5,1},{9,5},... | collective-permute-start | bytes 393224 | tf_op jit(solution)/shard_map/ppermute | solution.py:832
  53.3 2.4 %collective-permute-start.20 = (bf16[128,896]{1,0:T(8,128)(2,1)S(1)}, bf16[128,896]{1,0:T(8,128)(2,1)S(1)}, u32[]{:S(2)}, u32[]{:S(2)}) collective-permute-start(bf16[128,896]{1,0:T(8,128)(2,1)S(1)} %share.1), channel_id=1, source_target_pairs={{0,1},{1,0},{2,3},{3,2},{4,5},{5,4},{6,7},{7,6},{8,9},{9,8},{10,11... | collective-permute-start | bytes 688136 | tf_op jit(solution)/shard_map/ppermute | solution.py:835
  53.6 5.7 %collective-permute-start.8 = (bf16[32,2048]{1,0:T(8,128)(2,1)S(1)}, bf16[32,2048]{1,0:T(8,128)(2,1)S(1)}, u32[]{:S(2)}, u32[]{:S(2)}) collective-permute-start(bf16[32,2048]{1,0:T(8,128)(2,1)S(1)} %broadcast_select_fusion.7), channel_id=1, source_target_pairs={{0,4},{4,8},{8,12},{12,14},{14,10},{10,6},{6,2},{2,0},{1,5},{5,9},... | collective-permute-start | bytes 393224 | tf_op jit(solution)/shard_map/ppermute | solution.py:829
  54.2 6.3 %collective-permute-start.9 = (bf16[32,2048]{1,0:T(8,128)(2,1)S(1)}, bf16[32,2048]{1,0:T(8,128)(2,1)S(1)}, u32[]{:S(2)}, u32[]{:S(2)}) collective-permute-start(bf16[32,2048]{1,0:T(8,128)(2,1)S(1)} %broadcast_select_fusion.6), channel_id=1, source_target_pairs={{4,0},{8,4},{12,8},{14,12},{10,14},{6,10},{2,6},{0,2},{5,1},{9,5},... | collective-permute-start | bytes 393224 | tf_op jit(solution)/shard_map/ppermute | solution.py:832
  55.7 10.7 %slice-start = ((s8[8257536]{0:T(1024)(128)(4,1)}), s8[4194304]{0:T(1024)(128)(4,1)S(1)}, s32[]{:S(2)}) async-start(s8[8257536]{0:T(1024)(128)(4,1)} %bitcast.11), calls=%async_computation | async-start | bytes 8388608
  57.6 8.8 %slice-start.1 = ((s8[8257536]{0:T(1024)(128)(4,1)}), s8[4063232]{0:T(1024)(128)(4,1)S(1)}, s32[]{:S(2)}) async-start(s8[8257536]{0:T(1024)(128)(4,1)} %bitcast.11), calls=%async_computation.1 | async-start | bytes 8126464
  57.7 8.8 %slice-start.3 = ((s8[8257536]{0:T(1024)(128)(4,1)}), s8[4063232]{0:T(1024)(128)(4,1)S(1)}, s32[]{:S(2)}) async-start(s8[8257536]{0:T(1024)(128)(4,1)} %bitcast.19), calls=%async_computation.3 | async-start | bytes 8126464
  57.7 8.8 %copy-start = (f32[7168]{0:T(1024)S(1)}, f32[7168]{0:T(1024)}, u32[]{:S(2)}) copy-start(f32[7168]{0:T(1024)} %param.24) | copy-start | bytes 86020
  62.5 1.6 %collective-permute-start.21 = (bf16[144,896]{1,0:T(8,128)(2,1)S(1)}, bf16[144,896]{1,0:T(8,128)(2,1)S(1)}, u32[]{:S(2)}, u32[]{:S(2)}) collective-permute-start(bf16[144,896]{1,0:T(8,128)(2,1)S(1)} %get-tuple-element.193), channel_id=1, source_target_pairs={{0,1},{1,0},{2,3},{3,2},{4,5},{5,4},{6,7},{7,6},{8,9},{9,8},{10,11... | collective-permute-start | bytes 774152 | tf_op jit(solution)/shard_map/ppermute | solution.py:835
  64.2 2.2 %collective-permute-start.24 = (bf16[144,896]{1,0:T(8,128)(2,1)S(1)}, bf16[144,896]{1,0:T(8,128)(2,1)S(1)}, u32[]{:S(2)}, u32[]{:S(2)}) collective-permute-start(bf16[144,896]{1,0:T(8,128)(2,1)S(1)} %add_convert_fusion.refs_0_.refs_1_), channel_id=1, source_target_pairs={{0,1},{1,0},{2,3},{3,2},{4,5},{5,4},{6,7},{7,6},{8,9},{9,8},{10,11... | collective-permute-start | bytes 774152 | tf_op jit(solution)/shard_map/ppermute | solution.py:835
  64.4 8.5 %collective-permute-start.22 = (bf16[144,896]{1,0:T(8,128)(2,1)S(1)}, bf16[144,896]{1,0:T(8,128)(2,1)S(1)}, u32[]{:S(2)}, u32[]{:S(2)}) collective-permute-start(bf16[144,896]{1,0:T(8,128)(2,1)S(1)} %add_convert_fusion.refs_0_.refs_1_), channel_id=1, source_target_pairs={{0,4},{4,8},{8,12},{12,14},{14,10},{10,6},{6,2},{2,0},{1,5},{5,9},... | collective-permute-start | bytes 774152 | tf_op jit(solution)/shard_map/ppermute | solution.py:829
  66.1 8.2 %collective-permute-start.23 = (bf16[144,896]{1,0:T(8,128)(2,1)S(1)}, bf16[144,896]{1,0:T(8,128)(2,1)S(1)}, u32[]{:S(2)}, u32[]{:S(2)}) collective-permute-start(bf16[144,896]{1,0:T(8,128)(2,1)S(1)} %add_convert_fusion.refs_0_.refs_1_), channel_id=1, source_target_pairs={{4,0},{8,4},{12,8},{14,12},{10,14},{6,10},{2,6},{0,2},{5,1},{9,5},... | collective-permute-start | bytes 774152 | tf_op jit(solution)/shard_map/ppermute | solution.py:832
  74.4 2.2 %collective-permute-start.27 = (bf16[288,896]{1,0:T(8,128)(2,1)S(1)}, bf16[288,896]{1,0:T(8,128)(2,1)S(1)}, u32[]{:S(2)}, u32[]{:S(2)}) collective-permute-start(bf16[288,896]{1,0:T(8,128)(2,1)S(1)} %pad_maximum_fusion), channel_id=1, source_target_pairs={{0,1},{1,0},{2,3},{3,2},{4,5},{5,4},{6,7},{7,6},{8,9},{9,8},{10,11... | collective-permute-start | bytes 1548296 | tf_op jit(solution)/shard_map/ppermute | solution.py:835
  74.5 8.6 %collective-permute-start.25 = (bf16[144,896]{1,0:T(8,128)(2,1)S(1)}, bf16[144,896]{1,0:T(8,128)(2,1)S(1)}, u32[]{:S(2)}, u32[]{:S(2)}) collective-permute-start(bf16[144,896]{1,0:T(8,128)(2,1)S(1)} %collective-permute-done.22.refs_0_.refs_2_.refs_3_), channel_id=1, source_target_pairs={{0,4},{4,8},{8,12},{12,14},{14,10},{10,6},{6,2},{2,0},{1,5},{5,9},... | collective-permute-start | bytes 774152 | tf_op jit(solution)/shard_map/ppermute | solution.py:829
  74.9 8.3 %collective-permute-start.26 = (bf16[144,896]{1,0:T(8,128)(2,1)S(1)}, bf16[144,896]{1,0:T(8,128)(2,1)S(1)}, u32[]{:S(2)}, u32[]{:S(2)}) collective-permute-start(bf16[144,896]{1,0:T(8,128)(2,1)S(1)} %collective-permute-done.23.refs_1_.refs_4_.refs_5_), channel_id=1, source_target_pairs={{4,0},{8,4},{12,8},{14,12},{10,14},{6,10},{2,6},{0,2},{5,1},{9,5},... | collective-permute-start | bytes 774152 | tf_op jit(solution)/shard_map/ppermute | solution.py:832
  83.2 2.2 %collective-permute-start.30 = (bf16[288,896]{1,0:T(8,128)(2,1)S(1)}, bf16[288,896]{1,0:T(8,128)(2,1)S(1)}, u32[]{:S(2)}, u32[]{:S(2)}) collective-permute-start(bf16[288,896]{1,0:T(8,128)(2,1)S(1)} %pad_maximum_fusion.1), channel_id=1, source_target_pairs={{0,1},{1,0},{2,3},{3,2},{4,5},{5,4},{6,7},{7,6},{8,9},{9,8},{10,11... | collective-permute-start | bytes 1548296 | tf_op jit(solution)/shard_map/ppermute | solution.py:835
  83.3 8.6 %collective-permute-start.28 = (bf16[144,896]{1,0:T(8,128)(2,1)S(1)}, bf16[144,896]{1,0:T(8,128)(2,1)S(1)}, u32[]{:S(2)}, u32[]{:S(2)}) collective-permute-start(bf16[144,896]{1,0:T(8,128)(2,1)S(1)} %collective-permute-done.25.refs_0_.refs_6_.refs_7_), channel_id=1, source_target_pairs={{0,4},{4,8},{8,12},{12,14},{14,10},{10,6},{6,2},{2,0},{1,5},{5,9},... | collective-permute-start | bytes 774152 | tf_op jit(solution)/shard_map/ppermute | solution.py:829
  84.7 8.3 %collective-permute-start.29 = (bf16[144,896]{1,0:T(8,128)(2,1)S(1)}, bf16[144,896]{1,0:T(8,128)(2,1)S(1)}, u32[]{:S(2)}, u32[]{:S(2)}) collective-permute-start(bf16[144,896]{1,0:T(8,128)(2,1)S(1)} %collective-permute-done.26.refs_1_.refs_8_.refs_9_), channel_id=1, source_target_pairs={{4,0},{8,4},{12,8},{14,12},{10,14},{6,10},{2,6},{0,2},{5,1},{9,5},... | collective-permute-start | bytes 774152 | tf_op jit(solution)/shard_map/ppermute | solution.py:832
  93.0 2.2 %collective-permute-start.33 = (bf16[288,896]{1,0:T(8,128)(2,1)S(1)}, bf16[288,896]{1,0:T(8,128)(2,1)S(1)}, u32[]{:S(2)}, u32[]{:S(2)}) collective-permute-start(bf16[288,896]{1,0:T(8,128)(2,1)S(1)} %pad_maximum_fusion.2), channel_id=1, source_target_pairs={{0,1},{1,0},{2,3},{3,2},{4,5},{5,4},{6,7},{7,6},{8,9},{9,8},{10,11... | collective-permute-start | bytes 1548296 | tf_op jit(solution)/shard_map/ppermute | solution.py:835
  93.1 7.1 %collective-permute-start.31 = (bf16[80,896]{1,0:T(8,128)(2,1)S(1)}, bf16[80,896]{1,0:T(8,128)(2,1)S(1)}, u32[]{:S(2)}, u32[]{:S(2)}) collective-permute-start(bf16[80,896]{1,0:T(8,128)(2,1)S(1)} %slice.18), channel_id=1, source_target_pairs={{0,4},{4,8},{8,12},{12,14},{14,10},{10,6},{6,2},{2,0},{1,5},{5,9},... | collective-permute-start | bytes 430088 | tf_op jit(solution)/shard_map/ppermute | solution.py:829
  94.9 5.3 %collective-permute-start.32 = (bf16[64,896]{1,0:T(8,128)(2,1)S(1)}, bf16[64,896]{1,0:T(8,128)(2,1)S(1)}, u32[]{:S(2)}, u32[]{:S(2)}) collective-permute-start(bf16[64,896]{1,0:T(8,128)(2,1)S(1)} %slice.19), channel_id=1, source_target_pairs={{4,0},{8,4},{12,8},{14,12},{10,14},{6,10},{2,6},{0,2},{5,1},{9,5},... | collective-permute-start | bytes 344072 | tf_op jit(solution)/shard_map/ppermute | solution.py:832
  100.3 1.6 %collective-permute-start.34 = (bf16[80,896]{1,0:T(8,128)(2,1)S(1)}, bf16[80,896]{1,0:T(8,128)(2,1)S(1)}, u32[]{:S(2)}, u32[]{:S(2)}) collective-permute-start(bf16[80,896]{1,0:T(8,128)(2,1)S(1)} %collective-permute-done.31.refs_0_), channel_id=1, source_target_pairs={{0,1},{1,0},{2,3},{3,2},{4,5},{5,4},{6,7},{7,6},{8,9},{9,8},{10,11... | collective-permute-start | bytes 430088 | tf_op jit(solution)/shard_map/ppermute | solution.py:835
  100.3 1.5 %collective-permute-start.35 = (bf16[64,896]{1,0:T(8,128)(2,1)S(1)}, bf16[64,896]{1,0:T(8,128)(2,1)S(1)}, u32[]{:S(2)}, u32[]{:S(2)}) collective-permute-start(bf16[64,896]{1,0:T(8,128)(2,1)S(1)} %collective-permute-done.32.refs_1_), channel_id=1, source_target_pairs={{0,1},{1,0},{2,3},{3,2},{4,5},{5,4},{6,7},{7,6},{8,9},{9,8},{10,11... | collective-permute-start | bytes 344072 | tf_op jit(solution)/shard_map/ppermute | solution.py:835
  104.9 4.6 %collective-permute-start.46 = (bf16[144,3584]{1,0:T(8,128)(2,1)S(1)}, bf16[144,3584]{1,0:T(8,128)(2,1)S(1)}, u32[]{:S(2)}, u32[]{:S(2)}) collective-permute-start(bf16[144,3584]{1,0:T(8,128)(2,1)S(1)} %contract.7), channel_id=1, source_target_pairs={{0,1},{1,0},{2,3},{3,2},{4,5},{5,4},{6,7},{7,6},{8,9},{9,8},{10,11... | collective-permute-start | bytes 3096584 | tf_op jit(solution)/shard_map/ppermute | solution.py:835
  106.3 8.4 %collective-permute-start.36 = (bf16[144,3584]{1,0:T(8,128)(2,1)S(1)}, bf16[144,3584]{1,0:T(8,128)(2,1)S(1)}, u32[]{:S(2)}, u32[]{:S(2)}) collective-permute-start(bf16[144,3584]{1,0:T(8,128)(2,1)S(1)} %contract.5), channel_id=1, source_target_pairs={{0,1},{1,0},{2,3},{3,2},{4,5},{5,4},{6,7},{7,6},{8,9},{9,8},{10,11... | collective-permute-start | bytes 3096584 | tf_op jit(solution)/shard_map/ppermute | solution.py:835
  110.4 7.2 %collective-permute-start.48 = (bf16[16,3584]{1,0:T(8,128)(2,1)S(1)}, bf16[16,3584]{1,0:T(8,128)(2,1)S(1)}, u32[]{:S(2)}, u32[]{:S(2)}) collective-permute-start(bf16[16,3584]{1,0:T(8,128)(2,1)S(1)} %convert_element_type.162), channel_id=1, source_target_pairs={{4,0},{8,4},{12,8},{14,12},{10,14},{6,10},{2,6},{0,2},{5,1},{9,5},... | collective-permute-start | bytes 344072 | tf_op jit(solution)/shard_map/ppermute | solution.py:832
  112.9 4.9 %collective-permute-start.47 = (bf16[16,3584]{1,0:T(8,128)(2,1)S(1)}, bf16[16,3584]{1,0:T(8,128)(2,1)S(1)}, u32[]{:S(2)}, u32[]{:S(2)}) collective-permute-start(bf16[16,3584]{1,0:T(8,128)(2,1)S(1)} %convert_element_type.161), channel_id=1, source_target_pairs={{0,4},{4,8},{8,12},{12,14},{14,10},{10,6},{6,2},{2,0},{1,5},{5,9},... | collective-permute-start | bytes 344072 | tf_op jit(solution)/shard_map/ppermute | solution.py:829
  115.5 6.0 %collective-permute-start.38 = (bf16[16,3584]{1,0:T(8,128)(2,1)S(1)}, bf16[16,3584]{1,0:T(8,128)(2,1)S(1)}, u32[]{:S(2)}, u32[]{:S(2)}) collective-permute-start(bf16[16,3584]{1,0:T(8,128)(2,1)S(1)} %convert_element_type.142), channel_id=1, source_target_pairs={{4,0},{8,4},{12,8},{14,12},{10,14},{6,10},{2,6},{0,2},{5,1},{9,5},... | collective-permute-start | bytes 344072 | tf_op jit(solution)/shard_map/ppermute | solution.py:832
  115.9 5.7 %collective-permute-start.37 = (bf16[16,3584]{1,0:T(8,128)(2,1)S(1)}, bf16[16,3584]{1,0:T(8,128)(2,1)S(1)}, u32[]{:S(2)}, u32[]{:S(2)}) collective-permute-start(bf16[16,3584]{1,0:T(8,128)(2,1)S(1)} %convert_element_type.141), channel_id=1, source_target_pairs={{0,4},{4,8},{8,12},{12,14},{14,10},{10,6},{6,2},{2,0},{1,5},{5,9},... | collective-permute-start | bytes 344072 | tf_op jit(solution)/shard_map/ppermute | solution.py:829
  117.8 6.0 %collective-permute-start.50 = (bf16[16,3584]{1,0:T(8,128)(2,1)S(1)}, bf16[16,3584]{1,0:T(8,128)(2,1)S(1)}, u32[]{:S(2)}, u32[]{:S(2)}) collective-permute-start(bf16[16,3584]{1,0:T(8,128)(2,1)S(1)} %add_convert_fusion.5), channel_id=1, source_target_pairs={{4,0},{8,4},{12,8},{14,12},{10,14},{6,10},{2,6},{0,2},{5,1},{9,5},... | collective-permute-start | bytes 344072 | tf_op jit(solution)/shard_map/ppermute | solution.py:832
  119.1 6.0 %collective-permute-start.49 = (bf16[16,3584]{1,0:T(8,128)(2,1)S(1)}, bf16[16,3584]{1,0:T(8,128)(2,1)S(1)}, u32[]{:S(2)}, u32[]{:S(2)}) collective-permute-start(bf16[16,3584]{1,0:T(8,128)(2,1)S(1)} %add_convert_fusion.6), channel_id=1, source_target_pairs={{0,4},{4,8},{8,12},{12,14},{14,10},{10,6},{6,2},{2,0},{1,5},{5,9},... | collective-permute-start | bytes 344072 | tf_op jit(solution)/shard_map/ppermute | solution.py:829
  121.6 5.6 %collective-permute-start.40 = (bf16[16,3584]{1,0:T(8,128)(2,1)S(1)}, bf16[16,3584]{1,0:T(8,128)(2,1)S(1)}, u32[]{:S(2)}, u32[]{:S(2)}) collective-permute-start(bf16[16,3584]{1,0:T(8,128)(2,1)S(1)} %add_convert_fusion.11), channel_id=1, source_target_pairs={{4,0},{8,4},{12,8},{14,12},{10,14},{6,10},{2,6},{0,2},{5,1},{9,5},... | collective-permute-start | bytes 344072 | tf_op jit(solution)/shard_map/ppermute | solution.py:832
  122.7 5.3 %collective-permute-start.39 = (bf16[16,3584]{1,0:T(8,128)(2,1)S(1)}, bf16[16,3584]{1,0:T(8,128)(2,1)S(1)}, u32[]{:S(2)}, u32[]{:S(2)}) collective-permute-start(bf16[16,3584]{1,0:T(8,128)(2,1)S(1)} %add_convert_fusion.12), channel_id=1, source_target_pairs={{0,4},{4,8},{8,12},{12,14},{14,10},{10,6},{6,2},{2,0},{1,5},{5,9},... | collective-permute-start | bytes 344072 | tf_op jit(solution)/shard_map/ppermute | solution.py:829
  125.1 5.2 %collective-permute-start.52 = (bf16[16,3584]{1,0:T(8,128)(2,1)S(1)}, bf16[16,3584]{1,0:T(8,128)(2,1)S(1)}, u32[]{:S(2)}, u32[]{:S(2)}) collective-permute-start(bf16[16,3584]{1,0:T(8,128)(2,1)S(1)} %add_convert_fusion.3), channel_id=1, source_target_pairs={{4,0},{8,4},{12,8},{14,12},{10,14},{6,10},{2,6},{0,2},{5,1},{9,5},... | collective-permute-start | bytes 344072 | tf_op jit(solution)/shard_map/ppermute | solution.py:832
  126.4 6.0 %collective-permute-start.51 = (bf16[16,3584]{1,0:T(8,128)(2,1)S(1)}, bf16[16,3584]{1,0:T(8,128)(2,1)S(1)}, u32[]{:S(2)}, u32[]{:S(2)}) collective-permute-start(bf16[16,3584]{1,0:T(8,128)(2,1)S(1)} %add_convert_fusion.4), channel_id=1, source_target_pairs={{0,4},{4,8},{8,12},{12,14},{14,10},{10,6},{6,2},{2,0},{1,5},{5,9},... | collective-permute-start | bytes 344072 | tf_op jit(solution)/shard_map/ppermute | solution.py:829
  128.1 6.4 %collective-permute-start.42 = (bf16[16,3584]{1,0:T(8,128)(2,1)S(1)}, bf16[16,3584]{1,0:T(8,128)(2,1)S(1)}, u32[]{:S(2)}, u32[]{:S(2)}) collective-permute-start(bf16[16,3584]{1,0:T(8,128)(2,1)S(1)} %add_convert_fusion.9), channel_id=1, source_target_pairs={{4,0},{8,4},{12,8},{14,12},{10,14},{6,10},{2,6},{0,2},{5,1},{9,5},... | collective-permute-start | bytes 344072 | tf_op jit(solution)/shard_map/ppermute | solution.py:832
  129.1 5.8 %collective-permute-start.41 = (bf16[16,3584]{1,0:T(8,128)(2,1)S(1)}, bf16[16,3584]{1,0:T(8,128)(2,1)S(1)}, u32[]{:S(2)}, u32[]{:S(2)}) collective-permute-start(bf16[16,3584]{1,0:T(8,128)(2,1)S(1)} %add_convert_fusion.10), channel_id=1, source_target_pairs={{0,4},{4,8},{8,12},{12,14},{14,10},{10,6},{6,2},{2,0},{1,5},{5,9},... | collective-permute-start | bytes 344072 | tf_op jit(solution)/shard_map/ppermute | solution.py:829
  132.4 5.2 %collective-permute-start.53 = (bf16[16,3584]{1,0:T(8,128)(2,1)S(1)}, bf16[16,3584]{1,0:T(8,128)(2,1)S(1)}, u32[]{:S(2)}, u32[]{:S(2)}) collective-permute-start(bf16[16,3584]{1,0:T(8,128)(2,1)S(1)} %add_convert_fusion.2), channel_id=1, source_target_pairs={{0,4},{4,8},{8,12},{12,14},{14,10},{10,6},{6,2},{2,0},{1,5},{5,9},... | collective-permute-start | bytes 344072 | tf_op jit(solution)/shard_map/ppermute | solution.py:829
  133.3 4.8 %collective-permute-start.54 = (bf16[16,3584]{1,0:T(8,128)(2,1)S(1)}, bf16[16,3584]{1,0:T(8,128)(2,1)S(1)}, u32[]{:S(2)}, u32[]{:S(2)}) collective-permute-start(bf16[16,3584]{1,0:T(8,128)(2,1)S(1)} %add_convert_fusion.1), channel_id=1, source_target_pairs={{4,0},{8,4},{12,8},{14,12},{10,14},{6,10},{2,6},{0,2},{5,1},{9,5},... | collective-permute-start | bytes 344072 | tf_op jit(solution)/shard_map/ppermute | solution.py:832
  134.9 4.8 %collective-permute-start.43 = (bf16[16,3584]{1,0:T(8,128)(2,1)S(1)}, bf16[16,3584]{1,0:T(8,128)(2,1)S(1)}, u32[]{:S(2)}, u32[]{:S(2)}) collective-permute-start(bf16[16,3584]{1,0:T(8,128)(2,1)S(1)} %add_convert_fusion.8), channel_id=1, source_target_pairs={{0,4},{4,8},{8,12},{12,14},{14,10},{10,6},{6,2},{2,0},{1,5},{5,9},... | collective-permute-start | bytes 344072 | tf_op jit(solution)/shard_map/ppermute | solution.py:829
  136.2 4.8 %collective-permute-start.44 = (bf16[16,3584]{1,0:T(8,128)(2,1)S(1)}, bf16[16,3584]{1,0:T(8,128)(2,1)S(1)}, u32[]{:S(2)}, u32[]{:S(2)}) collective-permute-start(bf16[16,3584]{1,0:T(8,128)(2,1)S(1)} %add_convert_fusion.7), channel_id=1, source_target_pairs={{4,0},{8,4},{12,8},{14,12},{10,14},{6,10},{2,6},{0,2},{5,1},{9,5},... | collective-permute-start | bytes 344072 | tf_op jit(solution)/shard_map/ppermute | solution.py:832
  141.2 2.0 %collective-permute-start.45 = (bf16[16,3584]{1,0:T(8,128)(2,1)S(1)}, bf16[16,3584]{1,0:T(8,128)(2,1)S(1)}, u32[]{:S(2)}, u32[]{:S(2)}) collective-permute-start(bf16[16,3584]{1,0:T(8,128)(2,1)S(1)} %get-tuple-element.263), channel_id=1, source_target_pairs={{0,1},{1,0},{2,3},{3,2},{4,5},{5,4},{6,7},{7,6},{8,9},{9,8},{10,11... | collective-permute-start | bytes 344072 | tf_op jit(solution)/shard_map/ppermute | solution.py:835
  142.6 1.5 %collective-permute-start.55 = (bf16[16,3584]{1,0:T(8,128)(2,1)S(1)}, bf16[16,3584]{1,0:T(8,128)(2,1)S(1)}, u32[]{:S(2)}, u32[]{:S(2)}) collective-permute-start(bf16[16,3584]{1,0:T(8,128)(2,1)S(1)} %get-tuple-element.269), channel_id=1, source_target_pairs={{0,1},{1,0},{2,3},{3,2},{4,5},{5,4},{6,7},{7,6},{8,9},{9,8},{10,11... | collective-permute-start | bytes 344072 | tf_op jit(solution)/shard_map/ppermute | solution.py:835
  (2 other events, 6.5 us)

commit v10 on v8

--- a/solution.py
+++ b/solution.py
@@ -138,13 +138,13 @@
 ):
     if lead:
         given, refs = refs[0], refs[1:]
-        q_hbm, cache_hbm, fresh, vw_hbm, tab, head, main, extra, later = refs[:9]
+        q_hbm, cache_hbm, fresh_hbm, vw_hbm, tab, head, main, extra, later = refs[:9]
         flags, refs = refs[9:12], refs[12:]
-        q, keys, vw, latent, fz, q_sem, key_sem, vw_sem, dq = refs
+        q, keys, vw, latent, fz, fresh, q_sem, key_sem, vw_sem, dq = refs
         loaded, base = heads, 0
     else:
-        tab, q_hbm, cache_hbm, fresh, vw_hbm, decoded_here, head, main, extra = refs[:9]
-        q, keys, vw, latent, fz, q_sem, key_sem, vw_sem = refs[9:]
+        tab, q_hbm, cache_hbm, fresh_hbm, vw_hbm, decoded_here, head, main, extra = refs[:9]
+        q, keys, vw, latent, fz, fresh, q_sem, key_sem, vw_sem = refs[9:]
         loaded, base = count, first
     cached, wide = keys.shape[2], keys.shape[1]
     slots = cache_hbm.shape[0] - 1
@@ -179,6 +179,8 @@
         for _ in range(min(number, len(waiting))):
             waiting.pop(0).start()
 
+    fresh_copy = pltpu.make_async_copy(fresh_hbm, fresh, key_sem.at[3])
+    fresh_copy.start()
     even_copy.start()
     q_copy(0).start()
     odd_copy.start()
@@ -197,6 +199,7 @@
         keys[s, lat:] = tail
     keys[odd_slot, :shift] = tail
     fz[...] = jnp.zeros_like(fz)
+    fresh_copy.wait()
     fz[:rows, :lat] = fresh[...].astype(f32)
     fresh_even = fz[...].astype(bf16)
     fresh_odd = pltpu.roll(fz[...], shift, 1).astype(bf16)
@@ -318,13 +321,14 @@
         pltpu.VMEM((count, value, vh), bf16),
         pltpu.VMEM((count // group, 2, group // 2 * rows, value), bf16),
         pltpu.VMEM((-(-rows // 128) * 128, wide), f32),
+        pltpu.VMEM(fresh.shape[::-1], bf16),
         pltpu.SemaphoreType.DMA((loaded // group,)),
-        pltpu.SemaphoreType.DMA((3,)),
+        pltpu.SemaphoreType.DMA((4,)),
         pltpu.SemaphoreType.DMA((count // group,)),
     ]
     out_shape, out_specs = [half] * 3, [whole()] * 3
-    ins = [smem(), hbm, hbm, whole(), hbm]
-    args = [numbers, in_hbm(queries), in_hbm(cache), fresh.T, in_hbm(vw)]
+    ins = [smem()] + [hbm] * 4
+    args = [numbers, in_hbm(queries), in_hbm(cache), in_hbm(fresh.T), in_hbm(vw)]
     if lead:
         scratch.append(pltpu.VMEM((heads * 8, wide), f32))
         out_shape = [jax.ShapeDtypeStruct((table.size,), i32)] + out_shape
@@ -814,15 +818,15 @@
         ]
         pieces[k] = lax.ppermute(packed[k], ("blk", "head"), pairs)
 
-    early = len(packed) // 2
-    for k in range(early):
+    for k in range(1, len(packed)):
         send_piece(k)
     decoded, packed = lax.optimization_barrier((decoded, packed))
     packed = list(packed)
     follow = attend(table, order, tab, *caches, 1, 2, decoded)
-    follow, pieces[:early], out_weight = lax.optimization_barrier(
-        (follow, pieces[:early], out_weight)
+    follow, pieces[1:], packed[0], out_weight = lax.optimization_barrier(
+        (follow, pieces[1:], packed[0], out_weight)
     )
+    send_piece(0)
 
     total = None
     chains = []
@@ -837,15 +841,11 @@
             else:
                 out_f = choose(behind[step - 2], behind[step - 1])
                 out_b = choose(ahead[step - 2], ahead[step - 1])
-            piece = early + step - 1 + part * (len(packed) - early) // 2
-            if 0 < step <= (len(packed) - early) // 2:
-                out_f, out_b, packed[piece] = lax.optimization_barrier((out_f, out_b, packed[piece]))
-                send_piece(piece)
-            else:
-                out_f, out_b = lax.optimization_barrier((out_f, out_b))
+            out_f, out_b = lax.optimization_barrier((out_f, out_b))
             behind.append(send_next(out_f))
             ahead.append(send_prev(out_b))
     gathered = [[main] + behind + ahead + [extra] for _, main, extra, behind, ahead in chains]
+    gathered[0][2], pieces = lax.optimization_barrier((gathered[0][2], pieces))
     shared = swap(share(tab, packed[0], pieces, cores))
     gathered[0], shared = lax.optimization_barrier((gathered[0], shared))
     for part in range(2):
@@ -857,31 +857,28 @@
     gain = norm_gain.reshape(ranks, 1, features)
     weights = (gain, gate_weight, up_weight)
     cut = -(-stream.shape[0] // 32) * 16
-    backs = [stream[:cut], stream[cut:]]
-    fores = list(backs)
-    swapped, backs[1], fores[1] = lax.optimization_barrier((swap(stream), backs[1], fores[1]))
-    sums = expand(tab, [[stream]], [swapped], [RANK], *weights, None, False)
+    back, fore = stream, stream
+    sums = expand(tab, [[stream]], [swap(stream)], [RANK], *weights, None, False)
     blocks, owners = [stream], [RANK]
     done = None
     for step in range(1, reach + 1):
         if done is not None:
-            backs[0], fores[0], done = lax.optimization_barrier((backs[0], fores[0], done))
+            back, fore, done = lax.optimization_barrier((back, fore, done))
         done = sums
         if step < reach:
-            for n in range(2):
-                back, fore = lax.optimization_barrier((backs[n], fores[n]))
-                backs[n], fores[n] = send_next(back), send_prev(fore)
-            arrived = [list(backs), list(fores)]
+            back, fore = send_next(back), send_prev(fore)
+            arrived = [[back], [fore]]
             from_owner = [table.owner_back + step, table.owner_fore + step]
         else:
-            arrived = [[send_next(backs[0]), send_prev(fores[1])]]
+            arrived = [[send_next(back[:cut]), send_prev(fore[cut:])]]
             from_owner = [table.owner_back + step]
-        others = []
-        for chain in zip(*arrived):
-            tied, sums = lax.optimization_barrier((chain, sums))
-            others.append(swap(jnp.concatenate(tied, 0)))
+        tied, sums = lax.optimization_barrier((arrived, sums))
+        if step < reach:
+            others = [swap(jnp.concatenate([x for (x,) in tied], 0))]
+        else:
+            others = [swap(x) for x in tied[0]]
         sums = expand(tab, arrived, others, from_owner, *weights, sums, step == reach)
-        blocks += [jnp.concatenate(x, 0) for x in arrived]
+        blocks += [x[0] if len(x) == 1 else jnp.concatenate(x, 0) for x in arrived]
         owners += from_owner
     (hidden,) = sums
     own = collect(tab, blocks, owners, half).astype(f32)

time: 140 us -> 138 us (0.986)
  starting transfers between devices: 59.3 us -> 53.8 us
  waiting for transfers between devices: 32.8 us -> 37.8 us
    ppermute x23 -> x20, waiting for transfers between devices: 14 us -> 24.6 us  [send_next(): return lax.ppermute(x, 'blk', forward)]
    ppermute x23 -> x20, starting transfers between devices: 24 us -> 19.4 us  [send_prev(): return lax.ppermute(x, 'blk', backward)]
    ppermute x23 -> x20, starting transfers between devices: 28.9 us -> 25 us  [send_next(): return lax.ppermute(x, 'blk', forward)]
    ppermute x23 -> x20, waiting for transfers between devices: 13.8 us -> 10.3 us  [send_prev(): return lax.ppermute(x, 'blk', backward)]
    ppermute x4, starting transfers between devices: 2.82 us -> 6.28 us  [send_piece(): pieces[k] = lax.ppermute(packed[k], ('blk', 'head'), pairs)]
    ppermute x4, waiting for transfers between devices: 2.11 us -> 0.01 us  [send_piece(): pieces[k] = lax.ppermute(packed[k], ('blk', 'head'), pairs)]
    ppermute x15 -> x12, starting transfers between devices: 3.52 us -> 3.1 us  [swap(): return lax.ppermute(x, 'head', exchange)]
    ppermute x15 -> x12, waiting for transfers between devices: 2.87 us -> 2.86 us  [swap(): return lax.ppermute(x, 'head', exchange)]
  transfers between devices with their start and end apart: 65 -> 56, of which waited for: 35 -> 31; matrix products, arithmetic and copies ran while one was open for 1% -> 1% of each run, Pallas kernels for 19% -> 19%
where the time goes in v10:
time: 138 us
  starting transfers between devices  53.8 us (39%)
  Pallas kernels  39.1 us (28%)
  waiting for transfers between devices  37.8 us (27%)
  between operations  3.33 us (2%)
  other arithmetic  2.9 us (2%)
    ppermute x20, starting transfers between devices, send_next(): return lax.ppermute(x, 'blk', forward)  25 us
    ppermute x20, waiting for transfers between devices, send_next(): return lax.ppermute(x, 'blk', forward)  24.6 us
    ppermute x20, starting transfers between devices, send_prev(): return lax.ppermute(x, 'blk', backward)  19.4 us
    pallas_call x2, Pallas kernels, attend(): pl.pallas_call(functools.partial(attend_kernel, table, order, heads, part...  14.1 us
    pallas_call x5, Pallas kernels, expand(): pl.pallas_call(functools.partial(expand_kernel, pieces, len(theirs), firs...  12.1 us
    ppermute x20, waiting for transfers between devices, send_prev(): return lax.ppermute(x, 'blk', backward)  10.3 us
    ppermute x4, starting transfers between devices, send_piece(): pieces[k] = lax.ppermute(packed[k], ('blk', 'head'), pairs)  6.28 us
    pallas_call x4, Pallas kernels, contract(): pl.pallas_call(functools.partial(contract_kernel, part * columns), grid=(...  5.01 us
  transfers between devices with their start and end apart: 56, of which 31 were waited for; matrix products, arithmetic and copies ran while one was open for 1% of the time, Pallas kernels for 19%

profile of v10, /device:TPU:0, one launch (start us, length us, event | category | flops | bytes accessed | tf_op | source)
XLA Modules:
  0.0 137.8 jit_solution(6463884054930869656)
XLA Ops:
  1.5 8.2 %attend.2 = (s32[60]{0:T(128)S(1)}, bf16[32,2048]{1,0:T(8,128)(2,1)S(1)}, bf16[32,2048]{1,0:T(8,128)(2,1)S(1)}, bf16[32,2048]{1,0:T(8,128)(2,1)S(1)}, bf16[128,5...) custom-call(s32[26]{0:T(128)S(1)} %concatenate.24.refs_0_, bf16[64,18432]{1,0:T(8,128)(2,1)} %refs_1_.3, ...), custom_call_target="tpu_custom_call" | custom-call | flops 713031680 | bytes 4456448 | tf_op jit(solution)/shard_map/attend/pallas_call | solution.py:341
  9.7 3.1 %collective-permute-start.11 = (bf16[32,2048]{1,0:T(8,128)(2,1)S(1)}, bf16[32,2048]{1,0:T(8,128)(2,1)S(1)}, u32[]{:S(2)}, u32[]{:S(2)}) collective-permute-start(bf16[32,2048]{1,0:T(8,128)(2,1)S(1)} %get-tuple-element.159), channel_id=1, source_target_pairs={{0,4},{4,8},{8,12},{12,14},{14,10},{10,6},{6,2},{2,0},{1,5},{5,9},... | collective-permute-start | bytes 393224 | tf_op jit(solution)/shard_map/ppermute | solution.py:792
  13.4 2.0 %collective-permute-start.1 = (bf16[64,896]{1,0:T(8,128)(2,1)S(1)}, bf16[64,896]{1,0:T(8,128)(2,1)S(1)}, u32[]{:S(2)}, u32[]{:S(2)}) collective-permute-start(bf16[64,896]{1,0:T(8,128)(2,1)S(1)} %get-tuple-element.138), channel_id=1, source_target_pairs={{0,4},{1,13},{2,6},{3,15},{4,8},{5,1},{6,10},{7,3},{8,12},{9,5},{1... | collective-permute-start | bytes 344072 | tf_op jit(solution)/shard_map/ppermute | solution.py:819
  15.4 3.6 %collective-permute-start.2 = (bf16[64,896]{1,0:T(8,128)(2,1)S(1)}, bf16[64,896]{1,0:T(8,128)(2,1)S(1)}, u32[]{:S(2)}, u32[]{:S(2)}) collective-permute-start(bf16[64,896]{1,0:T(8,128)(2,1)S(1)} %get-tuple-element.139), channel_id=1, source_target_pairs={{0,6},{1,15},{2,8},{3,1},{4,10},{5,3},{6,12},{7,5},{8,14},{9,7},{1... | collective-permute-start | bytes 344072 | tf_op jit(solution)/shard_map/ppermute | solution.py:819
  20.1 5.9 %attend.3 = (bf16[32,2048]{1,0:T(8,128)(2,1)S(1)}, bf16[32,2048]{1,0:T(8,128)(2,1)S(1)}, bf16[32,2048]{1,0:T(8,128)(2,1)S(1)}) custom-call(s32[60]{0:T(128)S(1)} %get-tuple-element.134.tab.refs_0_, bf16[64,18432]{1,0:T(8,128)(2,1)} %refs_1_.3, bf16[8,576,256]{2,1,0:T(8,128)(2,1)} %refs_2_.3, bf16[64,576]{1,0:T(8,128)(2,1)} %bitcast.35, ...), custom_call_target="tpu_custom_call" | custom-call | flops 713031680 | bytes 4456448 | tf_op jit(solution)/shard_map/attend/pallas_call | solution.py:341
  27.3 1.6 %collective-permute-start.3 = (bf16[32,2048]{1,0:T(8,128)(2,1)S(1)}, bf16[32,2048]{1,0:T(8,128)(2,1)S(1)}, u32[]{:S(2)}, u32[]{:S(2)}) collective-permute-start(bf16[32,2048]{1,0:T(8,128)(2,1)S(1)} %get-tuple-element.147), channel_id=1, source_target_pairs={{0,4},{4,8},{8,12},{12,14},{14,10},{10,6},{6,2},{2,0},{1,5},{5,9},... | collective-permute-start | bytes 393224 | tf_op jit(solution)/shard_map/ppermute | solution.py:792
  28.9 1.6 %collective-permute-start.13 = (bf16[32,2048]{1,0:T(8,128)(2,1)S(1)}, bf16[32,2048]{1,0:T(8,128)(2,1)S(1)}, u32[]{:S(2)}, u32[]{:S(2)}) collective-permute-start(bf16[32,2048]{1,0:T(8,128)(2,1)S(1)} %broadcast_select_fusion.5), channel_id=1, source_target_pairs={{0,4},{4,8},{8,12},{12,14},{14,10},{10,6},{6,2},{2,0},{1,5},{5,9},... | collective-permute-start | bytes 393224 | tf_op jit(solution)/shard_map/ppermute | solution.py:792
  31.0 2.3 %collective-permute-done.3.refs_1_ = bf16[32,2048]{1,0:T(8,128)(2,1)S(1)} collective-permute-done((bf16[32,2048]{1,0:T(8,128)(2,1)S(1)}, bf16[32,2048]{1,0:T(8,128)(2,1)S(1)}, u32[]{:S(2)}, u32[]{:S(2)}) %collective-permute-start.3) | collective-permute-done | bytes 131104 | tf_op jit(solution)/shard_map/ppermute | solution.py:792
  33.5 2.6 %collective-permute-start.6 = (bf16[32,2048]{1,0:T(8,128)(2,1)S(1)}, bf16[32,2048]{1,0:T(8,128)(2,1)S(1)}, u32[]{:S(2)}, u32[]{:S(2)}) collective-permute-start(bf16[32,2048]{1,0:T(8,128)(2,1)S(1)} %broadcast_select_fusion.10), channel_id=1, source_target_pairs={{4,0},{8,4},{12,8},{14,12},{10,14},{6,10},{2,6},{0,2},{5,1},{9,5},... | collective-permute-start | bytes 393224 | tf_op jit(solution)/shard_map/ppermute | solution.py:795
  36.7 0.8 collective-permute-start.20
  37.5 1.8 %collective-permute-start.17 = (bf16[32,2048]{1,0:T(8,128)(2,1)S(1)}, bf16[32,2048]{1,0:T(8,128)(2,1)S(1)}, u32[]{:S(2)}, u32[]{:S(2)}) collective-permute-start(bf16[32,2048]{1,0:T(8,128)(2,1)S(1)} %broadcast_select_fusion.2), channel_id=1, source_target_pairs={{4,0},{8,4},{12,8},{14,12},{10,14},{6,10},{2,6},{0,2},{5,1},{9,5},... | collective-permute-start | bytes 393224 | tf_op jit(solution)/shard_map/ppermute | solution.py:795
  39.3 0.8 collective-permute-start.16
  40.2 1.2 collective-permute-done.5.refs_2_
  41.4 1.1 collective-permute-start.8
  42.5 0.9 collective-permute-start.7
  44.0 0.9 collective-permute-done.16.refs_3_
  44.9 0.9 collective-permute-start.18
  45.8 1.2 collective-permute-start.19
  47.0 1.6 %collective-permute-done.7.refs_3_ = bf16[32,2048]{1,0:T(8,128)(2,1)S(1)} collective-permute-done((bf16[32,2048]{1,0:T(8,128)(2,1)S(1)}, bf16[32,2048]{1,0:T(8,128)(2,1)S(1)}, u32[]{:S(2)}, u32[]{:S(2)}) %collective-permute-start.7) | collective-permute-done | bytes 131104 | tf_op jit(solution)/shard_map/ppermute | solution.py:792
  48.7 1.5 %collective-permute-start.10 = (bf16[32,2048]{1,0:T(8,128)(2,1)S(1)}, bf16[32,2048]{1,0:T(8,128)(2,1)S(1)}, u32[]{:S(2)}, u32[]{:S(2)}) collective-permute-start(bf16[32,2048]{1,0:T(8,128)(2,1)S(1)} %broadcast_select_fusion.6), channel_id=1, source_target_pairs={{4,0},{8,4},{12,8},{14,12},{10,14},{6,10},{2,6},{0,2},{5,1},{9,5},... | collective-permute-start | bytes 393224 | tf_op jit(solution)/shard_map/ppermute | solution.py:795
  51.3 0.8 collective-permute-done.19.refs_8_
  52.2 1.9 %project.2.refs_10_ = f32[288,896]{1,0:T(8,128)S(1)} custom-call(s32[60]{0:T(128)S(1)} %get-tuple-element.134.tab.refs_0_, bf16[32,2048]{1,0:T(8,128)(2,1)S(1)} %get-tuple-element.177.refs_0_, bf16[32,2048]{1,0:T(8,128)(2,1)S(1)} %collective-permute-done.11.refs_1_, bf16[32,2048]{1,0:T(8,128)(2,1)S(1)} %collective-permute-done.13.refs_2_, ...), custom_call_target="tpu_custom_call" | custom-call | flops 1056964608 | bytes 4849664 | tf_op jit(solution)/shard_map/project/pallas_call | solution.py:486
  54.1 1.0 collective-permute-done.9.refs_4_
  55.2 2.0 %project.3 = (f32[144,896]{1,0:T(8,128)S(1)}, bf16[144,896]{1,0:T(8,128)(2,1)S(1)}) custom-call(s32[60]{0:T(128)S(1)} %get-tuple-element.134.tab.refs_0_, bf16[32,2048]{1,0:T(8,128)(2,1)S(1)} %get-tuple-element.150.refs_0_, bf16[32,2048]{1,0:T(8,128)(2,1)S(1)} %collective-permute-done.3.refs_1_, bf16[32,2048]{1,0:T(8,128)(2,1)S(1)} %collective-permute-done.5.refs_2_, ...), custom_call_target="tpu_custom_call" | custom-call | flops 1056964608 | bytes 4849664 | tf_op jit(solution)/shard_map/project/pallas_call | solution.py:496
  57.9 0.9 collective-permute-done.21
  59.6 1.5 %collective-permute-start.23 = (bf16[144,896]{1,0:T(8,128)(2,1)S(1)}, bf16[144,896]{1,0:T(8,128)(2,1)S(1)}, u32[]{:S(2)}, u32[]{:S(2)}) collective-permute-start(bf16[144,896]{1,0:T(8,128)(2,1)S(1)} %add_convert_fusion.refs_0_.refs_1_), channel_id=1, source_target_pairs={{4,0},{8,4},{12,8},{14,12},{10,14},{6,10},{2,6},{0,2},{5,1},{9,5},... | collective-permute-start | bytes 774152 | tf_op jit(solution)/shard_map/ppermute | solution.py:795
  61.2 1.7 %expand.5 = (f32[288,576]{1,0:T(8,128)S(1)}, f32[288,576]{1,0:T(8,128)S(1)}, f32[288,1]{1,0:T(8,128)S(1)}) custom-call(s32[60]{0:T(128)S(1)} %get-tuple-element.134.tab.refs_0_, bf16[144,896]{1,0:T(8,128)(2,1)S(1)} %add_convert_fusion.refs_0_.refs_1_, bf16[144,896]{1,0:T(8,128)(2,1)S(1)} %collective-permute-done.24.refs_1_, f32[8,1,896]{2,1,0:T(1,128)S(1)} %bitcast.29, ...), custom_call_target="tpu_custom_call" | custom-call | flops 1 | bytes 1 | tf_op jit(solution)/shard_map/expand/pallas_call | solution.py:648
  62.8 4.7 %collective-permute-done.22.refs_0_.refs_2_.refs_3_ = bf16[144,896]{1,0:T(8,128)(2,1)S(1)} collective-permute-done((bf16[144,896]{1,0:T(8,128)(2,1)S(1)}, bf16[144,896]{1,0:T(8,128)(2,1)S(1)}, u32[]{:S(2)}, u32[]{:S(2)}) %collective-permute-start.22) | collective-permute-done | bytes 258080 | tf_op jit(solution)/shard_map/ppermute | solution.py:792
  68.0 1.7 %collective-permute-start.25 = (bf16[144,896]{1,0:T(8,128)(2,1)S(1)}, bf16[144,896]{1,0:T(8,128)(2,1)S(1)}, u32[]{:S(2)}, u32[]{:S(2)}) collective-permute-start(bf16[144,896]{1,0:T(8,128)(2,1)S(1)} %collective-permute-done.22.refs_0_.refs_2_.refs_3_), channel_id=1, source_target_pairs={{0,4},{4,8},{8,12},{12,14},{14,10},{10,6},{6,2},{2,0},{1,5},{5,9},... | collective-permute-start | bytes 774152 | tf_op jit(solution)/shard_map/ppermute | solution.py:792
  70.1 2.9 %expand.6 = (f32[288,576]{1,0:T(8,128)S(1)}, f32[288,576]{1,0:T(8,128)S(1)}, f32[288,1]{1,0:T(8,128)S(1)}) custom-call(s32[60]{0:T(128)S(1)} %get-tuple-element.134.tab.refs_0_, bf16[144,896]{1,0:T(8,128)(2,1)S(1)} %collective-permute-done.22.refs_0_.refs_2_.refs_3_, bf16[144,896]{1,0:T(8,128)(2,1)S(1)} %collective-permute-done.23.refs_1_.refs_4_.refs_5_, ...), custom_call_target="tpu_custom_call" | custom-call | flops 1 | bytes 1 | tf_op jit(solution)/shard_map/expand/pallas_call | solution.py:648
  72.9 3.7 %collective-permute-done.25.refs_0_.refs_6_.refs_7_ = bf16[144,896]{1,0:T(8,128)(2,1)S(1)} collective-permute-done((bf16[144,896]{1,0:T(8,128)(2,1)S(1)}, bf16[144,896]{1,0:T(8,128)(2,1)S(1)}, u32[]{:S(2)}, u32[]{:S(2)}) %collective-permute-start.25) | collective-permute-done | bytes 258080 | tf_op jit(solution)/shard_map/ppermute | solution.py:792
  76.6 1.4 %collective-permute-done.26.refs_1_.refs_8_.refs_9_ = bf16[144,896]{1,0:T(8,128)(2,1)S(1)} collective-permute-done((bf16[144,896]{1,0:T(8,128)(2,1)S(1)}, bf16[144,896]{1,0:T(8,128)(2,1)S(1)}, u32[]{:S(2)}, u32[]{:S(2)}) %collective-permute-start.26) | collective-permute-done | bytes 258080 | tf_op jit(solution)/shard_map/ppermute | solution.py:795
  78.1 0.9 collective-permute-start.28
  79.0 1.1 collective-permute-start.29
  80.2 2.9 %expand.7 = (f32[288,576]{1,0:T(8,128)S(1)}, f32[288,576]{1,0:T(8,128)S(1)}, f32[288,1]{1,0:T(8,128)S(1)}) custom-call(s32[60]{0:T(128)S(1)} %get-tuple-element.134.tab.refs_0_, bf16[144,896]{1,0:T(8,128)(2,1)S(1)} %collective-permute-done.25.refs_0_.refs_6_.refs_7_, bf16[144,896]{1,0:T(8,128)(2,1)S(1)} %collective-permute-done.26.refs_1_.refs_8_.refs_9_, ...), custom_call_target="tpu_custom_call" | custom-call | flops 1 | bytes 1 | tf_op jit(solution)/shard_map/expand/pallas_call | solution.py:648
  83.1 3.7 %collective-permute-done.28.refs_0_.refs_10_.refs_11_ = bf16[144,896]{1,0:T(8,128)(2,1)S(1)} collective-permute-done((bf16[144,896]{1,0:T(8,128)(2,1)S(1)}, bf16[144,896]{1,0:T(8,128)(2,1)S(1)}, u32[]{:S(2)}, u32[]{:S(2)}) %collective-permute-start.28) | collective-permute-done | bytes 258080 | tf_op jit(solution)/shard_map/ppermute | solution.py:792
  87.5 1.2 collective-permute-start.31
  88.7 0.9 collective-permute-start.32
  89.6 2.9 %expand.8 = (f32[288,576]{1,0:T(8,128)S(1)}, f32[288,576]{1,0:T(8,128)S(1)}, f32[288,1]{1,0:T(8,128)S(1)}) custom-call(s32[60]{0:T(128)S(1)} %get-tuple-element.134.tab.refs_0_, bf16[144,896]{1,0:T(8,128)(2,1)S(1)} %collective-permute-done.28.refs_0_.refs_10_.refs_11_, bf16[144,896]{1,0:T(8,128)(2,1)S(1)} %collective-permute-done.29.refs_1_.refs_12_.refs_13_, ...), custom_call_target="tpu_custom_call" | custom-call | flops 1 | bytes 1 | tf_op jit(solution)/shard_map/expand/pallas_call | solution.py:648
  92.5 1.5 %collective-permute-done.32.refs_1_ = bf16[64,896]{1,0:T(8,128)(2,1)S(1)} collective-permute-done((bf16[64,896]{1,0:T(8,128)(2,1)S(1)}, bf16[64,896]{1,0:T(8,128)(2,1)S(1)}, u32[]{:S(2)}, u32[]{:S(2)}) %collective-permute-start.32) | collective-permute-done | bytes 114720 | tf_op jit(solution)/shard_map/ppermute | solution.py:795
  94.6 1.0 collective-permute-done.35.refs_3_
  95.6 1.8 %expand.9.hidden = bf16[288,576]{1,0:T(8,128)(2,1)S(1)} custom-call(s32[60]{0:T(128)S(1)} %get-tuple-element.134.tab.refs_0_, bf16[80,896]{1,0:T(8,128)(2,1)S(1)} %collective-permute-done.31.refs_0_, bf16[64,896]{1,0:T(8,128)(2,1)S(1)} %collective-permute-done.32.refs_1_, bf16[80,896]{1,0:T(8,128)(2,1)S(1)} %collective-permute-done.34.refs_2_, ...), custom_call_target="tpu_custom_call" | custom-call | flops 1 | bytes 1 | tf_op jit(solution)/shard_map/expand/pallas_call | solution.py:648
  97.5 1.3 contract.7
  99.1 1.2 contract.5
  100.6 1.2 contract.6.mine
  102.7 0.9 collective-permute-start.48
  104.3 1.3 contract.4.mine
  105.6 1.4 %collective-permute-start.47 = (bf16[16,3584]{1,0:T(8,128)(2,1)S(1)}, bf16[16,3584]{1,0:T(8,128)(2,1)S(1)}, u32[]{:S(2)}, u32[]{:S(2)}) collective-permute-start(bf16[16,3584]{1,0:T(8,128)(2,1)S(1)} %convert_element_type.161), channel_id=1, source_target_pairs={{0,4},{4,8},{8,12},{12,14},{14,10},{10,6},{6,2},{2,0},{1,5},{5,9},... | collective-permute-start | bytes 344072 | tf_op jit(solution)/shard_map/ppermute | solution.py:792
  107.9 0.9 collective-permute-start.38
  108.8 1.2 collective-permute-start.37
  110.0 1.0 collective-permute-done.47
  111.0 1.2 collective-permute-start.50
  112.2 0.9 collective-permute-start.49
  113.6 1.8 %collective-permute-start.40 = (bf16[16,3584]{1,0:T(8,128)(2,1)S(1)}, bf16[16,3584]{1,0:T(8,128)(2,1)S(1)}, u32[]{:S(2)}, u32[]{:S(2)}) collective-permute-start(bf16[16,3584]{1,0:T(8,128)(2,1)S(1)} %add_convert_fusion.11), channel_id=1, source_target_pairs={{4,0},{8,4},{12,8},{14,12},{10,14},{6,10},{2,6},{0,2},{5,1},{9,5},... | collective-permute-start | bytes 344072 | tf_op jit(solution)/shard_map/ppermute | solution.py:795
  115.7 1.1 collective-permute-done.50
  116.8 1.4 %collective-permute-done.49 = bf16[16,3584]{1,0:T(8,128)(2,1)S(1)} collective-permute-done((bf16[16,3584]{1,0:T(8,128)(2,1)S(1)}, bf16[16,3584]{1,0:T(8,128)(2,1)S(1)}, u32[]{:S(2)}, u32[]{:S(2)}) %collective-permute-start.49) | collective-permute-done | bytes 114720 | tf_op jit(solution)/shard_map/ppermute | solution.py:792
  118.9 1.5 %collective-permute-start.51 = (bf16[16,3584]{1,0:T(8,128)(2,1)S(1)}, bf16[16,3584]{1,0:T(8,128)(2,1)S(1)}, u32[]{:S(2)}, u32[]{:S(2)}) collective-permute-start(bf16[16,3584]{1,0:T(8,128)(2,1)S(1)} %add_convert_fusion.4), channel_id=1, source_target_pairs={{0,4},{4,8},{8,12},{12,14},{14,10},{10,6},{6,2},{2,0},{1,5},{5,9},... | collective-permute-start | bytes 344072 | tf_op jit(solution)/shard_map/ppermute | solution.py:792
  121.4 1.7 %collective-permute-start.41 = (bf16[16,3584]{1,0:T(8,128)(2,1)S(1)}, bf16[16,3584]{1,0:T(8,128)(2,1)S(1)}, u32[]{:S(2)}, u32[]{:S(2)}) collective-permute-start(bf16[16,3584]{1,0:T(8,128)(2,1)S(1)} %add_convert_fusion.10), channel_id=1, source_target_pairs={{0,4},{4,8},{8,12},{12,14},{14,10},{10,6},{6,2},{2,0},{1,5},{5,9},... | collective-permute-start | bytes 344072 | tf_op jit(solution)/shard_map/ppermute | solution.py:792
  124.2 2.1 %collective-permute-start.53 = (bf16[16,3584]{1,0:T(8,128)(2,1)S(1)}, bf16[16,3584]{1,0:T(8,128)(2,1)S(1)}, u32[]{:S(2)}, u32[]{:S(2)}) collective-permute-start(bf16[16,3584]{1,0:T(8,128)(2,1)S(1)} %add_convert_fusion.2), channel_id=1, source_target_pairs={{0,4},{4,8},{8,12},{12,14},{14,10},{10,6},{6,2},{2,0},{1,5},{5,9},... | collective-permute-start | bytes 344072 | tf_op jit(solution)/shard_map/ppermute | solution.py:792
  126.9 2.0 %collective-permute-start.43 = (bf16[16,3584]{1,0:T(8,128)(2,1)S(1)}, bf16[16,3584]{1,0:T(8,128)(2,1)S(1)}, u32[]{:S(2)}, u32[]{:S(2)}) collective-permute-start(bf16[16,3584]{1,0:T(8,128)(2,1)S(1)} %add_convert_fusion.8), channel_id=1, source_target_pairs={{0,4},{4,8},{8,12},{12,14},{14,10},{10,6},{6,2},{2,0},{1,5},{5,9},... | collective-permute-start | bytes 344072 | tf_op jit(solution)/shard_map/ppermute | solution.py:792
  129.7 1.4 %collective-permute-done.54 = bf16[16,3584]{1,0:T(8,128)(2,1)S(1)} collective-permute-done((bf16[16,3584]{1,0:T(8,128)(2,1)S(1)}, bf16[16,3584]{1,0:T(8,128)(2,1)S(1)}, u32[]{:S(2)}, u32[]{:S(2)}) %collective-permute-start.54) | collective-permute-done | bytes 114720 | tf_op jit(solution)/shard_map/ppermute | solution.py:795
  131.7 1.9 %collective-permute-done.44 = bf16[16,3584]{1,0:T(8,128)(2,1)S(1)} collective-permute-done((bf16[16,3584]{1,0:T(8,128)(2,1)S(1)}, bf16[16,3584]{1,0:T(8,128)(2,1)S(1)}, u32[]{:S(2)}, u32[]{:S(2)}) %collective-permute-start.44) | collective-permute-done | bytes 114720 | tf_op jit(solution)/shard_map/ppermute | solution.py:795
  135.9 0.9 collective-permute-done.55
  136.9 0.9 maximum_select_fusion
  (133 shorter events, 19.5 us)
Async XLA Ops:
  0.0 12.8 %copy-start = (bf16[64,7168]{1,0:T(8,128)(2,1)S(1)}, bf16[64,7168]{1,0:T(8,128)(2,1)}, u32[]{:S(2)}) copy-start(bf16[64,7168]{1,0:T(8,128)(2,1)} %res.1) | copy-start | bytes 2752516
  9.7 19.2 %collective-permute-start.11 = (bf16[32,2048]{1,0:T(8,128)(2,1)S(1)}, bf16[32,2048]{1,0:T(8,128)(2,1)S(1)}, u32[]{:S(2)}, u32[]{:S(2)}) collective-permute-start(bf16[32,2048]{1,0:T(8,128)(2,1)S(1)} %get-tuple-element.159), channel_id=1, source_target_pairs={{0,4},{4,8},{8,12},{12,14},{14,10},{10,6},{6,2},{2,0},{1,5},{5,9},... | collective-permute-start | bytes 393224 | tf_op jit(solution)/shard_map/ppermute | solution.py:792
  13.3 38.8 %slice-start.6 = ((s8[7340032]{0:T(1024)(128)(4,1)}), s8[4194304]{0:T(1024)(128)(4,1)S(1)}, s32[]{:S(2)}) async-start(s8[7340032]{0:T(1024)(128)(4,1)} %bitcast.27), calls=%async_computation.6 | async-start | bytes 8388608
  13.4 12.7 %collective-permute-start = (bf16[64,896]{1,0:T(8,128)(2,1)S(1)}, bf16[64,896]{1,0:T(8,128)(2,1)S(1)}, u32[]{:S(2)}, u32[]{:S(2)}) collective-permute-start(bf16[64,896]{1,0:T(8,128)(2,1)S(1)} %get-tuple-element.137), channel_id=1, source_target_pairs={{0,2},{1,11},{2,4},{3,13},{4,6},{5,15},{6,8},{7,1},{8,10},{9,3},{1... | collective-permute-start | bytes 344072 | tf_op jit(solution)/shard_map/ppermute | solution.py:819
  13.4 12.6 %collective-permute-start.1 = (bf16[64,896]{1,0:T(8,128)(2,1)S(1)}, bf16[64,896]{1,0:T(8,128)(2,1)S(1)}, u32[]{:S(2)}, u32[]{:S(2)}) collective-permute-start(bf16[64,896]{1,0:T(8,128)(2,1)S(1)} %get-tuple-element.138), channel_id=1, source_target_pairs={{0,4},{1,13},{2,6},{3,15},{4,8},{5,1},{6,10},{7,3},{8,12},{9,5},{1... | collective-permute-start | bytes 344072 | tf_op jit(solution)/shard_map/ppermute | solution.py:819
  15.4 10.7 %collective-permute-start.2 = (bf16[64,896]{1,0:T(8,128)(2,1)S(1)}, bf16[64,896]{1,0:T(8,128)(2,1)S(1)}, u32[]{:S(2)}, u32[]{:S(2)}) collective-permute-start(bf16[64,896]{1,0:T(8,128)(2,1)S(1)} %get-tuple-element.139), channel_id=1, source_target_pairs={{0,6},{1,15},{2,8},{3,1},{4,10},{5,3},{6,12},{7,5},{8,14},{9,7},{1... | collective-permute-start | bytes 344072 | tf_op jit(solution)/shard_map/ppermute | solution.py:819
  19.0 9.9 %collective-permute-start.12 = (bf16[32,2048]{1,0:T(8,128)(2,1)S(1)}, bf16[32,2048]{1,0:T(8,128)(2,1)S(1)}, u32[]{:S(2)}, u32[]{:S(2)}) collective-permute-start(bf16[32,2048]{1,0:T(8,128)(2,1)S(1)} %get-tuple-element.177.refs_0_), channel_id=1, source_target_pairs={{4,0},{8,4},{12,8},{14,12},{10,14},{6,10},{2,6},{0,2},{5,1},{9,5},... | collective-permute-start | bytes 393224 | tf_op jit(solution)/shard_map/ppermute | solution.py:795
  20.1 32.1 %slice-start.7 = ((s8[7340032]{0:T(1024)(128)(4,1)}), s8[3145728]{0:T(1024)(128)(4,1)S(1)}, s32[]{:S(2)}) async-start(s8[7340032]{0:T(1024)(128)(4,1)} %bitcast.27), calls=%async_computation.7 | async-start | bytes 6291456
  26.1 10.0 %collective-permute-start.14 = (bf16[64,896]{1,0:T(8,128)(2,1)S(1)}, bf16[64,896]{1,0:T(8,128)(2,1)S(1)}, u32[]{:S(2)}, u32[]{:S(2)}) collective-permute-start(bf16[64,896]{1,0:T(8,128)(2,1)S(1)} %get-tuple-element.163.own), channel_id=1, source_target_pairs={{1,9},{3,11},{5,13},{7,15},{9,1},{11,3},{13,5},{15,7},{17,25},{19,... | collective-permute-start | bytes 344072 | tf_op jit(solution)/shard_map/ppermute | solution.py:819
  26.8 6.7 %collective-permute-start.4 = (bf16[32,2048]{1,0:T(8,128)(2,1)S(1)}, bf16[32,2048]{1,0:T(8,128)(2,1)S(1)}, u32[]{:S(2)}, u32[]{:S(2)}) collective-permute-start(bf16[32,2048]{1,0:T(8,128)(2,1)S(1)} %get-tuple-element.150.refs_0_), channel_id=1, source_target_pairs={{4,0},{8,4},{12,8},{14,12},{10,14},{6,10},{2,6},{0,2},{5,1},{9,5},... | collective-permute-start | bytes 393224 | tf_op jit(solution)/shard_map/ppermute | solution.py:795
  27.3 6.0 %collective-permute-start.3 = (bf16[32,2048]{1,0:T(8,128)(2,1)S(1)}, bf16[32,2048]{1,0:T(8,128)(2,1)S(1)}, u32[]{:S(2)}, u32[]{:S(2)}) collective-permute-start(bf16[32,2048]{1,0:T(8,128)(2,1)S(1)} %get-tuple-element.147), channel_id=1, source_target_pairs={{0,4},{4,8},{8,12},{12,14},{14,10},{10,6},{6,2},{2,0},{1,5},{5,9},... | collective-permute-start | bytes 393224 | tf_op jit(solution)/shard_map/ppermute | solution.py:792
  28.9 7.2 %collective-permute-start.13 = (bf16[32,2048]{1,0:T(8,128)(2,1)S(1)}, bf16[32,2048]{1,0:T(8,128)(2,1)S(1)}, u32[]{:S(2)}, u32[]{:S(2)}) collective-permute-start(bf16[32,2048]{1,0:T(8,128)(2,1)S(1)} %broadcast_select_fusion.5), channel_id=1, source_target_pairs={{0,4},{4,8},{8,12},{12,14},{14,10},{10,6},{6,2},{2,0},{1,5},{5,9},... | collective-permute-start | bytes 393224 | tf_op jit(solution)/shard_map/ppermute | solution.py:792
  30.5 7.0 %collective-permute-start.15 = (bf16[32,2048]{1,0:T(8,128)(2,1)S(1)}, bf16[32,2048]{1,0:T(8,128)(2,1)S(1)}, u32[]{:S(2)}, u32[]{:S(2)}) collective-permute-start(bf16[32,2048]{1,0:T(8,128)(2,1)S(1)} %broadcast_select_fusion.4), channel_id=1, source_target_pairs={{4,0},{8,4},{12,8},{14,12},{10,14},{6,10},{2,6},{0,2},{5,1},{9,5},... | collective-permute-start | bytes 393224 | tf_op jit(solution)/shard_map/ppermute | solution.py:795
  33.5 6.6 %collective-permute-start.6 = (bf16[32,2048]{1,0:T(8,128)(2,1)S(1)}, bf16[32,2048]{1,0:T(8,128)(2,1)S(1)}, u32[]{:S(2)}, u32[]{:S(2)}) collective-permute-start(bf16[32,2048]{1,0:T(8,128)(2,1)S(1)} %broadcast_select_fusion.10), channel_id=1, source_target_pairs={{4,0},{8,4},{12,8},{14,12},{10,14},{6,10},{2,6},{0,2},{5,1},{9,5},... | collective-permute-start | bytes 393224 | tf_op jit(solution)/shard_map/ppermute | solution.py:795
  36.1 5.3 %collective-permute-start.5 = (bf16[32,2048]{1,0:T(8,128)(2,1)S(1)}, bf16[32,2048]{1,0:T(8,128)(2,1)S(1)}, u32[]{:S(2)}, u32[]{:S(2)}) collective-permute-start(bf16[32,2048]{1,0:T(8,128)(2,1)S(1)} %broadcast_select_fusion.11), channel_id=1, source_target_pairs={{0,4},{4,8},{8,12},{12,14},{14,10},{10,6},{6,2},{2,0},{1,5},{5,9},... | collective-permute-start | bytes 393224 | tf_op jit(solution)/shard_map/ppermute | solution.py:792
  36.7 14.1 %collective-permute-start.20 = (bf16[128,896]{1,0:T(8,128)(2,1)S(1)}, bf16[128,896]{1,0:T(8,128)(2,1)S(1)}, u32[]{:S(2)}, u32[]{:S(2)}) collective-permute-start(bf16[128,896]{1,0:T(8,128)(2,1)S(1)} %share.1), channel_id=1, source_target_pairs={{0,1},{1,0},{2,3},{3,2},{4,5},{5,4},{6,7},{7,6},{8,9},{9,8},{10,11... | collective-permute-start | bytes 688136 | tf_op jit(solution)/shard_map/ppermute | solution.py:798
  37.5 6.4 %collective-permute-start.17 = (bf16[32,2048]{1,0:T(8,128)(2,1)S(1)}, bf16[32,2048]{1,0:T(8,128)(2,1)S(1)}, u32[]{:S(2)}, u32[]{:S(2)}) collective-permute-start(bf16[32,2048]{1,0:T(8,128)(2,1)S(1)} %broadcast_select_fusion.2), channel_id=1, source_target_pairs={{4,0},{8,4},{12,8},{14,12},{10,14},{6,10},{2,6},{0,2},{5,1},{9,5},... | collective-permute-start | bytes 393224 | tf_op jit(solution)/shard_map/ppermute | solution.py:795
  39.3 5.6 %collective-permute-start.16 = (bf16[32,2048]{1,0:T(8,128)(2,1)S(1)}, bf16[32,2048]{1,0:T(8,128)(2,1)S(1)}, u32[]{:S(2)}, u32[]{:S(2)}) collective-permute-start(bf16[32,2048]{1,0:T(8,128)(2,1)S(1)} %broadcast_select_fusion.3), channel_id=1, source_target_pairs={{0,4},{4,8},{8,12},{12,14},{14,10},{10,6},{6,2},{2,0},{1,5},{5,9},... | collective-permute-start | bytes 393224 | tf_op jit(solution)/shard_map/ppermute | solution.py:792
  41.4 5.6 %collective-permute-start.8 = (bf16[32,2048]{1,0:T(8,128)(2,1)S(1)}, bf16[32,2048]{1,0:T(8,128)(2,1)S(1)}, u32[]{:S(2)}, u32[]{:S(2)}) collective-permute-start(bf16[32,2048]{1,0:T(8,128)(2,1)S(1)} %broadcast_select_fusion.8), channel_id=1, source_target_pairs={{4,0},{8,4},{12,8},{14,12},{10,14},{6,10},{2,6},{0,2},{5,1},{9,5},... | collective-permute-start | bytes 393224 | tf_op jit(solution)/shard_map/ppermute | solution.py:795
  42.5 6.1 %collective-permute-start.7 = (bf16[32,2048]{1,0:T(8,128)(2,1)S(1)}, bf16[32,2048]{1,0:T(8,128)(2,1)S(1)}, u32[]{:S(2)}, u32[]{:S(2)}) collective-permute-start(bf16[32,2048]{1,0:T(8,128)(2,1)S(1)} %broadcast_select_fusion.9), channel_id=1, source_target_pairs={{0,4},{4,8},{8,12},{12,14},{14,10},{10,6},{6,2},{2,0},{1,5},{5,9},... | collective-permute-start | bytes 393224 | tf_op jit(solution)/shard_map/ppermute | solution.py:792
  44.0 17.2 %slice-start.2 = ((s8[8257536]{0:T(1024)(128)(4,1)}), s8[4194304]{0:T(1024)(128)(4,1)S(1)}, s32[]{:S(2)}) async-start(s8[8257536]{0:T(1024)(128)(4,1)} %bitcast.18), calls=%async_computation.2 | async-start | bytes 8388608
  44.9 6.4 %collective-permute-start.18 = (bf16[32,2048]{1,0:T(8,128)(2,1)S(1)}, bf16[32,2048]{1,0:T(8,128)(2,1)S(1)}, u32[]{:S(2)}, u32[]{:S(2)}) collective-permute-start(bf16[32,2048]{1,0:T(8,128)(2,1)S(1)} %broadcast_select_fusion.1), channel_id=1, source_target_pairs={{0,4},{4,8},{8,12},{12,14},{14,10},{10,6},{6,2},{2,0},{1,5},{5,9},... | collective-permute-start | bytes 393224 | tf_op jit(solution)/shard_map/ppermute | solution.py:792
  45.8 6.3 %collective-permute-start.19 = (bf16[32,2048]{1,0:T(8,128)(2,1)S(1)}, bf16[32,2048]{1,0:T(8,128)(2,1)S(1)}, u32[]{:S(2)}, u32[]{:S(2)}) collective-permute-start(bf16[32,2048]{1,0:T(8,128)(2,1)S(1)} %broadcast_select_fusion), channel_id=1, source_target_pairs={{4,0},{8,4},{12,8},{14,12},{10,14},{6,10},{2,6},{0,2},{5,1},{9,5},... | collective-permute-start | bytes 393224 | tf_op jit(solution)/shard_map/ppermute | solution.py:795
  48.7 5.5 %collective-permute-start.10 = (bf16[32,2048]{1,0:T(8,128)(2,1)S(1)}, bf16[32,2048]{1,0:T(8,128)(2,1)S(1)}, u32[]{:S(2)}, u32[]{:S(2)}) collective-permute-start(bf16[32,2048]{1,0:T(8,128)(2,1)S(1)} %broadcast_select_fusion.6), channel_id=1, source_target_pairs={{4,0},{8,4},{12,8},{14,12},{10,14},{6,10},{2,6},{0,2},{5,1},{9,5},... | collective-permute-start | bytes 393224 | tf_op jit(solution)/shard_map/ppermute | solution.py:795
  50.2 5.0 %collective-permute-start.9 = (bf16[32,2048]{1,0:T(8,128)(2,1)S(1)}, bf16[32,2048]{1,0:T(8,128)(2,1)S(1)}, u32[]{:S(2)}, u32[]{:S(2)}) collective-permute-start(bf16[32,2048]{1,0:T(8,128)(2,1)S(1)} %broadcast_select_fusion.7), channel_id=1, source_target_pairs={{0,4},{4,8},{8,12},{12,14},{14,10},{10,6},{6,2},{2,0},{1,5},{5,9},... | collective-permute-start | bytes 393224 | tf_op jit(solution)/shard_map/ppermute | solution.py:792
  52.1 9.0 %slice-start = ((s8[8257536]{0:T(1024)(128)(4,1)}), s8[4194304]{0:T(1024)(128)(4,1)S(1)}, s32[]{:S(2)}) async-start(s8[8257536]{0:T(1024)(128)(4,1)} %bitcast.11), calls=%async_computation | async-start | bytes 8388608
  54.1 7.0 %slice-start.1 = ((s8[8257536]{0:T(1024)(128)(4,1)}), s8[4063232]{0:T(1024)(128)(4,1)S(1)}, s32[]{:S(2)}) async-start(s8[8257536]{0:T(1024)(128)(4,1)} %bitcast.11), calls=%async_computation.1 | async-start | bytes 8126464
  54.1 7.0 %slice-start.3 = ((s8[8257536]{0:T(1024)(128)(4,1)}), s8[4063232]{0:T(1024)(128)(4,1)S(1)}, s32[]{:S(2)}) async-start(s8[8257536]{0:T(1024)(128)(4,1)} %bitcast.18), calls=%async_computation.3 | async-start | bytes 8126464
  54.1 7.0 %copy-start.1 = (f32[7168]{0:T(1024)S(1)}, f32[7168]{0:T(1024)}, u32[]{:S(2)}) copy-start(f32[7168]{0:T(1024)} %param.24) | copy-start | bytes 86020
  57.2 1.6 %collective-permute-start.21 = (bf16[144,896]{1,0:T(8,128)(2,1)S(1)}, bf16[144,896]{1,0:T(8,128)(2,1)S(1)}, u32[]{:S(2)}, u32[]{:S(2)}) collective-permute-start(bf16[144,896]{1,0:T(8,128)(2,1)S(1)} %get-tuple-element.189), channel_id=1, source_target_pairs={{0,1},{1,0},{2,3},{3,2},{4,5},{5,4},{6,7},{7,6},{8,9},{9,8},{10,11... | collective-permute-start | bytes 774152 | tf_op jit(solution)/shard_map/ppermute | solution.py:798
  58.9 2.2 %collective-permute-start.24 = (bf16[144,896]{1,0:T(8,128)(2,1)S(1)}, bf16[144,896]{1,0:T(8,128)(2,1)S(1)}, u32[]{:S(2)}, u32[]{:S(2)}) collective-permute-start(bf16[144,896]{1,0:T(8,128)(2,1)S(1)} %add_convert_fusion.refs_0_.refs_1_), channel_id=1, source_target_pairs={{0,1},{1,0},{2,3},{3,2},{4,5},{5,4},{6,7},{7,6},{8,9},{9,8},{10,11... | collective-permute-start | bytes 774152 | tf_op jit(solution)/shard_map/ppermute | solution.py:798
  59.1 8.5 %collective-permute-start.22 = (bf16[144,896]{1,0:T(8,128)(2,1)S(1)}, bf16[144,896]{1,0:T(8,128)(2,1)S(1)}, u32[]{:S(2)}, u32[]{:S(2)}) collective-permute-start(bf16[144,896]{1,0:T(8,128)(2,1)S(1)} %add_convert_fusion.refs_0_.refs_1_), channel_id=1, source_target_pairs={{0,4},{4,8},{8,12},{12,14},{14,10},{10,6},{6,2},{2,0},{1,5},{5,9},... | collective-permute-start | bytes 774152 | tf_op jit(solution)/shard_map/ppermute | solution.py:792
  59.6 8.2 %collective-permute-start.23 = (bf16[144,896]{1,0:T(8,128)(2,1)S(1)}, bf16[144,896]{1,0:T(8,128)(2,1)S(1)}, u32[]{:S(2)}, u32[]{:S(2)}) collective-permute-start(bf16[144,896]{1,0:T(8,128)(2,1)S(1)} %add_convert_fusion.refs_0_.refs_1_), channel_id=1, source_target_pairs={{4,0},{8,4},{12,8},{14,12},{10,14},{6,10},{2,6},{0,2},{5,1},{9,5},... | collective-permute-start | bytes 774152 | tf_op jit(solution)/shard_map/ppermute | solution.py:795
  67.9 2.2 %collective-permute-start.27 = (bf16[288,896]{1,0:T(8,128)(2,1)S(1)}, bf16[288,896]{1,0:T(8,128)(2,1)S(1)}, u32[]{:S(2)}, u32[]{:S(2)}) collective-permute-start(bf16[288,896]{1,0:T(8,128)(2,1)S(1)} %pad_maximum_fusion), channel_id=1, source_target_pairs={{0,1},{1,0},{2,3},{3,2},{4,5},{5,4},{6,7},{7,6},{8,9},{9,8},{10,11... | collective-permute-start | bytes 1548296 | tf_op jit(solution)/shard_map/ppermute | solution.py:798
  68.0 8.6 %collective-permute-start.25 = (bf16[144,896]{1,0:T(8,128)(2,1)S(1)}, bf16[144,896]{1,0:T(8,128)(2,1)S(1)}, u32[]{:S(2)}, u32[]{:S(2)}) collective-permute-start(bf16[144,896]{1,0:T(8,128)(2,1)S(1)} %collective-permute-done.22.refs_0_.refs_2_.refs_3_), channel_id=1, source_target_pairs={{0,4},{4,8},{8,12},{12,14},{14,10},{10,6},{6,2},{2,0},{1,5},{5,9},... | collective-permute-start | bytes 774152 | tf_op jit(solution)/shard_map/ppermute | solution.py:792
  69.7 8.3 %collective-permute-start.26 = (bf16[144,896]{1,0:T(8,128)(2,1)S(1)}, bf16[144,896]{1,0:T(8,128)(2,1)S(1)}, u32[]{:S(2)}, u32[]{:S(2)}) collective-permute-start(bf16[144,896]{1,0:T(8,128)(2,1)S(1)} %collective-permute-done.23.refs_1_.refs_4_.refs_5_), channel_id=1, source_target_pairs={{4,0},{8,4},{12,8},{14,12},{10,14},{6,10},{2,6},{0,2},{5,1},{9,5},... | collective-permute-start | bytes 774152 | tf_op jit(solution)/shard_map/ppermute | solution.py:795
  78.0 2.2 %collective-permute-start.30 = (bf16[288,896]{1,0:T(8,128)(2,1)S(1)}, bf16[288,896]{1,0:T(8,128)(2,1)S(1)}, u32[]{:S(2)}, u32[]{:S(2)}) collective-permute-start(bf16[288,896]{1,0:T(8,128)(2,1)S(1)} %pad_maximum_fusion.1), channel_id=1, source_target_pairs={{0,1},{1,0},{2,3},{3,2},{4,5},{5,4},{6,7},{7,6},{8,9},{9,8},{10,11... | collective-permute-start | bytes 1548296 | tf_op jit(solution)/shard_map/ppermute | solution.py:798
  78.1 8.6 %collective-permute-start.28 = (bf16[144,896]{1,0:T(8,128)(2,1)S(1)}, bf16[144,896]{1,0:T(8,128)(2,1)S(1)}, u32[]{:S(2)}, u32[]{:S(2)}) collective-permute-start(bf16[144,896]{1,0:T(8,128)(2,1)S(1)} %collective-permute-done.25.refs_0_.refs_6_.refs_7_), channel_id=1, source_target_pairs={{0,4},{4,8},{8,12},{12,14},{14,10},{10,6},{6,2},{2,0},{1,5},{5,9},... | collective-permute-start | bytes 774152 | tf_op jit(solution)/shard_map/ppermute | solution.py:792
  79.0 8.3 %collective-permute-start.29 = (bf16[144,896]{1,0:T(8,128)(2,1)S(1)}, bf16[144,896]{1,0:T(8,128)(2,1)S(1)}, u32[]{:S(2)}, u32[]{:S(2)}) collective-permute-start(bf16[144,896]{1,0:T(8,128)(2,1)S(1)} %collective-permute-done.26.refs_1_.refs_8_.refs_9_), channel_id=1, source_target_pairs={{4,0},{8,4},{12,8},{14,12},{10,14},{6,10},{2,6},{0,2},{5,1},{9,5},... | collective-permute-start | bytes 774152 | tf_op jit(solution)/shard_map/ppermute | solution.py:795
  87.4 2.2 %collective-permute-start.33 = (bf16[288,896]{1,0:T(8,128)(2,1)S(1)}, bf16[288,896]{1,0:T(8,128)(2,1)S(1)}, u32[]{:S(2)}, u32[]{:S(2)}) collective-permute-start(bf16[288,896]{1,0:T(8,128)(2,1)S(1)} %pad_maximum_fusion.2), channel_id=1, source_target_pairs={{0,1},{1,0},{2,3},{3,2},{4,5},{5,4},{6,7},{7,6},{8,9},{9,8},{10,11... | collective-permute-start | bytes 1548296 | tf_op jit(solution)/shard_map/ppermute | solution.py:798
  87.5 6.6 %collective-permute-start.31 = (bf16[80,896]{1,0:T(8,128)(2,1)S(1)}, bf16[80,896]{1,0:T(8,128)(2,1)S(1)}, u32[]{:S(2)}, u32[]{:S(2)}) collective-permute-start(bf16[80,896]{1,0:T(8,128)(2,1)S(1)} %slice.18), channel_id=1, source_target_pairs={{0,4},{4,8},{8,12},{12,14},{14,10},{10,6},{6,2},{2,0},{1,5},{5,9},... | collective-permute-start | bytes 430088 | tf_op jit(solution)/shard_map/ppermute | solution.py:792
  88.7 5.3 %collective-permute-start.32 = (bf16[64,896]{1,0:T(8,128)(2,1)S(1)}, bf16[64,896]{1,0:T(8,128)(2,1)S(1)}, u32[]{:S(2)}, u32[]{:S(2)}) collective-permute-start(bf16[64,896]{1,0:T(8,128)(2,1)S(1)} %slice.19), channel_id=1, source_target_pairs={{4,0},{8,4},{12,8},{14,12},{10,14},{6,10},{2,6},{0,2},{5,1},{9,5},... | collective-permute-start | bytes 344072 | tf_op jit(solution)/shard_map/ppermute | solution.py:795
  94.1 1.6 %collective-permute-start.34 = (bf16[80,896]{1,0:T(8,128)(2,1)S(1)}, bf16[80,896]{1,0:T(8,128)(2,1)S(1)}, u32[]{:S(2)}, u32[]{:S(2)}) collective-permute-start(bf16[80,896]{1,0:T(8,128)(2,1)S(1)} %collective-permute-done.31.refs_0_), channel_id=1, source_target_pairs={{0,1},{1,0},{2,3},{3,2},{4,5},{5,4},{6,7},{7,6},{8,9},{9,8},{10,11... | collective-permute-start | bytes 430088 | tf_op jit(solution)/shard_map/ppermute | solution.py:798
  94.1 1.5 %collective-permute-start.35 = (bf16[64,896]{1,0:T(8,128)(2,1)S(1)}, bf16[64,896]{1,0:T(8,128)(2,1)S(1)}, u32[]{:S(2)}, u32[]{:S(2)}) collective-permute-start(bf16[64,896]{1,0:T(8,128)(2,1)S(1)} %collective-permute-done.32.refs_1_), channel_id=1, source_target_pairs={{0,1},{1,0},{2,3},{3,2},{4,5},{5,4},{6,7},{7,6},{8,9},{9,8},{10,11... | collective-permute-start | bytes 344072 | tf_op jit(solution)/shard_map/ppermute | solution.py:798
  98.7 3.1 %collective-permute-start.46 = (bf16[144,3584]{1,0:T(8,128)(2,1)S(1)}, bf16[144,3584]{1,0:T(8,128)(2,1)S(1)}, u32[]{:S(2)}, u32[]{:S(2)}) collective-permute-start(bf16[144,3584]{1,0:T(8,128)(2,1)S(1)} %contract.7), channel_id=1, source_target_pairs={{0,1},{1,0},{2,3},{3,2},{4,5},{5,4},{6,7},{7,6},{8,9},{9,8},{10,11... | collective-permute-start | bytes 3096584 | tf_op jit(solution)/shard_map/ppermute | solution.py:798
  100.4 6.7 %collective-permute-start.36 = (bf16[144,3584]{1,0:T(8,128)(2,1)S(1)}, bf16[144,3584]{1,0:T(8,128)(2,1)S(1)}, u32[]{:S(2)}, u32[]{:S(2)}) collective-permute-start(bf16[144,3584]{1,0:T(8,128)(2,1)S(1)} %contract.5), channel_id=1, source_target_pairs={{0,1},{1,0},{2,3},{3,2},{4,5},{5,4},{6,7},{7,6},{8,9},{9,8},{10,11... | collective-permute-start | bytes 3096584 | tf_op jit(solution)/shard_map/ppermute | solution.py:798
  102.7 7.2 %collective-permute-start.48 = (bf16[16,3584]{1,0:T(8,128)(2,1)S(1)}, bf16[16,3584]{1,0:T(8,128)(2,1)S(1)}, u32[]{:S(2)}, u32[]{:S(2)}) collective-permute-start(bf16[16,3584]{1,0:T(8,128)(2,1)S(1)} %convert_element_type.162), channel_id=1, source_target_pairs={{4,0},{8,4},{12,8},{14,12},{10,14},{6,10},{2,6},{0,2},{5,1},{9,5},... | collective-permute-start | bytes 344072 | tf_op jit(solution)/shard_map/ppermute | solution.py:795
  105.6 5.4 %collective-permute-start.47 = (bf16[16,3584]{1,0:T(8,128)(2,1)S(1)}, bf16[16,3584]{1,0:T(8,128)(2,1)S(1)}, u32[]{:S(2)}, u32[]{:S(2)}) collective-permute-start(bf16[16,3584]{1,0:T(8,128)(2,1)S(1)} %convert_element_type.161), channel_id=1, source_target_pairs={{0,4},{4,8},{8,12},{12,14},{14,10},{10,6},{6,2},{2,0},{1,5},{5,9},... | collective-permute-start | bytes 344072 | tf_op jit(solution)/shard_map/ppermute | solution.py:792
  107.9 5.2 %collective-permute-start.38 = (bf16[16,3584]{1,0:T(8,128)(2,1)S(1)}, bf16[16,3584]{1,0:T(8,128)(2,1)S(1)}, u32[]{:S(2)}, u32[]{:S(2)}) collective-permute-start(bf16[16,3584]{1,0:T(8,128)(2,1)S(1)} %convert_element_type.142), channel_id=1, source_target_pairs={{4,0},{8,4},{12,8},{14,12},{10,14},{6,10},{2,6},{0,2},{5,1},{9,5},... | collective-permute-start | bytes 344072 | tf_op jit(solution)/shard_map/ppermute | solution.py:795
  108.8 4.8 %collective-permute-start.37 = (bf16[16,3584]{1,0:T(8,128)(2,1)S(1)}, bf16[16,3584]{1,0:T(8,128)(2,1)S(1)}, u32[]{:S(2)}, u32[]{:S(2)}) collective-permute-start(bf16[16,3584]{1,0:T(8,128)(2,1)S(1)} %convert_element_type.141), channel_id=1, source_target_pairs={{0,4},{4,8},{8,12},{12,14},{14,10},{10,6},{6,2},{2,0},{1,5},{5,9},... | collective-permute-start | bytes 344072 | tf_op jit(solution)/shard_map/ppermute | solution.py:792
  111.0 5.7 %collective-permute-start.50 = (bf16[16,3584]{1,0:T(8,128)(2,1)S(1)}, bf16[16,3584]{1,0:T(8,128)(2,1)S(1)}, u32[]{:S(2)}, u32[]{:S(2)}) collective-permute-start(bf16[16,3584]{1,0:T(8,128)(2,1)S(1)} %add_convert_fusion.5), channel_id=1, source_target_pairs={{4,0},{8,4},{12,8},{14,12},{10,14},{6,10},{2,6},{0,2},{5,1},{9,5},... | collective-permute-start | bytes 344072 | tf_op jit(solution)/shard_map/ppermute | solution.py:795
  112.2 6.0 %collective-permute-start.49 = (bf16[16,3584]{1,0:T(8,128)(2,1)S(1)}, bf16[16,3584]{1,0:T(8,128)(2,1)S(1)}, u32[]{:S(2)}, u32[]{:S(2)}) collective-permute-start(bf16[16,3584]{1,0:T(8,128)(2,1)S(1)} %add_convert_fusion.6), channel_id=1, source_target_pairs={{0,4},{4,8},{8,12},{12,14},{14,10},{10,6},{6,2},{2,0},{1,5},{5,9},... | collective-permute-start | bytes 344072 | tf_op jit(solution)/shard_map/ppermute | solution.py:792
  113.6 6.7 %collective-permute-start.40 = (bf16[16,3584]{1,0:T(8,128)(2,1)S(1)}, bf16[16,3584]{1,0:T(8,128)(2,1)S(1)}, u32[]{:S(2)}, u32[]{:S(2)}) collective-permute-start(bf16[16,3584]{1,0:T(8,128)(2,1)S(1)} %add_convert_fusion.11), channel_id=1, source_target_pairs={{4,0},{8,4},{12,8},{14,12},{10,14},{6,10},{2,6},{0,2},{5,1},{9,5},... | collective-permute-start | bytes 344072 | tf_op jit(solution)/shard_map/ppermute | solution.py:795
  115.4 5.5 %collective-permute-start.39 = (bf16[16,3584]{1,0:T(8,128)(2,1)S(1)}, bf16[16,3584]{1,0:T(8,128)(2,1)S(1)}, u32[]{:S(2)}, u32[]{:S(2)}) collective-permute-start(bf16[16,3584]{1,0:T(8,128)(2,1)S(1)} %add_convert_fusion.12), channel_id=1, source_target_pairs={{0,4},{4,8},{8,12},{12,14},{14,10},{10,6},{6,2},{2,0},{1,5},{5,9},... | collective-permute-start | bytes 344072 | tf_op jit(solution)/shard_map/ppermute | solution.py:792
  118.2 5.3 %collective-permute-start.52 = (bf16[16,3584]{1,0:T(8,128)(2,1)S(1)}, bf16[16,3584]{1,0:T(8,128)(2,1)S(1)}, u32[]{:S(2)}, u32[]{:S(2)}) collective-permute-start(bf16[16,3584]{1,0:T(8,128)(2,1)S(1)} %add_convert_fusion.3), channel_id=1, source_target_pairs={{4,0},{8,4},{12,8},{14,12},{10,14},{6,10},{2,6},{0,2},{5,1},{9,5},... | collective-permute-start | bytes 344072 | tf_op jit(solution)/shard_map/ppermute | solution.py:795
  118.9 5.3 %collective-permute-start.51 = (bf16[16,3584]{1,0:T(8,128)(2,1)S(1)}, bf16[16,3584]{1,0:T(8,128)(2,1)S(1)}, u32[]{:S(2)}, u32[]{:S(2)}) collective-permute-start(bf16[16,3584]{1,0:T(8,128)(2,1)S(1)} %add_convert_fusion.4), channel_id=1, source_target_pairs={{0,4},{4,8},{8,12},{12,14},{14,10},{10,6},{6,2},{2,0},{1,5},{5,9},... | collective-permute-start | bytes 344072 | tf_op jit(solution)/shard_map/ppermute | solution.py:792
  121.0 5.5 %collective-permute-start.42 = (bf16[16,3584]{1,0:T(8,128)(2,1)S(1)}, bf16[16,3584]{1,0:T(8,128)(2,1)S(1)}, u32[]{:S(2)}, u32[]{:S(2)}) collective-permute-start(bf16[16,3584]{1,0:T(8,128)(2,1)S(1)} %add_convert_fusion.9), channel_id=1, source_target_pairs={{4,0},{8,4},{12,8},{14,12},{10,14},{6,10},{2,6},{0,2},{5,1},{9,5},... | collective-permute-start | bytes 344072 | tf_op jit(solution)/shard_map/ppermute | solution.py:795
  121.4 5.5 %collective-permute-start.41 = (bf16[16,3584]{1,0:T(8,128)(2,1)S(1)}, bf16[16,3584]{1,0:T(8,128)(2,1)S(1)}, u32[]{:S(2)}, u32[]{:S(2)}) collective-permute-start(bf16[16,3584]{1,0:T(8,128)(2,1)S(1)} %add_convert_fusion.10), channel_id=1, source_target_pairs={{0,4},{4,8},{8,12},{12,14},{14,10},{10,6},{6,2},{2,0},{1,5},{5,9},... | collective-permute-start | bytes 344072 | tf_op jit(solution)/shard_map/ppermute | solution.py:792
  124.2 5.5 %collective-permute-start.53 = (bf16[16,3584]{1,0:T(8,128)(2,1)S(1)}, bf16[16,3584]{1,0:T(8,128)(2,1)S(1)}, u32[]{:S(2)}, u32[]{:S(2)}) collective-permute-start(bf16[16,3584]{1,0:T(8,128)(2,1)S(1)} %add_convert_fusion.2), channel_id=1, source_target_pairs={{0,4},{4,8},{8,12},{12,14},{14,10},{10,6},{6,2},{2,0},{1,5},{5,9},... | collective-permute-start | bytes 344072 | tf_op jit(solution)/shard_map/ppermute | solution.py:792
  126.3 4.8 %collective-permute-start.54 = (bf16[16,3584]{1,0:T(8,128)(2,1)S(1)}, bf16[16,3584]{1,0:T(8,128)(2,1)S(1)}, u32[]{:S(2)}, u32[]{:S(2)}) collective-permute-start(bf16[16,3584]{1,0:T(8,128)(2,1)S(1)} %add_convert_fusion.1), channel_id=1, source_target_pairs={{4,0},{8,4},{12,8},{14,12},{10,14},{6,10},{2,6},{0,2},{5,1},{9,5},... | collective-permute-start | bytes 344072 | tf_op jit(solution)/shard_map/ppermute | solution.py:795
  126.9 4.8 %collective-permute-start.43 = (bf16[16,3584]{1,0:T(8,128)(2,1)S(1)}, bf16[16,3584]{1,0:T(8,128)(2,1)S(1)}, u32[]{:S(2)}, u32[]{:S(2)}) collective-permute-start(bf16[16,3584]{1,0:T(8,128)(2,1)S(1)} %add_convert_fusion.8), channel_id=1, source_target_pairs={{0,4},{4,8},{8,12},{12,14},{14,10},{10,6},{6,2},{2,0},{1,5},{5,9},... | collective-permute-start | bytes 344072 | tf_op jit(solution)/shard_map/ppermute | solution.py:792
  128.9 4.8 %collective-permute-start.44 = (bf16[16,3584]{1,0:T(8,128)(2,1)S(1)}, bf16[16,3584]{1,0:T(8,128)(2,1)S(1)}, u32[]{:S(2)}, u32[]{:S(2)}) collective-permute-start(bf16[16,3584]{1,0:T(8,128)(2,1)S(1)} %add_convert_fusion.7), channel_id=1, source_target_pairs={{4,0},{8,4},{12,8},{14,12},{10,14},{6,10},{2,6},{0,2},{5,1},{9,5},... | collective-permute-start | bytes 344072 | tf_op jit(solution)/shard_map/ppermute | solution.py:795
  133.9 2.0 %collective-permute-start.45 = (bf16[16,3584]{1,0:T(8,128)(2,1)S(1)}, bf16[16,3584]{1,0:T(8,128)(2,1)S(1)}, u32[]{:S(2)}, u32[]{:S(2)}) collective-permute-start(bf16[16,3584]{1,0:T(8,128)(2,1)S(1)} %get-tuple-element.259), channel_id=1, source_target_pairs={{0,1},{1,0},{2,3},{3,2},{4,5},{5,4},{6,7},{7,6},{8,9},{9,8},{10,11... | collective-permute-start | bytes 344072 | tf_op jit(solution)/shard_map/ppermute | solution.py:798
  135.3 1.5 %collective-permute-start.55 = (bf16[16,3584]{1,0:T(8,128)(2,1)S(1)}, bf16[16,3584]{1,0:T(8,128)(2,1)S(1)}, u32[]{:S(2)}, u32[]{:S(2)}) collective-permute-start(bf16[16,3584]{1,0:T(8,128)(2,1)S(1)} %get-tuple-element.265), channel_id=1, source_target_pairs={{0,1},{1,0},{2,3},{3,2},{4,5},{5,4},{6,7},{7,6},{8,9},{9,8},{10,11... | collective-permute-start | bytes 344072 | tf_op jit(solution)/shard_map/ppermute | solution.py:798
  (2 other events, 6.8 us)

commit v11 on v10

--- a/solution.py
+++ b/solution.py
@@ -269,8 +269,11 @@
         own_value = jnp.broadcast_to(own_value[None], (heads, dr, value)).reshape(n, value)
         dec = (acc + (e_own / total).astype(bf16).astype(f32) * own_value).astype(bf16)
         later[...] = dec[count * dr :]
-        for flag, at in zip(flags, (BUSY, CORE, LIVE)):
+        for flag, at in zip(flags, (BUSY, CORE)):
             flag[...] = jnp.full(flag.shape, tab[at].astype(f32))
+        block = rows // 2
+        slot_row = tab[CORE] * block + lax.broadcasted_iota(i32, (block, 1), 0)
+        flags[2][...] = jnp.where(slot_row < tab[LIVE], 1.0, 0.0)
         dec = dec[: count * dr]
     else:
         dec = decoded_here[...]
@@ -333,7 +336,7 @@
         scratch.append(pltpu.VMEM((heads * 8, wide), f32))
         out_shape = [jax.ShapeDtypeStruct((table.size,), i32)] + out_shape
         out_shape += [jax.ShapeDtypeStruct(((heads - count) * 8, value), bf16)]
-        out_shape += [jax.ShapeDtypeStruct((1, 1), f32)] * 3
+        out_shape += [jax.ShapeDtypeStruct((n, 1), f32) for n in (1, 1, rows // 2)]
         out_specs = [smem()] + out_specs + [whole()] * 4
     else:
         ins.append(whole())
@@ -800,7 +803,7 @@
     ids = jnp.stack([lax.axis_index("blk"), lax.axis_index("head")]).astype(i32)
     given = jnp.concatenate([ids, span_len, dec_count, span_start, cache_len[0]])
     caches = (queries, latent_cache, new_latent, value_weight)
-    tab, *lead, decoded, busy, which, live = attend(table, order, given, *caches, 0, 2, None)
+    tab, *lead, decoded, busy, which, alive = attend(table, order, given, *caches, 0, 2, None)
 
     def choose(special, usual, flag=busy):
         return jnp.where(jnp.broadcast_to(flag > 0, usual.shape), special, usual)
@@ -886,6 +889,7 @@
     parts = contract_parts
     theirs = [swap(contract(hidden, down_weight, part, parts, 1)) for part in range(parts)]
     mine = [contract(hidden, down_weight, part, parts, 0) for part in range(parts)]
+    mine = lax.optimization_barrier(mine)
     columns = width // parts
     lows, highs = [], []
     for part in range(parts):
@@ -902,6 +906,8 @@
             out_f, out_b = lax.optimization_barrier((out_f.astype(bf16), out_b.astype(bf16)))
             got_f.append(send_next(out_f))
             got_b.append(send_prev(out_b))
+        if part > 0:
+            lows, highs, got_f[-1] = lax.optimization_barrier((lows, highs, got_f[-1]))
         at = slice(part * columns, (part + 1) * columns)
         main = main + own[:half, at] + got_f[-1].astype(f32)
         main = (main + choose(got_b[-2], got_b[-1]).astype(f32)).astype(bf16)
@@ -912,8 +918,7 @@
         lows.append(choose(received, stays, which))
         highs.append(choose(stays, received, which))
     result = jnp.concatenate([jnp.concatenate(lows, 1), jnp.concatenate(highs, 1)], 0)
-    row = which * (2 * half) + lax.broadcasted_iota(i32, result.shape, 0).astype(f32)
-    return jnp.where(row < live, result, jnp.zeros_like(result))
+    return choose(result, jnp.zeros_like(result), alive)
 
 
 def solution(mesh):

time: 138 us -> 140 us (1.014)
  waiting for transfers between devices: 37.8 us -> 43.5 us
  starting transfers between devices: 53.8 us -> 51.6 us
    ppermute x20, waiting for transfers between devices: 10.3 us -> 21.5 us  [send_prev(): return lax.ppermute(x, 'blk', backward)]
    ppermute x20, waiting for transfers between devices: 24.6 us -> 18.9 us  [send_next(): return lax.ppermute(x, 'blk', forward)]
    ppermute x20, starting transfers between devices: 19.4 us -> 17.8 us  [send_prev(): return lax.ppermute(x, 'blk', backward)]
  transfers between devices with their start and end apart: 56 -> 56, of which waited for: 31 -> 32; matrix products, arithmetic and copies ran while one was open for 1% -> 1% of each run, Pallas kernels for 19% -> 19%
where the time goes in v11:
time: 140 us
  starting transfers between devices  51.6 us (37%)
  waiting for transfers between devices  43.5 us (31%)
  Pallas kernels  39.1 us (28%)
  between operations  2.54 us (2%)
  other arithmetic  2.33 us (2%)
    ppermute x20, starting transfers between devices, send_next(): return lax.ppermute(x, 'blk', forward)  25.6 us
    ppermute x20, waiting for transfers between devices, send_prev(): return lax.ppermute(x, 'blk', backward)  21.5 us
    ppermute x20, waiting for transfers between devices, send_next(): return lax.ppermute(x, 'blk', forward)  18.9 us
    ppermute x20, starting transfers between devices, send_prev(): return lax.ppermute(x, 'blk', backward)  17.8 us
    pallas_call x2, Pallas kernels, attend(): pl.pallas_call(functools.partial(attend_kernel, table, order, heads, part...  14.1 us
    pallas_call x5, Pallas kernels, expand(): pl.pallas_call(functools.partial(expand_kernel, pieces, len(theirs), firs...  12.1 us
    ppermute x4, starting transfers between devices, send_piece(): pieces[k] = lax.ppermute(packed[k], ('blk', 'head'), pairs)  6.28 us
    pallas_call x4, Pallas kernels, contract(): pl.pallas_call(functools.partial(contract_kernel, part * columns), grid=(...  5.01 us
  transfers between devices with their start and end apart: 56, of which 32 were waited for; matrix products, arithmetic and copies ran while one was open for 1% of the time, Pallas kernels for 19%

profile of v11, /device:TPU:0, one launch (start us, length us, event | category | flops | bytes accessed | tf_op | source)
XLA Modules:
  0.0 140.0 jit_solution(9042791886528452437)
XLA Ops:
  0.7 0.8 concatenate.24.refs_0_
  1.5 8.2 %attend.2 = (s32[60]{0:T(128)S(1)}, bf16[32,2048]{1,0:T(8,128)(2,1)S(1)}, bf16[32,2048]{1,0:T(8,128)(2,1)S(1)}, bf16[32,2048]{1,0:T(8,128)(2,1)S(1)}, bf16[128,5...) custom-call(s32[26]{0:T(128)S(1)} %concatenate.24.refs_0_, ...), custom_call_target="tpu_custom_call" | custom-call | flops 713031680 | bytes 4456448 | tf_op jit(solution)/shard_map/attend/pallas_call | solution.py:344
  9.7 3.1 %collective-permute-start.11 = (bf16[32,2048]{1,0:T(8,128)(2,1)S(1)}, bf16[32,2048]{1,0:T(8,128)(2,1)S(1)}, u32[]{:S(2)}, u32[]{:S(2)}) collective-permute-start(bf16[32,2048]{1,0:T(8,128)(2,1)S(1)} %get-tuple-element.164), channel_id=1, source_target_pairs={{0,4},{4,8},{8,12},{12,14},{14,10},{10,6},{6,2},{2,0},{1,5},{5,9},... | collective-permute-start | bytes 393224 | tf_op jit(solution)/shard_map/ppermute | solution.py:795
  13.4 2.0 %collective-permute-start.1 = (bf16[64,896]{1,0:T(8,128)(2,1)S(1)}, bf16[64,896]{1,0:T(8,128)(2,1)S(1)}, u32[]{:S(2)}, u32[]{:S(2)}) collective-permute-start(bf16[64,896]{1,0:T(8,128)(2,1)S(1)} %get-tuple-element.143), channel_id=1, source_target_pairs={{0,4},{1,13},{2,6},{3,15},{4,8},{5,1},{6,10},{7,3},{8,12},{9,5},{1... | collective-permute-start | bytes 344072 | tf_op jit(solution)/shard_map/ppermute | solution.py:822
  15.4 3.6 %collective-permute-start.2 = (bf16[64,896]{1,0:T(8,128)(2,1)S(1)}, bf16[64,896]{1,0:T(8,128)(2,1)S(1)}, u32[]{:S(2)}, u32[]{:S(2)}) collective-permute-start(bf16[64,896]{1,0:T(8,128)(2,1)S(1)} %get-tuple-element.144), channel_id=1, source_target_pairs={{0,6},{1,15},{2,8},{3,1},{4,10},{5,3},{6,12},{7,5},{8,14},{9,7},{1... | collective-permute-start | bytes 344072 | tf_op jit(solution)/shard_map/ppermute | solution.py:822
  20.1 5.9 %attend.3 = (bf16[32,2048]{1,0:T(8,128)(2,1)S(1)}, bf16[32,2048]{1,0:T(8,128)(2,1)S(1)}, bf16[32,2048]{1,0:T(8,128)(2,1)S(1)}) custom-call(s32[60]{0:T(128)S(1)} %get-tuple-element.139.tab.refs_0_, bf16[64,18432]{1,0:T(8,128)(2,1)} %refs_1_.3, bf16[8,576,256]{2,1,0:T(8,128)(2,1)} %refs_2_.3, bf16[64,576]{1,0:T(8,128)(2,1)} %bitcast.33, ...), custom_call_target="tpu_custom_call" | custom-call | flops 713031680 | bytes 4456448 | tf_op jit(solution)/shard_map/attend/pallas_call | solution.py:344
  26.8 1.6 %collective-permute-start.3 = (bf16[32,2048]{1,0:T(8,128)(2,1)S(1)}, bf16[32,2048]{1,0:T(8,128)(2,1)S(1)}, u32[]{:S(2)}, u32[]{:S(2)}) collective-permute-start(bf16[32,2048]{1,0:T(8,128)(2,1)S(1)} %get-tuple-element.152), channel_id=1, source_target_pairs={{0,4},{4,8},{8,12},{12,14},{14,10},{10,6},{6,2},{2,0},{1,5},{5,9},... | collective-permute-start | bytes 393224 | tf_op jit(solution)/shard_map/ppermute | solution.py:795
  28.9 1.6 %collective-permute-start.13 = (bf16[32,2048]{1,0:T(8,128)(2,1)S(1)}, bf16[32,2048]{1,0:T(8,128)(2,1)S(1)}, u32[]{:S(2)}, u32[]{:S(2)}) collective-permute-start(bf16[32,2048]{1,0:T(8,128)(2,1)S(1)} %broadcast_select_fusion.5), channel_id=1, source_target_pairs={{0,4},{4,8},{8,12},{12,14},{14,10},{10,6},{6,2},{2,0},{1,5},{5,9},... | collective-permute-start | bytes 393224 | tf_op jit(solution)/shard_map/ppermute | solution.py:795
  31.0 1.4 collective-permute-done.3.refs_1_
  32.4 2.2 %collective-permute-done.4.refs_5_ = bf16[32,2048]{1,0:T(8,128)(2,1)S(1)} collective-permute-done((bf16[32,2048]{1,0:T(8,128)(2,1)S(1)}, bf16[32,2048]{1,0:T(8,128)(2,1)S(1)}, u32[]{:S(2)}, u32[]{:S(2)}) %collective-permute-start.4) | collective-permute-done | bytes 131104 | tf_op jit(solution)/shard_map/ppermute | solution.py:798
  34.6 1.9 %collective-permute-start.5 = (bf16[32,2048]{1,0:T(8,128)(2,1)S(1)}, bf16[32,2048]{1,0:T(8,128)(2,1)S(1)}, u32[]{:S(2)}, u32[]{:S(2)}) collective-permute-start(bf16[32,2048]{1,0:T(8,128)(2,1)S(1)} %broadcast_select_fusion.11), channel_id=1, source_target_pairs={{0,4},{4,8},{8,12},{12,14},{14,10},{10,6},{6,2},{2,0},{1,5},{5,9},... | collective-permute-start | bytes 393224 | tf_op jit(solution)/shard_map/ppermute | solution.py:795
  36.8 0.7 collective-permute-done.15.refs_6_
  37.5 1.3 collective-permute-start.16
  38.7 0.8 collective-permute-start.17
  40.2 0.9 collective-permute-done.5.refs_2_
  41.1 1.8 %collective-permute-done.6.refs_6_ = bf16[32,2048]{1,0:T(8,128)(2,1)S(1)} collective-permute-done((bf16[32,2048]{1,0:T(8,128)(2,1)S(1)}, bf16[32,2048]{1,0:T(8,128)(2,1)S(1)}, u32[]{:S(2)}, u32[]{:S(2)}) %collective-permute-start.6) | collective-permute-done | bytes 131104 | tf_op jit(solution)/shard_map/ppermute | solution.py:798
  42.9 1.4 %collective-permute-start.7 = (bf16[32,2048]{1,0:T(8,128)(2,1)S(1)}, bf16[32,2048]{1,0:T(8,128)(2,1)S(1)}, u32[]{:S(2)}, u32[]{:S(2)}) collective-permute-start(bf16[32,2048]{1,0:T(8,128)(2,1)S(1)} %broadcast_select_fusion.9), channel_id=1, source_target_pairs={{0,4},{4,8},{8,12},{12,14},{14,10},{10,6},{6,2},{2,0},{1,5},{5,9},... | collective-permute-start | bytes 393224 | tf_op jit(solution)/shard_map/ppermute | solution.py:795
  45.3 1.8 %collective-permute-start.18 = (bf16[32,2048]{1,0:T(8,128)(2,1)S(1)}, bf16[32,2048]{1,0:T(8,128)(2,1)S(1)}, u32[]{:S(2)}, u32[]{:S(2)}) collective-permute-start(bf16[32,2048]{1,0:T(8,128)(2,1)S(1)} %broadcast_select_fusion.1), channel_id=1, source_target_pairs={{0,4},{4,8},{8,12},{12,14},{14,10},{10,6},{6,2},{2,0},{1,5},{5,9},... | collective-permute-start | bytes 393224 | tf_op jit(solution)/shard_map/ppermute | solution.py:795
  48.1 1.5 %collective-permute-done.8.refs_7_ = bf16[32,2048]{1,0:T(8,128)(2,1)S(1)} collective-permute-done((bf16[32,2048]{1,0:T(8,128)(2,1)S(1)}, bf16[32,2048]{1,0:T(8,128)(2,1)S(1)}, u32[]{:S(2)}, u32[]{:S(2)}) %collective-permute-start.8) | collective-permute-done | bytes 131104 | tf_op jit(solution)/shard_map/ppermute | solution.py:798
  49.6 2.1 %collective-permute-start.9 = (bf16[32,2048]{1,0:T(8,128)(2,1)S(1)}, bf16[32,2048]{1,0:T(8,128)(2,1)S(1)}, u32[]{:S(2)}, u32[]{:S(2)}) collective-permute-start(bf16[32,2048]{1,0:T(8,128)(2,1)S(1)} %broadcast_select_fusion.7), channel_id=1, source_target_pairs={{0,4},{4,8},{8,12},{12,14},{14,10},{10,6},{6,2},{2,0},{1,5},{5,9},... | collective-permute-start | bytes 393224 | tf_op jit(solution)/shard_map/ppermute | solution.py:795
  51.7 1.5 %collective-permute-done.19.refs_8_ = bf16[32,2048]{1,0:T(8,128)(2,1)S(1)} collective-permute-done((bf16[32,2048]{1,0:T(8,128)(2,1)S(1)}, bf16[32,2048]{1,0:T(8,128)(2,1)S(1)}, u32[]{:S(2)}, u32[]{:S(2)}) %collective-permute-start.19) | collective-permute-done | bytes 131104 | tf_op jit(solution)/shard_map/ppermute | solution.py:798
  53.2 1.9 %project.2.refs_10_ = f32[288,896]{1,0:T(8,128)S(1)} custom-call(s32[60]{0:T(128)S(1)} %get-tuple-element.139.tab.refs_0_, bf16[32,2048]{1,0:T(8,128)(2,1)S(1)} %get-tuple-element.182.refs_0_, bf16[32,2048]{1,0:T(8,128)(2,1)S(1)} %collective-permute-done.11.refs_1_, bf16[32,2048]{1,0:T(8,128)(2,1)S(1)} %collective-permute-done.13.refs_2_, ...), custom_call_target="tpu_custom_call" | custom-call | flops 1056964608 | bytes 4849664 | tf_op jit(solution)/shard_map/project/pallas_call | solution.py:489
  55.2 1.4 %collective-permute-done.10.refs_8_ = bf16[32,2048]{1,0:T(8,128)(2,1)S(1)} collective-permute-done((bf16[32,2048]{1,0:T(8,128)(2,1)S(1)}, bf16[32,2048]{1,0:T(8,128)(2,1)S(1)}, u32[]{:S(2)}, u32[]{:S(2)}) %collective-permute-start.10) | collective-permute-done | bytes 131104 | tf_op jit(solution)/shard_map/ppermute | solution.py:798
  56.7 2.0 %project.3 = (f32[144,896]{1,0:T(8,128)S(1)}, bf16[144,896]{1,0:T(8,128)(2,1)S(1)}) custom-call(s32[60]{0:T(128)S(1)} %get-tuple-element.139.tab.refs_0_, bf16[32,2048]{1,0:T(8,128)(2,1)S(1)} %get-tuple-element.155.refs_0_, bf16[32,2048]{1,0:T(8,128)(2,1)S(1)} %collective-permute-done.3.refs_1_, bf16[32,2048]{1,0:T(8,128)(2,1)S(1)} %collective-permute-done.5.refs_2_, ...), custom_call_target="tpu_custom_call" | custom-call | flops 1056964608 | bytes 4849664 | tf_op jit(solution)/shard_map/project/pallas_call | solution.py:499
  59.4 0.9 collective-permute-done.21
  60.7 2.0 %collective-permute-start.22 = (bf16[144,896]{1,0:T(8,128)(2,1)S(1)}, bf16[144,896]{1,0:T(8,128)(2,1)S(1)}, u32[]{:S(2)}, u32[]{:S(2)}) collective-permute-start(bf16[144,896]{1,0:T(8,128)(2,1)S(1)} %add_convert_fusion.refs_0_.refs_1_), channel_id=1, source_target_pairs={{0,4},{4,8},{8,12},{12,14},{14,10},{10,6},{6,2},{2,0},{1,5},{5,9},... | collective-permute-start | bytes 774152 | tf_op jit(solution)/shard_map/ppermute | solution.py:795
  62.8 1.7 %expand.5 = (f32[288,576]{1,0:T(8,128)S(1)}, f32[288,576]{1,0:T(8,128)S(1)}, f32[288,1]{1,0:T(8,128)S(1)}) custom-call(s32[60]{0:T(128)S(1)} %get-tuple-element.139.tab.refs_0_, bf16[144,896]{1,0:T(8,128)(2,1)S(1)} %add_convert_fusion.refs_0_.refs_1_, bf16[144,896]{1,0:T(8,128)(2,1)S(1)} %collective-permute-done.24.refs_1_, f32[8,1,896]{2,1,0:T(1,128)S(1)} %bitcast.27, ...), custom_call_target="tpu_custom_call" | custom-call | flops 1 | bytes 1 | tf_op jit(solution)/shard_map/expand/pallas_call | solution.py:651
  64.4 4.6 %collective-permute-done.23.refs_1_.refs_4_.refs_5_ = bf16[144,896]{1,0:T(8,128)(2,1)S(1)} collective-permute-done((bf16[144,896]{1,0:T(8,128)(2,1)S(1)}, bf16[144,896]{1,0:T(8,128)(2,1)S(1)}, u32[]{:S(2)}, u32[]{:S(2)}) %collective-permute-start.23) | collective-permute-done | bytes 258080 | tf_op jit(solution)/shard_map/ppermute | solution.py:798
  69.2 1.8 %collective-permute-start.25 = (bf16[144,896]{1,0:T(8,128)(2,1)S(1)}, bf16[144,896]{1,0:T(8,128)(2,1)S(1)}, u32[]{:S(2)}, u32[]{:S(2)}) collective-permute-start(bf16[144,896]{1,0:T(8,128)(2,1)S(1)} %collective-permute-done.22.refs_0_.refs_2_.refs_3_), channel_id=1, source_target_pairs={{0,4},{4,8},{8,12},{12,14},{14,10},{10,6},{6,2},{2,0},{1,5},{5,9},... | collective-permute-start | bytes 774152 | tf_op jit(solution)/shard_map/ppermute | solution.py:795
  71.3 2.9 %expand.6 = (f32[288,576]{1,0:T(8,128)S(1)}, f32[288,576]{1,0:T(8,128)S(1)}, f32[288,1]{1,0:T(8,128)S(1)}) custom-call(s32[60]{0:T(128)S(1)} %get-tuple-element.139.tab.refs_0_, bf16[144,896]{1,0:T(8,128)(2,1)S(1)} %collective-permute-done.22.refs_0_.refs_2_.refs_3_, bf16[144,896]{1,0:T(8,128)(2,1)S(1)} %collective-permute-done.23.refs_1_.refs_4_.refs_5_, ...), custom_call_target="tpu_custom_call" | custom-call | flops 1 | bytes 1 | tf_op jit(solution)/shard_map/expand/pallas_call | solution.py:651
  74.2 3.7 %collective-permute-done.25.refs_0_.refs_6_.refs_7_ = bf16[144,896]{1,0:T(8,128)(2,1)S(1)} collective-permute-done((bf16[144,896]{1,0:T(8,128)(2,1)S(1)}, bf16[144,896]{1,0:T(8,128)(2,1)S(1)}, u32[]{:S(2)}, u32[]{:S(2)}) %collective-permute-start.25) | collective-permute-done | bytes 258080 | tf_op jit(solution)/shard_map/ppermute | solution.py:795
  77.8 1.5 %collective-permute-done.26.refs_1_.refs_8_.refs_9_ = bf16[144,896]{1,0:T(8,128)(2,1)S(1)} collective-permute-done((bf16[144,896]{1,0:T(8,128)(2,1)S(1)}, bf16[144,896]{1,0:T(8,128)(2,1)S(1)}, u32[]{:S(2)}, u32[]{:S(2)}) %collective-permute-start.26) | collective-permute-done | bytes 258080 | tf_op jit(solution)/shard_map/ppermute | solution.py:798
  79.7 1.7 %collective-permute-start.29 = (bf16[144,896]{1,0:T(8,128)(2,1)S(1)}, bf16[144,896]{1,0:T(8,128)(2,1)S(1)}, u32[]{:S(2)}, u32[]{:S(2)}) collective-permute-start(bf16[144,896]{1,0:T(8,128)(2,1)S(1)} %collective-permute-done.26.refs_1_.refs_8_.refs_9_), channel_id=1, source_target_pairs={{4,0},{8,4},{12,8},{14,12},{10,14},{6,10},{2,6},{0,2},{5,1},{9,5},... | collective-permute-start | bytes 774152 | tf_op jit(solution)/shard_map/ppermute | solution.py:798
  81.5 2.9 %expand.7 = (f32[288,576]{1,0:T(8,128)S(1)}, f32[288,576]{1,0:T(8,128)S(1)}, f32[288,1]{1,0:T(8,128)S(1)}) custom-call(s32[60]{0:T(128)S(1)} %get-tuple-element.139.tab.refs_0_, bf16[144,896]{1,0:T(8,128)(2,1)S(1)} %collective-permute-done.25.refs_0_.refs_6_.refs_7_, bf16[144,896]{1,0:T(8,128)(2,1)S(1)} %collective-permute-done.26.refs_1_.refs_8_.refs_9_, ...), custom_call_target="tpu_custom_call" | custom-call | flops 1 | bytes 1 | tf_op jit(solution)/shard_map/expand/pallas_call | solution.py:651
  84.4 3.7 %collective-permute-done.28.refs_0_.refs_10_.refs_11_ = bf16[144,896]{1,0:T(8,128)(2,1)S(1)} collective-permute-done((bf16[144,896]{1,0:T(8,128)(2,1)S(1)}, bf16[144,896]{1,0:T(8,128)(2,1)S(1)}, u32[]{:S(2)}, u32[]{:S(2)}) %collective-permute-start.28) | collective-permute-done | bytes 258080 | tf_op jit(solution)/shard_map/ppermute | solution.py:795
  88.5 1.8 %collective-permute-start.32 = (bf16[64,896]{1,0:T(8,128)(2,1)S(1)}, bf16[64,896]{1,0:T(8,128)(2,1)S(1)}, u32[]{:S(2)}, u32[]{:S(2)}) collective-permute-start(bf16[64,896]{1,0:T(8,128)(2,1)S(1)} %slice.19), channel_id=1, source_target_pairs={{4,0},{8,4},{12,8},{14,12},{10,14},{6,10},{2,6},{0,2},{5,1},{9,5},... | collective-permute-start | bytes 344072 | tf_op jit(solution)/shard_map/ppermute | solution.py:798
  90.3 2.9 %expand.8 = (f32[288,576]{1,0:T(8,128)S(1)}, f32[288,576]{1,0:T(8,128)S(1)}, f32[288,1]{1,0:T(8,128)S(1)}) custom-call(s32[60]{0:T(128)S(1)} %get-tuple-element.139.tab.refs_0_, bf16[144,896]{1,0:T(8,128)(2,1)S(1)} %collective-permute-done.28.refs_0_.refs_10_.refs_11_, bf16[144,896]{1,0:T(8,128)(2,1)S(1)} %collective-permute-done.29.refs_1_.refs_12_.refs_13_, ...), custom_call_target="tpu_custom_call" | custom-call | flops 1 | bytes 1 | tf_op jit(solution)/shard_map/expand/pallas_call | solution.py:651
  94.9 1.0 collective-permute-done.35.refs_3_
  95.9 1.8 %expand.9.hidden = bf16[288,576]{1,0:T(8,128)(2,1)S(1)} custom-call(s32[60]{0:T(128)S(1)} %get-tuple-element.139.tab.refs_0_, bf16[80,896]{1,0:T(8,128)(2,1)S(1)} %collective-permute-done.31.refs_0_, bf16[64,896]{1,0:T(8,128)(2,1)S(1)} %collective-permute-done.32.refs_1_, bf16[80,896]{1,0:T(8,128)(2,1)S(1)} %collective-permute-done.34.refs_2_, ...), custom_call_target="tpu_custom_call" | custom-call | flops 1 | bytes 1 | tf_op jit(solution)/shard_map/expand/pallas_call | solution.py:651
  97.8 1.2 contract.6
  99.4 1.2 contract.7
  101.5 1.3 contract.5.mine
  102.8 1.3 contract.4.mine
  104.1 0.8 pick.2
  106.2 1.8 %collective-permute-start.38 = (bf16[16,3584]{1,0:T(8,128)(2,1)S(1)}, bf16[16,3584]{1,0:T(8,128)(2,1)S(1)}, u32[]{:S(2)}, u32[]{:S(2)}) collective-permute-start(bf16[16,3584]{1,0:T(8,128)(2,1)S(1)} %convert_element_type.137), channel_id=1, source_target_pairs={{4,0},{8,4},{12,8},{14,12},{10,14},{6,10},{2,6},{0,2},{5,1},{9,5},... | collective-permute-start | bytes 344072 | tf_op jit(solution)/shard_map/ppermute | solution.py:798
  108.0 0.8 pick.3
  109.2 1.8 %collective-permute-start.48 = (bf16[16,3584]{1,0:T(8,128)(2,1)S(1)}, bf16[16,3584]{1,0:T(8,128)(2,1)S(1)}, u32[]{:S(2)}, u32[]{:S(2)}) collective-permute-start(bf16[16,3584]{1,0:T(8,128)(2,1)S(1)} %convert_element_type.157), channel_id=1, source_target_pairs={{4,0},{8,4},{12,8},{14,12},{10,14},{6,10},{2,6},{0,2},{5,1},{9,5},... | collective-permute-start | bytes 344072 | tf_op jit(solution)/shard_map/ppermute | solution.py:798
  111.7 1.7 %collective-permute-start.40 = (bf16[16,3584]{1,0:T(8,128)(2,1)S(1)}, bf16[16,3584]{1,0:T(8,128)(2,1)S(1)}, u32[]{:S(2)}, u32[]{:S(2)}) collective-permute-start(bf16[16,3584]{1,0:T(8,128)(2,1)S(1)} %add_convert_fusion.11), channel_id=1, source_target_pairs={{4,0},{8,4},{12,8},{14,12},{10,14},{6,10},{2,6},{0,2},{5,1},{9,5},... | collective-permute-start | bytes 344072 | tf_op jit(solution)/shard_map/ppermute | solution.py:798
  113.4 0.8 collective-permute-done.47
  114.8 2.0 %collective-permute-start.50 = (bf16[16,3584]{1,0:T(8,128)(2,1)S(1)}, bf16[16,3584]{1,0:T(8,128)(2,1)S(1)}, u32[]{:S(2)}, u32[]{:S(2)}) collective-permute-start(bf16[16,3584]{1,0:T(8,128)(2,1)S(1)} %add_convert_fusion.5), channel_id=1, source_target_pairs={{4,0},{8,4},{12,8},{14,12},{10,14},{6,10},{2,6},{0,2},{5,1},{9,5},... | collective-permute-start | bytes 344072 | tf_op jit(solution)/shard_map/ppermute | solution.py:798
  117.6 1.4 collective-permute-start.41
  119.0 0.7 collective-permute-start.42
  119.7 0.8 collective-permute-done.49
  121.2 1.6 %collective-permute-start.52 = (bf16[16,3584]{1,0:T(8,128)(2,1)S(1)}, bf16[16,3584]{1,0:T(8,128)(2,1)S(1)}, u32[]{:S(2)}, u32[]{:S(2)}) collective-permute-start(bf16[16,3584]{1,0:T(8,128)(2,1)S(1)} %add_convert_fusion.3), channel_id=1, source_target_pairs={{4,0},{8,4},{12,8},{14,12},{10,14},{6,10},{2,6},{0,2},{5,1},{9,5},... | collective-permute-start | bytes 344072 | tf_op jit(solution)/shard_map/ppermute | solution.py:798
  123.0 1.1 collective-permute-done.42
  124.2 1.3 collective-permute-start.43
  125.5 0.8 collective-permute-start.44
  126.3 2.7 %collective-permute-done.43 = bf16[16,3584]{1,0:T(8,128)(2,1)S(1)} collective-permute-done((bf16[16,3584]{1,0:T(8,128)(2,1)S(1)}, bf16[16,3584]{1,0:T(8,128)(2,1)S(1)}, u32[]{:S(2)}, u32[]{:S(2)}) %collective-permute-start.43) | collective-permute-done | bytes 114720 | tf_op jit(solution)/shard_map/ppermute | solution.py:795
  129.0 1.3 collective-permute-done.44
  130.5 1.8 %collective-permute-start.53 = (bf16[16,3584]{1,0:T(8,128)(2,1)S(1)}, bf16[16,3584]{1,0:T(8,128)(2,1)S(1)}, u32[]{:S(2)}, u32[]{:S(2)}) collective-permute-start(bf16[16,3584]{1,0:T(8,128)(2,1)S(1)} %add_convert_fusion.2), channel_id=1, source_target_pairs={{0,4},{4,8},{8,12},{12,14},{14,10},{10,6},{6,2},{2,0},{1,5},{5,9},... | collective-permute-start | bytes 344072 | tf_op jit(solution)/shard_map/ppermute | solution.py:795
  132.6 3.5 %collective-permute-done.53 = bf16[16,3584]{1,0:T(8,128)(2,1)S(1)} collective-permute-done((bf16[16,3584]{1,0:T(8,128)(2,1)S(1)}, bf16[16,3584]{1,0:T(8,128)(2,1)S(1)}, u32[]{:S(2)}, u32[]{:S(2)}) %collective-permute-start.53) | collective-permute-done | bytes 114720 | tf_op jit(solution)/shard_map/ppermute | solution.py:795
  136.1 1.5 %collective-permute-done.54 = bf16[16,3584]{1,0:T(8,128)(2,1)S(1)} collective-permute-done((bf16[16,3584]{1,0:T(8,128)(2,1)S(1)}, bf16[16,3584]{1,0:T(8,128)(2,1)S(1)}, u32[]{:S(2)}, u32[]{:S(2)}) %collective-permute-start.54) | collective-permute-done | bytes 114720 | tf_op jit(solution)/shard_map/ppermute | solution.py:798
  137.9 1.2 collective-permute-done.55
  139.1 0.9 maximum_select_fusion
  (134 shorter events, 16.1 us)
Async XLA Ops:
  0.0 12.8 %copy-start = (bf16[64,7168]{1,0:T(8,128)(2,1)S(1)}, bf16[64,7168]{1,0:T(8,128)(2,1)}, u32[]{:S(2)}) copy-start(bf16[64,7168]{1,0:T(8,128)(2,1)} %res.1) | copy-start | bytes 2752516
  9.7 19.2 %collective-permute-start.11 = (bf16[32,2048]{1,0:T(8,128)(2,1)S(1)}, bf16[32,2048]{1,0:T(8,128)(2,1)S(1)}, u32[]{:S(2)}, u32[]{:S(2)}) collective-permute-start(bf16[32,2048]{1,0:T(8,128)(2,1)S(1)} %get-tuple-element.164), channel_id=1, source_target_pairs={{0,4},{4,8},{8,12},{12,14},{14,10},{10,6},{6,2},{2,0},{1,5},{5,9},... | collective-permute-start | bytes 393224 | tf_op jit(solution)/shard_map/ppermute | solution.py:795
  13.4 39.9 %slice-start.6 = ((s8[7340032]{0:T(1024)(128)(4,1)}), s8[4194304]{0:T(1024)(128)(4,1)S(1)}, s32[]{:S(2)}) async-start(s8[7340032]{0:T(1024)(128)(4,1)} %bitcast.25), calls=%async_computation.6 | async-start | bytes 8388608
  13.4 12.7 %collective-permute-start = (bf16[64,896]{1,0:T(8,128)(2,1)S(1)}, bf16[64,896]{1,0:T(8,128)(2,1)S(1)}, u32[]{:S(2)}, u32[]{:S(2)}) collective-permute-start(bf16[64,896]{1,0:T(8,128)(2,1)S(1)} %get-tuple-element.142), channel_id=1, source_target_pairs={{0,2},{1,11},{2,4},{3,13},{4,6},{5,15},{6,8},{7,1},{8,10},{9,3},{1... | collective-permute-start | bytes 344072 | tf_op jit(solution)/shard_map/ppermute | solution.py:822
  13.4 12.6 %collective-permute-start.1 = (bf16[64,896]{1,0:T(8,128)(2,1)S(1)}, bf16[64,896]{1,0:T(8,128)(2,1)S(1)}, u32[]{:S(2)}, u32[]{:S(2)}) collective-permute-start(bf16[64,896]{1,0:T(8,128)(2,1)S(1)} %get-tuple-element.143), channel_id=1, source_target_pairs={{0,4},{1,13},{2,6},{3,15},{4,8},{5,1},{6,10},{7,3},{8,12},{9,5},{1... | collective-permute-start | bytes 344072 | tf_op jit(solution)/shard_map/ppermute | solution.py:822
  15.4 10.7 %collective-permute-start.2 = (bf16[64,896]{1,0:T(8,128)(2,1)S(1)}, bf16[64,896]{1,0:T(8,128)(2,1)S(1)}, u32[]{:S(2)}, u32[]{:S(2)}) collective-permute-start(bf16[64,896]{1,0:T(8,128)(2,1)S(1)} %get-tuple-element.144), channel_id=1, source_target_pairs={{0,6},{1,15},{2,8},{3,1},{4,10},{5,3},{6,12},{7,5},{8,14},{9,7},{1... | collective-permute-start | bytes 344072 | tf_op jit(solution)/shard_map/ppermute | solution.py:822
  19.0 9.9 %collective-permute-start.12 = (bf16[32,2048]{1,0:T(8,128)(2,1)S(1)}, bf16[32,2048]{1,0:T(8,128)(2,1)S(1)}, u32[]{:S(2)}, u32[]{:S(2)}) collective-permute-start(bf16[32,2048]{1,0:T(8,128)(2,1)S(1)} %get-tuple-element.182.refs_0_), channel_id=1, source_target_pairs={{4,0},{8,4},{12,8},{14,12},{10,14},{6,10},{2,6},{0,2},{5,1},{9,5},... | collective-permute-start | bytes 393224 | tf_op jit(solution)/shard_map/ppermute | solution.py:798
  20.1 33.1 %slice-start.7 = ((s8[7340032]{0:T(1024)(128)(4,1)}), s8[3145728]{0:T(1024)(128)(4,1)S(1)}, s32[]{:S(2)}) async-start(s8[7340032]{0:T(1024)(128)(4,1)} %bitcast.25), calls=%async_computation.7 | async-start | bytes 6291456
  26.1 13.4 %collective-permute-start.14 = (bf16[64,896]{1,0:T(8,128)(2,1)S(1)}, bf16[64,896]{1,0:T(8,128)(2,1)S(1)}, u32[]{:S(2)}, u32[]{:S(2)}) collective-permute-start(bf16[64,896]{1,0:T(8,128)(2,1)S(1)} %get-tuple-element.168.own), channel_id=1, source_target_pairs={{1,9},{3,11},{5,13},{7,15},{9,1},{11,3},{13,5},{15,7},{17,25},{19,... | collective-permute-start | bytes 344072 | tf_op jit(solution)/shard_map/ppermute | solution.py:822
  26.8 5.6 %collective-permute-start.3 = (bf16[32,2048]{1,0:T(8,128)(2,1)S(1)}, bf16[32,2048]{1,0:T(8,128)(2,1)S(1)}, u32[]{:S(2)}, u32[]{:S(2)}) collective-permute-start(bf16[32,2048]{1,0:T(8,128)(2,1)S(1)} %get-tuple-element.152), channel_id=1, source_target_pairs={{0,4},{4,8},{8,12},{12,14},{14,10},{10,6},{6,2},{2,0},{1,5},{5,9},... | collective-permute-start | bytes 393224 | tf_op jit(solution)/shard_map/ppermute | solution.py:795
  28.4 6.2 %collective-permute-start.4 = (bf16[32,2048]{1,0:T(8,128)(2,1)S(1)}, bf16[32,2048]{1,0:T(8,128)(2,1)S(1)}, u32[]{:S(2)}, u32[]{:S(2)}) collective-permute-start(bf16[32,2048]{1,0:T(8,128)(2,1)S(1)} %get-tuple-element.155.refs_0_), channel_id=1, source_target_pairs={{4,0},{8,4},{12,8},{14,12},{10,14},{6,10},{2,6},{0,2},{5,1},{9,5},... | collective-permute-start | bytes 393224 | tf_op jit(solution)/shard_map/ppermute | solution.py:798
  28.9 7.8 %collective-permute-start.13 = (bf16[32,2048]{1,0:T(8,128)(2,1)S(1)}, bf16[32,2048]{1,0:T(8,128)(2,1)S(1)}, u32[]{:S(2)}, u32[]{:S(2)}) collective-permute-start(bf16[32,2048]{1,0:T(8,128)(2,1)S(1)} %broadcast_select_fusion.5), channel_id=1, source_target_pairs={{0,4},{4,8},{8,12},{12,14},{14,10},{10,6},{6,2},{2,0},{1,5},{5,9},... | collective-permute-start | bytes 393224 | tf_op jit(solution)/shard_map/ppermute | solution.py:795
  30.5 6.9 %collective-permute-start.15 = (bf16[32,2048]{1,0:T(8,128)(2,1)S(1)}, bf16[32,2048]{1,0:T(8,128)(2,1)S(1)}, u32[]{:S(2)}, u32[]{:S(2)}) collective-permute-start(bf16[32,2048]{1,0:T(8,128)(2,1)S(1)} %broadcast_select_fusion.4), channel_id=1, source_target_pairs={{4,0},{8,4},{12,8},{14,12},{10,14},{6,10},{2,6},{0,2},{5,1},{9,5},... | collective-permute-start | bytes 393224 | tf_op jit(solution)/shard_map/ppermute | solution.py:798
  34.6 6.4 %collective-permute-start.5 = (bf16[32,2048]{1,0:T(8,128)(2,1)S(1)}, bf16[32,2048]{1,0:T(8,128)(2,1)S(1)}, u32[]{:S(2)}, u32[]{:S(2)}) collective-permute-start(bf16[32,2048]{1,0:T(8,128)(2,1)S(1)} %broadcast_select_fusion.11), channel_id=1, source_target_pairs={{0,4},{4,8},{8,12},{12,14},{14,10},{10,6},{6,2},{2,0},{1,5},{5,9},... | collective-permute-start | bytes 393224 | tf_op jit(solution)/shard_map/ppermute | solution.py:795
  36.6 6.3 %collective-permute-start.6 = (bf16[32,2048]{1,0:T(8,128)(2,1)S(1)}, bf16[32,2048]{1,0:T(8,128)(2,1)S(1)}, u32[]{:S(2)}, u32[]{:S(2)}) collective-permute-start(bf16[32,2048]{1,0:T(8,128)(2,1)S(1)} %broadcast_select_fusion.10), channel_id=1, source_target_pairs={{4,0},{8,4},{12,8},{14,12},{10,14},{6,10},{2,6},{0,2},{5,1},{9,5},... | collective-permute-start | bytes 393224 | tf_op jit(solution)/shard_map/ppermute | solution.py:798
  37.5 7.5 %collective-permute-start.16 = (bf16[32,2048]{1,0:T(8,128)(2,1)S(1)}, bf16[32,2048]{1,0:T(8,128)(2,1)S(1)}, u32[]{:S(2)}, u32[]{:S(2)}) collective-permute-start(bf16[32,2048]{1,0:T(8,128)(2,1)S(1)} %broadcast_select_fusion.3), channel_id=1, source_target_pairs={{0,4},{4,8},{8,12},{12,14},{14,10},{10,6},{6,2},{2,0},{1,5},{5,9},... | collective-permute-start | bytes 393224 | tf_op jit(solution)/shard_map/ppermute | solution.py:795
  38.7 6.6 %collective-permute-start.17 = (bf16[32,2048]{1,0:T(8,128)(2,1)S(1)}, bf16[32,2048]{1,0:T(8,128)(2,1)S(1)}, u32[]{:S(2)}, u32[]{:S(2)}) collective-permute-start(bf16[32,2048]{1,0:T(8,128)(2,1)S(1)} %broadcast_select_fusion.2), channel_id=1, source_target_pairs={{4,0},{8,4},{12,8},{14,12},{10,14},{6,10},{2,6},{0,2},{5,1},{9,5},... | collective-permute-start | bytes 393224 | tf_op jit(solution)/shard_map/ppermute | solution.py:798
  40.1 11.6 %collective-permute-start.20 = (bf16[128,896]{1,0:T(8,128)(2,1)S(1)}, bf16[128,896]{1,0:T(8,128)(2,1)S(1)}, u32[]{:S(2)}, u32[]{:S(2)}) collective-permute-start(bf16[128,896]{1,0:T(8,128)(2,1)S(1)} %share.1), channel_id=1, source_target_pairs={{0,1},{1,0},{2,3},{3,2},{4,5},{5,4},{6,7},{7,6},{8,9},{9,8},{10,11... | collective-permute-start | bytes 688136 | tf_op jit(solution)/shard_map/ppermute | solution.py:801
  42.9 5.2 %collective-permute-start.7 = (bf16[32,2048]{1,0:T(8,128)(2,1)S(1)}, bf16[32,2048]{1,0:T(8,128)(2,1)S(1)}, u32[]{:S(2)}, u32[]{:S(2)}) collective-permute-start(bf16[32,2048]{1,0:T(8,128)(2,1)S(1)} %broadcast_select_fusion.9), channel_id=1, source_target_pairs={{0,4},{4,8},{8,12},{12,14},{14,10},{10,6},{6,2},{2,0},{1,5},{5,9},... | collective-permute-start | bytes 393224 | tf_op jit(solution)/shard_map/ppermute | solution.py:795
  44.3 5.2 %collective-permute-start.8 = (bf16[32,2048]{1,0:T(8,128)(2,1)S(1)}, bf16[32,2048]{1,0:T(8,128)(2,1)S(1)}, u32[]{:S(2)}, u32[]{:S(2)}) collective-permute-start(bf16[32,2048]{1,0:T(8,128)(2,1)S(1)} %broadcast_select_fusion.8), channel_id=1, source_target_pairs={{4,0},{8,4},{12,8},{14,12},{10,14},{6,10},{2,6},{0,2},{5,1},{9,5},... | collective-permute-start | bytes 393224 | tf_op jit(solution)/shard_map/ppermute | solution.py:798
  45.0 17.7 %slice-start.2 = ((s8[8257536]{0:T(1024)(128)(4,1)}), s8[4194304]{0:T(1024)(128)(4,1)S(1)}, s32[]{:S(2)}) async-start(s8[8257536]{0:T(1024)(128)(4,1)} %bitcast.16), calls=%async_computation.2 | async-start | bytes 8388608
  45.3 6.4 %collective-permute-start.18 = (bf16[32,2048]{1,0:T(8,128)(2,1)S(1)}, bf16[32,2048]{1,0:T(8,128)(2,1)S(1)}, u32[]{:S(2)}, u32[]{:S(2)}) collective-permute-start(bf16[32,2048]{1,0:T(8,128)(2,1)S(1)} %broadcast_select_fusion.1), channel_id=1, source_target_pairs={{0,4},{4,8},{8,12},{12,14},{14,10},{10,6},{6,2},{2,0},{1,5},{5,9},... | collective-permute-start | bytes 393224 | tf_op jit(solution)/shard_map/ppermute | solution.py:795
  47.1 6.1 %collective-permute-start.19 = (bf16[32,2048]{1,0:T(8,128)(2,1)S(1)}, bf16[32,2048]{1,0:T(8,128)(2,1)S(1)}, u32[]{:S(2)}, u32[]{:S(2)}) collective-permute-start(bf16[32,2048]{1,0:T(8,128)(2,1)S(1)} %broadcast_select_fusion), channel_id=1, source_target_pairs={{4,0},{8,4},{12,8},{14,12},{10,14},{6,10},{2,6},{0,2},{5,1},{9,5},... | collective-permute-start | bytes 393224 | tf_op jit(solution)/shard_map/ppermute | solution.py:798
  49.6 5.6 %collective-permute-start.9 = (bf16[32,2048]{1,0:T(8,128)(2,1)S(1)}, bf16[32,2048]{1,0:T(8,128)(2,1)S(1)}, u32[]{:S(2)}, u32[]{:S(2)}) collective-permute-start(bf16[32,2048]{1,0:T(8,128)(2,1)S(1)} %broadcast_select_fusion.7), channel_id=1, source_target_pairs={{0,4},{4,8},{8,12},{12,14},{14,10},{10,6},{6,2},{2,0},{1,5},{5,9},... | collective-permute-start | bytes 393224 | tf_op jit(solution)/shard_map/ppermute | solution.py:795
  51.7 5.0 %collective-permute-start.10 = (bf16[32,2048]{1,0:T(8,128)(2,1)S(1)}, bf16[32,2048]{1,0:T(8,128)(2,1)S(1)}, u32[]{:S(2)}, u32[]{:S(2)}) collective-permute-start(bf16[32,2048]{1,0:T(8,128)(2,1)S(1)} %broadcast_select_fusion.6), channel_id=1, source_target_pairs={{4,0},{8,4},{12,8},{14,12},{10,14},{6,10},{2,6},{0,2},{5,1},{9,5},... | collective-permute-start | bytes 393224 | tf_op jit(solution)/shard_map/ppermute | solution.py:798
  53.2 9.5 %slice-start = ((s8[8257536]{0:T(1024)(128)(4,1)}), s8[4194304]{0:T(1024)(128)(4,1)S(1)}, s32[]{:S(2)}) async-start(s8[8257536]{0:T(1024)(128)(4,1)} %bitcast.9), calls=%async_computation | async-start | bytes 8388608
  55.2 7.5 %slice-start.1 = ((s8[8257536]{0:T(1024)(128)(4,1)}), s8[4063232]{0:T(1024)(128)(4,1)S(1)}, s32[]{:S(2)}) async-start(s8[8257536]{0:T(1024)(128)(4,1)} %bitcast.9), calls=%async_computation.1 | async-start | bytes 8126464
  55.2 7.5 %slice-start.3 = ((s8[8257536]{0:T(1024)(128)(4,1)}), s8[4063232]{0:T(1024)(128)(4,1)S(1)}, s32[]{:S(2)}) async-start(s8[8257536]{0:T(1024)(128)(4,1)} %bitcast.16), calls=%async_computation.3 | async-start | bytes 8126464
  55.2 7.5 %copy-start.1 = (f32[7168]{0:T(1024)S(1)}, f32[7168]{0:T(1024)}, u32[]{:S(2)}) copy-start(f32[7168]{0:T(1024)} %param.24) | copy-start | bytes 86020
  58.7 1.6 %collective-permute-start.21 = (bf16[144,896]{1,0:T(8,128)(2,1)S(1)}, bf16[144,896]{1,0:T(8,128)(2,1)S(1)}, u32[]{:S(2)}, u32[]{:S(2)}) collective-permute-start(bf16[144,896]{1,0:T(8,128)(2,1)S(1)} %get-tuple-element.194), channel_id=1, source_target_pairs={{0,1},{1,0},{2,3},{3,2},{4,5},{5,4},{6,7},{7,6},{8,9},{9,8},{10,11... | collective-permute-start | bytes 774152 | tf_op jit(solution)/shard_map/ppermute | solution.py:801
  60.4 2.3 %collective-permute-start.24 = (bf16[144,896]{1,0:T(8,128)(2,1)S(1)}, bf16[144,896]{1,0:T(8,128)(2,1)S(1)}, u32[]{:S(2)}, u32[]{:S(2)}) collective-permute-start(bf16[144,896]{1,0:T(8,128)(2,1)S(1)} %add_convert_fusion.refs_0_.refs_1_), channel_id=1, source_target_pairs={{0,1},{1,0},{2,3},{3,2},{4,5},{5,4},{6,7},{7,6},{8,9},{9,8},{10,11... | collective-permute-start | bytes 774152 | tf_op jit(solution)/shard_map/ppermute | solution.py:801
  60.6 8.5 %collective-permute-start.23 = (bf16[144,896]{1,0:T(8,128)(2,1)S(1)}, bf16[144,896]{1,0:T(8,128)(2,1)S(1)}, u32[]{:S(2)}, u32[]{:S(2)}) collective-permute-start(bf16[144,896]{1,0:T(8,128)(2,1)S(1)} %add_convert_fusion.refs_0_.refs_1_), channel_id=1, source_target_pairs={{4,0},{8,4},{12,8},{14,12},{10,14},{6,10},{2,6},{0,2},{5,1},{9,5},... | collective-permute-start | bytes 774152 | tf_op jit(solution)/shard_map/ppermute | solution.py:798
  60.7 8.4 %collective-permute-start.22 = (bf16[144,896]{1,0:T(8,128)(2,1)S(1)}, bf16[144,896]{1,0:T(8,128)(2,1)S(1)}, u32[]{:S(2)}, u32[]{:S(2)}) collective-permute-start(bf16[144,896]{1,0:T(8,128)(2,1)S(1)} %add_convert_fusion.refs_0_.refs_1_), channel_id=1, source_target_pairs={{0,4},{4,8},{8,12},{12,14},{14,10},{10,6},{6,2},{2,0},{1,5},{5,9},... | collective-permute-start | bytes 774152 | tf_op jit(solution)/shard_map/ppermute | solution.py:795
  69.1 2.2 %collective-permute-start.27 = (bf16[288,896]{1,0:T(8,128)(2,1)S(1)}, bf16[288,896]{1,0:T(8,128)(2,1)S(1)}, u32[]{:S(2)}, u32[]{:S(2)}) collective-permute-start(bf16[288,896]{1,0:T(8,128)(2,1)S(1)} %pad_maximum_fusion), channel_id=1, source_target_pairs={{0,1},{1,0},{2,3},{3,2},{4,5},{5,4},{6,7},{7,6},{8,9},{9,8},{10,11... | collective-permute-start | bytes 1548296 | tf_op jit(solution)/shard_map/ppermute | solution.py:801
  69.2 8.6 %collective-permute-start.25 = (bf16[144,896]{1,0:T(8,128)(2,1)S(1)}, bf16[144,896]{1,0:T(8,128)(2,1)S(1)}, u32[]{:S(2)}, u32[]{:S(2)}) collective-permute-start(bf16[144,896]{1,0:T(8,128)(2,1)S(1)} %collective-permute-done.22.refs_0_.refs_2_.refs_3_), channel_id=1, source_target_pairs={{0,4},{4,8},{8,12},{12,14},{14,10},{10,6},{6,2},{2,0},{1,5},{5,9},... | collective-permute-start | bytes 774152 | tf_op jit(solution)/shard_map/ppermute | solution.py:795
  71.0 8.3 %collective-permute-start.26 = (bf16[144,896]{1,0:T(8,128)(2,1)S(1)}, bf16[144,896]{1,0:T(8,128)(2,1)S(1)}, u32[]{:S(2)}, u32[]{:S(2)}) collective-permute-start(bf16[144,896]{1,0:T(8,128)(2,1)S(1)} %collective-permute-done.23.refs_1_.refs_4_.refs_5_), channel_id=1, source_target_pairs={{4,0},{8,4},{12,8},{14,12},{10,14},{6,10},{2,6},{0,2},{5,1},{9,5},... | collective-permute-start | bytes 774152 | tf_op jit(solution)/shard_map/ppermute | solution.py:798
  79.3 2.2 %collective-permute-start.30 = (bf16[288,896]{1,0:T(8,128)(2,1)S(1)}, bf16[288,896]{1,0:T(8,128)(2,1)S(1)}, u32[]{:S(2)}, u32[]{:S(2)}) collective-permute-start(bf16[288,896]{1,0:T(8,128)(2,1)S(1)} %pad_maximum_fusion.1), channel_id=1, source_target_pairs={{0,1},{1,0},{2,3},{3,2},{4,5},{5,4},{6,7},{7,6},{8,9},{9,8},{10,11... | collective-permute-start | bytes 1548296 | tf_op jit(solution)/shard_map/ppermute | solution.py:801
  79.4 8.6 %collective-permute-start.28 = (bf16[144,896]{1,0:T(8,128)(2,1)S(1)}, bf16[144,896]{1,0:T(8,128)(2,1)S(1)}, u32[]{:S(2)}, u32[]{:S(2)}) collective-permute-start(bf16[144,896]{1,0:T(8,128)(2,1)S(1)} %collective-permute-done.25.refs_0_.refs_6_.refs_7_), channel_id=1, source_target_pairs={{0,4},{4,8},{8,12},{12,14},{14,10},{10,6},{6,2},{2,0},{1,5},{5,9},... | collective-permute-start | bytes 774152 | tf_op jit(solution)/shard_map/ppermute | solution.py:795
  79.7 8.3 %collective-permute-start.29 = (bf16[144,896]{1,0:T(8,128)(2,1)S(1)}, bf16[144,896]{1,0:T(8,128)(2,1)S(1)}, u32[]{:S(2)}, u32[]{:S(2)}) collective-permute-start(bf16[144,896]{1,0:T(8,128)(2,1)S(1)} %collective-permute-done.26.refs_1_.refs_8_.refs_9_), channel_id=1, source_target_pairs={{4,0},{8,4},{12,8},{14,12},{10,14},{6,10},{2,6},{0,2},{5,1},{9,5},... | collective-permute-start | bytes 774152 | tf_op jit(solution)/shard_map/ppermute | solution.py:798
  88.1 2.2 %collective-permute-start.33 = (bf16[288,896]{1,0:T(8,128)(2,1)S(1)}, bf16[288,896]{1,0:T(8,128)(2,1)S(1)}, u32[]{:S(2)}, u32[]{:S(2)}) collective-permute-start(bf16[288,896]{1,0:T(8,128)(2,1)S(1)} %pad_maximum_fusion.2), channel_id=1, source_target_pairs={{0,1},{1,0},{2,3},{3,2},{4,5},{5,4},{6,7},{7,6},{8,9},{9,8},{10,11... | collective-permute-start | bytes 1548296 | tf_op jit(solution)/shard_map/ppermute | solution.py:801
  88.2 6.2 %collective-permute-start.31 = (bf16[80,896]{1,0:T(8,128)(2,1)S(1)}, bf16[80,896]{1,0:T(8,128)(2,1)S(1)}, u32[]{:S(2)}, u32[]{:S(2)}) collective-permute-start(bf16[80,896]{1,0:T(8,128)(2,1)S(1)} %slice.18), channel_id=1, source_target_pairs={{0,4},{4,8},{8,12},{12,14},{14,10},{10,6},{6,2},{2,0},{1,5},{5,9},... | collective-permute-start | bytes 430088 | tf_op jit(solution)/shard_map/ppermute | solution.py:795
  88.5 5.3 %collective-permute-start.32 = (bf16[64,896]{1,0:T(8,128)(2,1)S(1)}, bf16[64,896]{1,0:T(8,128)(2,1)S(1)}, u32[]{:S(2)}, u32[]{:S(2)}) collective-permute-start(bf16[64,896]{1,0:T(8,128)(2,1)S(1)} %slice.19), channel_id=1, source_target_pairs={{4,0},{8,4},{12,8},{14,12},{10,14},{6,10},{2,6},{0,2},{5,1},{9,5},... | collective-permute-start | bytes 344072 | tf_op jit(solution)/shard_map/ppermute | solution.py:798
  94.4 1.5 %collective-permute-start.34 = (bf16[80,896]{1,0:T(8,128)(2,1)S(1)}, bf16[80,896]{1,0:T(8,128)(2,1)S(1)}, u32[]{:S(2)}, u32[]{:S(2)}) collective-permute-start(bf16[80,896]{1,0:T(8,128)(2,1)S(1)} %collective-permute-done.31.refs_0_), channel_id=1, source_target_pairs={{0,1},{1,0},{2,3},{3,2},{4,5},{5,4},{6,7},{7,6},{8,9},{9,8},{10,11... | collective-permute-start | bytes 430088 | tf_op jit(solution)/shard_map/ppermute | solution.py:801
  94.4 1.5 %collective-permute-start.35 = (bf16[64,896]{1,0:T(8,128)(2,1)S(1)}, bf16[64,896]{1,0:T(8,128)(2,1)S(1)}, u32[]{:S(2)}, u32[]{:S(2)}) collective-permute-start(bf16[64,896]{1,0:T(8,128)(2,1)S(1)} %collective-permute-done.32.refs_1_), channel_id=1, source_target_pairs={{0,1},{1,0},{2,3},{3,2},{4,5},{5,4},{6,7},{7,6},{8,9},{9,8},{10,11... | collective-permute-start | bytes 344072 | tf_op jit(solution)/shard_map/ppermute | solution.py:801
  99.1 5.0 %collective-permute-start.36 = (bf16[144,3584]{1,0:T(8,128)(2,1)S(1)}, bf16[144,3584]{1,0:T(8,128)(2,1)S(1)}, u32[]{:S(2)}, u32[]{:S(2)}) collective-permute-start(bf16[144,3584]{1,0:T(8,128)(2,1)S(1)} %contract.6), channel_id=1, source_target_pairs={{0,1},{1,0},{2,3},{3,2},{4,5},{5,4},{6,7},{7,6},{8,9},{9,8},{10,11... | collective-permute-start | bytes 3096584 | tf_op jit(solution)/shard_map/ppermute | solution.py:801
  100.6 7.4 %collective-permute-start.46 = (bf16[144,3584]{1,0:T(8,128)(2,1)S(1)}, bf16[144,3584]{1,0:T(8,128)(2,1)S(1)}, u32[]{:S(2)}, u32[]{:S(2)}) collective-permute-start(bf16[144,3584]{1,0:T(8,128)(2,1)S(1)} %contract.7), channel_id=1, source_target_pairs={{0,1},{1,0},{2,3},{3,2},{4,5},{5,4},{6,7},{7,6},{8,9},{9,8},{10,11... | collective-permute-start | bytes 3096584 | tf_op jit(solution)/shard_map/ppermute | solution.py:801
  105.0 6.0 %collective-permute-start.37 = (bf16[16,3584]{1,0:T(8,128)(2,1)S(1)}, bf16[16,3584]{1,0:T(8,128)(2,1)S(1)}, u32[]{:S(2)}, u32[]{:S(2)}) collective-permute-start(bf16[16,3584]{1,0:T(8,128)(2,1)S(1)} %convert_element_type.136), channel_id=1, source_target_pairs={{0,4},{4,8},{8,12},{12,14},{14,10},{10,6},{6,2},{2,0},{1,5},{5,9},... | collective-permute-start | bytes 344072 | tf_op jit(solution)/shard_map/ppermute | solution.py:795
  106.2 5.1 %collective-permute-start.38 = (bf16[16,3584]{1,0:T(8,128)(2,1)S(1)}, bf16[16,3584]{1,0:T(8,128)(2,1)S(1)}, u32[]{:S(2)}, u32[]{:S(2)}) collective-permute-start(bf16[16,3584]{1,0:T(8,128)(2,1)S(1)} %convert_element_type.137), channel_id=1, source_target_pairs={{4,0},{8,4},{12,8},{14,12},{10,14},{6,10},{2,6},{0,2},{5,1},{9,5},... | collective-permute-start | bytes 344072 | tf_op jit(solution)/shard_map/ppermute | solution.py:798
  108.8 5.4 %collective-permute-start.47 = (bf16[16,3584]{1,0:T(8,128)(2,1)S(1)}, bf16[16,3584]{1,0:T(8,128)(2,1)S(1)}, u32[]{:S(2)}, u32[]{:S(2)}) collective-permute-start(bf16[16,3584]{1,0:T(8,128)(2,1)S(1)} %convert_element_type.156), channel_id=1, source_target_pairs={{0,4},{4,8},{8,12},{12,14},{14,10},{10,6},{6,2},{2,0},{1,5},{5,9},... | collective-permute-start | bytes 344072 | tf_op jit(solution)/shard_map/ppermute | solution.py:795
  109.2 5.6 %collective-permute-start.48 = (bf16[16,3584]{1,0:T(8,128)(2,1)S(1)}, bf16[16,3584]{1,0:T(8,128)(2,1)S(1)}, u32[]{:S(2)}, u32[]{:S(2)}) collective-permute-start(bf16[16,3584]{1,0:T(8,128)(2,1)S(1)} %convert_element_type.157), channel_id=1, source_target_pairs={{4,0},{8,4},{12,8},{14,12},{10,14},{6,10},{2,6},{0,2},{5,1},{9,5},... | collective-permute-start | bytes 344072 | tf_op jit(solution)/shard_map/ppermute | solution.py:798
  111.4 5.8 %collective-permute-start.39 = (bf16[16,3584]{1,0:T(8,128)(2,1)S(1)}, bf16[16,3584]{1,0:T(8,128)(2,1)S(1)}, u32[]{:S(2)}, u32[]{:S(2)}) collective-permute-start(bf16[16,3584]{1,0:T(8,128)(2,1)S(1)} %add_convert_fusion.12), channel_id=1, source_target_pairs={{0,4},{4,8},{8,12},{12,14},{14,10},{10,6},{6,2},{2,0},{1,5},{5,9},... | collective-permute-start | bytes 344072 | tf_op jit(solution)/shard_map/ppermute | solution.py:795
  111.7 5.9 %collective-permute-start.40 = (bf16[16,3584]{1,0:T(8,128)(2,1)S(1)}, bf16[16,3584]{1,0:T(8,128)(2,1)S(1)}, u32[]{:S(2)}, u32[]{:S(2)}) collective-permute-start(bf16[16,3584]{1,0:T(8,128)(2,1)S(1)} %add_convert_fusion.11), channel_id=1, source_target_pairs={{4,0},{8,4},{12,8},{14,12},{10,14},{6,10},{2,6},{0,2},{5,1},{9,5},... | collective-permute-start | bytes 344072 | tf_op jit(solution)/shard_map/ppermute | solution.py:798
  114.8 5.7 %collective-permute-start.49 = (bf16[16,3584]{1,0:T(8,128)(2,1)S(1)}, bf16[16,3584]{1,0:T(8,128)(2,1)S(1)}, u32[]{:S(2)}, u32[]{:S(2)}) collective-permute-start(bf16[16,3584]{1,0:T(8,128)(2,1)S(1)} %add_convert_fusion.6), channel_id=1, source_target_pairs={{0,4},{4,8},{8,12},{12,14},{14,10},{10,6},{6,2},{2,0},{1,5},{5,9},... | collective-permute-start | bytes 344072 | tf_op jit(solution)/shard_map/ppermute | solution.py:795
  114.8 5.8 %collective-permute-start.50 = (bf16[16,3584]{1,0:T(8,128)(2,1)S(1)}, bf16[16,3584]{1,0:T(8,128)(2,1)S(1)}, u32[]{:S(2)}, u32[]{:S(2)}) collective-permute-start(bf16[16,3584]{1,0:T(8,128)(2,1)S(1)} %add_convert_fusion.5), channel_id=1, source_target_pairs={{4,0},{8,4},{12,8},{14,12},{10,14},{6,10},{2,6},{0,2},{5,1},{9,5},... | collective-permute-start | bytes 344072 | tf_op jit(solution)/shard_map/ppermute | solution.py:798
  117.6 5.3 %collective-permute-start.41 = (bf16[16,3584]{1,0:T(8,128)(2,1)S(1)}, bf16[16,3584]{1,0:T(8,128)(2,1)S(1)}, u32[]{:S(2)}, u32[]{:S(2)}) collective-permute-start(bf16[16,3584]{1,0:T(8,128)(2,1)S(1)} %add_convert_fusion.10), channel_id=1, source_target_pairs={{0,4},{4,8},{8,12},{12,14},{14,10},{10,6},{6,2},{2,0},{1,5},{5,9},... | collective-permute-start | bytes 344072 | tf_op jit(solution)/shard_map/ppermute | solution.py:795
  119.0 5.1 %collective-permute-start.42 = (bf16[16,3584]{1,0:T(8,128)(2,1)S(1)}, bf16[16,3584]{1,0:T(8,128)(2,1)S(1)}, u32[]{:S(2)}, u32[]{:S(2)}) collective-permute-start(bf16[16,3584]{1,0:T(8,128)(2,1)S(1)} %add_convert_fusion.9), channel_id=1, source_target_pairs={{4,0},{8,4},{12,8},{14,12},{10,14},{6,10},{2,6},{0,2},{5,1},{9,5},... | collective-permute-start | bytes 344072 | tf_op jit(solution)/shard_map/ppermute | solution.py:798
  120.7 5.5 %collective-permute-start.51 = (bf16[16,3584]{1,0:T(8,128)(2,1)S(1)}, bf16[16,3584]{1,0:T(8,128)(2,1)S(1)}, u32[]{:S(2)}, u32[]{:S(2)}) collective-permute-start(bf16[16,3584]{1,0:T(8,128)(2,1)S(1)} %add_convert_fusion.4), channel_id=1, source_target_pairs={{0,4},{4,8},{8,12},{12,14},{14,10},{10,6},{6,2},{2,0},{1,5},{5,9},... | collective-permute-start | bytes 344072 | tf_op jit(solution)/shard_map/ppermute | solution.py:795
  121.2 9.2 %collective-permute-start.52 = (bf16[16,3584]{1,0:T(8,128)(2,1)S(1)}, bf16[16,3584]{1,0:T(8,128)(2,1)S(1)}, u32[]{:S(2)}, u32[]{:S(2)}) collective-permute-start(bf16[16,3584]{1,0:T(8,128)(2,1)S(1)} %add_convert_fusion.3), channel_id=1, source_target_pairs={{4,0},{8,4},{12,8},{14,12},{10,14},{6,10},{2,6},{0,2},{5,1},{9,5},... | collective-permute-start | bytes 344072 | tf_op jit(solution)/shard_map/ppermute | solution.py:798
  124.2 4.8 %collective-permute-start.43 = (bf16[16,3584]{1,0:T(8,128)(2,1)S(1)}, bf16[16,3584]{1,0:T(8,128)(2,1)S(1)}, u32[]{:S(2)}, u32[]{:S(2)}) collective-permute-start(bf16[16,3584]{1,0:T(8,128)(2,1)S(1)} %add_convert_fusion.8), channel_id=1, source_target_pairs={{0,4},{4,8},{8,12},{12,14},{14,10},{10,6},{6,2},{2,0},{1,5},{5,9},... | collective-permute-start | bytes 344072 | tf_op jit(solution)/shard_map/ppermute | solution.py:795
  125.5 4.8 %collective-permute-start.44 = (bf16[16,3584]{1,0:T(8,128)(2,1)S(1)}, bf16[16,3584]{1,0:T(8,128)(2,1)S(1)}, u32[]{:S(2)}, u32[]{:S(2)}) collective-permute-start(bf16[16,3584]{1,0:T(8,128)(2,1)S(1)} %add_convert_fusion.7), channel_id=1, source_target_pairs={{4,0},{8,4},{12,8},{14,12},{10,14},{6,10},{2,6},{0,2},{5,1},{9,5},... | collective-permute-start | bytes 344072 | tf_op jit(solution)/shard_map/ppermute | solution.py:798
  130.4 2.2 %collective-permute-start.45 = (bf16[16,3584]{1,0:T(8,128)(2,1)S(1)}, bf16[16,3584]{1,0:T(8,128)(2,1)S(1)}, u32[]{:S(2)}, u32[]{:S(2)}) collective-permute-start(bf16[16,3584]{1,0:T(8,128)(2,1)S(1)} %get-tuple-element.272), channel_id=1, source_target_pairs={{0,1},{1,0},{2,3},{3,2},{4,5},{5,4},{6,7},{7,6},{8,9},{9,8},{10,11... | collective-permute-start | bytes 344072 | tf_op jit(solution)/shard_map/ppermute | solution.py:801
  130.5 5.6 %collective-permute-start.53 = (bf16[16,3584]{1,0:T(8,128)(2,1)S(1)}, bf16[16,3584]{1,0:T(8,128)(2,1)S(1)}, u32[]{:S(2)}, u32[]{:S(2)}) collective-permute-start(bf16[16,3584]{1,0:T(8,128)(2,1)S(1)} %add_convert_fusion.2), channel_id=1, source_target_pairs={{0,4},{4,8},{8,12},{12,14},{14,10},{10,6},{6,2},{2,0},{1,5},{5,9},... | collective-permute-start | bytes 344072 | tf_op jit(solution)/shard_map/ppermute | solution.py:795
  132.3 5.3 %collective-permute-start.54 = (bf16[16,3584]{1,0:T(8,128)(2,1)S(1)}, bf16[16,3584]{1,0:T(8,128)(2,1)S(1)}, u32[]{:S(2)}, u32[]{:S(2)}) collective-permute-start(bf16[16,3584]{1,0:T(8,128)(2,1)S(1)} %add_convert_fusion.1), channel_id=1, source_target_pairs={{4,0},{8,4},{12,8},{14,12},{10,14},{6,10},{2,6},{0,2},{5,1},{9,5},... | collective-permute-start | bytes 344072 | tf_op jit(solution)/shard_map/ppermute | solution.py:798
  137.7 1.4 collective-permute-start.55
  (2 other events, 6.8 us)

commit v12 on v11

--- a/solution.py
+++ b/solution.py
@@ -884,7 +884,6 @@
         blocks += [x[0] if len(x) == 1 else jnp.concatenate(x, 0) for x in arrived]
         owners += from_owner
     (hidden,) = sums
-    own = collect(tab, blocks, owners, half).astype(f32)
 
     parts = contract_parts
     theirs = [swap(contract(hidden, down_weight, part, parts, 1)) for part in range(parts)]
@@ -906,8 +905,9 @@
             out_f, out_b = lax.optimization_barrier((out_f.astype(bf16), out_b.astype(bf16)))
             got_f.append(send_next(out_f))
             got_b.append(send_prev(out_b))
-        if part > 0:
-            lows, highs, got_f[-1] = lax.optimization_barrier((lows, highs, got_f[-1]))
+        if part == 0:
+            blocks[-1], got_f[1] = lax.optimization_barrier((blocks[-1], got_f[1]))
+            own = collect(tab, blocks, owners, half).astype(f32)
         at = slice(part * columns, (part + 1) * columns)
         main = main + own[:half, at] + got_f[-1].astype(f32)
         main = (main + choose(got_b[-2], got_b[-1]).astype(f32)).astype(bf16)

time: 140 us -> 136 us (0.971)
  waiting for transfers between devices: 43.5 us -> 37.2 us
  starting transfers between devices: 51.6 us -> 54 us
    ppermute x20, waiting for transfers between devices: 21.5 us -> 7.2 us  [send_prev(): return lax.ppermute(x, 'blk', backward)]
    ppermute x20, waiting for transfers between devices: 18.9 us -> 27.1 us  [send_next(): return lax.ppermute(x, 'blk', forward)]
    ppermute x20, starting transfers between devices: 17.8 us -> 22.1 us  [send_prev(): return lax.ppermute(x, 'blk', backward)]
    ppermute x20, starting transfers between devices: 25.6 us -> 22.5 us  [send_next(): return lax.ppermute(x, 'blk', forward)]
  transfers between devices with their start and end apart: 56 -> 56, of which waited for: 32 -> 29; matrix products, arithmetic and copies ran while one was open for 1% -> 1% of each run, Pallas kernels for 19% -> 19%
where the time goes in v12:
time: 136 us
  starting transfers between devices  54 us (40%)
  Pallas kernels  39.1 us (29%)
  waiting for transfers between devices  37.2 us (27%)
  between operations  2.63 us (2%)
  other arithmetic  2.36 us (2%)
    ppermute x20, waiting for transfers between devices, send_next(): return lax.ppermute(x, 'blk', forward)  27.1 us
    ppermute x20, starting transfers between devices, send_next(): return lax.ppermute(x, 'blk', forward)  22.5 us
    ppermute x20, starting transfers between devices, send_prev(): return lax.ppermute(x, 'blk', backward)  22.1 us
    pallas_call x2, Pallas kernels, attend(): pl.pallas_call(functools.partial(attend_kernel, table, order, heads, part...  14.1 us
    pallas_call x5, Pallas kernels, expand(): pl.pallas_call(functools.partial(expand_kernel, pieces, len(theirs), firs...  12.1 us
    ppermute x20, waiting for transfers between devices, send_prev(): return lax.ppermute(x, 'blk', backward)  7.2 us
    ppermute x4, starting transfers between devices, send_piece(): pieces[k] = lax.ppermute(packed[k], ('blk', 'head'), pairs)  6.28 us
    pallas_call x4, Pallas kernels, contract(): pl.pallas_call(functools.partial(contract_kernel, part * columns), grid=(...  5 us
  transfers between devices with their start and end apart: 56, of which 29 were waited for; matrix products, arithmetic and copies ran while one was open for 1% of the time, Pallas kernels for 19%

profile of v12, /device:TPU:0, one launch (start us, length us, event | category | flops | bytes accessed | tf_op | source)
XLA Modules:
  0.0 136.2 jit_solution(3789780778321969543)
XLA Ops:
  1.5 8.2 %attend.2 = (s32[60]{0:T(128)S(1)}, bf16[32,2048]{1,0:T(8,128)(2,1)S(1)}, bf16[32,2048]{1,0:T(8,128)(2,1)S(1)}, bf16[32,2048]{1,0:T(8,128)(2,1)S(1)}, bf16[128,5...) custom-call(s32[26]{0:T(128)S(1)} %concatenate.24.refs_0_, ...), custom_call_target="tpu_custom_call" | custom-call | flops 713031680 | bytes 4456448 | tf_op jit(solution)/shard_map/attend/pallas_call | solution.py:344
  9.7 3.1 %collective-permute-start.11 = (bf16[32,2048]{1,0:T(8,128)(2,1)S(1)}, bf16[32,2048]{1,0:T(8,128)(2,1)S(1)}, u32[]{:S(2)}, u32[]{:S(2)}) collective-permute-start(bf16[32,2048]{1,0:T(8,128)(2,1)S(1)} %get-tuple-element.162), channel_id=1, source_target_pairs={{0,4},{4,8},{8,12},{12,14},{14,10},{10,6},{6,2},{2,0},{1,5},{5,9},... | collective-permute-start | bytes 393224 | tf_op jit(solution)/shard_map/ppermute | solution.py:795
  13.4 2.0 %collective-permute-start.1 = (bf16[64,896]{1,0:T(8,128)(2,1)S(1)}, bf16[64,896]{1,0:T(8,128)(2,1)S(1)}, u32[]{:S(2)}, u32[]{:S(2)}) collective-permute-start(bf16[64,896]{1,0:T(8,128)(2,1)S(1)} %get-tuple-element.141), channel_id=1, source_target_pairs={{0,4},{1,13},{2,6},{3,15},{4,8},{5,1},{6,10},{7,3},{8,12},{9,5},{1... | collective-permute-start | bytes 344072 | tf_op jit(solution)/shard_map/ppermute | solution.py:822
  15.4 3.6 %collective-permute-start.2 = (bf16[64,896]{1,0:T(8,128)(2,1)S(1)}, bf16[64,896]{1,0:T(8,128)(2,1)S(1)}, u32[]{:S(2)}, u32[]{:S(2)}) collective-permute-start(bf16[64,896]{1,0:T(8,128)(2,1)S(1)} %get-tuple-element.142), channel_id=1, source_target_pairs={{0,6},{1,15},{2,8},{3,1},{4,10},{5,3},{6,12},{7,5},{8,14},{9,7},{1... | collective-permute-start | bytes 344072 | tf_op jit(solution)/shard_map/ppermute | solution.py:822
  20.1 5.9 %attend.3 = (bf16[32,2048]{1,0:T(8,128)(2,1)S(1)}, bf16[32,2048]{1,0:T(8,128)(2,1)S(1)}, bf16[32,2048]{1,0:T(8,128)(2,1)S(1)}) custom-call(s32[60]{0:T(128)S(1)} %get-tuple-element.137.tab.refs_0_, bf16[64,18432]{1,0:T(8,128)(2,1)} %refs_1_.3, bf16[8,576,256]{2,1,0:T(8,128)(2,1)} %refs_2_.3, bf16[64,576]{1,0:T(8,128)(2,1)} %bitcast.33, ...), custom_call_target="tpu_custom_call" | custom-call | flops 713031680 | bytes 4456448 | tf_op jit(solution)/shard_map/attend/pallas_call | solution.py:344
  27.3 1.6 %collective-permute-start.3 = (bf16[32,2048]{1,0:T(8,128)(2,1)S(1)}, bf16[32,2048]{1,0:T(8,128)(2,1)S(1)}, u32[]{:S(2)}, u32[]{:S(2)}) collective-permute-start(bf16[32,2048]{1,0:T(8,128)(2,1)S(1)} %get-tuple-element.150), channel_id=1, source_target_pairs={{0,4},{4,8},{8,12},{12,14},{14,10},{10,6},{6,2},{2,0},{1,5},{5,9},... | collective-permute-start | bytes 393224 | tf_op jit(solution)/shard_map/ppermute | solution.py:795
  28.9 1.6 %collective-permute-start.13 = (bf16[32,2048]{1,0:T(8,128)(2,1)S(1)}, bf16[32,2048]{1,0:T(8,128)(2,1)S(1)}, u32[]{:S(2)}, u32[]{:S(2)}) collective-permute-start(bf16[32,2048]{1,0:T(8,128)(2,1)S(1)} %broadcast_select_fusion.5), channel_id=1, source_target_pairs={{0,4},{4,8},{8,12},{12,14},{14,10},{10,6},{6,2},{2,0},{1,5},{5,9},... | collective-permute-start | bytes 393224 | tf_op jit(solution)/shard_map/ppermute | solution.py:795
  31.0 2.3 %collective-permute-done.3.refs_1_ = bf16[32,2048]{1,0:T(8,128)(2,1)S(1)} collective-permute-done((bf16[32,2048]{1,0:T(8,128)(2,1)S(1)}, bf16[32,2048]{1,0:T(8,128)(2,1)S(1)}, u32[]{:S(2)}, u32[]{:S(2)}) %collective-permute-start.3) | collective-permute-done | bytes 131104 | tf_op jit(solution)/shard_map/ppermute | solution.py:795
  33.5 2.6 %collective-permute-start.6 = (bf16[32,2048]{1,0:T(8,128)(2,1)S(1)}, bf16[32,2048]{1,0:T(8,128)(2,1)S(1)}, u32[]{:S(2)}, u32[]{:S(2)}) collective-permute-start(bf16[32,2048]{1,0:T(8,128)(2,1)S(1)} %broadcast_select_fusion.10), channel_id=1, source_target_pairs={{4,0},{8,4},{12,8},{14,12},{10,14},{6,10},{2,6},{0,2},{5,1},{9,5},... | collective-permute-start | bytes 393224 | tf_op jit(solution)/shard_map/ppermute | solution.py:798
  37.5 1.8 %collective-permute-start.17 = (bf16[32,2048]{1,0:T(8,128)(2,1)S(1)}, bf16[32,2048]{1,0:T(8,128)(2,1)S(1)}, u32[]{:S(2)}, u32[]{:S(2)}) collective-permute-start(bf16[32,2048]{1,0:T(8,128)(2,1)S(1)} %broadcast_select_fusion.2), channel_id=1, source_target_pairs={{4,0},{8,4},{12,8},{14,12},{10,14},{6,10},{2,6},{0,2},{5,1},{9,5},... | collective-permute-start | bytes 393224 | tf_op jit(solution)/shard_map/ppermute | solution.py:798
  40.2 1.2 collective-permute-done.5.refs_2_
  41.4 1.2 collective-permute-start.8
  42.5 0.9 collective-permute-start.7
  43.9 1.0 collective-permute-done.16.refs_3_
  44.9 0.9 collective-permute-start.18
  45.8 1.2 collective-permute-start.19
  47.0 1.6 %collective-permute-done.7.refs_3_ = bf16[32,2048]{1,0:T(8,128)(2,1)S(1)} collective-permute-done((bf16[32,2048]{1,0:T(8,128)(2,1)S(1)}, bf16[32,2048]{1,0:T(8,128)(2,1)S(1)}, u32[]{:S(2)}, u32[]{:S(2)}) %collective-permute-start.7) | collective-permute-done | bytes 131104 | tf_op jit(solution)/shard_map/ppermute | solution.py:795
  48.7 1.5 %collective-permute-start.10 = (bf16[32,2048]{1,0:T(8,128)(2,1)S(1)}, bf16[32,2048]{1,0:T(8,128)(2,1)S(1)}, u32[]{:S(2)}, u32[]{:S(2)}) collective-permute-start(bf16[32,2048]{1,0:T(8,128)(2,1)S(1)} %broadcast_select_fusion.6), channel_id=1, source_target_pairs={{4,0},{8,4},{12,8},{14,12},{10,14},{6,10},{2,6},{0,2},{5,1},{9,5},... | collective-permute-start | bytes 393224 | tf_op jit(solution)/shard_map/ppermute | solution.py:798
  52.1 1.9 %project.2.refs_10_ = f32[288,896]{1,0:T(8,128)S(1)} custom-call(s32[60]{0:T(128)S(1)} %get-tuple-element.137.tab.refs_0_, bf16[32,2048]{1,0:T(8,128)(2,1)S(1)} %get-tuple-element.180.refs_0_, bf16[32,2048]{1,0:T(8,128)(2,1)S(1)} %collective-permute-done.11.refs_1_, bf16[32,2048]{1,0:T(8,128)(2,1)S(1)} %collective-permute-done.13.refs_2_, ...), custom_call_target="tpu_custom_call" | custom-call | flops 1056964608 | bytes 4849664 | tf_op jit(solution)/shard_map/project/pallas_call | solution.py:489
  54.1 1.1 collective-permute-done.9.refs_4_
  55.2 2.0 %project.3 = (f32[144,896]{1,0:T(8,128)S(1)}, bf16[144,896]{1,0:T(8,128)(2,1)S(1)}) custom-call(s32[60]{0:T(128)S(1)} %get-tuple-element.137.tab.refs_0_, bf16[32,2048]{1,0:T(8,128)(2,1)S(1)} %get-tuple-element.153.refs_0_, bf16[32,2048]{1,0:T(8,128)(2,1)S(1)} %collective-permute-done.3.refs_1_, bf16[32,2048]{1,0:T(8,128)(2,1)S(1)} %collective-permute-done.5.refs_2_, ...), custom_call_target="tpu_custom_call" | custom-call | flops 1056964608 | bytes 4849664 | tf_op jit(solution)/shard_map/project/pallas_call | solution.py:499
  57.9 0.9 collective-permute-done.21
  59.7 1.5 %collective-permute-start.23 = (bf16[144,896]{1,0:T(8,128)(2,1)S(1)}, bf16[144,896]{1,0:T(8,128)(2,1)S(1)}, u32[]{:S(2)}, u32[]{:S(2)}) collective-permute-start(bf16[144,896]{1,0:T(8,128)(2,1)S(1)} %add_convert_fusion.refs_0_.refs_1_), channel_id=1, source_target_pairs={{4,0},{8,4},{12,8},{14,12},{10,14},{6,10},{2,6},{0,2},{5,1},{9,5},... | collective-permute-start | bytes 774152 | tf_op jit(solution)/shard_map/ppermute | solution.py:798
  61.3 1.7 %expand.5 = (f32[288,576]{1,0:T(8,128)S(1)}, f32[288,576]{1,0:T(8,128)S(1)}, f32[288,1]{1,0:T(8,128)S(1)}) custom-call(s32[60]{0:T(128)S(1)} %get-tuple-element.137.tab.refs_0_, bf16[144,896]{1,0:T(8,128)(2,1)S(1)} %add_convert_fusion.refs_0_.refs_1_, bf16[144,896]{1,0:T(8,128)(2,1)S(1)} %collective-permute-done.24.refs_1_, f32[8,1,896]{2,1,0:T(1,128)S(1)} %bitcast.27, ...), custom_call_target="tpu_custom_call" | custom-call | flops 1 | bytes 1 | tf_op jit(solution)/shard_map/expand/pallas_call | solution.py:651
  62.9 4.6 %collective-permute-done.22.refs_0_.refs_2_.refs_3_ = bf16[144,896]{1,0:T(8,128)(2,1)S(1)} collective-permute-done((bf16[144,896]{1,0:T(8,128)(2,1)S(1)}, bf16[144,896]{1,0:T(8,128)(2,1)S(1)}, u32[]{:S(2)}, u32[]{:S(2)}) %collective-permute-start.22) | collective-permute-done | bytes 258080 | tf_op jit(solution)/shard_map/ppermute | solution.py:795
  68.0 1.7 %collective-permute-start.25 = (bf16[144,896]{1,0:T(8,128)(2,1)S(1)}, bf16[144,896]{1,0:T(8,128)(2,1)S(1)}, u32[]{:S(2)}, u32[]{:S(2)}) collective-permute-start(bf16[144,896]{1,0:T(8,128)(2,1)S(1)} %collective-permute-done.22.refs_0_.refs_2_.refs_3_), channel_id=1, source_target_pairs={{0,4},{4,8},{8,12},{12,14},{14,10},{10,6},{6,2},{2,0},{1,5},{5,9},... | collective-permute-start | bytes 774152 | tf_op jit(solution)/shard_map/ppermute | solution.py:795
  70.1 2.9 %expand.6 = (f32[288,576]{1,0:T(8,128)S(1)}, f32[288,576]{1,0:T(8,128)S(1)}, f32[288,1]{1,0:T(8,128)S(1)}) custom-call(s32[60]{0:T(128)S(1)} %get-tuple-element.137.tab.refs_0_, bf16[144,896]{1,0:T(8,128)(2,1)S(1)} %collective-permute-done.22.refs_0_.refs_2_.refs_3_, bf16[144,896]{1,0:T(8,128)(2,1)S(1)} %collective-permute-done.23.refs_1_.refs_4_.refs_5_, ...), custom_call_target="tpu_custom_call" | custom-call | flops 1 | bytes 1 | tf_op jit(solution)/shard_map/expand/pallas_call | solution.py:651
  72.9 3.7 %collective-permute-done.25.refs_0_.refs_6_.refs_7_ = bf16[144,896]{1,0:T(8,128)(2,1)S(1)} collective-permute-done((bf16[144,896]{1,0:T(8,128)(2,1)S(1)}, bf16[144,896]{1,0:T(8,128)(2,1)S(1)}, u32[]{:S(2)}, u32[]{:S(2)}) %collective-permute-start.25) | collective-permute-done | bytes 258080 | tf_op jit(solution)/shard_map/ppermute | solution.py:795
  76.6 1.4 %collective-permute-done.26.refs_1_.refs_8_.refs_9_ = bf16[144,896]{1,0:T(8,128)(2,1)S(1)} collective-permute-done((bf16[144,896]{1,0:T(8,128)(2,1)S(1)}, bf16[144,896]{1,0:T(8,128)(2,1)S(1)}, u32[]{:S(2)}, u32[]{:S(2)}) %collective-permute-start.26) | collective-permute-done | bytes 258080 | tf_op jit(solution)/shard_map/ppermute | solution.py:798
  78.1 0.9 collective-permute-start.28
  79.1 1.1 collective-permute-start.29
  80.2 2.9 %expand.7 = (f32[288,576]{1,0:T(8,128)S(1)}, f32[288,576]{1,0:T(8,128)S(1)}, f32[288,1]{1,0:T(8,128)S(1)}) custom-call(s32[60]{0:T(128)S(1)} %get-tuple-element.137.tab.refs_0_, bf16[144,896]{1,0:T(8,128)(2,1)S(1)} %collective-permute-done.25.refs_0_.refs_6_.refs_7_, bf16[144,896]{1,0:T(8,128)(2,1)S(1)} %collective-permute-done.26.refs_1_.refs_8_.refs_9_, ...), custom_call_target="tpu_custom_call" | custom-call | flops 1 | bytes 1 | tf_op jit(solution)/shard_map/expand/pallas_call | solution.py:651
  83.1 3.7 %collective-permute-done.28.refs_0_.refs_10_.refs_11_ = bf16[144,896]{1,0:T(8,128)(2,1)S(1)} collective-permute-done((bf16[144,896]{1,0:T(8,128)(2,1)S(1)}, bf16[144,896]{1,0:T(8,128)(2,1)S(1)}, u32[]{:S(2)}, u32[]{:S(2)}) %collective-permute-start.28) | collective-permute-done | bytes 258080 | tf_op jit(solution)/shard_map/ppermute | solution.py:795
  87.5 1.2 collective-permute-start.31
  88.7 0.9 collective-permute-start.32
  89.7 2.9 %expand.8 = (f32[288,576]{1,0:T(8,128)S(1)}, f32[288,576]{1,0:T(8,128)S(1)}, f32[288,1]{1,0:T(8,128)S(1)}) custom-call(s32[60]{0:T(128)S(1)} %get-tuple-element.137.tab.refs_0_, bf16[144,896]{1,0:T(8,128)(2,1)S(1)} %collective-permute-done.28.refs_0_.refs_10_.refs_11_, bf16[144,896]{1,0:T(8,128)(2,1)S(1)} %collective-permute-done.29.refs_1_.refs_12_.refs_13_, ...), custom_call_target="tpu_custom_call" | custom-call | flops 1 | bytes 1 | tf_op jit(solution)/shard_map/expand/pallas_call | solution.py:651
  92.5 1.5 %collective-permute-done.32.refs_1_ = bf16[64,896]{1,0:T(8,128)(2,1)S(1)} collective-permute-done((bf16[64,896]{1,0:T(8,128)(2,1)S(1)}, bf16[64,896]{1,0:T(8,128)(2,1)S(1)}, u32[]{:S(2)}, u32[]{:S(2)}) %collective-permute-start.32) | collective-permute-done | bytes 114720 | tf_op jit(solution)/shard_map/ppermute | solution.py:798
  94.6 1.0 collective-permute-done.35.refs_3_
  95.7 1.8 %expand.9.hidden = bf16[288,576]{1,0:T(8,128)(2,1)S(1)} custom-call(s32[60]{0:T(128)S(1)} %get-tuple-element.137.tab.refs_0_, bf16[80,896]{1,0:T(8,128)(2,1)S(1)} %collective-permute-done.31.refs_0_, bf16[64,896]{1,0:T(8,128)(2,1)S(1)} %collective-permute-done.32.refs_1_, bf16[80,896]{1,0:T(8,128)(2,1)S(1)} %collective-permute-done.34.refs_2_, ...), custom_call_target="tpu_custom_call" | custom-call | flops 1 | bytes 1 | tf_op jit(solution)/shard_map/expand/pallas_call | solution.py:651
  97.5 1.3 contract.7
  99.1 1.2 contract.6
  100.6 1.2 contract.4.mine
  101.9 1.3 contract.5.mine
  103.2 0.8 pick.3
  104.1 0.9 collective-permute-start.48
  105.6 1.4 %collective-permute-start.47 = (bf16[16,3584]{1,0:T(8,128)(2,1)S(1)}, bf16[16,3584]{1,0:T(8,128)(2,1)S(1)}, u32[]{:S(2)}, u32[]{:S(2)}) collective-permute-start(bf16[16,3584]{1,0:T(8,128)(2,1)S(1)} %convert_element_type.156), channel_id=1, source_target_pairs={{0,4},{4,8},{8,12},{12,14},{14,10},{10,6},{6,2},{2,0},{1,5},{5,9},... | collective-permute-start | bytes 344072 | tf_op jit(solution)/shard_map/ppermute | solution.py:795
  107.9 0.9 collective-permute-start.38
  108.8 1.2 collective-permute-start.37
  110.0 1.0 collective-permute-done.47
  111.1 1.2 collective-permute-start.50
  112.3 0.9 collective-permute-start.49
  113.6 1.5 %collective-permute-start.39 = (bf16[16,3584]{1,0:T(8,128)(2,1)S(1)}, bf16[16,3584]{1,0:T(8,128)(2,1)S(1)}, u32[]{:S(2)}, u32[]{:S(2)}) collective-permute-start(bf16[16,3584]{1,0:T(8,128)(2,1)S(1)} %add_convert_fusion.12), channel_id=1, source_target_pairs={{0,4},{4,8},{8,12},{12,14},{14,10},{10,6},{6,2},{2,0},{1,5},{5,9},... | collective-permute-start | bytes 344072 | tf_op jit(solution)/shard_map/ppermute | solution.py:795
  116.0 1.5 %collective-permute-done.49 = bf16[16,3584]{1,0:T(8,128)(2,1)S(1)} collective-permute-done((bf16[16,3584]{1,0:T(8,128)(2,1)S(1)}, bf16[16,3584]{1,0:T(8,128)(2,1)S(1)}, u32[]{:S(2)}, u32[]{:S(2)}) %collective-permute-start.49) | collective-permute-done | bytes 114720 | tf_op jit(solution)/shard_map/ppermute | solution.py:795
  117.5 1.2 collective-permute-start.52
  118.7 0.9 collective-permute-start.51
  120.5 1.0 collective-permute-start.42
  121.4 1.4 %collective-permute-start.41 = (bf16[16,3584]{1,0:T(8,128)(2,1)S(1)}, bf16[16,3584]{1,0:T(8,128)(2,1)S(1)}, u32[]{:S(2)}, u32[]{:S(2)}) collective-permute-start(bf16[16,3584]{1,0:T(8,128)(2,1)S(1)} %add_convert_fusion.10), channel_id=1, source_target_pairs={{0,4},{4,8},{8,12},{12,14},{14,10},{10,6},{6,2},{2,0},{1,5},{5,9},... | collective-permute-start | bytes 344072 | tf_op jit(solution)/shard_map/ppermute | solution.py:795
  122.8 1.5 %collective-permute-done.51 = bf16[16,3584]{1,0:T(8,128)(2,1)S(1)} collective-permute-done((bf16[16,3584]{1,0:T(8,128)(2,1)S(1)}, bf16[16,3584]{1,0:T(8,128)(2,1)S(1)}, u32[]{:S(2)}, u32[]{:S(2)}) %collective-permute-start.51) | collective-permute-done | bytes 114720 | tf_op jit(solution)/shard_map/ppermute | solution.py:795
  124.9 1.5 %collective-permute-start.54 = (bf16[16,3584]{1,0:T(8,128)(2,1)S(1)}, bf16[16,3584]{1,0:T(8,128)(2,1)S(1)}, u32[]{:S(2)}, u32[]{:S(2)}) collective-permute-start(bf16[16,3584]{1,0:T(8,128)(2,1)S(1)} %add_convert_fusion.1), channel_id=1, source_target_pairs={{4,0},{8,4},{12,8},{14,12},{10,14},{6,10},{2,6},{0,2},{5,1},{9,5},... | collective-permute-start | bytes 344072 | tf_op jit(solution)/shard_map/ppermute | solution.py:798
  126.5 0.9 collective-permute-done.41
  128.2 1.4 collective-permute-start.44
  130.2 2.1 %collective-permute-done.43 = bf16[16,3584]{1,0:T(8,128)(2,1)S(1)} collective-permute-done((bf16[16,3584]{1,0:T(8,128)(2,1)S(1)}, bf16[16,3584]{1,0:T(8,128)(2,1)S(1)}, u32[]{:S(2)}, u32[]{:S(2)}) %collective-permute-start.43) | collective-permute-done | bytes 114720 | tf_op jit(solution)/shard_map/ppermute | solution.py:795
  132.3 1.0 collective-permute-done.44
  135.3 0.9 maximum_select_fusion
  (133 shorter events, 20.2 us)
Async XLA Ops:
  0.0 12.8 %copy-start = (bf16[64,7168]{1,0:T(8,128)(2,1)S(1)}, bf16[64,7168]{1,0:T(8,128)(2,1)}, u32[]{:S(2)}) copy-start(bf16[64,7168]{1,0:T(8,128)(2,1)} %res.1) | copy-start | bytes 2752516
  9.7 19.2 %collective-permute-start.11 = (bf16[32,2048]{1,0:T(8,128)(2,1)S(1)}, bf16[32,2048]{1,0:T(8,128)(2,1)S(1)}, u32[]{:S(2)}, u32[]{:S(2)}) collective-permute-start(bf16[32,2048]{1,0:T(8,128)(2,1)S(1)} %get-tuple-element.162), channel_id=1, source_target_pairs={{0,4},{4,8},{8,12},{12,14},{14,10},{10,6},{6,2},{2,0},{1,5},{5,9},... | collective-permute-start | bytes 393224 | tf_op jit(solution)/shard_map/ppermute | solution.py:795
  13.4 38.7 %slice-start.6 = ((s8[7340032]{0:T(1024)(128)(4,1)}), s8[4194304]{0:T(1024)(128)(4,1)S(1)}, s32[]{:S(2)}) async-start(s8[7340032]{0:T(1024)(128)(4,1)} %bitcast.25), calls=%async_computation.6 | async-start | bytes 8388608
  13.4 12.7 %collective-permute-start = (bf16[64,896]{1,0:T(8,128)(2,1)S(1)}, bf16[64,896]{1,0:T(8,128)(2,1)S(1)}, u32[]{:S(2)}, u32[]{:S(2)}) collective-permute-start(bf16[64,896]{1,0:T(8,128)(2,1)S(1)} %get-tuple-element.140), channel_id=1, source_target_pairs={{0,2},{1,11},{2,4},{3,13},{4,6},{5,15},{6,8},{7,1},{8,10},{9,3},{1... | collective-permute-start | bytes 344072 | tf_op jit(solution)/shard_map/ppermute | solution.py:822
  13.4 12.6 %collective-permute-start.1 = (bf16[64,896]{1,0:T(8,128)(2,1)S(1)}, bf16[64,896]{1,0:T(8,128)(2,1)S(1)}, u32[]{:S(2)}, u32[]{:S(2)}) collective-permute-start(bf16[64,896]{1,0:T(8,128)(2,1)S(1)} %get-tuple-element.141), channel_id=1, source_target_pairs={{0,4},{1,13},{2,6},{3,15},{4,8},{5,1},{6,10},{7,3},{8,12},{9,5},{1... | collective-permute-start | bytes 344072 | tf_op jit(solution)/shard_map/ppermute | solution.py:822
  15.4 10.7 %collective-permute-start.2 = (bf16[64,896]{1,0:T(8,128)(2,1)S(1)}, bf16[64,896]{1,0:T(8,128)(2,1)S(1)}, u32[]{:S(2)}, u32[]{:S(2)}) collective-permute-start(bf16[64,896]{1,0:T(8,128)(2,1)S(1)} %get-tuple-element.142), channel_id=1, source_target_pairs={{0,6},{1,15},{2,8},{3,1},{4,10},{5,3},{6,12},{7,5},{8,14},{9,7},{1... | collective-permute-start | bytes 344072 | tf_op jit(solution)/shard_map/ppermute | solution.py:822
  19.0 9.9 %collective-permute-start.12 = (bf16[32,2048]{1,0:T(8,128)(2,1)S(1)}, bf16[32,2048]{1,0:T(8,128)(2,1)S(1)}, u32[]{:S(2)}, u32[]{:S(2)}) collective-permute-start(bf16[32,2048]{1,0:T(8,128)(2,1)S(1)} %get-tuple-element.180.refs_0_), channel_id=1, source_target_pairs={{4,0},{8,4},{12,8},{14,12},{10,14},{6,10},{2,6},{0,2},{5,1},{9,5},... | collective-permute-start | bytes 393224 | tf_op jit(solution)/shard_map/ppermute | solution.py:798
  20.1 32.0 %slice-start.7 = ((s8[7340032]{0:T(1024)(128)(4,1)}), s8[3145728]{0:T(1024)(128)(4,1)S(1)}, s32[]{:S(2)}) async-start(s8[7340032]{0:T(1024)(128)(4,1)} %bitcast.25), calls=%async_computation.7 | async-start | bytes 6291456
  26.1 10.0 %collective-permute-start.14 = (bf16[64,896]{1,0:T(8,128)(2,1)S(1)}, bf16[64,896]{1,0:T(8,128)(2,1)S(1)}, u32[]{:S(2)}, u32[]{:S(2)}) collective-permute-start(bf16[64,896]{1,0:T(8,128)(2,1)S(1)} %get-tuple-element.166.own), channel_id=1, source_target_pairs={{1,9},{3,11},{5,13},{7,15},{9,1},{11,3},{13,5},{15,7},{17,25},{19,... | collective-permute-start | bytes 344072 | tf_op jit(solution)/shard_map/ppermute | solution.py:822
  26.8 6.7 %collective-permute-start.4 = (bf16[32,2048]{1,0:T(8,128)(2,1)S(1)}, bf16[32,2048]{1,0:T(8,128)(2,1)S(1)}, u32[]{:S(2)}, u32[]{:S(2)}) collective-permute-start(bf16[32,2048]{1,0:T(8,128)(2,1)S(1)} %get-tuple-element.153.refs_0_), channel_id=1, source_target_pairs={{4,0},{8,4},{12,8},{14,12},{10,14},{6,10},{2,6},{0,2},{5,1},{9,5},... | collective-permute-start | bytes 393224 | tf_op jit(solution)/shard_map/ppermute | solution.py:798
  27.3 6.0 %collective-permute-start.3 = (bf16[32,2048]{1,0:T(8,128)(2,1)S(1)}, bf16[32,2048]{1,0:T(8,128)(2,1)S(1)}, u32[]{:S(2)}, u32[]{:S(2)}) collective-permute-start(bf16[32,2048]{1,0:T(8,128)(2,1)S(1)} %get-tuple-element.150), channel_id=1, source_target_pairs={{0,4},{4,8},{8,12},{12,14},{14,10},{10,6},{6,2},{2,0},{1,5},{5,9},... | collective-permute-start | bytes 393224 | tf_op jit(solution)/shard_map/ppermute | solution.py:795
  28.9 7.2 %collective-permute-start.13 = (bf16[32,2048]{1,0:T(8,128)(2,1)S(1)}, bf16[32,2048]{1,0:T(8,128)(2,1)S(1)}, u32[]{:S(2)}, u32[]{:S(2)}) collective-permute-start(bf16[32,2048]{1,0:T(8,128)(2,1)S(1)} %broadcast_select_fusion.5), channel_id=1, source_target_pairs={{0,4},{4,8},{8,12},{12,14},{14,10},{10,6},{6,2},{2,0},{1,5},{5,9},... | collective-permute-start | bytes 393224 | tf_op jit(solution)/shard_map/ppermute | solution.py:795
  30.5 7.0 %collective-permute-start.15 = (bf16[32,2048]{1,0:T(8,128)(2,1)S(1)}, bf16[32,2048]{1,0:T(8,128)(2,1)S(1)}, u32[]{:S(2)}, u32[]{:S(2)}) collective-permute-start(bf16[32,2048]{1,0:T(8,128)(2,1)S(1)} %broadcast_select_fusion.4), channel_id=1, source_target_pairs={{4,0},{8,4},{12,8},{14,12},{10,14},{6,10},{2,6},{0,2},{5,1},{9,5},... | collective-permute-start | bytes 393224 | tf_op jit(solution)/shard_map/ppermute | solution.py:798
  33.5 6.6 %collective-permute-start.6 = (bf16[32,2048]{1,0:T(8,128)(2,1)S(1)}, bf16[32,2048]{1,0:T(8,128)(2,1)S(1)}, u32[]{:S(2)}, u32[]{:S(2)}) collective-permute-start(bf16[32,2048]{1,0:T(8,128)(2,1)S(1)} %broadcast_select_fusion.10), channel_id=1, source_target_pairs={{4,0},{8,4},{12,8},{14,12},{10,14},{6,10},{2,6},{0,2},{5,1},{9,5},... | collective-permute-start | bytes 393224 | tf_op jit(solution)/shard_map/ppermute | solution.py:798
  36.1 5.3 %collective-permute-start.5 = (bf16[32,2048]{1,0:T(8,128)(2,1)S(1)}, bf16[32,2048]{1,0:T(8,128)(2,1)S(1)}, u32[]{:S(2)}, u32[]{:S(2)}) collective-permute-start(bf16[32,2048]{1,0:T(8,128)(2,1)S(1)} %broadcast_select_fusion.11), channel_id=1, source_target_pairs={{0,4},{4,8},{8,12},{12,14},{14,10},{10,6},{6,2},{2,0},{1,5},{5,9},... | collective-permute-start | bytes 393224 | tf_op jit(solution)/shard_map/ppermute | solution.py:795
  36.7 14.1 %collective-permute-start.20 = (bf16[128,896]{1,0:T(8,128)(2,1)S(1)}, bf16[128,896]{1,0:T(8,128)(2,1)S(1)}, u32[]{:S(2)}, u32[]{:S(2)}) collective-permute-start(bf16[128,896]{1,0:T(8,128)(2,1)S(1)} %share.1), channel_id=1, source_target_pairs={{0,1},{1,0},{2,3},{3,2},{4,5},{5,4},{6,7},{7,6},{8,9},{9,8},{10,11... | collective-permute-start | bytes 688136 | tf_op jit(solution)/shard_map/ppermute | solution.py:801
  37.5 6.4 %collective-permute-start.17 = (bf16[32,2048]{1,0:T(8,128)(2,1)S(1)}, bf16[32,2048]{1,0:T(8,128)(2,1)S(1)}, u32[]{:S(2)}, u32[]{:S(2)}) collective-permute-start(bf16[32,2048]{1,0:T(8,128)(2,1)S(1)} %broadcast_select_fusion.2), channel_id=1, source_target_pairs={{4,0},{8,4},{12,8},{14,12},{10,14},{6,10},{2,6},{0,2},{5,1},{9,5},... | collective-permute-start | bytes 393224 | tf_op jit(solution)/shard_map/ppermute | solution.py:798
  39.3 5.6 %collective-permute-start.16 = (bf16[32,2048]{1,0:T(8,128)(2,1)S(1)}, bf16[32,2048]{1,0:T(8,128)(2,1)S(1)}, u32[]{:S(2)}, u32[]{:S(2)}) collective-permute-start(bf16[32,2048]{1,0:T(8,128)(2,1)S(1)} %broadcast_select_fusion.3), channel_id=1, source_target_pairs={{0,4},{4,8},{8,12},{12,14},{14,10},{10,6},{6,2},{2,0},{1,5},{5,9},... | collective-permute-start | bytes 393224 | tf_op jit(solution)/shard_map/ppermute | solution.py:795
  41.4 5.6 %collective-permute-start.8 = (bf16[32,2048]{1,0:T(8,128)(2,1)S(1)}, bf16[32,2048]{1,0:T(8,128)(2,1)S(1)}, u32[]{:S(2)}, u32[]{:S(2)}) collective-permute-start(bf16[32,2048]{1,0:T(8,128)(2,1)S(1)} %broadcast_select_fusion.8), channel_id=1, source_target_pairs={{4,0},{8,4},{12,8},{14,12},{10,14},{6,10},{2,6},{0,2},{5,1},{9,5},... | collective-permute-start | bytes 393224 | tf_op jit(solution)/shard_map/ppermute | solution.py:798
  42.5 6.1 %collective-permute-start.7 = (bf16[32,2048]{1,0:T(8,128)(2,1)S(1)}, bf16[32,2048]{1,0:T(8,128)(2,1)S(1)}, u32[]{:S(2)}, u32[]{:S(2)}) collective-permute-start(bf16[32,2048]{1,0:T(8,128)(2,1)S(1)} %broadcast_select_fusion.9), channel_id=1, source_target_pairs={{0,4},{4,8},{8,12},{12,14},{14,10},{10,6},{6,2},{2,0},{1,5},{5,9},... | collective-permute-start | bytes 393224 | tf_op jit(solution)/shard_map/ppermute | solution.py:795
  43.9 17.3 %slice-start.2 = ((s8[8257536]{0:T(1024)(128)(4,1)}), s8[4194304]{0:T(1024)(128)(4,1)S(1)}, s32[]{:S(2)}) async-start(s8[8257536]{0:T(1024)(128)(4,1)} %bitcast.16), calls=%async_computation.2 | async-start | bytes 8388608
  44.9 6.4 %collective-permute-start.18 = (bf16[32,2048]{1,0:T(8,128)(2,1)S(1)}, bf16[32,2048]{1,0:T(8,128)(2,1)S(1)}, u32[]{:S(2)}, u32[]{:S(2)}) collective-permute-start(bf16[32,2048]{1,0:T(8,128)(2,1)S(1)} %broadcast_select_fusion.1), channel_id=1, source_target_pairs={{0,4},{4,8},{8,12},{12,14},{14,10},{10,6},{6,2},{2,0},{1,5},{5,9},... | collective-permute-start | bytes 393224 | tf_op jit(solution)/shard_map/ppermute | solution.py:795
  45.8 6.3 %collective-permute-start.19 = (bf16[32,2048]{1,0:T(8,128)(2,1)S(1)}, bf16[32,2048]{1,0:T(8,128)(2,1)S(1)}, u32[]{:S(2)}, u32[]{:S(2)}) collective-permute-start(bf16[32,2048]{1,0:T(8,128)(2,1)S(1)} %broadcast_select_fusion), channel_id=1, source_target_pairs={{4,0},{8,4},{12,8},{14,12},{10,14},{6,10},{2,6},{0,2},{5,1},{9,5},... | collective-permute-start | bytes 393224 | tf_op jit(solution)/shard_map/ppermute | solution.py:798
  48.7 5.4 %collective-permute-start.10 = (bf16[32,2048]{1,0:T(8,128)(2,1)S(1)}, bf16[32,2048]{1,0:T(8,128)(2,1)S(1)}, u32[]{:S(2)}, u32[]{:S(2)}) collective-permute-start(bf16[32,2048]{1,0:T(8,128)(2,1)S(1)} %broadcast_select_fusion.6), channel_id=1, source_target_pairs={{4,0},{8,4},{12,8},{14,12},{10,14},{6,10},{2,6},{0,2},{5,1},{9,5},... | collective-permute-start | bytes 393224 | tf_op jit(solution)/shard_map/ppermute | solution.py:798
  50.2 5.0 %collective-permute-start.9 = (bf16[32,2048]{1,0:T(8,128)(2,1)S(1)}, bf16[32,2048]{1,0:T(8,128)(2,1)S(1)}, u32[]{:S(2)}, u32[]{:S(2)}) collective-permute-start(bf16[32,2048]{1,0:T(8,128)(2,1)S(1)} %broadcast_select_fusion.7), channel_id=1, source_target_pairs={{0,4},{4,8},{8,12},{12,14},{14,10},{10,6},{6,2},{2,0},{1,5},{5,9},... | collective-permute-start | bytes 393224 | tf_op jit(solution)/shard_map/ppermute | solution.py:795
  52.1 9.1 %slice-start = ((s8[8257536]{0:T(1024)(128)(4,1)}), s8[4194304]{0:T(1024)(128)(4,1)S(1)}, s32[]{:S(2)}) async-start(s8[8257536]{0:T(1024)(128)(4,1)} %bitcast.9), calls=%async_computation | async-start | bytes 8388608
  54.0 7.2 %slice-start.1 = ((s8[8257536]{0:T(1024)(128)(4,1)}), s8[4063232]{0:T(1024)(128)(4,1)S(1)}, s32[]{:S(2)}) async-start(s8[8257536]{0:T(1024)(128)(4,1)} %bitcast.9), calls=%async_computation.1 | async-start | bytes 8126464
  54.0 7.2 %slice-start.3 = ((s8[8257536]{0:T(1024)(128)(4,1)}), s8[4063232]{0:T(1024)(128)(4,1)S(1)}, s32[]{:S(2)}) async-start(s8[8257536]{0:T(1024)(128)(4,1)} %bitcast.16), calls=%async_computation.3 | async-start | bytes 8126464
  54.0 7.2 %copy-start.1 = (f32[7168]{0:T(1024)S(1)}, f32[7168]{0:T(1024)}, u32[]{:S(2)}) copy-start(f32[7168]{0:T(1024)} %param.24) | copy-start | bytes 86020
  57.2 1.6 %collective-permute-start.21 = (bf16[144,896]{1,0:T(8,128)(2,1)S(1)}, bf16[144,896]{1,0:T(8,128)(2,1)S(1)}, u32[]{:S(2)}, u32[]{:S(2)}) collective-permute-start(bf16[144,896]{1,0:T(8,128)(2,1)S(1)} %get-tuple-element.192), channel_id=1, source_target_pairs={{0,1},{1,0},{2,3},{3,2},{4,5},{5,4},{6,7},{7,6},{8,9},{9,8},{10,11... | collective-permute-start | bytes 774152 | tf_op jit(solution)/shard_map/ppermute | solution.py:801
  58.9 2.3 %collective-permute-start.24 = (bf16[144,896]{1,0:T(8,128)(2,1)S(1)}, bf16[144,896]{1,0:T(8,128)(2,1)S(1)}, u32[]{:S(2)}, u32[]{:S(2)}) collective-permute-start(bf16[144,896]{1,0:T(8,128)(2,1)S(1)} %add_convert_fusion.refs_0_.refs_1_), channel_id=1, source_target_pairs={{0,1},{1,0},{2,3},{3,2},{4,5},{5,4},{6,7},{7,6},{8,9},{9,8},{10,11... | collective-permute-start | bytes 774152 | tf_op jit(solution)/shard_map/ppermute | solution.py:801
  59.1 8.5 %collective-permute-start.22 = (bf16[144,896]{1,0:T(8,128)(2,1)S(1)}, bf16[144,896]{1,0:T(8,128)(2,1)S(1)}, u32[]{:S(2)}, u32[]{:S(2)}) collective-permute-start(bf16[144,896]{1,0:T(8,128)(2,1)S(1)} %add_convert_fusion.refs_0_.refs_1_), channel_id=1, source_target_pairs={{0,4},{4,8},{8,12},{12,14},{14,10},{10,6},{6,2},{2,0},{1,5},{5,9},... | collective-permute-start | bytes 774152 | tf_op jit(solution)/shard_map/ppermute | solution.py:795
  59.7 8.1 %collective-permute-start.23 = (bf16[144,896]{1,0:T(8,128)(2,1)S(1)}, bf16[144,896]{1,0:T(8,128)(2,1)S(1)}, u32[]{:S(2)}, u32[]{:S(2)}) collective-permute-start(bf16[144,896]{1,0:T(8,128)(2,1)S(1)} %add_convert_fusion.refs_0_.refs_1_), channel_id=1, source_target_pairs={{4,0},{8,4},{12,8},{14,12},{10,14},{6,10},{2,6},{0,2},{5,1},{9,5},... | collective-permute-start | bytes 774152 | tf_op jit(solution)/shard_map/ppermute | solution.py:798
  67.9 2.2 %collective-permute-start.27 = (bf16[288,896]{1,0:T(8,128)(2,1)S(1)}, bf16[288,896]{1,0:T(8,128)(2,1)S(1)}, u32[]{:S(2)}, u32[]{:S(2)}) collective-permute-start(bf16[288,896]{1,0:T(8,128)(2,1)S(1)} %pad_maximum_fusion), channel_id=1, source_target_pairs={{0,1},{1,0},{2,3},{3,2},{4,5},{5,4},{6,7},{7,6},{8,9},{9,8},{10,11... | collective-permute-start | bytes 1548296 | tf_op jit(solution)/shard_map/ppermute | solution.py:801
  68.0 8.6 %collective-permute-start.25 = (bf16[144,896]{1,0:T(8,128)(2,1)S(1)}, bf16[144,896]{1,0:T(8,128)(2,1)S(1)}, u32[]{:S(2)}, u32[]{:S(2)}) collective-permute-start(bf16[144,896]{1,0:T(8,128)(2,1)S(1)} %collective-permute-done.22.refs_0_.refs_2_.refs_3_), channel_id=1, source_target_pairs={{0,4},{4,8},{8,12},{12,14},{14,10},{10,6},{6,2},{2,0},{1,5},{5,9},... | collective-permute-start | bytes 774152 | tf_op jit(solution)/shard_map/ppermute | solution.py:795
  69.7 8.3 %collective-permute-start.26 = (bf16[144,896]{1,0:T(8,128)(2,1)S(1)}, bf16[144,896]{1,0:T(8,128)(2,1)S(1)}, u32[]{:S(2)}, u32[]{:S(2)}) collective-permute-start(bf16[144,896]{1,0:T(8,128)(2,1)S(1)} %collective-permute-done.23.refs_1_.refs_4_.refs_5_), channel_id=1, source_target_pairs={{4,0},{8,4},{12,8},{14,12},{10,14},{6,10},{2,6},{0,2},{5,1},{9,5},... | collective-permute-start | bytes 774152 | tf_op jit(solution)/shard_map/ppermute | solution.py:798
  78.0 2.2 %collective-permute-start.30 = (bf16[288,896]{1,0:T(8,128)(2,1)S(1)}, bf16[288,896]{1,0:T(8,128)(2,1)S(1)}, u32[]{:S(2)}, u32[]{:S(2)}) collective-permute-start(bf16[288,896]{1,0:T(8,128)(2,1)S(1)} %pad_maximum_fusion.1), channel_id=1, source_target_pairs={{0,1},{1,0},{2,3},{3,2},{4,5},{5,4},{6,7},{7,6},{8,9},{9,8},{10,11... | collective-permute-start | bytes 1548296 | tf_op jit(solution)/shard_map/ppermute | solution.py:801
  78.1 8.6 %collective-permute-start.28 = (bf16[144,896]{1,0:T(8,128)(2,1)S(1)}, bf16[144,896]{1,0:T(8,128)(2,1)S(1)}, u32[]{:S(2)}, u32[]{:S(2)}) collective-permute-start(bf16[144,896]{1,0:T(8,128)(2,1)S(1)} %collective-permute-done.25.refs_0_.refs_6_.refs_7_), channel_id=1, source_target_pairs={{0,4},{4,8},{8,12},{12,14},{14,10},{10,6},{6,2},{2,0},{1,5},{5,9},... | collective-permute-start | bytes 774152 | tf_op jit(solution)/shard_map/ppermute | solution.py:795
  79.1 8.3 %collective-permute-start.29 = (bf16[144,896]{1,0:T(8,128)(2,1)S(1)}, bf16[144,896]{1,0:T(8,128)(2,1)S(1)}, u32[]{:S(2)}, u32[]{:S(2)}) collective-permute-start(bf16[144,896]{1,0:T(8,128)(2,1)S(1)} %collective-permute-done.26.refs_1_.refs_8_.refs_9_), channel_id=1, source_target_pairs={{4,0},{8,4},{12,8},{14,12},{10,14},{6,10},{2,6},{0,2},{5,1},{9,5},... | collective-permute-start | bytes 774152 | tf_op jit(solution)/shard_map/ppermute | solution.py:798
  87.4 2.2 %collective-permute-start.33 = (bf16[288,896]{1,0:T(8,128)(2,1)S(1)}, bf16[288,896]{1,0:T(8,128)(2,1)S(1)}, u32[]{:S(2)}, u32[]{:S(2)}) collective-permute-start(bf16[288,896]{1,0:T(8,128)(2,1)S(1)} %pad_maximum_fusion.2), channel_id=1, source_target_pairs={{0,1},{1,0},{2,3},{3,2},{4,5},{5,4},{6,7},{7,6},{8,9},{9,8},{10,11... | collective-permute-start | bytes 1548296 | tf_op jit(solution)/shard_map/ppermute | solution.py:801
  87.5 6.6 %collective-permute-start.31 = (bf16[80,896]{1,0:T(8,128)(2,1)S(1)}, bf16[80,896]{1,0:T(8,128)(2,1)S(1)}, u32[]{:S(2)}, u32[]{:S(2)}) collective-permute-start(bf16[80,896]{1,0:T(8,128)(2,1)S(1)} %slice.18), channel_id=1, source_target_pairs={{0,4},{4,8},{8,12},{12,14},{14,10},{10,6},{6,2},{2,0},{1,5},{5,9},... | collective-permute-start | bytes 430088 | tf_op jit(solution)/shard_map/ppermute | solution.py:795
  88.7 5.3 %collective-permute-start.32 = (bf16[64,896]{1,0:T(8,128)(2,1)S(1)}, bf16[64,896]{1,0:T(8,128)(2,1)S(1)}, u32[]{:S(2)}, u32[]{:S(2)}) collective-permute-start(bf16[64,896]{1,0:T(8,128)(2,1)S(1)} %slice.19), channel_id=1, source_target_pairs={{4,0},{8,4},{12,8},{14,12},{10,14},{6,10},{2,6},{0,2},{5,1},{9,5},... | collective-permute-start | bytes 344072 | tf_op jit(solution)/shard_map/ppermute | solution.py:798
  94.1 1.6 %collective-permute-start.34 = (bf16[80,896]{1,0:T(8,128)(2,1)S(1)}, bf16[80,896]{1,0:T(8,128)(2,1)S(1)}, u32[]{:S(2)}, u32[]{:S(2)}) collective-permute-start(bf16[80,896]{1,0:T(8,128)(2,1)S(1)} %collective-permute-done.31.refs_0_), channel_id=1, source_target_pairs={{0,1},{1,0},{2,3},{3,2},{4,5},{5,4},{6,7},{7,6},{8,9},{9,8},{10,11... | collective-permute-start | bytes 430088 | tf_op jit(solution)/shard_map/ppermute | solution.py:801
  94.1 1.5 %collective-permute-start.35 = (bf16[64,896]{1,0:T(8,128)(2,1)S(1)}, bf16[64,896]{1,0:T(8,128)(2,1)S(1)}, u32[]{:S(2)}, u32[]{:S(2)}) collective-permute-start(bf16[64,896]{1,0:T(8,128)(2,1)S(1)} %collective-permute-done.32.refs_1_), channel_id=1, source_target_pairs={{0,1},{1,0},{2,3},{3,2},{4,5},{5,4},{6,7},{7,6},{8,9},{9,8},{10,11... | collective-permute-start | bytes 344072 | tf_op jit(solution)/shard_map/ppermute | solution.py:801
  98.8 4.4 %collective-permute-start.46 = (bf16[144,3584]{1,0:T(8,128)(2,1)S(1)}, bf16[144,3584]{1,0:T(8,128)(2,1)S(1)}, u32[]{:S(2)}, u32[]{:S(2)}) collective-permute-start(bf16[144,3584]{1,0:T(8,128)(2,1)S(1)} %contract.7), channel_id=1, source_target_pairs={{0,1},{1,0},{2,3},{3,2},{4,5},{5,4},{6,7},{7,6},{8,9},{9,8},{10,11... | collective-permute-start | bytes 3096584 | tf_op jit(solution)/shard_map/ppermute | solution.py:801
  100.4 6.7 %collective-permute-start.36 = (bf16[144,3584]{1,0:T(8,128)(2,1)S(1)}, bf16[144,3584]{1,0:T(8,128)(2,1)S(1)}, u32[]{:S(2)}, u32[]{:S(2)}) collective-permute-start(bf16[144,3584]{1,0:T(8,128)(2,1)S(1)} %contract.6), channel_id=1, source_target_pairs={{0,1},{1,0},{2,3},{3,2},{4,5},{5,4},{6,7},{7,6},{8,9},{9,8},{10,11... | collective-permute-start | bytes 3096584 | tf_op jit(solution)/shard_map/ppermute | solution.py:801
  104.1 5.9 %collective-permute-start.48 = (bf16[16,3584]{1,0:T(8,128)(2,1)S(1)}, bf16[16,3584]{1,0:T(8,128)(2,1)S(1)}, u32[]{:S(2)}, u32[]{:S(2)}) collective-permute-start(bf16[16,3584]{1,0:T(8,128)(2,1)S(1)} %convert_element_type.157), channel_id=1, source_target_pairs={{4,0},{8,4},{12,8},{14,12},{10,14},{6,10},{2,6},{0,2},{5,1},{9,5},... | collective-permute-start | bytes 344072 | tf_op jit(solution)/shard_map/ppermute | solution.py:798
  105.6 5.4 %collective-permute-start.47 = (bf16[16,3584]{1,0:T(8,128)(2,1)S(1)}, bf16[16,3584]{1,0:T(8,128)(2,1)S(1)}, u32[]{:S(2)}, u32[]{:S(2)}) collective-permute-start(bf16[16,3584]{1,0:T(8,128)(2,1)S(1)} %convert_element_type.156), channel_id=1, source_target_pairs={{0,4},{4,8},{8,12},{12,14},{14,10},{10,6},{6,2},{2,0},{1,5},{5,9},... | collective-permute-start | bytes 344072 | tf_op jit(solution)/shard_map/ppermute | solution.py:795
  107.9 5.3 %collective-permute-start.38 = (bf16[16,3584]{1,0:T(8,128)(2,1)S(1)}, bf16[16,3584]{1,0:T(8,128)(2,1)S(1)}, u32[]{:S(2)}, u32[]{:S(2)}) collective-permute-start(bf16[16,3584]{1,0:T(8,128)(2,1)S(1)} %convert_element_type.136), channel_id=1, source_target_pairs={{4,0},{8,4},{12,8},{14,12},{10,14},{6,10},{2,6},{0,2},{5,1},{9,5},... | collective-permute-start | bytes 344072 | tf_op jit(solution)/shard_map/ppermute | solution.py:798
  108.8 4.8 %collective-permute-start.37 = (bf16[16,3584]{1,0:T(8,128)(2,1)S(1)}, bf16[16,3584]{1,0:T(8,128)(2,1)S(1)}, u32[]{:S(2)}, u32[]{:S(2)}) collective-permute-start(bf16[16,3584]{1,0:T(8,128)(2,1)S(1)} %convert_element_type.135), channel_id=1, source_target_pairs={{0,4},{4,8},{8,12},{12,14},{14,10},{10,6},{6,2},{2,0},{1,5},{5,9},... | collective-permute-start | bytes 344072 | tf_op jit(solution)/shard_map/ppermute | solution.py:795
  111.1 4.8 %collective-permute-start.50 = (bf16[16,3584]{1,0:T(8,128)(2,1)S(1)}, bf16[16,3584]{1,0:T(8,128)(2,1)S(1)}, u32[]{:S(2)}, u32[]{:S(2)}) collective-permute-start(bf16[16,3584]{1,0:T(8,128)(2,1)S(1)} %add_convert_fusion.5), channel_id=1, source_target_pairs={{4,0},{8,4},{12,8},{14,12},{10,14},{6,10},{2,6},{0,2},{5,1},{9,5},... | collective-permute-start | bytes 344072 | tf_op jit(solution)/shard_map/ppermute | solution.py:798
  112.3 5.2 %collective-permute-start.49 = (bf16[16,3584]{1,0:T(8,128)(2,1)S(1)}, bf16[16,3584]{1,0:T(8,128)(2,1)S(1)}, u32[]{:S(2)}, u32[]{:S(2)}) collective-permute-start(bf16[16,3584]{1,0:T(8,128)(2,1)S(1)} %add_convert_fusion.6), channel_id=1, source_target_pairs={{0,4},{4,8},{8,12},{12,14},{14,10},{10,6},{6,2},{2,0},{1,5},{5,9},... | collective-permute-start | bytes 344072 | tf_op jit(solution)/shard_map/ppermute | solution.py:795
  113.6 6.7 %collective-permute-start.39 = (bf16[16,3584]{1,0:T(8,128)(2,1)S(1)}, bf16[16,3584]{1,0:T(8,128)(2,1)S(1)}, u32[]{:S(2)}, u32[]{:S(2)}) collective-permute-start(bf16[16,3584]{1,0:T(8,128)(2,1)S(1)} %add_convert_fusion.12), channel_id=1, source_target_pairs={{0,4},{4,8},{8,12},{12,14},{14,10},{10,6},{6,2},{2,0},{1,5},{5,9},... | collective-permute-start | bytes 344072 | tf_op jit(solution)/shard_map/ppermute | solution.py:795
  115.1 5.2 %collective-permute-start.40 = (bf16[16,3584]{1,0:T(8,128)(2,1)S(1)}, bf16[16,3584]{1,0:T(8,128)(2,1)S(1)}, u32[]{:S(2)}, u32[]{:S(2)}) collective-permute-start(bf16[16,3584]{1,0:T(8,128)(2,1)S(1)} %add_convert_fusion.11), channel_id=1, source_target_pairs={{4,0},{8,4},{12,8},{14,12},{10,14},{6,10},{2,6},{0,2},{5,1},{9,5},... | collective-permute-start | bytes 344072 | tf_op jit(solution)/shard_map/ppermute | solution.py:798
  117.5 5.3 %collective-permute-start.52 = (bf16[16,3584]{1,0:T(8,128)(2,1)S(1)}, bf16[16,3584]{1,0:T(8,128)(2,1)S(1)}, u32[]{:S(2)}, u32[]{:S(2)}) collective-permute-start(bf16[16,3584]{1,0:T(8,128)(2,1)S(1)} %add_convert_fusion.3), channel_id=1, source_target_pairs={{4,0},{8,4},{12,8},{14,12},{10,14},{6,10},{2,6},{0,2},{5,1},{9,5},... | collective-permute-start | bytes 344072 | tf_op jit(solution)/shard_map/ppermute | solution.py:798
  118.7 5.6 %collective-permute-start.51 = (bf16[16,3584]{1,0:T(8,128)(2,1)S(1)}, bf16[16,3584]{1,0:T(8,128)(2,1)S(1)}, u32[]{:S(2)}, u32[]{:S(2)}) collective-permute-start(bf16[16,3584]{1,0:T(8,128)(2,1)S(1)} %add_convert_fusion.4), channel_id=1, source_target_pairs={{0,4},{4,8},{8,12},{12,14},{14,10},{10,6},{6,2},{2,0},{1,5},{5,9},... | collective-permute-start | bytes 344072 | tf_op jit(solution)/shard_map/ppermute | solution.py:795
  120.5 6.0 %collective-permute-start.42 = (bf16[16,3584]{1,0:T(8,128)(2,1)S(1)}, bf16[16,3584]{1,0:T(8,128)(2,1)S(1)}, u32[]{:S(2)}, u32[]{:S(2)}) collective-permute-start(bf16[16,3584]{1,0:T(8,128)(2,1)S(1)} %add_convert_fusion.9), channel_id=1, source_target_pairs={{4,0},{8,4},{12,8},{14,12},{10,14},{6,10},{2,6},{0,2},{5,1},{9,5},... | collective-permute-start | bytes 344072 | tf_op jit(solution)/shard_map/ppermute | solution.py:798
  121.4 6.0 %collective-permute-start.41 = (bf16[16,3584]{1,0:T(8,128)(2,1)S(1)}, bf16[16,3584]{1,0:T(8,128)(2,1)S(1)}, u32[]{:S(2)}, u32[]{:S(2)}) collective-permute-start(bf16[16,3584]{1,0:T(8,128)(2,1)S(1)} %add_convert_fusion.10), channel_id=1, source_target_pairs={{0,4},{4,8},{8,12},{12,14},{14,10},{10,6},{6,2},{2,0},{1,5},{5,9},... | collective-permute-start | bytes 344072 | tf_op jit(solution)/shard_map/ppermute | solution.py:795
  124.4 5.9 %collective-permute-start.53 = (bf16[16,3584]{1,0:T(8,128)(2,1)S(1)}, bf16[16,3584]{1,0:T(8,128)(2,1)S(1)}, u32[]{:S(2)}, u32[]{:S(2)}) collective-permute-start(bf16[16,3584]{1,0:T(8,128)(2,1)S(1)} %add_convert_fusion.2), channel_id=1, source_target_pairs={{0,4},{4,8},{8,12},{12,14},{14,10},{10,6},{6,2},{2,0},{1,5},{5,9},... | collective-permute-start | bytes 344072 | tf_op jit(solution)/shard_map/ppermute | solution.py:795
  124.9 5.3 %collective-permute-start.54 = (bf16[16,3584]{1,0:T(8,128)(2,1)S(1)}, bf16[16,3584]{1,0:T(8,128)(2,1)S(1)}, u32[]{:S(2)}, u32[]{:S(2)}) collective-permute-start(bf16[16,3584]{1,0:T(8,128)(2,1)S(1)} %add_convert_fusion.1), channel_id=1, source_target_pairs={{4,0},{8,4},{12,8},{14,12},{10,14},{6,10},{2,6},{0,2},{5,1},{9,5},... | collective-permute-start | bytes 344072 | tf_op jit(solution)/shard_map/ppermute | solution.py:798
  127.5 4.8 %collective-permute-start.43 = (bf16[16,3584]{1,0:T(8,128)(2,1)S(1)}, bf16[16,3584]{1,0:T(8,128)(2,1)S(1)}, u32[]{:S(2)}, u32[]{:S(2)}) collective-permute-start(bf16[16,3584]{1,0:T(8,128)(2,1)S(1)} %add_convert_fusion.8), channel_id=1, source_target_pairs={{0,4},{4,8},{8,12},{12,14},{14,10},{10,6},{6,2},{2,0},{1,5},{5,9},... | collective-permute-start | bytes 344072 | tf_op jit(solution)/shard_map/ppermute | solution.py:795
  128.2 5.2 %collective-permute-start.44 = (bf16[16,3584]{1,0:T(8,128)(2,1)S(1)}, bf16[16,3584]{1,0:T(8,128)(2,1)S(1)}, u32[]{:S(2)}, u32[]{:S(2)}) collective-permute-start(bf16[16,3584]{1,0:T(8,128)(2,1)S(1)} %add_convert_fusion.7), channel_id=1, source_target_pairs={{4,0},{8,4},{12,8},{14,12},{10,14},{6,10},{2,6},{0,2},{5,1},{9,5},... | collective-permute-start | bytes 344072 | tf_op jit(solution)/shard_map/ppermute | solution.py:798
  133.6 1.4 %collective-permute-start.45 = (bf16[16,3584]{1,0:T(8,128)(2,1)S(1)}, bf16[16,3584]{1,0:T(8,128)(2,1)S(1)}, u32[]{:S(2)}, u32[]{:S(2)}) collective-permute-start(bf16[16,3584]{1,0:T(8,128)(2,1)S(1)} %get-tuple-element.265), channel_id=1, source_target_pairs={{0,1},{1,0},{2,3},{3,2},{4,5},{5,4},{6,7},{7,6},{8,9},{9,8},{10,11... | collective-permute-start | bytes 344072 | tf_op jit(solution)/shard_map/ppermute | solution.py:801
  133.8 1.5 %collective-permute-start.55 = (bf16[16,3584]{1,0:T(8,128)(2,1)S(1)}, bf16[16,3584]{1,0:T(8,128)(2,1)S(1)}, u32[]{:S(2)}, u32[]{:S(2)}) collective-permute-start(bf16[16,3584]{1,0:T(8,128)(2,1)S(1)} %get-tuple-element.271), channel_id=1, source_target_pairs={{0,1},{1,0},{2,3},{3,2},{4,5},{5,4},{6,7},{7,6},{8,9},{9,8},{10,11... | collective-permute-start | bytes 344072 | tf_op jit(solution)/shard_map/ppermute | solution.py:801
  (2 other events, 6.8 us)

commit v13 on v12

--- a/solution.py
+++ b/solution.py
@@ -359,10 +359,18 @@
     )(*args)
 
 
+def partner(rank, j, ranks, back=False):
+    if ranks & (ranks - 1) == 0:
+        return rank ^ j
+    if isinstance(rank, int):
+        return (rank - j if back else rank + j) % ranks
+    other = rank - j if back else rank + j
+    return jnp.where(other < 0, other + ranks, jnp.where(other >= ranks, other - ranks, other))
+
+
 def pack_kernel(ranks, cores, features, tab, res, *outs):
     for k in range(ranks // cores):
-        target = tab[RANK] + k + (ranks // cores) * tab[CORE]
-        target = jnp.where(target >= ranks, target - ranks, target)
+        target = partner(tab[RANK], k + (ranks // cores) * tab[CORE], ranks)
 
         def put(columns, k=k):
             outs[k][...] = res[:, columns]
@@ -529,8 +537,7 @@
             put(ranks, extra())
 
     def owner_of(k, c):
-        owner = rank - k - count * c
-        return jnp.where(owner < 0, owner + ranks, owner)
+        return partner(rank, k + count * c, ranks, True)
 
     low = pl.ds(pl.multiple_of(core * half, half), half)
     high = pl.ds(pl.multiple_of(block + core * half, half), half)
@@ -814,7 +821,7 @@
 
     def send_piece(k):
         pairs = [
-            (i * cores + c, (i + k + len(packed) * c) % ranks * cores + c)
+            (i * cores + c, partner(i, k + len(packed) * c, ranks) * cores + c)
             for i in range(ranks)
             for c in range(cores)
             if k + c > 0
@@ -848,7 +855,7 @@
             behind.append(send_next(out_f))
             ahead.append(send_prev(out_b))
     gathered = [[main] + behind + ahead + [extra] for _, main, extra, behind, ahead in chains]
-    gathered[0][2], pieces = lax.optimization_barrier((gathered[0][2], pieces))
+    gathered[0][reach], pieces = lax.optimization_barrier((gathered[0][reach], pieces))
     shared = swap(share(tab, packed[0], pieces, cores))
     gathered[0], shared = lax.optimization_barrier((gathered[0], shared))
     for part in range(2):

time: 136 us -> 139 us (1.022)
  waiting for transfers between devices: 37.2 us -> 42.4 us
  starting transfers between devices: 54 us -> 51.7 us
    ppermute x20, starting transfers between devices: 22.1 us -> 26.7 us  [send_prev(): return lax.ppermute(x, 'blk', backward)]
    ppermute x20, starting transfers between devices: 22.5 us -> 18.3 us  [send_next(): return lax.ppermute(x, 'blk', forward)]
    ppermute x20, waiting for transfers between devices: 27.1 us -> 31 us  [send_next(): return lax.ppermute(x, 'blk', forward)]
    ppermute x4, starting transfers between devices: 6.28 us -> 4.21 us  [send_piece(): pieces[k] = lax.ppermute(packed[k], ('blk', 'head'), pairs)]
where the time goes in v13:
time: 139 us
  starting transfers between devices  51.7 us (37%)
  waiting for transfers between devices  42.4 us (31%)
  Pallas kernels  39.1 us (28%)
  between operations  2.67 us (2%)
  other arithmetic  2.36 us (2%)
    ppermute x20, waiting for transfers between devices, send_next(): return lax.ppermute(x, 'blk', forward)  31 us
    ppermute x20, starting transfers between devices, send_prev(): return lax.ppermute(x, 'blk', backward)  26.7 us
    ppermute x20, starting transfers between devices, send_next(): return lax.ppermute(x, 'blk', forward)  18.3 us
    pallas_call x2, Pallas kernels, attend(): pl.pallas_call(functools.partial(attend_kernel, table, order, heads, part...  14.1 us
    pallas_call x5, Pallas kernels, expand(): pl.pallas_call(functools.partial(expand_kernel, pieces, len(theirs), firs...  12.1 us
    ppermute x20, waiting for transfers between devices, send_prev(): return lax.ppermute(x, 'blk', backward)  8.42 us
    pallas_call x4, Pallas kernels, contract(): pl.pallas_call(functools.partial(contract_kernel, part * columns), grid=(...  5.02 us
    ppermute x4, starting transfers between devices, send_piece(): pieces[k] = lax.ppermute(packed[k], ('blk', 'head'), pairs)  4.21 us
  transfers between devices with their start and end apart: 56, of which 29 were waited for; matrix products, arithmetic and copies ran while one was open for 1% of the time, Pallas kernels for 19%

profile of v13, /device:TPU:0, one launch (start us, length us, event | category | flops | bytes accessed | tf_op | source)
XLA Modules:
  0.0 139.0 jit_solution(15493511697904875390)
XLA Ops:
  0.7 0.8 concatenate.24.refs_0_
  1.5 8.2 %attend.2 = (s32[60]{0:T(128)S(1)}, bf16[32,2048]{1,0:T(8,128)(2,1)S(1)}, bf16[32,2048]{1,0:T(8,128)(2,1)S(1)}, bf16[32,2048]{1,0:T(8,128)(2,1)S(1)}, bf16[128,5...) custom-call(s32[26]{0:T(128)S(1)} %concatenate.24.refs_0_, ...), custom_call_target="tpu_custom_call" | custom-call | flops 713031680 | bytes 4456448 | tf_op jit(solution)/shard_map/attend/pallas_call | solution.py:344
  9.7 3.1 %collective-permute-start.11 = (bf16[32,2048]{1,0:T(8,128)(2,1)S(1)}, bf16[32,2048]{1,0:T(8,128)(2,1)S(1)}, u32[]{:S(2)}, u32[]{:S(2)}) collective-permute-start(bf16[32,2048]{1,0:T(8,128)(2,1)S(1)} %get-tuple-element.162), channel_id=1, source_target_pairs={{0,4},{4,8},{8,12},{12,14},{14,10},{10,6},{6,2},{2,0},{1,5},{5,9},... | collective-permute-start | bytes 393224 | tf_op jit(solution)/shard_map/ppermute | solution.py:802
  13.4 2.0 %collective-permute-start.1 = (bf16[64,896]{1,0:T(8,128)(2,1)S(1)}, bf16[64,896]{1,0:T(8,128)(2,1)S(1)}, u32[]{:S(2)}, u32[]{:S(2)}) collective-permute-start(bf16[64,896]{1,0:T(8,128)(2,1)S(1)} %get-tuple-element.141), channel_id=1, source_target_pairs={{0,4},{1,13},{2,6},{3,15},{4,0},{5,9},{6,2},{7,11},{8,12},{9,5},{1... | collective-permute-start | bytes 344072 | tf_op jit(solution)/shard_map/ppermute | solution.py:829
  15.4 1.5 %collective-permute-start.2 = (bf16[64,896]{1,0:T(8,128)(2,1)S(1)}, bf16[64,896]{1,0:T(8,128)(2,1)S(1)}, u32[]{:S(2)}, u32[]{:S(2)}) collective-permute-start(bf16[64,896]{1,0:T(8,128)(2,1)S(1)} %get-tuple-element.142), channel_id=1, source_target_pairs={{0,6},{1,15},{2,4},{3,13},{4,2},{5,11},{6,0},{7,9},{8,14},{9,7},{1... | collective-permute-start | bytes 344072 | tf_op jit(solution)/shard_map/ppermute | solution.py:829
  17.7 5.9 %attend.3 = (bf16[32,2048]{1,0:T(8,128)(2,1)S(1)}, bf16[32,2048]{1,0:T(8,128)(2,1)S(1)}, bf16[32,2048]{1,0:T(8,128)(2,1)S(1)}) custom-call(s32[60]{0:T(128)S(1)} %get-tuple-element.137.tab.refs_0_, bf16[64,18432]{1,0:T(8,128)(2,1)} %refs_1_.3, bf16[8,576,256]{2,1,0:T(8,128)(2,1)} %refs_2_.3, bf16[64,576]{1,0:T(8,128)(2,1)} %bitcast.33, ...), custom_call_target="tpu_custom_call" | custom-call | flops 713031680 | bytes 4456448 | tf_op jit(solution)/shard_map/attend/pallas_call | solution.py:344
  23.7 0.7 collective-permute-start.18
  24.4 1.9 %collective-permute-start.4 = (bf16[32,2048]{1,0:T(8,128)(2,1)S(1)}, bf16[32,2048]{1,0:T(8,128)(2,1)S(1)}, u32[]{:S(2)}, u32[]{:S(2)}) collective-permute-start(bf16[32,2048]{1,0:T(8,128)(2,1)S(1)} %get-tuple-element.153.refs_0_), channel_id=1, source_target_pairs={{4,0},{8,4},{12,8},{14,12},{10,14},{6,10},{2,6},{0,2},{5,1},{9,5},... | collective-permute-start | bytes 393224 | tf_op jit(solution)/shard_map/ppermute | solution.py:805
  26.5 1.9 %collective-permute-start.14 = (bf16[32,2048]{1,0:T(8,128)(2,1)S(1)}, bf16[32,2048]{1,0:T(8,128)(2,1)S(1)}, u32[]{:S(2)}, u32[]{:S(2)}) collective-permute-start(bf16[32,2048]{1,0:T(8,128)(2,1)S(1)} %broadcast_select_fusion.4), channel_id=1, source_target_pairs={{4,0},{8,4},{12,8},{14,12},{10,14},{6,10},{2,6},{0,2},{5,1},{9,5},... | collective-permute-start | bytes 393224 | tf_op jit(solution)/shard_map/ppermute | solution.py:805
  28.6 2.7 %collective-permute-done.3.refs_1_ = bf16[32,2048]{1,0:T(8,128)(2,1)S(1)} collective-permute-done((bf16[32,2048]{1,0:T(8,128)(2,1)S(1)}, bf16[32,2048]{1,0:T(8,128)(2,1)S(1)}, u32[]{:S(2)}, u32[]{:S(2)}) %collective-permute-start.3) | collective-permute-done | bytes 131104 | tf_op jit(solution)/shard_map/ppermute | solution.py:802
  31.3 2.2 %collective-permute-start.6 = (bf16[32,2048]{1,0:T(8,128)(2,1)S(1)}, bf16[32,2048]{1,0:T(8,128)(2,1)S(1)}, u32[]{:S(2)}, u32[]{:S(2)}) collective-permute-start(bf16[32,2048]{1,0:T(8,128)(2,1)S(1)} %broadcast_select_fusion.10), channel_id=1, source_target_pairs={{4,0},{8,4},{12,8},{14,12},{10,14},{6,10},{2,6},{0,2},{5,1},{9,5},... | collective-permute-start | bytes 393224 | tf_op jit(solution)/shard_map/ppermute | solution.py:805
  33.8 3.3 %collective-permute-start.16 = (bf16[32,2048]{1,0:T(8,128)(2,1)S(1)}, bf16[32,2048]{1,0:T(8,128)(2,1)S(1)}, u32[]{:S(2)}, u32[]{:S(2)}) collective-permute-start(bf16[32,2048]{1,0:T(8,128)(2,1)S(1)} %broadcast_select_fusion.2), channel_id=1, source_target_pairs={{4,0},{8,4},{12,8},{14,12},{10,14},{6,10},{2,6},{0,2},{5,1},{9,5},... | collective-permute-start | bytes 393224 | tf_op jit(solution)/shard_map/ppermute | solution.py:805
  37.3 3.1 %collective-permute-done.5.refs_2_ = bf16[32,2048]{1,0:T(8,128)(2,1)S(1)} collective-permute-done((bf16[32,2048]{1,0:T(8,128)(2,1)S(1)}, bf16[32,2048]{1,0:T(8,128)(2,1)S(1)}, u32[]{:S(2)}, u32[]{:S(2)}) %collective-permute-start.5) | collective-permute-done | bytes 131104 | tf_op jit(solution)/shard_map/ppermute | solution.py:802
  40.4 2.8 %collective-permute-start.8 = (bf16[32,2048]{1,0:T(8,128)(2,1)S(1)}, bf16[32,2048]{1,0:T(8,128)(2,1)S(1)}, u32[]{:S(2)}, u32[]{:S(2)}) collective-permute-start(bf16[32,2048]{1,0:T(8,128)(2,1)S(1)} %broadcast_select_fusion.8), channel_id=1, source_target_pairs={{4,0},{8,4},{12,8},{14,12},{10,14},{6,10},{2,6},{0,2},{5,1},{9,5},... | collective-permute-start | bytes 393224 | tf_op jit(solution)/shard_map/ppermute | solution.py:805
  43.2 1.0 collective-permute-done.15.refs_3_
  44.3 2.1 %collective-permute-start.19 = (bf16[32,2048]{1,0:T(8,128)(2,1)S(1)}, bf16[32,2048]{1,0:T(8,128)(2,1)S(1)}, u32[]{:S(2)}, u32[]{:S(2)}) collective-permute-start(bf16[32,2048]{1,0:T(8,128)(2,1)S(1)} %broadcast_select_fusion), channel_id=1, source_target_pairs={{4,0},{8,4},{12,8},{14,12},{10,14},{6,10},{2,6},{0,2},{5,1},{9,5},... | collective-permute-start | bytes 393224 | tf_op jit(solution)/shard_map/ppermute | solution.py:805
  46.8 4.7 %collective-permute-done.17.refs_4_ = bf16[32,2048]{1,0:T(8,128)(2,1)S(1)} collective-permute-done((bf16[32,2048]{1,0:T(8,128)(2,1)S(1)}, bf16[32,2048]{1,0:T(8,128)(2,1)S(1)}, u32[]{:S(2)}, u32[]{:S(2)}) %collective-permute-start.17) | collective-permute-done | bytes 131104 | tf_op jit(solution)/shard_map/ppermute | solution.py:802
  52.6 1.7 %collective-permute-start.9 = (bf16[32,2048]{1,0:T(8,128)(2,1)S(1)}, bf16[32,2048]{1,0:T(8,128)(2,1)S(1)}, u32[]{:S(2)}, u32[]{:S(2)}) collective-permute-start(bf16[32,2048]{1,0:T(8,128)(2,1)S(1)} %broadcast_select_fusion.7), channel_id=1, source_target_pairs={{0,4},{4,8},{8,12},{12,14},{14,10},{10,6},{6,2},{2,0},{1,5},{5,9},... | collective-permute-start | bytes 393224 | tf_op jit(solution)/shard_map/ppermute | solution.py:802
  54.4 1.9 %project.2.refs_10_ = f32[288,896]{1,0:T(8,128)S(1)} custom-call(s32[60]{0:T(128)S(1)} %get-tuple-element.137.tab.refs_0_, bf16[32,2048]{1,0:T(8,128)(2,1)S(1)} %get-tuple-element.180.refs_0_, bf16[32,2048]{1,0:T(8,128)(2,1)S(1)} %collective-permute-done.11.refs_1_, bf16[32,2048]{1,0:T(8,128)(2,1)S(1)} %collective-permute-done.13.refs_2_, ...), custom_call_target="tpu_custom_call" | custom-call | flops 1056964608 | bytes 4849664 | tf_op jit(solution)/shard_map/project/pallas_call | solution.py:497
  56.3 1.8 %collective-permute-done.10.refs_8_ = bf16[32,2048]{1,0:T(8,128)(2,1)S(1)} collective-permute-done((bf16[32,2048]{1,0:T(8,128)(2,1)S(1)}, bf16[32,2048]{1,0:T(8,128)(2,1)S(1)}, u32[]{:S(2)}, u32[]{:S(2)}) %collective-permute-start.10) | collective-permute-done | bytes 131104 | tf_op jit(solution)/shard_map/ppermute | solution.py:805
  58.2 2.0 %project.3 = (f32[144,896]{1,0:T(8,128)S(1)}, bf16[144,896]{1,0:T(8,128)(2,1)S(1)}) custom-call(s32[60]{0:T(128)S(1)} %get-tuple-element.137.tab.refs_0_, bf16[32,2048]{1,0:T(8,128)(2,1)S(1)} %get-tuple-element.153.refs_0_, bf16[32,2048]{1,0:T(8,128)(2,1)S(1)} %collective-permute-done.3.refs_1_, bf16[32,2048]{1,0:T(8,128)(2,1)S(1)} %collective-permute-done.5.refs_2_, ...), custom_call_target="tpu_custom_call" | custom-call | flops 1056964608 | bytes 4849664 | tf_op jit(solution)/shard_map/project/pallas_call | solution.py:507
  61.0 0.9 collective-permute-done.21
  62.2 1.7 %collective-permute-start.22 = (bf16[144,896]{1,0:T(8,128)(2,1)S(1)}, bf16[144,896]{1,0:T(8,128)(2,1)S(1)}, u32[]{:S(2)}, u32[]{:S(2)}) collective-permute-start(bf16[144,896]{1,0:T(8,128)(2,1)S(1)} %add_convert_fusion.refs_0_.refs_1_), channel_id=1, source_target_pairs={{0,4},{4,8},{8,12},{12,14},{14,10},{10,6},{6,2},{2,0},{1,5},{5,9},... | collective-permute-start | bytes 774152 | tf_op jit(solution)/shard_map/ppermute | solution.py:802
  64.3 1.7 %expand.5 = (f32[288,576]{1,0:T(8,128)S(1)}, f32[288,576]{1,0:T(8,128)S(1)}, f32[288,1]{1,0:T(8,128)S(1)}) custom-call(s32[60]{0:T(128)S(1)} %get-tuple-element.137.tab.refs_0_, bf16[144,896]{1,0:T(8,128)(2,1)S(1)} %add_convert_fusion.refs_0_.refs_1_, bf16[144,896]{1,0:T(8,128)(2,1)S(1)} %collective-permute-done.24.refs_1_, f32[8,1,896]{2,1,0:T(1,128)S(1)} %bitcast.27, ...), custom_call_target="tpu_custom_call" | custom-call | flops 1 | bytes 1 | tf_op jit(solution)/shard_map/expand/pallas_call | solution.py:658
  65.9 4.7 %collective-permute-done.22.refs_0_.refs_2_.refs_3_ = bf16[144,896]{1,0:T(8,128)(2,1)S(1)} collective-permute-done((bf16[144,896]{1,0:T(8,128)(2,1)S(1)}, bf16[144,896]{1,0:T(8,128)(2,1)S(1)}, u32[]{:S(2)}, u32[]{:S(2)}) %collective-permute-start.22) | collective-permute-done | bytes 258080 | tf_op jit(solution)/shard_map/ppermute | solution.py:802
  70.7 1.4 %collective-permute-done.23.refs_1_.refs_4_.refs_5_ = bf16[144,896]{1,0:T(8,128)(2,1)S(1)} collective-permute-done((bf16[144,896]{1,0:T(8,128)(2,1)S(1)}, bf16[144,896]{1,0:T(8,128)(2,1)S(1)}, u32[]{:S(2)}, u32[]{:S(2)}) %collective-permute-start.23) | collective-permute-done | bytes 258080 | tf_op jit(solution)/shard_map/ppermute | solution.py:805
  72.5 1.7 %collective-permute-start.26 = (bf16[144,896]{1,0:T(8,128)(2,1)S(1)}, bf16[144,896]{1,0:T(8,128)(2,1)S(1)}, u32[]{:S(2)}, u32[]{:S(2)}) collective-permute-start(bf16[144,896]{1,0:T(8,128)(2,1)S(1)} %collective-permute-done.23.refs_1_.refs_4_.refs_5_), channel_id=1, source_target_pairs={{4,0},{8,4},{12,8},{14,12},{10,14},{6,10},{2,6},{0,2},{5,1},{9,5},... | collective-permute-start | bytes 774152 | tf_op jit(solution)/shard_map/ppermute | solution.py:805
  74.3 2.9 %expand.6 = (f32[288,576]{1,0:T(8,128)S(1)}, f32[288,576]{1,0:T(8,128)S(1)}, f32[288,1]{1,0:T(8,128)S(1)}) custom-call(s32[60]{0:T(128)S(1)} %get-tuple-element.137.tab.refs_0_, bf16[144,896]{1,0:T(8,128)(2,1)S(1)} %collective-permute-done.22.refs_0_.refs_2_.refs_3_, bf16[144,896]{1,0:T(8,128)(2,1)S(1)} %collective-permute-done.23.refs_1_.refs_4_.refs_5_, ...), custom_call_target="tpu_custom_call" | custom-call | flops 1 | bytes 1 | tf_op jit(solution)/shard_map/expand/pallas_call | solution.py:658
  77.1 3.7 %collective-permute-done.25.refs_0_.refs_6_.refs_7_ = bf16[144,896]{1,0:T(8,128)(2,1)S(1)} collective-permute-done((bf16[144,896]{1,0:T(8,128)(2,1)S(1)}, bf16[144,896]{1,0:T(8,128)(2,1)S(1)}, u32[]{:S(2)}, u32[]{:S(2)}) %collective-permute-start.25) | collective-permute-done | bytes 258080 | tf_op jit(solution)/shard_map/ppermute | solution.py:802
  81.4 1.7 %collective-permute-start.29 = (bf16[144,896]{1,0:T(8,128)(2,1)S(1)}, bf16[144,896]{1,0:T(8,128)(2,1)S(1)}, u32[]{:S(2)}, u32[]{:S(2)}) collective-permute-start(bf16[144,896]{1,0:T(8,128)(2,1)S(1)} %collective-permute-done.26.refs_1_.refs_8_.refs_9_), channel_id=1, source_target_pairs={{4,0},{8,4},{12,8},{14,12},{10,14},{6,10},{2,6},{0,2},{5,1},{9,5},... | collective-permute-start | bytes 774152 | tf_op jit(solution)/shard_map/ppermute | solution.py:805
  83.0 2.9 %expand.7 = (f32[288,576]{1,0:T(8,128)S(1)}, f32[288,576]{1,0:T(8,128)S(1)}, f32[288,1]{1,0:T(8,128)S(1)}) custom-call(s32[60]{0:T(128)S(1)} %get-tuple-element.137.tab.refs_0_, bf16[144,896]{1,0:T(8,128)(2,1)S(1)} %collective-permute-done.25.refs_0_.refs_6_.refs_7_, bf16[144,896]{1,0:T(8,128)(2,1)S(1)} %collective-permute-done.26.refs_1_.refs_8_.refs_9_, ...), custom_call_target="tpu_custom_call" | custom-call | flops 1 | bytes 1 | tf_op jit(solution)/shard_map/expand/pallas_call | solution.py:658
  85.9 3.7 %collective-permute-done.28.refs_0_.refs_10_.refs_11_ = bf16[144,896]{1,0:T(8,128)(2,1)S(1)} collective-permute-done((bf16[144,896]{1,0:T(8,128)(2,1)S(1)}, bf16[144,896]{1,0:T(8,128)(2,1)S(1)}, u32[]{:S(2)}, u32[]{:S(2)}) %collective-permute-start.28) | collective-permute-done | bytes 258080 | tf_op jit(solution)/shard_map/ppermute | solution.py:802
  89.8 1.7 %collective-permute-start.31 = (bf16[80,896]{1,0:T(8,128)(2,1)S(1)}, bf16[80,896]{1,0:T(8,128)(2,1)S(1)}, u32[]{:S(2)}, u32[]{:S(2)}) collective-permute-start(bf16[80,896]{1,0:T(8,128)(2,1)S(1)} %slice.18), channel_id=1, source_target_pairs={{0,4},{4,8},{8,12},{12,14},{14,10},{10,6},{6,2},{2,0},{1,5},{5,9},... | collective-permute-start | bytes 430088 | tf_op jit(solution)/shard_map/ppermute | solution.py:802
  91.9 2.9 %expand.8 = (f32[288,576]{1,0:T(8,128)S(1)}, f32[288,576]{1,0:T(8,128)S(1)}, f32[288,1]{1,0:T(8,128)S(1)}) custom-call(s32[60]{0:T(128)S(1)} %get-tuple-element.137.tab.refs_0_, bf16[144,896]{1,0:T(8,128)(2,1)S(1)} %collective-permute-done.28.refs_0_.refs_10_.refs_11_, bf16[144,896]{1,0:T(8,128)(2,1)S(1)} %collective-permute-done.29.refs_1_.refs_12_.refs_13_, ...), custom_call_target="tpu_custom_call" | custom-call | flops 1 | bytes 1 | tf_op jit(solution)/shard_map/expand/pallas_call | solution.py:658
  94.8 2.0 %collective-permute-done.32.refs_1_ = bf16[64,896]{1,0:T(8,128)(2,1)S(1)} collective-permute-done((bf16[64,896]{1,0:T(8,128)(2,1)S(1)}, bf16[64,896]{1,0:T(8,128)(2,1)S(1)}, u32[]{:S(2)}, u32[]{:S(2)}) %collective-permute-start.32) | collective-permute-done | bytes 114720 | tf_op jit(solution)/shard_map/ppermute | solution.py:805
  97.4 1.0 collective-permute-done.35.refs_3_
  98.5 1.8 %expand.9.hidden = bf16[288,576]{1,0:T(8,128)(2,1)S(1)} custom-call(s32[60]{0:T(128)S(1)} %get-tuple-element.137.tab.refs_0_, bf16[80,896]{1,0:T(8,128)(2,1)S(1)} %collective-permute-done.31.refs_0_, bf16[64,896]{1,0:T(8,128)(2,1)S(1)} %collective-permute-done.32.refs_1_, bf16[80,896]{1,0:T(8,128)(2,1)S(1)} %collective-permute-done.34.refs_2_, ...), custom_call_target="tpu_custom_call" | custom-call | flops 1 | bytes 1 | tf_op jit(solution)/shard_map/expand/pallas_call | solution.py:658
  100.3 1.3 contract.7
  101.9 1.2 contract.6
  103.4 1.2 contract.4.mine
  104.7 1.3 contract.5.mine
  106.0 0.8 pick.3
  106.9 0.8 collective-permute-start.48
  108.3 1.5 %collective-permute-start.47 = (bf16[16,3584]{1,0:T(8,128)(2,1)S(1)}, bf16[16,3584]{1,0:T(8,128)(2,1)S(1)}, u32[]{:S(2)}, u32[]{:S(2)}) collective-permute-start(bf16[16,3584]{1,0:T(8,128)(2,1)S(1)} %convert_element_type.156), channel_id=1, source_target_pairs={{0,4},{4,8},{8,12},{12,14},{14,10},{10,6},{6,2},{2,0},{1,5},{5,9},... | collective-permute-start | bytes 344072 | tf_op jit(solution)/shard_map/ppermute | solution.py:802
  109.9 0.8 pick.2
  110.7 0.8 collective-permute-start.38
  111.5 1.3 collective-permute-start.37
  112.8 0.9 collective-permute-done.47
  113.7 1.8 %collective-permute-start.50 = (bf16[16,3584]{1,0:T(8,128)(2,1)S(1)}, bf16[16,3584]{1,0:T(8,128)(2,1)S(1)}, u32[]{:S(2)}, u32[]{:S(2)}) collective-permute-start(bf16[16,3584]{1,0:T(8,128)(2,1)S(1)} %add_convert_fusion.5), channel_id=1, source_target_pairs={{4,0},{8,4},{12,8},{14,12},{10,14},{6,10},{2,6},{0,2},{5,1},{9,5},... | collective-permute-start | bytes 344072 | tf_op jit(solution)/shard_map/ppermute | solution.py:805
  116.3 1.6 %collective-permute-start.39 = (bf16[16,3584]{1,0:T(8,128)(2,1)S(1)}, bf16[16,3584]{1,0:T(8,128)(2,1)S(1)}, u32[]{:S(2)}, u32[]{:S(2)}) collective-permute-start(bf16[16,3584]{1,0:T(8,128)(2,1)S(1)} %add_convert_fusion.12), channel_id=1, source_target_pairs={{0,4},{4,8},{8,12},{12,14},{14,10},{10,6},{6,2},{2,0},{1,5},{5,9},... | collective-permute-start | bytes 344072 | tf_op jit(solution)/shard_map/ppermute | solution.py:802
  118.8 1.8 %collective-permute-done.49 = bf16[16,3584]{1,0:T(8,128)(2,1)S(1)} collective-permute-done((bf16[16,3584]{1,0:T(8,128)(2,1)S(1)}, bf16[16,3584]{1,0:T(8,128)(2,1)S(1)}, u32[]{:S(2)}, u32[]{:S(2)}) %collective-permute-start.49) | collective-permute-done | bytes 114720 | tf_op jit(solution)/shard_map/ppermute | solution.py:802
  120.7 1.3 collective-permute-start.52
  122.0 0.7 collective-permute-start.51
  122.8 1.1 collective-permute-done.40
  124.3 1.8 %collective-permute-start.41 = (bf16[16,3584]{1,0:T(8,128)(2,1)S(1)}, bf16[16,3584]{1,0:T(8,128)(2,1)S(1)}, u32[]{:S(2)}, u32[]{:S(2)}) collective-permute-start(bf16[16,3584]{1,0:T(8,128)(2,1)S(1)} %add_convert_fusion.10), channel_id=1, source_target_pairs={{0,4},{4,8},{8,12},{12,14},{14,10},{10,6},{6,2},{2,0},{1,5},{5,9},... | collective-permute-start | bytes 344072 | tf_op jit(solution)/shard_map/ppermute | solution.py:802
  126.2 1.5 %collective-permute-done.51 = bf16[16,3584]{1,0:T(8,128)(2,1)S(1)} collective-permute-done((bf16[16,3584]{1,0:T(8,128)(2,1)S(1)}, bf16[16,3584]{1,0:T(8,128)(2,1)S(1)}, u32[]{:S(2)}, u32[]{:S(2)}) %collective-permute-start.51) | collective-permute-done | bytes 114720 | tf_op jit(solution)/shard_map/ppermute | solution.py:802
  127.7 0.8 collective-permute-start.53
  128.5 1.3 collective-permute-start.54
  130.4 1.0 collective-permute-start.43
  131.4 1.1 collective-permute-start.44
  133.3 1.9 %collective-permute-done.43 = bf16[16,3584]{1,0:T(8,128)(2,1)S(1)} collective-permute-done((bf16[16,3584]{1,0:T(8,128)(2,1)S(1)}, bf16[16,3584]{1,0:T(8,128)(2,1)S(1)}, u32[]{:S(2)}, u32[]{:S(2)}) %collective-permute-start.43) | collective-permute-done | bytes 114720 | tf_op jit(solution)/shard_map/ppermute | solution.py:802
  135.2 0.9 collective-permute-done.44
  137.1 0.6 collective-permute-done.45
  138.1 0.9 maximum_select_fusion
  (133 shorter events, 12.6 us)
Async XLA Ops:
  0.0 12.8 %copy-start = (bf16[64,7168]{1,0:T(8,128)(2,1)S(1)}, bf16[64,7168]{1,0:T(8,128)(2,1)}, u32[]{:S(2)}) copy-start(bf16[64,7168]{1,0:T(8,128)(2,1)} %res.1) | copy-start | bytes 2752516
  9.7 16.8 %collective-permute-start.11 = (bf16[32,2048]{1,0:T(8,128)(2,1)S(1)}, bf16[32,2048]{1,0:T(8,128)(2,1)S(1)}, u32[]{:S(2)}, u32[]{:S(2)}) collective-permute-start(bf16[32,2048]{1,0:T(8,128)(2,1)S(1)} %get-tuple-element.162), channel_id=1, source_target_pairs={{0,4},{4,8},{8,12},{12,14},{14,10},{10,6},{6,2},{2,0},{1,5},{5,9},... | collective-permute-start | bytes 393224 | tf_op jit(solution)/shard_map/ppermute | solution.py:802
  13.4 41.0 %slice-start.6 = ((s8[7340032]{0:T(1024)(128)(4,1)}), s8[4194304]{0:T(1024)(128)(4,1)S(1)}, s32[]{:S(2)}) async-start(s8[7340032]{0:T(1024)(128)(4,1)} %bitcast.25), calls=%async_computation.6 | async-start | bytes 8388608
  13.4 10.3 %collective-permute-start = (bf16[64,896]{1,0:T(8,128)(2,1)S(1)}, bf16[64,896]{1,0:T(8,128)(2,1)S(1)}, u32[]{:S(2)}, u32[]{:S(2)}) collective-permute-start(bf16[64,896]{1,0:T(8,128)(2,1)S(1)} %get-tuple-element.140), channel_id=1, source_target_pairs={{0,2},{1,11},{2,0},{3,9},{4,6},{5,15},{6,4},{7,13},{8,10},{9,3},{1... | collective-permute-start | bytes 344072 | tf_op jit(solution)/shard_map/ppermute | solution.py:829
  13.4 10.2 %collective-permute-start.1 = (bf16[64,896]{1,0:T(8,128)(2,1)S(1)}, bf16[64,896]{1,0:T(8,128)(2,1)S(1)}, u32[]{:S(2)}, u32[]{:S(2)}) collective-permute-start(bf16[64,896]{1,0:T(8,128)(2,1)S(1)} %get-tuple-element.141), channel_id=1, source_target_pairs={{0,4},{1,13},{2,6},{3,15},{4,0},{5,9},{6,2},{7,11},{8,12},{9,5},{1... | collective-permute-start | bytes 344072 | tf_op jit(solution)/shard_map/ppermute | solution.py:829
  15.4 8.3 %collective-permute-start.2 = (bf16[64,896]{1,0:T(8,128)(2,1)S(1)}, bf16[64,896]{1,0:T(8,128)(2,1)S(1)}, u32[]{:S(2)}, u32[]{:S(2)}) collective-permute-start(bf16[64,896]{1,0:T(8,128)(2,1)S(1)} %get-tuple-element.142), channel_id=1, source_target_pairs={{0,6},{1,15},{2,4},{3,13},{4,2},{5,11},{6,0},{7,9},{8,14},{9,7},{1... | collective-permute-start | bytes 344072 | tf_op jit(solution)/shard_map/ppermute | solution.py:829
  16.9 9.5 %collective-permute-start.12 = (bf16[32,2048]{1,0:T(8,128)(2,1)S(1)}, bf16[32,2048]{1,0:T(8,128)(2,1)S(1)}, u32[]{:S(2)}, u32[]{:S(2)}) collective-permute-start(bf16[32,2048]{1,0:T(8,128)(2,1)S(1)} %get-tuple-element.180.refs_0_), channel_id=1, source_target_pairs={{4,0},{8,4},{12,8},{14,12},{10,14},{6,10},{2,6},{0,2},{5,1},{9,5},... | collective-permute-start | bytes 393224 | tf_op jit(solution)/shard_map/ppermute | solution.py:805
  17.7 36.7 %slice-start.7 = ((s8[7340032]{0:T(1024)(128)(4,1)}), s8[3145728]{0:T(1024)(128)(4,1)S(1)}, s32[]{:S(2)}) async-start(s8[7340032]{0:T(1024)(128)(4,1)} %bitcast.25), calls=%async_computation.7 | async-start | bytes 6291456
  23.7 23.1 %collective-permute-start.18 = (bf16[64,896]{1,0:T(8,128)(2,1)S(1)}, bf16[64,896]{1,0:T(8,128)(2,1)S(1)}, u32[]{:S(2)}, u32[]{:S(2)}) collective-permute-start(bf16[64,896]{1,0:T(8,128)(2,1)S(1)} %get-tuple-element.170.own), channel_id=1, source_target_pairs={{1,9},{3,11},{5,13},{7,15},{9,1},{11,3},{13,5},{15,7},{17,25},{19,... | collective-permute-start | bytes 344072 | tf_op jit(solution)/shard_map/ppermute | solution.py:829
  24.4 6.9 %collective-permute-start.4 = (bf16[32,2048]{1,0:T(8,128)(2,1)S(1)}, bf16[32,2048]{1,0:T(8,128)(2,1)S(1)}, u32[]{:S(2)}, u32[]{:S(2)}) collective-permute-start(bf16[32,2048]{1,0:T(8,128)(2,1)S(1)} %get-tuple-element.153.refs_0_), channel_id=1, source_target_pairs={{4,0},{8,4},{12,8},{14,12},{10,14},{6,10},{2,6},{0,2},{5,1},{9,5},... | collective-permute-start | bytes 393224 | tf_op jit(solution)/shard_map/ppermute | solution.py:805
  26.3 5.0 %collective-permute-start.3 = (bf16[32,2048]{1,0:T(8,128)(2,1)S(1)}, bf16[32,2048]{1,0:T(8,128)(2,1)S(1)}, u32[]{:S(2)}, u32[]{:S(2)}) collective-permute-start(bf16[32,2048]{1,0:T(8,128)(2,1)S(1)} %get-tuple-element.150), channel_id=1, source_target_pairs={{0,4},{4,8},{8,12},{12,14},{14,10},{10,6},{6,2},{2,0},{1,5},{5,9},... | collective-permute-start | bytes 393224 | tf_op jit(solution)/shard_map/ppermute | solution.py:802
  26.5 7.0 %collective-permute-start.14 = (bf16[32,2048]{1,0:T(8,128)(2,1)S(1)}, bf16[32,2048]{1,0:T(8,128)(2,1)S(1)}, u32[]{:S(2)}, u32[]{:S(2)}) collective-permute-start(bf16[32,2048]{1,0:T(8,128)(2,1)S(1)} %broadcast_select_fusion.4), channel_id=1, source_target_pairs={{4,0},{8,4},{12,8},{14,12},{10,14},{6,10},{2,6},{0,2},{5,1},{9,5},... | collective-permute-start | bytes 393224 | tf_op jit(solution)/shard_map/ppermute | solution.py:805
  28.4 5.4 %collective-permute-start.13 = (bf16[32,2048]{1,0:T(8,128)(2,1)S(1)}, bf16[32,2048]{1,0:T(8,128)(2,1)S(1)}, u32[]{:S(2)}, u32[]{:S(2)}) collective-permute-start(bf16[32,2048]{1,0:T(8,128)(2,1)S(1)} %broadcast_select_fusion.5), channel_id=1, source_target_pairs={{0,4},{4,8},{8,12},{12,14},{14,10},{10,6},{6,2},{2,0},{1,5},{5,9},... | collective-permute-start | bytes 393224 | tf_op jit(solution)/shard_map/ppermute | solution.py:802
  31.3 6.0 %collective-permute-start.6 = (bf16[32,2048]{1,0:T(8,128)(2,1)S(1)}, bf16[32,2048]{1,0:T(8,128)(2,1)S(1)}, u32[]{:S(2)}, u32[]{:S(2)}) collective-permute-start(bf16[32,2048]{1,0:T(8,128)(2,1)S(1)} %broadcast_select_fusion.10), channel_id=1, source_target_pairs={{4,0},{8,4},{12,8},{14,12},{10,14},{6,10},{2,6},{0,2},{5,1},{9,5},... | collective-permute-start | bytes 393224 | tf_op jit(solution)/shard_map/ppermute | solution.py:805
  33.4 7.0 %collective-permute-start.5 = (bf16[32,2048]{1,0:T(8,128)(2,1)S(1)}, bf16[32,2048]{1,0:T(8,128)(2,1)S(1)}, u32[]{:S(2)}, u32[]{:S(2)}) collective-permute-start(bf16[32,2048]{1,0:T(8,128)(2,1)S(1)} %broadcast_select_fusion.11), channel_id=1, source_target_pairs={{0,4},{4,8},{8,12},{12,14},{14,10},{10,6},{6,2},{2,0},{1,5},{5,9},... | collective-permute-start | bytes 393224 | tf_op jit(solution)/shard_map/ppermute | solution.py:802
  33.8 9.4 %collective-permute-start.16 = (bf16[32,2048]{1,0:T(8,128)(2,1)S(1)}, bf16[32,2048]{1,0:T(8,128)(2,1)S(1)}, u32[]{:S(2)}, u32[]{:S(2)}) collective-permute-start(bf16[32,2048]{1,0:T(8,128)(2,1)S(1)} %broadcast_select_fusion.2), channel_id=1, source_target_pairs={{4,0},{8,4},{12,8},{14,12},{10,14},{6,10},{2,6},{0,2},{5,1},{9,5},... | collective-permute-start | bytes 393224 | tf_op jit(solution)/shard_map/ppermute | solution.py:805
  37.2 7.0 %collective-permute-start.15 = (bf16[32,2048]{1,0:T(8,128)(2,1)S(1)}, bf16[32,2048]{1,0:T(8,128)(2,1)S(1)}, u32[]{:S(2)}, u32[]{:S(2)}) collective-permute-start(bf16[32,2048]{1,0:T(8,128)(2,1)S(1)} %broadcast_select_fusion.3), channel_id=1, source_target_pairs={{0,4},{4,8},{8,12},{12,14},{14,10},{10,6},{6,2},{2,0},{1,5},{5,9},... | collective-permute-start | bytes 393224 | tf_op jit(solution)/shard_map/ppermute | solution.py:802
  40.4 6.4 %collective-permute-start.8 = (bf16[32,2048]{1,0:T(8,128)(2,1)S(1)}, bf16[32,2048]{1,0:T(8,128)(2,1)S(1)}, u32[]{:S(2)}, u32[]{:S(2)}) collective-permute-start(bf16[32,2048]{1,0:T(8,128)(2,1)S(1)} %broadcast_select_fusion.8), channel_id=1, source_target_pairs={{4,0},{8,4},{12,8},{14,12},{10,14},{6,10},{2,6},{0,2},{5,1},{9,5},... | collective-permute-start | bytes 393224 | tf_op jit(solution)/shard_map/ppermute | solution.py:805
  43.2 9.0 %collective-permute-start.7 = (bf16[32,2048]{1,0:T(8,128)(2,1)S(1)}, bf16[32,2048]{1,0:T(8,128)(2,1)S(1)}, u32[]{:S(2)}, u32[]{:S(2)}) collective-permute-start(bf16[32,2048]{1,0:T(8,128)(2,1)S(1)} %broadcast_select_fusion.9), channel_id=1, source_target_pairs={{0,4},{4,8},{8,12},{12,14},{14,10},{10,6},{6,2},{2,0},{1,5},{5,9},... | collective-permute-start | bytes 393224 | tf_op jit(solution)/shard_map/ppermute | solution.py:802
  44.2 20.0 %slice-start.2 = ((s8[8257536]{0:T(1024)(128)(4,1)}), s8[4194304]{0:T(1024)(128)(4,1)S(1)}, s32[]{:S(2)}) async-start(s8[8257536]{0:T(1024)(128)(4,1)} %bitcast.16), calls=%async_computation.2 | async-start | bytes 8388608
  44.2 7.3 %collective-permute-start.17 = (bf16[32,2048]{1,0:T(8,128)(2,1)S(1)}, bf16[32,2048]{1,0:T(8,128)(2,1)S(1)}, u32[]{:S(2)}, u32[]{:S(2)}) collective-permute-start(bf16[32,2048]{1,0:T(8,128)(2,1)S(1)} %broadcast_select_fusion.1), channel_id=1, source_target_pairs={{0,4},{4,8},{8,12},{12,14},{14,10},{10,6},{6,2},{2,0},{1,5},{5,9},... | collective-permute-start | bytes 393224 | tf_op jit(solution)/shard_map/ppermute | solution.py:802
  44.3 10.0 %collective-permute-start.19 = (bf16[32,2048]{1,0:T(8,128)(2,1)S(1)}, bf16[32,2048]{1,0:T(8,128)(2,1)S(1)}, u32[]{:S(2)}, u32[]{:S(2)}) collective-permute-start(bf16[32,2048]{1,0:T(8,128)(2,1)S(1)} %broadcast_select_fusion), channel_id=1, source_target_pairs={{4,0},{8,4},{12,8},{14,12},{10,14},{6,10},{2,6},{0,2},{5,1},{9,5},... | collective-permute-start | bytes 393224 | tf_op jit(solution)/shard_map/ppermute | solution.py:805
  52.1 2.2 %collective-permute-start.20 = (bf16[128,896]{1,0:T(8,128)(2,1)S(1)}, bf16[128,896]{1,0:T(8,128)(2,1)S(1)}, u32[]{:S(2)}, u32[]{:S(2)}) collective-permute-start(bf16[128,896]{1,0:T(8,128)(2,1)S(1)} %share.1), channel_id=1, source_target_pairs={{0,1},{1,0},{2,3},{3,2},{4,5},{5,4},{6,7},{7,6},{8,9},{9,8},{10,11... | collective-permute-start | bytes 688136 | tf_op jit(solution)/shard_map/ppermute | solution.py:808
  52.2 5.9 %collective-permute-start.10 = (bf16[32,2048]{1,0:T(8,128)(2,1)S(1)}, bf16[32,2048]{1,0:T(8,128)(2,1)S(1)}, u32[]{:S(2)}, u32[]{:S(2)}) collective-permute-start(bf16[32,2048]{1,0:T(8,128)(2,1)S(1)} %broadcast_select_fusion.6), channel_id=1, source_target_pairs={{4,0},{8,4},{12,8},{14,12},{10,14},{6,10},{2,6},{0,2},{5,1},{9,5},... | collective-permute-start | bytes 393224 | tf_op jit(solution)/shard_map/ppermute | solution.py:805
  52.6 5.6 %collective-permute-start.9 = (bf16[32,2048]{1,0:T(8,128)(2,1)S(1)}, bf16[32,2048]{1,0:T(8,128)(2,1)S(1)}, u32[]{:S(2)}, u32[]{:S(2)}) collective-permute-start(bf16[32,2048]{1,0:T(8,128)(2,1)S(1)} %broadcast_select_fusion.7), channel_id=1, source_target_pairs={{0,4},{4,8},{8,12},{12,14},{14,10},{10,6},{6,2},{2,0},{1,5},{5,9},... | collective-permute-start | bytes 393224 | tf_op jit(solution)/shard_map/ppermute | solution.py:802
  54.4 9.9 %slice-start = ((s8[8257536]{0:T(1024)(128)(4,1)}), s8[4194304]{0:T(1024)(128)(4,1)S(1)}, s32[]{:S(2)}) async-start(s8[8257536]{0:T(1024)(128)(4,1)} %bitcast.9), calls=%async_computation | async-start | bytes 8388608
  56.3 7.9 %slice-start.1 = ((s8[8257536]{0:T(1024)(128)(4,1)}), s8[4063232]{0:T(1024)(128)(4,1)S(1)}, s32[]{:S(2)}) async-start(s8[8257536]{0:T(1024)(128)(4,1)} %bitcast.9), calls=%async_computation.1 | async-start | bytes 8126464
  56.3 7.9 %slice-start.3 = ((s8[8257536]{0:T(1024)(128)(4,1)}), s8[4063232]{0:T(1024)(128)(4,1)S(1)}, s32[]{:S(2)}) async-start(s8[8257536]{0:T(1024)(128)(4,1)} %bitcast.16), calls=%async_computation.3 | async-start | bytes 8126464
  56.3 7.9 %copy-start.1 = (f32[7168]{0:T(1024)S(1)}, f32[7168]{0:T(1024)}, u32[]{:S(2)}) copy-start(f32[7168]{0:T(1024)} %param.24) | copy-start | bytes 86020
  60.3 1.6 %collective-permute-start.21 = (bf16[144,896]{1,0:T(8,128)(2,1)S(1)}, bf16[144,896]{1,0:T(8,128)(2,1)S(1)}, u32[]{:S(2)}, u32[]{:S(2)}) collective-permute-start(bf16[144,896]{1,0:T(8,128)(2,1)S(1)} %get-tuple-element.192), channel_id=1, source_target_pairs={{0,1},{1,0},{2,3},{3,2},{4,5},{5,4},{6,7},{7,6},{8,9},{9,8},{10,11... | collective-permute-start | bytes 774152 | tf_op jit(solution)/shard_map/ppermute | solution.py:808
  62.0 2.2 %collective-permute-start.24 = (bf16[144,896]{1,0:T(8,128)(2,1)S(1)}, bf16[144,896]{1,0:T(8,128)(2,1)S(1)}, u32[]{:S(2)}, u32[]{:S(2)}) collective-permute-start(bf16[144,896]{1,0:T(8,128)(2,1)S(1)} %add_convert_fusion.refs_0_.refs_1_), channel_id=1, source_target_pairs={{0,1},{1,0},{2,3},{3,2},{4,5},{5,4},{6,7},{7,6},{8,9},{9,8},{10,11... | collective-permute-start | bytes 774152 | tf_op jit(solution)/shard_map/ppermute | solution.py:808
  62.2 8.5 %collective-permute-start.22 = (bf16[144,896]{1,0:T(8,128)(2,1)S(1)}, bf16[144,896]{1,0:T(8,128)(2,1)S(1)}, u32[]{:S(2)}, u32[]{:S(2)}) collective-permute-start(bf16[144,896]{1,0:T(8,128)(2,1)S(1)} %add_convert_fusion.refs_0_.refs_1_), channel_id=1, source_target_pairs={{0,4},{4,8},{8,12},{12,14},{14,10},{10,6},{6,2},{2,0},{1,5},{5,9},... | collective-permute-start | bytes 774152 | tf_op jit(solution)/shard_map/ppermute | solution.py:802
  63.9 8.2 %collective-permute-start.23 = (bf16[144,896]{1,0:T(8,128)(2,1)S(1)}, bf16[144,896]{1,0:T(8,128)(2,1)S(1)}, u32[]{:S(2)}, u32[]{:S(2)}) collective-permute-start(bf16[144,896]{1,0:T(8,128)(2,1)S(1)} %add_convert_fusion.refs_0_.refs_1_), channel_id=1, source_target_pairs={{4,0},{8,4},{12,8},{14,12},{10,14},{6,10},{2,6},{0,2},{5,1},{9,5},... | collective-permute-start | bytes 774152 | tf_op jit(solution)/shard_map/ppermute | solution.py:805
  72.1 2.2 %collective-permute-start.27 = (bf16[288,896]{1,0:T(8,128)(2,1)S(1)}, bf16[288,896]{1,0:T(8,128)(2,1)S(1)}, u32[]{:S(2)}, u32[]{:S(2)}) collective-permute-start(bf16[288,896]{1,0:T(8,128)(2,1)S(1)} %pad_maximum_fusion), channel_id=1, source_target_pairs={{0,1},{1,0},{2,3},{3,2},{4,5},{5,4},{6,7},{7,6},{8,9},{9,8},{10,11... | collective-permute-start | bytes 1548296 | tf_op jit(solution)/shard_map/ppermute | solution.py:808
  72.2 8.6 %collective-permute-start.25 = (bf16[144,896]{1,0:T(8,128)(2,1)S(1)}, bf16[144,896]{1,0:T(8,128)(2,1)S(1)}, u32[]{:S(2)}, u32[]{:S(2)}) collective-permute-start(bf16[144,896]{1,0:T(8,128)(2,1)S(1)} %collective-permute-done.22.refs_0_.refs_2_.refs_3_), channel_id=1, source_target_pairs={{0,4},{4,8},{8,12},{12,14},{14,10},{10,6},{6,2},{2,0},{1,5},{5,9},... | collective-permute-start | bytes 774152 | tf_op jit(solution)/shard_map/ppermute | solution.py:802
  72.5 8.3 %collective-permute-start.26 = (bf16[144,896]{1,0:T(8,128)(2,1)S(1)}, bf16[144,896]{1,0:T(8,128)(2,1)S(1)}, u32[]{:S(2)}, u32[]{:S(2)}) collective-permute-start(bf16[144,896]{1,0:T(8,128)(2,1)S(1)} %collective-permute-done.23.refs_1_.refs_4_.refs_5_), channel_id=1, source_target_pairs={{4,0},{8,4},{12,8},{14,12},{10,14},{6,10},{2,6},{0,2},{5,1},{9,5},... | collective-permute-start | bytes 774152 | tf_op jit(solution)/shard_map/ppermute | solution.py:805
  80.9 2.2 %collective-permute-start.30 = (bf16[288,896]{1,0:T(8,128)(2,1)S(1)}, bf16[288,896]{1,0:T(8,128)(2,1)S(1)}, u32[]{:S(2)}, u32[]{:S(2)}) collective-permute-start(bf16[288,896]{1,0:T(8,128)(2,1)S(1)} %pad_maximum_fusion.1), channel_id=1, source_target_pairs={{0,1},{1,0},{2,3},{3,2},{4,5},{5,4},{6,7},{7,6},{8,9},{9,8},{10,11... | collective-permute-start | bytes 1548296 | tf_op jit(solution)/shard_map/ppermute | solution.py:808
  80.9 8.6 %collective-permute-start.28 = (bf16[144,896]{1,0:T(8,128)(2,1)S(1)}, bf16[144,896]{1,0:T(8,128)(2,1)S(1)}, u32[]{:S(2)}, u32[]{:S(2)}) collective-permute-start(bf16[144,896]{1,0:T(8,128)(2,1)S(1)} %collective-permute-done.25.refs_0_.refs_6_.refs_7_), channel_id=1, source_target_pairs={{0,4},{4,8},{8,12},{12,14},{14,10},{10,6},{6,2},{2,0},{1,5},{5,9},... | collective-permute-start | bytes 774152 | tf_op jit(solution)/shard_map/ppermute | solution.py:802
  81.4 8.3 %collective-permute-start.29 = (bf16[144,896]{1,0:T(8,128)(2,1)S(1)}, bf16[144,896]{1,0:T(8,128)(2,1)S(1)}, u32[]{:S(2)}, u32[]{:S(2)}) collective-permute-start(bf16[144,896]{1,0:T(8,128)(2,1)S(1)} %collective-permute-done.26.refs_1_.refs_8_.refs_9_), channel_id=1, source_target_pairs={{4,0},{8,4},{12,8},{14,12},{10,14},{6,10},{2,6},{0,2},{5,1},{9,5},... | collective-permute-start | bytes 774152 | tf_op jit(solution)/shard_map/ppermute | solution.py:805
  89.7 2.2 %collective-permute-start.33 = (bf16[288,896]{1,0:T(8,128)(2,1)S(1)}, bf16[288,896]{1,0:T(8,128)(2,1)S(1)}, u32[]{:S(2)}, u32[]{:S(2)}) collective-permute-start(bf16[288,896]{1,0:T(8,128)(2,1)S(1)} %pad_maximum_fusion.2), channel_id=1, source_target_pairs={{0,1},{1,0},{2,3},{3,2},{4,5},{5,4},{6,7},{7,6},{8,9},{9,8},{10,11... | collective-permute-start | bytes 1548296 | tf_op jit(solution)/shard_map/ppermute | solution.py:808
  89.8 7.1 %collective-permute-start.31 = (bf16[80,896]{1,0:T(8,128)(2,1)S(1)}, bf16[80,896]{1,0:T(8,128)(2,1)S(1)}, u32[]{:S(2)}, u32[]{:S(2)}) collective-permute-start(bf16[80,896]{1,0:T(8,128)(2,1)S(1)} %slice.18), channel_id=1, source_target_pairs={{0,4},{4,8},{8,12},{12,14},{14,10},{10,6},{6,2},{2,0},{1,5},{5,9},... | collective-permute-start | bytes 430088 | tf_op jit(solution)/shard_map/ppermute | solution.py:802
  91.5 5.3 %collective-permute-start.32 = (bf16[64,896]{1,0:T(8,128)(2,1)S(1)}, bf16[64,896]{1,0:T(8,128)(2,1)S(1)}, u32[]{:S(2)}, u32[]{:S(2)}) collective-permute-start(bf16[64,896]{1,0:T(8,128)(2,1)S(1)} %slice.19), channel_id=1, source_target_pairs={{4,0},{8,4},{12,8},{14,12},{10,14},{6,10},{2,6},{0,2},{5,1},{9,5},... | collective-permute-start | bytes 344072 | tf_op jit(solution)/shard_map/ppermute | solution.py:805
  96.9 1.6 %collective-permute-start.34 = (bf16[80,896]{1,0:T(8,128)(2,1)S(1)}, bf16[80,896]{1,0:T(8,128)(2,1)S(1)}, u32[]{:S(2)}, u32[]{:S(2)}) collective-permute-start(bf16[80,896]{1,0:T(8,128)(2,1)S(1)} %collective-permute-done.31.refs_0_), channel_id=1, source_target_pairs={{0,1},{1,0},{2,3},{3,2},{4,5},{5,4},{6,7},{7,6},{8,9},{9,8},{10,11... | collective-permute-start | bytes 430088 | tf_op jit(solution)/shard_map/ppermute | solution.py:808
  96.9 1.5 %collective-permute-start.35 = (bf16[64,896]{1,0:T(8,128)(2,1)S(1)}, bf16[64,896]{1,0:T(8,128)(2,1)S(1)}, u32[]{:S(2)}, u32[]{:S(2)}) collective-permute-start(bf16[64,896]{1,0:T(8,128)(2,1)S(1)} %collective-permute-done.32.refs_1_), channel_id=1, source_target_pairs={{0,1},{1,0},{2,3},{3,2},{4,5},{5,4},{6,7},{7,6},{8,9},{9,8},{10,11... | collective-permute-start | bytes 344072 | tf_op jit(solution)/shard_map/ppermute | solution.py:808
  101.6 4.4 %collective-permute-start.46 = (bf16[144,3584]{1,0:T(8,128)(2,1)S(1)}, bf16[144,3584]{1,0:T(8,128)(2,1)S(1)}, u32[]{:S(2)}, u32[]{:S(2)}) collective-permute-start(bf16[144,3584]{1,0:T(8,128)(2,1)S(1)} %contract.7), channel_id=1, source_target_pairs={{0,1},{1,0},{2,3},{3,2},{4,5},{5,4},{6,7},{7,6},{8,9},{9,8},{10,11... | collective-permute-start | bytes 3096584 | tf_op jit(solution)/shard_map/ppermute | solution.py:808
  103.2 6.7 %collective-permute-start.36 = (bf16[144,3584]{1,0:T(8,128)(2,1)S(1)}, bf16[144,3584]{1,0:T(8,128)(2,1)S(1)}, u32[]{:S(2)}, u32[]{:S(2)}) collective-permute-start(bf16[144,3584]{1,0:T(8,128)(2,1)S(1)} %contract.6), channel_id=1, source_target_pairs={{0,1},{1,0},{2,3},{3,2},{4,5},{5,4},{6,7},{7,6},{8,9},{9,8},{10,11... | collective-permute-start | bytes 3096584 | tf_op jit(solution)/shard_map/ppermute | solution.py:808
  106.9 5.9 %collective-permute-start.48 = (bf16[16,3584]{1,0:T(8,128)(2,1)S(1)}, bf16[16,3584]{1,0:T(8,128)(2,1)S(1)}, u32[]{:S(2)}, u32[]{:S(2)}) collective-permute-start(bf16[16,3584]{1,0:T(8,128)(2,1)S(1)} %convert_element_type.157), channel_id=1, source_target_pairs={{4,0},{8,4},{12,8},{14,12},{10,14},{6,10},{2,6},{0,2},{5,1},{9,5},... | collective-permute-start | bytes 344072 | tf_op jit(solution)/shard_map/ppermute | solution.py:805
  108.3 5.4 %collective-permute-start.47 = (bf16[16,3584]{1,0:T(8,128)(2,1)S(1)}, bf16[16,3584]{1,0:T(8,128)(2,1)S(1)}, u32[]{:S(2)}, u32[]{:S(2)}) collective-permute-start(bf16[16,3584]{1,0:T(8,128)(2,1)S(1)} %convert_element_type.156), channel_id=1, source_target_pairs={{0,4},{4,8},{8,12},{12,14},{14,10},{10,6},{6,2},{2,0},{1,5},{5,9},... | collective-permute-start | bytes 344072 | tf_op jit(solution)/shard_map/ppermute | solution.py:802
  110.7 5.1 %collective-permute-start.38 = (bf16[16,3584]{1,0:T(8,128)(2,1)S(1)}, bf16[16,3584]{1,0:T(8,128)(2,1)S(1)}, u32[]{:S(2)}, u32[]{:S(2)}) collective-permute-start(bf16[16,3584]{1,0:T(8,128)(2,1)S(1)} %convert_element_type.136), channel_id=1, source_target_pairs={{4,0},{8,4},{12,8},{14,12},{10,14},{6,10},{2,6},{0,2},{5,1},{9,5},... | collective-permute-start | bytes 344072 | tf_op jit(solution)/shard_map/ppermute | solution.py:805
  111.5 4.8 %collective-permute-start.37 = (bf16[16,3584]{1,0:T(8,128)(2,1)S(1)}, bf16[16,3584]{1,0:T(8,128)(2,1)S(1)}, u32[]{:S(2)}, u32[]{:S(2)}) collective-permute-start(bf16[16,3584]{1,0:T(8,128)(2,1)S(1)} %convert_element_type.135), channel_id=1, source_target_pairs={{0,4},{4,8},{8,12},{12,14},{14,10},{10,6},{6,2},{2,0},{1,5},{5,9},... | collective-permute-start | bytes 344072 | tf_op jit(solution)/shard_map/ppermute | solution.py:802
  113.7 5.0 %collective-permute-start.50 = (bf16[16,3584]{1,0:T(8,128)(2,1)S(1)}, bf16[16,3584]{1,0:T(8,128)(2,1)S(1)}, u32[]{:S(2)}, u32[]{:S(2)}) collective-permute-start(bf16[16,3584]{1,0:T(8,128)(2,1)S(1)} %add_convert_fusion.5), channel_id=1, source_target_pairs={{4,0},{8,4},{12,8},{14,12},{10,14},{6,10},{2,6},{0,2},{5,1},{9,5},... | collective-permute-start | bytes 344072 | tf_op jit(solution)/shard_map/ppermute | solution.py:805
  115.6 5.1 %collective-permute-start.49 = (bf16[16,3584]{1,0:T(8,128)(2,1)S(1)}, bf16[16,3584]{1,0:T(8,128)(2,1)S(1)}, u32[]{:S(2)}, u32[]{:S(2)}) collective-permute-start(bf16[16,3584]{1,0:T(8,128)(2,1)S(1)} %add_convert_fusion.6), channel_id=1, source_target_pairs={{0,4},{4,8},{8,12},{12,14},{14,10},{10,6},{6,2},{2,0},{1,5},{5,9},... | collective-permute-start | bytes 344072 | tf_op jit(solution)/shard_map/ppermute | solution.py:802
  116.3 7.6 %collective-permute-start.39 = (bf16[16,3584]{1,0:T(8,128)(2,1)S(1)}, bf16[16,3584]{1,0:T(8,128)(2,1)S(1)}, u32[]{:S(2)}, u32[]{:S(2)}) collective-permute-start(bf16[16,3584]{1,0:T(8,128)(2,1)S(1)} %add_convert_fusion.12), channel_id=1, source_target_pairs={{0,4},{4,8},{8,12},{12,14},{14,10},{10,6},{6,2},{2,0},{1,5},{5,9},... | collective-permute-start | bytes 344072 | tf_op jit(solution)/shard_map/ppermute | solution.py:802
  118.0 6.0 %collective-permute-start.40 = (bf16[16,3584]{1,0:T(8,128)(2,1)S(1)}, bf16[16,3584]{1,0:T(8,128)(2,1)S(1)}, u32[]{:S(2)}, u32[]{:S(2)}) collective-permute-start(bf16[16,3584]{1,0:T(8,128)(2,1)S(1)} %add_convert_fusion.11), channel_id=1, source_target_pairs={{4,0},{8,4},{12,8},{14,12},{10,14},{6,10},{2,6},{0,2},{5,1},{9,5},... | collective-permute-start | bytes 344072 | tf_op jit(solution)/shard_map/ppermute | solution.py:805
  120.7 5.4 %collective-permute-start.52 = (bf16[16,3584]{1,0:T(8,128)(2,1)S(1)}, bf16[16,3584]{1,0:T(8,128)(2,1)S(1)}, u32[]{:S(2)}, u32[]{:S(2)}) collective-permute-start(bf16[16,3584]{1,0:T(8,128)(2,1)S(1)} %add_convert_fusion.3), channel_id=1, source_target_pairs={{4,0},{8,4},{12,8},{14,12},{10,14},{6,10},{2,6},{0,2},{5,1},{9,5},... | collective-permute-start | bytes 344072 | tf_op jit(solution)/shard_map/ppermute | solution.py:805
  122.0 5.6 %collective-permute-start.51 = (bf16[16,3584]{1,0:T(8,128)(2,1)S(1)}, bf16[16,3584]{1,0:T(8,128)(2,1)S(1)}, u32[]{:S(2)}, u32[]{:S(2)}) collective-permute-start(bf16[16,3584]{1,0:T(8,128)(2,1)S(1)} %add_convert_fusion.4), channel_id=1, source_target_pairs={{0,4},{4,8},{8,12},{12,14},{14,10},{10,6},{6,2},{2,0},{1,5},{5,9},... | collective-permute-start | bytes 344072 | tf_op jit(solution)/shard_map/ppermute | solution.py:802
  124.0 5.8 %collective-permute-start.42 = (bf16[16,3584]{1,0:T(8,128)(2,1)S(1)}, bf16[16,3584]{1,0:T(8,128)(2,1)S(1)}, u32[]{:S(2)}, u32[]{:S(2)}) collective-permute-start(bf16[16,3584]{1,0:T(8,128)(2,1)S(1)} %add_convert_fusion.9), channel_id=1, source_target_pairs={{4,0},{8,4},{12,8},{14,12},{10,14},{6,10},{2,6},{0,2},{5,1},{9,5},... | collective-permute-start | bytes 344072 | tf_op jit(solution)/shard_map/ppermute | solution.py:805
  124.3 6.0 %collective-permute-start.41 = (bf16[16,3584]{1,0:T(8,128)(2,1)S(1)}, bf16[16,3584]{1,0:T(8,128)(2,1)S(1)}, u32[]{:S(2)}, u32[]{:S(2)}) collective-permute-start(bf16[16,3584]{1,0:T(8,128)(2,1)S(1)} %add_convert_fusion.10), channel_id=1, source_target_pairs={{0,4},{4,8},{8,12},{12,14},{14,10},{10,6},{6,2},{2,0},{1,5},{5,9},... | collective-permute-start | bytes 344072 | tf_op jit(solution)/shard_map/ppermute | solution.py:802
  127.7 5.4 %collective-permute-start.53 = (bf16[16,3584]{1,0:T(8,128)(2,1)S(1)}, bf16[16,3584]{1,0:T(8,128)(2,1)S(1)}, u32[]{:S(2)}, u32[]{:S(2)}) collective-permute-start(bf16[16,3584]{1,0:T(8,128)(2,1)S(1)} %add_convert_fusion.2), channel_id=1, source_target_pairs={{0,4},{4,8},{8,12},{12,14},{14,10},{10,6},{6,2},{2,0},{1,5},{5,9},... | collective-permute-start | bytes 344072 | tf_op jit(solution)/shard_map/ppermute | solution.py:802
  128.5 4.8 %collective-permute-start.54 = (bf16[16,3584]{1,0:T(8,128)(2,1)S(1)}, bf16[16,3584]{1,0:T(8,128)(2,1)S(1)}, u32[]{:S(2)}, u32[]{:S(2)}) collective-permute-start(bf16[16,3584]{1,0:T(8,128)(2,1)S(1)} %add_convert_fusion.1), channel_id=1, source_target_pairs={{4,0},{8,4},{12,8},{14,12},{10,14},{6,10},{2,6},{0,2},{5,1},{9,5},... | collective-permute-start | bytes 344072 | tf_op jit(solution)/shard_map/ppermute | solution.py:805
  130.4 4.8 %collective-permute-start.43 = (bf16[16,3584]{1,0:T(8,128)(2,1)S(1)}, bf16[16,3584]{1,0:T(8,128)(2,1)S(1)}, u32[]{:S(2)}, u32[]{:S(2)}) collective-permute-start(bf16[16,3584]{1,0:T(8,128)(2,1)S(1)} %add_convert_fusion.8), channel_id=1, source_target_pairs={{0,4},{4,8},{8,12},{12,14},{14,10},{10,6},{6,2},{2,0},{1,5},{5,9},... | collective-permute-start | bytes 344072 | tf_op jit(solution)/shard_map/ppermute | solution.py:802
  131.4 4.8 %collective-permute-start.44 = (bf16[16,3584]{1,0:T(8,128)(2,1)S(1)}, bf16[16,3584]{1,0:T(8,128)(2,1)S(1)}, u32[]{:S(2)}, u32[]{:S(2)}) collective-permute-start(bf16[16,3584]{1,0:T(8,128)(2,1)S(1)} %add_convert_fusion.7), channel_id=1, source_target_pairs={{4,0},{8,4},{12,8},{14,12},{10,14},{6,10},{2,6},{0,2},{5,1},{9,5},... | collective-permute-start | bytes 344072 | tf_op jit(solution)/shard_map/ppermute | solution.py:805
  136.4 1.4 collective-permute-start.45
  136.6 1.5 %collective-permute-start.55 = (bf16[16,3584]{1,0:T(8,128)(2,1)S(1)}, bf16[16,3584]{1,0:T(8,128)(2,1)S(1)}, u32[]{:S(2)}, u32[]{:S(2)}) collective-permute-start(bf16[16,3584]{1,0:T(8,128)(2,1)S(1)} %get-tuple-element.271), channel_id=1, source_target_pairs={{0,1},{1,0},{2,3},{3,2},{4,5},{5,4},{6,7},{7,6},{8,9},{9,8},{10,11... | collective-permute-start | bytes 344072 | tf_op jit(solution)/shard_map/ppermute | solution.py:808
  (2 other events, 6.8 us)

commit v14 on v13

--- a/solution.py
+++ b/solution.py
@@ -855,7 +855,7 @@
             behind.append(send_next(out_f))
             ahead.append(send_prev(out_b))
     gathered = [[main] + behind + ahead + [extra] for _, main, extra, behind, ahead in chains]
-    gathered[0][reach], pieces = lax.optimization_barrier((gathered[0][reach], pieces))
+    gathered[0][2], pieces = lax.optimization_barrier((gathered[0][2], pieces))
     shared = swap(share(tab, packed[0], pieces, cores))
     gathered[0], shared = lax.optimization_barrier((gathered[0], shared))
     for part in range(2):

time: 139 us -> 137 us (0.986)
  waiting for transfers between devices: 42.4 us -> 37.7 us
  starting transfers between devices: 51.7 us -> 54 us
    ppermute x20, starting transfers between devices: 26.7 us -> 17.9 us  [send_prev(): return lax.ppermute(x, 'blk', backward)]
    ppermute x20, starting transfers between devices: 18.3 us -> 25.6 us  [send_next(): return lax.ppermute(x, 'blk', forward)]
    ppermute x20, waiting for transfers between devices: 31 us -> 24.8 us  [send_next(): return lax.ppermute(x, 'blk', forward)]
    ppermute x12, starting transfers between devices: 2.38 us -> 6.23 us  [swap(): return lax.ppermute(x, 'head', exchange)]
    ppermute x20, waiting for transfers between devices: 8.42 us -> 10.1 us  [send_prev(): return lax.ppermute(x, 'blk', backward)]
  transfers between devices with their start and end apart: 56 -> 56, of which waited for: 29 -> 30; matrix products, arithmetic and copies ran while one was open for 1% -> 1% of each run, Pallas kernels for 19% -> 19%
where the time goes in v14:
time: 137 us
  starting transfers between devices  54 us (39%)
  Pallas kernels  39.1 us (29%)
  waiting for transfers between devices  37.7 us (28%)
  between operations  2.65 us (2%)
  other arithmetic  2.36 us (2%)
    ppermute x20, starting transfers between devices, send_next(): return lax.ppermute(x, 'blk', forward)  25.6 us
    ppermute x20, waiting for transfers between devices, send_next(): return lax.ppermute(x, 'blk', forward)  24.8 us
    ppermute x20, starting transfers between devices, send_prev(): return lax.ppermute(x, 'blk', backward)  17.9 us
    pallas_call x2, Pallas kernels, attend(): pl.pallas_call(functools.partial(attend_kernel, table, order, heads, part...  14.1 us
    pallas_call x5, Pallas kernels, expand(): pl.pallas_call(functools.partial(expand_kernel, pieces, len(theirs), firs...  12.1 us
    ppermute x20, waiting for transfers between devices, send_prev(): return lax.ppermute(x, 'blk', backward)  10.1 us
    ppermute x12, starting transfers between devices, swap(): return lax.ppermute(x, 'head', exchange)  6.23 us
    pallas_call x4, Pallas kernels, contract(): pl.pallas_call(functools.partial(contract_kernel, part * columns), grid=(...  5 us
  transfers between devices with their start and end apart: 56, of which 30 were waited for; matrix products, arithmetic and copies ran while one was open for 1% of the time, Pallas kernels for 19%

profile of v14, /device:TPU:0, one launch (start us, length us, event | category | flops | bytes accessed | tf_op | source)
XLA Modules:
  0.0 136.7 jit_solution(3692021310080143794)
XLA Ops:
  0.7 0.8 concatenate.24.refs_0_
  1.5 8.2 %attend.2 = (s32[60]{0:T(128)S(1)}, bf16[32,2048]{1,0:T(8,128)(2,1)S(1)}, bf16[32,2048]{1,0:T(8,128)(2,1)S(1)}, bf16[32,2048]{1,0:T(8,128)(2,1)S(1)}, bf16[128,5...) custom-call(s32[26]{0:T(128)S(1)} %concatenate.24.refs_0_, ...), custom_call_target="tpu_custom_call" | custom-call | flops 713031680 | bytes 4456448 | tf_op jit(solution)/shard_map/attend/pallas_call | solution.py:344
  9.7 3.1 %collective-permute-start.11 = (bf16[32,2048]{1,0:T(8,128)(2,1)S(1)}, bf16[32,2048]{1,0:T(8,128)(2,1)S(1)}, u32[]{:S(2)}, u32[]{:S(2)}) collective-permute-start(bf16[32,2048]{1,0:T(8,128)(2,1)S(1)} %get-tuple-element.162), channel_id=1, source_target_pairs={{0,4},{4,8},{8,12},{12,14},{14,10},{10,6},{6,2},{2,0},{1,5},{5,9},... | collective-permute-start | bytes 393224 | tf_op jit(solution)/shard_map/ppermute | solution.py:802
  13.4 2.0 %collective-permute-start.1 = (bf16[64,896]{1,0:T(8,128)(2,1)S(1)}, bf16[64,896]{1,0:T(8,128)(2,1)S(1)}, u32[]{:S(2)}, u32[]{:S(2)}) collective-permute-start(bf16[64,896]{1,0:T(8,128)(2,1)S(1)} %get-tuple-element.141), channel_id=1, source_target_pairs={{0,4},{1,13},{2,6},{3,15},{4,0},{5,9},{6,2},{7,11},{8,12},{9,5},{1... | collective-permute-start | bytes 344072 | tf_op jit(solution)/shard_map/ppermute | solution.py:829
  15.4 1.5 %collective-permute-start.2 = (bf16[64,896]{1,0:T(8,128)(2,1)S(1)}, bf16[64,896]{1,0:T(8,128)(2,1)S(1)}, u32[]{:S(2)}, u32[]{:S(2)}) collective-permute-start(bf16[64,896]{1,0:T(8,128)(2,1)S(1)} %get-tuple-element.142), channel_id=1, source_target_pairs={{0,6},{1,15},{2,4},{3,13},{4,2},{5,11},{6,0},{7,9},{8,14},{9,7},{1... | collective-permute-start | bytes 344072 | tf_op jit(solution)/shard_map/ppermute | solution.py:829
  17.7 5.9 %attend.3 = (bf16[32,2048]{1,0:T(8,128)(2,1)S(1)}, bf16[32,2048]{1,0:T(8,128)(2,1)S(1)}, bf16[32,2048]{1,0:T(8,128)(2,1)S(1)}) custom-call(s32[60]{0:T(128)S(1)} %get-tuple-element.137.tab.refs_0_, bf16[64,18432]{1,0:T(8,128)(2,1)} %refs_1_.3, bf16[8,576,256]{2,1,0:T(8,128)(2,1)} %refs_2_.3, bf16[64,576]{1,0:T(8,128)(2,1)} %bitcast.33, ...), custom_call_target="tpu_custom_call" | custom-call | flops 713031680 | bytes 4456448 | tf_op jit(solution)/shard_map/attend/pallas_call | solution.py:344
  23.7 0.7 collective-permute-start.14
  24.4 1.9 %collective-permute-start.4 = (bf16[32,2048]{1,0:T(8,128)(2,1)S(1)}, bf16[32,2048]{1,0:T(8,128)(2,1)S(1)}, u32[]{:S(2)}, u32[]{:S(2)}) collective-permute-start(bf16[32,2048]{1,0:T(8,128)(2,1)S(1)} %get-tuple-element.153.refs_0_), channel_id=1, source_target_pairs={{4,0},{8,4},{12,8},{14,12},{10,14},{6,10},{2,6},{0,2},{5,1},{9,5},... | collective-permute-start | bytes 393224 | tf_op jit(solution)/shard_map/ppermute | solution.py:805
  26.5 2.0 %collective-permute-start.13 = (bf16[32,2048]{1,0:T(8,128)(2,1)S(1)}, bf16[32,2048]{1,0:T(8,128)(2,1)S(1)}, u32[]{:S(2)}, u32[]{:S(2)}) collective-permute-start(bf16[32,2048]{1,0:T(8,128)(2,1)S(1)} %broadcast_select_fusion.5), channel_id=1, source_target_pairs={{0,4},{4,8},{8,12},{12,14},{14,10},{10,6},{6,2},{2,0},{1,5},{5,9},... | collective-permute-start | bytes 393224 | tf_op jit(solution)/shard_map/ppermute | solution.py:802
  28.6 2.7 %collective-permute-done.3.refs_1_ = bf16[32,2048]{1,0:T(8,128)(2,1)S(1)} collective-permute-done((bf16[32,2048]{1,0:T(8,128)(2,1)S(1)}, bf16[32,2048]{1,0:T(8,128)(2,1)S(1)}, u32[]{:S(2)}, u32[]{:S(2)}) %collective-permute-start.3) | collective-permute-done | bytes 131104 | tf_op jit(solution)/shard_map/ppermute | solution.py:802
  31.3 2.2 %collective-permute-start.6 = (bf16[32,2048]{1,0:T(8,128)(2,1)S(1)}, bf16[32,2048]{1,0:T(8,128)(2,1)S(1)}, u32[]{:S(2)}, u32[]{:S(2)}) collective-permute-start(bf16[32,2048]{1,0:T(8,128)(2,1)S(1)} %broadcast_select_fusion.10), channel_id=1, source_target_pairs={{4,0},{8,4},{12,8},{14,12},{10,14},{6,10},{2,6},{0,2},{5,1},{9,5},... | collective-permute-start | bytes 393224 | tf_op jit(solution)/shard_map/ppermute | solution.py:805
  34.0 3.9 %collective-permute-start.20 = (bf16[128,896]{1,0:T(8,128)(2,1)S(1)}, bf16[128,896]{1,0:T(8,128)(2,1)S(1)}, u32[]{:S(2)}, u32[]{:S(2)}) collective-permute-start(bf16[128,896]{1,0:T(8,128)(2,1)S(1)} %share.1), channel_id=1, source_target_pairs={{0,1},{1,0},{2,3},{3,2},{4,5},{5,4},{6,7},{7,6},{8,9},{9,8},{10,11... | collective-permute-start | bytes 688136 | tf_op jit(solution)/shard_map/ppermute | solution.py:808
  38.0 1.2 collective-permute-start.17
  39.2 0.9 collective-permute-start.16
  40.8 2.4 %collective-permute-start.8 = (bf16[32,2048]{1,0:T(8,128)(2,1)S(1)}, bf16[32,2048]{1,0:T(8,128)(2,1)S(1)}, u32[]{:S(2)}, u32[]{:S(2)}) collective-permute-start(bf16[32,2048]{1,0:T(8,128)(2,1)S(1)} %broadcast_select_fusion.8), channel_id=1, source_target_pairs={{4,0},{8,4},{12,8},{14,12},{10,14},{6,10},{2,6},{0,2},{5,1},{9,5},... | collective-permute-start | bytes 393224 | tf_op jit(solution)/shard_map/ppermute | solution.py:805
  43.2 1.0 collective-permute-done.17.refs_7_
  44.5 1.6 %collective-permute-start.18 = (bf16[32,2048]{1,0:T(8,128)(2,1)S(1)}, bf16[32,2048]{1,0:T(8,128)(2,1)S(1)}, u32[]{:S(2)}, u32[]{:S(2)}) collective-permute-start(bf16[32,2048]{1,0:T(8,128)(2,1)S(1)} %broadcast_select_fusion.1), channel_id=1, source_target_pairs={{0,4},{4,8},{8,12},{12,14},{14,10},{10,6},{6,2},{2,0},{1,5},{5,9},... | collective-permute-start | bytes 393224 | tf_op jit(solution)/shard_map/ppermute | solution.py:802
  47.0 2.5 %collective-permute-done.7.refs_3_ = bf16[32,2048]{1,0:T(8,128)(2,1)S(1)} collective-permute-done((bf16[32,2048]{1,0:T(8,128)(2,1)S(1)}, bf16[32,2048]{1,0:T(8,128)(2,1)S(1)}, u32[]{:S(2)}, u32[]{:S(2)}) %collective-permute-start.7) | collective-permute-done | bytes 131104 | tf_op jit(solution)/shard_map/ppermute | solution.py:802
  49.9 1.7 %collective-permute-start.9 = (bf16[32,2048]{1,0:T(8,128)(2,1)S(1)}, bf16[32,2048]{1,0:T(8,128)(2,1)S(1)}, u32[]{:S(2)}, u32[]{:S(2)}) collective-permute-start(bf16[32,2048]{1,0:T(8,128)(2,1)S(1)} %broadcast_select_fusion.7), channel_id=1, source_target_pairs={{0,4},{4,8},{8,12},{12,14},{14,10},{10,6},{6,2},{2,0},{1,5},{5,9},... | collective-permute-start | bytes 393224 | tf_op jit(solution)/shard_map/ppermute | solution.py:802
  52.0 1.9 %project.2.refs_10_ = f32[288,896]{1,0:T(8,128)S(1)} custom-call(s32[60]{0:T(128)S(1)} %get-tuple-element.137.tab.refs_0_, bf16[32,2048]{1,0:T(8,128)(2,1)S(1)} %get-tuple-element.180.refs_0_, bf16[32,2048]{1,0:T(8,128)(2,1)S(1)} %collective-permute-done.11.refs_1_, bf16[32,2048]{1,0:T(8,128)(2,1)S(1)} %collective-permute-done.13.refs_2_, ...), custom_call_target="tpu_custom_call" | custom-call | flops 1056964608 | bytes 4849664 | tf_op jit(solution)/shard_map/project/pallas_call | solution.py:497
  54.9 2.0 %project.3 = (f32[144,896]{1,0:T(8,128)S(1)}, bf16[144,896]{1,0:T(8,128)(2,1)S(1)}) custom-call(s32[60]{0:T(128)S(1)} %get-tuple-element.137.tab.refs_0_, bf16[32,2048]{1,0:T(8,128)(2,1)S(1)} %get-tuple-element.153.refs_0_, bf16[32,2048]{1,0:T(8,128)(2,1)S(1)} %collective-permute-done.3.refs_1_, bf16[32,2048]{1,0:T(8,128)(2,1)S(1)} %collective-permute-done.5.refs_2_, ...), custom_call_target="tpu_custom_call" | custom-call | flops 1056964608 | bytes 4849664 | tf_op jit(solution)/shard_map/project/pallas_call | solution.py:507
  57.6 0.9 collective-permute-done.21
  58.8 1.7 %collective-permute-start.22 = (bf16[144,896]{1,0:T(8,128)(2,1)S(1)}, bf16[144,896]{1,0:T(8,128)(2,1)S(1)}, u32[]{:S(2)}, u32[]{:S(2)}) collective-permute-start(bf16[144,896]{1,0:T(8,128)(2,1)S(1)} %add_convert_fusion.refs_0_.refs_1_), channel_id=1, source_target_pairs={{0,4},{4,8},{8,12},{12,14},{14,10},{10,6},{6,2},{2,0},{1,5},{5,9},... | collective-permute-start | bytes 774152 | tf_op jit(solution)/shard_map/ppermute | solution.py:802
  61.1 1.7 %expand.5 = (f32[288,576]{1,0:T(8,128)S(1)}, f32[288,576]{1,0:T(8,128)S(1)}, f32[288,1]{1,0:T(8,128)S(1)}) custom-call(s32[60]{0:T(128)S(1)} %get-tuple-element.137.tab.refs_0_, bf16[144,896]{1,0:T(8,128)(2,1)S(1)} %add_convert_fusion.refs_0_.refs_1_, bf16[144,896]{1,0:T(8,128)(2,1)S(1)} %collective-permute-done.24.refs_1_, f32[8,1,896]{2,1,0:T(1,128)S(1)} %bitcast.27, ...), custom_call_target="tpu_custom_call" | custom-call | flops 1 | bytes 1 | tf_op jit(solution)/shard_map/expand/pallas_call | solution.py:658
  62.7 4.9 %collective-permute-done.22.refs_0_.refs_2_.refs_3_ = bf16[144,896]{1,0:T(8,128)(2,1)S(1)} collective-permute-done((bf16[144,896]{1,0:T(8,128)(2,1)S(1)}, bf16[144,896]{1,0:T(8,128)(2,1)S(1)}, u32[]{:S(2)}, u32[]{:S(2)}) %collective-permute-start.22) | collective-permute-done | bytes 258080 | tf_op jit(solution)/shard_map/ppermute | solution.py:802
  67.6 1.1 collective-permute-done.23.refs_1_.refs_4_.refs_5_
  69.5 1.4 %collective-permute-start.26 = (bf16[144,896]{1,0:T(8,128)(2,1)S(1)}, bf16[144,896]{1,0:T(8,128)(2,1)S(1)}, u32[]{:S(2)}, u32[]{:S(2)}) collective-permute-start(bf16[144,896]{1,0:T(8,128)(2,1)S(1)} %collective-permute-done.23.refs_1_.refs_4_.refs_5_), channel_id=1, source_target_pairs={{4,0},{8,4},{12,8},{14,12},{10,14},{6,10},{2,6},{0,2},{5,1},{9,5},... | collective-permute-start | bytes 774152 | tf_op jit(solution)/shard_map/ppermute | solution.py:805
  70.9 2.9 %expand.6 = (f32[288,576]{1,0:T(8,128)S(1)}, f32[288,576]{1,0:T(8,128)S(1)}, f32[288,1]{1,0:T(8,128)S(1)}) custom-call(s32[60]{0:T(128)S(1)} %get-tuple-element.137.tab.refs_0_, bf16[144,896]{1,0:T(8,128)(2,1)S(1)} %collective-permute-done.22.refs_0_.refs_2_.refs_3_, bf16[144,896]{1,0:T(8,128)(2,1)S(1)} %collective-permute-done.23.refs_1_.refs_4_.refs_5_, ...), custom_call_target="tpu_custom_call" | custom-call | flops 1 | bytes 1 | tf_op jit(solution)/shard_map/expand/pallas_call | solution.py:658
  73.8 3.7 %collective-permute-done.25.refs_0_.refs_6_.refs_7_ = bf16[144,896]{1,0:T(8,128)(2,1)S(1)} collective-permute-done((bf16[144,896]{1,0:T(8,128)(2,1)S(1)}, bf16[144,896]{1,0:T(8,128)(2,1)S(1)}, u32[]{:S(2)}, u32[]{:S(2)}) %collective-permute-start.25) | collective-permute-done | bytes 258080 | tf_op jit(solution)/shard_map/ppermute | solution.py:802
  77.9 1.3 collective-permute-start.28
  79.2 0.8 collective-permute-start.29
  80.0 2.9 %expand.7 = (f32[288,576]{1,0:T(8,128)S(1)}, f32[288,576]{1,0:T(8,128)S(1)}, f32[288,1]{1,0:T(8,128)S(1)}) custom-call(s32[60]{0:T(128)S(1)} %get-tuple-element.137.tab.refs_0_, bf16[144,896]{1,0:T(8,128)(2,1)S(1)} %collective-permute-done.25.refs_0_.refs_6_.refs_7_, bf16[144,896]{1,0:T(8,128)(2,1)S(1)} %collective-permute-done.26.refs_1_.refs_8_.refs_9_, ...), custom_call_target="tpu_custom_call" | custom-call | flops 1 | bytes 1 | tf_op jit(solution)/shard_map/expand/pallas_call | solution.py:658
  82.9 3.7 %collective-permute-done.28.refs_0_.refs_10_.refs_11_ = bf16[144,896]{1,0:T(8,128)(2,1)S(1)} collective-permute-done((bf16[144,896]{1,0:T(8,128)(2,1)S(1)}, bf16[144,896]{1,0:T(8,128)(2,1)S(1)}, u32[]{:S(2)}, u32[]{:S(2)}) %collective-permute-start.28) | collective-permute-done | bytes 258080 | tf_op jit(solution)/shard_map/ppermute | solution.py:802
  86.5 1.0 collective-permute-done.29.refs_1_.refs_12_.refs_13_
  87.7 1.6 %collective-permute-start.31 = (bf16[80,896]{1,0:T(8,128)(2,1)S(1)}, bf16[80,896]{1,0:T(8,128)(2,1)S(1)}, u32[]{:S(2)}, u32[]{:S(2)}) collective-permute-start(bf16[80,896]{1,0:T(8,128)(2,1)S(1)} %slice.18), channel_id=1, source_target_pairs={{0,4},{4,8},{8,12},{12,14},{14,10},{10,6},{6,2},{2,0},{1,5},{5,9},... | collective-permute-start | bytes 430088 | tf_op jit(solution)/shard_map/ppermute | solution.py:802
  89.8 2.9 %expand.8 = (f32[288,576]{1,0:T(8,128)S(1)}, f32[288,576]{1,0:T(8,128)S(1)}, f32[288,1]{1,0:T(8,128)S(1)}) custom-call(s32[60]{0:T(128)S(1)} %get-tuple-element.137.tab.refs_0_, bf16[144,896]{1,0:T(8,128)(2,1)S(1)} %collective-permute-done.28.refs_0_.refs_10_.refs_11_, bf16[144,896]{1,0:T(8,128)(2,1)S(1)} %collective-permute-done.29.refs_1_.refs_12_.refs_13_, ...), custom_call_target="tpu_custom_call" | custom-call | flops 1 | bytes 1 | tf_op jit(solution)/shard_map/expand/pallas_call | solution.py:658
  92.7 1.9 %collective-permute-done.32.refs_1_ = bf16[64,896]{1,0:T(8,128)(2,1)S(1)} collective-permute-done((bf16[64,896]{1,0:T(8,128)(2,1)S(1)}, bf16[64,896]{1,0:T(8,128)(2,1)S(1)}, u32[]{:S(2)}, u32[]{:S(2)}) %collective-permute-start.32) | collective-permute-done | bytes 114720 | tf_op jit(solution)/shard_map/ppermute | solution.py:805
  95.2 1.0 collective-permute-done.35.refs_3_
  96.2 1.8 %expand.9.hidden = bf16[288,576]{1,0:T(8,128)(2,1)S(1)} custom-call(s32[60]{0:T(128)S(1)} %get-tuple-element.137.tab.refs_0_, bf16[80,896]{1,0:T(8,128)(2,1)S(1)} %collective-permute-done.31.refs_0_, bf16[64,896]{1,0:T(8,128)(2,1)S(1)} %collective-permute-done.32.refs_1_, bf16[80,896]{1,0:T(8,128)(2,1)S(1)} %collective-permute-done.34.refs_2_, ...), custom_call_target="tpu_custom_call" | custom-call | flops 1 | bytes 1 | tf_op jit(solution)/shard_map/expand/pallas_call | solution.py:658
  98.0 1.3 contract.7
  99.7 1.2 contract.6
  101.2 1.2 contract.4.mine
  102.4 1.3 contract.5.mine
  103.7 0.8 pick.3
  105.8 1.8 %collective-permute-start.47 = (bf16[16,3584]{1,0:T(8,128)(2,1)S(1)}, bf16[16,3584]{1,0:T(8,128)(2,1)S(1)}, u32[]{:S(2)}, u32[]{:S(2)}) collective-permute-start(bf16[16,3584]{1,0:T(8,128)(2,1)S(1)} %convert_element_type.156), channel_id=1, source_target_pairs={{0,4},{4,8},{8,12},{12,14},{14,10},{10,6},{6,2},{2,0},{1,5},{5,9},... | collective-permute-start | bytes 344072 | tf_op jit(solution)/shard_map/ppermute | solution.py:802
  107.6 0.8 pick.2
  109.0 1.5 %collective-permute-start.37 = (bf16[16,3584]{1,0:T(8,128)(2,1)S(1)}, bf16[16,3584]{1,0:T(8,128)(2,1)S(1)}, u32[]{:S(2)}, u32[]{:S(2)}) collective-permute-start(bf16[16,3584]{1,0:T(8,128)(2,1)S(1)} %convert_element_type.135), channel_id=1, source_target_pairs={{0,4},{4,8},{8,12},{12,14},{14,10},{10,6},{6,2},{2,0},{1,5},{5,9},... | collective-permute-start | bytes 344072 | tf_op jit(solution)/shard_map/ppermute | solution.py:802
  111.3 1.0 collective-permute-start.50
  112.2 1.1 collective-permute-start.49
  114.0 2.0 %collective-permute-start.39 = (bf16[16,3584]{1,0:T(8,128)(2,1)S(1)}, bf16[16,3584]{1,0:T(8,128)(2,1)S(1)}, u32[]{:S(2)}, u32[]{:S(2)}) collective-permute-start(bf16[16,3584]{1,0:T(8,128)(2,1)S(1)} %add_convert_fusion.12), channel_id=1, source_target_pairs={{0,4},{4,8},{8,12},{12,14},{14,10},{10,6},{6,2},{2,0},{1,5},{5,9},... | collective-permute-start | bytes 344072 | tf_op jit(solution)/shard_map/ppermute | solution.py:802
  116.1 1.5 %collective-permute-done.49 = bf16[16,3584]{1,0:T(8,128)(2,1)S(1)} collective-permute-done((bf16[16,3584]{1,0:T(8,128)(2,1)S(1)}, bf16[16,3584]{1,0:T(8,128)(2,1)S(1)}, u32[]{:S(2)}, u32[]{:S(2)}) %collective-permute-start.49) | collective-permute-done | bytes 114720 | tf_op jit(solution)/shard_map/ppermute | solution.py:802
  117.7 1.0 collective-permute-start.52
  118.7 1.1 collective-permute-start.51
  119.8 1.2 collective-permute-done.40
  121.1 0.7 collective-permute-start.42
  121.8 1.4 %collective-permute-start.41 = (bf16[16,3584]{1,0:T(8,128)(2,1)S(1)}, bf16[16,3584]{1,0:T(8,128)(2,1)S(1)}, u32[]{:S(2)}, u32[]{:S(2)}) collective-permute-start(bf16[16,3584]{1,0:T(8,128)(2,1)S(1)} %add_convert_fusion.10), channel_id=1, source_target_pairs={{0,4},{4,8},{8,12},{12,14},{14,10},{10,6},{6,2},{2,0},{1,5},{5,9},... | collective-permute-start | bytes 344072 | tf_op jit(solution)/shard_map/ppermute | solution.py:802
  123.3 0.8 collective-permute-done.51
  124.8 1.4 %collective-permute-start.54 = (bf16[16,3584]{1,0:T(8,128)(2,1)S(1)}, bf16[16,3584]{1,0:T(8,128)(2,1)S(1)}, u32[]{:S(2)}, u32[]{:S(2)}) collective-permute-start(bf16[16,3584]{1,0:T(8,128)(2,1)S(1)} %add_convert_fusion.1), channel_id=1, source_target_pairs={{4,0},{8,4},{12,8},{14,12},{10,14},{6,10},{2,6},{0,2},{5,1},{9,5},... | collective-permute-start | bytes 344072 | tf_op jit(solution)/shard_map/ppermute | solution.py:805
  126.2 0.9 collective-permute-done.42
  127.7 1.3 collective-permute-start.43
  129.0 0.7 collective-permute-start.44
  130.5 2.1 %collective-permute-done.43 = bf16[16,3584]{1,0:T(8,128)(2,1)S(1)} collective-permute-done((bf16[16,3584]{1,0:T(8,128)(2,1)S(1)}, bf16[16,3584]{1,0:T(8,128)(2,1)S(1)}, u32[]{:S(2)}, u32[]{:S(2)}) %collective-permute-start.43) | collective-permute-done | bytes 114720 | tf_op jit(solution)/shard_map/ppermute | solution.py:802
  132.5 1.3 collective-permute-done.44
  135.8 0.9 maximum_select_fusion
  (133 shorter events, 16.8 us)
Async XLA Ops:
  0.0 12.8 %copy-start = (bf16[64,7168]{1,0:T(8,128)(2,1)S(1)}, bf16[64,7168]{1,0:T(8,128)(2,1)}, u32[]{:S(2)}) copy-start(bf16[64,7168]{1,0:T(8,128)(2,1)} %res.1) | copy-start | bytes 2752516
  9.7 16.8 %collective-permute-start.11 = (bf16[32,2048]{1,0:T(8,128)(2,1)S(1)}, bf16[32,2048]{1,0:T(8,128)(2,1)S(1)}, u32[]{:S(2)}, u32[]{:S(2)}) collective-permute-start(bf16[32,2048]{1,0:T(8,128)(2,1)S(1)} %get-tuple-element.162), channel_id=1, source_target_pairs={{0,4},{4,8},{8,12},{12,14},{14,10},{10,6},{6,2},{2,0},{1,5},{5,9},... | collective-permute-start | bytes 393224 | tf_op jit(solution)/shard_map/ppermute | solution.py:802
  13.4 38.6 %slice-start.6 = ((s8[7340032]{0:T(1024)(128)(4,1)}), s8[4194304]{0:T(1024)(128)(4,1)S(1)}, s32[]{:S(2)}) async-start(s8[7340032]{0:T(1024)(128)(4,1)} %bitcast.25), calls=%async_computation.6 | async-start | bytes 8388608
  13.4 10.3 %collective-permute-start = (bf16[64,896]{1,0:T(8,128)(2,1)S(1)}, bf16[64,896]{1,0:T(8,128)(2,1)S(1)}, u32[]{:S(2)}, u32[]{:S(2)}) collective-permute-start(bf16[64,896]{1,0:T(8,128)(2,1)S(1)} %get-tuple-element.140), channel_id=1, source_target_pairs={{0,2},{1,11},{2,0},{3,9},{4,6},{5,15},{6,4},{7,13},{8,10},{9,3},{1... | collective-permute-start | bytes 344072 | tf_op jit(solution)/shard_map/ppermute | solution.py:829
  13.4 10.2 %collective-permute-start.1 = (bf16[64,896]{1,0:T(8,128)(2,1)S(1)}, bf16[64,896]{1,0:T(8,128)(2,1)S(1)}, u32[]{:S(2)}, u32[]{:S(2)}) collective-permute-start(bf16[64,896]{1,0:T(8,128)(2,1)S(1)} %get-tuple-element.141), channel_id=1, source_target_pairs={{0,4},{1,13},{2,6},{3,15},{4,0},{5,9},{6,2},{7,11},{8,12},{9,5},{1... | collective-permute-start | bytes 344072 | tf_op jit(solution)/shard_map/ppermute | solution.py:829
  15.4 8.3 %collective-permute-start.2 = (bf16[64,896]{1,0:T(8,128)(2,1)S(1)}, bf16[64,896]{1,0:T(8,128)(2,1)S(1)}, u32[]{:S(2)}, u32[]{:S(2)}) collective-permute-start(bf16[64,896]{1,0:T(8,128)(2,1)S(1)} %get-tuple-element.142), channel_id=1, source_target_pairs={{0,6},{1,15},{2,4},{3,13},{4,2},{5,11},{6,0},{7,9},{8,14},{9,7},{1... | collective-permute-start | bytes 344072 | tf_op jit(solution)/shard_map/ppermute | solution.py:829
  16.9 9.5 %collective-permute-start.12 = (bf16[32,2048]{1,0:T(8,128)(2,1)S(1)}, bf16[32,2048]{1,0:T(8,128)(2,1)S(1)}, u32[]{:S(2)}, u32[]{:S(2)}) collective-permute-start(bf16[32,2048]{1,0:T(8,128)(2,1)S(1)} %get-tuple-element.180.refs_0_), channel_id=1, source_target_pairs={{4,0},{8,4},{12,8},{14,12},{10,14},{6,10},{2,6},{0,2},{5,1},{9,5},... | collective-permute-start | bytes 393224 | tf_op jit(solution)/shard_map/ppermute | solution.py:805
  17.7 34.3 %slice-start.7 = ((s8[7340032]{0:T(1024)(128)(4,1)}), s8[3145728]{0:T(1024)(128)(4,1)S(1)}, s32[]{:S(2)}) async-start(s8[7340032]{0:T(1024)(128)(4,1)} %bitcast.25), calls=%async_computation.7 | async-start | bytes 6291456
  23.7 9.8 %collective-permute-start.14 = (bf16[64,896]{1,0:T(8,128)(2,1)S(1)}, bf16[64,896]{1,0:T(8,128)(2,1)S(1)}, u32[]{:S(2)}, u32[]{:S(2)}) collective-permute-start(bf16[64,896]{1,0:T(8,128)(2,1)S(1)} %get-tuple-element.166.own), channel_id=1, source_target_pairs={{1,9},{3,11},{5,13},{7,15},{9,1},{11,3},{13,5},{15,7},{17,25},{19,... | collective-permute-start | bytes 344072 | tf_op jit(solution)/shard_map/ppermute | solution.py:829
  24.4 6.9 %collective-permute-start.4 = (bf16[32,2048]{1,0:T(8,128)(2,1)S(1)}, bf16[32,2048]{1,0:T(8,128)(2,1)S(1)}, u32[]{:S(2)}, u32[]{:S(2)}) collective-permute-start(bf16[32,2048]{1,0:T(8,128)(2,1)S(1)} %get-tuple-element.153.refs_0_), channel_id=1, source_target_pairs={{4,0},{8,4},{12,8},{14,12},{10,14},{6,10},{2,6},{0,2},{5,1},{9,5},... | collective-permute-start | bytes 393224 | tf_op jit(solution)/shard_map/ppermute | solution.py:805
  26.3 5.0 %collective-permute-start.3 = (bf16[32,2048]{1,0:T(8,128)(2,1)S(1)}, bf16[32,2048]{1,0:T(8,128)(2,1)S(1)}, u32[]{:S(2)}, u32[]{:S(2)}) collective-permute-start(bf16[32,2048]{1,0:T(8,128)(2,1)S(1)} %get-tuple-element.150), channel_id=1, source_target_pairs={{0,4},{4,8},{8,12},{12,14},{14,10},{10,6},{6,2},{2,0},{1,5},{5,9},... | collective-permute-start | bytes 393224 | tf_op jit(solution)/shard_map/ppermute | solution.py:802
  26.5 7.0 %collective-permute-start.13 = (bf16[32,2048]{1,0:T(8,128)(2,1)S(1)}, bf16[32,2048]{1,0:T(8,128)(2,1)S(1)}, u32[]{:S(2)}, u32[]{:S(2)}) collective-permute-start(bf16[32,2048]{1,0:T(8,128)(2,1)S(1)} %broadcast_select_fusion.5), channel_id=1, source_target_pairs={{0,4},{4,8},{8,12},{12,14},{14,10},{10,6},{6,2},{2,0},{1,5},{5,9},... | collective-permute-start | bytes 393224 | tf_op jit(solution)/shard_map/ppermute | solution.py:802
  28.5 9.5 %collective-permute-start.15 = (bf16[32,2048]{1,0:T(8,128)(2,1)S(1)}, bf16[32,2048]{1,0:T(8,128)(2,1)S(1)}, u32[]{:S(2)}, u32[]{:S(2)}) collective-permute-start(bf16[32,2048]{1,0:T(8,128)(2,1)S(1)} %broadcast_select_fusion.4), channel_id=1, source_target_pairs={{4,0},{8,4},{12,8},{14,12},{10,14},{6,10},{2,6},{0,2},{5,1},{9,5},... | collective-permute-start | bytes 393224 | tf_op jit(solution)/shard_map/ppermute | solution.py:805
  31.3 8.8 %collective-permute-start.6 = (bf16[32,2048]{1,0:T(8,128)(2,1)S(1)}, bf16[32,2048]{1,0:T(8,128)(2,1)S(1)}, u32[]{:S(2)}, u32[]{:S(2)}) collective-permute-start(bf16[32,2048]{1,0:T(8,128)(2,1)S(1)} %broadcast_select_fusion.10), channel_id=1, source_target_pairs={{4,0},{8,4},{12,8},{14,12},{10,14},{6,10},{2,6},{0,2},{5,1},{9,5},... | collective-permute-start | bytes 393224 | tf_op jit(solution)/shard_map/ppermute | solution.py:805
  33.4 7.3 %collective-permute-start.5 = (bf16[32,2048]{1,0:T(8,128)(2,1)S(1)}, bf16[32,2048]{1,0:T(8,128)(2,1)S(1)}, u32[]{:S(2)}, u32[]{:S(2)}) collective-permute-start(bf16[32,2048]{1,0:T(8,128)(2,1)S(1)} %broadcast_select_fusion.11), channel_id=1, source_target_pairs={{0,4},{4,8},{8,12},{12,14},{14,10},{10,6},{6,2},{2,0},{1,5},{5,9},... | collective-permute-start | bytes 393224 | tf_op jit(solution)/shard_map/ppermute | solution.py:802
  34.0 17.6 %collective-permute-start.20 = (bf16[128,896]{1,0:T(8,128)(2,1)S(1)}, bf16[128,896]{1,0:T(8,128)(2,1)S(1)}, u32[]{:S(2)}, u32[]{:S(2)}) collective-permute-start(bf16[128,896]{1,0:T(8,128)(2,1)S(1)} %share.1), channel_id=1, source_target_pairs={{0,1},{1,0},{2,3},{3,2},{4,5},{5,4},{6,7},{7,6},{8,9},{9,8},{10,11... | collective-permute-start | bytes 688136 | tf_op jit(solution)/shard_map/ppermute | solution.py:808
  38.0 6.1 %collective-permute-start.17 = (bf16[32,2048]{1,0:T(8,128)(2,1)S(1)}, bf16[32,2048]{1,0:T(8,128)(2,1)S(1)}, u32[]{:S(2)}, u32[]{:S(2)}) collective-permute-start(bf16[32,2048]{1,0:T(8,128)(2,1)S(1)} %broadcast_select_fusion.2), channel_id=1, source_target_pairs={{4,0},{8,4},{12,8},{14,12},{10,14},{6,10},{2,6},{0,2},{5,1},{9,5},... | collective-permute-start | bytes 393224 | tf_op jit(solution)/shard_map/ppermute | solution.py:805
  39.2 5.3 %collective-permute-start.16 = (bf16[32,2048]{1,0:T(8,128)(2,1)S(1)}, bf16[32,2048]{1,0:T(8,128)(2,1)S(1)}, u32[]{:S(2)}, u32[]{:S(2)}) collective-permute-start(bf16[32,2048]{1,0:T(8,128)(2,1)S(1)} %broadcast_select_fusion.3), channel_id=1, source_target_pairs={{0,4},{4,8},{8,12},{12,14},{14,10},{10,6},{6,2},{2,0},{1,5},{5,9},... | collective-permute-start | bytes 393224 | tf_op jit(solution)/shard_map/ppermute | solution.py:802
  40.8 6.2 %collective-permute-start.8 = (bf16[32,2048]{1,0:T(8,128)(2,1)S(1)}, bf16[32,2048]{1,0:T(8,128)(2,1)S(1)}, u32[]{:S(2)}, u32[]{:S(2)}) collective-permute-start(bf16[32,2048]{1,0:T(8,128)(2,1)S(1)} %broadcast_select_fusion.8), channel_id=1, source_target_pairs={{4,0},{8,4},{12,8},{14,12},{10,14},{6,10},{2,6},{0,2},{5,1},{9,5},... | collective-permute-start | bytes 393224 | tf_op jit(solution)/shard_map/ppermute | solution.py:805
  43.2 6.3 %collective-permute-start.7 = (bf16[32,2048]{1,0:T(8,128)(2,1)S(1)}, bf16[32,2048]{1,0:T(8,128)(2,1)S(1)}, u32[]{:S(2)}, u32[]{:S(2)}) collective-permute-start(bf16[32,2048]{1,0:T(8,128)(2,1)S(1)} %broadcast_select_fusion.9), channel_id=1, source_target_pairs={{0,4},{4,8},{8,12},{12,14},{14,10},{10,6},{6,2},{2,0},{1,5},{5,9},... | collective-permute-start | bytes 393224 | tf_op jit(solution)/shard_map/ppermute | solution.py:802
  44.1 16.9 %slice-start.2 = ((s8[8257536]{0:T(1024)(128)(4,1)}), s8[4194304]{0:T(1024)(128)(4,1)S(1)}, s32[]{:S(2)}) async-start(s8[8257536]{0:T(1024)(128)(4,1)} %bitcast.16), calls=%async_computation.2 | async-start | bytes 8388608
  44.5 7.4 %collective-permute-start.18 = (bf16[32,2048]{1,0:T(8,128)(2,1)S(1)}, bf16[32,2048]{1,0:T(8,128)(2,1)S(1)}, u32[]{:S(2)}, u32[]{:S(2)}) collective-permute-start(bf16[32,2048]{1,0:T(8,128)(2,1)S(1)} %broadcast_select_fusion.1), channel_id=1, source_target_pairs={{0,4},{4,8},{8,12},{12,14},{14,10},{10,6},{6,2},{2,0},{1,5},{5,9},... | collective-permute-start | bytes 393224 | tf_op jit(solution)/shard_map/ppermute | solution.py:802
  46.1 5.8 %collective-permute-start.19 = (bf16[32,2048]{1,0:T(8,128)(2,1)S(1)}, bf16[32,2048]{1,0:T(8,128)(2,1)S(1)}, u32[]{:S(2)}, u32[]{:S(2)}) collective-permute-start(bf16[32,2048]{1,0:T(8,128)(2,1)S(1)} %broadcast_select_fusion), channel_id=1, source_target_pairs={{4,0},{8,4},{12,8},{14,12},{10,14},{6,10},{2,6},{0,2},{5,1},{9,5},... | collective-permute-start | bytes 393224 | tf_op jit(solution)/shard_map/ppermute | solution.py:805
  49.5 5.0 %collective-permute-start.10 = (bf16[32,2048]{1,0:T(8,128)(2,1)S(1)}, bf16[32,2048]{1,0:T(8,128)(2,1)S(1)}, u32[]{:S(2)}, u32[]{:S(2)}) collective-permute-start(bf16[32,2048]{1,0:T(8,128)(2,1)S(1)} %broadcast_select_fusion.6), channel_id=1, source_target_pairs={{4,0},{8,4},{12,8},{14,12},{10,14},{6,10},{2,6},{0,2},{5,1},{9,5},... | collective-permute-start | bytes 393224 | tf_op jit(solution)/shard_map/ppermute | solution.py:805
  49.9 5.0 %collective-permute-start.9 = (bf16[32,2048]{1,0:T(8,128)(2,1)S(1)}, bf16[32,2048]{1,0:T(8,128)(2,1)S(1)}, u32[]{:S(2)}, u32[]{:S(2)}) collective-permute-start(bf16[32,2048]{1,0:T(8,128)(2,1)S(1)} %broadcast_select_fusion.7), channel_id=1, source_target_pairs={{0,4},{4,8},{8,12},{12,14},{14,10},{10,6},{6,2},{2,0},{1,5},{5,9},... | collective-permute-start | bytes 393224 | tf_op jit(solution)/shard_map/ppermute | solution.py:802
  52.0 9.1 %slice-start = ((s8[8257536]{0:T(1024)(128)(4,1)}), s8[4194304]{0:T(1024)(128)(4,1)S(1)}, s32[]{:S(2)}) async-start(s8[8257536]{0:T(1024)(128)(4,1)} %bitcast.9), calls=%async_computation | async-start | bytes 8388608
  53.9 7.1 %slice-start.1 = ((s8[8257536]{0:T(1024)(128)(4,1)}), s8[4063232]{0:T(1024)(128)(4,1)S(1)}, s32[]{:S(2)}) async-start(s8[8257536]{0:T(1024)(128)(4,1)} %bitcast.9), calls=%async_computation.1 | async-start | bytes 8126464
  53.9 7.1 %slice-start.3 = ((s8[8257536]{0:T(1024)(128)(4,1)}), s8[4063232]{0:T(1024)(128)(4,1)S(1)}, s32[]{:S(2)}) async-start(s8[8257536]{0:T(1024)(128)(4,1)} %bitcast.16), calls=%async_computation.3 | async-start | bytes 8126464
  53.9 7.1 %copy-start.1 = (f32[7168]{0:T(1024)S(1)}, f32[7168]{0:T(1024)}, u32[]{:S(2)}) copy-start(f32[7168]{0:T(1024)} %param.24) | copy-start | bytes 86020
  56.9 1.6 %collective-permute-start.21 = (bf16[144,896]{1,0:T(8,128)(2,1)S(1)}, bf16[144,896]{1,0:T(8,128)(2,1)S(1)}, u32[]{:S(2)}, u32[]{:S(2)}) collective-permute-start(bf16[144,896]{1,0:T(8,128)(2,1)S(1)} %get-tuple-element.192), channel_id=1, source_target_pairs={{0,1},{1,0},{2,3},{3,2},{4,5},{5,4},{6,7},{7,6},{8,9},{9,8},{10,11... | collective-permute-start | bytes 774152 | tf_op jit(solution)/shard_map/ppermute | solution.py:808
  58.6 2.4 %collective-permute-start.24 = (bf16[144,896]{1,0:T(8,128)(2,1)S(1)}, bf16[144,896]{1,0:T(8,128)(2,1)S(1)}, u32[]{:S(2)}, u32[]{:S(2)}) collective-permute-start(bf16[144,896]{1,0:T(8,128)(2,1)S(1)} %add_convert_fusion.refs_0_.refs_1_), channel_id=1, source_target_pairs={{0,1},{1,0},{2,3},{3,2},{4,5},{5,4},{6,7},{7,6},{8,9},{9,8},{10,11... | collective-permute-start | bytes 774152 | tf_op jit(solution)/shard_map/ppermute | solution.py:808
  58.8 8.8 %collective-permute-start.22 = (bf16[144,896]{1,0:T(8,128)(2,1)S(1)}, bf16[144,896]{1,0:T(8,128)(2,1)S(1)}, u32[]{:S(2)}, u32[]{:S(2)}) collective-permute-start(bf16[144,896]{1,0:T(8,128)(2,1)S(1)} %add_convert_fusion.refs_0_.refs_1_), channel_id=1, source_target_pairs={{0,4},{4,8},{8,12},{12,14},{14,10},{10,6},{6,2},{2,0},{1,5},{5,9},... | collective-permute-start | bytes 774152 | tf_op jit(solution)/shard_map/ppermute | solution.py:802
  60.5 8.2 %collective-permute-start.23 = (bf16[144,896]{1,0:T(8,128)(2,1)S(1)}, bf16[144,896]{1,0:T(8,128)(2,1)S(1)}, u32[]{:S(2)}, u32[]{:S(2)}) collective-permute-start(bf16[144,896]{1,0:T(8,128)(2,1)S(1)} %add_convert_fusion.refs_0_.refs_1_), channel_id=1, source_target_pairs={{4,0},{8,4},{12,8},{14,12},{10,14},{6,10},{2,6},{0,2},{5,1},{9,5},... | collective-permute-start | bytes 774152 | tf_op jit(solution)/shard_map/ppermute | solution.py:805
  68.8 2.2 %collective-permute-start.27 = (bf16[288,896]{1,0:T(8,128)(2,1)S(1)}, bf16[288,896]{1,0:T(8,128)(2,1)S(1)}, u32[]{:S(2)}, u32[]{:S(2)}) collective-permute-start(bf16[288,896]{1,0:T(8,128)(2,1)S(1)} %pad_maximum_fusion), channel_id=1, source_target_pairs={{0,1},{1,0},{2,3},{3,2},{4,5},{5,4},{6,7},{7,6},{8,9},{9,8},{10,11... | collective-permute-start | bytes 1548296 | tf_op jit(solution)/shard_map/ppermute | solution.py:808
  68.8 8.6 %collective-permute-start.25 = (bf16[144,896]{1,0:T(8,128)(2,1)S(1)}, bf16[144,896]{1,0:T(8,128)(2,1)S(1)}, u32[]{:S(2)}, u32[]{:S(2)}) collective-permute-start(bf16[144,896]{1,0:T(8,128)(2,1)S(1)} %collective-permute-done.22.refs_0_.refs_2_.refs_3_), channel_id=1, source_target_pairs={{0,4},{4,8},{8,12},{12,14},{14,10},{10,6},{6,2},{2,0},{1,5},{5,9},... | collective-permute-start | bytes 774152 | tf_op jit(solution)/shard_map/ppermute | solution.py:802
  69.5 8.3 %collective-permute-start.26 = (bf16[144,896]{1,0:T(8,128)(2,1)S(1)}, bf16[144,896]{1,0:T(8,128)(2,1)S(1)}, u32[]{:S(2)}, u32[]{:S(2)}) collective-permute-start(bf16[144,896]{1,0:T(8,128)(2,1)S(1)} %collective-permute-done.23.refs_1_.refs_4_.refs_5_), channel_id=1, source_target_pairs={{4,0},{8,4},{12,8},{14,12},{10,14},{6,10},{2,6},{0,2},{5,1},{9,5},... | collective-permute-start | bytes 774152 | tf_op jit(solution)/shard_map/ppermute | solution.py:805
  77.8 2.2 %collective-permute-start.30 = (bf16[288,896]{1,0:T(8,128)(2,1)S(1)}, bf16[288,896]{1,0:T(8,128)(2,1)S(1)}, u32[]{:S(2)}, u32[]{:S(2)}) collective-permute-start(bf16[288,896]{1,0:T(8,128)(2,1)S(1)} %pad_maximum_fusion.1), channel_id=1, source_target_pairs={{0,1},{1,0},{2,3},{3,2},{4,5},{5,4},{6,7},{7,6},{8,9},{9,8},{10,11... | collective-permute-start | bytes 1548296 | tf_op jit(solution)/shard_map/ppermute | solution.py:808
  77.9 8.6 %collective-permute-start.28 = (bf16[144,896]{1,0:T(8,128)(2,1)S(1)}, bf16[144,896]{1,0:T(8,128)(2,1)S(1)}, u32[]{:S(2)}, u32[]{:S(2)}) collective-permute-start(bf16[144,896]{1,0:T(8,128)(2,1)S(1)} %collective-permute-done.25.refs_0_.refs_6_.refs_7_), channel_id=1, source_target_pairs={{0,4},{4,8},{8,12},{12,14},{14,10},{10,6},{6,2},{2,0},{1,5},{5,9},... | collective-permute-start | bytes 774152 | tf_op jit(solution)/shard_map/ppermute | solution.py:802
  79.2 8.3 %collective-permute-start.29 = (bf16[144,896]{1,0:T(8,128)(2,1)S(1)}, bf16[144,896]{1,0:T(8,128)(2,1)S(1)}, u32[]{:S(2)}, u32[]{:S(2)}) collective-permute-start(bf16[144,896]{1,0:T(8,128)(2,1)S(1)} %collective-permute-done.26.refs_1_.refs_8_.refs_9_), channel_id=1, source_target_pairs={{4,0},{8,4},{12,8},{14,12},{10,14},{6,10},{2,6},{0,2},{5,1},{9,5},... | collective-permute-start | bytes 774152 | tf_op jit(solution)/shard_map/ppermute | solution.py:805
  87.6 2.2 %collective-permute-start.33 = (bf16[288,896]{1,0:T(8,128)(2,1)S(1)}, bf16[288,896]{1,0:T(8,128)(2,1)S(1)}, u32[]{:S(2)}, u32[]{:S(2)}) collective-permute-start(bf16[288,896]{1,0:T(8,128)(2,1)S(1)} %pad_maximum_fusion.2), channel_id=1, source_target_pairs={{0,1},{1,0},{2,3},{3,2},{4,5},{5,4},{6,7},{7,6},{8,9},{9,8},{10,11... | collective-permute-start | bytes 1548296 | tf_op jit(solution)/shard_map/ppermute | solution.py:808
  87.7 6.9 %collective-permute-start.31 = (bf16[80,896]{1,0:T(8,128)(2,1)S(1)}, bf16[80,896]{1,0:T(8,128)(2,1)S(1)}, u32[]{:S(2)}, u32[]{:S(2)}) collective-permute-start(bf16[80,896]{1,0:T(8,128)(2,1)S(1)} %slice.18), channel_id=1, source_target_pairs={{0,4},{4,8},{8,12},{12,14},{14,10},{10,6},{6,2},{2,0},{1,5},{5,9},... | collective-permute-start | bytes 430088 | tf_op jit(solution)/shard_map/ppermute | solution.py:802
  89.3 5.3 %collective-permute-start.32 = (bf16[64,896]{1,0:T(8,128)(2,1)S(1)}, bf16[64,896]{1,0:T(8,128)(2,1)S(1)}, u32[]{:S(2)}, u32[]{:S(2)}) collective-permute-start(bf16[64,896]{1,0:T(8,128)(2,1)S(1)} %slice.19), channel_id=1, source_target_pairs={{4,0},{8,4},{12,8},{14,12},{10,14},{6,10},{2,6},{0,2},{5,1},{9,5},... | collective-permute-start | bytes 344072 | tf_op jit(solution)/shard_map/ppermute | solution.py:805
  94.6 1.6 %collective-permute-start.34 = (bf16[80,896]{1,0:T(8,128)(2,1)S(1)}, bf16[80,896]{1,0:T(8,128)(2,1)S(1)}, u32[]{:S(2)}, u32[]{:S(2)}) collective-permute-start(bf16[80,896]{1,0:T(8,128)(2,1)S(1)} %collective-permute-done.31.refs_0_), channel_id=1, source_target_pairs={{0,1},{1,0},{2,3},{3,2},{4,5},{5,4},{6,7},{7,6},{8,9},{9,8},{10,11... | collective-permute-start | bytes 430088 | tf_op jit(solution)/shard_map/ppermute | solution.py:808
  94.7 1.5 %collective-permute-start.35 = (bf16[64,896]{1,0:T(8,128)(2,1)S(1)}, bf16[64,896]{1,0:T(8,128)(2,1)S(1)}, u32[]{:S(2)}, u32[]{:S(2)}) collective-permute-start(bf16[64,896]{1,0:T(8,128)(2,1)S(1)} %collective-permute-done.32.refs_1_), channel_id=1, source_target_pairs={{0,1},{1,0},{2,3},{3,2},{4,5},{5,4},{6,7},{7,6},{8,9},{9,8},{10,11... | collective-permute-start | bytes 344072 | tf_op jit(solution)/shard_map/ppermute | solution.py:808
  99.3 4.4 %collective-permute-start.46 = (bf16[144,3584]{1,0:T(8,128)(2,1)S(1)}, bf16[144,3584]{1,0:T(8,128)(2,1)S(1)}, u32[]{:S(2)}, u32[]{:S(2)}) collective-permute-start(bf16[144,3584]{1,0:T(8,128)(2,1)S(1)} %contract.7), channel_id=1, source_target_pairs={{0,1},{1,0},{2,3},{3,2},{4,5},{5,4},{6,7},{7,6},{8,9},{9,8},{10,11... | collective-permute-start | bytes 3096584 | tf_op jit(solution)/shard_map/ppermute | solution.py:808
  100.9 6.7 %collective-permute-start.36 = (bf16[144,3584]{1,0:T(8,128)(2,1)S(1)}, bf16[144,3584]{1,0:T(8,128)(2,1)S(1)}, u32[]{:S(2)}, u32[]{:S(2)}) collective-permute-start(bf16[144,3584]{1,0:T(8,128)(2,1)S(1)} %contract.6), channel_id=1, source_target_pairs={{0,1},{1,0},{2,3},{3,2},{4,5},{5,4},{6,7},{7,6},{8,9},{9,8},{10,11... | collective-permute-start | bytes 3096584 | tf_op jit(solution)/shard_map/ppermute | solution.py:808
  104.6 5.9 %collective-permute-start.48 = (bf16[16,3584]{1,0:T(8,128)(2,1)S(1)}, bf16[16,3584]{1,0:T(8,128)(2,1)S(1)}, u32[]{:S(2)}, u32[]{:S(2)}) collective-permute-start(bf16[16,3584]{1,0:T(8,128)(2,1)S(1)} %convert_element_type.157), channel_id=1, source_target_pairs={{4,0},{8,4},{12,8},{14,12},{10,14},{6,10},{2,6},{0,2},{5,1},{9,5},... | collective-permute-start | bytes 344072 | tf_op jit(solution)/shard_map/ppermute | solution.py:805
  105.8 5.4 %collective-permute-start.47 = (bf16[16,3584]{1,0:T(8,128)(2,1)S(1)}, bf16[16,3584]{1,0:T(8,128)(2,1)S(1)}, u32[]{:S(2)}, u32[]{:S(2)}) collective-permute-start(bf16[16,3584]{1,0:T(8,128)(2,1)S(1)} %convert_element_type.156), channel_id=1, source_target_pairs={{0,4},{4,8},{8,12},{12,14},{14,10},{10,6},{6,2},{2,0},{1,5},{5,9},... | collective-permute-start | bytes 344072 | tf_op jit(solution)/shard_map/ppermute | solution.py:802
  108.4 5.1 %collective-permute-start.38 = (bf16[16,3584]{1,0:T(8,128)(2,1)S(1)}, bf16[16,3584]{1,0:T(8,128)(2,1)S(1)}, u32[]{:S(2)}, u32[]{:S(2)}) collective-permute-start(bf16[16,3584]{1,0:T(8,128)(2,1)S(1)} %convert_element_type.136), channel_id=1, source_target_pairs={{4,0},{8,4},{12,8},{14,12},{10,14},{6,10},{2,6},{0,2},{5,1},{9,5},... | collective-permute-start | bytes 344072 | tf_op jit(solution)/shard_map/ppermute | solution.py:805
  109.0 5.0 %collective-permute-start.37 = (bf16[16,3584]{1,0:T(8,128)(2,1)S(1)}, bf16[16,3584]{1,0:T(8,128)(2,1)S(1)}, u32[]{:S(2)}, u32[]{:S(2)}) collective-permute-start(bf16[16,3584]{1,0:T(8,128)(2,1)S(1)} %convert_element_type.135), channel_id=1, source_target_pairs={{0,4},{4,8},{8,12},{12,14},{14,10},{10,6},{6,2},{2,0},{1,5},{5,9},... | collective-permute-start | bytes 344072 | tf_op jit(solution)/shard_map/ppermute | solution.py:802
  111.3 4.8 %collective-permute-start.50 = (bf16[16,3584]{1,0:T(8,128)(2,1)S(1)}, bf16[16,3584]{1,0:T(8,128)(2,1)S(1)}, u32[]{:S(2)}, u32[]{:S(2)}) collective-permute-start(bf16[16,3584]{1,0:T(8,128)(2,1)S(1)} %add_convert_fusion.5), channel_id=1, source_target_pairs={{4,0},{8,4},{12,8},{14,12},{10,14},{6,10},{2,6},{0,2},{5,1},{9,5},... | collective-permute-start | bytes 344072 | tf_op jit(solution)/shard_map/ppermute | solution.py:805
  112.2 5.4 %collective-permute-start.49 = (bf16[16,3584]{1,0:T(8,128)(2,1)S(1)}, bf16[16,3584]{1,0:T(8,128)(2,1)S(1)}, u32[]{:S(2)}, u32[]{:S(2)}) collective-permute-start(bf16[16,3584]{1,0:T(8,128)(2,1)S(1)} %add_convert_fusion.6), channel_id=1, source_target_pairs={{0,4},{4,8},{8,12},{12,14},{14,10},{10,6},{6,2},{2,0},{1,5},{5,9},... | collective-permute-start | bytes 344072 | tf_op jit(solution)/shard_map/ppermute | solution.py:802
  114.0 7.1 %collective-permute-start.39 = (bf16[16,3584]{1,0:T(8,128)(2,1)S(1)}, bf16[16,3584]{1,0:T(8,128)(2,1)S(1)}, u32[]{:S(2)}, u32[]{:S(2)}) collective-permute-start(bf16[16,3584]{1,0:T(8,128)(2,1)S(1)} %add_convert_fusion.12), channel_id=1, source_target_pairs={{0,4},{4,8},{8,12},{12,14},{14,10},{10,6},{6,2},{2,0},{1,5},{5,9},... | collective-permute-start | bytes 344072 | tf_op jit(solution)/shard_map/ppermute | solution.py:802
  116.0 5.0 %collective-permute-start.40 = (bf16[16,3584]{1,0:T(8,128)(2,1)S(1)}, bf16[16,3584]{1,0:T(8,128)(2,1)S(1)}, u32[]{:S(2)}, u32[]{:S(2)}) collective-permute-start(bf16[16,3584]{1,0:T(8,128)(2,1)S(1)} %add_convert_fusion.11), channel_id=1, source_target_pairs={{4,0},{8,4},{12,8},{14,12},{10,14},{6,10},{2,6},{0,2},{5,1},{9,5},... | collective-permute-start | bytes 344072 | tf_op jit(solution)/shard_map/ppermute | solution.py:805
  117.7 5.5 %collective-permute-start.52 = (bf16[16,3584]{1,0:T(8,128)(2,1)S(1)}, bf16[16,3584]{1,0:T(8,128)(2,1)S(1)}, u32[]{:S(2)}, u32[]{:S(2)}) collective-permute-start(bf16[16,3584]{1,0:T(8,128)(2,1)S(1)} %add_convert_fusion.3), channel_id=1, source_target_pairs={{4,0},{8,4},{12,8},{14,12},{10,14},{6,10},{2,6},{0,2},{5,1},{9,5},... | collective-permute-start | bytes 344072 | tf_op jit(solution)/shard_map/ppermute | solution.py:805
  118.7 5.4 %collective-permute-start.51 = (bf16[16,3584]{1,0:T(8,128)(2,1)S(1)}, bf16[16,3584]{1,0:T(8,128)(2,1)S(1)}, u32[]{:S(2)}, u32[]{:S(2)}) collective-permute-start(bf16[16,3584]{1,0:T(8,128)(2,1)S(1)} %add_convert_fusion.4), channel_id=1, source_target_pairs={{0,4},{4,8},{8,12},{12,14},{14,10},{10,6},{6,2},{2,0},{1,5},{5,9},... | collective-permute-start | bytes 344072 | tf_op jit(solution)/shard_map/ppermute | solution.py:802
  121.1 6.1 %collective-permute-start.42 = (bf16[16,3584]{1,0:T(8,128)(2,1)S(1)}, bf16[16,3584]{1,0:T(8,128)(2,1)S(1)}, u32[]{:S(2)}, u32[]{:S(2)}) collective-permute-start(bf16[16,3584]{1,0:T(8,128)(2,1)S(1)} %add_convert_fusion.9), channel_id=1, source_target_pairs={{4,0},{8,4},{12,8},{14,12},{10,14},{6,10},{2,6},{0,2},{5,1},{9,5},... | collective-permute-start | bytes 344072 | tf_op jit(solution)/shard_map/ppermute | solution.py:805
  121.8 5.8 %collective-permute-start.41 = (bf16[16,3584]{1,0:T(8,128)(2,1)S(1)}, bf16[16,3584]{1,0:T(8,128)(2,1)S(1)}, u32[]{:S(2)}, u32[]{:S(2)}) collective-permute-start(bf16[16,3584]{1,0:T(8,128)(2,1)S(1)} %add_convert_fusion.10), channel_id=1, source_target_pairs={{0,4},{4,8},{8,12},{12,14},{14,10},{10,6},{6,2},{2,0},{1,5},{5,9},... | collective-permute-start | bytes 344072 | tf_op jit(solution)/shard_map/ppermute | solution.py:802
  124.2 6.3 %collective-permute-start.53 = (bf16[16,3584]{1,0:T(8,128)(2,1)S(1)}, bf16[16,3584]{1,0:T(8,128)(2,1)S(1)}, u32[]{:S(2)}, u32[]{:S(2)}) collective-permute-start(bf16[16,3584]{1,0:T(8,128)(2,1)S(1)} %add_convert_fusion.2), channel_id=1, source_target_pairs={{0,4},{4,8},{8,12},{12,14},{14,10},{10,6},{6,2},{2,0},{1,5},{5,9},... | collective-permute-start | bytes 344072 | tf_op jit(solution)/shard_map/ppermute | solution.py:802
  124.8 5.6 %collective-permute-start.54 = (bf16[16,3584]{1,0:T(8,128)(2,1)S(1)}, bf16[16,3584]{1,0:T(8,128)(2,1)S(1)}, u32[]{:S(2)}, u32[]{:S(2)}) collective-permute-start(bf16[16,3584]{1,0:T(8,128)(2,1)S(1)} %add_convert_fusion.1), channel_id=1, source_target_pairs={{4,0},{8,4},{12,8},{14,12},{10,14},{6,10},{2,6},{0,2},{5,1},{9,5},... | collective-permute-start | bytes 344072 | tf_op jit(solution)/shard_map/ppermute | solution.py:805
  127.7 4.8 %collective-permute-start.43 = (bf16[16,3584]{1,0:T(8,128)(2,1)S(1)}, bf16[16,3584]{1,0:T(8,128)(2,1)S(1)}, u32[]{:S(2)}, u32[]{:S(2)}) collective-permute-start(bf16[16,3584]{1,0:T(8,128)(2,1)S(1)} %add_convert_fusion.8), channel_id=1, source_target_pairs={{0,4},{4,8},{8,12},{12,14},{14,10},{10,6},{6,2},{2,0},{1,5},{5,9},... | collective-permute-start | bytes 344072 | tf_op jit(solution)/shard_map/ppermute | solution.py:802
  129.0 4.8 %collective-permute-start.44 = (bf16[16,3584]{1,0:T(8,128)(2,1)S(1)}, bf16[16,3584]{1,0:T(8,128)(2,1)S(1)}, u32[]{:S(2)}, u32[]{:S(2)}) collective-permute-start(bf16[16,3584]{1,0:T(8,128)(2,1)S(1)} %add_convert_fusion.7), channel_id=1, source_target_pairs={{4,0},{8,4},{12,8},{14,12},{10,14},{6,10},{2,6},{0,2},{5,1},{9,5},... | collective-permute-start | bytes 344072 | tf_op jit(solution)/shard_map/ppermute | solution.py:805
  134.1 1.4 %collective-permute-start.45 = (bf16[16,3584]{1,0:T(8,128)(2,1)S(1)}, bf16[16,3584]{1,0:T(8,128)(2,1)S(1)}, u32[]{:S(2)}, u32[]{:S(2)}) collective-permute-start(bf16[16,3584]{1,0:T(8,128)(2,1)S(1)} %get-tuple-element.265), channel_id=1, source_target_pairs={{0,1},{1,0},{2,3},{3,2},{4,5},{5,4},{6,7},{7,6},{8,9},{9,8},{10,11... | collective-permute-start | bytes 344072 | tf_op jit(solution)/shard_map/ppermute | solution.py:808
  134.2 1.5 %collective-permute-start.55 = (bf16[16,3584]{1,0:T(8,128)(2,1)S(1)}, bf16[16,3584]{1,0:T(8,128)(2,1)S(1)}, u32[]{:S(2)}, u32[]{:S(2)}) collective-permute-start(bf16[16,3584]{1,0:T(8,128)(2,1)S(1)} %get-tuple-element.271), channel_id=1, source_target_pairs={{0,1},{1,0},{2,3},{3,2},{4,5},{5,4},{6,7},{7,6},{8,9},{9,8},{10,11... | collective-permute-start | bytes 344072 | tf_op jit(solution)/shard_map/ppermute | solution.py:808
  (2 other events, 6.8 us)

commit v15 on v12

--- a/solution.py
+++ b/solution.py
@@ -137,56 +137,54 @@
     table, order, heads, first, count, group, rows, lat, value, lead, *refs
 ):
     if lead:
-        given, refs = refs[0], refs[1:]
-        q_hbm, cache_hbm, fresh_hbm, vw_hbm, tab, head, main, extra, later = refs[:9]
-        flags, refs = refs[9:12], refs[12:]
-        q, keys, vw, latent, fz, fresh, q_sem, key_sem, vw_sem, dq = refs
-        loaded, base = heads, 0
+        given, q_hbm, cache_hbm, fresh_hbm, vw_hbm, tab, head, main, extra, later = refs[:10]
+        flags, refs = refs[10:13], refs[13:]
+        q, keys, fresh, vw, latent, fz, vw_sem, q_sem, key_sem, dq = refs
     else:
-        tab, q_hbm, cache_hbm, fresh_hbm, vw_hbm, decoded_here, head, main, extra = refs[:9]
-        q, keys, vw, latent, fz, fresh, q_sem, key_sem, vw_sem = refs[9:]
-        loaded, base = count, first
+        tab, vw_hbm, decoded_here, q, keys, fresh, head, main, extra = refs[:9]
+        vw, latent, fz, vw_sem = refs[9:]
     cached, wide = keys.shape[2], keys.shape[1]
-    slots = cache_hbm.shape[0] - 1
     odd_slot = keys.shape[0] - 1
+    slots = odd_slot - 1
     shift, pair, dr = wide - lat, 2 * lat, 8
     groups, pairs = count // group, group // 2
-    loads = loaded // group
+    loads = heads // group
 
     def q_copy(g):
-        source = pl.ds((base + g * group) * lat, group * lat)
-        return pltpu.make_async_copy(
-            q_hbm.at[:, source], q.at[:, pl.ds(g * group * lat, group * lat)], q_sem.at[g]
-        )
+        at = pl.ds(g * group * lat, group * lat)
+        return pltpu.make_async_copy(q_hbm.at[:, at], q.at[:, at], q_sem.at[g])
 
     def vw_copy(g):
         source = pl.ds(first + g * group, group)
         return pltpu.make_async_copy(vw_hbm.at[source], vw.at[pl.ds(g * group, group)], vw_sem.at[g])
 
-    even_copy = pltpu.make_async_copy(cache_hbm.at[0], keys.at[0, pl.ds(0, lat)], key_sem.at[0])
-    odd_copy = pltpu.make_async_copy(
-        cache_hbm.at[0], keys.at[odd_slot, pl.ds(shift, lat)], key_sem.at[1]
-    )
-    waiting = [q_copy(g) for g in range(1, loads)]
+    waiting = []
     if lead:
+        first_copies = [
+            pltpu.make_async_copy(fresh_hbm, fresh, key_sem.at[3]),
+            pltpu.make_async_copy(cache_hbm.at[0], keys.at[0, pl.ds(0, lat)], key_sem.at[0]),
+            q_copy(0),
+            pltpu.make_async_copy(
+                cache_hbm.at[0], keys.at[odd_slot, pl.ds(shift, lat)], key_sem.at[1]
+            ),
+        ]
         rest_copy = pltpu.make_async_copy(
             cache_hbm.at[pl.ds(1, slots)], keys.at[pl.ds(1, slots), pl.ds(0, lat)], key_sem.at[2]
         )
-        waiting.append(rest_copy)
+        waiting += [q_copy(1), rest_copy] + [q_copy(g) for g in range(2, loads)]
     waiting += [vw_copy(g) for g in range(groups)]
 
     def start_next(number):
         for _ in range(min(number, len(waiting))):
             waiting.pop(0).start()
 
-    fresh_copy = pltpu.make_async_copy(fresh_hbm, fresh, key_sem.at[3])
-    fresh_copy.start()
-    even_copy.start()
-    q_copy(0).start()
-    odd_copy.start()
-    start_next(1)
     if lead:
+        for copy in first_copies:
+            copy.start()
+        start_next(1)
         table_kernel(table, order, given, tab)
+    else:
+        start_next(len(waiting))
     span, decs = tab[SPAN], tab[DEC]
 
     def onehot(shape, row_dim, slot_dim):
@@ -194,12 +192,14 @@
         j = lax.broadcasted_iota(i32, shape, slot_dim)
         return jnp.where((r == span + j) & (j < decs), 1.0, 0.0).astype(bf16)
 
-    tail = jnp.zeros((shift, cached), bf16)
-    for s in range(odd_slot):
-        keys[s, lat:] = tail
-    keys[odd_slot, :shift] = tail
+    if lead:
+        tail = jnp.zeros((shift, cached), bf16)
+        for s in range(odd_slot):
+            keys[s, lat:] = tail
+        keys[odd_slot, :shift] = tail
     fz[...] = jnp.zeros_like(fz)
-    fresh_copy.wait()
+    if lead:
+        first_copies[0].wait()
     fz[:rows, :lat] = fresh[...].astype(f32)
     fresh_even = fz[...].astype(bf16)
     fresh_odd = pltpu.roll(fz[...], shift, 1).astype(bf16)
@@ -218,12 +218,14 @@
         o = mm_nt(w[:, :cached], keys[0, :value]) + mm(w[:, cached:], fresh_even[:, :value])
         return jnp.where(row < span, o, 0.0).astype(bf16)
 
-    even_copy.wait()
-    odd_copy.wait()
+    if lead:
+        first_copies[1].wait()
+        first_copies[3].wait()
     for g in range(groups):
-        q_copy(g).wait()
-        start_next(2)
-        start = g * group * lat
+        if lead:
+            q_copy(g).wait()
+            start_next(3)
+        start = (first + g * group) * lat
         for odd in range(2):
             off = start + odd * (pair - wide)
             lhs = jnp.concatenate(
@@ -306,57 +308,80 @@
         head[:, at] = jnp.where(tab[BUSY] == 1, out[block:], out[:block])
 
 
-def attend(table, order, numbers, queries, cache, fresh, vw, part, parts, decoded):
+def attend(table, order, queries, cache, fresh, vw, numbers):
     rows, heads = queries.shape[0], vw.shape[0]
     lat = queries.shape[1] // heads
     slots, _, cached = cache.shape
     value, vh = vw.shape[1:]
-    count = heads // parts
+    count = heads // 2
     group = min(8, count)
-    lead = decoded is None
-    loaded = heads if lead else count
     wide = -(-lat // 128) * 128
+    hbm = pl.BlockSpec(memory_space=pltpu.HBM)
     half = jax.ShapeDtypeStruct((rows // 2, count * vh), bf16)
-    hbm = pl.BlockSpec(memory_space=pltpu.HBM)
-    scratch = [
-        pltpu.VMEM((rows, loaded * lat), bf16),
-        pltpu.VMEM((slots + 1 if lead else 2, wide, cached), bf16),
+    out_shape = [jax.ShapeDtypeStruct((table.size,), i32)] + [half] * 3
+    out_shape += [jax.ShapeDtypeStruct(((heads - count) * 8, value), bf16)]
+    out_shape += [jax.ShapeDtypeStruct((n, 1), f32) for n in (1, 1, rows // 2)]
+    out_shape += [
+        jax.ShapeDtypeStruct(queries.shape, bf16),
+        jax.ShapeDtypeStruct((slots + 1, wide, cached), bf16),
+        jax.ShapeDtypeStruct(fresh.shape[::-1], bf16),
+    ]
+    return pl.pallas_call(
+        functools.partial(
+            attend_kernel, table, order, heads, 0, count, group, rows, lat, value, True
+        ),
+        in_specs=[smem()] + [hbm] * 4,
+        out_specs=[smem()] + [whole()] * (len(out_shape) - 1),
+        out_shape=out_shape,
+        scratch_shapes=attend_scratch(rows, count, group, value, vh, wide)
+        + [
+            pltpu.SemaphoreType.DMA((heads // group,)),
+            pltpu.SemaphoreType.DMA((4,)),
+            pltpu.VMEM((heads * 8, wide), f32),
+        ],
+        compiler_params=params(24),
+        cost_estimate=cost(
+            2 * rows * count * (cached + rows) * (lat + value),
+            2 * (queries.size + cache.size + vw.size // 2),
+            rows * count * (cached + rows),
+        ),
+        name="attend",
+    )(numbers, in_hbm(queries), in_hbm(cache), in_hbm(fresh.T), in_hbm(vw))
+
+
+def attend_scratch(rows, count, group, value, vh, wide):
+    return [
         pltpu.VMEM((count, value, vh), bf16),
         pltpu.VMEM((count // group, 2, group // 2 * rows, value), bf16),
         pltpu.VMEM((-(-rows // 128) * 128, wide), f32),
-        pltpu.VMEM(fresh.shape[::-1], bf16),
-        pltpu.SemaphoreType.DMA((loaded // group,)),
-        pltpu.SemaphoreType.DMA((4,)),
         pltpu.SemaphoreType.DMA((count // group,)),
     ]
-    out_shape, out_specs = [half] * 3, [whole()] * 3
-    ins = [smem()] + [hbm] * 4
-    args = [numbers, in_hbm(queries), in_hbm(cache), in_hbm(fresh.T), in_hbm(vw)]
-    if lead:
-        scratch.append(pltpu.VMEM((heads * 8, wide), f32))
-        out_shape = [jax.ShapeDtypeStruct((table.size,), i32)] + out_shape
-        out_shape += [jax.ShapeDtypeStruct(((heads - count) * 8, value), bf16)]
-        out_shape += [jax.ShapeDtypeStruct((n, 1), f32) for n in (1, 1, rows // 2)]
-        out_specs = [smem()] + out_specs + [whole()] * 4
-    else:
-        ins.append(whole())
-        args.append(decoded)
+
+
+def attend_more(table, order, tab, vw, decoded, queries, keys, fresh):
+    rows, heads = queries.shape[0], vw.shape[0]
+    lat = queries.shape[1] // heads
+    value, vh = vw.shape[1:]
+    count = heads - heads // 2
+    group = min(8, count)
+    _, wide, cached = keys.shape
+    half = jax.ShapeDtypeStruct((rows // 2, count * vh), bf16)
     return pl.pallas_call(
         functools.partial(
-            attend_kernel, table, order, heads, part * count, count, group, rows, lat, value, lead
+            attend_kernel, table, order, heads, heads - count, count, group, rows, lat, value, False
         ),
-        in_specs=ins,
-        out_specs=out_specs,
-        out_shape=out_shape,
-        scratch_shapes=scratch,
-        compiler_params=params(24),
+        in_specs=[smem(), pl.BlockSpec(memory_space=pltpu.HBM)] + [whole()] * 4,
+        out_specs=[whole()] * 3,
+        out_shape=[half] * 3,
+        scratch_shapes=attend_scratch(rows, count, group, value, vh, wide),
+        compiler_params=params(20),
         cost_estimate=cost(
             2 * rows * count * (cached + rows) * (lat + value),
-            2 * (queries.size + cache.size + vw.size) // parts,
+            vw.size,
             rows * count * (cached + rows),
         ),
         name="attend",
-    )(*args)
+    )(tab, in_hbm(vw), decoded, queries, keys, fresh)
 
 
 def pack_kernel(ranks, cores, features, tab, res, *outs):
@@ -802,8 +827,9 @@
 
     ids = jnp.stack([lax.axis_index("blk"), lax.axis_index("head")]).astype(i32)
     given = jnp.concatenate([ids, span_len, dec_count, span_start, cache_len[0]])
-    caches = (queries, latent_cache, new_latent, value_weight)
-    tab, *lead, decoded, busy, which, alive = attend(table, order, given, *caches, 0, 2, None)
+    tab, *lead, decoded, busy, which, alive, held, keys, fresh = attend(
+        table, order, queries, latent_cache, new_latent, value_weight, given
+    )
 
     def choose(special, usual, flag=busy):
         return jnp.where(jnp.broadcast_to(flag > 0, usual.shape), special, usual)
@@ -825,7 +851,7 @@
         send_piece(k)
     decoded, packed = lax.optimization_barrier((decoded, packed))
     packed = list(packed)
-    follow = attend(table, order, tab, *caches, 1, 2, decoded)
+    follow = attend_more(table, order, tab, value_weight, decoded, held, keys, fresh)
     follow, pieces[1:], packed[0], out_weight = lax.optimization_barrier(
         (follow, pieces[1:], packed[0], out_weight)
     )

time: 136 us -> 137 us (level)
  waiting for transfers between devices: 37.2 us -> 39.1 us
    ppermute x20, starting transfers between devices: 22.5 us -> 28.1 us  [send_next(): return lax.ppermute(x, 'blk', forward)]
    ppermute x20, starting transfers between devices: 22.1 us -> 16.8 us  [send_prev(): return lax.ppermute(x, 'blk', backward)]
    ppermute x20, waiting for transfers between devices: 7.2 us -> 10.3 us  [send_prev(): return lax.ppermute(x, 'blk', backward)]
    ppermute x20, waiting for transfers between devices: 27.1 us -> 25 us  [send_next(): return lax.ppermute(x, 'blk', forward)]
  transfers between devices with their start and end apart: 56 -> 56, of which waited for: 29 -> 32; matrix products, arithmetic and copies ran while one was open for 1% -> 1% of each run, Pallas kernels for 19% -> 18%
where the time goes in v15:
time: 137 us; the launch traced here: 136 us
  starting transfers between devices  53.5 us (39%)
  waiting for transfers between devices  39.1 us (29%)
  Pallas kernels  38 us (28%)
  between operations  2.59 us (2%)
  other arithmetic  2.33 us (2%)
    ppermute x20, starting transfers between devices, send_next(): return lax.ppermute(x, 'blk', forward)  28.1 us
    ppermute x20, waiting for transfers between devices, send_next(): return lax.ppermute(x, 'blk', forward)  25 us
    ppermute x20, starting transfers between devices, send_prev(): return lax.ppermute(x, 'blk', backward)  16.8 us
    pallas_call x5, Pallas kernels, expand(): pl.pallas_call(functools.partial(expand_kernel, pieces, len(theirs), firs...  12.1 us
    ppermute x20, waiting for transfers between devices, send_prev(): return lax.ppermute(x, 'blk', backward)  10.3 us
    pallas_call x1, Pallas kernels, attend(): pl.pallas_call(functools.partial(attend_kernel, table, order, heads, 0, c...  8.22 us
    ppermute x4, starting transfers between devices, send_piece(): pieces[k] = lax.ppermute(packed[k], ('blk', 'head'), pairs)  6.27 us
    pallas_call x4, Pallas kernels, contract(): pl.pallas_call(functools.partial(contract_kernel, part * columns), grid=(...  5.01 us
  transfers between devices with their start and end apart: 56, of which 32 were waited for; matrix products, arithmetic and copies ran while one was open for 1% of the time, Pallas kernels for 18%

profile of v15, /device:TPU:0, one launch (start us, length us, event | category | flops | bytes accessed | tf_op | source)
XLA Modules:
  0.0 136.3 jit_solution(9036599809668491944)
XLA Ops:
  0.7 0.8 concatenate.24.refs_0_
  1.4 8.2 %attend.2 = (s32[60]{0:T(128)S(1)}, bf16[32,2048]{1,0:T(8,128)(2,1)S(1)}, bf16[32,2048]{1,0:T(8,128)(2,1)S(1)}, bf16[32,2048]{1,0:T(8,128)(2,1)S(1)}, bf16[128,5...) custom-call(s32[26]{0:T(128)S(1)} %concatenate.24.refs_0_, ...), custom_call_target="tpu_custom_call" | custom-call | flops 713031680 | bytes 6815744 | tf_op jit(solution)/shard_map/attend/pallas_call | solution.py:329
  9.6 3.1 %collective-permute-start.11 = (bf16[32,2048]{1,0:T(8,128)(2,1)S(1)}, bf16[32,2048]{1,0:T(8,128)(2,1)S(1)}, u32[]{:S(2)}, u32[]{:S(2)}) collective-permute-start(bf16[32,2048]{1,0:T(8,128)(2,1)S(1)} %get-tuple-element.168), channel_id=1, source_target_pairs={{0,4},{4,8},{8,12},{12,14},{14,10},{10,6},{6,2},{2,0},{1,5},{5,9},... | collective-permute-start | bytes 393224 | tf_op jit(solution)/shard_map/ppermute | solution.py:820
  13.4 1.9 %collective-permute-start.1 = (bf16[64,896]{1,0:T(8,128)(2,1)S(1)}, bf16[64,896]{1,0:T(8,128)(2,1)S(1)}, u32[]{:S(2)}, u32[]{:S(2)}) collective-permute-start(bf16[64,896]{1,0:T(8,128)(2,1)S(1)} %get-tuple-element.144), channel_id=1, source_target_pairs={{0,4},{1,13},{2,6},{3,15},{4,8},{5,1},{6,10},{7,3},{8,12},{9,5},{1... | collective-permute-start | bytes 344072 | tf_op jit(solution)/shard_map/ppermute | solution.py:848
  15.3 3.6 %collective-permute-start.2 = (bf16[64,896]{1,0:T(8,128)(2,1)S(1)}, bf16[64,896]{1,0:T(8,128)(2,1)S(1)}, u32[]{:S(2)}, u32[]{:S(2)}) collective-permute-start(bf16[64,896]{1,0:T(8,128)(2,1)S(1)} %get-tuple-element.145), channel_id=1, source_target_pairs={{0,6},{1,15},{2,8},{3,1},{4,10},{5,3},{6,12},{7,5},{8,14},{9,7},{1... | collective-permute-start | bytes 344072 | tf_op jit(solution)/shard_map/ppermute | solution.py:848
  20.1 4.7 %attend.3 = (bf16[32,2048]{1,0:T(8,128)(2,1)S(1)}, bf16[32,2048]{1,0:T(8,128)(2,1)S(1)}, bf16[32,2048]{1,0:T(8,128)(2,1)S(1)}) custom-call(s32[60]{0:T(128)S(1)} %get-tuple-element.140.tab.refs_0_, bf16[32,512,128]{2,1,0:T(8,128)(2,1)} %refs_1_.3, bf16[128,512]{1,0:T(8,128)(2,1)S(1)} %get-tuple-element.146.refs_2_, ...), custom_call_target="tpu_custom_call" | custom-call | flops 713031680 | bytes 2097152 | tf_op jit(solution)/shard_map/attend/pallas_call | solution.py:369
  24.8 0.9 collective-permute-done.2.refs_3_
  26.4 0.8 collective-permute-start.4
  27.3 1.2 collective-permute-start.3
  28.5 0.7 collective-permute-start.13
  29.3 1.4 collective-permute-start.15
  30.6 2.9 %collective-permute-done.3.refs_1_ = bf16[32,2048]{1,0:T(8,128)(2,1)S(1)} collective-permute-done((bf16[32,2048]{1,0:T(8,128)(2,1)S(1)}, bf16[32,2048]{1,0:T(8,128)(2,1)S(1)}, u32[]{:S(2)}, u32[]{:S(2)}) %collective-permute-start.3) | collective-permute-done | bytes 131104 | tf_op jit(solution)/shard_map/ppermute | solution.py:820
  33.6 1.9 %collective-permute-start.6 = (bf16[32,2048]{1,0:T(8,128)(2,1)S(1)}, bf16[32,2048]{1,0:T(8,128)(2,1)S(1)}, u32[]{:S(2)}, u32[]{:S(2)}) collective-permute-start(bf16[32,2048]{1,0:T(8,128)(2,1)S(1)} %broadcast_select_fusion.10), channel_id=1, source_target_pairs={{4,0},{8,4},{12,8},{14,12},{10,14},{6,10},{2,6},{0,2},{5,1},{9,5},... | collective-permute-start | bytes 393224 | tf_op jit(solution)/shard_map/ppermute | solution.py:823
  36.5 2.5 %collective-permute-start.17 = (bf16[32,2048]{1,0:T(8,128)(2,1)S(1)}, bf16[32,2048]{1,0:T(8,128)(2,1)S(1)}, u32[]{:S(2)}, u32[]{:S(2)}) collective-permute-start(bf16[32,2048]{1,0:T(8,128)(2,1)S(1)} %broadcast_select_fusion.2), channel_id=1, source_target_pairs={{4,0},{8,4},{12,8},{14,12},{10,14},{6,10},{2,6},{0,2},{5,1},{9,5},... | collective-permute-start | bytes 393224 | tf_op jit(solution)/shard_map/ppermute | solution.py:823
  39.4 1.3 collective-permute-done.5.refs_2_
  41.4 1.4 %collective-permute-start.7 = (bf16[32,2048]{1,0:T(8,128)(2,1)S(1)}, bf16[32,2048]{1,0:T(8,128)(2,1)S(1)}, u32[]{:S(2)}, u32[]{:S(2)}) collective-permute-start(bf16[32,2048]{1,0:T(8,128)(2,1)S(1)} %broadcast_select_fusion.9), channel_id=1, source_target_pairs={{0,4},{4,8},{8,12},{12,14},{14,10},{10,6},{6,2},{2,0},{1,5},{5,9},... | collective-permute-start | bytes 393224 | tf_op jit(solution)/shard_map/ppermute | solution.py:820
  42.9 2.5 %collective-permute-done.16.refs_3_ = bf16[32,2048]{1,0:T(8,128)(2,1)S(1)} collective-permute-done((bf16[32,2048]{1,0:T(8,128)(2,1)S(1)}, bf16[32,2048]{1,0:T(8,128)(2,1)S(1)}, u32[]{:S(2)}, u32[]{:S(2)}) %collective-permute-start.16) | collective-permute-done | bytes 131104 | tf_op jit(solution)/shard_map/ppermute | solution.py:820
  45.5 2.0 %collective-permute-start.19 = (bf16[32,2048]{1,0:T(8,128)(2,1)S(1)}, bf16[32,2048]{1,0:T(8,128)(2,1)S(1)}, u32[]{:S(2)}, u32[]{:S(2)}) collective-permute-start(bf16[32,2048]{1,0:T(8,128)(2,1)S(1)} %broadcast_select_fusion), channel_id=1, source_target_pairs={{4,0},{8,4},{12,8},{14,12},{10,14},{6,10},{2,6},{0,2},{5,1},{9,5},... | collective-permute-start | bytes 393224 | tf_op jit(solution)/shard_map/ppermute | solution.py:823
  47.5 0.7 collective-permute-done.7.refs_3_
  48.7 1.6 %collective-permute-start.9 = (bf16[32,2048]{1,0:T(8,128)(2,1)S(1)}, bf16[32,2048]{1,0:T(8,128)(2,1)S(1)}, u32[]{:S(2)}, u32[]{:S(2)}) collective-permute-start(bf16[32,2048]{1,0:T(8,128)(2,1)S(1)} %broadcast_select_fusion.7), channel_id=1, source_target_pairs={{0,4},{4,8},{8,12},{12,14},{14,10},{10,6},{6,2},{2,0},{1,5},{5,9},... | collective-permute-start | bytes 393224 | tf_op jit(solution)/shard_map/ppermute | solution.py:820
  50.3 0.9 collective-permute-done.18.refs_4_
  51.6 1.9 %project.2.refs_10_ = f32[288,896]{1,0:T(8,128)S(1)} custom-call(s32[60]{0:T(128)S(1)} %get-tuple-element.140.tab.refs_0_, bf16[32,2048]{1,0:T(8,128)(2,1)S(1)} %get-tuple-element.186.refs_0_, bf16[32,2048]{1,0:T(8,128)(2,1)S(1)} %collective-permute-done.11.refs_1_, bf16[32,2048]{1,0:T(8,128)(2,1)S(1)} %collective-permute-done.13.refs_2_, ...), custom_call_target="tpu_custom_call" | custom-call | flops 1056964608 | bytes 4849664 | tf_op jit(solution)/shard_map/project/pallas_call | solution.py:514
  53.7 2.0 %project.3 = (f32[144,896]{1,0:T(8,128)S(1)}, bf16[144,896]{1,0:T(8,128)(2,1)S(1)}) custom-call(s32[60]{0:T(128)S(1)} %get-tuple-element.140.tab.refs_0_, bf16[32,2048]{1,0:T(8,128)(2,1)S(1)} %get-tuple-element.159.refs_0_, bf16[32,2048]{1,0:T(8,128)(2,1)S(1)} %collective-permute-done.3.refs_1_, bf16[32,2048]{1,0:T(8,128)(2,1)S(1)} %collective-permute-done.5.refs_2_, ...), custom_call_target="tpu_custom_call" | custom-call | flops 1056964608 | bytes 4849664 | tf_op jit(solution)/shard_map/project/pallas_call | solution.py:524
  56.4 0.9 collective-permute-done.21
  57.6 1.6 %collective-permute-start.22 = (bf16[144,896]{1,0:T(8,128)(2,1)S(1)}, bf16[144,896]{1,0:T(8,128)(2,1)S(1)}, u32[]{:S(2)}, u32[]{:S(2)}) collective-permute-start(bf16[144,896]{1,0:T(8,128)(2,1)S(1)} %add_convert_fusion.refs_0_.refs_1_), channel_id=1, source_target_pairs={{0,4},{4,8},{8,12},{12,14},{14,10},{10,6},{6,2},{2,0},{1,5},{5,9},... | collective-permute-start | bytes 774152 | tf_op jit(solution)/shard_map/ppermute | solution.py:820
  59.7 1.7 %expand.5 = (f32[288,576]{1,0:T(8,128)S(1)}, f32[288,576]{1,0:T(8,128)S(1)}, f32[288,1]{1,0:T(8,128)S(1)}) custom-call(s32[60]{0:T(128)S(1)} %get-tuple-element.140.tab.refs_0_, bf16[144,896]{1,0:T(8,128)(2,1)S(1)} %add_convert_fusion.refs_0_.refs_1_, bf16[144,896]{1,0:T(8,128)(2,1)S(1)} %collective-permute-done.24.refs_1_, f32[8,1,896]{2,1,0:T(1,128)S(1)} %bitcast.27, ...), custom_call_target="tpu_custom_call" | custom-call | flops 1 | bytes 1 | tf_op jit(solution)/shard_map/expand/pallas_call | solution.py:676
  61.4 4.7 %collective-permute-done.22.refs_0_.refs_2_.refs_3_ = bf16[144,896]{1,0:T(8,128)(2,1)S(1)} collective-permute-done((bf16[144,896]{1,0:T(8,128)(2,1)S(1)}, bf16[144,896]{1,0:T(8,128)(2,1)S(1)}, u32[]{:S(2)}, u32[]{:S(2)}) %collective-permute-start.22) | collective-permute-done | bytes 258080 | tf_op jit(solution)/shard_map/ppermute | solution.py:820
  66.1 1.3 collective-permute-done.23.refs_1_.refs_4_.refs_5_
  67.5 0.9 collective-permute-start.25
  68.4 1.2 collective-permute-start.26
  69.6 2.9 %expand.6 = (f32[288,576]{1,0:T(8,128)S(1)}, f32[288,576]{1,0:T(8,128)S(1)}, f32[288,1]{1,0:T(8,128)S(1)}) custom-call(s32[60]{0:T(128)S(1)} %get-tuple-element.140.tab.refs_0_, bf16[144,896]{1,0:T(8,128)(2,1)S(1)} %collective-permute-done.22.refs_0_.refs_2_.refs_3_, bf16[144,896]{1,0:T(8,128)(2,1)S(1)} %collective-permute-done.23.refs_1_.refs_4_.refs_5_, ...), custom_call_target="tpu_custom_call" | custom-call | flops 1 | bytes 1 | tf_op jit(solution)/shard_map/expand/pallas_call | solution.py:676
  72.5 3.7 %collective-permute-done.25.refs_0_.refs_6_.refs_7_ = bf16[144,896]{1,0:T(8,128)(2,1)S(1)} collective-permute-done((bf16[144,896]{1,0:T(8,128)(2,1)S(1)}, bf16[144,896]{1,0:T(8,128)(2,1)S(1)}, u32[]{:S(2)}, u32[]{:S(2)}) %collective-permute-start.25) | collective-permute-done | bytes 258080 | tf_op jit(solution)/shard_map/ppermute | solution.py:820
  76.8 1.4 %collective-permute-start.28 = (bf16[144,896]{1,0:T(8,128)(2,1)S(1)}, bf16[144,896]{1,0:T(8,128)(2,1)S(1)}, u32[]{:S(2)}, u32[]{:S(2)}) collective-permute-start(bf16[144,896]{1,0:T(8,128)(2,1)S(1)} %collective-permute-done.25.refs_0_.refs_6_.refs_7_), channel_id=1, source_target_pairs={{0,4},{4,8},{8,12},{12,14},{14,10},{10,6},{6,2},{2,0},{1,5},{5,9},... | collective-permute-start | bytes 774152 | tf_op jit(solution)/shard_map/ppermute | solution.py:820
  78.9 2.9 %expand.7 = (f32[288,576]{1,0:T(8,128)S(1)}, f32[288,576]{1,0:T(8,128)S(1)}, f32[288,1]{1,0:T(8,128)S(1)}) custom-call(s32[60]{0:T(128)S(1)} %get-tuple-element.140.tab.refs_0_, bf16[144,896]{1,0:T(8,128)(2,1)S(1)} %collective-permute-done.25.refs_0_.refs_6_.refs_7_, bf16[144,896]{1,0:T(8,128)(2,1)S(1)} %collective-permute-done.26.refs_1_.refs_8_.refs_9_, ...), custom_call_target="tpu_custom_call" | custom-call | flops 1 | bytes 1 | tf_op jit(solution)/shard_map/expand/pallas_call | solution.py:676
  81.8 3.7 %collective-permute-done.28.refs_0_.refs_10_.refs_11_ = bf16[144,896]{1,0:T(8,128)(2,1)S(1)} collective-permute-done((bf16[144,896]{1,0:T(8,128)(2,1)S(1)}, bf16[144,896]{1,0:T(8,128)(2,1)S(1)}, u32[]{:S(2)}, u32[]{:S(2)}) %collective-permute-start.28) | collective-permute-done | bytes 258080 | tf_op jit(solution)/shard_map/ppermute | solution.py:820
  85.5 1.1 collective-permute-done.29.refs_1_.refs_12_.refs_13_
  86.7 1.5 %collective-permute-start.31 = (bf16[80,896]{1,0:T(8,128)(2,1)S(1)}, bf16[80,896]{1,0:T(8,128)(2,1)S(1)}, u32[]{:S(2)}, u32[]{:S(2)}) collective-permute-start(bf16[80,896]{1,0:T(8,128)(2,1)S(1)} %slice.18), channel_id=1, source_target_pairs={{0,4},{4,8},{8,12},{12,14},{14,10},{10,6},{6,2},{2,0},{1,5},{5,9},... | collective-permute-start | bytes 430088 | tf_op jit(solution)/shard_map/ppermute | solution.py:820
  88.9 2.9 %expand.8 = (f32[288,576]{1,0:T(8,128)S(1)}, f32[288,576]{1,0:T(8,128)S(1)}, f32[288,1]{1,0:T(8,128)S(1)}) custom-call(s32[60]{0:T(128)S(1)} %get-tuple-element.140.tab.refs_0_, bf16[144,896]{1,0:T(8,128)(2,1)S(1)} %collective-permute-done.28.refs_0_.refs_10_.refs_11_, bf16[144,896]{1,0:T(8,128)(2,1)S(1)} %collective-permute-done.29.refs_1_.refs_12_.refs_13_, ...), custom_call_target="tpu_custom_call" | custom-call | flops 1 | bytes 1 | tf_op jit(solution)/shard_map/expand/pallas_call | solution.py:676
  91.8 1.8 %collective-permute-done.32.refs_1_ = bf16[64,896]{1,0:T(8,128)(2,1)S(1)} collective-permute-done((bf16[64,896]{1,0:T(8,128)(2,1)S(1)}, bf16[64,896]{1,0:T(8,128)(2,1)S(1)}, u32[]{:S(2)}, u32[]{:S(2)}) %collective-permute-start.32) | collective-permute-done | bytes 114720 | tf_op jit(solution)/shard_map/ppermute | solution.py:823
  94.1 1.0 collective-permute-done.35.refs_3_
  95.1 1.8 %expand.9.hidden = bf16[288,576]{1,0:T(8,128)(2,1)S(1)} custom-call(s32[60]{0:T(128)S(1)} %get-tuple-element.140.tab.refs_0_, bf16[80,896]{1,0:T(8,128)(2,1)S(1)} %collective-permute-done.31.refs_0_, bf16[64,896]{1,0:T(8,128)(2,1)S(1)} %collective-permute-done.32.refs_1_, bf16[80,896]{1,0:T(8,128)(2,1)S(1)} %collective-permute-done.34.refs_2_, ...), custom_call_target="tpu_custom_call" | custom-call | flops 1 | bytes 1 | tf_op jit(solution)/shard_map/expand/pallas_call | solution.py:676
  96.9 1.3 contract.7
  98.6 1.2 contract.6
  100.1 1.2 contract.4.mine
  101.3 1.3 contract.5.mine
  102.6 0.8 pick.3
  104.8 1.7 %collective-permute-start.47 = (bf16[16,3584]{1,0:T(8,128)(2,1)S(1)}, bf16[16,3584]{1,0:T(8,128)(2,1)S(1)}, u32[]{:S(2)}, u32[]{:S(2)}) collective-permute-start(bf16[16,3584]{1,0:T(8,128)(2,1)S(1)} %convert_element_type.156), channel_id=1, source_target_pairs={{0,4},{4,8},{8,12},{12,14},{14,10},{10,6},{6,2},{2,0},{1,5},{5,9},... | collective-permute-start | bytes 344072 | tf_op jit(solution)/shard_map/ppermute | solution.py:820
  106.5 0.8 pick.2
  108.0 1.5 %collective-permute-start.37 = (bf16[16,3584]{1,0:T(8,128)(2,1)S(1)}, bf16[16,3584]{1,0:T(8,128)(2,1)S(1)}, u32[]{:S(2)}, u32[]{:S(2)}) collective-permute-start(bf16[16,3584]{1,0:T(8,128)(2,1)S(1)} %convert_element_type.135), channel_id=1, source_target_pairs={{0,4},{4,8},{8,12},{12,14},{14,10},{10,6},{6,2},{2,0},{1,5},{5,9},... | collective-permute-start | bytes 344072 | tf_op jit(solution)/shard_map/ppermute | solution.py:820
  109.5 0.7 collective-permute-done.47
  110.2 0.7 collective-permute-start.50
  110.9 1.4 %collective-permute-start.49 = (bf16[16,3584]{1,0:T(8,128)(2,1)S(1)}, bf16[16,3584]{1,0:T(8,128)(2,1)S(1)}, u32[]{:S(2)}, u32[]{:S(2)}) collective-permute-start(bf16[16,3584]{1,0:T(8,128)(2,1)S(1)} %add_convert_fusion.6), channel_id=1, source_target_pairs={{0,4},{4,8},{8,12},{12,14},{14,10},{10,6},{6,2},{2,0},{1,5},{5,9},... | collective-permute-start | bytes 344072 | tf_op jit(solution)/shard_map/ppermute | solution.py:820
  113.2 1.6 %collective-permute-start.39 = (bf16[16,3584]{1,0:T(8,128)(2,1)S(1)}, bf16[16,3584]{1,0:T(8,128)(2,1)S(1)}, u32[]{:S(2)}, u32[]{:S(2)}) collective-permute-start(bf16[16,3584]{1,0:T(8,128)(2,1)S(1)} %add_convert_fusion.12), channel_id=1, source_target_pairs={{0,4},{4,8},{8,12},{12,14},{14,10},{10,6},{6,2},{2,0},{1,5},{5,9},... | collective-permute-start | bytes 344072 | tf_op jit(solution)/shard_map/ppermute | solution.py:820
  115.3 1.3 collective-permute-done.49
  116.7 0.7 collective-permute-start.52
  117.4 1.4 %collective-permute-start.51 = (bf16[16,3584]{1,0:T(8,128)(2,1)S(1)}, bf16[16,3584]{1,0:T(8,128)(2,1)S(1)}, u32[]{:S(2)}, u32[]{:S(2)}) collective-permute-start(bf16[16,3584]{1,0:T(8,128)(2,1)S(1)} %add_convert_fusion.4), channel_id=1, source_target_pairs={{0,4},{4,8},{8,12},{12,14},{14,10},{10,6},{6,2},{2,0},{1,5},{5,9},... | collective-permute-start | bytes 344072 | tf_op jit(solution)/shard_map/ppermute | solution.py:820
  118.7 1.0 collective-permute-done.40
  120.2 2.4 %collective-permute-start.41 = (bf16[16,3584]{1,0:T(8,128)(2,1)S(1)}, bf16[16,3584]{1,0:T(8,128)(2,1)S(1)}, u32[]{:S(2)}, u32[]{:S(2)}) collective-permute-start(bf16[16,3584]{1,0:T(8,128)(2,1)S(1)} %add_convert_fusion.10), channel_id=1, source_target_pairs={{0,4},{4,8},{8,12},{12,14},{14,10},{10,6},{6,2},{2,0},{1,5},{5,9},... | collective-permute-start | bytes 344072 | tf_op jit(solution)/shard_map/ppermute | solution.py:820
  122.7 2.0 %collective-permute-start.53 = (bf16[16,3584]{1,0:T(8,128)(2,1)S(1)}, bf16[16,3584]{1,0:T(8,128)(2,1)S(1)}, u32[]{:S(2)}, u32[]{:S(2)}) collective-permute-start(bf16[16,3584]{1,0:T(8,128)(2,1)S(1)} %add_convert_fusion.2), channel_id=1, source_target_pairs={{0,4},{4,8},{8,12},{12,14},{14,10},{10,6},{6,2},{2,0},{1,5},{5,9},... | collective-permute-start | bytes 344072 | tf_op jit(solution)/shard_map/ppermute | solution.py:820
  124.8 1.0 collective-permute-done.42
  126.1 2.5 %collective-permute-start.43 = (bf16[16,3584]{1,0:T(8,128)(2,1)S(1)}, bf16[16,3584]{1,0:T(8,128)(2,1)S(1)}, u32[]{:S(2)}, u32[]{:S(2)}) collective-permute-start(bf16[16,3584]{1,0:T(8,128)(2,1)S(1)} %add_convert_fusion.8), channel_id=1, source_target_pairs={{0,4},{4,8},{8,12},{12,14},{14,10},{10,6},{6,2},{2,0},{1,5},{5,9},... | collective-permute-start | bytes 344072 | tf_op jit(solution)/shard_map/ppermute | solution.py:820
  129.5 1.5 %collective-permute-done.43 = bf16[16,3584]{1,0:T(8,128)(2,1)S(1)} collective-permute-done((bf16[16,3584]{1,0:T(8,128)(2,1)S(1)}, bf16[16,3584]{1,0:T(8,128)(2,1)S(1)}, u32[]{:S(2)}, u32[]{:S(2)}) %collective-permute-start.43) | collective-permute-done | bytes 114720 | tf_op jit(solution)/shard_map/ppermute | solution.py:820
  131.0 2.4 %collective-permute-done.44 = bf16[16,3584]{1,0:T(8,128)(2,1)S(1)} collective-permute-done((bf16[16,3584]{1,0:T(8,128)(2,1)S(1)}, bf16[16,3584]{1,0:T(8,128)(2,1)S(1)}, u32[]{:S(2)}, u32[]{:S(2)}) %collective-permute-start.44) | collective-permute-done | bytes 114720 | tf_op jit(solution)/shard_map/ppermute | solution.py:823
  135.4 0.9 maximum_select_fusion
  (133 shorter events, 16.5 us)
Async XLA Ops:
  1.4 11.3 %copy-start = (bf16[64,7168]{1,0:T(8,128)(2,1)S(1)}, bf16[64,7168]{1,0:T(8,128)(2,1)}, u32[]{:S(2)}) copy-start(bf16[64,7168]{1,0:T(8,128)(2,1)} %res.1) | copy-start | bytes 2752516
  9.6 18.8 %collective-permute-start.11 = (bf16[32,2048]{1,0:T(8,128)(2,1)S(1)}, bf16[32,2048]{1,0:T(8,128)(2,1)S(1)}, u32[]{:S(2)}, u32[]{:S(2)}) collective-permute-start(bf16[32,2048]{1,0:T(8,128)(2,1)S(1)} %get-tuple-element.168), channel_id=1, source_target_pairs={{0,4},{4,8},{8,12},{12,14},{14,10},{10,6},{6,2},{2,0},{1,5},{5,9},... | collective-permute-start | bytes 393224 | tf_op jit(solution)/shard_map/ppermute | solution.py:820
  13.3 11.5 %collective-permute-start = (bf16[64,896]{1,0:T(8,128)(2,1)S(1)}, bf16[64,896]{1,0:T(8,128)(2,1)S(1)}, u32[]{:S(2)}, u32[]{:S(2)}) collective-permute-start(bf16[64,896]{1,0:T(8,128)(2,1)S(1)} %get-tuple-element.143), channel_id=1, source_target_pairs={{0,2},{1,11},{2,4},{3,13},{4,6},{5,15},{6,8},{7,1},{8,10},{9,3},{1... | collective-permute-start | bytes 344072 | tf_op jit(solution)/shard_map/ppermute | solution.py:848
  13.4 11.4 %collective-permute-start.1 = (bf16[64,896]{1,0:T(8,128)(2,1)S(1)}, bf16[64,896]{1,0:T(8,128)(2,1)S(1)}, u32[]{:S(2)}, u32[]{:S(2)}) collective-permute-start(bf16[64,896]{1,0:T(8,128)(2,1)S(1)} %get-tuple-element.144), channel_id=1, source_target_pairs={{0,4},{1,13},{2,6},{3,15},{4,8},{5,1},{6,10},{7,3},{8,12},{9,5},{1... | collective-permute-start | bytes 344072 | tf_op jit(solution)/shard_map/ppermute | solution.py:848
  15.3 10.4 %collective-permute-start.2 = (bf16[64,896]{1,0:T(8,128)(2,1)S(1)}, bf16[64,896]{1,0:T(8,128)(2,1)S(1)}, u32[]{:S(2)}, u32[]{:S(2)}) collective-permute-start(bf16[64,896]{1,0:T(8,128)(2,1)S(1)} %get-tuple-element.145), channel_id=1, source_target_pairs={{0,6},{1,15},{2,8},{3,1},{4,10},{5,3},{6,12},{7,5},{8,14},{9,7},{1... | collective-permute-start | bytes 344072 | tf_op jit(solution)/shard_map/ppermute | solution.py:848
  19.0 9.6 %collective-permute-start.12 = (bf16[32,2048]{1,0:T(8,128)(2,1)S(1)}, bf16[32,2048]{1,0:T(8,128)(2,1)S(1)}, u32[]{:S(2)}, u32[]{:S(2)}) collective-permute-start(bf16[32,2048]{1,0:T(8,128)(2,1)S(1)} %get-tuple-element.186.refs_0_), channel_id=1, source_target_pairs={{4,0},{8,4},{12,8},{14,12},{10,14},{6,10},{2,6},{0,2},{5,1},{9,5},... | collective-permute-start | bytes 393224 | tf_op jit(solution)/shard_map/ppermute | solution.py:823
  20.1 31.5 %slice-start.6 = ((s8[7340032]{0:T(1024)(128)(4,1)}), s8[4194304]{0:T(1024)(128)(4,1)S(1)}, s32[]{:S(2)}) async-start(s8[7340032]{0:T(1024)(128)(4,1)} %bitcast.25), calls=%async_computation.6 | async-start | bytes 8388608
  20.1 31.5 %slice-start.7 = ((s8[7340032]{0:T(1024)(128)(4,1)}), s8[3145728]{0:T(1024)(128)(4,1)S(1)}, s32[]{:S(2)}) async-start(s8[7340032]{0:T(1024)(128)(4,1)} %bitcast.25), calls=%async_computation.7 | async-start | bytes 6291456
  25.7 10.0 %collective-permute-start.14 = (bf16[64,896]{1,0:T(8,128)(2,1)S(1)}, bf16[64,896]{1,0:T(8,128)(2,1)S(1)}, u32[]{:S(2)}, u32[]{:S(2)}) collective-permute-start(bf16[64,896]{1,0:T(8,128)(2,1)S(1)} %get-tuple-element.172.own), channel_id=1, source_target_pairs={{1,9},{3,11},{5,13},{7,15},{9,1},{11,3},{13,5},{15,7},{17,25},{19,... | collective-permute-start | bytes 344072 | tf_op jit(solution)/shard_map/ppermute | solution.py:848
  26.4 7.2 %collective-permute-start.4 = (bf16[32,2048]{1,0:T(8,128)(2,1)S(1)}, bf16[32,2048]{1,0:T(8,128)(2,1)S(1)}, u32[]{:S(2)}, u32[]{:S(2)}) collective-permute-start(bf16[32,2048]{1,0:T(8,128)(2,1)S(1)} %get-tuple-element.159.refs_0_), channel_id=1, source_target_pairs={{4,0},{8,4},{12,8},{14,12},{10,14},{6,10},{2,6},{0,2},{5,1},{9,5},... | collective-permute-start | bytes 393224 | tf_op jit(solution)/shard_map/ppermute | solution.py:823
  27.3 6.3 %collective-permute-start.3 = (bf16[32,2048]{1,0:T(8,128)(2,1)S(1)}, bf16[32,2048]{1,0:T(8,128)(2,1)S(1)}, u32[]{:S(2)}, u32[]{:S(2)}) collective-permute-start(bf16[32,2048]{1,0:T(8,128)(2,1)S(1)} %get-tuple-element.156), channel_id=1, source_target_pairs={{0,4},{4,8},{8,12},{12,14},{14,10},{10,6},{6,2},{2,0},{1,5},{5,9},... | collective-permute-start | bytes 393224 | tf_op jit(solution)/shard_map/ppermute | solution.py:820
  28.5 7.2 %collective-permute-start.13 = (bf16[32,2048]{1,0:T(8,128)(2,1)S(1)}, bf16[32,2048]{1,0:T(8,128)(2,1)S(1)}, u32[]{:S(2)}, u32[]{:S(2)}) collective-permute-start(bf16[32,2048]{1,0:T(8,128)(2,1)S(1)} %broadcast_select_fusion.5), channel_id=1, source_target_pairs={{0,4},{4,8},{8,12},{12,14},{14,10},{10,6},{6,2},{2,0},{1,5},{5,9},... | collective-permute-start | bytes 393224 | tf_op jit(solution)/shard_map/ppermute | solution.py:820
  29.3 7.2 %collective-permute-start.15 = (bf16[32,2048]{1,0:T(8,128)(2,1)S(1)}, bf16[32,2048]{1,0:T(8,128)(2,1)S(1)}, u32[]{:S(2)}, u32[]{:S(2)}) collective-permute-start(bf16[32,2048]{1,0:T(8,128)(2,1)S(1)} %broadcast_select_fusion.4), channel_id=1, source_target_pairs={{4,0},{8,4},{12,8},{14,12},{10,14},{6,10},{2,6},{0,2},{5,1},{9,5},... | collective-permute-start | bytes 393224 | tf_op jit(solution)/shard_map/ppermute | solution.py:823
  33.6 5.7 %collective-permute-start.6 = (bf16[32,2048]{1,0:T(8,128)(2,1)S(1)}, bf16[32,2048]{1,0:T(8,128)(2,1)S(1)}, u32[]{:S(2)}, u32[]{:S(2)}) collective-permute-start(bf16[32,2048]{1,0:T(8,128)(2,1)S(1)} %broadcast_select_fusion.10), channel_id=1, source_target_pairs={{4,0},{8,4},{12,8},{14,12},{10,14},{6,10},{2,6},{0,2},{5,1},{9,5},... | collective-permute-start | bytes 393224 | tf_op jit(solution)/shard_map/ppermute | solution.py:823
  35.5 5.2 %collective-permute-start.5 = (bf16[32,2048]{1,0:T(8,128)(2,1)S(1)}, bf16[32,2048]{1,0:T(8,128)(2,1)S(1)}, u32[]{:S(2)}, u32[]{:S(2)}) collective-permute-start(bf16[32,2048]{1,0:T(8,128)(2,1)S(1)} %broadcast_select_fusion.11), channel_id=1, source_target_pairs={{0,4},{4,8},{8,12},{12,14},{14,10},{10,6},{6,2},{2,0},{1,5},{5,9},... | collective-permute-start | bytes 393224 | tf_op jit(solution)/shard_map/ppermute | solution.py:820
  36.4 13.9 %collective-permute-start.20 = (bf16[128,896]{1,0:T(8,128)(2,1)S(1)}, bf16[128,896]{1,0:T(8,128)(2,1)S(1)}, u32[]{:S(2)}, u32[]{:S(2)}) collective-permute-start(bf16[128,896]{1,0:T(8,128)(2,1)S(1)} %share.1), channel_id=1, source_target_pairs={{0,1},{1,0},{2,3},{3,2},{4,5},{5,4},{6,7},{7,6},{8,9},{9,8},{10,11... | collective-permute-start | bytes 688136 | tf_op jit(solution)/shard_map/ppermute | solution.py:826
  36.5 6.4 %collective-permute-start.17 = (bf16[32,2048]{1,0:T(8,128)(2,1)S(1)}, bf16[32,2048]{1,0:T(8,128)(2,1)S(1)}, u32[]{:S(2)}, u32[]{:S(2)}) collective-permute-start(bf16[32,2048]{1,0:T(8,128)(2,1)S(1)} %broadcast_select_fusion.2), channel_id=1, source_target_pairs={{4,0},{8,4},{12,8},{14,12},{10,14},{6,10},{2,6},{0,2},{5,1},{9,5},... | collective-permute-start | bytes 393224 | tf_op jit(solution)/shard_map/ppermute | solution.py:823
  39.0 6.3 %collective-permute-start.16 = (bf16[32,2048]{1,0:T(8,128)(2,1)S(1)}, bf16[32,2048]{1,0:T(8,128)(2,1)S(1)}, u32[]{:S(2)}, u32[]{:S(2)}) collective-permute-start(bf16[32,2048]{1,0:T(8,128)(2,1)S(1)} %broadcast_select_fusion.3), channel_id=1, source_target_pairs={{0,4},{4,8},{8,12},{12,14},{14,10},{10,6},{6,2},{2,0},{1,5},{5,9},... | collective-permute-start | bytes 393224 | tf_op jit(solution)/shard_map/ppermute | solution.py:820
  40.7 6.8 %collective-permute-start.8 = (bf16[32,2048]{1,0:T(8,128)(2,1)S(1)}, bf16[32,2048]{1,0:T(8,128)(2,1)S(1)}, u32[]{:S(2)}, u32[]{:S(2)}) collective-permute-start(bf16[32,2048]{1,0:T(8,128)(2,1)S(1)} %broadcast_select_fusion.8), channel_id=1, source_target_pairs={{4,0},{8,4},{12,8},{14,12},{10,14},{6,10},{2,6},{0,2},{5,1},{9,5},... | collective-permute-start | bytes 393224 | tf_op jit(solution)/shard_map/ppermute | solution.py:823
  41.4 6.8 %collective-permute-start.7 = (bf16[32,2048]{1,0:T(8,128)(2,1)S(1)}, bf16[32,2048]{1,0:T(8,128)(2,1)S(1)}, u32[]{:S(2)}, u32[]{:S(2)}) collective-permute-start(bf16[32,2048]{1,0:T(8,128)(2,1)S(1)} %broadcast_select_fusion.9), channel_id=1, source_target_pairs={{0,4},{4,8},{8,12},{12,14},{14,10},{10,6},{6,2},{2,0},{1,5},{5,9},... | collective-permute-start | bytes 393224 | tf_op jit(solution)/shard_map/ppermute | solution.py:820
  42.9 16.8 %slice-start.2 = ((s8[8257536]{0:T(1024)(128)(4,1)}), s8[4194304]{0:T(1024)(128)(4,1)S(1)}, s32[]{:S(2)}) async-start(s8[8257536]{0:T(1024)(128)(4,1)} %bitcast.16), calls=%async_computation.2 | async-start | bytes 8388608
  45.4 5.7 %collective-permute-start.18 = (bf16[32,2048]{1,0:T(8,128)(2,1)S(1)}, bf16[32,2048]{1,0:T(8,128)(2,1)S(1)}, u32[]{:S(2)}, u32[]{:S(2)}) collective-permute-start(bf16[32,2048]{1,0:T(8,128)(2,1)S(1)} %broadcast_select_fusion.1), channel_id=1, source_target_pairs={{0,4},{4,8},{8,12},{12,14},{14,10},{10,6},{6,2},{2,0},{1,5},{5,9},... | collective-permute-start | bytes 393224 | tf_op jit(solution)/shard_map/ppermute | solution.py:820
  45.5 6.1 %collective-permute-start.19 = (bf16[32,2048]{1,0:T(8,128)(2,1)S(1)}, bf16[32,2048]{1,0:T(8,128)(2,1)S(1)}, u32[]{:S(2)}, u32[]{:S(2)}) collective-permute-start(bf16[32,2048]{1,0:T(8,128)(2,1)S(1)} %broadcast_select_fusion), channel_id=1, source_target_pairs={{4,0},{8,4},{12,8},{14,12},{10,14},{6,10},{2,6},{0,2},{5,1},{9,5},... | collective-permute-start | bytes 393224 | tf_op jit(solution)/shard_map/ppermute | solution.py:823
  48.2 5.4 %collective-permute-start.10 = (bf16[32,2048]{1,0:T(8,128)(2,1)S(1)}, bf16[32,2048]{1,0:T(8,128)(2,1)S(1)}, u32[]{:S(2)}, u32[]{:S(2)}) collective-permute-start(bf16[32,2048]{1,0:T(8,128)(2,1)S(1)} %broadcast_select_fusion.6), channel_id=1, source_target_pairs={{4,0},{8,4},{12,8},{14,12},{10,14},{6,10},{2,6},{0,2},{5,1},{9,5},... | collective-permute-start | bytes 393224 | tf_op jit(solution)/shard_map/ppermute | solution.py:823
  48.7 5.0 %collective-permute-start.9 = (bf16[32,2048]{1,0:T(8,128)(2,1)S(1)}, bf16[32,2048]{1,0:T(8,128)(2,1)S(1)}, u32[]{:S(2)}, u32[]{:S(2)}) collective-permute-start(bf16[32,2048]{1,0:T(8,128)(2,1)S(1)} %broadcast_select_fusion.7), channel_id=1, source_target_pairs={{0,4},{4,8},{8,12},{12,14},{14,10},{10,6},{6,2},{2,0},{1,5},{5,9},... | collective-permute-start | bytes 393224 | tf_op jit(solution)/shard_map/ppermute | solution.py:820
  51.6 8.1 %slice-start = ((s8[8257536]{0:T(1024)(128)(4,1)}), s8[4194304]{0:T(1024)(128)(4,1)S(1)}, s32[]{:S(2)}) async-start(s8[8257536]{0:T(1024)(128)(4,1)} %bitcast.9), calls=%async_computation | async-start | bytes 8388608
  53.5 6.1 %slice-start.1 = ((s8[8257536]{0:T(1024)(128)(4,1)}), s8[4063232]{0:T(1024)(128)(4,1)S(1)}, s32[]{:S(2)}) async-start(s8[8257536]{0:T(1024)(128)(4,1)} %bitcast.9), calls=%async_computation.1 | async-start | bytes 8126464
  55.7 1.6 %collective-permute-start.21 = (bf16[144,896]{1,0:T(8,128)(2,1)S(1)}, bf16[144,896]{1,0:T(8,128)(2,1)S(1)}, u32[]{:S(2)}, u32[]{:S(2)}) collective-permute-start(bf16[144,896]{1,0:T(8,128)(2,1)S(1)} %get-tuple-element.198), channel_id=1, source_target_pairs={{0,1},{1,0},{2,3},{3,2},{4,5},{5,4},{6,7},{7,6},{8,9},{9,8},{10,11... | collective-permute-start | bytes 774152 | tf_op jit(solution)/shard_map/ppermute | solution.py:826
  57.4 2.2 %collective-permute-start.24 = (bf16[144,896]{1,0:T(8,128)(2,1)S(1)}, bf16[144,896]{1,0:T(8,128)(2,1)S(1)}, u32[]{:S(2)}, u32[]{:S(2)}) collective-permute-start(bf16[144,896]{1,0:T(8,128)(2,1)S(1)} %add_convert_fusion.refs_0_.refs_1_), channel_id=1, source_target_pairs={{0,1},{1,0},{2,3},{3,2},{4,5},{5,4},{6,7},{7,6},{8,9},{9,8},{10,11... | collective-permute-start | bytes 774152 | tf_op jit(solution)/shard_map/ppermute | solution.py:826
  57.6 8.5 %collective-permute-start.22 = (bf16[144,896]{1,0:T(8,128)(2,1)S(1)}, bf16[144,896]{1,0:T(8,128)(2,1)S(1)}, u32[]{:S(2)}, u32[]{:S(2)}) collective-permute-start(bf16[144,896]{1,0:T(8,128)(2,1)S(1)} %add_convert_fusion.refs_0_.refs_1_), channel_id=1, source_target_pairs={{0,4},{4,8},{8,12},{12,14},{14,10},{10,6},{6,2},{2,0},{1,5},{5,9},... | collective-permute-start | bytes 774152 | tf_op jit(solution)/shard_map/ppermute | solution.py:820
  59.2 8.2 %collective-permute-start.23 = (bf16[144,896]{1,0:T(8,128)(2,1)S(1)}, bf16[144,896]{1,0:T(8,128)(2,1)S(1)}, u32[]{:S(2)}, u32[]{:S(2)}) collective-permute-start(bf16[144,896]{1,0:T(8,128)(2,1)S(1)} %add_convert_fusion.refs_0_.refs_1_), channel_id=1, source_target_pairs={{4,0},{8,4},{12,8},{14,12},{10,14},{6,10},{2,6},{0,2},{5,1},{9,5},... | collective-permute-start | bytes 774152 | tf_op jit(solution)/shard_map/ppermute | solution.py:823
  67.4 2.2 %collective-permute-start.27 = (bf16[288,896]{1,0:T(8,128)(2,1)S(1)}, bf16[288,896]{1,0:T(8,128)(2,1)S(1)}, u32[]{:S(2)}, u32[]{:S(2)}) collective-permute-start(bf16[288,896]{1,0:T(8,128)(2,1)S(1)} %pad_maximum_fusion), channel_id=1, source_target_pairs={{0,1},{1,0},{2,3},{3,2},{4,5},{5,4},{6,7},{7,6},{8,9},{9,8},{10,11... | collective-permute-start | bytes 1548296 | tf_op jit(solution)/shard_map/ppermute | solution.py:826
  67.5 8.6 %collective-permute-start.25 = (bf16[144,896]{1,0:T(8,128)(2,1)S(1)}, bf16[144,896]{1,0:T(8,128)(2,1)S(1)}, u32[]{:S(2)}, u32[]{:S(2)}) collective-permute-start(bf16[144,896]{1,0:T(8,128)(2,1)S(1)} %collective-permute-done.22.refs_0_.refs_2_.refs_3_), channel_id=1, source_target_pairs={{0,4},{4,8},{8,12},{12,14},{14,10},{10,6},{6,2},{2,0},{1,5},{5,9},... | collective-permute-start | bytes 774152 | tf_op jit(solution)/shard_map/ppermute | solution.py:820
  68.4 8.3 %collective-permute-start.26 = (bf16[144,896]{1,0:T(8,128)(2,1)S(1)}, bf16[144,896]{1,0:T(8,128)(2,1)S(1)}, u32[]{:S(2)}, u32[]{:S(2)}) collective-permute-start(bf16[144,896]{1,0:T(8,128)(2,1)S(1)} %collective-permute-done.23.refs_1_.refs_4_.refs_5_), channel_id=1, source_target_pairs={{4,0},{8,4},{12,8},{14,12},{10,14},{6,10},{2,6},{0,2},{5,1},{9,5},... | collective-permute-start | bytes 774152 | tf_op jit(solution)/shard_map/ppermute | solution.py:823
  76.8 2.2 %collective-permute-start.30 = (bf16[288,896]{1,0:T(8,128)(2,1)S(1)}, bf16[288,896]{1,0:T(8,128)(2,1)S(1)}, u32[]{:S(2)}, u32[]{:S(2)}) collective-permute-start(bf16[288,896]{1,0:T(8,128)(2,1)S(1)} %pad_maximum_fusion.1), channel_id=1, source_target_pairs={{0,1},{1,0},{2,3},{3,2},{4,5},{5,4},{6,7},{7,6},{8,9},{9,8},{10,11... | collective-permute-start | bytes 1548296 | tf_op jit(solution)/shard_map/ppermute | solution.py:826
  76.8 8.6 %collective-permute-start.28 = (bf16[144,896]{1,0:T(8,128)(2,1)S(1)}, bf16[144,896]{1,0:T(8,128)(2,1)S(1)}, u32[]{:S(2)}, u32[]{:S(2)}) collective-permute-start(bf16[144,896]{1,0:T(8,128)(2,1)S(1)} %collective-permute-done.25.refs_0_.refs_6_.refs_7_), channel_id=1, source_target_pairs={{0,4},{4,8},{8,12},{12,14},{14,10},{10,6},{6,2},{2,0},{1,5},{5,9},... | collective-permute-start | bytes 774152 | tf_op jit(solution)/shard_map/ppermute | solution.py:820
  78.3 8.3 %collective-permute-start.29 = (bf16[144,896]{1,0:T(8,128)(2,1)S(1)}, bf16[144,896]{1,0:T(8,128)(2,1)S(1)}, u32[]{:S(2)}, u32[]{:S(2)}) collective-permute-start(bf16[144,896]{1,0:T(8,128)(2,1)S(1)} %collective-permute-done.26.refs_1_.refs_8_.refs_9_), channel_id=1, source_target_pairs={{4,0},{8,4},{12,8},{14,12},{10,14},{6,10},{2,6},{0,2},{5,1},{9,5},... | collective-permute-start | bytes 774152 | tf_op jit(solution)/shard_map/ppermute | solution.py:823
  86.6 10.3 %slice-start.4 = ((s8[8257536]{0:T(1024)(128)(4,1)}), s8[4194304]{0:T(1024)(128)(4,1)S(1)}, s32[]{:S(2)}) async-start(s8[8257536]{0:T(1024)(128)(4,1)} %bitcast.23), calls=%async_computation.4 | async-start | bytes 8388608
  86.6 2.3 %collective-permute-start.33 = (bf16[288,896]{1,0:T(8,128)(2,1)S(1)}, bf16[288,896]{1,0:T(8,128)(2,1)S(1)}, u32[]{:S(2)}, u32[]{:S(2)}) collective-permute-start(bf16[288,896]{1,0:T(8,128)(2,1)S(1)} %pad_maximum_fusion.2), channel_id=1, source_target_pairs={{0,1},{1,0},{2,3},{3,2},{4,5},{5,4},{6,7},{7,6},{8,9},{9,8},{10,11... | collective-permute-start | bytes 1548296 | tf_op jit(solution)/shard_map/ppermute | solution.py:826
  86.7 6.9 %collective-permute-start.31 = (bf16[80,896]{1,0:T(8,128)(2,1)S(1)}, bf16[80,896]{1,0:T(8,128)(2,1)S(1)}, u32[]{:S(2)}, u32[]{:S(2)}) collective-permute-start(bf16[80,896]{1,0:T(8,128)(2,1)S(1)} %slice.18), channel_id=1, source_target_pairs={{0,4},{4,8},{8,12},{12,14},{14,10},{10,6},{6,2},{2,0},{1,5},{5,9},... | collective-permute-start | bytes 430088 | tf_op jit(solution)/shard_map/ppermute | solution.py:820
  88.2 8.7 %slice-start.5 = ((s8[8257536]{0:T(1024)(128)(4,1)}), s8[4063232]{0:T(1024)(128)(4,1)S(1)}, s32[]{:S(2)}) async-start(s8[8257536]{0:T(1024)(128)(4,1)} %bitcast.23), calls=%async_computation.5 | async-start | bytes 8126464
  88.2 5.3 %collective-permute-start.32 = (bf16[64,896]{1,0:T(8,128)(2,1)S(1)}, bf16[64,896]{1,0:T(8,128)(2,1)S(1)}, u32[]{:S(2)}, u32[]{:S(2)}) collective-permute-start(bf16[64,896]{1,0:T(8,128)(2,1)S(1)} %slice.19), channel_id=1, source_target_pairs={{4,0},{8,4},{12,8},{14,12},{10,14},{6,10},{2,6},{0,2},{5,1},{9,5},... | collective-permute-start | bytes 344072 | tf_op jit(solution)/shard_map/ppermute | solution.py:823
  93.6 1.5 %collective-permute-start.34 = (bf16[80,896]{1,0:T(8,128)(2,1)S(1)}, bf16[80,896]{1,0:T(8,128)(2,1)S(1)}, u32[]{:S(2)}, u32[]{:S(2)}) collective-permute-start(bf16[80,896]{1,0:T(8,128)(2,1)S(1)} %collective-permute-done.31.refs_0_), channel_id=1, source_target_pairs={{0,1},{1,0},{2,3},{3,2},{4,5},{5,4},{6,7},{7,6},{8,9},{9,8},{10,11... | collective-permute-start | bytes 430088 | tf_op jit(solution)/shard_map/ppermute | solution.py:826
  93.6 1.5 %collective-permute-start.35 = (bf16[64,896]{1,0:T(8,128)(2,1)S(1)}, bf16[64,896]{1,0:T(8,128)(2,1)S(1)}, u32[]{:S(2)}, u32[]{:S(2)}) collective-permute-start(bf16[64,896]{1,0:T(8,128)(2,1)S(1)} %collective-permute-done.32.refs_1_), channel_id=1, source_target_pairs={{0,1},{1,0},{2,3},{3,2},{4,5},{5,4},{6,7},{7,6},{8,9},{9,8},{10,11... | collective-permute-start | bytes 344072 | tf_op jit(solution)/shard_map/ppermute | solution.py:826
  98.2 4.4 %collective-permute-start.46 = (bf16[144,3584]{1,0:T(8,128)(2,1)S(1)}, bf16[144,3584]{1,0:T(8,128)(2,1)S(1)}, u32[]{:S(2)}, u32[]{:S(2)}) collective-permute-start(bf16[144,3584]{1,0:T(8,128)(2,1)S(1)} %contract.7), channel_id=1, source_target_pairs={{0,1},{1,0},{2,3},{3,2},{4,5},{5,4},{6,7},{7,6},{8,9},{9,8},{10,11... | collective-permute-start | bytes 3096584 | tf_op jit(solution)/shard_map/ppermute | solution.py:826
  99.8 6.7 %collective-permute-start.36 = (bf16[144,3584]{1,0:T(8,128)(2,1)S(1)}, bf16[144,3584]{1,0:T(8,128)(2,1)S(1)}, u32[]{:S(2)}, u32[]{:S(2)}) collective-permute-start(bf16[144,3584]{1,0:T(8,128)(2,1)S(1)} %contract.6), channel_id=1, source_target_pairs={{0,1},{1,0},{2,3},{3,2},{4,5},{5,4},{6,7},{7,6},{8,9},{9,8},{10,11... | collective-permute-start | bytes 3096584 | tf_op jit(solution)/shard_map/ppermute | solution.py:826
  103.5 5.9 %collective-permute-start.48 = (bf16[16,3584]{1,0:T(8,128)(2,1)S(1)}, bf16[16,3584]{1,0:T(8,128)(2,1)S(1)}, u32[]{:S(2)}, u32[]{:S(2)}) collective-permute-start(bf16[16,3584]{1,0:T(8,128)(2,1)S(1)} %convert_element_type.157), channel_id=1, source_target_pairs={{4,0},{8,4},{12,8},{14,12},{10,14},{6,10},{2,6},{0,2},{5,1},{9,5},... | collective-permute-start | bytes 344072 | tf_op jit(solution)/shard_map/ppermute | solution.py:823
  104.8 5.4 %collective-permute-start.47 = (bf16[16,3584]{1,0:T(8,128)(2,1)S(1)}, bf16[16,3584]{1,0:T(8,128)(2,1)S(1)}, u32[]{:S(2)}, u32[]{:S(2)}) collective-permute-start(bf16[16,3584]{1,0:T(8,128)(2,1)S(1)} %convert_element_type.156), channel_id=1, source_target_pairs={{0,4},{4,8},{8,12},{12,14},{14,10},{10,6},{6,2},{2,0},{1,5},{5,9},... | collective-permute-start | bytes 344072 | tf_op jit(solution)/shard_map/ppermute | solution.py:820
  107.3 5.1 %collective-permute-start.38 = (bf16[16,3584]{1,0:T(8,128)(2,1)S(1)}, bf16[16,3584]{1,0:T(8,128)(2,1)S(1)}, u32[]{:S(2)}, u32[]{:S(2)}) collective-permute-start(bf16[16,3584]{1,0:T(8,128)(2,1)S(1)} %convert_element_type.136), channel_id=1, source_target_pairs={{4,0},{8,4},{12,8},{14,12},{10,14},{6,10},{2,6},{0,2},{5,1},{9,5},... | collective-permute-start | bytes 344072 | tf_op jit(solution)/shard_map/ppermute | solution.py:823
  108.0 5.2 %collective-permute-start.37 = (bf16[16,3584]{1,0:T(8,128)(2,1)S(1)}, bf16[16,3584]{1,0:T(8,128)(2,1)S(1)}, u32[]{:S(2)}, u32[]{:S(2)}) collective-permute-start(bf16[16,3584]{1,0:T(8,128)(2,1)S(1)} %convert_element_type.135), channel_id=1, source_target_pairs={{0,4},{4,8},{8,12},{12,14},{14,10},{10,6},{6,2},{2,0},{1,5},{5,9},... | collective-permute-start | bytes 344072 | tf_op jit(solution)/shard_map/ppermute | solution.py:820
  110.2 5.0 %collective-permute-start.50 = (bf16[16,3584]{1,0:T(8,128)(2,1)S(1)}, bf16[16,3584]{1,0:T(8,128)(2,1)S(1)}, u32[]{:S(2)}, u32[]{:S(2)}) collective-permute-start(bf16[16,3584]{1,0:T(8,128)(2,1)S(1)} %add_convert_fusion.5), channel_id=1, source_target_pairs={{4,0},{8,4},{12,8},{14,12},{10,14},{6,10},{2,6},{0,2},{5,1},{9,5},... | collective-permute-start | bytes 344072 | tf_op jit(solution)/shard_map/ppermute | solution.py:823
  110.9 5.7 %collective-permute-start.49 = (bf16[16,3584]{1,0:T(8,128)(2,1)S(1)}, bf16[16,3584]{1,0:T(8,128)(2,1)S(1)}, u32[]{:S(2)}, u32[]{:S(2)}) collective-permute-start(bf16[16,3584]{1,0:T(8,128)(2,1)S(1)} %add_convert_fusion.6), channel_id=1, source_target_pairs={{0,4},{4,8},{8,12},{12,14},{14,10},{10,6},{6,2},{2,0},{1,5},{5,9},... | collective-permute-start | bytes 344072 | tf_op jit(solution)/shard_map/ppermute | solution.py:820
  113.2 6.6 %collective-permute-start.39 = (bf16[16,3584]{1,0:T(8,128)(2,1)S(1)}, bf16[16,3584]{1,0:T(8,128)(2,1)S(1)}, u32[]{:S(2)}, u32[]{:S(2)}) collective-permute-start(bf16[16,3584]{1,0:T(8,128)(2,1)S(1)} %add_convert_fusion.12), channel_id=1, source_target_pairs={{0,4},{4,8},{8,12},{12,14},{14,10},{10,6},{6,2},{2,0},{1,5},{5,9},... | collective-permute-start | bytes 344072 | tf_op jit(solution)/shard_map/ppermute | solution.py:820
  114.8 5.0 %collective-permute-start.40 = (bf16[16,3584]{1,0:T(8,128)(2,1)S(1)}, bf16[16,3584]{1,0:T(8,128)(2,1)S(1)}, u32[]{:S(2)}, u32[]{:S(2)}) collective-permute-start(bf16[16,3584]{1,0:T(8,128)(2,1)S(1)} %add_convert_fusion.11), channel_id=1, source_target_pairs={{4,0},{8,4},{12,8},{14,12},{10,14},{6,10},{2,6},{0,2},{5,1},{9,5},... | collective-permute-start | bytes 344072 | tf_op jit(solution)/shard_map/ppermute | solution.py:823
  116.7 5.9 %collective-permute-start.52 = (bf16[16,3584]{1,0:T(8,128)(2,1)S(1)}, bf16[16,3584]{1,0:T(8,128)(2,1)S(1)}, u32[]{:S(2)}, u32[]{:S(2)}) collective-permute-start(bf16[16,3584]{1,0:T(8,128)(2,1)S(1)} %add_convert_fusion.3), channel_id=1, source_target_pairs={{4,0},{8,4},{12,8},{14,12},{10,14},{6,10},{2,6},{0,2},{5,1},{9,5},... | collective-permute-start | bytes 344072 | tf_op jit(solution)/shard_map/ppermute | solution.py:823
  117.4 5.3 %collective-permute-start.51 = (bf16[16,3584]{1,0:T(8,128)(2,1)S(1)}, bf16[16,3584]{1,0:T(8,128)(2,1)S(1)}, u32[]{:S(2)}, u32[]{:S(2)}) collective-permute-start(bf16[16,3584]{1,0:T(8,128)(2,1)S(1)} %add_convert_fusion.4), channel_id=1, source_target_pairs={{0,4},{4,8},{8,12},{12,14},{14,10},{10,6},{6,2},{2,0},{1,5},{5,9},... | collective-permute-start | bytes 344072 | tf_op jit(solution)/shard_map/ppermute | solution.py:820
  119.9 5.9 %collective-permute-start.42 = (bf16[16,3584]{1,0:T(8,128)(2,1)S(1)}, bf16[16,3584]{1,0:T(8,128)(2,1)S(1)}, u32[]{:S(2)}, u32[]{:S(2)}) collective-permute-start(bf16[16,3584]{1,0:T(8,128)(2,1)S(1)} %add_convert_fusion.9), channel_id=1, source_target_pairs={{4,0},{8,4},{12,8},{14,12},{10,14},{6,10},{2,6},{0,2},{5,1},{9,5},... | collective-permute-start | bytes 344072 | tf_op jit(solution)/shard_map/ppermute | solution.py:823
  120.2 5.8 %collective-permute-start.41 = (bf16[16,3584]{1,0:T(8,128)(2,1)S(1)}, bf16[16,3584]{1,0:T(8,128)(2,1)S(1)}, u32[]{:S(2)}, u32[]{:S(2)}) collective-permute-start(bf16[16,3584]{1,0:T(8,128)(2,1)S(1)} %add_convert_fusion.10), channel_id=1, source_target_pairs={{0,4},{4,8},{8,12},{12,14},{14,10},{10,6},{6,2},{2,0},{1,5},{5,9},... | collective-permute-start | bytes 344072 | tf_op jit(solution)/shard_map/ppermute | solution.py:820
  122.7 6.6 %collective-permute-start.53 = (bf16[16,3584]{1,0:T(8,128)(2,1)S(1)}, bf16[16,3584]{1,0:T(8,128)(2,1)S(1)}, u32[]{:S(2)}, u32[]{:S(2)}) collective-permute-start(bf16[16,3584]{1,0:T(8,128)(2,1)S(1)} %add_convert_fusion.2), channel_id=1, source_target_pairs={{0,4},{4,8},{8,12},{12,14},{14,10},{10,6},{6,2},{2,0},{1,5},{5,9},... | collective-permute-start | bytes 344072 | tf_op jit(solution)/shard_map/ppermute | solution.py:820
  124.7 4.8 %collective-permute-start.54 = (bf16[16,3584]{1,0:T(8,128)(2,1)S(1)}, bf16[16,3584]{1,0:T(8,128)(2,1)S(1)}, u32[]{:S(2)}, u32[]{:S(2)}) collective-permute-start(bf16[16,3584]{1,0:T(8,128)(2,1)S(1)} %add_convert_fusion.1), channel_id=1, source_target_pairs={{4,0},{8,4},{12,8},{14,12},{10,14},{6,10},{2,6},{0,2},{5,1},{9,5},... | collective-permute-start | bytes 344072 | tf_op jit(solution)/shard_map/ppermute | solution.py:823
  126.1 4.9 %collective-permute-start.43 = (bf16[16,3584]{1,0:T(8,128)(2,1)S(1)}, bf16[16,3584]{1,0:T(8,128)(2,1)S(1)}, u32[]{:S(2)}, u32[]{:S(2)}) collective-permute-start(bf16[16,3584]{1,0:T(8,128)(2,1)S(1)} %add_convert_fusion.8), channel_id=1, source_target_pairs={{0,4},{4,8},{8,12},{12,14},{14,10},{10,6},{6,2},{2,0},{1,5},{5,9},... | collective-permute-start | bytes 344072 | tf_op jit(solution)/shard_map/ppermute | solution.py:820
  128.7 4.8 %collective-permute-start.44 = (bf16[16,3584]{1,0:T(8,128)(2,1)S(1)}, bf16[16,3584]{1,0:T(8,128)(2,1)S(1)}, u32[]{:S(2)}, u32[]{:S(2)}) collective-permute-start(bf16[16,3584]{1,0:T(8,128)(2,1)S(1)} %add_convert_fusion.7), channel_id=1, source_target_pairs={{4,0},{8,4},{12,8},{14,12},{10,14},{6,10},{2,6},{0,2},{5,1},{9,5},... | collective-permute-start | bytes 344072 | tf_op jit(solution)/shard_map/ppermute | solution.py:823
  133.7 1.4 %collective-permute-start.45 = (bf16[16,3584]{1,0:T(8,128)(2,1)S(1)}, bf16[16,3584]{1,0:T(8,128)(2,1)S(1)}, u32[]{:S(2)}, u32[]{:S(2)}) collective-permute-start(bf16[16,3584]{1,0:T(8,128)(2,1)S(1)} %get-tuple-element.271), channel_id=1, source_target_pairs={{0,1},{1,0},{2,3},{3,2},{4,5},{5,4},{6,7},{7,6},{8,9},{9,8},{10,11... | collective-permute-start | bytes 344072 | tf_op jit(solution)/shard_map/ppermute | solution.py:826
  133.9 1.5 %collective-permute-start.55 = (bf16[16,3584]{1,0:T(8,128)(2,1)S(1)}, bf16[16,3584]{1,0:T(8,128)(2,1)S(1)}, u32[]{:S(2)}, u32[]{:S(2)}) collective-permute-start(bf16[16,3584]{1,0:T(8,128)(2,1)S(1)} %get-tuple-element.277), channel_id=1, source_target_pairs={{0,1},{1,0},{2,3},{3,2},{4,5},{5,4},{6,7},{7,6},{8,9},{9,8},{10,11... | collective-permute-start | bytes 344072 | tf_op jit(solution)/shard_map/ppermute | solution.py:826
  (2 other events, 12.3 us)

commit v16 on v15

--- a/solution.py
+++ b/solution.py
@@ -384,10 +384,18 @@
     )(tab, in_hbm(vw), decoded, queries, keys, fresh)
 
 
+def partner(rank, j, ranks, back=False):
+    if ranks & (ranks - 1) == 0:
+        return rank ^ j
+    if isinstance(rank, int):
+        return (rank - j if back else rank + j) % ranks
+    other = rank - j if back else rank + j
+    return jnp.where(other < 0, other + ranks, jnp.where(other >= ranks, other - ranks, other))
+
+
 def pack_kernel(ranks, cores, features, tab, res, *outs):
     for k in range(ranks // cores):
-        target = tab[RANK] + k + (ranks // cores) * tab[CORE]
-        target = jnp.where(target >= ranks, target - ranks, target)
+        target = partner(tab[RANK], k + (ranks // cores) * tab[CORE], ranks)
 
         def put(columns, k=k):
             outs[k][...] = res[:, columns]
@@ -554,8 +562,7 @@
             put(ranks, extra())
 
     def owner_of(k, c):
-        owner = rank - k - count * c
-        return jnp.where(owner < 0, owner + ranks, owner)
+        return partner(rank, k + count * c, ranks, True)
 
     low = pl.ds(pl.multiple_of(core * half, half), half)
     high = pl.ds(pl.multiple_of(block + core * half, half), half)
@@ -840,7 +847,7 @@
 
     def send_piece(k):
         pairs = [
-            (i * cores + c, (i + k + len(packed) * c) % ranks * cores + c)
+            (i * cores + c, partner(i, k + len(packed) * c, ranks) * cores + c)
             for i in range(ranks)
             for c in range(cores)
             if k + c > 0

time: 137 us -> 137 us (level)
  starting transfers between devices: 53.5 us -> 55.6 us
  waiting for transfers between devices: 39.1 us -> 37.1 us
    ppermute x20, waiting for transfers between devices: 25 us -> 21.6 us  [send_next(): return lax.ppermute(x, 'blk', forward)]
    ppermute x12, starting transfers between devices: 2.33 us -> 5.54 us  [swap(): return lax.ppermute(x, 'head', exchange)]
    ppermute x20, waiting for transfers between devices: 10.3 us -> 12.7 us  [send_prev(): return lax.ppermute(x, 'blk', backward)]
    ppermute x20, starting transfers between devices: 16.8 us -> 19.1 us  [send_prev(): return lax.ppermute(x, 'blk', backward)]
    ppermute x4, starting transfers between devices: 6.27 us -> 4.21 us  [send_piece(): pieces[k] = lax.ppermute(packed[k], ('blk', 'head'), pairs)]
  transfers between devices with their start and end apart: 56 -> 56, of which waited for: 32 -> 28; matrix products, arithmetic and copies ran while one was open for 1% -> 1% of each run, Pallas kernels for 18% -> 18%
where the time goes in v16:
time: 137 us; the launch traced here: 136 us
  starting transfers between devices  55.6 us (41%)
  Pallas kernels  38 us (28%)
  waiting for transfers between devices  37.1 us (27%)
  between operations  2.58 us (2%)
  other arithmetic  2.33 us (2%)
    ppermute x20, starting transfers between devices, send_next(): return lax.ppermute(x, 'blk', forward)  26.7 us
    ppermute x20, waiting for transfers between devices, send_next(): return lax.ppermute(x, 'blk', forward)  21.6 us
    ppermute x20, starting transfers between devices, send_prev(): return lax.ppermute(x, 'blk', backward)  19.1 us
    ppermute x20, waiting for transfers between devices, send_prev(): return lax.ppermute(x, 'blk', backward)  12.7 us
    pallas_call x5, Pallas kernels, expand(): pl.pallas_call(functools.partial(expand_kernel, pieces, len(theirs), firs...  12.1 us
    pallas_call x1, Pallas kernels, attend(): pl.pallas_call(functools.partial(attend_kernel, table, order, heads, 0, c...  8.22 us
    ppermute x12, starting transfers between devices, swap(): return lax.ppermute(x, 'head', exchange)  5.54 us
    pallas_call x4, Pallas kernels, contract(): pl.pallas_call(functools.partial(contract_kernel, part * columns), grid=(...  5.01 us
  transfers between devices with their start and end apart: 56, of which 28 were waited for; matrix products, arithmetic and copies ran while one was open for 1% of the time, Pallas kernels for 18%

profile of v16, /device:TPU:0, one launch (start us, length us, event | category | flops | bytes accessed | tf_op | source)
XLA Modules:
  0.0 136.4 jit_solution(17952040560846552959)
XLA Ops:
  0.7 0.8 concatenate.24.refs_0_
  1.4 8.2 %attend.2 = (s32[60]{0:T(128)S(1)}, bf16[32,2048]{1,0:T(8,128)(2,1)S(1)}, bf16[32,2048]{1,0:T(8,128)(2,1)S(1)}, bf16[32,2048]{1,0:T(8,128)(2,1)S(1)}, bf16[128,5...) custom-call(s32[26]{0:T(128)S(1)} %concatenate.24.refs_0_, ...), custom_call_target="tpu_custom_call" | custom-call | flops 713031680 | bytes 6815744 | tf_op jit(solution)/shard_map/attend/pallas_call | solution.py:329
  9.6 3.1 %collective-permute-start.11 = (bf16[32,2048]{1,0:T(8,128)(2,1)S(1)}, bf16[32,2048]{1,0:T(8,128)(2,1)S(1)}, u32[]{:S(2)}, u32[]{:S(2)}) collective-permute-start(bf16[32,2048]{1,0:T(8,128)(2,1)S(1)} %get-tuple-element.168), channel_id=1, source_target_pairs={{0,4},{4,8},{8,12},{12,14},{14,10},{10,6},{6,2},{2,0},{1,5},{5,9},... | collective-permute-start | bytes 393224 | tf_op jit(solution)/shard_map/ppermute | solution.py:827
  13.4 1.9 %collective-permute-start.1 = (bf16[64,896]{1,0:T(8,128)(2,1)S(1)}, bf16[64,896]{1,0:T(8,128)(2,1)S(1)}, u32[]{:S(2)}, u32[]{:S(2)}) collective-permute-start(bf16[64,896]{1,0:T(8,128)(2,1)S(1)} %get-tuple-element.144), channel_id=1, source_target_pairs={{0,4},{1,13},{2,6},{3,15},{4,0},{5,9},{6,2},{7,11},{8,12},{9,5},{1... | collective-permute-start | bytes 344072 | tf_op jit(solution)/shard_map/ppermute | solution.py:855
  15.3 1.5 %collective-permute-start.2 = (bf16[64,896]{1,0:T(8,128)(2,1)S(1)}, bf16[64,896]{1,0:T(8,128)(2,1)S(1)}, u32[]{:S(2)}, u32[]{:S(2)}) collective-permute-start(bf16[64,896]{1,0:T(8,128)(2,1)S(1)} %get-tuple-element.145), channel_id=1, source_target_pairs={{0,6},{1,15},{2,4},{3,13},{4,2},{5,11},{6,0},{7,9},{8,14},{9,7},{1... | collective-permute-start | bytes 344072 | tf_op jit(solution)/shard_map/ppermute | solution.py:855
  17.7 4.7 %attend.3 = (bf16[32,2048]{1,0:T(8,128)(2,1)S(1)}, bf16[32,2048]{1,0:T(8,128)(2,1)S(1)}, bf16[32,2048]{1,0:T(8,128)(2,1)S(1)}) custom-call(s32[60]{0:T(128)S(1)} %get-tuple-element.140.tab.refs_0_, bf16[32,512,128]{2,1,0:T(8,128)(2,1)} %refs_1_.3, bf16[128,512]{1,0:T(8,128)(2,1)S(1)} %get-tuple-element.146.refs_2_, ...), custom_call_target="tpu_custom_call" | custom-call | flops 713031680 | bytes 2097152 | tf_op jit(solution)/shard_map/attend/pallas_call | solution.py:369
  22.4 0.7 collective-permute-start.14
  23.1 2.3 %collective-permute-start.4 = (bf16[32,2048]{1,0:T(8,128)(2,1)S(1)}, bf16[32,2048]{1,0:T(8,128)(2,1)S(1)}, u32[]{:S(2)}, u32[]{:S(2)}) collective-permute-start(bf16[32,2048]{1,0:T(8,128)(2,1)S(1)} %get-tuple-element.159.refs_0_), channel_id=1, source_target_pairs={{4,0},{8,4},{12,8},{14,12},{10,14},{6,10},{2,6},{0,2},{5,1},{9,5},... | collective-permute-start | bytes 393224 | tf_op jit(solution)/shard_map/ppermute | solution.py:830
  26.3 1.5 %collective-permute-start.13 = (bf16[32,2048]{1,0:T(8,128)(2,1)S(1)}, bf16[32,2048]{1,0:T(8,128)(2,1)S(1)}, u32[]{:S(2)}, u32[]{:S(2)}) collective-permute-start(bf16[32,2048]{1,0:T(8,128)(2,1)S(1)} %broadcast_select_fusion.5), channel_id=1, source_target_pairs={{0,4},{4,8},{8,12},{12,14},{14,10},{10,6},{6,2},{2,0},{1,5},{5,9},... | collective-permute-start | bytes 393224 | tf_op jit(solution)/shard_map/ppermute | solution.py:827
  28.3 2.0 %collective-permute-done.3.refs_1_ = bf16[32,2048]{1,0:T(8,128)(2,1)S(1)} collective-permute-done((bf16[32,2048]{1,0:T(8,128)(2,1)S(1)}, bf16[32,2048]{1,0:T(8,128)(2,1)S(1)}, u32[]{:S(2)}, u32[]{:S(2)}) %collective-permute-start.3) | collective-permute-done | bytes 131104 | tf_op jit(solution)/shard_map/ppermute | solution.py:827
  30.4 4.2 %collective-permute-start.6 = (bf16[32,2048]{1,0:T(8,128)(2,1)S(1)}, bf16[32,2048]{1,0:T(8,128)(2,1)S(1)}, u32[]{:S(2)}, u32[]{:S(2)}) collective-permute-start(bf16[32,2048]{1,0:T(8,128)(2,1)S(1)} %broadcast_select_fusion.10), channel_id=1, source_target_pairs={{4,0},{8,4},{12,8},{14,12},{10,14},{6,10},{2,6},{0,2},{5,1},{9,5},... | collective-permute-start | bytes 393224 | tf_op jit(solution)/shard_map/ppermute | solution.py:830
  35.1 3.3 %collective-permute-start.20 = (bf16[128,896]{1,0:T(8,128)(2,1)S(1)}, bf16[128,896]{1,0:T(8,128)(2,1)S(1)}, u32[]{:S(2)}, u32[]{:S(2)}) collective-permute-start(bf16[128,896]{1,0:T(8,128)(2,1)S(1)} %share.1), channel_id=1, source_target_pairs={{0,1},{1,0},{2,3},{3,2},{4,5},{5,4},{6,7},{7,6},{8,9},{9,8},{10,11... | collective-permute-start | bytes 688136 | tf_op jit(solution)/shard_map/ppermute | solution.py:833
  38.9 1.7 %collective-permute-start.16 = (bf16[32,2048]{1,0:T(8,128)(2,1)S(1)}, bf16[32,2048]{1,0:T(8,128)(2,1)S(1)}, u32[]{:S(2)}, u32[]{:S(2)}) collective-permute-start(bf16[32,2048]{1,0:T(8,128)(2,1)S(1)} %broadcast_select_fusion.3), channel_id=1, source_target_pairs={{0,4},{4,8},{8,12},{12,14},{14,10},{10,6},{6,2},{2,0},{1,5},{5,9},... | collective-permute-start | bytes 393224 | tf_op jit(solution)/shard_map/ppermute | solution.py:827
  41.0 2.1 %collective-permute-start.8 = (bf16[32,2048]{1,0:T(8,128)(2,1)S(1)}, bf16[32,2048]{1,0:T(8,128)(2,1)S(1)}, u32[]{:S(2)}, u32[]{:S(2)}) collective-permute-start(bf16[32,2048]{1,0:T(8,128)(2,1)S(1)} %broadcast_select_fusion.8), channel_id=1, source_target_pairs={{4,0},{8,4},{12,8},{14,12},{10,14},{6,10},{2,6},{0,2},{5,1},{9,5},... | collective-permute-start | bytes 393224 | tf_op jit(solution)/shard_map/ppermute | solution.py:830
  43.1 1.7 %collective-permute-done.17.refs_7_ = bf16[32,2048]{1,0:T(8,128)(2,1)S(1)} collective-permute-done((bf16[32,2048]{1,0:T(8,128)(2,1)S(1)}, bf16[32,2048]{1,0:T(8,128)(2,1)S(1)}, u32[]{:S(2)}, u32[]{:S(2)}) %collective-permute-start.17) | collective-permute-done | bytes 131104 | tf_op jit(solution)/shard_map/ppermute | solution.py:830
  44.9 2.1 %collective-permute-start.18 = (bf16[32,2048]{1,0:T(8,128)(2,1)S(1)}, bf16[32,2048]{1,0:T(8,128)(2,1)S(1)}, u32[]{:S(2)}, u32[]{:S(2)}) collective-permute-start(bf16[32,2048]{1,0:T(8,128)(2,1)S(1)} %broadcast_select_fusion.1), channel_id=1, source_target_pairs={{0,4},{4,8},{8,12},{12,14},{14,10},{10,6},{6,2},{2,0},{1,5},{5,9},... | collective-permute-start | bytes 393224 | tf_op jit(solution)/shard_map/ppermute | solution.py:827
  47.3 1.8 %collective-permute-done.7.refs_3_ = bf16[32,2048]{1,0:T(8,128)(2,1)S(1)} collective-permute-done((bf16[32,2048]{1,0:T(8,128)(2,1)S(1)}, bf16[32,2048]{1,0:T(8,128)(2,1)S(1)}, u32[]{:S(2)}, u32[]{:S(2)}) %collective-permute-start.7) | collective-permute-done | bytes 131104 | tf_op jit(solution)/shard_map/ppermute | solution.py:827
  49.8 1.5 %collective-permute-start.9 = (bf16[32,2048]{1,0:T(8,128)(2,1)S(1)}, bf16[32,2048]{1,0:T(8,128)(2,1)S(1)}, u32[]{:S(2)}, u32[]{:S(2)}) collective-permute-start(bf16[32,2048]{1,0:T(8,128)(2,1)S(1)} %broadcast_select_fusion.7), channel_id=1, source_target_pairs={{0,4},{4,8},{8,12},{12,14},{14,10},{10,6},{6,2},{2,0},{1,5},{5,9},... | collective-permute-start | bytes 393224 | tf_op jit(solution)/shard_map/ppermute | solution.py:827
  51.3 1.3 collective-permute-done.19.refs_8_
  52.7 1.9 %project.2.refs_10_ = f32[288,896]{1,0:T(8,128)S(1)} custom-call(s32[60]{0:T(128)S(1)} %get-tuple-element.140.tab.refs_0_, bf16[32,2048]{1,0:T(8,128)(2,1)S(1)} %get-tuple-element.186.refs_0_, bf16[32,2048]{1,0:T(8,128)(2,1)S(1)} %collective-permute-done.11.refs_1_, bf16[32,2048]{1,0:T(8,128)(2,1)S(1)} %collective-permute-done.13.refs_2_, ...), custom_call_target="tpu_custom_call" | custom-call | flops 1056964608 | bytes 4849664 | tf_op jit(solution)/shard_map/project/pallas_call | solution.py:522
  54.8 2.0 %project.3 = (f32[144,896]{1,0:T(8,128)S(1)}, bf16[144,896]{1,0:T(8,128)(2,1)S(1)}) custom-call(s32[60]{0:T(128)S(1)} %get-tuple-element.140.tab.refs_0_, bf16[32,2048]{1,0:T(8,128)(2,1)S(1)} %get-tuple-element.159.refs_0_, bf16[32,2048]{1,0:T(8,128)(2,1)S(1)} %collective-permute-done.3.refs_1_, bf16[32,2048]{1,0:T(8,128)(2,1)S(1)} %collective-permute-done.5.refs_2_, ...), custom_call_target="tpu_custom_call" | custom-call | flops 1056964608 | bytes 4849664 | tf_op jit(solution)/shard_map/project/pallas_call | solution.py:532
  57.5 0.9 collective-permute-done.21
  58.7 1.5 %collective-permute-start.22 = (bf16[144,896]{1,0:T(8,128)(2,1)S(1)}, bf16[144,896]{1,0:T(8,128)(2,1)S(1)}, u32[]{:S(2)}, u32[]{:S(2)}) collective-permute-start(bf16[144,896]{1,0:T(8,128)(2,1)S(1)} %add_convert_fusion.refs_0_.refs_1_), channel_id=1, source_target_pairs={{0,4},{4,8},{8,12},{12,14},{14,10},{10,6},{6,2},{2,0},{1,5},{5,9},... | collective-permute-start | bytes 774152 | tf_op jit(solution)/shard_map/ppermute | solution.py:827
  60.8 1.7 %expand.5 = (f32[288,576]{1,0:T(8,128)S(1)}, f32[288,576]{1,0:T(8,128)S(1)}, f32[288,1]{1,0:T(8,128)S(1)}) custom-call(s32[60]{0:T(128)S(1)} %get-tuple-element.140.tab.refs_0_, bf16[144,896]{1,0:T(8,128)(2,1)S(1)} %add_convert_fusion.refs_0_.refs_1_, bf16[144,896]{1,0:T(8,128)(2,1)S(1)} %collective-permute-done.24.refs_1_, f32[8,1,896]{2,1,0:T(1,128)S(1)} %bitcast.27, ...), custom_call_target="tpu_custom_call" | custom-call | flops 1 | bytes 1 | tf_op jit(solution)/shard_map/expand/pallas_call | solution.py:683
  62.5 4.8 %collective-permute-done.22.refs_0_.refs_2_.refs_3_ = bf16[144,896]{1,0:T(8,128)(2,1)S(1)} collective-permute-done((bf16[144,896]{1,0:T(8,128)(2,1)S(1)}, bf16[144,896]{1,0:T(8,128)(2,1)S(1)}, u32[]{:S(2)}, u32[]{:S(2)}) %collective-permute-start.22) | collective-permute-done | bytes 258080 | tf_op jit(solution)/shard_map/ppermute | solution.py:827
  67.3 1.1 collective-permute-done.23.refs_1_.refs_4_.refs_5_
  68.5 0.6 collective-permute-start.25
  69.2 1.4 %collective-permute-start.26 = (bf16[144,896]{1,0:T(8,128)(2,1)S(1)}, bf16[144,896]{1,0:T(8,128)(2,1)S(1)}, u32[]{:S(2)}, u32[]{:S(2)}) collective-permute-start(bf16[144,896]{1,0:T(8,128)(2,1)S(1)} %collective-permute-done.23.refs_1_.refs_4_.refs_5_), channel_id=1, source_target_pairs={{4,0},{8,4},{12,8},{14,12},{10,14},{6,10},{2,6},{0,2},{5,1},{9,5},... | collective-permute-start | bytes 774152 | tf_op jit(solution)/shard_map/ppermute | solution.py:830
  70.6 2.9 %expand.6 = (f32[288,576]{1,0:T(8,128)S(1)}, f32[288,576]{1,0:T(8,128)S(1)}, f32[288,1]{1,0:T(8,128)S(1)}) custom-call(s32[60]{0:T(128)S(1)} %get-tuple-element.140.tab.refs_0_, bf16[144,896]{1,0:T(8,128)(2,1)S(1)} %collective-permute-done.22.refs_0_.refs_2_.refs_3_, bf16[144,896]{1,0:T(8,128)(2,1)S(1)} %collective-permute-done.23.refs_1_.refs_4_.refs_5_, ...), custom_call_target="tpu_custom_call" | custom-call | flops 1 | bytes 1 | tf_op jit(solution)/shard_map/expand/pallas_call | solution.py:683
  73.5 3.7 %collective-permute-done.25.refs_0_.refs_6_.refs_7_ = bf16[144,896]{1,0:T(8,128)(2,1)S(1)} collective-permute-done((bf16[144,896]{1,0:T(8,128)(2,1)S(1)}, bf16[144,896]{1,0:T(8,128)(2,1)S(1)}, u32[]{:S(2)}, u32[]{:S(2)}) %collective-permute-start.25) | collective-permute-done | bytes 258080 | tf_op jit(solution)/shard_map/ppermute | solution.py:827
  77.6 1.3 collective-permute-start.28
  78.8 0.8 collective-permute-start.29
  79.7 2.9 %expand.7 = (f32[288,576]{1,0:T(8,128)S(1)}, f32[288,576]{1,0:T(8,128)S(1)}, f32[288,1]{1,0:T(8,128)S(1)}) custom-call(s32[60]{0:T(128)S(1)} %get-tuple-element.140.tab.refs_0_, bf16[144,896]{1,0:T(8,128)(2,1)S(1)} %collective-permute-done.25.refs_0_.refs_6_.refs_7_, bf16[144,896]{1,0:T(8,128)(2,1)S(1)} %collective-permute-done.26.refs_1_.refs_8_.refs_9_, ...), custom_call_target="tpu_custom_call" | custom-call | flops 1 | bytes 1 | tf_op jit(solution)/shard_map/expand/pallas_call | solution.py:683
  82.5 3.7 %collective-permute-done.28.refs_0_.refs_10_.refs_11_ = bf16[144,896]{1,0:T(8,128)(2,1)S(1)} collective-permute-done((bf16[144,896]{1,0:T(8,128)(2,1)S(1)}, bf16[144,896]{1,0:T(8,128)(2,1)S(1)}, u32[]{:S(2)}, u32[]{:S(2)}) %collective-permute-start.28) | collective-permute-done | bytes 258080 | tf_op jit(solution)/shard_map/ppermute | solution.py:827
  86.2 0.9 collective-permute-done.29.refs_1_.refs_12_.refs_13_
  87.3 1.7 %collective-permute-start.31 = (bf16[80,896]{1,0:T(8,128)(2,1)S(1)}, bf16[80,896]{1,0:T(8,128)(2,1)S(1)}, u32[]{:S(2)}, u32[]{:S(2)}) collective-permute-start(bf16[80,896]{1,0:T(8,128)(2,1)S(1)} %slice.18), channel_id=1, source_target_pairs={{0,4},{4,8},{8,12},{12,14},{14,10},{10,6},{6,2},{2,0},{1,5},{5,9},... | collective-permute-start | bytes 430088 | tf_op jit(solution)/shard_map/ppermute | solution.py:827
  89.4 2.9 %expand.8 = (f32[288,576]{1,0:T(8,128)S(1)}, f32[288,576]{1,0:T(8,128)S(1)}, f32[288,1]{1,0:T(8,128)S(1)}) custom-call(s32[60]{0:T(128)S(1)} %get-tuple-element.140.tab.refs_0_, bf16[144,896]{1,0:T(8,128)(2,1)S(1)} %collective-permute-done.28.refs_0_.refs_10_.refs_11_, bf16[144,896]{1,0:T(8,128)(2,1)S(1)} %collective-permute-done.29.refs_1_.refs_12_.refs_13_, ...), custom_call_target="tpu_custom_call" | custom-call | flops 1 | bytes 1 | tf_op jit(solution)/shard_map/expand/pallas_call | solution.py:683
  92.3 2.0 %collective-permute-done.32.refs_1_ = bf16[64,896]{1,0:T(8,128)(2,1)S(1)} collective-permute-done((bf16[64,896]{1,0:T(8,128)(2,1)S(1)}, bf16[64,896]{1,0:T(8,128)(2,1)S(1)}, u32[]{:S(2)}, u32[]{:S(2)}) %collective-permute-start.32) | collective-permute-done | bytes 114720 | tf_op jit(solution)/shard_map/ppermute | solution.py:830
  94.8 1.0 collective-permute-done.35.refs_3_
  95.8 1.8 %expand.9.hidden = bf16[288,576]{1,0:T(8,128)(2,1)S(1)} custom-call(s32[60]{0:T(128)S(1)} %get-tuple-element.140.tab.refs_0_, bf16[80,896]{1,0:T(8,128)(2,1)S(1)} %collective-permute-done.31.refs_0_, bf16[64,896]{1,0:T(8,128)(2,1)S(1)} %collective-permute-done.32.refs_1_, bf16[80,896]{1,0:T(8,128)(2,1)S(1)} %collective-permute-done.34.refs_2_, ...), custom_call_target="tpu_custom_call" | custom-call | flops 1 | bytes 1 | tf_op jit(solution)/shard_map/expand/pallas_call | solution.py:683
  97.6 1.3 contract.7
  99.3 1.2 contract.6
  100.8 1.2 contract.4.mine
  102.0 1.3 contract.5.mine
  103.3 0.8 pick.3
  105.4 1.9 %collective-permute-start.47 = (bf16[16,3584]{1,0:T(8,128)(2,1)S(1)}, bf16[16,3584]{1,0:T(8,128)(2,1)S(1)}, u32[]{:S(2)}, u32[]{:S(2)}) collective-permute-start(bf16[16,3584]{1,0:T(8,128)(2,1)S(1)} %convert_element_type.156), channel_id=1, source_target_pairs={{0,4},{4,8},{8,12},{12,14},{14,10},{10,6},{6,2},{2,0},{1,5},{5,9},... | collective-permute-start | bytes 344072 | tf_op jit(solution)/shard_map/ppermute | solution.py:827
  107.2 0.8 pick.2
  108.5 1.6 %collective-permute-start.37 = (bf16[16,3584]{1,0:T(8,128)(2,1)S(1)}, bf16[16,3584]{1,0:T(8,128)(2,1)S(1)}, u32[]{:S(2)}, u32[]{:S(2)}) collective-permute-start(bf16[16,3584]{1,0:T(8,128)(2,1)S(1)} %convert_element_type.135), channel_id=1, source_target_pairs={{0,4},{4,8},{8,12},{12,14},{14,10},{10,6},{6,2},{2,0},{1,5},{5,9},... | collective-permute-start | bytes 344072 | tf_op jit(solution)/shard_map/ppermute | solution.py:827
  110.8 1.1 collective-permute-start.50
  111.9 1.0 collective-permute-start.49
  113.4 2.3 %collective-permute-start.39 = (bf16[16,3584]{1,0:T(8,128)(2,1)S(1)}, bf16[16,3584]{1,0:T(8,128)(2,1)S(1)}, u32[]{:S(2)}, u32[]{:S(2)}) collective-permute-start(bf16[16,3584]{1,0:T(8,128)(2,1)S(1)} %add_convert_fusion.12), channel_id=1, source_target_pairs={{0,4},{4,8},{8,12},{12,14},{14,10},{10,6},{6,2},{2,0},{1,5},{5,9},... | collective-permute-start | bytes 344072 | tf_op jit(solution)/shard_map/ppermute | solution.py:827
  115.7 1.5 %collective-permute-done.49 = bf16[16,3584]{1,0:T(8,128)(2,1)S(1)} collective-permute-done((bf16[16,3584]{1,0:T(8,128)(2,1)S(1)}, bf16[16,3584]{1,0:T(8,128)(2,1)S(1)}, u32[]{:S(2)}, u32[]{:S(2)}) %collective-permute-start.49) | collective-permute-done | bytes 114720 | tf_op jit(solution)/shard_map/ppermute | solution.py:827
  117.2 1.1 collective-permute-start.52
  118.3 1.0 collective-permute-start.51
  119.3 1.5 %collective-permute-done.40 = bf16[16,3584]{1,0:T(8,128)(2,1)S(1)} collective-permute-done((bf16[16,3584]{1,0:T(8,128)(2,1)S(1)}, bf16[16,3584]{1,0:T(8,128)(2,1)S(1)}, u32[]{:S(2)}, u32[]{:S(2)}) %collective-permute-start.40) | collective-permute-done | bytes 114720 | tf_op jit(solution)/shard_map/ppermute | solution.py:830
  121.4 1.6 %collective-permute-start.41 = (bf16[16,3584]{1,0:T(8,128)(2,1)S(1)}, bf16[16,3584]{1,0:T(8,128)(2,1)S(1)}, u32[]{:S(2)}, u32[]{:S(2)}) collective-permute-start(bf16[16,3584]{1,0:T(8,128)(2,1)S(1)} %add_convert_fusion.10), channel_id=1, source_target_pairs={{0,4},{4,8},{8,12},{12,14},{14,10},{10,6},{6,2},{2,0},{1,5},{5,9},... | collective-permute-start | bytes 344072 | tf_op jit(solution)/shard_map/ppermute | solution.py:827
  123.0 0.8 collective-permute-done.51
  124.5 1.5 %collective-permute-start.54 = (bf16[16,3584]{1,0:T(8,128)(2,1)S(1)}, bf16[16,3584]{1,0:T(8,128)(2,1)S(1)}, u32[]{:S(2)}, u32[]{:S(2)}) collective-permute-start(bf16[16,3584]{1,0:T(8,128)(2,1)S(1)} %add_convert_fusion.1), channel_id=1, source_target_pairs={{4,0},{8,4},{12,8},{14,12},{10,14},{6,10},{2,6},{0,2},{5,1},{9,5},... | collective-permute-start | bytes 344072 | tf_op jit(solution)/shard_map/ppermute | solution.py:830
  126.0 0.9 collective-permute-done.42
  127.1 1.7 %collective-permute-start.43 = (bf16[16,3584]{1,0:T(8,128)(2,1)S(1)}, bf16[16,3584]{1,0:T(8,128)(2,1)S(1)}, u32[]{:S(2)}, u32[]{:S(2)}) collective-permute-start(bf16[16,3584]{1,0:T(8,128)(2,1)S(1)} %add_convert_fusion.8), channel_id=1, source_target_pairs={{0,4},{4,8},{8,12},{12,14},{14,10},{10,6},{6,2},{2,0},{1,5},{5,9},... | collective-permute-start | bytes 344072 | tf_op jit(solution)/shard_map/ppermute | solution.py:827
  129.9 2.1 %collective-permute-done.43 = bf16[16,3584]{1,0:T(8,128)(2,1)S(1)} collective-permute-done((bf16[16,3584]{1,0:T(8,128)(2,1)S(1)}, bf16[16,3584]{1,0:T(8,128)(2,1)S(1)}, u32[]{:S(2)}, u32[]{:S(2)}) %collective-permute-start.43) | collective-permute-done | bytes 114720 | tf_op jit(solution)/shard_map/ppermute | solution.py:827
  131.9 1.6 %collective-permute-done.44 = bf16[16,3584]{1,0:T(8,128)(2,1)S(1)} collective-permute-done((bf16[16,3584]{1,0:T(8,128)(2,1)S(1)}, bf16[16,3584]{1,0:T(8,128)(2,1)S(1)}, u32[]{:S(2)}, u32[]{:S(2)}) %collective-permute-start.44) | collective-permute-done | bytes 114720 | tf_op jit(solution)/shard_map/ppermute | solution.py:830
  134.5 0.6 collective-permute-done.45
  135.5 0.9 maximum_select_fusion
  (133 shorter events, 14.9 us)
Async XLA Ops:
  1.4 11.3 %copy-start = (bf16[64,7168]{1,0:T(8,128)(2,1)S(1)}, bf16[64,7168]{1,0:T(8,128)(2,1)}, u32[]{:S(2)}) copy-start(bf16[64,7168]{1,0:T(8,128)(2,1)} %res.1) | copy-start | bytes 2752516
  9.6 16.0 %collective-permute-start.11 = (bf16[32,2048]{1,0:T(8,128)(2,1)S(1)}, bf16[32,2048]{1,0:T(8,128)(2,1)S(1)}, u32[]{:S(2)}, u32[]{:S(2)}) collective-permute-start(bf16[32,2048]{1,0:T(8,128)(2,1)S(1)} %get-tuple-element.168), channel_id=1, source_target_pairs={{0,4},{4,8},{8,12},{12,14},{14,10},{10,6},{6,2},{2,0},{1,5},{5,9},... | collective-permute-start | bytes 393224 | tf_op jit(solution)/shard_map/ppermute | solution.py:827
  13.3 9.1 %collective-permute-start = (bf16[64,896]{1,0:T(8,128)(2,1)S(1)}, bf16[64,896]{1,0:T(8,128)(2,1)S(1)}, u32[]{:S(2)}, u32[]{:S(2)}) collective-permute-start(bf16[64,896]{1,0:T(8,128)(2,1)S(1)} %get-tuple-element.143), channel_id=1, source_target_pairs={{0,2},{1,11},{2,0},{3,9},{4,6},{5,15},{6,4},{7,13},{8,10},{9,3},{1... | collective-permute-start | bytes 344072 | tf_op jit(solution)/shard_map/ppermute | solution.py:855
  13.4 9.0 %collective-permute-start.1 = (bf16[64,896]{1,0:T(8,128)(2,1)S(1)}, bf16[64,896]{1,0:T(8,128)(2,1)S(1)}, u32[]{:S(2)}, u32[]{:S(2)}) collective-permute-start(bf16[64,896]{1,0:T(8,128)(2,1)S(1)} %get-tuple-element.144), channel_id=1, source_target_pairs={{0,4},{1,13},{2,6},{3,15},{4,0},{5,9},{6,2},{7,11},{8,12},{9,5},{1... | collective-permute-start | bytes 344072 | tf_op jit(solution)/shard_map/ppermute | solution.py:855
  15.3 7.1 %collective-permute-start.2 = (bf16[64,896]{1,0:T(8,128)(2,1)S(1)}, bf16[64,896]{1,0:T(8,128)(2,1)S(1)}, u32[]{:S(2)}, u32[]{:S(2)}) collective-permute-start(bf16[64,896]{1,0:T(8,128)(2,1)S(1)} %get-tuple-element.145), channel_id=1, source_target_pairs={{0,6},{1,15},{2,4},{3,13},{4,2},{5,11},{6,0},{7,9},{8,14},{9,7},{1... | collective-permute-start | bytes 344072 | tf_op jit(solution)/shard_map/ppermute | solution.py:855
  16.9 9.4 %collective-permute-start.12 = (bf16[32,2048]{1,0:T(8,128)(2,1)S(1)}, bf16[32,2048]{1,0:T(8,128)(2,1)S(1)}, u32[]{:S(2)}, u32[]{:S(2)}) collective-permute-start(bf16[32,2048]{1,0:T(8,128)(2,1)S(1)} %get-tuple-element.186.refs_0_), channel_id=1, source_target_pairs={{4,0},{8,4},{12,8},{14,12},{10,14},{6,10},{2,6},{0,2},{5,1},{9,5},... | collective-permute-start | bytes 393224 | tf_op jit(solution)/shard_map/ppermute | solution.py:830
  17.7 35.0 %slice-start.6 = ((s8[7340032]{0:T(1024)(128)(4,1)}), s8[4194304]{0:T(1024)(128)(4,1)S(1)}, s32[]{:S(2)}) async-start(s8[7340032]{0:T(1024)(128)(4,1)} %bitcast.25), calls=%async_computation.6 | async-start | bytes 8388608
  17.7 35.0 %slice-start.7 = ((s8[7340032]{0:T(1024)(128)(4,1)}), s8[3145728]{0:T(1024)(128)(4,1)S(1)}, s32[]{:S(2)}) async-start(s8[7340032]{0:T(1024)(128)(4,1)} %bitcast.25), calls=%async_computation.7 | async-start | bytes 6291456
  22.4 12.1 %collective-permute-start.14 = (bf16[64,896]{1,0:T(8,128)(2,1)S(1)}, bf16[64,896]{1,0:T(8,128)(2,1)S(1)}, u32[]{:S(2)}, u32[]{:S(2)}) collective-permute-start(bf16[64,896]{1,0:T(8,128)(2,1)S(1)} %get-tuple-element.172.own), channel_id=1, source_target_pairs={{1,9},{3,11},{5,13},{7,15},{9,1},{11,3},{13,5},{15,7},{17,25},{19,... | collective-permute-start | bytes 344072 | tf_op jit(solution)/shard_map/ppermute | solution.py:855
  23.1 7.2 %collective-permute-start.4 = (bf16[32,2048]{1,0:T(8,128)(2,1)S(1)}, bf16[32,2048]{1,0:T(8,128)(2,1)S(1)}, u32[]{:S(2)}, u32[]{:S(2)}) collective-permute-start(bf16[32,2048]{1,0:T(8,128)(2,1)S(1)} %get-tuple-element.159.refs_0_), channel_id=1, source_target_pairs={{4,0},{8,4},{12,8},{14,12},{10,14},{6,10},{2,6},{0,2},{5,1},{9,5},... | collective-permute-start | bytes 393224 | tf_op jit(solution)/shard_map/ppermute | solution.py:830
  25.4 5.0 %collective-permute-start.3 = (bf16[32,2048]{1,0:T(8,128)(2,1)S(1)}, bf16[32,2048]{1,0:T(8,128)(2,1)S(1)}, u32[]{:S(2)}, u32[]{:S(2)}) collective-permute-start(bf16[32,2048]{1,0:T(8,128)(2,1)S(1)} %get-tuple-element.156), channel_id=1, source_target_pairs={{0,4},{4,8},{8,12},{12,14},{14,10},{10,6},{6,2},{2,0},{1,5},{5,9},... | collective-permute-start | bytes 393224 | tf_op jit(solution)/shard_map/ppermute | solution.py:827
  26.3 8.3 %collective-permute-start.13 = (bf16[32,2048]{1,0:T(8,128)(2,1)S(1)}, bf16[32,2048]{1,0:T(8,128)(2,1)S(1)}, u32[]{:S(2)}, u32[]{:S(2)}) collective-permute-start(bf16[32,2048]{1,0:T(8,128)(2,1)S(1)} %broadcast_select_fusion.5), channel_id=1, source_target_pairs={{0,4},{4,8},{8,12},{12,14},{14,10},{10,6},{6,2},{2,0},{1,5},{5,9},... | collective-permute-start | bytes 393224 | tf_op jit(solution)/shard_map/ppermute | solution.py:827
  27.8 10.7 %collective-permute-start.15 = (bf16[32,2048]{1,0:T(8,128)(2,1)S(1)}, bf16[32,2048]{1,0:T(8,128)(2,1)S(1)}, u32[]{:S(2)}, u32[]{:S(2)}) collective-permute-start(bf16[32,2048]{1,0:T(8,128)(2,1)S(1)} %broadcast_select_fusion.4), channel_id=1, source_target_pairs={{4,0},{8,4},{12,8},{14,12},{10,14},{6,10},{2,6},{0,2},{5,1},{9,5},... | collective-permute-start | bytes 393224 | tf_op jit(solution)/shard_map/ppermute | solution.py:830
  30.4 10.2 %collective-permute-start.6 = (bf16[32,2048]{1,0:T(8,128)(2,1)S(1)}, bf16[32,2048]{1,0:T(8,128)(2,1)S(1)}, u32[]{:S(2)}, u32[]{:S(2)}) collective-permute-start(bf16[32,2048]{1,0:T(8,128)(2,1)S(1)} %broadcast_select_fusion.10), channel_id=1, source_target_pairs={{4,0},{8,4},{12,8},{14,12},{10,14},{6,10},{2,6},{0,2},{5,1},{9,5},... | collective-permute-start | bytes 393224 | tf_op jit(solution)/shard_map/ppermute | solution.py:830
  34.5 6.5 %collective-permute-start.5 = (bf16[32,2048]{1,0:T(8,128)(2,1)S(1)}, bf16[32,2048]{1,0:T(8,128)(2,1)S(1)}, u32[]{:S(2)}, u32[]{:S(2)}) collective-permute-start(bf16[32,2048]{1,0:T(8,128)(2,1)S(1)} %broadcast_select_fusion.11), channel_id=1, source_target_pairs={{0,4},{4,8},{8,12},{12,14},{14,10},{10,6},{6,2},{2,0},{1,5},{5,9},... | collective-permute-start | bytes 393224 | tf_op jit(solution)/shard_map/ppermute | solution.py:827
  35.1 16.2 %collective-permute-start.20 = (bf16[128,896]{1,0:T(8,128)(2,1)S(1)}, bf16[128,896]{1,0:T(8,128)(2,1)S(1)}, u32[]{:S(2)}, u32[]{:S(2)}) collective-permute-start(bf16[128,896]{1,0:T(8,128)(2,1)S(1)} %share.1), channel_id=1, source_target_pairs={{0,1},{1,0},{2,3},{3,2},{4,5},{5,4},{6,7},{7,6},{8,9},{9,8},{10,11... | collective-permute-start | bytes 688136 | tf_op jit(solution)/shard_map/ppermute | solution.py:833
  38.5 6.3 %collective-permute-start.17 = (bf16[32,2048]{1,0:T(8,128)(2,1)S(1)}, bf16[32,2048]{1,0:T(8,128)(2,1)S(1)}, u32[]{:S(2)}, u32[]{:S(2)}) collective-permute-start(bf16[32,2048]{1,0:T(8,128)(2,1)S(1)} %broadcast_select_fusion.2), channel_id=1, source_target_pairs={{4,0},{8,4},{12,8},{14,12},{10,14},{6,10},{2,6},{0,2},{5,1},{9,5},... | collective-permute-start | bytes 393224 | tf_op jit(solution)/shard_map/ppermute | solution.py:830
  38.9 6.0 %collective-permute-start.16 = (bf16[32,2048]{1,0:T(8,128)(2,1)S(1)}, bf16[32,2048]{1,0:T(8,128)(2,1)S(1)}, u32[]{:S(2)}, u32[]{:S(2)}) collective-permute-start(bf16[32,2048]{1,0:T(8,128)(2,1)S(1)} %broadcast_select_fusion.3), channel_id=1, source_target_pairs={{0,4},{4,8},{8,12},{12,14},{14,10},{10,6},{6,2},{2,0},{1,5},{5,9},... | collective-permute-start | bytes 393224 | tf_op jit(solution)/shard_map/ppermute | solution.py:827
  41.0 6.3 %collective-permute-start.8 = (bf16[32,2048]{1,0:T(8,128)(2,1)S(1)}, bf16[32,2048]{1,0:T(8,128)(2,1)S(1)}, u32[]{:S(2)}, u32[]{:S(2)}) collective-permute-start(bf16[32,2048]{1,0:T(8,128)(2,1)S(1)} %broadcast_select_fusion.8), channel_id=1, source_target_pairs={{4,0},{8,4},{12,8},{14,12},{10,14},{6,10},{2,6},{0,2},{5,1},{9,5},... | collective-permute-start | bytes 393224 | tf_op jit(solution)/shard_map/ppermute | solution.py:830
  43.1 6.0 %collective-permute-start.7 = (bf16[32,2048]{1,0:T(8,128)(2,1)S(1)}, bf16[32,2048]{1,0:T(8,128)(2,1)S(1)}, u32[]{:S(2)}, u32[]{:S(2)}) collective-permute-start(bf16[32,2048]{1,0:T(8,128)(2,1)S(1)} %broadcast_select_fusion.9), channel_id=1, source_target_pairs={{0,4},{4,8},{8,12},{12,14},{14,10},{10,6},{6,2},{2,0},{1,5},{5,9},... | collective-permute-start | bytes 393224 | tf_op jit(solution)/shard_map/ppermute | solution.py:827
  44.8 15.9 %slice-start.2 = ((s8[8257536]{0:T(1024)(128)(4,1)}), s8[4194304]{0:T(1024)(128)(4,1)S(1)}, s32[]{:S(2)}) async-start(s8[8257536]{0:T(1024)(128)(4,1)} %bitcast.16), calls=%async_computation.2 | async-start | bytes 8388608
  44.9 6.4 %collective-permute-start.18 = (bf16[32,2048]{1,0:T(8,128)(2,1)S(1)}, bf16[32,2048]{1,0:T(8,128)(2,1)S(1)}, u32[]{:S(2)}, u32[]{:S(2)}) collective-permute-start(bf16[32,2048]{1,0:T(8,128)(2,1)S(1)} %broadcast_select_fusion.1), channel_id=1, source_target_pairs={{0,4},{4,8},{8,12},{12,14},{14,10},{10,6},{6,2},{2,0},{1,5},{5,9},... | collective-permute-start | bytes 393224 | tf_op jit(solution)/shard_map/ppermute | solution.py:827
  47.0 5.7 %collective-permute-start.19 = (bf16[32,2048]{1,0:T(8,128)(2,1)S(1)}, bf16[32,2048]{1,0:T(8,128)(2,1)S(1)}, u32[]{:S(2)}, u32[]{:S(2)}) collective-permute-start(bf16[32,2048]{1,0:T(8,128)(2,1)S(1)} %broadcast_select_fusion), channel_id=1, source_target_pairs={{4,0},{8,4},{12,8},{14,12},{10,14},{6,10},{2,6},{0,2},{5,1},{9,5},... | collective-permute-start | bytes 393224 | tf_op jit(solution)/shard_map/ppermute | solution.py:830
  49.2 5.4 %collective-permute-start.10 = (bf16[32,2048]{1,0:T(8,128)(2,1)S(1)}, bf16[32,2048]{1,0:T(8,128)(2,1)S(1)}, u32[]{:S(2)}, u32[]{:S(2)}) collective-permute-start(bf16[32,2048]{1,0:T(8,128)(2,1)S(1)} %broadcast_select_fusion.6), channel_id=1, source_target_pairs={{4,0},{8,4},{12,8},{14,12},{10,14},{6,10},{2,6},{0,2},{5,1},{9,5},... | collective-permute-start | bytes 393224 | tf_op jit(solution)/shard_map/ppermute | solution.py:830
  49.8 5.0 %collective-permute-start.9 = (bf16[32,2048]{1,0:T(8,128)(2,1)S(1)}, bf16[32,2048]{1,0:T(8,128)(2,1)S(1)}, u32[]{:S(2)}, u32[]{:S(2)}) collective-permute-start(bf16[32,2048]{1,0:T(8,128)(2,1)S(1)} %broadcast_select_fusion.7), channel_id=1, source_target_pairs={{0,4},{4,8},{8,12},{12,14},{14,10},{10,6},{6,2},{2,0},{1,5},{5,9},... | collective-permute-start | bytes 393224 | tf_op jit(solution)/shard_map/ppermute | solution.py:827
  52.6 8.1 %slice-start = ((s8[8257536]{0:T(1024)(128)(4,1)}), s8[4194304]{0:T(1024)(128)(4,1)S(1)}, s32[]{:S(2)}) async-start(s8[8257536]{0:T(1024)(128)(4,1)} %bitcast.9), calls=%async_computation | async-start | bytes 8388608
  54.6 6.2 %slice-start.1 = ((s8[8257536]{0:T(1024)(128)(4,1)}), s8[4063232]{0:T(1024)(128)(4,1)S(1)}, s32[]{:S(2)}) async-start(s8[8257536]{0:T(1024)(128)(4,1)} %bitcast.9), calls=%async_computation.1 | async-start | bytes 8126464
  56.8 1.6 %collective-permute-start.21 = (bf16[144,896]{1,0:T(8,128)(2,1)S(1)}, bf16[144,896]{1,0:T(8,128)(2,1)S(1)}, u32[]{:S(2)}, u32[]{:S(2)}) collective-permute-start(bf16[144,896]{1,0:T(8,128)(2,1)S(1)} %get-tuple-element.198), channel_id=1, source_target_pairs={{0,1},{1,0},{2,3},{3,2},{4,5},{5,4},{6,7},{7,6},{8,9},{9,8},{10,11... | collective-permute-start | bytes 774152 | tf_op jit(solution)/shard_map/ppermute | solution.py:833
  58.5 2.2 %collective-permute-start.24 = (bf16[144,896]{1,0:T(8,128)(2,1)S(1)}, bf16[144,896]{1,0:T(8,128)(2,1)S(1)}, u32[]{:S(2)}, u32[]{:S(2)}) collective-permute-start(bf16[144,896]{1,0:T(8,128)(2,1)S(1)} %add_convert_fusion.refs_0_.refs_1_), channel_id=1, source_target_pairs={{0,1},{1,0},{2,3},{3,2},{4,5},{5,4},{6,7},{7,6},{8,9},{9,8},{10,11... | collective-permute-start | bytes 774152 | tf_op jit(solution)/shard_map/ppermute | solution.py:833
  58.7 8.6 %collective-permute-start.22 = (bf16[144,896]{1,0:T(8,128)(2,1)S(1)}, bf16[144,896]{1,0:T(8,128)(2,1)S(1)}, u32[]{:S(2)}, u32[]{:S(2)}) collective-permute-start(bf16[144,896]{1,0:T(8,128)(2,1)S(1)} %add_convert_fusion.refs_0_.refs_1_), channel_id=1, source_target_pairs={{0,4},{4,8},{8,12},{12,14},{14,10},{10,6},{6,2},{2,0},{1,5},{5,9},... | collective-permute-start | bytes 774152 | tf_op jit(solution)/shard_map/ppermute | solution.py:827
  60.2 8.2 %collective-permute-start.23 = (bf16[144,896]{1,0:T(8,128)(2,1)S(1)}, bf16[144,896]{1,0:T(8,128)(2,1)S(1)}, u32[]{:S(2)}, u32[]{:S(2)}) collective-permute-start(bf16[144,896]{1,0:T(8,128)(2,1)S(1)} %add_convert_fusion.refs_0_.refs_1_), channel_id=1, source_target_pairs={{4,0},{8,4},{12,8},{14,12},{10,14},{6,10},{2,6},{0,2},{5,1},{9,5},... | collective-permute-start | bytes 774152 | tf_op jit(solution)/shard_map/ppermute | solution.py:830
  68.4 2.2 %collective-permute-start.27 = (bf16[288,896]{1,0:T(8,128)(2,1)S(1)}, bf16[288,896]{1,0:T(8,128)(2,1)S(1)}, u32[]{:S(2)}, u32[]{:S(2)}) collective-permute-start(bf16[288,896]{1,0:T(8,128)(2,1)S(1)} %pad_maximum_fusion), channel_id=1, source_target_pairs={{0,1},{1,0},{2,3},{3,2},{4,5},{5,4},{6,7},{7,6},{8,9},{9,8},{10,11... | collective-permute-start | bytes 1548296 | tf_op jit(solution)/shard_map/ppermute | solution.py:833
  68.5 8.6 %collective-permute-start.25 = (bf16[144,896]{1,0:T(8,128)(2,1)S(1)}, bf16[144,896]{1,0:T(8,128)(2,1)S(1)}, u32[]{:S(2)}, u32[]{:S(2)}) collective-permute-start(bf16[144,896]{1,0:T(8,128)(2,1)S(1)} %collective-permute-done.22.refs_0_.refs_2_.refs_3_), channel_id=1, source_target_pairs={{0,4},{4,8},{8,12},{12,14},{14,10},{10,6},{6,2},{2,0},{1,5},{5,9},... | collective-permute-start | bytes 774152 | tf_op jit(solution)/shard_map/ppermute | solution.py:827
  69.2 8.3 %collective-permute-start.26 = (bf16[144,896]{1,0:T(8,128)(2,1)S(1)}, bf16[144,896]{1,0:T(8,128)(2,1)S(1)}, u32[]{:S(2)}, u32[]{:S(2)}) collective-permute-start(bf16[144,896]{1,0:T(8,128)(2,1)S(1)} %collective-permute-done.23.refs_1_.refs_4_.refs_5_), channel_id=1, source_target_pairs={{4,0},{8,4},{12,8},{14,12},{10,14},{6,10},{2,6},{0,2},{5,1},{9,5},... | collective-permute-start | bytes 774152 | tf_op jit(solution)/shard_map/ppermute | solution.py:830
  77.5 2.2 %collective-permute-start.30 = (bf16[288,896]{1,0:T(8,128)(2,1)S(1)}, bf16[288,896]{1,0:T(8,128)(2,1)S(1)}, u32[]{:S(2)}, u32[]{:S(2)}) collective-permute-start(bf16[288,896]{1,0:T(8,128)(2,1)S(1)} %pad_maximum_fusion.1), channel_id=1, source_target_pairs={{0,1},{1,0},{2,3},{3,2},{4,5},{5,4},{6,7},{7,6},{8,9},{9,8},{10,11... | collective-permute-start | bytes 1548296 | tf_op jit(solution)/shard_map/ppermute | solution.py:833
  77.6 8.6 %collective-permute-start.28 = (bf16[144,896]{1,0:T(8,128)(2,1)S(1)}, bf16[144,896]{1,0:T(8,128)(2,1)S(1)}, u32[]{:S(2)}, u32[]{:S(2)}) collective-permute-start(bf16[144,896]{1,0:T(8,128)(2,1)S(1)} %collective-permute-done.25.refs_0_.refs_6_.refs_7_), channel_id=1, source_target_pairs={{0,4},{4,8},{8,12},{12,14},{14,10},{10,6},{6,2},{2,0},{1,5},{5,9},... | collective-permute-start | bytes 774152 | tf_op jit(solution)/shard_map/ppermute | solution.py:827
  78.8 8.3 %collective-permute-start.29 = (bf16[144,896]{1,0:T(8,128)(2,1)S(1)}, bf16[144,896]{1,0:T(8,128)(2,1)S(1)}, u32[]{:S(2)}, u32[]{:S(2)}) collective-permute-start(bf16[144,896]{1,0:T(8,128)(2,1)S(1)} %collective-permute-done.26.refs_1_.refs_8_.refs_9_), channel_id=1, source_target_pairs={{4,0},{8,4},{12,8},{14,12},{10,14},{6,10},{2,6},{0,2},{5,1},{9,5},... | collective-permute-start | bytes 774152 | tf_op jit(solution)/shard_map/ppermute | solution.py:830
  87.1 10.5 %slice-start.4 = ((s8[8257536]{0:T(1024)(128)(4,1)}), s8[4194304]{0:T(1024)(128)(4,1)S(1)}, s32[]{:S(2)}) async-start(s8[8257536]{0:T(1024)(128)(4,1)} %bitcast.23), calls=%async_computation.4 | async-start | bytes 8388608
  87.2 2.3 %collective-permute-start.33 = (bf16[288,896]{1,0:T(8,128)(2,1)S(1)}, bf16[288,896]{1,0:T(8,128)(2,1)S(1)}, u32[]{:S(2)}, u32[]{:S(2)}) collective-permute-start(bf16[288,896]{1,0:T(8,128)(2,1)S(1)} %pad_maximum_fusion.2), channel_id=1, source_target_pairs={{0,1},{1,0},{2,3},{3,2},{4,5},{5,4},{6,7},{7,6},{8,9},{9,8},{10,11... | collective-permute-start | bytes 1548296 | tf_op jit(solution)/shard_map/ppermute | solution.py:833
  87.3 7.0 %collective-permute-start.31 = (bf16[80,896]{1,0:T(8,128)(2,1)S(1)}, bf16[80,896]{1,0:T(8,128)(2,1)S(1)}, u32[]{:S(2)}, u32[]{:S(2)}) collective-permute-start(bf16[80,896]{1,0:T(8,128)(2,1)S(1)} %slice.18), channel_id=1, source_target_pairs={{0,4},{4,8},{8,12},{12,14},{14,10},{10,6},{6,2},{2,0},{1,5},{5,9},... | collective-permute-start | bytes 430088 | tf_op jit(solution)/shard_map/ppermute | solution.py:827
  89.0 8.7 %slice-start.5 = ((s8[8257536]{0:T(1024)(128)(4,1)}), s8[4063232]{0:T(1024)(128)(4,1)S(1)}, s32[]{:S(2)}) async-start(s8[8257536]{0:T(1024)(128)(4,1)} %bitcast.23), calls=%async_computation.5 | async-start | bytes 8126464
  89.0 5.3 %collective-permute-start.32 = (bf16[64,896]{1,0:T(8,128)(2,1)S(1)}, bf16[64,896]{1,0:T(8,128)(2,1)S(1)}, u32[]{:S(2)}, u32[]{:S(2)}) collective-permute-start(bf16[64,896]{1,0:T(8,128)(2,1)S(1)} %slice.19), channel_id=1, source_target_pairs={{4,0},{8,4},{12,8},{14,12},{10,14},{6,10},{2,6},{0,2},{5,1},{9,5},... | collective-permute-start | bytes 344072 | tf_op jit(solution)/shard_map/ppermute | solution.py:830
  94.3 1.5 %collective-permute-start.34 = (bf16[80,896]{1,0:T(8,128)(2,1)S(1)}, bf16[80,896]{1,0:T(8,128)(2,1)S(1)}, u32[]{:S(2)}, u32[]{:S(2)}) collective-permute-start(bf16[80,896]{1,0:T(8,128)(2,1)S(1)} %collective-permute-done.31.refs_0_), channel_id=1, source_target_pairs={{0,1},{1,0},{2,3},{3,2},{4,5},{5,4},{6,7},{7,6},{8,9},{9,8},{10,11... | collective-permute-start | bytes 430088 | tf_op jit(solution)/shard_map/ppermute | solution.py:833
  94.3 1.5 %collective-permute-start.35 = (bf16[64,896]{1,0:T(8,128)(2,1)S(1)}, bf16[64,896]{1,0:T(8,128)(2,1)S(1)}, u32[]{:S(2)}, u32[]{:S(2)}) collective-permute-start(bf16[64,896]{1,0:T(8,128)(2,1)S(1)} %collective-permute-done.32.refs_1_), channel_id=1, source_target_pairs={{0,1},{1,0},{2,3},{3,2},{4,5},{5,4},{6,7},{7,6},{8,9},{9,8},{10,11... | collective-permute-start | bytes 344072 | tf_op jit(solution)/shard_map/ppermute | solution.py:833
  98.9 4.4 %collective-permute-start.46 = (bf16[144,3584]{1,0:T(8,128)(2,1)S(1)}, bf16[144,3584]{1,0:T(8,128)(2,1)S(1)}, u32[]{:S(2)}, u32[]{:S(2)}) collective-permute-start(bf16[144,3584]{1,0:T(8,128)(2,1)S(1)} %contract.7), channel_id=1, source_target_pairs={{0,1},{1,0},{2,3},{3,2},{4,5},{5,4},{6,7},{7,6},{8,9},{9,8},{10,11... | collective-permute-start | bytes 3096584 | tf_op jit(solution)/shard_map/ppermute | solution.py:833
  100.5 6.7 %collective-permute-start.36 = (bf16[144,3584]{1,0:T(8,128)(2,1)S(1)}, bf16[144,3584]{1,0:T(8,128)(2,1)S(1)}, u32[]{:S(2)}, u32[]{:S(2)}) collective-permute-start(bf16[144,3584]{1,0:T(8,128)(2,1)S(1)} %contract.6), channel_id=1, source_target_pairs={{0,1},{1,0},{2,3},{3,2},{4,5},{5,4},{6,7},{7,6},{8,9},{9,8},{10,11... | collective-permute-start | bytes 3096584 | tf_op jit(solution)/shard_map/ppermute | solution.py:833
  104.2 5.9 %collective-permute-start.48 = (bf16[16,3584]{1,0:T(8,128)(2,1)S(1)}, bf16[16,3584]{1,0:T(8,128)(2,1)S(1)}, u32[]{:S(2)}, u32[]{:S(2)}) collective-permute-start(bf16[16,3584]{1,0:T(8,128)(2,1)S(1)} %convert_element_type.157), channel_id=1, source_target_pairs={{4,0},{8,4},{12,8},{14,12},{10,14},{6,10},{2,6},{0,2},{5,1},{9,5},... | collective-permute-start | bytes 344072 | tf_op jit(solution)/shard_map/ppermute | solution.py:830
  105.4 5.4 %collective-permute-start.47 = (bf16[16,3584]{1,0:T(8,128)(2,1)S(1)}, bf16[16,3584]{1,0:T(8,128)(2,1)S(1)}, u32[]{:S(2)}, u32[]{:S(2)}) collective-permute-start(bf16[16,3584]{1,0:T(8,128)(2,1)S(1)} %convert_element_type.156), channel_id=1, source_target_pairs={{0,4},{4,8},{8,12},{12,14},{14,10},{10,6},{6,2},{2,0},{1,5},{5,9},... | collective-permute-start | bytes 344072 | tf_op jit(solution)/shard_map/ppermute | solution.py:827
  108.1 5.2 %collective-permute-start.38 = (bf16[16,3584]{1,0:T(8,128)(2,1)S(1)}, bf16[16,3584]{1,0:T(8,128)(2,1)S(1)}, u32[]{:S(2)}, u32[]{:S(2)}) collective-permute-start(bf16[16,3584]{1,0:T(8,128)(2,1)S(1)} %convert_element_type.136), channel_id=1, source_target_pairs={{4,0},{8,4},{12,8},{14,12},{10,14},{6,10},{2,6},{0,2},{5,1},{9,5},... | collective-permute-start | bytes 344072 | tf_op jit(solution)/shard_map/ppermute | solution.py:830
  108.5 4.8 %collective-permute-start.37 = (bf16[16,3584]{1,0:T(8,128)(2,1)S(1)}, bf16[16,3584]{1,0:T(8,128)(2,1)S(1)}, u32[]{:S(2)}, u32[]{:S(2)}) collective-permute-start(bf16[16,3584]{1,0:T(8,128)(2,1)S(1)} %convert_element_type.135), channel_id=1, source_target_pairs={{0,4},{4,8},{8,12},{12,14},{14,10},{10,6},{6,2},{2,0},{1,5},{5,9},... | collective-permute-start | bytes 344072 | tf_op jit(solution)/shard_map/ppermute | solution.py:827
  110.8 4.9 %collective-permute-start.50 = (bf16[16,3584]{1,0:T(8,128)(2,1)S(1)}, bf16[16,3584]{1,0:T(8,128)(2,1)S(1)}, u32[]{:S(2)}, u32[]{:S(2)}) collective-permute-start(bf16[16,3584]{1,0:T(8,128)(2,1)S(1)} %add_convert_fusion.5), channel_id=1, source_target_pairs={{4,0},{8,4},{12,8},{14,12},{10,14},{6,10},{2,6},{0,2},{5,1},{9,5},... | collective-permute-start | bytes 344072 | tf_op jit(solution)/shard_map/ppermute | solution.py:830
  111.9 5.3 %collective-permute-start.49 = (bf16[16,3584]{1,0:T(8,128)(2,1)S(1)}, bf16[16,3584]{1,0:T(8,128)(2,1)S(1)}, u32[]{:S(2)}, u32[]{:S(2)}) collective-permute-start(bf16[16,3584]{1,0:T(8,128)(2,1)S(1)} %add_convert_fusion.6), channel_id=1, source_target_pairs={{0,4},{4,8},{8,12},{12,14},{14,10},{10,6},{6,2},{2,0},{1,5},{5,9},... | collective-permute-start | bytes 344072 | tf_op jit(solution)/shard_map/ppermute | solution.py:827
  113.4 7.5 %collective-permute-start.39 = (bf16[16,3584]{1,0:T(8,128)(2,1)S(1)}, bf16[16,3584]{1,0:T(8,128)(2,1)S(1)}, u32[]{:S(2)}, u32[]{:S(2)}) collective-permute-start(bf16[16,3584]{1,0:T(8,128)(2,1)S(1)} %add_convert_fusion.12), channel_id=1, source_target_pairs={{0,4},{4,8},{8,12},{12,14},{14,10},{10,6},{6,2},{2,0},{1,5},{5,9},... | collective-permute-start | bytes 344072 | tf_op jit(solution)/shard_map/ppermute | solution.py:827
  115.7 5.1 %collective-permute-start.40 = (bf16[16,3584]{1,0:T(8,128)(2,1)S(1)}, bf16[16,3584]{1,0:T(8,128)(2,1)S(1)}, u32[]{:S(2)}, u32[]{:S(2)}) collective-permute-start(bf16[16,3584]{1,0:T(8,128)(2,1)S(1)} %add_convert_fusion.11), channel_id=1, source_target_pairs={{4,0},{8,4},{12,8},{14,12},{10,14},{6,10},{2,6},{0,2},{5,1},{9,5},... | collective-permute-start | bytes 344072 | tf_op jit(solution)/shard_map/ppermute | solution.py:830
  117.2 5.7 %collective-permute-start.52 = (bf16[16,3584]{1,0:T(8,128)(2,1)S(1)}, bf16[16,3584]{1,0:T(8,128)(2,1)S(1)}, u32[]{:S(2)}, u32[]{:S(2)}) collective-permute-start(bf16[16,3584]{1,0:T(8,128)(2,1)S(1)} %add_convert_fusion.3), channel_id=1, source_target_pairs={{4,0},{8,4},{12,8},{14,12},{10,14},{6,10},{2,6},{0,2},{5,1},{9,5},... | collective-permute-start | bytes 344072 | tf_op jit(solution)/shard_map/ppermute | solution.py:830
  118.3 5.5 %collective-permute-start.51 = (bf16[16,3584]{1,0:T(8,128)(2,1)S(1)}, bf16[16,3584]{1,0:T(8,128)(2,1)S(1)}, u32[]{:S(2)}, u32[]{:S(2)}) collective-permute-start(bf16[16,3584]{1,0:T(8,128)(2,1)S(1)} %add_convert_fusion.4), channel_id=1, source_target_pairs={{0,4},{4,8},{8,12},{12,14},{14,10},{10,6},{6,2},{2,0},{1,5},{5,9},... | collective-permute-start | bytes 344072 | tf_op jit(solution)/shard_map/ppermute | solution.py:827
  120.9 6.0 %collective-permute-start.42 = (bf16[16,3584]{1,0:T(8,128)(2,1)S(1)}, bf16[16,3584]{1,0:T(8,128)(2,1)S(1)}, u32[]{:S(2)}, u32[]{:S(2)}) collective-permute-start(bf16[16,3584]{1,0:T(8,128)(2,1)S(1)} %add_convert_fusion.9), channel_id=1, source_target_pairs={{4,0},{8,4},{12,8},{14,12},{10,14},{6,10},{2,6},{0,2},{5,1},{9,5},... | collective-permute-start | bytes 344072 | tf_op jit(solution)/shard_map/ppermute | solution.py:830
  121.4 5.6 %collective-permute-start.41 = (bf16[16,3584]{1,0:T(8,128)(2,1)S(1)}, bf16[16,3584]{1,0:T(8,128)(2,1)S(1)}, u32[]{:S(2)}, u32[]{:S(2)}) collective-permute-start(bf16[16,3584]{1,0:T(8,128)(2,1)S(1)} %add_convert_fusion.10), channel_id=1, source_target_pairs={{0,4},{4,8},{8,12},{12,14},{14,10},{10,6},{6,2},{2,0},{1,5},{5,9},... | collective-permute-start | bytes 344072 | tf_op jit(solution)/shard_map/ppermute | solution.py:827
  123.9 5.9 %collective-permute-start.53 = (bf16[16,3584]{1,0:T(8,128)(2,1)S(1)}, bf16[16,3584]{1,0:T(8,128)(2,1)S(1)}, u32[]{:S(2)}, u32[]{:S(2)}) collective-permute-start(bf16[16,3584]{1,0:T(8,128)(2,1)S(1)} %add_convert_fusion.2), channel_id=1, source_target_pairs={{0,4},{4,8},{8,12},{12,14},{14,10},{10,6},{6,2},{2,0},{1,5},{5,9},... | collective-permute-start | bytes 344072 | tf_op jit(solution)/shard_map/ppermute | solution.py:827
  124.5 5.4 %collective-permute-start.54 = (bf16[16,3584]{1,0:T(8,128)(2,1)S(1)}, bf16[16,3584]{1,0:T(8,128)(2,1)S(1)}, u32[]{:S(2)}, u32[]{:S(2)}) collective-permute-start(bf16[16,3584]{1,0:T(8,128)(2,1)S(1)} %add_convert_fusion.1), channel_id=1, source_target_pairs={{4,0},{8,4},{12,8},{14,12},{10,14},{6,10},{2,6},{0,2},{5,1},{9,5},... | collective-permute-start | bytes 344072 | tf_op jit(solution)/shard_map/ppermute | solution.py:830
  127.1 4.8 %collective-permute-start.43 = (bf16[16,3584]{1,0:T(8,128)(2,1)S(1)}, bf16[16,3584]{1,0:T(8,128)(2,1)S(1)}, u32[]{:S(2)}, u32[]{:S(2)}) collective-permute-start(bf16[16,3584]{1,0:T(8,128)(2,1)S(1)} %add_convert_fusion.8), channel_id=1, source_target_pairs={{0,4},{4,8},{8,12},{12,14},{14,10},{10,6},{6,2},{2,0},{1,5},{5,9},... | collective-permute-start | bytes 344072 | tf_op jit(solution)/shard_map/ppermute | solution.py:827
  128.7 4.8 %collective-permute-start.44 = (bf16[16,3584]{1,0:T(8,128)(2,1)S(1)}, bf16[16,3584]{1,0:T(8,128)(2,1)S(1)}, u32[]{:S(2)}, u32[]{:S(2)}) collective-permute-start(bf16[16,3584]{1,0:T(8,128)(2,1)S(1)} %add_convert_fusion.7), channel_id=1, source_target_pairs={{4,0},{8,4},{12,8},{14,12},{10,14},{6,10},{2,6},{0,2},{5,1},{9,5},... | collective-permute-start | bytes 344072 | tf_op jit(solution)/shard_map/ppermute | solution.py:830
  133.8 1.4 %collective-permute-start.45 = (bf16[16,3584]{1,0:T(8,128)(2,1)S(1)}, bf16[16,3584]{1,0:T(8,128)(2,1)S(1)}, u32[]{:S(2)}, u32[]{:S(2)}) collective-permute-start(bf16[16,3584]{1,0:T(8,128)(2,1)S(1)} %get-tuple-element.271), channel_id=1, source_target_pairs={{0,1},{1,0},{2,3},{3,2},{4,5},{5,4},{6,7},{7,6},{8,9},{9,8},{10,11... | collective-permute-start | bytes 344072 | tf_op jit(solution)/shard_map/ppermute | solution.py:833
  133.9 1.5 %collective-permute-start.55 = (bf16[16,3584]{1,0:T(8,128)(2,1)S(1)}, bf16[16,3584]{1,0:T(8,128)(2,1)S(1)}, u32[]{:S(2)}, u32[]{:S(2)}) collective-permute-start(bf16[16,3584]{1,0:T(8,128)(2,1)S(1)} %get-tuple-element.277), channel_id=1, source_target_pairs={{0,1},{1,0},{2,3},{3,2},{4,5},{5,4},{6,7},{7,6},{8,9},{9,8},{10,11... | collective-permute-start | bytes 344072 | tf_op jit(solution)/shard_map/ppermute | solution.py:833
  (2 other events, 12.3 us)
